TPU v7x, 32 devices: a whole 2x2x4 slice. The times are simulated.
32 devices in a mesh: ctx: 16 (over z, y, core), head: 2 (over x).
Axes of the slice: x: 2, y: 2, z: 4, core: 2. Of those that a mesh axis runs over, the one named last changes fastest.
Arguments:
- queries: bfloat16 [64, 16384], P('ctx', 'head'), may hold values from -7 to 7
- grad_out: bfloat16 [64, 16384], P('ctx', 'head'), may hold values from -384 to 384
- outputs: bfloat16 [64, 16384], P('ctx', 'head'), may hold values from -6 to 6
- lse_self: float32 [64, 128], P('ctx', 'head'), may hold values from 0 to 20
- prompt_keys: bfloat16 [4096, 1024], P(('ctx', 'head')), may hold values from -11 to 11
- prompt_values: bfloat16 [4096, 1024], P(('ctx', 'head')), may hold values from -6 to 6
- resp_len: int32 [1], replicated, may hold values from 16 to 64, as said below
- prompt_end: int32 [1], replicated, may hold values from 2048 to 4096, as said below
Outputs:
- query_grad: bfloat16 [64, 16384], P('ctx', 'head')
- prompt_key_grad: bfloat16 [4096, 1024], P(('ctx', 'head'))
- prompt_value_grad: bfloat16 [4096, 1024], P(('ctx', 'head'))
Inputs may be any that keep to these rules, and one draw needn't show every extreme that they name: `resp_len`: at least one response has all 64 rows live. `prompt_end`: at least one response sees the whole prompt.
All inputs are finite; a program needn't handle non-finite values.
Results may differ from a plain program's by a relative error of at most 0.013.
Values may be sent and summed in bfloat16 or wider, within the bound.
No kernel may reach another device: no remote copies, remote signals or barrier semaphores. Data moves between devices by JAX's collectives and lax.ppermute only.
A program may use at most 64 MiB of HBM per device.

v0:
```python
import math

import jax
import jax.numpy as jnp
from jax import lax
from jax.sharding import PartitionSpec as P

DH = 128
RESP_LEN = 64


MASKED_SCORE = -1e30


def combined_all(x, axis, combine):
    everything = jax.tree.map(lambda part: lax.all_gather(part, axis), x)
    initial = jax.tree.map(lambda part: part[0], everything)

    def hop(k, so_far):
        return combine(so_far, jax.tree.map(lambda part: part[k], everything))

    return lax.fori_loop(1, lax.axis_size(axis), hop, initial)


def combine_rows(first_part, second_part):
    higher = jnp.maximum(first_part[0], second_part[0])
    merged_total = first_part[1] * jnp.exp(first_part[0] - higher) + second_part[1] * jnp.exp(
        second_part[0] - higher
    )
    return (higher, merged_total)


def shards(queries, grad_out, outputs, lse_self, prompt_keys, prompt_values, resp_len, prompt_end):
    key_local, value_local = (
        lax.all_to_all(prompt_keys, "head", split_axis=1, concat_axis=0, tiled=True),
        lax.all_to_all(prompt_values, "head", split_axis=1, concat_axis=0, tiled=True),
    )
    own_count = queries.shape[0]
    head_count = queries.shape[1] // DH
    group_count = key_local.shape[1] // DH
    per_group = head_count // group_count
    head_block = math.gcd(per_group, 2)
    block_count = head_count // head_block
    key_count = key_local.shape[0]
    ctx_index = lax.axis_index("ctx")
    own_start = ctx_index * own_count
    score_scale = DH ** (-0.5)
    query_all, grad_all, output_all = (
        lax.all_gather(queries, "ctx", axis=0, tiled=True),
        lax.all_gather(grad_out, "ctx", axis=0, tiled=True),
        lax.all_gather(outputs, "ctx", axis=0, tiled=True),
    )
    row_count = query_all.shape[0]
    row_dots = jnp.einsum(
        "rhd,rhd->rh",
        grad_all.reshape(row_count, head_count, DH),
        output_all.reshape(row_count, head_count, DH),
        preferred_element_type=jnp.float32,
    )
    row_ids = jnp.arange(row_count, dtype=jnp.int32)
    resp_ids = jnp.arange(resp_len.shape[0], dtype=jnp.int32)
    member = (row_ids // RESP_LEN)[:, None] == resp_ids[None, :]
    length_row = jnp.sum(jnp.where(member, resp_len[None, :], 0), axis=1)
    end_row = jnp.sum(jnp.where(member, prompt_end[None, :], 0), axis=1)
    live_rows = (row_ids % RESP_LEN < length_row).astype(jnp.float32)
    key_position = ctx_index * key_count + jnp.arange(key_count, dtype=jnp.int32)
    visible = key_position[None, :] < end_row[:, None]

    def block_scores(block_index):
        head_first = block_index * head_block
        query_block = lax.dynamic_slice_in_dim(
            query_all, head_first * DH, head_block * DH, 1
        ).reshape(row_count, head_block, DH)
        key_group = lax.dynamic_slice_in_dim(key_local, head_first // per_group * DH, DH, 1)
        scores = (
            jnp.einsum("rbd,kd->brk", query_block, key_group, preferred_element_type=jnp.float32)
            * score_scale
        )
        return (head_first, query_block, key_group, scores)

    def stat_step(unused, block_index):
        head_first, query_block, key_group, scores = block_scores(block_index)
        scores = jnp.where(visible[None], scores, MASKED_SCORE)
        block_peak = jnp.max(scores, axis=2)
        block_total = jnp.sum(
            jnp.where(visible[None], jnp.exp(scores - block_peak[:, :, None]), 0.0), axis=2
        )
        return (unused, (block_peak, block_total))

    _, (peaks, totals) = lax.scan(
        stat_step, jnp.zeros((), jnp.float32), jnp.arange(block_count, dtype=jnp.int32)
    )
    row_peak = peaks.reshape(head_count, row_count).T
    row_total = totals.reshape(head_count, row_count).T
    own_peak = lax.dynamic_slice_in_dim(row_peak, own_start, own_count, 0)
    own_total = lax.dynamic_slice_in_dim(row_total, own_start, own_count, 0)
    own_peak, own_total = combine_rows((own_peak, own_total), (lse_self, jnp.ones_like(lse_self)))
    row_peak = lax.dynamic_update_slice_in_dim(row_peak, own_peak, own_start, 0)
    row_total = lax.dynamic_update_slice_in_dim(row_total, own_total, own_start, 0)
    row_peak, row_total = combined_all((row_peak, row_total), "ctx", combine_rows)
    full_lse = row_peak + jnp.log(row_total)

    def grad_step(accums, block_index):
        key_acc, value_acc, query_acc = accums
        head_first, query_block, key_group, scores = block_scores(block_index)
        group_column = head_first // per_group * DH
        value_group = lax.dynamic_slice_in_dim(value_local, group_column, DH, 1)
        grad_block = lax.dynamic_slice_in_dim(
            grad_all, head_first * DH, head_block * DH, 1
        ).reshape(row_count, head_block, DH)
        lse_block = lax.dynamic_slice_in_dim(full_lse, head_first, head_block, 1).T
        dots_block = lax.dynamic_slice_in_dim(row_dots, head_first, head_block, 1).T
        prob = (
            jnp.where(visible[None], jnp.exp(scores - lse_block[:, :, None]), 0.0)
            * live_rows[None, :, None]
        )
        dprob = jnp.einsum(
            "rbd,kd->brk", grad_block, value_group, preferred_element_type=jnp.float32
        )
        dscore = (prob * (dprob - dots_block[:, :, None])).astype(jnp.bfloat16)
        value_add = jnp.einsum(
            "brk,rbd->kd", prob.astype(jnp.bfloat16), grad_block, preferred_element_type=jnp.float32
        )
        key_add = (
            jnp.einsum("brk,rbd->kd", dscore, query_block, preferred_element_type=jnp.float32)
            * score_scale
        )
        key_acc = lax.dynamic_update_slice_in_dim(
            key_acc,
            lax.dynamic_slice_in_dim(key_acc, group_column, DH, 1) + key_add,
            group_column,
            1,
        )
        value_acc = lax.dynamic_update_slice_in_dim(
            value_acc,
            lax.dynamic_slice_in_dim(value_acc, group_column, DH, 1) + value_add,
            group_column,
            1,
        )
        query_add = (
            jnp.einsum("brk,kd->rbd", dscore, key_group, preferred_element_type=jnp.float32)
            * score_scale
        )
        query_acc = lax.dynamic_update_slice_in_dim(
            query_acc, query_add.reshape(row_count, head_block * DH), head_first * DH, 1
        )
        return ((key_acc, value_acc, query_acc), None)

    zero_accums = (
        jnp.zeros((key_count, group_count * DH), jnp.float32),
        jnp.zeros((key_count, group_count * DH), jnp.float32),
        jnp.zeros((row_count, head_count * DH), jnp.float32),
    )
    (key_acc, value_acc, query_acc), _ = lax.scan(
        grad_step, zero_accums, jnp.arange(block_count, dtype=jnp.int32)
    )
    query_grad = lax.psum_scatter(query_acc, "ctx", scatter_dimension=0, tiled=True).astype(
        jnp.bfloat16
    )
    key_grad, value_grad = (
        lax.all_to_all(
            key_acc.astype(jnp.bfloat16), "head", split_axis=0, concat_axis=1, tiled=True
        ),
        lax.all_to_all(
            value_acc.astype(jnp.bfloat16), "head", split_axis=0, concat_axis=1, tiled=True
        ),
    )
    return (query_grad, key_grad, value_grad)


def solution(mesh):
    in_specs = (
        P("ctx", "head"),
        P("ctx", "head"),
        P("ctx", "head"),
        P("ctx", "head"),
        P(("ctx", "head"), None),
        P(("ctx", "head"), None),
        P(),
        P(),
    )
    out_specs = (P("ctx", "head"), P(("ctx", "head"), None), P(("ctx", "head"), None))
    return jax.shard_map(shards, mesh=mesh, in_specs=in_specs, out_specs=out_specs, check_vma=False)
```

profile of v0, /device:TPU:0, one launch (start us, length us, event | category | flops | bytes accessed | tf_op | source)
XLA Modules:
  0.0 470.0 jit_solution(9073103731076810439)
XLA Ops:
  8.6 1.7 copy.127
  10.3 4.2 all-to-all-start
  15.9 1.7 copy.126
  17.6 1.3 dynamic-slice.8
  19.6 31.3 %all-gather.7.cloned.1.call-done = bf16[16,4,8192]{2,1,0:T(4,128)(2,1)} async-done(((bf16[1,4,8192]{2,1,0:T(4,128)(2,1)}), bf16[16,4,8192]{2,1,0:T(4,128)(2,1)}) %all-gather.7.cloned.1.call-update) | async-done | bytes 1048592 | tf_op jit(solution)/shard_map/all_gather | solution.py:49
  50.8 1.3 reshape.110
  52.2 4.1 all-to-all-start.1
  56.4 79.3 %while.50 = (s32[]{:T(128)}, f32[32,2,64]{2,1,0:T(2,128)S(1)}, f32[32,2,64]{2,1,0:T(2,128)S(1)}, s32[32]{0:T(128)S(1)}, bf16[256,512]{1,0:T(8,128)(2,1)S(1)}, /*...) while((s32[]{:T(128)}, f32[32,2,64]{2,1,0:T(2,128)S(1)}, ...), condition=%wide.region_3.4_spmd.clone, body=%wide.region_0.3_spmd.clone.sunk | while | flops 8601370 | bytes 416955 | solution.py:90
  136.4 20.9 %all_gather.31 = f32[16,64,64]{2,1,0:T(8,128)S(1)} all-gather(f32[1,64,64]{2,1,0:T(8,128)S(1)} %copy.79), channel_id=1, replica_groups=mesh['ctx'=16,'head'=2] {'ctx'}, dimensions={0}, use_global_device_ids=true | all-gather | bytes 278528 | tf_op jit(solution)/shard_map/all_gather | solution.py:16
  157.7 19.0 %all_gather.28 = f32[16,64,64]{2,1,0:T(8,128)S(1)} all-gather(f32[1,64,64]{2,1,0:T(8,128)S(1)} %copy.76), channel_id=1, replica_groups=mesh['ctx'=16,'head'=2] {'ctx'}, dimensions={0}, use_global_device_ids=true | all-gather | bytes 278528 | tf_op jit(solution)/shard_map/all_gather | solution.py:16
  177.8 2.1 reshape.107
  180.0 2.2 reshape.108
  183.6 1.1 reshape.112
  185.0 190.5 %while.51 = (s32[]{:T(128)}, f32[256,512]{1,0:T(8,128)S(1)}, f32[256,512]{1,0:T(8,128)S(1)}, f32[64,8192]{1,0:T(8,128)S(1)}, s32[32]{0:T(128)S(1)}, /*index=5*/b...) while((s32[]{:T(128)}, f32[256,512]{1,0:T(8,128)S(1)}, ...), condition=%wide.region_7.8_spmd.clone, body=%wide.region_6.7_spmd.clone.sunk | while | flops 42337308 | bytes 1808420 | solution.py:154
  189.3 1.0 fusion.89
  195.3 1.0 fusion.89
  201.2 1.0 fusion.89
  207.2 1.0 fusion.89
  213.1 1.0 fusion.89
  219.1 1.0 fusion.89
  225.0 1.0 fusion.89
  231.0 1.0 fusion.89
  237.0 1.0 fusion.89
  242.9 1.0 fusion.89
  248.9 1.0 fusion.89
  254.8 1.0 fusion.89
  260.8 1.0 fusion.89
  266.7 1.0 fusion.89
  272.7 1.0 fusion.89
  278.6 1.0 fusion.89
  284.6 1.0 fusion.89
  290.5 1.0 fusion.89
  296.5 1.0 fusion.89
  302.4 1.0 fusion.89
  308.4 1.0 fusion.89
  314.4 1.0 fusion.89
  320.3 1.0 fusion.89
  326.3 1.0 fusion.89
  332.2 1.0 fusion.89
  338.2 1.0 fusion.89
  344.1 1.0 fusion.89
  350.1 1.0 fusion.89
  367.9 1.0 fusion.89
  376.2 3.4 all-to-all-start.2
  379.7 73.4 %all-reduce.2 = bf16[64,8192]{1,0:T(8,128)(2,1)} all-reduce(f32[64,8192]{1,0:T(8,128)S(1)} %get-tuple-element.397), channel_id=2, replica_groups=mesh['ctx'=16,'head'=2] {'ctx'}, use_global_device_ids=true, to_apply=%region_8.9.clone | all-reduce | flops 524288 | bytes 3145728
  453.8 3.4 all-to-all-start.3
  457.3 1.6 dynamic-slice_convert_fusion
  459.9 2.6 all-to-all-done.3
  (548 shorter events, 162.6 us)
Async XLA Ops:
  7.2 43.7 %all-gather.7.cloned.1.call-start = ((), (), s32[]{:S(2)}) async-start(), calls=%async_computation.4 | async-start | bytes 1114112 | tf_op jit(solution)/shard_map/all_gather | solution.py:49
  7.9 169.9 %all-gather.9.cloned.1.call-start = ((), (), s32[]{:S(2)}) async-start(), calls=%async_computation.5 | async-start | bytes 1114112 | tf_op jit(solution)/shard_map/all_gather | solution.py:50
  10.3 41.9 %all-to-all-start = ((bf16[128,2,512]{2,0,1:T(8,128)(2,1)}), bf16[128,2,512]{2,0,1:T(8,128)(2,1)S(1)}, u32[]{:S(2)}, u32[]{:S(2)}) async-start(bf16[128,2,512]{2,0,1:T(8,128)(2,1)} %bitcast.165), calls=%async_computation | async-start | bytes 524288 | tf_op jit(solution)/shard_map/all_to_all | solution.py:35
  14.5 165.5 %all-gather.11.cloned.1.call-start = ((), (), s32[]{:S(2)}) async-start(), calls=%async_computation.6 | async-start | bytes 1114112 | tf_op jit(solution)/shard_map/all_gather | solution.py:51
  52.2 83.7 %copy-start.2 = (f32[4,64]{1,0:T(4,128)S(1)}, f32[4,64]{1,0:T(4,128)}, u32[]{:S(2)}) copy-start(f32[4,64]{1,0:T(4,128)} %param.17) | copy-start | bytes 3076
  52.2 132.5 %all-to-all-start.1 = ((bf16[128,2,512]{2,0,1:T(8,128)(2,1)}), bf16[128,2,512]{2,0,1:T(8,128)(2,1)}, u32[]{:S(2)}, u32[]{:S(2)}) async-start(bf16[128,2,512]{2,0,1:T(8,128)(2,1)} %bitcast.164), calls=%async_computation.1 | async-start | bytes 524288 | tf_op jit(solution)/shard_map/all_to_all | solution.py:36
  135.7 42.1 %copy-start.1 = (bf16[64,8192]{1,0:T(8,128)(2,1)}, bf16[64,8192]{1,0:T(8,128)(2,1)S(1)}, u32[]{:S(2)}) copy-start(bf16[64,8192]{1,0:T(8,128)(2,1)S(1)} %get-tuple-element.872) | copy-start | bytes 3145732
  180.0 3.6 copy-start
  376.2 77.6 %all-to-all-start.2 = ((bf16[2,128,512]{2,1,0:T(8,128)(2,1)}), bf16[2,128,512]{2,1,0:T(8,128)(2,1)S(1)}, u32[]{:S(2)}, u32[]{:S(2)}) async-start(bf16[2,128,512]{2,1,0:T(8,128)(2,1)} %bitcast.24), calls=%async_computation.2 | async-start | bytes 524288 | tf_op jit(solution)/shard_map/all_to_all | solution.py:161
  453.8 8.6 %all-to-all-start.3 = ((bf16[2,128,512]{2,1,0:T(8,128)(2,1)}), bf16[2,128,512]{2,1,0:T(8,128)(2,1)S(1)}, u32[]{:S(2)}, u32[]{:S(2)}) async-start(bf16[2,128,512]{2,1,0:T(8,128)(2,1)} %bitcast.27), calls=%async_computation.3 | async-start | bytes 524288 | tf_op jit(solution)/shard_map/all_to_all | solution.py:164
Sparse Core Ops, SparseCore 0:
  10.2 40.6 all-gather.6
  53.0 36.9 all-gather.8
  92.1 37.0 all-gather.10
where the time goes:
time: 477 us; the launch traced here: 470 us
  blocking collectives  113 us (24%)
  local copies, waits for them, and re-layouts  103 us (22%)
  loops' own time  88.1 us (18%)
  matrix products  64.5 us (14%)
  waiting for transfers between devices  36 us (8%)
  other arithmetic  34.3 us (7%)
  starting transfers between devices  15.3 us (3%)
  between operations  15.3 us (3%)
    unnamed x1, blocking collectives  73.4 us
    another operation x1, loops' own time, shards(): lax.scan(grad_step, zero_accums, jnp.arange(block_count, dtype=jnp.int32))  44.3 us
    another operation x1, loops' own time, shards(): lax.scan(stat_step, jnp.zeros((), jnp.float32), jnp.arange(block_count, d...  43.4 us
    all_gather x2, blocking collectives, combined_all(): everything = jax.tree.map(lambda part: lax.all_gather(part, axis), x)  39.9 us
    dynamic_slice x64, local copies, waits for them, and re-layouts, shards(): lax.scan(stat_step, jnp.zeros((), jnp.float32), jnp.arange(block_count, d...  37.5 us
    dot_general x32, matrix products, grad_step(): jnp.einsum('rbd,kd->brk', grad_block, value_group, preferred_element_type...  32.5 us
    all_gather x1, waiting for transfers between devices, shards(): lax.all_gather(queries, 'ctx', axis=0, tiled=True)  31.3 us
    while x32, local copies, waits for them, and re-layouts  25.2 us
  transfers between devices with their start and end apart: 7, of which 2 were waited for; matrix products, arithmetic and copies ran while one was open for 11% of the time, Pallas kernels for 0%

commit v1 on v0

v1 whole, which is shorter than its diff:
```python
import functools

import jax
import jax.numpy as jnp
from jax import lax
from jax.experimental import pallas as pl
from jax.experimental.pallas import tpu as pltpu
from jax.sharding import Mesh, PartitionSpec as P

DH = 128
KVH = 8
RESP_LEN = 64
SCALE = DH ** (-0.5)
MASKED_SCORE = -1e30
DEAD_LSE = 1e30
PIECES = 3
STAT_ROWS = 16
PARAMS = pltpu.CompilerParams(vmem_limit_bytes=48 * 1024 * 1024)
ANY = pl.BlockSpec(memory_space=pl.ANY)
SMEM = pl.BlockSpec(memory_space=pltpu.SMEM)
VMEM = pl.BlockSpec(memory_space=pltpu.VMEM)


def split_pieces(x):
    first = x.astype(jnp.bfloat16)
    rest = x - first.astype(jnp.float32)
    second = rest.astype(jnp.bfloat16)
    third = (rest - second.astype(jnp.float32)).astype(jnp.bfloat16)
    return first, second, third


def group_of(member, groups, heads):
    return member % heads * groups + member // heads


def pack_kv_kernel(groups, heads, scalars, k_ref, v_ref, *rest):
    out_refs, sems = rest[:-1], rest[-1]
    tokens = k_ref.shape[0]
    copies = []
    for j in range(KVH):
        column = pl.multiple_of(group_of(scalars[0] ^ j, groups, heads) * DH, DH)
        for n, ref in enumerate((k_ref, v_ref)):
            copies.append(
                pltpu.make_async_copy(
                    ref.at[:, pl.ds(column, DH)],
                    out_refs[j].at[pl.ds(n * tokens, tokens), :],
                    sems.at[2 * j + n],
                )
            )
    for copy in copies:
        copy.start()
    for copy in copies:
        copy.wait()


def pack_rows_kernel(parts, groups, q_hbm, o_grad_hbm, o_hbm, lse_hbm, rows_ref, q_ref, o_grad_ref, o_ref, lse_ref, sems):
    copies = [
        pltpu.make_async_copy(source, target, sems.at[n])
        for n, (source, target) in enumerate(
            ((lse_hbm, lse_ref), (q_hbm, q_ref), (o_grad_hbm, o_grad_ref), (o_hbm, o_ref))
        )
    ]
    for copy in copies:
        copy.start()
    group_lines = q_ref.shape[0] // groups
    rows = lse_ref.shape[0]
    group_heads = group_lines // rows
    head_ids = lax.broadcasted_iota(jnp.int32, (lse_ref.shape[1], 2 * group_lines), 0)
    line_ids = lax.broadcasted_iota(jnp.int32, (lse_ref.shape[1], 2 * group_lines), 1) % group_lines
    row_ids = lax.broadcasted_iota(jnp.int32, (rows, 2 * group_lines), 0)
    row_of_line = lax.broadcasted_iota(jnp.int32, (rows, 2 * group_lines), 1) % rows
    for copy in copies:
        copy.wait()
    lse_pieces = [piece.astype(jnp.float32) for piece in split_pieces(lse_ref[...])]
    for g in range(groups):
        lines = pl.ds(g * group_lines, group_lines)
        q = q_ref[lines, :]
        o_grad = o_grad_ref[lines, :]
        product = o_grad.astype(jnp.float32) * o_ref[lines, :].astype(jnp.float32)
        dots = jnp.sum(jnp.concatenate([product, product], axis=0).T, axis=0, keepdims=True)
        chosen = (head_ids == g * group_heads + line_ids // rows).astype(jnp.float32)
        stats = []
        for piece in lse_pieces:
            spread = jnp.dot(piece, chosen, preferred_element_type=jnp.float32)
            stats.append(
                jnp.sum(jnp.where(row_ids == row_of_line, spread, 0.0), axis=0, keepdims=True)
            )
        stats += [piece.astype(jnp.float32) for piece in split_pieces(dots)]
        stats.append(jnp.zeros((STAT_ROWS - 2 * PIECES, 2 * group_lines), jnp.float32))
        stat_block = jnp.concatenate(stats, axis=0).astype(jnp.bfloat16)
        for part in range(parts):
            rows_ref[part * groups + g, 0:group_lines, :] = q
            rows_ref[part * groups + g, group_lines : 2 * group_lines, :] = o_grad
            rows_ref[part * groups + g, 2 * group_lines :, :] = stat_block


def line_limits(first_line, count, lines, rows, resp_len, prompt_end):
    line = first_line + lax.broadcasted_iota(jnp.int32, (1, count), 1)
    row = line // lines * rows + line % rows
    resp = row // RESP_LEN
    end = jnp.zeros_like(line)
    length = jnp.zeros_like(line)
    for r in range(resp_len.shape[0]):
        end = jnp.where(resp == r, prompt_end[r], end)
        length = jnp.where(resp == r, resp_len[r], length)
    return end, row % RESP_LEN < length


def line_values(rows_ref, first_source, count, lines, first_piece):
    low = lax.broadcasted_iota(jnp.int32, (1, 2 * lines), 1) < lines
    out = []
    for s in range(first_source, first_source + count, 2):
        total = None
        for k in range(first_piece, first_piece + PIECES):
            even = rows_ref[s, 2 * lines : 2 * lines + STAT_ROWS, :].astype(jnp.float32)[k : k + 1]
            odd = rows_ref[s + 1, 2 * lines : 2 * lines + STAT_ROWS, :].astype(jnp.float32)[k : k + 1]
            piece = jnp.where(low, even, odd)
            total = piece if total is None else total + piece
        out.append(total)
    return jnp.concatenate(out, axis=1)


def stat_kernel(rows, tokens, scalars, resp_len, prompt_end, rows_ref, *rest):
    kv_refs, lse_ref = rest[:-1], rest[-1]
    sources, lines = rows_ref.shape[0], (rows_ref.shape[1] - STAT_ROWS) // 2
    step = 256 // lines
    for c in range(sources // step):
        q = rows_ref[c * step : (c + 1) * step, 0:lines, :].reshape(step * lines, DH)
        end, _ = line_limits(c * step * lines, step * lines, lines, rows, resp_len, prompt_end)
        scores = []
        for j, ref in enumerate(kv_refs):
            part = lax.dot_general(
                ref[0:tokens, :], q, (((1,), (1,)), ((), ())), preferred_element_type=jnp.float32
            )
            offset = lax.broadcasted_iota(jnp.int32, part.shape, 0)
            visible = offset < end - scalars[1 + j]
            scores.append(jnp.where(visible, part * SCALE, MASKED_SCORE))
        scores = jnp.concatenate(scores, axis=0)
        peak = jnp.max(scores, axis=0, keepdims=True)
        total = jnp.sum(jnp.exp(scores - peak), axis=0, keepdims=True)
        lse = peak + jnp.log(total)
        for n in range(step * lines // DH):
            lse_ref[c * (step * lines // DH) + n, :] = lse[0, n * DH : (n + 1) * DH]


def grad_kernel(parts, rows, tokens, scalars, resp_len, prompt_end, rows_ref, *rest):
    kv_refs, lse_refs = rest[:KVH], rest[KVH : KVH + parts]
    dq_ref, dkv_refs = rest[KVH + parts], rest[KVH + parts + 1 : KVH + parts + 1 + KVH]
    dk_acc, dv_acc = rest[-2:]
    sources, lines = rows_ref.shape[0], (rows_ref.shape[1] - STAT_ROWS) // 2
    step = min(sources, 1024 // lines)
    count = step * lines
    pair = 2
    for c in range(sources // step):
        q = rows_ref[c * step : (c + 1) * step, 0:lines, :].reshape(count, DH)
        o_grad = rows_ref[c * step : (c + 1) * step, lines : 2 * lines, :].reshape(count, DH)
        end, live = line_limits(c * count, count, lines, rows, resp_len, prompt_end)
        dots = line_values(rows_ref, c * step, step, lines, PIECES)
        self_lse = line_values(rows_ref, c * step, step, lines, 0)
        tiles = range(c * count // DH, (c + 1) * count // DH)
        part_lse = [
            jnp.concatenate([ref[n : n + 1, :] for n in tiles], axis=1) for ref in lse_refs
        ]
        peak = functools.reduce(jnp.maximum, part_lse, self_lse)
        total = sum(jnp.exp(x - peak) for x in part_lse) + jnp.exp(self_lse - peak)
        lse = jnp.where(live, peak + jnp.log(total), DEAD_LSE)
        dq_t = jnp.zeros((DH, count), jnp.float32)
        for b in range(0, KVH, pair):
            blocks = range(b, b + pair)
            k = jnp.concatenate([kv_refs[j][0:tokens, :] for j in blocks], axis=0)
            v = jnp.concatenate([kv_refs[j][tokens:, :] for j in blocks], axis=0)
            scores = lax.dot_general(
                k, q, (((1,), (1,)), ((), ())), preferred_element_type=jnp.float32
            )
            offset = lax.broadcasted_iota(jnp.int32, (tokens, count), 0)
            visible = jnp.concatenate([offset < end - scalars[1 + j] for j in blocks], axis=0)
            prob = jnp.where(visible, jnp.exp(scores * SCALE - lse), 0.0)
            dprob = lax.dot_general(
                v, o_grad, (((1,), (1,)), ((), ())), preferred_element_type=jnp.float32
            )
            dscore = (prob * (dprob - dots)).astype(jnp.bfloat16)
            dv = jnp.dot(prob.astype(jnp.bfloat16), o_grad, preferred_element_type=jnp.float32)
            dk = jnp.dot(dscore, q, preferred_element_type=jnp.float32) * SCALE
            dq_t = dq_t + jnp.dot(k.T, dscore, preferred_element_type=jnp.float32)
            held = slice(b * tokens, (b + pair) * tokens)
            if c > 0:
                dk = dk + dk_acc[held, :]
                dv = dv + dv_acc[held, :]
            if c < sources // step - 1:
                dk_acc[held, :] = dk
                dv_acc[held, :] = dv
            else:
                for n, j in enumerate(blocks):
                    inner = slice(n * tokens, (n + 1) * tokens)
                    dkv_refs[j][0:tokens, :] = dk[inner].astype(jnp.bfloat16)
                    dkv_refs[j][tokens:, :] = dv[inner].astype(jnp.bfloat16)
        dq_ref[c * step : (c + 1) * step] = (
            (dq_t * SCALE).T.astype(jnp.bfloat16).reshape(step, lines, DH)
        )


def unpack_kernel(parts, groups, heads, scalars, dq_ref, *rest):
    dkv_refs, (out_q_ref, out_k_ref, out_v_ref) = rest[:KVH], rest[KVH:]
    lines = dq_ref.shape[1]
    tokens = out_k_ref.shape[0]
    for g in range(groups):
        total = dq_ref[g].astype(jnp.float32)
        for part in range(1, parts):
            total = total + dq_ref[part * groups + g].astype(jnp.float32)
        out_q_ref[g * lines : (g + 1) * lines, :] = total.astype(jnp.bfloat16)
    for j, ref in enumerate(dkv_refs):
        column = pl.multiple_of(group_of(scalars[0] ^ j, groups, heads) * DH, DH)
        out_k_ref[:, pl.ds(column, DH)] = ref[0:tokens, :]
        out_v_ref[:, pl.ds(column, DH)] = ref[tokens:, :]


def swap_with_peers(blocks):
    return [blocks[0]] + [
        lax.ppermute(blocks[j], ("group", "head"), [(i, i ^ j) for i in range(KVH)])
        for j in range(1, KVH)
    ]


def shards(parts, groups, heads, queries, grad_out, outputs, lse_self, keys, values, resp_len, prompt_end):
    rows = queries.shape[0]
    own_heads = queries.shape[1] // DH
    own_lines = rows * own_heads
    lines = own_lines // groups
    tokens = keys.shape[0]
    sources = parts * groups
    tiles = sources * lines // DH
    member = lax.axis_index("group") * heads + lax.axis_index("head")
    peers = member ^ jnp.arange(KVH, dtype=jnp.int32)
    starts = (lax.axis_index("part") * KVH + peers) * tokens
    scalars = jnp.concatenate([member.reshape(1), starts]).astype(jnp.int32)
    kv_shape = jax.ShapeDtypeStruct((2 * tokens, DH), jnp.bfloat16)

    def as_lines(x):
        return x.reshape(rows, own_heads, DH).transpose(1, 0, 2).reshape(own_lines, DH)

    kv_blocks = pl.pallas_call(
        functools.partial(pack_kv_kernel, groups, heads),
        in_specs=[SMEM, ANY, ANY],
        out_shape=[kv_shape] * KVH,
        scratch_shapes=[pltpu.SemaphoreType.DMA((2 * KVH,))],
        compiler_params=PARAMS,
    )(scalars, keys, values)
    kv_blocks = swap_with_peers(kv_blocks)
    row_block = pl.pallas_call(
        functools.partial(pack_rows_kernel, parts, groups),
        in_specs=[ANY] * 4,
        out_shape=jax.ShapeDtypeStruct((sources, 2 * lines + STAT_ROWS, DH), jnp.bfloat16),
        scratch_shapes=[pltpu.VMEM((own_lines, DH), jnp.bfloat16)] * 3
        + [pltpu.VMEM(lse_self.shape, jnp.float32), pltpu.SemaphoreType.DMA((4,))],
        compiler_params=PARAMS,
    )(as_lines(queries), as_lines(grad_out), as_lines(outputs), lse_self)
    row_block = lax.all_to_all(
        row_block, ("part", "group"), split_axis=0, concat_axis=0, tiled=True
    )

    part_lse = pl.pallas_call(
        functools.partial(stat_kernel, rows, tokens),
        in_specs=[SMEM] * 3 + [VMEM] * (1 + KVH),
        out_shape=jax.ShapeDtypeStruct((tiles, DH), jnp.float32),
        compiler_params=PARAMS,
    )(scalars, resp_len, prompt_end, row_block, *kv_blocks)
    every_lse = [part_lse] + [
        lax.ppermute(part_lse, "part", [(i, (i + j) % parts) for i in range(parts)])
        for j in range(1, parts)
    ]

    dq, *dkv_blocks = pl.pallas_call(
        functools.partial(grad_kernel, parts, rows, tokens),
        in_specs=[SMEM] * 3 + [VMEM] * (1 + KVH + parts),
        out_shape=[jax.ShapeDtypeStruct((sources, lines, DH), jnp.bfloat16)] + [kv_shape] * KVH,
        scratch_shapes=[pltpu.VMEM((KVH * tokens, DH), jnp.float32)] * 2,
        compiler_params=PARAMS,
    )(scalars, resp_len, prompt_end, row_block, *kv_blocks, *every_lse)
    dkv_blocks = swap_with_peers(dkv_blocks)
    dq = lax.all_to_all(dq, ("part", "group"), split_axis=0, concat_axis=0, tiled=True)
    out_q, out_k, out_v = pl.pallas_call(
        functools.partial(unpack_kernel, parts, groups, heads),
        in_specs=[SMEM] + [VMEM] * (1 + KVH),
        out_shape=[
            jax.ShapeDtypeStruct((own_lines, DH), jnp.bfloat16),
            jax.ShapeDtypeStruct(keys.shape, jnp.bfloat16),
            jax.ShapeDtypeStruct(values.shape, jnp.bfloat16),
        ],
        compiler_params=PARAMS,
    )(scalars, dq, *dkv_blocks)
    out_q = out_q.reshape(own_heads, rows, DH).transpose(1, 0, 2).reshape(rows, own_heads * DH)
    return out_q, out_k, out_v


def solution(mesh):
    ctx, heads = mesh.shape["ctx"], mesh.shape["head"]
    groups = KVH // heads
    parts = ctx // groups
    fine = Mesh(mesh.devices.reshape(parts, groups, heads), ("part", "group", "head"))
    rows = P(("part", "group"), "head")
    tokens = P(("part", "group", "head"), None)
    return jax.shard_map(
        functools.partial(shards, parts, groups, heads),
        mesh=fine,
        in_specs=(rows, rows, rows, rows, tokens, tokens, P(), P()),
        out_specs=(rows, tokens, tokens),
        check_vma=False,
    )
```

time: 477 us -> 61.1 us (0.13); the launches traced: 470 us -> 60.6 us
  blocking collectives: 113 us -> 0 us
  local copies, waits for them, and re-layouts: 103 us -> 3.2 us
  loops' own time: 88.1 us -> 0 us
  matrix products: 64.5 us -> 0 us
  other arithmetic: 34.3 us -> 0.08 us
  waiting for transfers between devices: 36 us -> 13.8 us
  starting transfers between devices: 15.3 us -> 31 us
  between operations: 15.3 us -> 2.03 us
  Pallas kernels: 0 us -> 10.5 us
    another operation x3 -> x0, loops' own time: 88.1 us -> none  [the longest x1 44.3 us: shards(): lax.scan(grad_step, zero_accums, jnp.arange(block_count, dtype=jnp.int32))]
    unnamed x1 -> x0, blocking collectives: 73.4 us -> none
    dot_general x192 -> x0, matrix products: 64.5 us -> none  [the longest x32 32.5 us: grad_step(): jnp.einsum('rbd,kd->brk', grad_block, value_group, preferred_element_type...]
    all_gather x2 -> x0, blocking collectives: 39.9 us -> none  [combined_all(): everything = jax.tree.map(lambda part: lax.all_gather(part, axis), x)]
    dynamic_slice x64 -> x0, local copies, waits for them, and re-layouts: 37.5 us -> none  [shards(): lax.scan(stat_step, jnp.zeros((), jnp.float32), jnp.arange(block_count, d...]
    all_gather x3 -> x0, waiting for transfers between devices: 31.3 us -> none  [the longest x1 31.3 us: shards(): lax.all_gather(queries, 'ctx', axis=0, tiled=True)]
    while x34 -> x0, local copies, waits for them, and re-layouts: 25.4 us -> none
    convert_element_type x34 -> x0, other arithmetic: 22.3 us -> none  [the longest x32 20.9 us: shards(): live_rows = (row_ids % RESP_LEN < length_row).astype(jnp.float32)]
  transfers between devices with their start and end apart: 7 -> 19, of which waited for: 2 -> 8; matrix products, arithmetic and copies ran while one was open for 11% -> 0% of each run, Pallas kernels for 0% -> 2%
where the time goes in v1:
time: 61.1 us; the launch traced here: 60.6 us
  starting transfers between devices  31 us (51%)
  waiting for transfers between devices  13.8 us (23%)
  Pallas kernels  10.5 us (17%)
  local copies, waits for them, and re-layouts  3.2 us (5%)
  between operations  2.03 us (3%)
    ppermute x14, starting transfers between devices, swap_with_peers(): lax.ppermute(blocks[j], ('group', 'head'), [(i, i ^ j) for i in range(KVH)])  15.3 us
    ppermute x14, waiting for transfers between devices, swap_with_peers(): lax.ppermute(blocks[j], ('group', 'head'), [(i, i ^ j) for i in range(KVH)])  8.81 us
    all_to_all x1, starting transfers between devices, shards(): lax.all_to_all(row_block, ('part', 'group'), split_axis=0, concat_axis=0,...  7.53 us
    ppermute x3, starting transfers between devices, shards(): lax.ppermute(part_lse, 'part', [(i, (i + j) % parts) for i in range(parts)])  4.66 us
    pallas_call x1, Pallas kernels, shards(): pl.pallas_call(functools.partial(grad_kernel, parts, rows, tokens), in_sp...  4.48 us
    ppermute x3, waiting for transfers between devices, shards(): lax.ppermute(part_lse, 'part', [(i, (i + j) % parts) for i in range(parts)])  3.75 us
    all_to_all x1, starting transfers between devices, shards(): lax.all_to_all(dq, ('part', 'group'), split_axis=0, concat_axis=0, tiled=...  3.53 us
    unnamed x12, local copies, waits for them, and re-layouts  3.2 us
  transfers between devices with their start and end apart: 19, of which 8 were waited for; matrix products, arithmetic and copies ran while one was open for 0% of the time, Pallas kernels for 2%

profile of v1, /device:TPU:0, one launch (start us, length us, event | category | flops | bytes accessed | tf_op | source)
XLA Modules:
  0.0 60.6 jit_solution(12929536134271982737)
XLA Ops:
  0.6 0.7 %copy-done.5 = f32[4,64]{1,0:T(4,128)S(1)} copy-done((f32[4,64]{1,0:T(4,128)S(1)}, f32[4,64]{1,0:T(4,128)}, u32[]{:S(2)}) %copy-start.5) | copy-done | bytes 1048
  1.3 0.8 %copy-done.2 = bf16[4,8192]{1,0:T(4,128)(2,1)S(1)} copy-done((bf16[4,8192]{1,0:T(4,128)(2,1)S(1)}, bf16[4,8192]{1,0:T(4,128)(2,1)}, u32[]{:S(2)}) %copy-start.2) | copy-done | bytes 65560
  2.2 0.8 %copy-done.3 = bf16[4,8192]{1,0:T(4,128)(2,1)S(1)} copy-done((bf16[4,8192]{1,0:T(4,128)(2,1)S(1)}, bf16[4,8192]{1,0:T(4,128)(2,1)}, u32[]{:S(2)}) %copy-start.3) | copy-done | bytes 65560
  3.0 0.8 %copy-done.4 = bf16[4,8192]{1,0:T(4,128)(2,1)S(1)} copy-done((bf16[4,8192]{1,0:T(4,128)(2,1)S(1)}, bf16[4,8192]{1,0:T(4,128)(2,1)}, u32[]{:S(2)}) %copy-start.4) | copy-done | bytes 65560
  3.8 1.3 %shard_map.103 = bf16[16,144,128]{2,1,0:T(8,128)(2,1)} custom-call(bf16[256,128]{1,0:T(8,128)(2,1)S(1)} %bitcast.21, bf16[256,128]{1,0:T(8,128)(2,1)S(1)} %bitcast.22, bf16[256,128]{1,0:T(8,128)(2,1)S(1)} %bitcast.23, f32[4,64]{1,0:T(4,128)S(1)} %copy-done.5), custom_call_target="tpu_custom_call" | custom-call | tf_op jit(solution)/shard_map/pallas_call | solution.py:249
  5.1 0.0 copy-start
  5.1 0.0 copy-start.1
  5.2 7.5 %all-to-all-start = ((bf16[16,144,128]{2,1,0:T(8,128)(2,1)}), bf16[16,144,128]{2,1,0:T(8,128)(2,1)S(1)}, u32[]{:S(2)}, u32[]{:S(2)}) async-start(bf16[16,144,128]{2,1,0:T(8,128)(2,1)} %shard_map.103), calls=%async_computation | async-start | bytes 1179648 | tf_op jit(solution)/shard_map/all_to_all | solution.py:257
  12.7 0.1 pad_add_fusion.scalars
  12.8 0.9 %shard_map.104 = (bf16[256,128]{1,0:T(8,128)(2,1)S(1)}, bf16[256,128]{1,0:T(8,128)(2,1)S(1)}, bf16[256,128]{1,0:T(8,128)(2,1)S(1)}, bf16[256,128]{1,0:T(8,128)(2...) custom-call(s32[9]{0:T(128)S(1)} %pad_add_fusion.scalars, ...), custom_call_target="tpu_custom_call" | custom-call | tf_op jit(solution)/shard_map/pallas_call | solution.py:241
  13.7 1.6 %collective-permute-start = (bf16[256,128]{1,0:T(8,128)(2,1)S(1)}, bf16[256,128]{1,0:T(8,128)(2,1)S(1)}, u32[]{:S(2)}, u32[]{:S(2)}) collective-permute-start(bf16[256,128]{1,0:T(8,128)(2,1)S(1)} %get-tuple-element.24), channel_id=1, source_target_pairs={{0,1},{1,0},{2,3},{3,2},{4,5},{5,4},{6,7},{7,6},{8,9},{9,8},{10,11... | collective-permute-start | bytes 196616 | tf_op jit(solution)/shard_map/ppermute | solution.py:219
  15.3 0.1 collective-permute-start.1
  15.4 0.5 collective-permute-start.2
  15.9 1.9 %collective-permute-start.3 = (bf16[256,128]{1,0:T(8,128)(2,1)S(1)}, bf16[256,128]{1,0:T(8,128)(2,1)S(1)}, u32[]{:S(2)}, u32[]{:S(2)}) collective-permute-start(bf16[256,128]{1,0:T(8,128)(2,1)S(1)} %get-tuple-element.27), channel_id=1, source_target_pairs={{0,4},{1,5},{2,6},{3,7},{4,0},{5,1},{6,2},{7,3},{8,12},{9,13},{10,... | collective-permute-start | bytes 196616 | tf_op jit(solution)/shard_map/ppermute | solution.py:219
  17.9 1.0 %collective-permute-start.4 = (bf16[256,128]{1,0:T(8,128)(2,1)S(1)}, bf16[256,128]{1,0:T(8,128)(2,1)S(1)}, u32[]{:S(2)}, u32[]{:S(2)}) collective-permute-start(bf16[256,128]{1,0:T(8,128)(2,1)S(1)} %get-tuple-element.28), channel_id=1, source_target_pairs={{0,5},{1,4},{2,7},{3,6},{4,1},{5,0},{6,3},{7,2},{8,13},{9,12},{10,... | collective-permute-start | bytes 196616 | tf_op jit(solution)/shard_map/ppermute | solution.py:219
  18.9 0.0 collective-permute-done.rest_1_
  18.9 1.0 %collective-permute-start.5 = (bf16[256,128]{1,0:T(8,128)(2,1)S(1)}, bf16[256,128]{1,0:T(8,128)(2,1)S(1)}, u32[]{:S(2)}, u32[]{:S(2)}) collective-permute-start(bf16[256,128]{1,0:T(8,128)(2,1)S(1)} %get-tuple-element.29), channel_id=1, source_target_pairs={{0,6},{1,7},{2,4},{3,5},{4,2},{5,3},{6,0},{7,1},{8,14},{9,15},{10,... | collective-permute-start | bytes 196616 | tf_op jit(solution)/shard_map/ppermute | solution.py:219
  19.9 0.0 collective-permute-done.1.rest_2_
  19.9 1.5 %collective-permute-start.6 = (bf16[256,128]{1,0:T(8,128)(2,1)S(1)}, bf16[256,128]{1,0:T(8,128)(2,1)S(1)}, u32[]{:S(2)}, u32[]{:S(2)}) collective-permute-start(bf16[256,128]{1,0:T(8,128)(2,1)S(1)} %get-tuple-element.30), channel_id=1, source_target_pairs={{0,7},{1,6},{2,5},{3,4},{4,3},{5,2},{6,1},{7,0},{8,15},{9,14},{10,... | collective-permute-start | bytes 196616 | tf_op jit(solution)/shard_map/ppermute | solution.py:219
  22.7 0.0 collective-permute-done.2.rest_3_
  22.7 2.7 %collective-permute-done.3.rest_4_ = bf16[256,128]{1,0:T(8,128)(2,1)S(1)} collective-permute-done((bf16[256,128]{1,0:T(8,128)(2,1)S(1)}, bf16[256,128]{1,0:T(8,128)(2,1)S(1)}, u32[]{:S(2)}, u32[]{:S(2)}) %collective-permute-start.3) | collective-permute-done | bytes 65568 | tf_op jit(solution)/shard_map/ppermute | solution.py:219
  25.4 0.0 collective-permute-done.4.rest_5_
  25.4 1.6 %collective-permute-done.5.rest_6_ = bf16[256,128]{1,0:T(8,128)(2,1)S(1)} collective-permute-done((bf16[256,128]{1,0:T(8,128)(2,1)S(1)}, bf16[256,128]{1,0:T(8,128)(2,1)S(1)}, u32[]{:S(2)}, u32[]{:S(2)}) %collective-permute-start.5) | collective-permute-done | bytes 65568 | tf_op jit(solution)/shard_map/ppermute | solution.py:219
  27.0 0.0 collective-permute-done.6.rest_7_
  27.0 1.2 %all-to-all-done.rows_ref = bf16[16,144,128]{2,1,0:T(8,128)(2,1)S(1)} async-done(((bf16[16,144,128]{2,1,0:T(8,128)(2,1)}), bf16[16,144,128]{2,1,0:T(8,128)(2,1)S(1)}, u32[]{:S(2)}, u32[]{:S(2)}) %all-to-all-start) | async-done | bytes 589856 | tf_op jit(solution)/shard_map/all_to_all | solution.py:257
  28.2 2.3 %shard_map.105.rest_8_ = f32[8,128]{1,0:T(8,128)S(1)} custom-call(s32[9]{0:T(128)S(1)} %pad_add_fusion.scalars, s32[1]{0:T(128)S(6)} %copy.15.resp_len, s32[1]{0:T(128)S(6)} %copy.16.prompt_end, bf16[16,144,128]{2,1,0:T(8,128)(2,1)S(1)} %all-to-all-done.rows_ref, bf16[256,128]{1,0:T(8,128)(2,1)S(1)} %get-tuple-element.23.rest_0_, ...), custom_call_target="tpu_custom_call" | custom-call | tf_op jit(solution)/shard_map/pallas_call | solution.py:261
  30.5 2.5 %collective-permute-start.9 = (f32[8,128]{1,0:T(8,128)S(1)}, f32[8,128]{1,0:T(8,128)S(1)}, u32[]{:S(2)}, u32[]{:S(2)}) collective-permute-start(f32[8,128]{1,0:T(8,128)S(1)} %shard_map.105.rest_8_), channel_id=1, source_target_pairs={{0,24},{8,0},{16,8},{24,16},{1,25},{9,1},{17,9},{25,17},{2,26},{10... | collective-permute-start | bytes 12296 | tf_op jit(solution)/shard_map/ppermute | solution.py:268
  33.0 0.5 collective-permute-start.8
  33.5 1.7 %collective-permute-start.7 = (f32[8,128]{1,0:T(8,128)S(1)}, f32[8,128]{1,0:T(8,128)S(1)}, u32[]{:S(2)}, u32[]{:S(2)}) collective-permute-start(f32[8,128]{1,0:T(8,128)S(1)} %shard_map.105.rest_8_), channel_id=1, source_target_pairs={{0,8},{8,16},{16,24},{24,0},{1,9},{9,17},{17,25},{25,1},{2,10},{10... | collective-permute-start | bytes 12296 | tf_op jit(solution)/shard_map/ppermute | solution.py:268
  35.2 0.0 collective-permute-done.9.rest_11_
  35.2 2.3 %collective-permute-done.8.rest_10_ = f32[8,128]{1,0:T(8,128)S(1)} collective-permute-done((f32[8,128]{1,0:T(8,128)S(1)}, f32[8,128]{1,0:T(8,128)S(1)}, u32[]{:S(2)}, u32[]{:S(2)}) %collective-permute-start.8) | collective-permute-done | bytes 4128 | tf_op jit(solution)/shard_map/ppermute | solution.py:268
  37.5 1.4 %collective-permute-done.7.rest_9_ = f32[8,128]{1,0:T(8,128)S(1)} collective-permute-done((f32[8,128]{1,0:T(8,128)S(1)}, f32[8,128]{1,0:T(8,128)S(1)}, u32[]{:S(2)}, u32[]{:S(2)}) %collective-permute-start.7) | collective-permute-done | bytes 4128 | tf_op jit(solution)/shard_map/ppermute | solution.py:268
  38.9 4.5 %shard_map.106 = (bf16[16,64,128]{2,1,0:T(8,128)(2,1)}, bf16[256,128]{1,0:T(8,128)(2,1)S(1)}, bf16[256,128]{1,0:T(8,128)(2,1)S(1)}, bf16[256,128]{1,0:T(8,128)(2...) custom-call(s32[9]{0:T(128)S(1)} %pad_add_fusion.scalars, ...), custom_call_target="tpu_custom_call" | custom-call | tf_op jit(solution)/shard_map/pallas_call | solution.py:272
  43.4 3.5 %all-to-all-start.1 = ((bf16[16,64,128]{2,1,0:T(8,128)(2,1)}), bf16[16,64,128]{2,1,0:T(8,128)(2,1)S(1)}, u32[]{:S(2)}, u32[]{:S(2)}) async-start(bf16[16,64,128]{2,1,0:T(8,128)(2,1)} %get-tuple-element.31), calls=%async_computation.1 | async-start | bytes 524288 | tf_op jit(solution)/shard_map/all_to_all | solution.py:280
  46.9 1.5 %collective-permute-start.10 = (bf16[256,128]{1,0:T(8,128)(2,1)S(1)}, bf16[256,128]{1,0:T(8,128)(2,1)S(1)}, u32[]{:S(2)}, u32[]{:S(2)}) collective-permute-start(bf16[256,128]{1,0:T(8,128)(2,1)S(1)} %get-tuple-element.33), channel_id=1, source_target_pairs={{0,1},{1,0},{2,3},{3,2},{4,5},{5,4},{6,7},{7,6},{8,9},{9,8},{10,11... | collective-permute-start | bytes 196616 | tf_op jit(solution)/shard_map/ppermute | solution.py:219
  48.5 0.0 collective-permute-start.11
  48.5 0.7 %collective-permute-start.12 = (bf16[256,128]{1,0:T(8,128)(2,1)S(1)}, bf16[256,128]{1,0:T(8,128)(2,1)S(1)}, u32[]{:S(2)}, u32[]{:S(2)}) collective-permute-start(bf16[256,128]{1,0:T(8,128)(2,1)S(1)} %get-tuple-element.35), channel_id=1, source_target_pairs={{0,3},{1,2},{2,1},{3,0},{4,7},{5,6},{6,5},{7,4},{8,11},{9,10},{10,... | collective-permute-start | bytes 196616 | tf_op jit(solution)/shard_map/ppermute | solution.py:219
  49.1 1.7 %collective-permute-start.13 = (bf16[256,128]{1,0:T(8,128)(2,1)S(1)}, bf16[256,128]{1,0:T(8,128)(2,1)S(1)}, u32[]{:S(2)}, u32[]{:S(2)}) collective-permute-start(bf16[256,128]{1,0:T(8,128)(2,1)S(1)} %get-tuple-element.36), channel_id=1, source_target_pairs={{0,4},{1,5},{2,6},{3,7},{4,0},{5,1},{6,2},{7,3},{8,12},{9,13},{10,... | collective-permute-start | bytes 196616 | tf_op jit(solution)/shard_map/ppermute | solution.py:219
  50.9 1.2 %collective-permute-start.14 = (bf16[256,128]{1,0:T(8,128)(2,1)S(1)}, bf16[256,128]{1,0:T(8,128)(2,1)S(1)}, u32[]{:S(2)}, u32[]{:S(2)}) collective-permute-start(bf16[256,128]{1,0:T(8,128)(2,1)S(1)} %get-tuple-element.37), channel_id=1, source_target_pairs={{0,5},{1,4},{2,7},{3,6},{4,1},{5,0},{6,3},{7,2},{8,13},{9,12},{10,... | collective-permute-start | bytes 196616 | tf_op jit(solution)/shard_map/ppermute | solution.py:219
  52.1 0.0 collective-permute-done.10.rest_1_
  52.1 0.8 %collective-permute-start.15 = (bf16[256,128]{1,0:T(8,128)(2,1)S(1)}, bf16[256,128]{1,0:T(8,128)(2,1)S(1)}, u32[]{:S(2)}, u32[]{:S(2)}) collective-permute-start(bf16[256,128]{1,0:T(8,128)(2,1)S(1)} %get-tuple-element.38), channel_id=1, source_target_pairs={{0,6},{1,7},{2,4},{3,5},{4,2},{5,3},{6,0},{7,1},{8,14},{9,15},{10,... | collective-permute-start | bytes 196616 | tf_op jit(solution)/shard_map/ppermute | solution.py:219
  52.9 0.0 collective-permute-done.11.rest_2_
  52.9 1.7 %collective-permute-start.16 = (bf16[256,128]{1,0:T(8,128)(2,1)S(1)}, bf16[256,128]{1,0:T(8,128)(2,1)S(1)}, u32[]{:S(2)}, u32[]{:S(2)}) collective-permute-start(bf16[256,128]{1,0:T(8,128)(2,1)S(1)} %get-tuple-element.39), channel_id=1, source_target_pairs={{0,7},{1,6},{2,5},{3,4},{4,3},{5,2},{6,1},{7,0},{8,15},{9,14},{10,... | collective-permute-start | bytes 196616 | tf_op jit(solution)/shard_map/ppermute | solution.py:219
  54.6 0.0 collective-permute-done.12.rest_3_
  54.6 0.7 %collective-permute-done.13.rest_4_ = bf16[256,128]{1,0:T(8,128)(2,1)S(1)} collective-permute-done((bf16[256,128]{1,0:T(8,128)(2,1)S(1)}, bf16[256,128]{1,0:T(8,128)(2,1)S(1)}, u32[]{:S(2)}, u32[]{:S(2)}) %collective-permute-start.13) | collective-permute-done | bytes 65568 | tf_op jit(solution)/shard_map/ppermute | solution.py:219
  55.3 0.9 %collective-permute-done.14.rest_5_ = bf16[256,128]{1,0:T(8,128)(2,1)S(1)} collective-permute-done((bf16[256,128]{1,0:T(8,128)(2,1)S(1)}, bf16[256,128]{1,0:T(8,128)(2,1)S(1)}, u32[]{:S(2)}, u32[]{:S(2)}) %collective-permute-start.14) | collective-permute-done | bytes 65568 | tf_op jit(solution)/shard_map/ppermute | solution.py:219
  56.2 2.9 %collective-permute-done.15.rest_6_ = bf16[256,128]{1,0:T(8,128)(2,1)S(1)} collective-permute-done((bf16[256,128]{1,0:T(8,128)(2,1)S(1)}, bf16[256,128]{1,0:T(8,128)(2,1)S(1)}, u32[]{:S(2)}, u32[]{:S(2)}) %collective-permute-start.15) | collective-permute-done | bytes 65568 | tf_op jit(solution)/shard_map/ppermute | solution.py:219
  59.1 1.5 %shard_map.107 = (bf16[256,128]{1,0:T(8,128)(2,1)}, bf16[128,1024]{1,0:T(8,128)(2,1)}, bf16[128,1024]{1,0:T(8,128)(2,1)}) custom-call(s32[9]{0:T(128)S(1)} %pad_add_fusion.scalars, bf16[16,64,128]{2,1,0:T(8,128)(2,1)S(1)} %all-to-all-done.1.dq_ref, bf16[256,128]{1,0:T(8,128)(2,1)S(1)} %get-tuple-element.32.rest_0_, ...), custom_call_target="tpu_custom_call" | custom-call | tf_op jit(solution)/shard_map/pallas_call | solution.py:281
  (9 shorter events, 0.0 us)
Async XLA Ops:
  0.6 0.7 %copy-start.5 = (f32[4,64]{1,0:T(4,128)S(1)}, f32[4,64]{1,0:T(4,128)}, u32[]{:S(2)}) copy-start(f32[4,64]{1,0:T(4,128)} %lse_hbm.1) | copy-start | bytes 3076
  1.3 0.8 %copy-start.2 = (bf16[4,8192]{1,0:T(4,128)(2,1)S(1)}, bf16[4,8192]{1,0:T(4,128)(2,1)}, u32[]{:S(2)}) copy-start(bf16[4,8192]{1,0:T(4,128)(2,1)} %param.8) | copy-start | bytes 196612
  2.2 0.8 %copy-start.3 = (bf16[4,8192]{1,0:T(4,128)(2,1)S(1)}, bf16[4,8192]{1,0:T(4,128)(2,1)}, u32[]{:S(2)}) copy-start(bf16[4,8192]{1,0:T(4,128)(2,1)} %param.9) | copy-start | bytes 196612
  3.0 0.8 %copy-start.4 = (bf16[4,8192]{1,0:T(4,128)(2,1)S(1)}, bf16[4,8192]{1,0:T(4,128)(2,1)}, u32[]{:S(2)}) copy-start(bf16[4,8192]{1,0:T(4,128)(2,1)} %param.10) | copy-start | bytes 196612
  5.1 7.7 %copy-start = (bf16[128,1024]{1,0:T(8,128)(2,1)S(1)}, bf16[128,1024]{1,0:T(8,128)(2,1)}, u32[]{:S(2)}) copy-start(bf16[128,1024]{1,0:T(8,128)(2,1)} %k_ref.1) | copy-start | bytes 786436
  5.1 7.7 %copy-start.1 = (bf16[128,1024]{1,0:T(8,128)(2,1)S(1)}, bf16[128,1024]{1,0:T(8,128)(2,1)}, u32[]{:S(2)}) copy-start(bf16[128,1024]{1,0:T(8,128)(2,1)} %v_ref.1) | copy-start | bytes 786436
  5.2 23.1 %all-to-all-start = ((bf16[16,144,128]{2,1,0:T(8,128)(2,1)}), bf16[16,144,128]{2,1,0:T(8,128)(2,1)S(1)}, u32[]{:S(2)}, u32[]{:S(2)}) async-start(bf16[16,144,128]{2,1,0:T(8,128)(2,1)} %shard_map.103), calls=%async_computation | async-start | bytes 1179648 | tf_op jit(solution)/shard_map/all_to_all | solution.py:257
  13.7 5.2 %collective-permute-start = (bf16[256,128]{1,0:T(8,128)(2,1)S(1)}, bf16[256,128]{1,0:T(8,128)(2,1)S(1)}, u32[]{:S(2)}, u32[]{:S(2)}) collective-permute-start(bf16[256,128]{1,0:T(8,128)(2,1)S(1)} %get-tuple-element.24), channel_id=1, source_target_pairs={{0,1},{1,0},{2,3},{3,2},{4,5},{5,4},{6,7},{7,6},{8,9},{9,8},{10,11... | collective-permute-start | bytes 196616 | tf_op jit(solution)/shard_map/ppermute | solution.py:219
  15.3 4.6 %collective-permute-start.1 = (bf16[256,128]{1,0:T(8,128)(2,1)S(1)}, bf16[256,128]{1,0:T(8,128)(2,1)S(1)}, u32[]{:S(2)}, u32[]{:S(2)}) collective-permute-start(bf16[256,128]{1,0:T(8,128)(2,1)S(1)} %get-tuple-element.25), channel_id=1, source_target_pairs={{0,2},{1,3},{2,0},{3,1},{4,6},{5,7},{6,4},{7,5},{8,10},{9,11},{10,... | collective-permute-start | bytes 196616 | tf_op jit(solution)/shard_map/ppermute | solution.py:219
  15.4 7.2 %collective-permute-start.2 = (bf16[256,128]{1,0:T(8,128)(2,1)S(1)}, bf16[256,128]{1,0:T(8,128)(2,1)S(1)}, u32[]{:S(2)}, u32[]{:S(2)}) collective-permute-start(bf16[256,128]{1,0:T(8,128)(2,1)S(1)} %get-tuple-element.26), channel_id=1, source_target_pairs={{0,3},{1,2},{2,1},{3,0},{4,7},{5,6},{6,5},{7,4},{8,11},{9,10},{10,... | collective-permute-start | bytes 196616 | tf_op jit(solution)/shard_map/ppermute | solution.py:219
  15.9 9.5 %collective-permute-start.3 = (bf16[256,128]{1,0:T(8,128)(2,1)S(1)}, bf16[256,128]{1,0:T(8,128)(2,1)S(1)}, u32[]{:S(2)}, u32[]{:S(2)}) collective-permute-start(bf16[256,128]{1,0:T(8,128)(2,1)S(1)} %get-tuple-element.27), channel_id=1, source_target_pairs={{0,4},{1,5},{2,6},{3,7},{4,0},{5,1},{6,2},{7,3},{8,12},{9,13},{10,... | collective-permute-start | bytes 196616 | tf_op jit(solution)/shard_map/ppermute | solution.py:219
  17.9 7.6 %collective-permute-start.4 = (bf16[256,128]{1,0:T(8,128)(2,1)S(1)}, bf16[256,128]{1,0:T(8,128)(2,1)S(1)}, u32[]{:S(2)}, u32[]{:S(2)}) collective-permute-start(bf16[256,128]{1,0:T(8,128)(2,1)S(1)} %get-tuple-element.28), channel_id=1, source_target_pairs={{0,5},{1,4},{2,7},{3,6},{4,1},{5,0},{6,3},{7,2},{8,13},{9,12},{10,... | collective-permute-start | bytes 196616 | tf_op jit(solution)/shard_map/ppermute | solution.py:219
  18.9 8.1 %collective-permute-start.5 = (bf16[256,128]{1,0:T(8,128)(2,1)S(1)}, bf16[256,128]{1,0:T(8,128)(2,1)S(1)}, u32[]{:S(2)}, u32[]{:S(2)}) collective-permute-start(bf16[256,128]{1,0:T(8,128)(2,1)S(1)} %get-tuple-element.29), channel_id=1, source_target_pairs={{0,6},{1,7},{2,4},{3,5},{4,2},{5,3},{6,0},{7,1},{8,14},{9,15},{10,... | collective-permute-start | bytes 196616 | tf_op jit(solution)/shard_map/ppermute | solution.py:219
  19.9 7.2 %collective-permute-start.6 = (bf16[256,128]{1,0:T(8,128)(2,1)S(1)}, bf16[256,128]{1,0:T(8,128)(2,1)S(1)}, u32[]{:S(2)}, u32[]{:S(2)}) collective-permute-start(bf16[256,128]{1,0:T(8,128)(2,1)S(1)} %get-tuple-element.30), channel_id=1, source_target_pairs={{0,7},{1,6},{2,5},{3,4},{4,3},{5,2},{6,1},{7,0},{8,15},{9,14},{10,... | collective-permute-start | bytes 196616 | tf_op jit(solution)/shard_map/ppermute | solution.py:219
  30.5 4.7 %collective-permute-start.9 = (f32[8,128]{1,0:T(8,128)S(1)}, f32[8,128]{1,0:T(8,128)S(1)}, u32[]{:S(2)}, u32[]{:S(2)}) collective-permute-start(f32[8,128]{1,0:T(8,128)S(1)} %shard_map.105.rest_8_), channel_id=1, source_target_pairs={{0,24},{8,0},{16,8},{24,16},{1,25},{9,1},{17,9},{25,17},{2,26},{10... | collective-permute-start | bytes 12296 | tf_op jit(solution)/shard_map/ppermute | solution.py:268
  33.0 4.5 %collective-permute-start.8 = (f32[8,128]{1,0:T(8,128)S(1)}, f32[8,128]{1,0:T(8,128)S(1)}, u32[]{:S(2)}, u32[]{:S(2)}) collective-permute-start(f32[8,128]{1,0:T(8,128)S(1)} %shard_map.105.rest_8_), channel_id=1, source_target_pairs={{0,16},{8,24},{16,0},{24,8},{1,17},{9,25},{17,1},{25,9},{2,18},{10... | collective-permute-start | bytes 12296 | tf_op jit(solution)/shard_map/ppermute | solution.py:268
  33.5 5.4 %collective-permute-start.7 = (f32[8,128]{1,0:T(8,128)S(1)}, f32[8,128]{1,0:T(8,128)S(1)}, u32[]{:S(2)}, u32[]{:S(2)}) collective-permute-start(f32[8,128]{1,0:T(8,128)S(1)} %shard_map.105.rest_8_), channel_id=1, source_target_pairs={{0,8},{8,16},{16,24},{24,0},{1,9},{9,17},{17,25},{25,1},{2,10},{10... | collective-permute-start | bytes 12296 | tf_op jit(solution)/shard_map/ppermute | solution.py:268
  43.4 15.7 %all-to-all-start.1 = ((bf16[16,64,128]{2,1,0:T(8,128)(2,1)}), bf16[16,64,128]{2,1,0:T(8,128)(2,1)S(1)}, u32[]{:S(2)}, u32[]{:S(2)}) async-start(bf16[16,64,128]{2,1,0:T(8,128)(2,1)} %get-tuple-element.31), calls=%async_computation.1 | async-start | bytes 524288 | tf_op jit(solution)/shard_map/all_to_all | solution.py:280
  46.9 5.2 %collective-permute-start.10 = (bf16[256,128]{1,0:T(8,128)(2,1)S(1)}, bf16[256,128]{1,0:T(8,128)(2,1)S(1)}, u32[]{:S(2)}, u32[]{:S(2)}) collective-permute-start(bf16[256,128]{1,0:T(8,128)(2,1)S(1)} %get-tuple-element.33), channel_id=1, source_target_pairs={{0,1},{1,0},{2,3},{3,2},{4,5},{5,4},{6,7},{7,6},{8,9},{9,8},{10,11... | collective-permute-start | bytes 196616 | tf_op jit(solution)/shard_map/ppermute | solution.py:219
  48.5 4.4 %collective-permute-start.11 = (bf16[256,128]{1,0:T(8,128)(2,1)S(1)}, bf16[256,128]{1,0:T(8,128)(2,1)S(1)}, u32[]{:S(2)}, u32[]{:S(2)}) collective-permute-start(bf16[256,128]{1,0:T(8,128)(2,1)S(1)} %get-tuple-element.34), channel_id=1, source_target_pairs={{0,2},{1,3},{2,0},{3,1},{4,6},{5,7},{6,4},{7,5},{8,10},{9,11},{10,... | collective-permute-start | bytes 196616 | tf_op jit(solution)/shard_map/ppermute | solution.py:219
  48.5 6.1 %collective-permute-start.12 = (bf16[256,128]{1,0:T(8,128)(2,1)S(1)}, bf16[256,128]{1,0:T(8,128)(2,1)S(1)}, u32[]{:S(2)}, u32[]{:S(2)}) collective-permute-start(bf16[256,128]{1,0:T(8,128)(2,1)S(1)} %get-tuple-element.35), channel_id=1, source_target_pairs={{0,3},{1,2},{2,1},{3,0},{4,7},{5,6},{6,5},{7,4},{8,11},{9,10},{10,... | collective-permute-start | bytes 196616 | tf_op jit(solution)/shard_map/ppermute | solution.py:219
  49.1 6.1 %collective-permute-start.13 = (bf16[256,128]{1,0:T(8,128)(2,1)S(1)}, bf16[256,128]{1,0:T(8,128)(2,1)S(1)}, u32[]{:S(2)}, u32[]{:S(2)}) collective-permute-start(bf16[256,128]{1,0:T(8,128)(2,1)S(1)} %get-tuple-element.36), channel_id=1, source_target_pairs={{0,4},{1,5},{2,6},{3,7},{4,0},{5,1},{6,2},{7,3},{8,12},{9,13},{10,... | collective-permute-start | bytes 196616 | tf_op jit(solution)/shard_map/ppermute | solution.py:219
  50.9 5.3 %collective-permute-start.14 = (bf16[256,128]{1,0:T(8,128)(2,1)S(1)}, bf16[256,128]{1,0:T(8,128)(2,1)S(1)}, u32[]{:S(2)}, u32[]{:S(2)}) collective-permute-start(bf16[256,128]{1,0:T(8,128)(2,1)S(1)} %get-tuple-element.37), channel_id=1, source_target_pairs={{0,5},{1,4},{2,7},{3,6},{4,1},{5,0},{6,3},{7,2},{8,13},{9,12},{10,... | collective-permute-start | bytes 196616 | tf_op jit(solution)/shard_map/ppermute | solution.py:219
  52.1 7.0 %collective-permute-start.15 = (bf16[256,128]{1,0:T(8,128)(2,1)S(1)}, bf16[256,128]{1,0:T(8,128)(2,1)S(1)}, u32[]{:S(2)}, u32[]{:S(2)}) collective-permute-start(bf16[256,128]{1,0:T(8,128)(2,1)S(1)} %get-tuple-element.38), channel_id=1, source_target_pairs={{0,6},{1,7},{2,4},{3,5},{4,2},{5,3},{6,0},{7,1},{8,14},{9,15},{10,... | collective-permute-start | bytes 196616 | tf_op jit(solution)/shard_map/ppermute | solution.py:219
  52.9 6.2 %collective-permute-start.16 = (bf16[256,128]{1,0:T(8,128)(2,1)S(1)}, bf16[256,128]{1,0:T(8,128)(2,1)S(1)}, u32[]{:S(2)}, u32[]{:S(2)}) collective-permute-start(bf16[256,128]{1,0:T(8,128)(2,1)S(1)} %get-tuple-element.39), channel_id=1, source_target_pairs={{0,7},{1,6},{2,5},{3,4},{4,3},{5,2},{6,1},{7,0},{8,15},{9,14},{10,... | collective-permute-start | bytes 196616 | tf_op jit(solution)/shard_map/ppermute | solution.py:219

commit v2 on v1

v2 whole, which is shorter than its diff:
```python
import functools

import jax
import jax.numpy as jnp
from jax import lax
from jax.experimental import pallas as pl
from jax.experimental.pallas import tpu as pltpu
from jax.sharding import Mesh, PartitionSpec as P

DH = 128
KVH = 8
RESP_LEN = 64
SCALE = DH ** (-0.5)
MASKED_SCORE = -1e30
DEAD_LSE = 1e30
PIECES = 3
STAT_ROWS = 16
STEP_BLOCKS = 4
PARAMS = pltpu.CompilerParams(vmem_limit_bytes=48 * 1024 * 1024)
HBM = pl.BlockSpec(memory_space=pltpu.HBM)
SMEM = pl.BlockSpec(memory_space=pltpu.SMEM)
VMEM = pl.BlockSpec(memory_space=pltpu.VMEM)

NEAR = 2
KEEP = (0, 1, 4, 5)


def split_pieces(x):
    first = x.astype(jnp.bfloat16)
    rest = x - first.astype(jnp.float32)
    second = rest.astype(jnp.bfloat16)
    third = (rest - second.astype(jnp.float32)).astype(jnp.bfloat16)
    return first, second, third


def shift_of(n):
    assert n & (n - 1) == 0
    return n.bit_length() - 1


def column_of(member, groups, heads):
    head_index, group_index = member & (heads - 1), member >> shift_of(heads)
    return pl.multiple_of((head_index * groups + group_index) * DH, DH)


def pack_kernel(groups, heads, scalars, q_hbm, o_grad_hbm, o_hbm, lse_hbm, k_hbm, v_hbm, *rest):
    slab_refs, (keep_ref, send_ref, o_ref, lse_ref, sems) = rest[:groups], rest[groups:]
    rows, own_heads = lse_ref.shape
    lines = o_ref.shape[0] // groups
    tokens = k_hbm.shape[0]
    member = scalars[0]
    own_group = member >> shift_of(heads)
    copies = [(lse_hbm, lse_ref), (o_hbm, o_ref)]
    firsts = []
    for j in range(groups):
        firsts.append(pl.multiple_of((own_group ^ j) * lines, lines))
        held = pl.ds(firsts[j], lines)
        copies.append((q_hbm.at[held, :], slab_refs[j].at[0:lines, :]))
        copies.append((o_grad_hbm.at[held, :], slab_refs[j].at[lines : 2 * lines, :]))
    row_copies = len(copies)
    for i, j in enumerate(KEEP):
        for ref, peer in ((keep_ref, j), (send_ref, j ^ NEAR)):
            columns = pl.ds(column_of(member ^ peer, groups, heads), DH)
            copies.append((k_hbm.at[:, columns], ref.at[i, 0:tokens, :]))
            copies.append((v_hbm.at[:, columns], ref.at[i, tokens : 2 * tokens, :]))
    copies = [pltpu.make_async_copy(s, t, sems.at[n]) for n, (s, t) in enumerate(copies)]
    for copy in copies:
        copy.start()

    wide = 2 * lines
    shape = (own_heads, wide)
    head_ids = lax.broadcasted_iota(jnp.int32, shape, 0)
    line_heads = (lax.broadcasted_iota(jnp.int32, shape, 1) & (lines - 1)) >> shift_of(rows)
    chosen = [
        (head_ids == line_heads + (firsts[j] >> shift_of(rows))).astype(jnp.bfloat16)
        for j in range(groups)
    ]
    shape = (rows, wide)
    own_row = lax.broadcasted_iota(jnp.int32, shape, 0) == (
        lax.broadcasted_iota(jnp.int32, shape, 1) & (rows - 1)
    )
    for copy in copies[:row_copies]:
        copy.wait()
    pieces = split_pieces(lse_ref[...])
    for j in range(groups):
        stats = []
        for piece in pieces:
            spread = jnp.dot(piece, chosen[j], preferred_element_type=jnp.float32)
            stats.append(jnp.sum(jnp.where(own_row, spread, 0.0), axis=0, keepdims=True))
        o_grad = slab_refs[j][lines : 2 * lines, :].astype(jnp.float32)
        product = o_grad * o_ref[pl.ds(firsts[j], lines), :].astype(jnp.float32)
        dots = jnp.sum(jnp.concatenate([product, product], axis=0).T, axis=0, keepdims=True)
        stats += [piece.astype(jnp.float32) for piece in split_pieces(dots)]
        stats.append(jnp.zeros((STAT_ROWS - 2 * PIECES, wide), jnp.float32))
        slab_refs[j][wide:, :] = jnp.concatenate(stats, axis=0).astype(jnp.bfloat16)
    for copy in copies[row_copies:]:
        copy.wait()


def pair_starts(scalars, i, tokens):
    first = scalars[1] * KVH
    return [(first + (scalars[0] ^ KEEP[i] ^ other)) * tokens for other in (0, NEAR)]


def pair_keys(ref, tokens):
    return jnp.concatenate([ref[0, 0:tokens, :], ref[1, 0:tokens, :]], axis=0)


def pair_values(ref, tokens):
    return jnp.concatenate([ref[0, tokens : 2 * tokens, :], ref[1, tokens : 2 * tokens, :]], axis=0)


def response_of(scalars, b, groups, rows):
    return ((scalars[1] ^ b) * (groups * rows)) >> shift_of(RESP_LEN)


def lse_rows(groups, lines):
    return max(1, groups * lines // DH)


def stat_kernel(parts, groups, rows, tokens, scalars, prompt_end, *refs):
    row_refs, pair_refs, lse_ref = refs[:parts], refs[parts:-1], refs[-1]
    lines = (row_refs[0].shape[1] - STAT_ROWS) // 2
    count = groups * lines
    offset = lax.broadcasted_iota(jnp.int32, (tokens, count), 0)
    for b in range(parts):
        q = row_refs[b][:, 0:lines, :].reshape(count, DH)
        end = prompt_end[response_of(scalars, b, groups, rows)]
        scores = []
        for i, ref in enumerate(pair_refs):
            part = lax.dot_general(
                pair_keys(ref, tokens),
                q,
                (((1,), (1,)), ((), ())),
                preferred_element_type=jnp.float32,
            )
            visible = jnp.concatenate(
                [offset < end - start for start in pair_starts(scalars, i, tokens)], axis=0
            )
            scores.append(jnp.where(visible, part * SCALE, MASKED_SCORE))
        scores = jnp.concatenate(scores, axis=0)
        peak = jnp.max(scores, axis=0, keepdims=True)
        total = jnp.sum(jnp.exp(scores - peak), axis=0, keepdims=True)
        lse = peak + jnp.log(total)
        if count < DH:
            lse = jnp.concatenate([lse] * (DH // count), axis=1)
        held = lse_rows(groups, lines)
        for n in range(held):
            at = (scalars[1] ^ b) * held + n
            lse_ref[pl.ds(at, 1), :] = lse[:, n * DH : (n + 1) * DH]


def line_values(slabs, lines, first_piece):
    low = lax.broadcasted_iota(jnp.int32, (1, 2 * lines), 1) < lines
    out = []
    for n in range(0, len(slabs), 2):
        held = [
            ref[j, 2 * lines : 2 * lines + STAT_ROWS, :].astype(jnp.float32)
            for ref, j in slabs[n : n + 2]
        ]
        total = None
        for k in range(first_piece, first_piece + PIECES):
            piece = jnp.where(low, held[0][k : k + 1], held[1][k : k + 1])
            total = piece if total is None else total + piece
        out.append(total)
    return jnp.concatenate(out, axis=1)


def grad_kernel(parts, order, groups, heads, rows, tokens, scalars, resp_len, prompt_end, *refs):
    row_refs, refs = refs[:parts], refs[parts:]
    pair_refs, refs = refs[: len(KEEP)], refs[len(KEEP) :]
    lse_refs, refs = refs[:-6], refs[-6:]
    dq_keep_ref, dq_send_ref, dkv_keep_ref, dkv_send_ref, dk_acc, dv_acc = refs
    lines = (row_refs[0].shape[1] - STAT_ROWS) // 2
    block = groups * lines
    step = min(parts, STEP_BLOCKS)
    own_group = scalars[0] >> shift_of(heads)
    held = lse_rows(groups, lines)
    offset = lax.broadcasted_iota(jnp.int32, (tokens, step * block), 0)
    lane = lax.broadcasted_iota(jnp.int32, (1, 2 * lines), 1)
    for c in range(0, parts, step):
        blocks = range(c, c + step)
        slabs = [(b, j) for b in blocks for j in range(groups)]
        q = jnp.concatenate([row_refs[b][j, 0:lines, :] for b, j in slabs], axis=0)
        o_grad = jnp.concatenate([row_refs[b][j, lines : 2 * lines, :] for b, j in slabs], axis=0)
        values = [(row_refs[b], j) for b, j in slabs]
        self_lse, dots = line_values(values, lines, 0), line_values(values, lines, PIECES)
        live = []
        for n in range(0, len(slabs), 2):
            row, length = [], []
            for b, j in slabs[n : n + 2]:
                source = (scalars[1] ^ b) * groups + (own_group ^ j)
                row.append(source * rows & (RESP_LEN - 1))
                length.append(resp_len[response_of(scalars, b, groups, rows)])
            row = jnp.where(lane < lines, row[0], row[1]) + (lane & (rows - 1))
            live.append(row < jnp.where(lane < lines, length[0], length[1]))
        live = jnp.concatenate(live, axis=1)
        end = jnp.concatenate(
            [
                jnp.full((1, block), prompt_end[response_of(scalars, b, groups, rows)], jnp.int32)
                for b in blocks
            ],
            axis=1,
        )
        part_lse = []
        for ref in lse_refs:
            tiles = []
            for b in blocks:
                for n in range(held):
                    tile = ref[pl.ds((scalars[1] ^ b) * held + n, 1), :]
                    tiles.append(tile[:, : min(block, DH)])
            part_lse.append(jnp.concatenate(tiles, axis=1))
        peak = functools.reduce(jnp.maximum, part_lse, self_lse)
        total = sum(jnp.exp(x - peak) for x in part_lse) + jnp.exp(self_lse - peak)
        lse = jnp.where(live, peak + jnp.log(total), DEAD_LSE)
        dq_t = jnp.zeros((DH, step * block), jnp.float32)
        for i, ref in enumerate(pair_refs):
            k, v = pair_keys(ref, tokens), pair_values(ref, tokens)
            scores = lax.dot_general(
                k, q, (((1,), (1,)), ((), ())), preferred_element_type=jnp.float32
            )
            visible = jnp.concatenate(
                [offset < end - start for start in pair_starts(scalars, i, tokens)], axis=0
            )
            prob = jnp.where(visible, jnp.exp(scores * SCALE - lse), 0.0)
            dprob = lax.dot_general(
                v, o_grad, (((1,), (1,)), ((), ())), preferred_element_type=jnp.float32
            )
            dscore = (prob * (dprob - dots)).astype(jnp.bfloat16)
            dv = jnp.dot(prob.astype(jnp.bfloat16), o_grad, preferred_element_type=jnp.float32)
            dk = jnp.dot(dscore, q, preferred_element_type=jnp.float32) * SCALE
            dq_t = dq_t + jnp.dot(k.T, dscore, preferred_element_type=jnp.float32)
            if c > 0:
                dk = dk + dk_acc[i]
                dv = dv + dv_acc[i]
            if c + step < parts:
                dk_acc[i] = dk
                dv_acc[i] = dv
            else:
                for n, out in enumerate((dkv_keep_ref, dkv_send_ref)):
                    inner = slice(n * tokens, (n + 1) * tokens)
                    out[i, 0:tokens, :] = dk[inner].astype(jnp.bfloat16)
                    out[i, tokens : 2 * tokens, :] = dv[inner].astype(jnp.bfloat16)
        for n, b in enumerate(blocks):
            dq = (dq_t[:, n * block : (n + 1) * block] * SCALE).T.astype(jnp.bfloat16)
            place = order.index(b)
            if place < parts // 2:
                dq_keep_ref[place] = dq
            else:
                dq_send_ref[place - parts // 2] = dq


def unpack_kernel(groups, heads, scalars, *refs):
    slab_refs, pair_refs = refs[:groups], refs[groups : groups + len(KEEP)]
    out_q_ref, out_k_ref, out_v_ref = refs[groups + len(KEEP) :]
    lines = slab_refs[0].shape[0]
    tokens = out_k_ref.shape[0]
    own_group = scalars[0] >> shift_of(heads)
    for j, ref in enumerate(slab_refs):
        out_q_ref[pl.ds(pl.multiple_of((own_group ^ j) * lines, lines), lines), :] = ref[...]
    for i, ref in enumerate(pair_refs):
        for n, other in enumerate((0, NEAR)):
            columns = pl.ds(column_of(scalars[0] ^ KEEP[i] ^ other, groups, heads), DH)
            out_k_ref[:, columns] = ref[n, 0:tokens, :]
            out_v_ref[:, columns] = ref[n, tokens : 2 * tokens, :]


def swap(x, axis, distance, size):
    return lax.ppermute(x, axis, [(i, i ^ distance) for i in range(size)])


def swap_pairs(keep, send):
    members = ("group", "head")
    came = swap(send, members, NEAR, KVH)
    pairs = [jnp.stack([keep[i], came[i]]) for i in range(len(KEEP))]
    return [swap(x, members, j, KVH) if j else x for x, j in zip(pairs, KEEP)]


def add_lse(a, b):
    peak = jnp.maximum(a, b)
    return peak + jnp.log(jnp.exp(a - peak) + jnp.exp(b - peak))


def shards(parts, groups, heads, queries, grad_out, outputs, lse_self, keys, values, resp_len, prompt_end):
    rows = queries.shape[0]
    own_heads = queries.shape[1] // DH
    own_lines = rows * own_heads
    lines = own_lines // groups
    tokens = keys.shape[0]
    assert 2 * lines == DH and RESP_LEN % (groups * rows) == 0 and parts % 2 == 0
    member = lax.axis_index("group") * heads + lax.axis_index("head")
    scalars = jnp.stack([member, lax.axis_index("part")]).astype(jnp.int32)
    far = [1 << n for n in reversed(range(shift_of(parts)))]

    def as_lines(x):
        return x.reshape(rows, own_heads, DH).transpose(1, 0, 2).reshape(own_lines, DH)

    slab_shape = jax.ShapeDtypeStruct((2 * lines + STAT_ROWS, DH), jnp.bfloat16)
    half_shape = jax.ShapeDtypeStruct((len(KEEP), 2 * tokens, DH), jnp.bfloat16)
    *slabs, kv_keep, kv_send = pl.pallas_call(
        functools.partial(pack_kernel, groups, heads),
        in_specs=[SMEM] + [HBM] * 6,
        out_specs=[VMEM] * (groups + 2),
        out_shape=[slab_shape] * groups + [half_shape] * 2,
        scratch_shapes=[
            pltpu.VMEM((own_lines, DH), jnp.bfloat16),
            pltpu.VMEM(lse_self.shape, jnp.float32),
            pltpu.SemaphoreType.DMA((2 + 2 * groups + 4 * len(KEEP),)),
        ],
        compiler_params=PARAMS,
    )(scalars, as_lines(queries), as_lines(grad_out), as_lines(outputs), lse_self, keys, values)

    own_block = jnp.stack([swap(x, "group", j, groups) if j else x for j, x in enumerate(slabs)])
    order, blocks = [0], [own_block]
    for d in far:
        blocks = blocks + [swap(x, "part", d, parts) for x in blocks]
        order = order + [b ^ d for b in order]
    blocks = [blocks[order.index(b)] for b in range(parts)]
    pairs = swap_pairs(kv_keep, kv_send)

    lse = pl.pallas_call(
        functools.partial(stat_kernel, parts, groups, rows, tokens),
        in_specs=[SMEM] * 2 + [VMEM] * (parts + len(KEEP)),
        out_shape=jax.ShapeDtypeStruct((parts * lse_rows(groups, lines), DH), jnp.float32),
        compiler_params=PARAMS,
    )(scalars, prompt_end, *blocks, *pairs)
    for d in far[:0:-1]:
        lse = add_lse(lse, swap(lse, "part", d, parts))
    every_lse = [lse, swap(lse, "part", far[0], parts)]

    dq_shape = jax.ShapeDtypeStruct((parts // 2, groups * lines, DH), jnp.bfloat16)
    acc = pltpu.VMEM((len(KEEP), 2 * tokens, DH), jnp.float32)
    dq_keep, dq_send, dkv_keep, dkv_send = pl.pallas_call(
        functools.partial(grad_kernel, parts, order, groups, heads, rows, tokens),
        in_specs=[SMEM] * 3 + [VMEM] * (parts + len(KEEP) + len(every_lse)),
        out_shape=[dq_shape] * 2 + [half_shape] * 2,
        scratch_shapes=[acc] * 2,
        compiler_params=PARAMS,
    )(scalars, resp_len, prompt_end, *blocks, *pairs, *every_lse)

    for d in far[::-1]:
        came = swap(dq_send, "part", d, parts)
        total = dq_keep.astype(jnp.float32) + came.astype(jnp.float32)
        half = total.shape[0] // 2
        dq_keep, dq_send = total[:half], total[half:].astype(jnp.bfloat16)
    dq = total.astype(jnp.bfloat16).reshape(groups, lines, DH)
    slabs = [swap(dq[j], "group", j, groups) if j else dq[j] for j in range(groups)]
    pairs = swap_pairs(dkv_keep, dkv_send)
    out_q, out_k, out_v = pl.pallas_call(
        functools.partial(unpack_kernel, groups, heads),
        in_specs=[SMEM] + [VMEM] * (groups + len(KEEP)),
        out_shape=[
            jax.ShapeDtypeStruct((own_lines, DH), jnp.bfloat16),
            jax.ShapeDtypeStruct(keys.shape, jnp.bfloat16),
            jax.ShapeDtypeStruct(values.shape, jnp.bfloat16),
        ],
        compiler_params=PARAMS,
    )(scalars, *slabs, *pairs)
    out_q = out_q.reshape(own_heads, rows, DH).transpose(1, 0, 2).reshape(rows, own_heads * DH)
    return out_q, out_k, out_v


def solution(mesh):
    ctx, heads = mesh.shape["ctx"], mesh.shape["head"]
    groups = KVH // heads
    parts = ctx // groups
    fine = Mesh(mesh.devices.reshape(parts, groups, heads), ("part", "group", "head"))
    rows = P(("part", "group"), "head")
    tokens = P(("part", "group", "head"), None)
    return jax.shard_map(
        functools.partial(shards, parts, groups, heads),
        mesh=fine,
        in_specs=(rows, rows, rows, rows, tokens, tokens, P(), P()),
        out_specs=(rows, tokens, tokens),
        check_vma=False,
    )
```

time: 61.1 us -> 71.9 us (1.18)
  waiting for transfers between devices: 13.8 us -> 30.7 us
  starting transfers between devices: 31 us -> 24.5 us
  local copies, waits for them, and re-layouts: 3.2 us -> 5.19 us
  Pallas kernels: 10.5 us -> 8.73 us
    ppermute x17 -> x21, waiting for transfers between devices: 12.6 us -> 30.7 us  [swap(): return lax.ppermute(x, axis, [(i, i ^ distance) for i in range(size)])]
    all_to_all x2 -> x0, starting transfers between devices: 11.1 us -> none  [the longest x1 7.53 us: shards(): lax.all_to_all(row_block, ('part', 'group'), split_axis=0, concat_axis=0,...]
    ppermute x17 -> x21, starting transfers between devices: 20 us -> 24.5 us  [swap(): return lax.ppermute(x, axis, [(i, i ^ distance) for i in range(size)])]
    unnamed x12, local copies, waits for them, and re-layouts: 3.2 us -> 5.1 us
    pallas_call x5 -> x4, Pallas kernels: 10.5 us -> 8.73 us  [the longest x1 3.61 us: shards(): pl.pallas_call(functools.partial(grad_kernel, parts, order, groups, heads...]
    all_to_all x2 -> x0, waiting for transfers between devices: 1.21 us -> none  [the longest x1 1.21 us: shards(): lax.all_to_all(row_block, ('part', 'group'), split_axis=0, concat_axis=0,...]
  transfers between devices with their start and end apart: 19 -> 21, of which waited for: 8 -> 11; matrix products, arithmetic and copies ran while one was open for 0% -> 0% of each run, Pallas kernels for 2% -> 0%
where the time goes in v2:
time: 71.9 us; the launch traced here: 71.5 us
  waiting for transfers between devices  30.7 us (43%)
  starting transfers between devices  24.5 us (34%)
  Pallas kernels  8.73 us (12%)
  local copies, waits for them, and re-layouts  5.19 us (7%)
  between operations  2.1 us (3%)
    ppermute x21, waiting for transfers between devices, swap(): return lax.ppermute(x, axis, [(i, i ^ distance) for i in range(size)])  30.7 us
    ppermute x21, starting transfers between devices, swap(): return lax.ppermute(x, axis, [(i, i ^ distance) for i in range(size)])  24.5 us
    unnamed x12, local copies, waits for them, and re-layouts  5.1 us
    pallas_call x1, Pallas kernels, shards(): pl.pallas_call(functools.partial(grad_kernel, parts, order, groups, heads...  3.61 us
    pallas_call x1, Pallas kernels, shards(): pl.pallas_call(functools.partial(stat_kernel, parts, groups, rows, tokens...  2.15 us
    pallas_call x1, Pallas kernels, shards(): pl.pallas_call(functools.partial(unpack_kernel, groups, heads), in_specs=...  1.51 us
    pallas_call x1, Pallas kernels, shards(): pl.pallas_call(functools.partial(pack_kernel, groups, heads), in_specs=[S...  1.46 us
  transfers between devices with their start and end apart: 21, of which 11 were waited for; matrix products, arithmetic and copies ran while one was open for 0% of the time, Pallas kernels for 0%

profile of v2, /device:TPU:0, one launch (start us, length us, event | category | flops | bytes accessed | tf_op | source)
XLA Modules:
  0.0 71.5 jit_solution(11268322878884262604)
XLA Ops:
  0.6 0.1 pad_add_fusion.scalars
  0.7 0.7 copy-done.5
  1.4 0.9 %copy-done = bf16[128,1024]{1,0:T(8,128)(2,1)S(1)} copy-done((bf16[128,1024]{1,0:T(8,128)(2,1)S(1)}, bf16[128,1024]{1,0:T(8,128)(2,1)}, u32[]{:S(2)}) %copy-start) | copy-done | bytes 262168
  2.3 0.9 %copy-done.1 = bf16[128,1024]{1,0:T(8,128)(2,1)S(1)} copy-done((bf16[128,1024]{1,0:T(8,128)(2,1)S(1)}, bf16[128,1024]{1,0:T(8,128)(2,1)}, u32[]{:S(2)}) %copy-start.1) | copy-done | bytes 262168
  3.3 0.8 %copy-done.2 = bf16[4,8192]{1,0:T(4,128)(2,1)S(1)} copy-done((bf16[4,8192]{1,0:T(4,128)(2,1)S(1)}, bf16[4,8192]{1,0:T(4,128)(2,1)}, u32[]{:S(2)}) %copy-start.2) | copy-done | bytes 65560
  4.1 0.8 %copy-done.3 = bf16[4,8192]{1,0:T(4,128)(2,1)S(1)} copy-done((bf16[4,8192]{1,0:T(4,128)(2,1)S(1)}, bf16[4,8192]{1,0:T(4,128)(2,1)}, u32[]{:S(2)}) %copy-start.3) | copy-done | bytes 65560
  5.0 0.8 %copy-done.4 = bf16[4,8192]{1,0:T(4,128)(2,1)S(1)} copy-done((bf16[4,8192]{1,0:T(4,128)(2,1)S(1)}, bf16[4,8192]{1,0:T(4,128)(2,1)}, u32[]{:S(2)}) %copy-start.4) | copy-done | bytes 65560
  5.8 1.5 %shard_map.103 = (bf16[144,128]{1,0:T(8,128)(2,1)S(1)}, bf16[144,128]{1,0:T(8,128)(2,1)S(1)}, bf16[144,128]{1,0:T(8,128)(2,1)S(1)}, bf16[144,128]{1,0:T(8,128)(2...) custom-call(s32[2]{0:T(128)S(1)} %pad_add_fusion.scalars, bf16[256,128]{1,0:T(8,128)(2,1)S(1)} %bitcast.34, ...), custom_call_target="tpu_custom_call" | custom-call | tf_op jit(solution)/shard_map/pallas_call | solution.py:300
  7.3 0.5 collective-permute-start
  7.8 2.6 %collective-permute-start.1 = (bf16[144,128]{1,0:T(8,128)(2,1)S(1)}, bf16[144,128]{1,0:T(8,128)(2,1)S(1)}, u32[]{:S(2)}, u32[]{:S(2)}) collective-permute-start(bf16[144,128]{1,0:T(8,128)(2,1)S(1)} %get-tuple-element.18), channel_id=1, source_target_pairs={{0,4},{2,6},{4,0},{6,2},{1,5},{3,7},{5,1},{7,3},{8,12},{10,14},{12... | collective-permute-start | bytes 110600 | tf_op jit(solution)/shard_map/ppermute | solution.py:269
  10.4 0.1 collective-permute-start.2
  10.5 0.1 collective-permute-start.6
  10.6 1.9 %collective-permute-done.1 = bf16[144,128]{1,0:T(8,128)(2,1)S(1)} collective-permute-done((bf16[144,128]{1,0:T(8,128)(2,1)S(1)}, bf16[144,128]{1,0:T(8,128)(2,1)S(1)}, u32[]{:S(2)}, u32[]{:S(2)}) %collective-permute-start.1) | collective-permute-done | bytes 36896 | tf_op jit(solution)/shard_map/ppermute | solution.py:269
  12.5 1.4 %collective-permute-done.2 = bf16[144,128]{1,0:T(8,128)(2,1)S(1)} collective-permute-done((bf16[144,128]{1,0:T(8,128)(2,1)S(1)}, bf16[144,128]{1,0:T(8,128)(2,1)S(1)}, u32[]{:S(2)}, u32[]{:S(2)}) %collective-permute-start.2) | collective-permute-done | bytes 36896 | tf_op jit(solution)/shard_map/ppermute | solution.py:269
  13.9 2.7 %collective-permute-start.4 = (bf16[4,144,128]{2,1,0:T(8,128)(2,1)S(1)}, bf16[4,144,128]{2,1,0:T(8,128)(2,1)S(1)}, u32[]{:S(2)}, u32[]{:S(2)}) collective-permute-start(bf16[4,144,128]{2,1,0:T(8,128)(2,1)S(1)} %pad_maximum_fusion.refs_0_), channel_id=1, source_target_pairs={{0,16},{8,24},{16,0},{24,8},{1,17},{9,25},{17,1},{25,9},{2,18},{10... | collective-permute-start | bytes 442376 | tf_op jit(solution)/shard_map/ppermute | solution.py:269
  16.5 1.6 %collective-permute-start.3 = (bf16[4,144,128]{2,1,0:T(8,128)(2,1)S(1)}, bf16[4,144,128]{2,1,0:T(8,128)(2,1)S(1)}, u32[]{:S(2)}, u32[]{:S(2)}) collective-permute-start(bf16[4,144,128]{2,1,0:T(8,128)(2,1)S(1)} %pad_maximum_fusion.refs_0_), channel_id=1, source_target_pairs={{0,8},{8,0},{16,24},{24,16},{1,9},{9,1},{17,25},{25,17},{2,10},{10... | collective-permute-start | bytes 442376 | tf_op jit(solution)/shard_map/ppermute | solution.py:269
  18.2 5.8 %collective-permute-done.4.refs_2_ = bf16[4,144,128]{2,1,0:T(8,128)(2,1)S(1)} collective-permute-done((bf16[4,144,128]{2,1,0:T(8,128)(2,1)S(1)}, bf16[4,144,128]{2,1,0:T(8,128)(2,1)S(1)}, u32[]{:S(2)}, u32[]{:S(2)}) %collective-permute-start.4) | collective-permute-done | bytes 147488 | tf_op jit(solution)/shard_map/ppermute | solution.py:269
  24.0 0.6 collective-permute-start.5
  24.6 0.0 collective-permute-done.6
  24.6 1.6 %collective-permute-start.7 = (bf16[2,256,128]{2,1,0:T(8,128)(2,1)S(1)}, bf16[2,256,128]{2,1,0:T(8,128)(2,1)S(1)}, u32[]{:S(2)}, u32[]{:S(2)}) collective-permute-start(bf16[2,256,128]{2,1,0:T(8,128)(2,1)S(1)} %pad_maximum_fusion.2), channel_id=1, source_target_pairs={{0,1},{1,0},{2,3},{3,2},{4,5},{5,4},{6,7},{7,6},{8,9},{9,8},{10,11... | collective-permute-start | bytes 393224 | tf_op jit(solution)/shard_map/ppermute | solution.py:269
  26.2 1.0 %collective-permute-start.8 = (bf16[2,256,128]{2,1,0:T(8,128)(2,1)S(1)}, bf16[2,256,128]{2,1,0:T(8,128)(2,1)S(1)}, u32[]{:S(2)}, u32[]{:S(2)}) collective-permute-start(bf16[2,256,128]{2,1,0:T(8,128)(2,1)S(1)} %pad_maximum_fusion.3), channel_id=1, source_target_pairs={{0,4},{1,5},{2,6},{3,7},{4,0},{5,1},{6,2},{7,3},{8,12},{9,13},{10,... | collective-permute-start | bytes 393224 | tf_op jit(solution)/shard_map/ppermute | solution.py:269
  27.2 1.2 %collective-permute-start.9 = (bf16[2,256,128]{2,1,0:T(8,128)(2,1)S(1)}, bf16[2,256,128]{2,1,0:T(8,128)(2,1)S(1)}, u32[]{:S(2)}, u32[]{:S(2)}) collective-permute-start(bf16[2,256,128]{2,1,0:T(8,128)(2,1)S(1)} %pad_maximum_fusion.4), channel_id=1, source_target_pairs={{0,5},{1,4},{2,7},{3,6},{4,1},{5,0},{6,3},{7,2},{8,13},{9,12},{10,... | collective-permute-start | bytes 393224 | tf_op jit(solution)/shard_map/ppermute | solution.py:269
  29.0 0.0 collective-permute-done.3.refs_1_
  29.0 0.1 collective-permute-done.5.refs_3_
  29.1 0.9 %collective-permute-done.7.refs_5_ = bf16[2,256,128]{2,1,0:T(8,128)(2,1)S(1)} collective-permute-done((bf16[2,256,128]{2,1,0:T(8,128)(2,1)S(1)}, bf16[2,256,128]{2,1,0:T(8,128)(2,1)S(1)}, u32[]{:S(2)}, u32[]{:S(2)}) %collective-permute-start.7) | collective-permute-done | bytes 131104 | tf_op jit(solution)/shard_map/ppermute | solution.py:269
  30.1 4.0 %collective-permute-done.8.refs_6_ = bf16[2,256,128]{2,1,0:T(8,128)(2,1)S(1)} collective-permute-done((bf16[2,256,128]{2,1,0:T(8,128)(2,1)S(1)}, bf16[2,256,128]{2,1,0:T(8,128)(2,1)S(1)}, u32[]{:S(2)}, u32[]{:S(2)}) %collective-permute-start.8) | collective-permute-done | bytes 131104 | tf_op jit(solution)/shard_map/ppermute | solution.py:269
  34.0 0.0 collective-permute-done.9.refs_7_
  34.1 2.1 %shard_map.104 = f32[8,128]{1,0:T(8,128)S(1)} custom-call(s32[2]{0:T(128)S(1)} %pad_add_fusion.scalars, s32[1]{0:T(128)S(6)} %copy.16.prompt_end, bf16[4,144,128]{2,1,0:T(8,128)(2,1)S(1)} %pad_maximum_fusion.refs_0_, bf16[4,144,128]{2,1,0:T(8,128)(2,1)S(1)} %collective-permute-done.3.refs_1_, bf16[4,144,128]{2,1,0:T(8,128)(2,1)S(1)} %collective-permute-done.4.refs_2_, ...), custom_call_target="tpu_custom_call" | custom-call | tf_op jit(solution)/shard_map/pallas_call | solution.py:321
  36.2 1.2 %collective-permute-start.10 = (f32[8,128]{1,0:T(8,128)S(1)}, f32[8,128]{1,0:T(8,128)S(1)}, u32[]{:S(2)}, u32[]{:S(2)}) collective-permute-start(f32[8,128]{1,0:T(8,128)S(1)} %shard_map.104), channel_id=1, source_target_pairs={{0,8},{8,0},{16,24},{24,16},{1,9},{9,1},{17,25},{25,17},{2,10},{10... | collective-permute-start | bytes 12296 | tf_op jit(solution)/shard_map/ppermute | solution.py:269
  37.4 2.5 %collective-permute-done.10 = f32[8,128]{1,0:T(8,128)S(1)} collective-permute-done((f32[8,128]{1,0:T(8,128)S(1)}, f32[8,128]{1,0:T(8,128)S(1)}, u32[]{:S(2)}, u32[]{:S(2)}) %collective-permute-start.10) | collective-permute-done | bytes 4128 | tf_op jit(solution)/shard_map/ppermute | solution.py:269
  39.9 3.4 %collective-permute-start.11 = (f32[8,128]{1,0:T(8,128)S(1)}, f32[8,128]{1,0:T(8,128)S(1)}, u32[]{:S(2)}, u32[]{:S(2)}) collective-permute-start(f32[8,128]{1,0:T(8,128)S(1)} %log_add_fusion.refs_8_), channel_id=1, source_target_pairs={{0,16},{8,24},{16,0},{24,8},{1,17},{9,25},{17,1},{25,9},{2,18},{10... | collective-permute-start | bytes 12296 | tf_op jit(solution)/shard_map/ppermute | solution.py:269
  44.0 0.9 %collective-permute-done.11.refs_9_ = f32[8,128]{1,0:T(8,128)S(1)} collective-permute-done((f32[8,128]{1,0:T(8,128)S(1)}, f32[8,128]{1,0:T(8,128)S(1)}, u32[]{:S(2)}, u32[]{:S(2)}) %collective-permute-start.11) | collective-permute-done | bytes 4128 | tf_op jit(solution)/shard_map/ppermute | solution.py:269
  44.9 3.6 %shard_map.105 = (bf16[2,256,128]{2,1,0:T(8,128)(2,1)S(1)}, bf16[2,256,128]{2,1,0:T(8,128)(2,1)S(1)}, bf16[4,256,128]{2,1,0:T(8,128)(2,1)S(1)}, bf16[4,256,128]{2,1,0:T(8,128)(2,1)S(1)}) custom-call(s32[2]{0:T(128)S(1)} %pad_add_fusion.scalars, s32[1]{0:T(128)S(6)} %copy.15.resp_len, s32[1]{0:T(128)S(6)} %copy.16.prompt_end, ...), custom_call_target="tpu_custom_call" | custom-call | tf_op jit(solution)/shard_map/pallas_call | solution.py:333
  48.5 0.7 collective-permute-start.12
  49.2 4.8 %collective-permute-done.12 = bf16[2,256,128]{2,1,0:T(8,128)(2,1)S(1)} collective-permute-done((bf16[2,256,128]{2,1,0:T(8,128)(2,1)S(1)}, bf16[2,256,128]{2,1,0:T(8,128)(2,1)S(1)}, u32[]{:S(2)}, u32[]{:S(2)}) %collective-permute-start.12) | collective-permute-done | bytes 131104 | tf_op jit(solution)/shard_map/ppermute | solution.py:269
  54.1 2.5 %collective-permute-start.13 = (bf16[1,256,128]{2,1,0:T(8,128)(2,1)S(1)}, bf16[1,256,128]{2,1,0:T(8,128)(2,1)S(1)}, u32[]{:S(2)}, u32[]{:S(2)}) collective-permute-start(bf16[1,256,128]{2,1,0:T(8,128)(2,1)S(1)} %slice.115), channel_id=1, source_target_pairs={{0,16},{8,24},{16,0},{24,8},{1,17},{9,25},{17,1},{25,9},{2,18},{10... | collective-permute-start | bytes 196616 | tf_op jit(solution)/shard_map/ppermute | solution.py:269
  56.6 0.1 collective-permute-start.17
  56.7 3.3 %collective-permute-done.13 = bf16[1,256,128]{2,1,0:T(8,128)(2,1)S(1)} collective-permute-done((bf16[1,256,128]{2,1,0:T(8,128)(2,1)S(1)}, bf16[1,256,128]{2,1,0:T(8,128)(2,1)S(1)}, u32[]{:S(2)}, u32[]{:S(2)}) %collective-permute-start.13) | collective-permute-done | bytes 65568 | tf_op jit(solution)/shard_map/ppermute | solution.py:269
  60.1 0.1 collective-permute-start.16
  60.2 0.0 collective-permute-done.17
  60.2 0.2 collective-permute-start.18
  60.5 1.1 %collective-permute-start.19 = (bf16[2,256,128]{2,1,0:T(8,128)(2,1)S(1)}, bf16[2,256,128]{2,1,0:T(8,128)(2,1)S(1)}, u32[]{:S(2)}, u32[]{:S(2)}) collective-permute-start(bf16[2,256,128]{2,1,0:T(8,128)(2,1)S(1)} %pad_maximum_fusion.7), channel_id=1, source_target_pairs={{0,4},{1,5},{2,6},{3,7},{4,0},{5,1},{6,2},{7,3},{8,12},{9,13},{10,... | collective-permute-start | bytes 393224 | tf_op jit(solution)/shard_map/ppermute | solution.py:269
  61.6 2.4 %collective-permute-start.20 = (bf16[2,256,128]{2,1,0:T(8,128)(2,1)S(1)}, bf16[2,256,128]{2,1,0:T(8,128)(2,1)S(1)}, u32[]{:S(2)}, u32[]{:S(2)}) collective-permute-start(bf16[2,256,128]{2,1,0:T(8,128)(2,1)S(1)} %pad_maximum_fusion.8), channel_id=1, source_target_pairs={{0,5},{1,4},{2,7},{3,6},{4,1},{5,0},{6,3},{7,2},{8,13},{9,12},{10,... | collective-permute-start | bytes 393224 | tf_op jit(solution)/shard_map/ppermute | solution.py:269
  63.9 0.9 %collective-permute-start.15 = (bf16[64,128]{1,0:T(8,128)(2,1)S(1)}, bf16[64,128]{1,0:T(8,128)(2,1)S(1)}, u32[]{:S(2)}, u32[]{:S(2)}) collective-permute-start(bf16[64,128]{1,0:T(8,128)(2,1)S(1)} %get-tuple-element.46), channel_id=1, source_target_pairs={{0,4},{2,6},{4,0},{6,2},{1,5},{3,7},{5,1},{7,3},{8,12},{10,14},{12... | collective-permute-start | bytes 49160 | tf_op jit(solution)/shard_map/ppermute | solution.py:269
  64.9 0.1 collective-permute-start.14
  64.9 5.0 %collective-permute-done.15.refs_2_ = bf16[64,128]{1,0:T(8,128)(2,1)S(1)} collective-permute-done((bf16[64,128]{1,0:T(8,128)(2,1)S(1)}, bf16[64,128]{1,0:T(8,128)(2,1)S(1)}, u32[]{:S(2)}, u32[]{:S(2)}) %collective-permute-start.15) | collective-permute-done | bytes 16416 | tf_op jit(solution)/shard_map/ppermute | solution.py:269
  70.0 0.0 collective-permute-done.20.refs_7_
  70.0 1.5 %shard_map.106 = (bf16[256,128]{1,0:T(8,128)(2,1)}, bf16[128,1024]{1,0:T(8,128)(2,1)}, bf16[128,1024]{1,0:T(8,128)(2,1)}) custom-call(s32[2]{0:T(128)S(1)} %pad_add_fusion.scalars, bf16[64,128]{1,0:T(8,128)(2,1)S(1)} %get-tuple-element.48.refs_0_, bf16[64,128]{1,0:T(8,128)(2,1)S(1)} %collective-permute-done.14.refs_1_, ...), custom_call_target="tpu_custom_call" | custom-call | tf_op jit(solution)/shard_map/pallas_call | solution.py:349
  (29 shorter events, 0.3 us)
Async XLA Ops:
  0.7 0.7 copy-start.5
  1.4 0.9 %copy-start = (bf16[128,1024]{1,0:T(8,128)(2,1)S(1)}, bf16[128,1024]{1,0:T(8,128)(2,1)}, u32[]{:S(2)}) copy-start(bf16[128,1024]{1,0:T(8,128)(2,1)} %k_hbm.1) | copy-start | bytes 786436
  2.3 0.9 %copy-start.1 = (bf16[128,1024]{1,0:T(8,128)(2,1)S(1)}, bf16[128,1024]{1,0:T(8,128)(2,1)}, u32[]{:S(2)}) copy-start(bf16[128,1024]{1,0:T(8,128)(2,1)} %v_hbm.1) | copy-start | bytes 786436
  3.3 0.8 %copy-start.2 = (bf16[4,8192]{1,0:T(4,128)(2,1)S(1)}, bf16[4,8192]{1,0:T(4,128)(2,1)}, u32[]{:S(2)}) copy-start(bf16[4,8192]{1,0:T(4,128)(2,1)} %param.8) | copy-start | bytes 196612
  4.1 0.8 %copy-start.3 = (bf16[4,8192]{1,0:T(4,128)(2,1)S(1)}, bf16[4,8192]{1,0:T(4,128)(2,1)}, u32[]{:S(2)}) copy-start(bf16[4,8192]{1,0:T(4,128)(2,1)} %param.9) | copy-start | bytes 196612
  5.0 0.8 %copy-start.4 = (bf16[4,8192]{1,0:T(4,128)(2,1)S(1)}, bf16[4,8192]{1,0:T(4,128)(2,1)}, u32[]{:S(2)}) copy-start(bf16[4,8192]{1,0:T(4,128)(2,1)} %param.10) | copy-start | bytes 196612
  7.3 3.3 %collective-permute-start = (bf16[144,128]{1,0:T(8,128)(2,1)S(1)}, bf16[144,128]{1,0:T(8,128)(2,1)S(1)}, u32[]{:S(2)}, u32[]{:S(2)}) collective-permute-start(bf16[144,128]{1,0:T(8,128)(2,1)S(1)} %get-tuple-element.17), channel_id=1, source_target_pairs={{0,2},{2,0},{4,6},{6,4},{1,3},{3,1},{5,7},{7,5},{8,10},{10,8},{12,... | collective-permute-start | bytes 110600 | tf_op jit(solution)/shard_map/ppermute | solution.py:269
  7.8 4.7 %collective-permute-start.1 = (bf16[144,128]{1,0:T(8,128)(2,1)S(1)}, bf16[144,128]{1,0:T(8,128)(2,1)S(1)}, u32[]{:S(2)}, u32[]{:S(2)}) collective-permute-start(bf16[144,128]{1,0:T(8,128)(2,1)S(1)} %get-tuple-element.18), channel_id=1, source_target_pairs={{0,4},{2,6},{4,0},{6,2},{1,5},{3,7},{5,1},{7,3},{8,12},{10,14},{12... | collective-permute-start | bytes 110600 | tf_op jit(solution)/shard_map/ppermute | solution.py:269
  10.4 3.4 %collective-permute-start.2 = (bf16[144,128]{1,0:T(8,128)(2,1)S(1)}, bf16[144,128]{1,0:T(8,128)(2,1)S(1)}, u32[]{:S(2)}, u32[]{:S(2)}) collective-permute-start(bf16[144,128]{1,0:T(8,128)(2,1)S(1)} %get-tuple-element.19), channel_id=1, source_target_pairs={{0,6},{2,4},{4,2},{6,0},{1,7},{3,5},{5,3},{7,1},{8,14},{10,12},{12... | collective-permute-start | bytes 110600 | tf_op jit(solution)/shard_map/ppermute | solution.py:269
  10.5 14.1 %collective-permute-start.6 = (bf16[4,256,128]{2,1,0:T(8,128)(2,1)S(1)}, bf16[4,256,128]{2,1,0:T(8,128)(2,1)S(1)}, u32[]{:S(2)}, u32[]{:S(2)}) collective-permute-start(bf16[4,256,128]{2,1,0:T(8,128)(2,1)S(1)} %get-tuple-element.21), channel_id=1, source_target_pairs={{0,2},{1,3},{2,0},{3,1},{4,6},{5,7},{6,4},{7,5},{8,10},{9,11},{10,... | collective-permute-start | bytes 786440 | tf_op jit(solution)/shard_map/ppermute | solution.py:269
  13.9 10.2 %collective-permute-start.4 = (bf16[4,144,128]{2,1,0:T(8,128)(2,1)S(1)}, bf16[4,144,128]{2,1,0:T(8,128)(2,1)S(1)}, u32[]{:S(2)}, u32[]{:S(2)}) collective-permute-start(bf16[4,144,128]{2,1,0:T(8,128)(2,1)S(1)} %pad_maximum_fusion.refs_0_), channel_id=1, source_target_pairs={{0,16},{8,24},{16,0},{24,8},{1,17},{9,25},{17,1},{25,9},{2,18},{10... | collective-permute-start | bytes 442376 | tf_op jit(solution)/shard_map/ppermute | solution.py:269
  16.5 12.5 %collective-permute-start.3 = (bf16[4,144,128]{2,1,0:T(8,128)(2,1)S(1)}, bf16[4,144,128]{2,1,0:T(8,128)(2,1)S(1)}, u32[]{:S(2)}, u32[]{:S(2)}) collective-permute-start(bf16[4,144,128]{2,1,0:T(8,128)(2,1)S(1)} %pad_maximum_fusion.refs_0_), channel_id=1, source_target_pairs={{0,8},{8,0},{16,24},{24,16},{1,9},{9,1},{17,25},{25,17},{2,10},{10... | collective-permute-start | bytes 442376 | tf_op jit(solution)/shard_map/ppermute | solution.py:269
  24.0 5.1 %collective-permute-start.5 = (bf16[4,144,128]{2,1,0:T(8,128)(2,1)S(1)}, bf16[4,144,128]{2,1,0:T(8,128)(2,1)S(1)}, u32[]{:S(2)}, u32[]{:S(2)}) collective-permute-start(bf16[4,144,128]{2,1,0:T(8,128)(2,1)S(1)} %collective-permute-done.4.refs_2_), channel_id=1, source_target_pairs={{0,8},{8,0},{16,24},{24,16},{1,9},{9,1},{17,25},{25,17},{2,10},{10... | collective-permute-start | bytes 442376 | tf_op jit(solution)/shard_map/ppermute | solution.py:269
  24.6 5.4 %collective-permute-start.7 = (bf16[2,256,128]{2,1,0:T(8,128)(2,1)S(1)}, bf16[2,256,128]{2,1,0:T(8,128)(2,1)S(1)}, u32[]{:S(2)}, u32[]{:S(2)}) collective-permute-start(bf16[2,256,128]{2,1,0:T(8,128)(2,1)S(1)} %pad_maximum_fusion.2), channel_id=1, source_target_pairs={{0,1},{1,0},{2,3},{3,2},{4,5},{5,4},{6,7},{7,6},{8,9},{9,8},{10,11... | collective-permute-start | bytes 393224 | tf_op jit(solution)/shard_map/ppermute | solution.py:269
  26.2 7.8 %collective-permute-start.8 = (bf16[2,256,128]{2,1,0:T(8,128)(2,1)S(1)}, bf16[2,256,128]{2,1,0:T(8,128)(2,1)S(1)}, u32[]{:S(2)}, u32[]{:S(2)}) collective-permute-start(bf16[2,256,128]{2,1,0:T(8,128)(2,1)S(1)} %pad_maximum_fusion.3), channel_id=1, source_target_pairs={{0,4},{1,5},{2,6},{3,7},{4,0},{5,1},{6,2},{7,3},{8,12},{9,13},{10,... | collective-permute-start | bytes 393224 | tf_op jit(solution)/shard_map/ppermute | solution.py:269
  27.2 6.9 %collective-permute-start.9 = (bf16[2,256,128]{2,1,0:T(8,128)(2,1)S(1)}, bf16[2,256,128]{2,1,0:T(8,128)(2,1)S(1)}, u32[]{:S(2)}, u32[]{:S(2)}) collective-permute-start(bf16[2,256,128]{2,1,0:T(8,128)(2,1)S(1)} %pad_maximum_fusion.4), channel_id=1, source_target_pairs={{0,5},{1,4},{2,7},{3,6},{4,1},{5,0},{6,3},{7,2},{8,13},{9,12},{10,... | collective-permute-start | bytes 393224 | tf_op jit(solution)/shard_map/ppermute | solution.py:269
  36.2 3.7 %collective-permute-start.10 = (f32[8,128]{1,0:T(8,128)S(1)}, f32[8,128]{1,0:T(8,128)S(1)}, u32[]{:S(2)}, u32[]{:S(2)}) collective-permute-start(f32[8,128]{1,0:T(8,128)S(1)} %shard_map.104), channel_id=1, source_target_pairs={{0,8},{8,0},{16,24},{24,16},{1,9},{9,1},{17,25},{25,17},{2,10},{10... | collective-permute-start | bytes 12296 | tf_op jit(solution)/shard_map/ppermute | solution.py:269
  39.9 5.0 %collective-permute-start.11 = (f32[8,128]{1,0:T(8,128)S(1)}, f32[8,128]{1,0:T(8,128)S(1)}, u32[]{:S(2)}, u32[]{:S(2)}) collective-permute-start(f32[8,128]{1,0:T(8,128)S(1)} %log_add_fusion.refs_8_), channel_id=1, source_target_pairs={{0,16},{8,24},{16,0},{24,8},{1,17},{9,25},{17,1},{25,9},{2,18},{10... | collective-permute-start | bytes 12296 | tf_op jit(solution)/shard_map/ppermute | solution.py:269
  48.5 5.5 %collective-permute-start.12 = (bf16[2,256,128]{2,1,0:T(8,128)(2,1)S(1)}, bf16[2,256,128]{2,1,0:T(8,128)(2,1)S(1)}, u32[]{:S(2)}, u32[]{:S(2)}) collective-permute-start(bf16[2,256,128]{2,1,0:T(8,128)(2,1)S(1)} %get-tuple-element.23), channel_id=1, source_target_pairs={{0,8},{8,0},{16,24},{24,16},{1,9},{9,1},{17,25},{25,17},{2,10},{10... | collective-permute-start | bytes 393224 | tf_op jit(solution)/shard_map/ppermute | solution.py:269
  54.1 5.9 %collective-permute-start.13 = (bf16[1,256,128]{2,1,0:T(8,128)(2,1)S(1)}, bf16[1,256,128]{2,1,0:T(8,128)(2,1)S(1)}, u32[]{:S(2)}, u32[]{:S(2)}) collective-permute-start(bf16[1,256,128]{2,1,0:T(8,128)(2,1)S(1)} %slice.115), channel_id=1, source_target_pairs={{0,16},{8,24},{16,0},{24,8},{1,17},{9,25},{17,1},{25,9},{2,18},{10... | collective-permute-start | bytes 196616 | tf_op jit(solution)/shard_map/ppermute | solution.py:269
  56.6 3.5 %collective-permute-start.17 = (bf16[4,256,128]{2,1,0:T(8,128)(2,1)S(1)}, bf16[4,256,128]{2,1,0:T(8,128)(2,1)S(1)}, u32[]{:S(2)}, u32[]{:S(2)}) collective-permute-start(bf16[4,256,128]{2,1,0:T(8,128)(2,1)S(1)} %get-tuple-element.25), channel_id=1, source_target_pairs={{0,2},{1,3},{2,0},{3,1},{4,6},{5,7},{6,4},{7,5},{8,10},{9,11},{10,... | collective-permute-start | bytes 786440 | tf_op jit(solution)/shard_map/ppermute | solution.py:269
  60.1 4.8 %collective-permute-start.16 = (bf16[64,128]{1,0:T(8,128)(2,1)S(1)}, bf16[64,128]{1,0:T(8,128)(2,1)S(1)}, u32[]{:S(2)}, u32[]{:S(2)}) collective-permute-start(bf16[64,128]{1,0:T(8,128)(2,1)S(1)} %get-tuple-element.45), channel_id=1, source_target_pairs={{0,6},{2,4},{4,2},{6,0},{1,7},{3,5},{5,3},{7,1},{8,14},{10,12},{12... | collective-permute-start | bytes 49160 | tf_op jit(solution)/shard_map/ppermute | solution.py:269
  60.2 9.8 %collective-permute-start.18 = (bf16[2,256,128]{2,1,0:T(8,128)(2,1)S(1)}, bf16[2,256,128]{2,1,0:T(8,128)(2,1)S(1)}, u32[]{:S(2)}, u32[]{:S(2)}) collective-permute-start(bf16[2,256,128]{2,1,0:T(8,128)(2,1)S(1)} %pad_maximum_fusion.6), channel_id=1, source_target_pairs={{0,1},{1,0},{2,3},{3,2},{4,5},{5,4},{6,7},{7,6},{8,9},{9,8},{10,11... | collective-permute-start | bytes 393224 | tf_op jit(solution)/shard_map/ppermute | solution.py:269
  60.5 9.5 %collective-permute-start.19 = (bf16[2,256,128]{2,1,0:T(8,128)(2,1)S(1)}, bf16[2,256,128]{2,1,0:T(8,128)(2,1)S(1)}, u32[]{:S(2)}, u32[]{:S(2)}) collective-permute-start(bf16[2,256,128]{2,1,0:T(8,128)(2,1)S(1)} %pad_maximum_fusion.7), channel_id=1, source_target_pairs={{0,4},{1,5},{2,6},{3,7},{4,0},{5,1},{6,2},{7,3},{8,12},{9,13},{10,... | collective-permute-start | bytes 393224 | tf_op jit(solution)/shard_map/ppermute | solution.py:269
  61.6 8.4 %collective-permute-start.20 = (bf16[2,256,128]{2,1,0:T(8,128)(2,1)S(1)}, bf16[2,256,128]{2,1,0:T(8,128)(2,1)S(1)}, u32[]{:S(2)}, u32[]{:S(2)}) collective-permute-start(bf16[2,256,128]{2,1,0:T(8,128)(2,1)S(1)} %pad_maximum_fusion.8), channel_id=1, source_target_pairs={{0,5},{1,4},{2,7},{3,6},{4,1},{5,0},{6,3},{7,2},{8,13},{9,12},{10,... | collective-permute-start | bytes 393224 | tf_op jit(solution)/shard_map/ppermute | solution.py:269
  63.9 6.0 %collective-permute-start.15 = (bf16[64,128]{1,0:T(8,128)(2,1)S(1)}, bf16[64,128]{1,0:T(8,128)(2,1)S(1)}, u32[]{:S(2)}, u32[]{:S(2)}) collective-permute-start(bf16[64,128]{1,0:T(8,128)(2,1)S(1)} %get-tuple-element.46), channel_id=1, source_target_pairs={{0,4},{2,6},{4,0},{6,2},{1,5},{3,7},{5,1},{7,3},{8,12},{10,14},{12... | collective-permute-start | bytes 49160 | tf_op jit(solution)/shard_map/ppermute | solution.py:269
  64.9 5.1 %collective-permute-start.14 = (bf16[64,128]{1,0:T(8,128)(2,1)S(1)}, bf16[64,128]{1,0:T(8,128)(2,1)S(1)}, u32[]{:S(2)}, u32[]{:S(2)}) collective-permute-start(bf16[64,128]{1,0:T(8,128)(2,1)S(1)} %get-tuple-element.47), channel_id=1, source_target_pairs={{0,2},{2,0},{4,6},{6,4},{1,3},{3,1},{5,7},{7,5},{8,10},{10,8},{12,... | collective-permute-start | bytes 49160 | tf_op jit(solution)/shard_map/ppermute | solution.py:269

commit v3 on v2

v3 whole, which is shorter than its diff:
```python
import functools

import jax
import jax.numpy as jnp
from jax import lax
from jax.experimental import pallas as pl
from jax.experimental.pallas import tpu as pltpu
from jax.sharding import Mesh, PartitionSpec as P

DH = 128
KVH = 8
RESP_LEN = 64
SCALE = DH ** (-0.5)
MASKED_SCORE = -1e30
DEAD_LSE = 1e30
PIECES = 3
STAT_ROWS = 16
STEP_LINES = 1024
PARAMS = pltpu.CompilerParams(vmem_limit_bytes=48 * 1024 * 1024)
HBM = pl.BlockSpec(memory_space=pltpu.HBM)
SMEM = pl.BlockSpec(memory_space=pltpu.SMEM)
VMEM = pl.BlockSpec(memory_space=pltpu.VMEM)

NEAR = 2
KEEP = (0, 1, 4, 5)


def split_pieces(x):
    first = x.astype(jnp.bfloat16)
    rest = x - first.astype(jnp.float32)
    second = rest.astype(jnp.bfloat16)
    third = (rest - second.astype(jnp.float32)).astype(jnp.bfloat16)
    return first, second, third


def shift_of(n):
    assert n & (n - 1) == 0
    return n.bit_length() - 1


def column_of(member, groups, heads):
    head_index, group_index = member & (heads - 1), member >> shift_of(heads)
    return pl.multiple_of((head_index * groups + group_index) * DH, DH)


def pack_kv_kernel(groups, heads, scalars, k_hbm, v_hbm, keep_ref, send_ref, sems):
    tokens = k_hbm.shape[0]
    copies = []
    for i, j in enumerate(KEEP):
        for ref, peer in ((send_ref, j ^ NEAR), (keep_ref, j)):
            columns = pl.ds(column_of(scalars[0] ^ peer, groups, heads), DH)
            copies.append((k_hbm.at[:, columns], ref.at[i, 0:tokens, :]))
            copies.append((v_hbm.at[:, columns], ref.at[i, tokens : 2 * tokens, :]))
    copies = [pltpu.make_async_copy(s, t, sems.at[n]) for n, (s, t) in enumerate(copies)]
    for copy in copies:
        copy.start()
    for copy in copies:
        copy.wait()


def pack_rows_kernel(parts, groups, q_hbm, o_grad_hbm, o_hbm, lse_hbm, rows_ref, o_ref, lse_ref, sems):
    rows, own_heads = lse_ref.shape
    lines = o_ref.shape[0] // groups
    copies = [(lse_hbm, lse_ref), (o_hbm, o_ref)]
    for g in range(groups):
        held = pl.ds(g * lines, lines)
        for part in range(parts):
            slab = rows_ref.at[part * groups + g]
            copies.append((q_hbm.at[held, :], slab.at[0:lines, :]))
            copies.append((o_grad_hbm.at[held, :], slab.at[lines : 2 * lines, :]))
    copies = [pltpu.make_async_copy(s, t, sems.at[n]) for n, (s, t) in enumerate(copies)]
    for copy in copies:
        copy.start()

    wide = 2 * lines
    shape = (own_heads, wide)
    head_ids = lax.broadcasted_iota(jnp.int32, shape, 0)
    line_heads = (lax.broadcasted_iota(jnp.int32, shape, 1) & (lines - 1)) >> shift_of(rows)
    group_heads = lines // rows
    chosen = [
        (head_ids == line_heads + g * group_heads).astype(jnp.bfloat16) for g in range(groups)
    ]
    shape = (rows, wide)
    own_row = lax.broadcasted_iota(jnp.int32, shape, 0) == (
        lax.broadcasted_iota(jnp.int32, shape, 1) & (rows - 1)
    )
    for copy in copies:
        copy.wait()
    pieces = split_pieces(lse_ref[...])
    for g in range(groups):
        stats = []
        for piece in pieces:
            spread = jnp.dot(piece, chosen[g], preferred_element_type=jnp.float32)
            stats.append(jnp.sum(jnp.where(own_row, spread, 0.0), axis=0, keepdims=True))
        o_grad = rows_ref[g, lines : 2 * lines, :].astype(jnp.float32)
        product = o_grad * o_ref[g * lines : (g + 1) * lines, :].astype(jnp.float32)
        dots = jnp.sum(jnp.concatenate([product, product], axis=0).T, axis=0, keepdims=True)
        stats += [piece.astype(jnp.float32) for piece in split_pieces(dots)]
        stats.append(jnp.zeros((STAT_ROWS - 2 * PIECES, wide), jnp.float32))
        stat_block = jnp.concatenate(stats, axis=0).astype(jnp.bfloat16)
        for part in range(parts):
            rows_ref[part * groups + g, wide:, :] = stat_block


def pair_starts(scalars, i, tokens):
    first = scalars[1] * KVH
    return [(first + (scalars[0] ^ KEEP[i] ^ other)) * tokens for other in (0, NEAR)]


def pair_keys(ref, tokens):
    return jnp.concatenate([ref[0, 0:tokens, :], ref[1, 0:tokens, :]], axis=0)


def pair_values(ref, tokens):
    return jnp.concatenate([ref[0, tokens : 2 * tokens, :], ref[1, tokens : 2 * tokens, :]], axis=0)


def response_of(source, rows):
    return source * rows // RESP_LEN


def stat_kernel(rows, tokens, scalars, prompt_end, rows_ref, *refs):
    pair_refs, lse_ref = refs[:-1], refs[-1]
    sources, lines = rows_ref.shape[0], (rows_ref.shape[1] - STAT_ROWS) // 2
    step = 256 // lines
    count = step * lines
    offset = lax.broadcasted_iota(jnp.int32, (tokens, count), 0)
    for c in range(0, sources, step):
        q = rows_ref[c : c + step, 0:lines, :].reshape(count, DH)
        end = prompt_end[response_of(c, rows)]
        scores = []
        for i, ref in enumerate(pair_refs):
            part = lax.dot_general(
                pair_keys(ref, tokens),
                q,
                (((1,), (1,)), ((), ())),
                preferred_element_type=jnp.float32,
            )
            visible = jnp.concatenate(
                [offset < end - start for start in pair_starts(scalars, i, tokens)], axis=0
            )
            scores.append(jnp.where(visible, part * SCALE, MASKED_SCORE))
        scores = jnp.concatenate(scores, axis=0)
        peak = jnp.max(scores, axis=0, keepdims=True)
        total = jnp.sum(jnp.exp(scores - peak), axis=0, keepdims=True)
        lse = peak + jnp.log(total)
        for n in range(count // DH):
            at = c * lines // DH + n
            lse_ref[at : at + 1, :] = lse[:, n * DH : (n + 1) * DH]


def line_values(rows_ref, sources, lines, first_piece):
    low = lax.broadcasted_iota(jnp.int32, (1, 2 * lines), 1) < lines
    out = []
    for n in sources[::2]:
        held = [
            rows_ref[s, 2 * lines : 2 * lines + STAT_ROWS, :].astype(jnp.float32)
            for s in (n, n + 1)
        ]
        total = None
        for k in range(first_piece, first_piece + PIECES):
            piece = jnp.where(low, held[0][k : k + 1], held[1][k : k + 1])
            total = piece if total is None else total + piece
        out.append(total)
    return jnp.concatenate(out, axis=1)


def grad_kernel(parts, rows, tokens, scalars, resp_len, prompt_end, rows_ref, *refs):
    pair_refs, refs = refs[: len(KEEP)], refs[len(KEEP) :]
    lse_refs, refs = refs[:parts], refs[parts:]
    dq_ref, dkv_keep_ref, dkv_send_ref, dk_acc, dv_acc = refs
    all_sources, lines = rows_ref.shape[0], (rows_ref.shape[1] - STAT_ROWS) // 2
    step = min(all_sources, STEP_LINES // lines)
    count = step * lines
    offset = lax.broadcasted_iota(jnp.int32, (tokens, count), 0)
    lane = lax.broadcasted_iota(jnp.int32, (1, 2 * lines), 1)
    for c in range(0, all_sources, step):
        sources = range(c, c + step)
        q = rows_ref[c : c + step, 0:lines, :].reshape(count, DH)
        o_grad = rows_ref[c : c + step, lines : 2 * lines, :].reshape(count, DH)
        self_lse = line_values(rows_ref, sources, lines, 0)
        dots = line_values(rows_ref, sources, lines, PIECES)
        live, end = [], []
        for s in sources[::2]:
            row = (s * rows + jnp.where(lane < lines, 0, rows) + (lane & (rows - 1))) & (RESP_LEN - 1)
            live.append(row < resp_len[response_of(s, rows)])
            end.append(jnp.full(lane.shape, prompt_end[response_of(s, rows)], jnp.int32))
        live = jnp.concatenate(live, axis=1)
        end = jnp.concatenate(end, axis=1)
        first = c * lines // DH
        part_lse = [
            jnp.concatenate([ref[n : n + 1, :] for n in range(first, first + count // DH)], axis=1)
            for ref in lse_refs
        ]
        peak = functools.reduce(jnp.maximum, part_lse, self_lse)
        total = sum(jnp.exp(x - peak) for x in part_lse) + jnp.exp(self_lse - peak)
        lse = jnp.where(live, peak + jnp.log(total), DEAD_LSE)
        dq_t = jnp.zeros((DH, count), jnp.float32)
        for i, ref in enumerate(pair_refs):
            k, v = pair_keys(ref, tokens), pair_values(ref, tokens)
            scores = lax.dot_general(
                k, q, (((1,), (1,)), ((), ())), preferred_element_type=jnp.float32
            )
            visible = jnp.concatenate(
                [offset < end - start for start in pair_starts(scalars, i, tokens)], axis=0
            )
            prob = jnp.where(visible, jnp.exp(scores * SCALE - lse), 0.0)
            dprob = lax.dot_general(
                v, o_grad, (((1,), (1,)), ((), ())), preferred_element_type=jnp.float32
            )
            dscore = (prob * (dprob - dots)).astype(jnp.bfloat16)
            dv = jnp.dot(prob.astype(jnp.bfloat16), o_grad, preferred_element_type=jnp.float32)
            dk = jnp.dot(dscore, q, preferred_element_type=jnp.float32) * SCALE
            dq_t = dq_t + jnp.dot(k.T, dscore, preferred_element_type=jnp.float32)
            if c > 0:
                dk = dk + dk_acc[i]
                dv = dv + dv_acc[i]
            if c + step < all_sources:
                dk_acc[i] = dk
                dv_acc[i] = dv
            else:
                for n, out in enumerate((dkv_keep_ref, dkv_send_ref)):
                    inner = slice(n * tokens, (n + 1) * tokens)
                    out[i, 0:tokens, :] = dk[inner].astype(jnp.bfloat16)
                    out[i, tokens : 2 * tokens, :] = dv[inner].astype(jnp.bfloat16)
        dq_ref[c : c + step] = (dq_t * SCALE).T.astype(jnp.bfloat16).reshape(step, lines, DH)


def unpack_kernel(parts, groups, heads, scalars, dq_ref, *refs):
    pair_refs, (out_q_ref, out_k_ref, out_v_ref) = refs[: len(KEEP)], refs[len(KEEP) :]
    lines = dq_ref.shape[1]
    tokens = out_k_ref.shape[0]
    for g in range(groups):
        total = dq_ref[g].astype(jnp.float32)
        for part in range(1, parts):
            total = total + dq_ref[part * groups + g].astype(jnp.float32)
        out_q_ref[g * lines : (g + 1) * lines, :] = total.astype(jnp.bfloat16)
    for i, ref in enumerate(pair_refs):
        for n, other in enumerate((0, NEAR)):
            columns = pl.ds(column_of(scalars[0] ^ KEEP[i] ^ other, groups, heads), DH)
            out_k_ref[:, columns] = ref[n, 0:tokens, :]
            out_v_ref[:, columns] = ref[n, tokens : 2 * tokens, :]


def swap(x, axis, distance, size):
    return lax.ppermute(x, axis, [(i, i ^ distance) for i in range(size)])


def swap_pairs(keep, send):
    members = ("group", "head")
    came = swap(send, members, NEAR, KVH)
    pairs = [jnp.stack([keep[i], came[i]]) for i in range(len(KEEP))]
    return [swap(x, members, j, KVH) if j else x for x, j in zip(pairs, KEEP)]


def exchange_rows(x, parts, groups, in_one_step):
    def one_step(x):
        return lax.all_to_all(x, ("part", "group"), split_axis=0, concat_axis=0, tiled=True)

    def two_steps(x):
        y = x.reshape(parts, groups, *x.shape[1:])
        y = lax.all_to_all(y, "group", split_axis=1, concat_axis=1, tiled=True)
        y = lax.all_to_all(y, "part", split_axis=0, concat_axis=0, tiled=True)
        return y.reshape(x.shape)

    return lax.cond(in_one_step, one_step, two_steps, x)


def shards(parts, groups, heads, queries, grad_out, outputs, lse_self, keys, values, resp_len, prompt_end):
    rows = queries.shape[0]
    own_heads = queries.shape[1] // DH
    own_lines = rows * own_heads
    lines = own_lines // groups
    tokens = keys.shape[0]
    sources = parts * groups
    assert 2 * lines == DH and RESP_LEN % (256 // lines * rows) == 0
    member = lax.axis_index("group") * heads + lax.axis_index("head")
    scalars = jnp.stack([member, lax.axis_index("part")]).astype(jnp.int32)
    in_one_step = prompt_end[0] > 0

    def as_lines(x):
        return x.reshape(rows, own_heads, DH).transpose(1, 0, 2).reshape(own_lines, DH)

    def in_hbm(x):
        return pltpu.with_memory_space_constraint(x, pltpu.HBM)

    half_shape = jax.ShapeDtypeStruct((len(KEEP), 2 * tokens, DH), jnp.bfloat16)
    kv_keep, kv_send = pl.pallas_call(
        functools.partial(pack_kv_kernel, groups, heads),
        in_specs=[SMEM] + [HBM] * 2,
        out_specs=[VMEM] * 2,
        out_shape=[half_shape] * 2,
        scratch_shapes=[pltpu.SemaphoreType.DMA((4 * len(KEEP),))],
        compiler_params=PARAMS,
    )(scalars, in_hbm(keys), in_hbm(values))
    row_block = pl.pallas_call(
        functools.partial(pack_rows_kernel, parts, groups),
        in_specs=[HBM] * 4,
        out_specs=VMEM,
        out_shape=jax.ShapeDtypeStruct((sources, 2 * lines + STAT_ROWS, DH), jnp.bfloat16),
        scratch_shapes=[
            pltpu.VMEM((own_lines, DH), jnp.bfloat16),
            pltpu.VMEM(lse_self.shape, jnp.float32),
            pltpu.SemaphoreType.DMA((2 + 2 * sources,)),
        ],
        compiler_params=PARAMS,
    )(in_hbm(as_lines(queries)), in_hbm(as_lines(grad_out)), in_hbm(as_lines(outputs)), in_hbm(lse_self))
    pairs = swap_pairs(kv_keep, kv_send)
    row_block = exchange_rows(row_block, parts, groups, in_one_step)

    lse = pl.pallas_call(
        functools.partial(stat_kernel, rows, tokens),
        in_specs=[SMEM] * 2 + [VMEM] * (1 + len(KEEP)),
        out_shape=jax.ShapeDtypeStruct((sources * lines // DH, DH), jnp.float32),
        compiler_params=PARAMS,
    )(scalars, prompt_end, row_block, *pairs)
    every_lse = [lse] + [swap(lse, "part", d, parts) for d in range(1, parts)]

    acc = pltpu.VMEM((len(KEEP), 2 * tokens, DH), jnp.float32)
    dq, dkv_keep, dkv_send = pl.pallas_call(
        functools.partial(grad_kernel, parts, rows, tokens),
        in_specs=[SMEM] * 3 + [VMEM] * (1 + len(KEEP) + parts),
        out_shape=[jax.ShapeDtypeStruct((sources, lines, DH), jnp.bfloat16)] + [half_shape] * 2,
        scratch_shapes=[acc] * 2,
        compiler_params=PARAMS,
    )(scalars, resp_len, prompt_end, row_block, *pairs, *every_lse)

    pairs = swap_pairs(dkv_keep, dkv_send)
    dq = exchange_rows(dq, parts, groups, in_one_step)
    out_q, out_k, out_v = pl.pallas_call(
        functools.partial(unpack_kernel, parts, groups, heads),
        in_specs=[SMEM] + [VMEM] * (1 + len(KEEP)),
        out_shape=[
            jax.ShapeDtypeStruct((own_lines, DH), jnp.bfloat16),
            jax.ShapeDtypeStruct(keys.shape, jnp.bfloat16),
            jax.ShapeDtypeStruct(values.shape, jnp.bfloat16),
        ],
        compiler_params=PARAMS,
    )(scalars, dq, *pairs)
    out_q = out_q.reshape(own_heads, rows, DH).transpose(1, 0, 2).reshape(rows, own_heads * DH)
    return out_q, out_k, out_v


def solution(mesh):
    ctx, heads = mesh.shape["ctx"], mesh.shape["head"]
    groups = KVH // heads
    parts = ctx // groups
    fine = Mesh(mesh.devices.reshape(parts, groups, heads), ("part", "group", "head"))
    rows = P(("part", "group"), "head")
    tokens = P(("part", "group", "head"), None)
    return jax.shard_map(
        functools.partial(shards, parts, groups, heads),
        mesh=fine,
        in_specs=(rows, rows, rows, rows, tokens, tokens, P(), P()),
        out_specs=(rows, tokens, tokens),
        check_vma=False,
    )
```

time: 71.9 us -> 68.6 us (0.954)
  blocking collectives: 0 us -> 37.1 us
  waiting for transfers between devices: 30.7 us -> 5.06 us
  starting transfers between devices: 24.5 us -> 13.3 us
  local copies, waits for them, and re-layouts: 5.19 us -> 0.07 us
  Pallas kernels: 8.73 us -> 10.4 us
    all_to_all x0 -> x2, blocking collectives: none -> 37.1 us  [one_step(): lax.all_to_all(x, ('part', 'group'), split_axis=0, concat_axis=0, tiled=T...]
    ppermute x21 -> x11, waiting for transfers between devices: 30.7 us -> 5.06 us  [swap(): return lax.ppermute(x, axis, [(i, i ^ distance) for i in range(size)])]
    ppermute x21 -> x11, starting transfers between devices: 24.5 us -> 13.3 us  [swap(): return lax.ppermute(x, axis, [(i, i ^ distance) for i in range(size)])]
    unnamed x12 -> x0, local copies, waits for them, and re-layouts: 5.1 us -> none
    pallas_call x4 -> x5, Pallas kernels: 8.73 us -> 10.4 us  [the longest x1 3.5 us: shards(): pl.pallas_call(functools.partial(grad_kernel, parts, rows, tokens), in_sp...]
  transfers between devices with their start and end apart: 21 -> 11, of which waited for: 11 -> 4; matrix products, arithmetic and copies ran while one was open for 0% -> 0% of each run, Pallas kernels for 0% -> 2%
where the time goes in v3:
time: 68.6 us; the launch traced here: 68.3 us
  blocking collectives  37.1 us (54%)
  starting transfers between devices  13.3 us (19%)
  Pallas kernels  10.4 us (15%)
  waiting for transfers between devices  5.06 us (7%)
  between operations  2.09 us (3%)
    all_to_all x2, blocking collectives, one_step(): lax.all_to_all(x, ('part', 'group'), split_axis=0, concat_axis=0, tiled=T...  37.1 us
    ppermute x11, starting transfers between devices, swap(): return lax.ppermute(x, axis, [(i, i ^ distance) for i in range(size)])  13.3 us
    ppermute x11, waiting for transfers between devices, swap(): return lax.ppermute(x, axis, [(i, i ^ distance) for i in range(size)])  5.06 us
    pallas_call x1, Pallas kernels, shards(): pl.pallas_call(functools.partial(grad_kernel, parts, rows, tokens), in_sp...  3.5 us
    pallas_call x1, Pallas kernels, shards(): pl.pallas_call(functools.partial(stat_kernel, rows, tokens), in_specs=[SM...  2.14 us
    pallas_call x1, Pallas kernels, shards(): pl.pallas_call(functools.partial(pack_kv_kernel, groups, heads), in_specs...  1.7 us
    pallas_call x1, Pallas kernels, shards(): pl.pallas_call(functools.partial(pack_rows_kernel, parts, groups), in_spe...  1.6 us
    pallas_call x1, Pallas kernels, shards(): pl.pallas_call(functools.partial(unpack_kernel, parts, groups, heads), in...  1.5 us
  transfers between devices with their start and end apart: 11, of which 4 were waited for; matrix products, arithmetic and copies ran while one was open for 0% of the time, Pallas kernels for 2%

profile of v3, /device:TPU:0, one launch (start us, length us, event | category | flops | bytes accessed | tf_op | source)
XLA Modules:
  0.0 68.3 jit_solution(18424206597707740033)
XLA Ops:
  0.6 0.1 pad_add_fusion.scalars
  0.7 1.7 %shard_map.104 = (bf16[4,256,128]{2,1,0:T(8,128)(2,1)S(1)}, bf16[4,256,128]{2,1,0:T(8,128)(2,1)S(1)}) custom-call(s32[2]{0:T(128)S(1)} %pad_add_fusion.scalars, bf16[128,1024]{1,0:T(8,128)(2,1)} %k_hbm.1, bf16[128,1024]{1,0:T(8,128)(2,1)} %v_hbm.1), custom_call_target="tpu_custom_call" | custom-call | tf_op jit(solution)/shard_map/pallas_call | solution.py:288
  2.4 0.5 collective-permute-start
  3.0 1.1 %collective-permute-done = bf16[4,256,128]{2,1,0:T(8,128)(2,1)S(1)} collective-permute-done((bf16[4,256,128]{2,1,0:T(8,128)(2,1)S(1)}, bf16[4,256,128]{2,1,0:T(8,128)(2,1)S(1)}, u32[]{:S(2)}, u32[]{:S(2)}) %collective-permute-start) | collective-permute-done | bytes 262176 | tf_op jit(solution)/shard_map/ppermute | solution.py:246
  4.1 2.9 %collective-permute-start.1 = (bf16[2,256,128]{2,1,0:T(8,128)(2,1)S(1)}, bf16[2,256,128]{2,1,0:T(8,128)(2,1)S(1)}, u32[]{:S(2)}, u32[]{:S(2)}) collective-permute-start(bf16[2,256,128]{2,1,0:T(8,128)(2,1)S(1)} %pad_maximum_fusion.1), channel_id=1, source_target_pairs={{0,1},{1,0},{2,3},{3,2},{4,5},{5,4},{6,7},{7,6},{8,9},{9,8},{10,11... | collective-permute-start | bytes 393224 | tf_op jit(solution)/shard_map/ppermute | solution.py:246
  7.1 1.6 %collective-permute-start.2 = (bf16[2,256,128]{2,1,0:T(8,128)(2,1)S(1)}, bf16[2,256,128]{2,1,0:T(8,128)(2,1)S(1)}, u32[]{:S(2)}, u32[]{:S(2)}) collective-permute-start(bf16[2,256,128]{2,1,0:T(8,128)(2,1)S(1)} %pad_maximum_fusion.2), channel_id=1, source_target_pairs={{0,4},{1,5},{2,6},{3,7},{4,0},{5,1},{6,2},{7,3},{8,12},{9,13},{10,... | collective-permute-start | bytes 393224 | tf_op jit(solution)/shard_map/ppermute | solution.py:246
  8.7 0.1 collective-permute-start.3
  9.4 1.6 %shard_map.103 = bf16[16,144,128]{2,1,0:T(8,128)(2,1)S(1)} custom-call(bf16[256,128]{1,0:T(8,128)(2,1)} %bitcast.31, bf16[256,128]{1,0:T(8,128)(2,1)} %bitcast.32, bf16[256,128]{1,0:T(8,128)(2,1)} %bitcast.33, f32[4,64]{1,0:T(4,128)} %lse_hbm.1), custom_call_target="tpu_custom_call" | custom-call | tf_op jit(solution)/shard_map/pallas_call | solution.py:296
  11.0 23.5 %conditional.2 = (bf16[16,144,128]{2,1,0:T(8,128)(2,1)S(1)}) conditional(s32[]{:T(128)} %bitcast.6, bf16[16,144,128]{2,1,0:T(8,128)(2,1)S(1)} %shard_map.103, bf16[16,144,128]{2,1,0:T(8,128)(2,1)S(1)} %shard_map.103), branch_computations={%region_0.0_spmd, %region_1.0_spmd} | conditional | bytes 4718600 | solution.py:266
  11.0 23.5 %all_to_all.26 = bf16[16,144,128]{2,1,0:T(8,128)(2,1)S(1)} all-to-all(bf16[16,144,128]{2,1,0:T(8,128)(2,1)S(1)} %param.1), channel_id=1, replica_groups=mesh['part'=4,'group'=4,'head'=2] {'part','group'}, dimensions={0} | all-to-all | bytes 1179648 | tf_op jit(solution)/shard_map/cond/branch_1_fun/all_to_all | solution.py:258
  34.6 0.0 collective-permute-done.1.refs_1_
  34.6 0.0 collective-permute-done.2.refs_2_
  34.6 0.0 collective-permute-done.3.refs_3_
  34.6 2.1 %shard_map.105.refs_4_ = f32[8,128]{1,0:T(8,128)S(1)} custom-call(s32[2]{0:T(128)S(1)} %pad_add_fusion.scalars, s32[1]{0:T(128)S(6)} %copy.32.prompt_end, bf16[16,144,128]{2,1,0:T(8,128)(2,1)S(1)} %get-tuple-element.45.rows_ref, bf16[2,256,128]{2,1,0:T(8,128)(2,1)S(1)} %pad_maximum_fusion.refs_0_, bf16[2,256,128]{2,1,0:T(8,128)(2,1)S(1)} %collective-permute-done.1.refs_1_, ...), custom_call_target="tpu_custom_call" | custom-call | tf_op jit(solution)/shard_map/pallas_call | solution.py:311
  36.7 0.7 %collective-permute-start.4 = (f32[8,128]{1,0:T(8,128)S(1)}, f32[8,128]{1,0:T(8,128)S(1)}, u32[]{:S(2)}, u32[]{:S(2)}) collective-permute-start(f32[8,128]{1,0:T(8,128)S(1)} %shard_map.105.refs_4_), channel_id=1, source_target_pairs={{0,8},{8,0},{16,24},{24,16},{1,9},{9,1},{17,25},{25,17},{2,10},{10... | collective-permute-start | bytes 12296 | tf_op jit(solution)/shard_map/ppermute | solution.py:246
  37.4 1.4 %collective-permute-start.5 = (f32[8,128]{1,0:T(8,128)S(1)}, f32[8,128]{1,0:T(8,128)S(1)}, u32[]{:S(2)}, u32[]{:S(2)}) collective-permute-start(f32[8,128]{1,0:T(8,128)S(1)} %shard_map.105.refs_4_), channel_id=1, source_target_pairs={{0,16},{8,24},{16,0},{24,8},{1,17},{9,25},{17,1},{25,9},{2,18},{10... | collective-permute-start | bytes 12296 | tf_op jit(solution)/shard_map/ppermute | solution.py:246
  38.8 2.3 %collective-permute-start.6 = (f32[8,128]{1,0:T(8,128)S(1)}, f32[8,128]{1,0:T(8,128)S(1)}, u32[]{:S(2)}, u32[]{:S(2)}) collective-permute-start(f32[8,128]{1,0:T(8,128)S(1)} %shard_map.105.refs_4_), channel_id=1, source_target_pairs={{0,24},{8,16},{16,8},{24,0},{1,25},{9,17},{17,9},{25,1},{2,26},{10... | collective-permute-start | bytes 12296 | tf_op jit(solution)/shard_map/ppermute | solution.py:246
  41.8 0.0 collective-permute-done.4.refs_5_
  41.8 0.1 collective-permute-done.5.refs_6_
  42.0 2.3 %collective-permute-done.6.refs_7_ = f32[8,128]{1,0:T(8,128)S(1)} collective-permute-done((f32[8,128]{1,0:T(8,128)S(1)}, f32[8,128]{1,0:T(8,128)S(1)}, u32[]{:S(2)}, u32[]{:S(2)}) %collective-permute-start.6) | collective-permute-done | bytes 4128 | tf_op jit(solution)/shard_map/ppermute | solution.py:246
  44.2 3.5 %shard_map.106 = (bf16[16,64,128]{2,1,0:T(8,128)(2,1)S(1)}, bf16[4,256,128]{2,1,0:T(8,128)(2,1)S(1)}, bf16[4,256,128]{2,1,0:T(8,128)(2,1)S(1)}) custom-call(s32[2]{0:T(128)S(1)} %pad_add_fusion.scalars, s32[1]{0:T(128)S(6)} %copy.31.resp_len, s32[1]{0:T(128)S(6)} %copy.32.prompt_end, bf16[16,144,128]{2,1,0:T(8,128)(2,1)S(1)} %get-tuple-element.45.rows_ref, ...), custom_call_target="tpu_custom_call" | custom-call | tf_op jit(solution)/shard_map/pallas_call | solution.py:320
  47.7 0.1 collective-permute-start.7
  47.9 1.5 %collective-permute-done.7 = bf16[4,256,128]{2,1,0:T(8,128)(2,1)S(1)} collective-permute-done((bf16[4,256,128]{2,1,0:T(8,128)(2,1)S(1)}, bf16[4,256,128]{2,1,0:T(8,128)(2,1)S(1)}, u32[]{:S(2)}, u32[]{:S(2)}) %collective-permute-start.7) | collective-permute-done | bytes 262176 | tf_op jit(solution)/shard_map/ppermute | solution.py:246
  49.4 1.6 %collective-permute-start.8 = (bf16[2,256,128]{2,1,0:T(8,128)(2,1)S(1)}, bf16[2,256,128]{2,1,0:T(8,128)(2,1)S(1)}, u32[]{:S(2)}, u32[]{:S(2)}) collective-permute-start(bf16[2,256,128]{2,1,0:T(8,128)(2,1)S(1)} %pad_maximum_fusion.5), channel_id=1, source_target_pairs={{0,1},{1,0},{2,3},{3,2},{4,5},{5,4},{6,7},{7,6},{8,9},{9,8},{10,11... | collective-permute-start | bytes 393224 | tf_op jit(solution)/shard_map/ppermute | solution.py:246
  51.0 0.8 %collective-permute-start.9 = (bf16[2,256,128]{2,1,0:T(8,128)(2,1)S(1)}, bf16[2,256,128]{2,1,0:T(8,128)(2,1)S(1)}, u32[]{:S(2)}, u32[]{:S(2)}) collective-permute-start(bf16[2,256,128]{2,1,0:T(8,128)(2,1)S(1)} %pad_maximum_fusion.6), channel_id=1, source_target_pairs={{0,4},{1,5},{2,6},{3,7},{4,0},{5,1},{6,2},{7,3},{8,12},{9,13},{10,... | collective-permute-start | bytes 393224 | tf_op jit(solution)/shard_map/ppermute | solution.py:246
  51.7 1.4 %collective-permute-start.10 = (bf16[2,256,128]{2,1,0:T(8,128)(2,1)S(1)}, bf16[2,256,128]{2,1,0:T(8,128)(2,1)S(1)}, u32[]{:S(2)}, u32[]{:S(2)}) collective-permute-start(bf16[2,256,128]{2,1,0:T(8,128)(2,1)S(1)} %pad_maximum_fusion.7), channel_id=1, source_target_pairs={{0,5},{1,4},{2,7},{3,6},{4,1},{5,0},{6,3},{7,2},{8,13},{9,12},{10,... | collective-permute-start | bytes 393224 | tf_op jit(solution)/shard_map/ppermute | solution.py:246
  53.1 13.6 %conditional.3 = (bf16[16,64,128]{2,1,0:T(8,128)(2,1)S(1)}) conditional(s32[]{:T(128)} %bitcast.6, bf16[16,64,128]{2,1,0:T(8,128)(2,1)S(1)} %get-tuple-element.23, bf16[16,64,128]{2,1,0:T(8,128)(2,1)S(1)} %get-tuple-element.23), branch_computations={%region_2.0_spmd, %region_3.0_spmd} | conditional | bytes 2097160 | solution.py:266
  53.1 13.6 %all_to_all.29 = bf16[16,64,128]{2,1,0:T(8,128)(2,1)S(1)} all-to-all(bf16[16,64,128]{2,1,0:T(8,128)(2,1)S(1)} %param.3), channel_id=1, replica_groups=mesh['part'=4,'group'=4,'head'=2] {'part','group'}, dimensions={0} | all-to-all | bytes 524288 | tf_op jit(solution)/shard_map/cond/branch_1_fun/all_to_all | solution.py:258
  66.7 0.0 collective-permute-done.8.refs_1_
  66.7 0.0 collective-permute-done.9.refs_2_
  66.8 0.0 collective-permute-done.10.refs_3_
  66.8 1.5 %shard_map.107 = (bf16[256,128]{1,0:T(8,128)(2,1)}, bf16[128,1024]{1,0:T(8,128)(2,1)}, bf16[128,1024]{1,0:T(8,128)(2,1)}) custom-call(s32[2]{0:T(128)S(1)} %pad_add_fusion.scalars, bf16[16,64,128]{2,1,0:T(8,128)(2,1)S(1)} %get-tuple-element.46.dq_ref, bf16[2,256,128]{2,1,0:T(8,128)(2,1)S(1)} %pad_maximum_fusion.4.refs_0_, ...), custom_call_target="tpu_custom_call" | custom-call | tf_op jit(solution)/shard_map/pallas_call | solution.py:330
  (12 shorter events, 0.2 us)
Async XLA Ops:
  2.4 1.7 %collective-permute-start = (bf16[4,256,128]{2,1,0:T(8,128)(2,1)S(1)}, bf16[4,256,128]{2,1,0:T(8,128)(2,1)S(1)}, u32[]{:S(2)}, u32[]{:S(2)}) collective-permute-start(bf16[4,256,128]{2,1,0:T(8,128)(2,1)S(1)} %get-tuple-element.22), channel_id=1, source_target_pairs={{0,2},{1,3},{2,0},{3,1},{4,6},{5,7},{6,4},{7,5},{8,10},{9,11},{10,... | collective-permute-start | bytes 786440 | tf_op jit(solution)/shard_map/ppermute | solution.py:246
  4.1 30.4 %collective-permute-start.1 = (bf16[2,256,128]{2,1,0:T(8,128)(2,1)S(1)}, bf16[2,256,128]{2,1,0:T(8,128)(2,1)S(1)}, u32[]{:S(2)}, u32[]{:S(2)}) collective-permute-start(bf16[2,256,128]{2,1,0:T(8,128)(2,1)S(1)} %pad_maximum_fusion.1), channel_id=1, source_target_pairs={{0,1},{1,0},{2,3},{3,2},{4,5},{5,4},{6,7},{7,6},{8,9},{9,8},{10,11... | collective-permute-start | bytes 393224 | tf_op jit(solution)/shard_map/ppermute | solution.py:246
  7.1 27.5 %collective-permute-start.2 = (bf16[2,256,128]{2,1,0:T(8,128)(2,1)S(1)}, bf16[2,256,128]{2,1,0:T(8,128)(2,1)S(1)}, u32[]{:S(2)}, u32[]{:S(2)}) collective-permute-start(bf16[2,256,128]{2,1,0:T(8,128)(2,1)S(1)} %pad_maximum_fusion.2), channel_id=1, source_target_pairs={{0,4},{1,5},{2,6},{3,7},{4,0},{5,1},{6,2},{7,3},{8,12},{9,13},{10,... | collective-permute-start | bytes 393224 | tf_op jit(solution)/shard_map/ppermute | solution.py:246
  8.7 25.9 %collective-permute-start.3 = (bf16[2,256,128]{2,1,0:T(8,128)(2,1)S(1)}, bf16[2,256,128]{2,1,0:T(8,128)(2,1)S(1)}, u32[]{:S(2)}, u32[]{:S(2)}) collective-permute-start(bf16[2,256,128]{2,1,0:T(8,128)(2,1)S(1)} %pad_maximum_fusion.3), channel_id=1, source_target_pairs={{0,5},{1,4},{2,7},{3,6},{4,1},{5,0},{6,3},{7,2},{8,13},{9,12},{10,... | collective-permute-start | bytes 393224 | tf_op jit(solution)/shard_map/ppermute | solution.py:246
  36.7 5.1 %collective-permute-start.4 = (f32[8,128]{1,0:T(8,128)S(1)}, f32[8,128]{1,0:T(8,128)S(1)}, u32[]{:S(2)}, u32[]{:S(2)}) collective-permute-start(f32[8,128]{1,0:T(8,128)S(1)} %shard_map.105.refs_4_), channel_id=1, source_target_pairs={{0,8},{8,0},{16,24},{24,16},{1,9},{9,1},{17,25},{25,17},{2,10},{10... | collective-permute-start | bytes 12296 | tf_op jit(solution)/shard_map/ppermute | solution.py:246
  37.4 4.5 %collective-permute-start.5 = (f32[8,128]{1,0:T(8,128)S(1)}, f32[8,128]{1,0:T(8,128)S(1)}, u32[]{:S(2)}, u32[]{:S(2)}) collective-permute-start(f32[8,128]{1,0:T(8,128)S(1)} %shard_map.105.refs_4_), channel_id=1, source_target_pairs={{0,16},{8,24},{16,0},{24,8},{1,17},{9,25},{17,1},{25,9},{2,18},{10... | collective-permute-start | bytes 12296 | tf_op jit(solution)/shard_map/ppermute | solution.py:246
  38.8 5.4 %collective-permute-start.6 = (f32[8,128]{1,0:T(8,128)S(1)}, f32[8,128]{1,0:T(8,128)S(1)}, u32[]{:S(2)}, u32[]{:S(2)}) collective-permute-start(f32[8,128]{1,0:T(8,128)S(1)} %shard_map.105.refs_4_), channel_id=1, source_target_pairs={{0,24},{8,16},{16,8},{24,0},{1,25},{9,17},{17,9},{25,1},{2,26},{10... | collective-permute-start | bytes 12296 | tf_op jit(solution)/shard_map/ppermute | solution.py:246
  47.7 1.6 %collective-permute-start.7 = (bf16[4,256,128]{2,1,0:T(8,128)(2,1)S(1)}, bf16[4,256,128]{2,1,0:T(8,128)(2,1)S(1)}, u32[]{:S(2)}, u32[]{:S(2)}) collective-permute-start(bf16[4,256,128]{2,1,0:T(8,128)(2,1)S(1)} %get-tuple-element.25), channel_id=1, source_target_pairs={{0,2},{1,3},{2,0},{3,1},{4,6},{5,7},{6,4},{7,5},{8,10},{9,11},{10,... | collective-permute-start | bytes 786440 | tf_op jit(solution)/shard_map/ppermute | solution.py:246
  49.4 17.3 %collective-permute-start.8 = (bf16[2,256,128]{2,1,0:T(8,128)(2,1)S(1)}, bf16[2,256,128]{2,1,0:T(8,128)(2,1)S(1)}, u32[]{:S(2)}, u32[]{:S(2)}) collective-permute-start(bf16[2,256,128]{2,1,0:T(8,128)(2,1)S(1)} %pad_maximum_fusion.5), channel_id=1, source_target_pairs={{0,1},{1,0},{2,3},{3,2},{4,5},{5,4},{6,7},{7,6},{8,9},{9,8},{10,11... | collective-permute-start | bytes 393224 | tf_op jit(solution)/shard_map/ppermute | solution.py:246
  51.0 15.8 %collective-permute-start.9 = (bf16[2,256,128]{2,1,0:T(8,128)(2,1)S(1)}, bf16[2,256,128]{2,1,0:T(8,128)(2,1)S(1)}, u32[]{:S(2)}, u32[]{:S(2)}) collective-permute-start(bf16[2,256,128]{2,1,0:T(8,128)(2,1)S(1)} %pad_maximum_fusion.6), channel_id=1, source_target_pairs={{0,4},{1,5},{2,6},{3,7},{4,0},{5,1},{6,2},{7,3},{8,12},{9,13},{10,... | collective-permute-start | bytes 393224 | tf_op jit(solution)/shard_map/ppermute | solution.py:246
  51.7 15.0 %collective-permute-start.10 = (bf16[2,256,128]{2,1,0:T(8,128)(2,1)S(1)}, bf16[2,256,128]{2,1,0:T(8,128)(2,1)S(1)}, u32[]{:S(2)}, u32[]{:S(2)}) collective-permute-start(bf16[2,256,128]{2,1,0:T(8,128)(2,1)S(1)} %pad_maximum_fusion.7), channel_id=1, source_target_pairs={{0,5},{1,4},{2,7},{3,6},{4,1},{5,0},{6,3},{7,2},{8,13},{9,12},{10,... | collective-permute-start | bytes 393224 | tf_op jit(solution)/shard_map/ppermute | solution.py:246

commit v4 on v3

v4 whole, which is shorter than its diff:
```python
import functools

import jax
import jax.numpy as jnp
from jax import lax
from jax.experimental import pallas as pl
from jax.experimental.pallas import tpu as pltpu
from jax.sharding import Mesh, PartitionSpec as P

DH = 128
KVH = 8
RESP_LEN = 64
SCALE = DH ** (-0.5)
MASKED_SCORE = -1e30
DEAD_LSE = 1e30
PIECES = 3
STAT_ROWS = 16
STEP_LINES = 512
PARAMS = pltpu.CompilerParams(vmem_limit_bytes=48 * 1024 * 1024)
HBM = pl.BlockSpec(memory_space=pltpu.HBM)
SMEM = pl.BlockSpec(memory_space=pltpu.SMEM)
VMEM = pl.BlockSpec(memory_space=pltpu.VMEM)

NEAR = 2
FIRST = 1
KEEP = (0, 2, 4, 6)


def split_pieces(x):
    first = x.astype(jnp.bfloat16)
    rest = x - first.astype(jnp.float32)
    second = rest.astype(jnp.bfloat16)
    third = (rest - second.astype(jnp.float32)).astype(jnp.bfloat16)
    return first, second, third


def shift_of(n):
    assert n & (n - 1) == 0
    return n.bit_length() - 1


def column_of(member, groups, heads):
    head_index, group_index = member & (heads - 1), member >> shift_of(heads)
    return pl.multiple_of((head_index * groups + group_index) * DH, DH)


def pack_kv_kernel(groups, heads, scalars, k_hbm, v_hbm, keep_ref, send_ref, sems):
    tokens = k_hbm.shape[0]
    copies = []
    for i, j in enumerate(KEEP):
        for ref, peer in ((send_ref, j ^ FIRST), (keep_ref, j)):
            columns = pl.ds(column_of(scalars[0] ^ peer, groups, heads), DH)
            copies.append((k_hbm.at[:, columns], ref.at[i, 0:tokens, :]))
            copies.append((v_hbm.at[:, columns], ref.at[i, tokens : 2 * tokens, :]))
    copies = [pltpu.make_async_copy(s, t, sems.at[n]) for n, (s, t) in enumerate(copies)]
    for copy in copies:
        copy.start()
    for copy in copies:
        copy.wait()


def pack_rows_kernel(far, groups, q_hbm, o_grad_hbm, o_hbm, lse_hbm, rows_ref, o_ref, lse_ref, sems):
    rows, own_heads = lse_ref.shape
    lines = o_ref.shape[0] // groups
    copies = [(lse_hbm, lse_ref), (o_hbm, o_ref)]
    for g in range(groups):
        held = pl.ds(g * lines, lines)
        for f in range(far):
            slab = rows_ref.at[f * groups + g]
            copies.append((q_hbm.at[held, :], slab.at[0:lines, :]))
            copies.append((o_grad_hbm.at[held, :], slab.at[lines : 2 * lines, :]))
    copies = [pltpu.make_async_copy(s, t, sems.at[n]) for n, (s, t) in enumerate(copies)]
    for copy in copies:
        copy.start()

    wide = 2 * lines
    shape = (own_heads, wide)
    head_ids = lax.broadcasted_iota(jnp.int32, shape, 0)
    line_heads = (lax.broadcasted_iota(jnp.int32, shape, 1) & (lines - 1)) >> shift_of(rows)
    group_heads = lines // rows
    chosen = [
        (head_ids == line_heads + g * group_heads).astype(jnp.bfloat16) for g in range(groups)
    ]
    shape = (rows, wide)
    own_row = lax.broadcasted_iota(jnp.int32, shape, 0) == (
        lax.broadcasted_iota(jnp.int32, shape, 1) & (rows - 1)
    )
    for copy in copies:
        copy.wait()
    pieces = split_pieces(lse_ref[...])
    for g in range(groups):
        stats = []
        for piece in pieces:
            spread = jnp.dot(piece, chosen[g], preferred_element_type=jnp.float32)
            stats.append(jnp.sum(jnp.where(own_row, spread, 0.0), axis=0, keepdims=True))
        o_grad = rows_ref[g, lines : 2 * lines, :].astype(jnp.float32)
        product = o_grad * o_ref[g * lines : (g + 1) * lines, :].astype(jnp.float32)
        dots = jnp.sum(jnp.concatenate([product, product], axis=0).T, axis=0, keepdims=True)
        stats += [piece.astype(jnp.float32) for piece in split_pieces(dots)]
        stats.append(jnp.zeros((STAT_ROWS - 2 * PIECES, wide), jnp.float32))
        stat_block = jnp.concatenate(stats, axis=0).astype(jnp.bfloat16)
        for f in range(far):
            rows_ref[f * groups + g, wide:, :] = stat_block


def pair_starts(scalars, i, groups, heads, tokens):
    starts = []
    for other in (0, FIRST):
        member = scalars[0] ^ KEEP[i] ^ other
        group_index, head_index = member >> shift_of(heads), member & (heads - 1)
        index = ((scalars[1] * groups + group_index) * NEAR + scalars[2]) * heads + head_index
        starts.append(index * tokens)
    return starts


def pair_keys(ref, tokens):
    return jnp.concatenate([ref[0, 0:tokens, :], ref[1, 0:tokens, :]], axis=0)


def pair_values(ref, tokens):
    return jnp.concatenate([ref[0, tokens : 2 * tokens, :], ref[1, tokens : 2 * tokens, :]], axis=0)


def response_of(source, rows):
    return source * NEAR * rows // RESP_LEN


def stat_kernel(groups, heads, rows, tokens, scalars, prompt_end, *refs):
    row_refs, pair_refs, lse_ref = refs[:NEAR], refs[NEAR:-1], refs[-1]
    sources, lines = row_refs[0].shape[0], (row_refs[0].shape[1] - STAT_ROWS) // 2
    step = 256 // lines
    count = step * lines
    offset = lax.broadcasted_iota(jnp.int32, (tokens, count), 0)
    for n, rows_ref in enumerate(row_refs):
        for c in range(0, sources, step):
            q = rows_ref[c : c + step, 0:lines, :].reshape(count, DH)
            end = prompt_end[response_of(c, rows)]
            scores = []
            for i, ref in enumerate(pair_refs):
                part = lax.dot_general(
                    pair_keys(ref, tokens),
                    q,
                    (((1,), (1,)), ((), ())),
                    preferred_element_type=jnp.float32,
                )
                starts = pair_starts(scalars, i, groups, heads, tokens)
                visible = jnp.concatenate([offset < end - start for start in starts], axis=0)
                scores.append(jnp.where(visible, part * SCALE, MASKED_SCORE))
            scores = jnp.concatenate(scores, axis=0)
            peak = jnp.max(scores, axis=0, keepdims=True)
            total = jnp.sum(jnp.exp(scores - peak), axis=0, keepdims=True)
            lse = peak + jnp.log(total)
            for k in range(count // DH):
                at = ((scalars[2] ^ n) * sources + c) * lines // DH + k
                lse_ref[pl.ds(at, 1), :] = lse[:, k * DH : (k + 1) * DH]


def line_values(rows_ref, sources, lines, first_piece):
    low = lax.broadcasted_iota(jnp.int32, (1, 2 * lines), 1) < lines
    out = []
    for n in sources[::2]:
        held = [
            rows_ref[s, 2 * lines : 2 * lines + STAT_ROWS, :].astype(jnp.float32)
            for s in (n, n + 1)
        ]
        total = None
        for k in range(first_piece, first_piece + PIECES):
            piece = jnp.where(low, held[0][k : k + 1], held[1][k : k + 1])
            total = piece if total is None else total + piece
        out.append(total)
    return jnp.concatenate(out, axis=1)


def grad_kernel(parts, groups, heads, rows, tokens, scalars, resp_len, prompt_end, *refs):
    row_refs, refs = refs[:NEAR], refs[NEAR:]
    pair_refs, refs = refs[: len(KEEP)], refs[len(KEEP) :]
    lse_refs, refs = refs[:parts], refs[parts:]
    dq_refs, (dkv_keep_ref, dkv_send_ref, dk_acc, dv_acc) = refs[:NEAR], refs[NEAR:]
    all_sources, lines = row_refs[0].shape[0], (row_refs[0].shape[1] - STAT_ROWS) // 2
    step = min(all_sources, STEP_LINES // lines)
    part_count = step * lines
    count = NEAR * part_count
    offset = lax.broadcasted_iota(jnp.int32, (tokens, count), 0)
    lane = lax.broadcasted_iota(jnp.int32, (1, 2 * lines), 1)
    for c in range(0, all_sources, step):
        sources = range(c, c + step)

        def both(part_of):
            return jnp.concatenate([part_of(n, ref) for n, ref in enumerate(row_refs)], axis=0)

        def both_lines(part_of):
            return jnp.concatenate([part_of(n, ref) for n, ref in enumerate(row_refs)], axis=1)

        def live_lines(n, _):
            live = []
            for s in sources[::2]:
                device = (s + jnp.where(lane < lines, 0, 1)) * NEAR + (scalars[2] ^ n)
                row = (device * rows + (lane & (rows - 1))) & (RESP_LEN - 1)
                live.append((row < resp_len[response_of(s, rows)]).astype(jnp.int32))
            return jnp.concatenate(live, axis=1)

        def end_lines(n, _):
            ends = [prompt_end[response_of(s, rows)] for s in sources[::2]]
            return jnp.concatenate([jnp.full(lane.shape, end, jnp.int32) for end in ends], axis=1)

        def lse_lines(ref):
            def part_of(n, _):
                first = ((scalars[2] ^ n) * all_sources + c) * lines // DH
                tiles = [ref[pl.ds(first + k, 1), :] for k in range(part_count // DH)]
                return jnp.concatenate(tiles, axis=1)

            return both_lines(part_of)

        q = both(lambda n, ref: ref[c : c + step, 0:lines, :].reshape(part_count, DH))
        o_grad = both(
            lambda n, ref: ref[c : c + step, lines : 2 * lines, :].reshape(part_count, DH)
        )
        self_lse = both_lines(lambda n, ref: line_values(ref, sources, lines, 0))
        dots = both_lines(lambda n, ref: line_values(ref, sources, lines, PIECES))
        live, end = both_lines(live_lines), both_lines(end_lines)
        part_lse = [lse_lines(ref) for ref in lse_refs]
        peak = functools.reduce(jnp.maximum, part_lse, self_lse)
        total = sum(jnp.exp(x - peak) for x in part_lse) + jnp.exp(self_lse - peak)
        lse = jnp.where(live > 0, peak + jnp.log(total), DEAD_LSE)
        dq_t = jnp.zeros((DH, count), jnp.float32)
        for i, ref in enumerate(pair_refs):
            k, v = pair_keys(ref, tokens), pair_values(ref, tokens)
            scores = lax.dot_general(
                k, q, (((1,), (1,)), ((), ())), preferred_element_type=jnp.float32
            )
            starts = pair_starts(scalars, i, groups, heads, tokens)
            visible = jnp.concatenate([offset < end - start for start in starts], axis=0)
            prob = jnp.where(visible, jnp.exp(scores * SCALE - lse), 0.0)
            dprob = lax.dot_general(
                v, o_grad, (((1,), (1,)), ((), ())), preferred_element_type=jnp.float32
            )
            dscore = (prob * (dprob - dots)).astype(jnp.bfloat16)
            dv = jnp.dot(prob.astype(jnp.bfloat16), o_grad, preferred_element_type=jnp.float32)
            dk = jnp.dot(dscore, q, preferred_element_type=jnp.float32) * SCALE
            dq_t = dq_t + jnp.dot(k.T, dscore, preferred_element_type=jnp.float32)
            if c > 0:
                dk = dk + dk_acc[i]
                dv = dv + dv_acc[i]
            if c + step < all_sources:
                dk_acc[i] = dk
                dv_acc[i] = dv
            else:
                for n, out in enumerate((dkv_keep_ref, dkv_send_ref)):
                    inner = slice(n * tokens, (n + 1) * tokens)
                    out[i, 0:tokens, :] = dk[inner].astype(jnp.bfloat16)
                    out[i, tokens : 2 * tokens, :] = dv[inner].astype(jnp.bfloat16)
        for n, ref in enumerate(dq_refs):
            dq = (dq_t[:, n * part_count : (n + 1) * part_count] * SCALE).T.astype(jnp.bfloat16)
            ref[c : c + step] = dq.reshape(step, lines, DH)


def write_query_kernel(far, groups, dq_ref, out_ref):
    lines = dq_ref.shape[1]
    for g in range(groups):
        total = dq_ref[g].astype(jnp.float32)
        for f in range(1, far):
            total = total + dq_ref[f * groups + g].astype(jnp.float32)
        out_ref[g * lines : (g + 1) * lines, :] = total.astype(jnp.bfloat16)


def write_kv_kernel(groups, heads, scalars, *refs):
    pair_refs, (out_k_ref, out_v_ref, sems) = refs[: len(KEEP)], refs[len(KEEP) :]
    tokens = out_k_ref.shape[0]
    copies = []
    for i, ref in enumerate(pair_refs):
        for n, other in enumerate((0, FIRST)):
            columns = pl.ds(column_of(scalars[0] ^ KEEP[i] ^ other, groups, heads), DH)
            copies.append((ref.at[n, 0:tokens, :], out_k_ref.at[:, columns]))
            copies.append((ref.at[n, tokens : 2 * tokens, :], out_v_ref.at[:, columns]))
    copies = [pltpu.make_async_copy(s, t, sems.at[n]) for n, (s, t) in enumerate(copies)]
    for copy in copies:
        copy.start()
    for copy in copies:
        copy.wait()


def swap(x, axis, distance, size):
    return lax.ppermute(x, axis, [(i, i ^ distance) for i in range(size)])


def swap_pairs(keep, send):
    members = ("group", "head")
    came = swap(send, members, FIRST, KVH)
    pairs = [jnp.stack([keep[i], came[i]]) for i in range(len(KEEP))]
    return [swap(x, members, j, KVH) if j else x for x, j in zip(pairs, KEEP)]


def exchange_slabs(x):
    return lax.all_to_all(x, ("far", "group"), split_axis=0, concat_axis=0, tiled=True)


def shards(far, groups, heads, queries, grad_out, outputs, lse_self, keys, values, resp_len, prompt_end):
    rows = queries.shape[0]
    own_heads = queries.shape[1] // DH
    own_lines = rows * own_heads
    lines = own_lines // groups
    tokens = keys.shape[0]
    sources = far * groups
    parts = far * NEAR
    assert 2 * lines == DH and RESP_LEN % (256 // lines * NEAR * rows) == 0
    member = lax.axis_index("group") * heads + lax.axis_index("head")
    scalars = jnp.stack([member, lax.axis_index("far"), lax.axis_index("near")]).astype(jnp.int32)

    def as_lines(x):
        return x.reshape(rows, own_heads, DH).transpose(1, 0, 2).reshape(own_lines, DH)

    def in_hbm(x):
        return pltpu.with_memory_space_constraint(x, pltpu.HBM)

    half_shape = jax.ShapeDtypeStruct((len(KEEP), 2 * tokens, DH), jnp.bfloat16)
    kv_keep, kv_send = pl.pallas_call(
        functools.partial(pack_kv_kernel, groups, heads),
        in_specs=[SMEM] + [HBM] * 2,
        out_specs=[VMEM] * 2,
        out_shape=[half_shape] * 2,
        scratch_shapes=[pltpu.SemaphoreType.DMA((4 * len(KEEP),))],
        compiler_params=PARAMS,
    )(scalars, in_hbm(keys), in_hbm(values))
    slabs = pl.pallas_call(
        functools.partial(pack_rows_kernel, far, groups),
        in_specs=[HBM] * 4,
        out_specs=VMEM,
        out_shape=jax.ShapeDtypeStruct((sources, 2 * lines + STAT_ROWS, DH), jnp.bfloat16),
        scratch_shapes=[
            pltpu.VMEM((own_lines, DH), jnp.bfloat16),
            pltpu.VMEM(lse_self.shape, jnp.float32),
            pltpu.SemaphoreType.DMA((2 + 2 * sources,)),
        ],
        compiler_params=PARAMS,
    )(in_hbm(as_lines(queries)), in_hbm(as_lines(grad_out)), in_hbm(as_lines(outputs)), in_hbm(lse_self))
    pairs = swap_pairs(kv_keep, kv_send)
    slabs = exchange_slabs(slabs)
    blocks = [slabs, swap(slabs, "near", 1, NEAR)]

    lse = pl.pallas_call(
        functools.partial(stat_kernel, groups, heads, rows, tokens),
        in_specs=[SMEM] * 2 + [VMEM] * (NEAR + len(KEEP)),
        out_shape=jax.ShapeDtypeStruct((NEAR * sources * lines // DH, DH), jnp.float32),
        compiler_params=PARAMS,
    )(scalars, prompt_end, *blocks, *pairs)
    every_lse = [lse] + [swap(lse, ("far", "near"), d, parts) for d in range(1, parts)]

    dq_shape = jax.ShapeDtypeStruct((sources, lines, DH), jnp.bfloat16)
    acc = pltpu.VMEM((len(KEEP), 2 * tokens, DH), jnp.float32)
    dq_keep, dq_send, dkv_keep, dkv_send = pl.pallas_call(
        functools.partial(grad_kernel, parts, groups, heads, rows, tokens),
        in_specs=[SMEM] * 3 + [VMEM] * (NEAR + len(KEEP) + parts),
        out_shape=[dq_shape] * NEAR + [half_shape] * 2,
        scratch_shapes=[acc] * 2,
        compiler_params=PARAMS,
    )(scalars, resp_len, prompt_end, *blocks, *pairs, *every_lse)

    pairs = swap_pairs(dkv_keep, dkv_send)
    came = swap(dq_send, "near", 1, NEAR)
    dq = (dq_keep.astype(jnp.float32) + came.astype(jnp.float32)).astype(jnp.bfloat16)
    dq = exchange_slabs(dq)
    out_q = pl.pallas_call(
        functools.partial(write_query_kernel, far, groups),
        in_specs=[VMEM],
        out_shape=jax.ShapeDtypeStruct((own_lines, DH), jnp.bfloat16),
        compiler_params=PARAMS,
    )(dq)
    out_k, out_v = pl.pallas_call(
        functools.partial(write_kv_kernel, groups, heads),
        in_specs=[SMEM] + [VMEM] * len(KEEP),
        out_specs=[HBM] * 2,
        out_shape=[
            jax.ShapeDtypeStruct(keys.shape, jnp.bfloat16),
            jax.ShapeDtypeStruct(values.shape, jnp.bfloat16),
        ],
        scratch_shapes=[pltpu.SemaphoreType.DMA((4 * len(KEEP),))],
        compiler_params=PARAMS,
    )(scalars, *pairs)
    out_q = out_q.reshape(own_heads, rows, DH).transpose(1, 0, 2).reshape(rows, own_heads * DH)
    return out_q, out_k, out_v


def solution(mesh):
    ctx, heads = mesh.shape["ctx"], mesh.shape["head"]
    groups = KVH // heads
    far = ctx // groups // NEAR
    fine = Mesh(mesh.devices.reshape(far, groups, NEAR, heads), ("far", "group", "near", "head"))
    rows = P(("far", "group", "near"), "head")
    tokens = P(("far", "group", "near", "head"), None)
    return jax.shard_map(
        functools.partial(shards, far, groups, heads),
        mesh=fine,
        in_specs=(rows, rows, rows, rows, tokens, tokens, P(), P()),
        out_specs=(rows, tokens, tokens),
        check_vma=False,
    )
```

time: 68.6 us -> 63.1 us (0.920)
  blocking collectives: 37.1 us -> 0 us
  waiting for transfers between devices: 5.06 us -> 23 us
  starting transfers between devices: 13.3 us -> 25.1 us
  Pallas kernels: 10.4 us -> 11.4 us
  other arithmetic: 0.19 us -> 0.89 us
    all_to_all x2 -> x0, blocking collectives: 37.1 us -> none  [one_step(): lax.all_to_all(x, ('part', 'group'), split_axis=0, concat_axis=0, tiled=T...]
    ppermute x11 -> x13, waiting for transfers between devices: 5.06 us -> 14.9 us  [swap(): return lax.ppermute(x, axis, [(i, i ^ distance) for i in range(size)])]
    all_to_all x0 -> x2, starting transfers between devices: none -> 9.8 us  [exchange_slabs(): lax.all_to_all(x, ('far', 'group'), split_axis=0, concat_axis=0, tiled=True)]
    all_to_all x0 -> x2, waiting for transfers between devices: none -> 8.14 us  [exchange_slabs(): lax.all_to_all(x, ('far', 'group'), split_axis=0, concat_axis=0, tiled=True)]
    ppermute x11 -> x13, starting transfers between devices: 13.3 us -> 15.3 us  [swap(): return lax.ppermute(x, axis, [(i, i ^ distance) for i in range(size)])]
    pallas_call x4 -> x5, Pallas kernels: 8.74 us -> 9.73 us  [the longest x1 3.49 us: shards(): pl.pallas_call(functools.partial(grad_kernel, parts, groups, heads, rows,...]
    convert_element_type x0 -> x1, other arithmetic: none -> 0.7 us  [shards(): (dq_keep.astype(jnp.float32) + came.astype(jnp.float32)).astype(jnp.bfloa...]
  transfers between devices with their start and end apart: 11 -> 15, of which waited for: 4 -> 11; matrix products, arithmetic and copies ran while one was open for 0% -> 1% of each run, Pallas kernels for 2% -> 4%
where the time goes in v4:
time: 63.1 us; the launch traced here: 62.6 us
  starting transfers between devices  25.1 us (40%)
  waiting for transfers between devices  23 us (36%)
  Pallas kernels  11.4 us (18%)
  between operations  2.06 us (3%)
  other arithmetic  0.89 us (1%)
    ppermute x13, starting transfers between devices, swap(): return lax.ppermute(x, axis, [(i, i ^ distance) for i in range(size)])  15.3 us
    ppermute x13, waiting for transfers between devices, swap(): return lax.ppermute(x, axis, [(i, i ^ distance) for i in range(size)])  14.9 us
    all_to_all x2, starting transfers between devices, exchange_slabs(): lax.all_to_all(x, ('far', 'group'), split_axis=0, concat_axis=0, tiled=True)  9.8 us
    all_to_all x2, waiting for transfers between devices, exchange_slabs(): lax.all_to_all(x, ('far', 'group'), split_axis=0, concat_axis=0, tiled=True)  8.14 us
    pallas_call x1, Pallas kernels, shards(): pl.pallas_call(functools.partial(grad_kernel, parts, groups, heads, rows,...  3.49 us
    pallas_call x1, Pallas kernels, shards(): pl.pallas_call(functools.partial(stat_kernel, groups, heads, rows, tokens...  2.15 us
    pallas_call x1, Pallas kernels, shards(): pl.pallas_call(functools.partial(pack_rows_kernel, far, groups), in_specs...  1.98 us
    pallas_call x1, Pallas kernels, shards(): pl.pallas_call(functools.partial(pack_kv_kernel, groups, heads), in_specs...  1.7 us
  transfers between devices with their start and end apart: 15, of which 11 were waited for; matrix products, arithmetic and copies ran while one was open for 1% of the time, Pallas kernels for 4%

profile of v4, /device:TPU:0, one launch (start us, length us, event | category | flops | bytes accessed | tf_op | source)
XLA Modules:
  0.0 62.6 jit_solution(4163720676742899987)
XLA Ops:
  0.6 0.1 pad_add_fusion.scalars
  0.7 1.7 %shard_map.104 = (bf16[4,256,128]{2,1,0:T(8,128)(2,1)S(1)}, bf16[4,256,128]{2,1,0:T(8,128)(2,1)S(1)}) custom-call(s32[3]{0:T(128)S(1)} %pad_add_fusion.scalars, bf16[128,1024]{1,0:T(8,128)(2,1)} %k_hbm.1, bf16[128,1024]{1,0:T(8,128)(2,1)} %v_hbm.1), custom_call_target="tpu_custom_call" | custom-call | tf_op jit(solution)/shard_map/pallas_call | solution.py:316
  2.4 3.0 %collective-permute-start.1 = (bf16[4,256,128]{2,1,0:T(8,128)(2,1)S(1)}, bf16[4,256,128]{2,1,0:T(8,128)(2,1)S(1)}, u32[]{:S(2)}, u32[]{:S(2)}) collective-permute-start(bf16[4,256,128]{2,1,0:T(8,128)(2,1)S(1)} %get-tuple-element.12), channel_id=1, source_target_pairs={{0,1},{1,0},{4,5},{5,4},{8,9},{9,8},{12,13},{13,12},{2,3},{3,2},{6... | collective-permute-start | bytes 786440 | tf_op jit(solution)/shard_map/ppermute | solution.py:283
  5.4 2.0 %shard_map.103 = bf16[8,144,128]{2,1,0:T(8,128)(2,1)} custom-call(bf16[256,128]{1,0:T(8,128)(2,1)} %bitcast.23, bf16[256,128]{1,0:T(8,128)(2,1)} %bitcast.24, bf16[256,128]{1,0:T(8,128)(2,1)} %bitcast.25, f32[4,64]{1,0:T(4,128)} %lse_hbm.1), custom_call_target="tpu_custom_call" | custom-call | tf_op jit(solution)/shard_map/pallas_call | solution.py:324
  7.4 5.8 %all-to-all-start = ((bf16[8,144,128]{2,1,0:T(8,128)(2,1)}), bf16[8,144,128]{2,1,0:T(8,128)(2,1)S(1)}, u32[]{:S(2)}, u32[]{:S(2)}) async-start(bf16[8,144,128]{2,1,0:T(8,128)(2,1)} %shard_map.103), calls=%async_computation | async-start | bytes 589824 | tf_op jit(solution)/shard_map/all_to_all | solution.py:294
  13.3 0.0 collective-permute-done.1
  13.3 2.1 %collective-permute-start.2 = (bf16[2,256,128]{2,1,0:T(8,128)(2,1)S(1)}, bf16[2,256,128]{2,1,0:T(8,128)(2,1)S(1)}, u32[]{:S(2)}, u32[]{:S(2)}) collective-permute-start(bf16[2,256,128]{2,1,0:T(8,128)(2,1)S(1)} %pad_maximum_fusion.1), channel_id=1, source_target_pairs={{0,4},{1,5},{4,0},{5,1},{8,12},{9,13},{12,8},{13,9},{2,6},{3,7},{6... | collective-permute-start | bytes 393224 | tf_op jit(solution)/shard_map/ppermute | solution.py:283
  15.4 7.1 %all-to-all-done.refs_0_ = bf16[8,144,128]{2,1,0:T(8,128)(2,1)S(1)} async-done(((bf16[8,144,128]{2,1,0:T(8,128)(2,1)}), bf16[8,144,128]{2,1,0:T(8,128)(2,1)S(1)}, u32[]{:S(2)}, u32[]{:S(2)}) %all-to-all-start) | async-done | bytes 294944 | tf_op jit(solution)/shard_map/all_to_all | solution.py:294
  22.5 0.0 collective-permute-start
  22.6 1.1 %collective-permute-start.3 = (bf16[2,256,128]{2,1,0:T(8,128)(2,1)S(1)}, bf16[2,256,128]{2,1,0:T(8,128)(2,1)S(1)}, u32[]{:S(2)}, u32[]{:S(2)}) collective-permute-start(bf16[2,256,128]{2,1,0:T(8,128)(2,1)S(1)} %pad_maximum_fusion.2), channel_id=1, source_target_pairs={{0,8},{1,9},{4,12},{5,13},{8,0},{9,1},{12,4},{13,5},{2,10},{3,11},... | collective-permute-start | bytes 393224 | tf_op jit(solution)/shard_map/ppermute | solution.py:283
  23.7 1.9 %collective-permute-start.4 = (bf16[2,256,128]{2,1,0:T(8,128)(2,1)S(1)}, bf16[2,256,128]{2,1,0:T(8,128)(2,1)S(1)}, u32[]{:S(2)}, u32[]{:S(2)}) collective-permute-start(bf16[2,256,128]{2,1,0:T(8,128)(2,1)S(1)} %pad_maximum_fusion.3), channel_id=1, source_target_pairs={{0,12},{1,13},{4,8},{5,9},{8,4},{9,5},{12,0},{13,1},{2,14},{3,15},... | collective-permute-start | bytes 393224 | tf_op jit(solution)/shard_map/ppermute | solution.py:283
  26.3 0.0 collective-permute-done.2.refs_3_
  26.3 2.6 %collective-permute-done.3.refs_4_ = bf16[2,256,128]{2,1,0:T(8,128)(2,1)S(1)} collective-permute-done((bf16[2,256,128]{2,1,0:T(8,128)(2,1)S(1)}, bf16[2,256,128]{2,1,0:T(8,128)(2,1)S(1)}, u32[]{:S(2)}, u32[]{:S(2)}) %collective-permute-start.3) | collective-permute-done | bytes 131104 | tf_op jit(solution)/shard_map/ppermute | solution.py:283
  28.9 3.3 %collective-permute-done.4.refs_5_ = bf16[2,256,128]{2,1,0:T(8,128)(2,1)S(1)} collective-permute-done((bf16[2,256,128]{2,1,0:T(8,128)(2,1)S(1)}, bf16[2,256,128]{2,1,0:T(8,128)(2,1)S(1)}, u32[]{:S(2)}, u32[]{:S(2)}) %collective-permute-start.4) | collective-permute-done | bytes 131104 | tf_op jit(solution)/shard_map/ppermute | solution.py:283
  32.3 0.0 collective-permute-done.refs_1_
  32.3 2.1 %shard_map.105.refs_6_ = f32[8,128]{1,0:T(8,128)S(1)} custom-call(s32[3]{0:T(128)S(1)} %pad_add_fusion.scalars, s32[1]{0:T(128)S(6)} %copy.16.prompt_end, bf16[8,144,128]{2,1,0:T(8,128)(2,1)S(1)} %all-to-all-done.refs_0_, bf16[8,144,128]{2,1,0:T(8,128)(2,1)S(1)} %collective-permute-done.refs_1_, bf16[2,256,128]{2,1,0:T(8,128)(2,1)S(1)} %pad_maximum_fusion.refs_2_, ...), custom_call_target="tpu_custom_call" | custom-call | tf_op jit(solution)/shard_map/pallas_call | solution.py:340
  34.4 0.1 collective-permute-start.7
  34.5 2.2 %collective-permute-start.6 = (f32[8,128]{1,0:T(8,128)S(1)}, f32[8,128]{1,0:T(8,128)S(1)}, u32[]{:S(2)}, u32[]{:S(2)}) collective-permute-start(f32[8,128]{1,0:T(8,128)S(1)} %shard_map.105.refs_6_), channel_id=1, source_target_pairs={{0,16},{2,18},{16,0},{18,2},{1,17},{3,19},{17,1},{19,3},{4,20},{6,... | collective-permute-start | bytes 12296 | tf_op jit(solution)/shard_map/ppermute | solution.py:283
  36.7 0.5 collective-permute-start.5
  37.9 0.5 collective-permute-done.7.refs_9_
  38.4 0.7 %collective-permute-done.6.refs_8_ = f32[8,128]{1,0:T(8,128)S(1)} collective-permute-done((f32[8,128]{1,0:T(8,128)S(1)}, f32[8,128]{1,0:T(8,128)S(1)}, u32[]{:S(2)}, u32[]{:S(2)}) %collective-permute-start.6) | collective-permute-done | bytes 4128 | tf_op jit(solution)/shard_map/ppermute | solution.py:283
  39.1 0.0 collective-permute-done.5.refs_7_
  39.1 3.5 %shard_map.106 = (bf16[8,64,128]{2,1,0:T(8,128)(2,1)S(1)}, bf16[8,64,128]{2,1,0:T(8,128)(2,1)S(1)}, bf16[4,256,128]{2,1,0:T(8,128)(2,1)S(1)}, bf16[4,256,128]{2,1,0:T(8,128)(2,1)S(1)}) custom-call(s32[3]{0:T(128)S(1)} %pad_add_fusion.scalars, s32[1]{0:T(128)S(6)} %copy.15.resp_len, s32[1]{0:T(128)S(6)} %copy.16.prompt_end, ...), custom_call_target="tpu_custom_call" | custom-call | tf_op jit(solution)/shard_map/pallas_call | solution.py:350
  42.6 0.1 collective-permute-start.8
  42.6 0.6 collective-permute-start.9
  43.3 0.7 %collective-permute-done.8 = bf16[8,64,128]{2,1,0:T(8,128)(2,1)S(1)} collective-permute-done((bf16[8,64,128]{2,1,0:T(8,128)(2,1)S(1)}, bf16[8,64,128]{2,1,0:T(8,128)(2,1)S(1)}, u32[]{:S(2)}, u32[]{:S(2)}) %collective-permute-start.8) | collective-permute-done | bytes 131104 | tf_op jit(solution)/shard_map/ppermute | solution.py:283
  44.0 0.7 %add_convert_fusion = bf16[8,64,128]{2,1,0:T(8,128)(2,1)} fusion(bf16[8,64,128]{2,1,0:T(8,128)(2,1)S(1)} %collective-permute-done.8, bf16[8,64,128]{2,1,0:T(8,128)(2,1)S(1)} %get-tuple-element.13), kind=kLoop, calls=%fused_computation | loop fusion | flops 262144 | bytes 393216 | tf_op jit(solution)/shard_map/convert_element_type | solution.py:360
  44.7 4.0 %all-to-all-start.1 = ((bf16[8,64,128]{2,1,0:T(8,128)(2,1)}), bf16[8,64,128]{2,1,0:T(8,128)(2,1)S(1)}, u32[]{:S(2)}, u32[]{:S(2)}) async-start(bf16[8,64,128]{2,1,0:T(8,128)(2,1)} %add_convert_fusion), calls=%async_computation.1 | async-start | bytes 262144 | tf_op jit(solution)/shard_map/all_to_all | solution.py:294
  48.6 2.7 %collective-permute-done.9 = bf16[4,256,128]{2,1,0:T(8,128)(2,1)S(1)} collective-permute-done((bf16[4,256,128]{2,1,0:T(8,128)(2,1)S(1)}, bf16[4,256,128]{2,1,0:T(8,128)(2,1)S(1)}, u32[]{:S(2)}, u32[]{:S(2)}) %collective-permute-start.9) | collective-permute-done | bytes 262176 | tf_op jit(solution)/shard_map/ppermute | solution.py:283
  51.4 1.0 %collective-permute-start.10 = (bf16[2,256,128]{2,1,0:T(8,128)(2,1)S(1)}, bf16[2,256,128]{2,1,0:T(8,128)(2,1)S(1)}, u32[]{:S(2)}, u32[]{:S(2)}) collective-permute-start(bf16[2,256,128]{2,1,0:T(8,128)(2,1)S(1)} %pad_maximum_fusion.5), channel_id=1, source_target_pairs={{0,4},{1,5},{4,0},{5,1},{8,12},{9,13},{12,8},{13,9},{2,6},{3,7},{6... | collective-permute-start | bytes 393224 | tf_op jit(solution)/shard_map/ppermute | solution.py:283
  52.4 0.8 %collective-permute-start.11 = (bf16[2,256,128]{2,1,0:T(8,128)(2,1)S(1)}, bf16[2,256,128]{2,1,0:T(8,128)(2,1)S(1)}, u32[]{:S(2)}, u32[]{:S(2)}) collective-permute-start(bf16[2,256,128]{2,1,0:T(8,128)(2,1)S(1)} %pad_maximum_fusion.6), channel_id=1, source_target_pairs={{0,8},{1,9},{4,12},{5,13},{8,0},{9,1},{12,4},{13,5},{2,10},{3,11},... | collective-permute-start | bytes 393224 | tf_op jit(solution)/shard_map/ppermute | solution.py:283
  53.2 1.9 %collective-permute-start.12 = (bf16[2,256,128]{2,1,0:T(8,128)(2,1)S(1)}, bf16[2,256,128]{2,1,0:T(8,128)(2,1)S(1)}, u32[]{:S(2)}, u32[]{:S(2)}) collective-permute-start(bf16[2,256,128]{2,1,0:T(8,128)(2,1)S(1)} %pad_maximum_fusion.7), channel_id=1, source_target_pairs={{0,12},{1,13},{4,8},{5,9},{8,4},{9,5},{12,0},{13,1},{2,14},{3,15},... | collective-permute-start | bytes 393224 | tf_op jit(solution)/shard_map/ppermute | solution.py:283
  55.1 1.0 %all-to-all-done.1.dq_ref = bf16[8,64,128]{2,1,0:T(8,128)(2,1)S(1)} async-done(((bf16[8,64,128]{2,1,0:T(8,128)(2,1)}), bf16[8,64,128]{2,1,0:T(8,128)(2,1)S(1)}, u32[]{:S(2)}, u32[]{:S(2)}) %all-to-all-start.1) | async-done | bytes 131104 | tf_op jit(solution)/shard_map/all_to_all | solution.py:294
  56.2 0.6 %shard_map.107 = bf16[256,128]{1,0:T(8,128)(2,1)} custom-call(bf16[8,64,128]{2,1,0:T(8,128)(2,1)S(1)} %all-to-all-done.1.dq_ref), custom_call_target="tpu_custom_call" | custom-call | tf_op jit(solution)/shard_map/pallas_call | solution.py:362
  56.8 0.3 collective-permute-done.10.refs_1_
  57.1 1.8 %collective-permute-done.11.refs_2_ = bf16[2,256,128]{2,1,0:T(8,128)(2,1)S(1)} collective-permute-done((bf16[2,256,128]{2,1,0:T(8,128)(2,1)S(1)}, bf16[2,256,128]{2,1,0:T(8,128)(2,1)S(1)}, u32[]{:S(2)}, u32[]{:S(2)}) %collective-permute-start.11) | collective-permute-done | bytes 131104 | tf_op jit(solution)/shard_map/ppermute | solution.py:283
  58.9 2.2 %collective-permute-done.12.refs_3_ = bf16[2,256,128]{2,1,0:T(8,128)(2,1)S(1)} collective-permute-done((bf16[2,256,128]{2,1,0:T(8,128)(2,1)S(1)}, bf16[2,256,128]{2,1,0:T(8,128)(2,1)S(1)}, u32[]{:S(2)}, u32[]{:S(2)}) %collective-permute-start.12) | collective-permute-done | bytes 131104 | tf_op jit(solution)/shard_map/ppermute | solution.py:283
  61.1 1.5 %shard_map.108 = (bf16[128,1024]{1,0:T(8,128)(2,1)}, bf16[128,1024]{1,0:T(8,128)(2,1)}) custom-call(s32[3]{0:T(128)S(1)} %pad_add_fusion.scalars, bf16[2,256,128]{2,1,0:T(8,128)(2,1)S(1)} %pad_maximum_fusion.4.refs_0_, bf16[2,256,128]{2,1,0:T(8,128)(2,1)S(1)} %collective-permute-done.10.refs_1_, bf16[2,256,128]{2,1,0:T(8,128)(2,1)S(1)} %collective-permute-done.11.refs_2_, ...), custom_call_target="tpu_custom_call" | custom-call | tf_op jit(solution)/shard_map/pallas_call | solution.py:368
  (12 shorter events, 0.2 us)
Async XLA Ops:
  2.4 10.9 %collective-permute-start.1 = (bf16[4,256,128]{2,1,0:T(8,128)(2,1)S(1)}, bf16[4,256,128]{2,1,0:T(8,128)(2,1)S(1)}, u32[]{:S(2)}, u32[]{:S(2)}) collective-permute-start(bf16[4,256,128]{2,1,0:T(8,128)(2,1)S(1)} %get-tuple-element.12), channel_id=1, source_target_pairs={{0,1},{1,0},{4,5},{5,4},{8,9},{9,8},{12,13},{13,12},{2,3},{3,2},{6... | collective-permute-start | bytes 786440 | tf_op jit(solution)/shard_map/ppermute | solution.py:283
  7.4 15.1 %all-to-all-start = ((bf16[8,144,128]{2,1,0:T(8,128)(2,1)}), bf16[8,144,128]{2,1,0:T(8,128)(2,1)S(1)}, u32[]{:S(2)}, u32[]{:S(2)}) async-start(bf16[8,144,128]{2,1,0:T(8,128)(2,1)} %shard_map.103), calls=%async_computation | async-start | bytes 589824 | tf_op jit(solution)/shard_map/all_to_all | solution.py:294
  13.3 13.0 %collective-permute-start.2 = (bf16[2,256,128]{2,1,0:T(8,128)(2,1)S(1)}, bf16[2,256,128]{2,1,0:T(8,128)(2,1)S(1)}, u32[]{:S(2)}, u32[]{:S(2)}) collective-permute-start(bf16[2,256,128]{2,1,0:T(8,128)(2,1)S(1)} %pad_maximum_fusion.1), channel_id=1, source_target_pairs={{0,4},{1,5},{4,0},{5,1},{8,12},{9,13},{12,8},{13,9},{2,6},{3,7},{6... | collective-permute-start | bytes 393224 | tf_op jit(solution)/shard_map/ppermute | solution.py:283
  22.5 9.7 %collective-permute-start = (bf16[8,144,128]{2,1,0:T(8,128)(2,1)S(1)}, bf16[8,144,128]{2,1,0:T(8,128)(2,1)S(1)}, u32[]{:S(2)}, u32[]{:S(2)}) collective-permute-start(bf16[8,144,128]{2,1,0:T(8,128)(2,1)S(1)} %all-to-all-done.refs_0_), channel_id=1, source_target_pairs={{0,2},{2,0},{1,3},{3,1},{4,6},{6,4},{5,7},{7,5},{8,10},{10,8},{9,1... | collective-permute-start | bytes 884744 | tf_op jit(solution)/shard_map/ppermute | solution.py:283
  22.6 6.4 %collective-permute-start.3 = (bf16[2,256,128]{2,1,0:T(8,128)(2,1)S(1)}, bf16[2,256,128]{2,1,0:T(8,128)(2,1)S(1)}, u32[]{:S(2)}, u32[]{:S(2)}) collective-permute-start(bf16[2,256,128]{2,1,0:T(8,128)(2,1)S(1)} %pad_maximum_fusion.2), channel_id=1, source_target_pairs={{0,8},{1,9},{4,12},{5,13},{8,0},{9,1},{12,4},{13,5},{2,10},{3,11},... | collective-permute-start | bytes 393224 | tf_op jit(solution)/shard_map/ppermute | solution.py:283
  23.7 8.5 %collective-permute-start.4 = (bf16[2,256,128]{2,1,0:T(8,128)(2,1)S(1)}, bf16[2,256,128]{2,1,0:T(8,128)(2,1)S(1)}, u32[]{:S(2)}, u32[]{:S(2)}) collective-permute-start(bf16[2,256,128]{2,1,0:T(8,128)(2,1)S(1)} %pad_maximum_fusion.3), channel_id=1, source_target_pairs={{0,12},{1,13},{4,8},{5,9},{8,4},{9,5},{12,0},{13,1},{2,14},{3,15},... | collective-permute-start | bytes 393224 | tf_op jit(solution)/shard_map/ppermute | solution.py:283
  34.4 4.0 %collective-permute-start.7 = (f32[8,128]{1,0:T(8,128)S(1)}, f32[8,128]{1,0:T(8,128)S(1)}, u32[]{:S(2)}, u32[]{:S(2)}) collective-permute-start(f32[8,128]{1,0:T(8,128)S(1)} %shard_map.105.refs_6_), channel_id=1, source_target_pairs={{0,18},{2,16},{16,2},{18,0},{1,19},{3,17},{17,3},{19,1},{4,22},{6,... | collective-permute-start | bytes 12296 | tf_op jit(solution)/shard_map/ppermute | solution.py:283
  34.5 4.6 %collective-permute-start.6 = (f32[8,128]{1,0:T(8,128)S(1)}, f32[8,128]{1,0:T(8,128)S(1)}, u32[]{:S(2)}, u32[]{:S(2)}) collective-permute-start(f32[8,128]{1,0:T(8,128)S(1)} %shard_map.105.refs_6_), channel_id=1, source_target_pairs={{0,16},{2,18},{16,0},{18,2},{1,17},{3,19},{17,1},{19,3},{4,20},{6,... | collective-permute-start | bytes 12296 | tf_op jit(solution)/shard_map/ppermute | solution.py:283
  36.7 2.3 %collective-permute-start.5 = (f32[8,128]{1,0:T(8,128)S(1)}, f32[8,128]{1,0:T(8,128)S(1)}, u32[]{:S(2)}, u32[]{:S(2)}) collective-permute-start(f32[8,128]{1,0:T(8,128)S(1)} %shard_map.105.refs_6_), channel_id=1, source_target_pairs={{0,2},{2,0},{16,18},{18,16},{1,3},{3,1},{17,19},{19,17},{4,6},{6,4... | collective-permute-start | bytes 12296 | tf_op jit(solution)/shard_map/ppermute | solution.py:283
  42.6 1.4 %collective-permute-start.8 = (bf16[8,64,128]{2,1,0:T(8,128)(2,1)S(1)}, bf16[8,64,128]{2,1,0:T(8,128)(2,1)S(1)}, u32[]{:S(2)}, u32[]{:S(2)}) collective-permute-start(bf16[8,64,128]{2,1,0:T(8,128)(2,1)S(1)} %get-tuple-element.14), channel_id=1, source_target_pairs={{0,2},{2,0},{1,3},{3,1},{4,6},{6,4},{5,7},{7,5},{8,10},{10,8},{9,1... | collective-permute-start | bytes 393224 | tf_op jit(solution)/shard_map/ppermute | solution.py:283
  42.6 8.7 %collective-permute-start.9 = (bf16[4,256,128]{2,1,0:T(8,128)(2,1)S(1)}, bf16[4,256,128]{2,1,0:T(8,128)(2,1)S(1)}, u32[]{:S(2)}, u32[]{:S(2)}) collective-permute-start(bf16[4,256,128]{2,1,0:T(8,128)(2,1)S(1)} %get-tuple-element.16), channel_id=1, source_target_pairs={{0,1},{1,0},{4,5},{5,4},{8,9},{9,8},{12,13},{13,12},{2,3},{3,2},{6... | collective-permute-start | bytes 786440 | tf_op jit(solution)/shard_map/ppermute | solution.py:283
  44.7 11.5 %all-to-all-start.1 = ((bf16[8,64,128]{2,1,0:T(8,128)(2,1)}), bf16[8,64,128]{2,1,0:T(8,128)(2,1)S(1)}, u32[]{:S(2)}, u32[]{:S(2)}) async-start(bf16[8,64,128]{2,1,0:T(8,128)(2,1)} %add_convert_fusion), calls=%async_computation.1 | async-start | bytes 262144 | tf_op jit(solution)/shard_map/all_to_all | solution.py:294
  51.4 5.7 %collective-permute-start.10 = (bf16[2,256,128]{2,1,0:T(8,128)(2,1)S(1)}, bf16[2,256,128]{2,1,0:T(8,128)(2,1)S(1)}, u32[]{:S(2)}, u32[]{:S(2)}) collective-permute-start(bf16[2,256,128]{2,1,0:T(8,128)(2,1)S(1)} %pad_maximum_fusion.5), channel_id=1, source_target_pairs={{0,4},{1,5},{4,0},{5,1},{8,12},{9,13},{12,8},{13,9},{2,6},{3,7},{6... | collective-permute-start | bytes 393224 | tf_op jit(solution)/shard_map/ppermute | solution.py:283
  52.4 6.5 %collective-permute-start.11 = (bf16[2,256,128]{2,1,0:T(8,128)(2,1)S(1)}, bf16[2,256,128]{2,1,0:T(8,128)(2,1)S(1)}, u32[]{:S(2)}, u32[]{:S(2)}) collective-permute-start(bf16[2,256,128]{2,1,0:T(8,128)(2,1)S(1)} %pad_maximum_fusion.6), channel_id=1, source_target_pairs={{0,8},{1,9},{4,12},{5,13},{8,0},{9,1},{12,4},{13,5},{2,10},{3,11},... | collective-permute-start | bytes 393224 | tf_op jit(solution)/shard_map/ppermute | solution.py:283
  53.2 7.9 %collective-permute-start.12 = (bf16[2,256,128]{2,1,0:T(8,128)(2,1)S(1)}, bf16[2,256,128]{2,1,0:T(8,128)(2,1)S(1)}, u32[]{:S(2)}, u32[]{:S(2)}) collective-permute-start(bf16[2,256,128]{2,1,0:T(8,128)(2,1)S(1)} %pad_maximum_fusion.7), channel_id=1, source_target_pairs={{0,12},{1,13},{4,8},{5,9},{8,4},{9,5},{12,0},{13,1},{2,14},{3,15},... | collective-permute-start | bytes 393224 | tf_op jit(solution)/shard_map/ppermute | solution.py:283

commit v5 on v4

v5 whole, which is shorter than its diff:
```python
import functools

import jax
import jax.numpy as jnp
from jax import lax
from jax.experimental import pallas as pl
from jax.experimental.pallas import tpu as pltpu
from jax.sharding import Mesh, PartitionSpec as P

DH = 128
KVH = 8
RESP_LEN = 64
SCALE = DH ** (-0.5)
MASKED_SCORE = -1e30
DEAD_LSE = 1e30
PIECES = 3
STAT_ROWS = 16
STEP_LINES = 512
PARAMS = pltpu.CompilerParams(vmem_limit_bytes=48 * 1024 * 1024)
ANY = pl.BlockSpec(memory_space=pl.ANY)
HBM = pl.BlockSpec(memory_space=pltpu.HBM)
SMEM = pl.BlockSpec(memory_space=pltpu.SMEM)
VMEM = pl.BlockSpec(memory_space=pltpu.VMEM)

NEAR = 2
FIRST = 1
KEEP = (0, 2, 4, 6)


def split_pieces(x):
    first = x.astype(jnp.bfloat16)
    rest = x - first.astype(jnp.float32)
    second = rest.astype(jnp.bfloat16)
    third = (rest - second.astype(jnp.float32)).astype(jnp.bfloat16)
    return first, second, third


def shift_of(n):
    assert n & (n - 1) == 0
    return n.bit_length() - 1


def column_of(member, groups, heads):
    head_index, group_index = member & (heads - 1), member >> shift_of(heads)
    return pl.multiple_of((head_index * groups + group_index) * DH, DH)


def pack_kernel(far, groups, heads, scalars, q_hbm, o_grad_hbm, o_hbm, lse_hbm, k_hbm, v_hbm, *rest):
    rows_ref, keep_ref, send_ref, o_ref, lse_ref, sems = rest
    rows, own_heads = lse_ref.shape
    lines = o_ref.shape[0] // groups
    tokens = k_hbm.shape[0]
    copies = [(lse_hbm, lse_ref), (o_hbm, o_ref)]
    for g in range(groups):
        held = pl.ds(g * lines, lines)
        for f in range(far):
            slab = rows_ref.at[f * groups + g]
            copies.append((q_hbm.at[held, :], slab.at[0:lines, :]))
            copies.append((o_grad_hbm.at[held, :], slab.at[lines : 2 * lines, :]))
    row_copies = len(copies)
    for i, j in enumerate(KEEP):
        for ref, peer in ((send_ref, j ^ FIRST), (keep_ref, j)):
            columns = pl.ds(column_of(scalars[0] ^ peer, groups, heads), DH)
            copies.append((k_hbm.at[:, columns], ref.at[i, 0:tokens, :]))
            copies.append((v_hbm.at[:, columns], ref.at[i, tokens : 2 * tokens, :]))
    copies = [pltpu.make_async_copy(s, t, sems.at[n]) for n, (s, t) in enumerate(copies)]
    for copy in copies:
        copy.start()

    wide = 2 * lines
    shape = (own_heads, wide)
    head_ids = lax.broadcasted_iota(jnp.int32, shape, 0)
    line_heads = (lax.broadcasted_iota(jnp.int32, shape, 1) & (lines - 1)) >> shift_of(rows)
    group_heads = lines // rows
    chosen = [
        (head_ids == line_heads + g * group_heads).astype(jnp.bfloat16) for g in range(groups)
    ]
    shape = (rows, wide)
    own_row = lax.broadcasted_iota(jnp.int32, shape, 0) == (
        lax.broadcasted_iota(jnp.int32, shape, 1) & (rows - 1)
    )
    for copy in copies[:row_copies]:
        copy.wait()
    pieces = split_pieces(lse_ref[...])
    for g in range(groups):
        stats = []
        for piece in pieces:
            spread = jnp.dot(piece, chosen[g], preferred_element_type=jnp.float32)
            stats.append(jnp.sum(jnp.where(own_row, spread, 0.0), axis=0, keepdims=True))
        o_grad = rows_ref[g, lines : 2 * lines, :].astype(jnp.float32)
        product = o_grad * o_ref[g * lines : (g + 1) * lines, :].astype(jnp.float32)
        dots = jnp.sum(jnp.concatenate([product, product], axis=0).T, axis=0, keepdims=True)
        stats += [piece.astype(jnp.float32) for piece in split_pieces(dots)]
        stats.append(jnp.zeros((STAT_ROWS - 2 * PIECES, wide), jnp.float32))
        stat_block = jnp.concatenate(stats, axis=0).astype(jnp.bfloat16)
        for f in range(far):
            rows_ref[f * groups + g, wide:, :] = stat_block
    for copy in copies[row_copies:]:
        copy.wait()


def pair_starts(scalars, i, groups, heads, tokens):
    starts = []
    for other in (0, FIRST):
        member = scalars[0] ^ KEEP[i] ^ other
        group_index, head_index = member >> shift_of(heads), member & (heads - 1)
        index = ((scalars[1] * groups + group_index) * NEAR + scalars[2]) * heads + head_index
        starts.append(index * tokens)
    return starts


def pair_keys(ref, tokens):
    return jnp.concatenate([ref[0, 0:tokens, :], ref[1, 0:tokens, :]], axis=0)


def pair_values(ref, tokens):
    return jnp.concatenate([ref[0, tokens : 2 * tokens, :], ref[1, tokens : 2 * tokens, :]], axis=0)


def response_of(source, rows):
    return source * NEAR * rows // RESP_LEN


def stat_kernel(n, groups, heads, rows, tokens, scalars, prompt_end, rows_ref, *refs):
    pair_refs, before_refs, lse_ref = refs[: len(KEEP)], refs[len(KEEP) : -1], refs[-1]
    sources, lines = rows_ref.shape[0], (rows_ref.shape[1] - STAT_ROWS) // 2
    step = 256 // lines
    count = step * lines
    held = sources * lines // DH
    first = (scalars[2] ^ n) * held if before_refs else 0
    for ref in before_refs:
        for k in range(held):
            lse_ref[pl.ds((scalars[2] ^ 0) * held + k, 1), :] = ref[k : k + 1, :]
    offset = lax.broadcasted_iota(jnp.int32, (tokens, count), 0)
    for c in range(0, sources, step):
        q = rows_ref[c : c + step, 0:lines, :].reshape(count, DH)
        end = prompt_end[response_of(c, rows)]
        scores = []
        for i, ref in enumerate(pair_refs):
            part = lax.dot_general(
                pair_keys(ref, tokens),
                q,
                (((1,), (1,)), ((), ())),
                preferred_element_type=jnp.float32,
            )
            starts = pair_starts(scalars, i, groups, heads, tokens)
            visible = jnp.concatenate([offset < end - start for start in starts], axis=0)
            scores.append(jnp.where(visible, part * SCALE, MASKED_SCORE))
        scores = jnp.concatenate(scores, axis=0)
        peak = jnp.max(scores, axis=0, keepdims=True)
        total = jnp.sum(jnp.exp(scores - peak), axis=0, keepdims=True)
        lse = peak + jnp.log(total)
        for k in range(count // DH):
            at = first + c * lines // DH + k
            lse_ref[pl.ds(at, 1), :] = lse[:, k * DH : (k + 1) * DH]


def line_values(rows_ref, sources, lines, first_piece):
    low = lax.broadcasted_iota(jnp.int32, (1, 2 * lines), 1) < lines
    out = []
    for n in sources[::2]:
        held = [
            rows_ref[s, 2 * lines : 2 * lines + STAT_ROWS, :].astype(jnp.float32)
            for s in (n, n + 1)
        ]
        total = None
        for k in range(first_piece, first_piece + PIECES):
            piece = jnp.where(low, held[0][k : k + 1], held[1][k : k + 1])
            total = piece if total is None else total + piece
        out.append(total)
    return jnp.concatenate(out, axis=1)


def over_blocks(part_of, row_refs, axis):
    return jnp.concatenate([part_of(n, ref) for n, ref in enumerate(row_refs)], axis=axis)


def lse_lines(lse_ref, n, scalars, first_source, count, held, lines):
    first = (scalars[2] ^ n) * held + first_source * lines // DH
    return jnp.concatenate([lse_ref[pl.ds(first + k, 1), :] for k in range(count // DH)], axis=1)


def part_kernel(groups, heads, rows, tokens, scalars, prompt_end, *refs):
    row_refs, refs = refs[:NEAR], refs[NEAR:]
    pair_refs, (lse_ref, prob_ref, dscore_ref, *dq_refs) = refs[: len(KEEP)], refs[len(KEEP) :]
    all_sources, lines = row_refs[0].shape[0], (row_refs[0].shape[1] - STAT_ROWS) // 2
    held = all_sources * lines // DH
    step = min(all_sources, STEP_LINES // lines)
    part_count = step * lines
    count = NEAR * part_count
    offset = lax.broadcasted_iota(jnp.int32, (tokens, count), 0)
    for c in range(0, all_sources, step):
        sources = range(c, c + step)

        def end_lines(n, _):
            ends = [prompt_end[response_of(s, rows)] for s in sources]
            return jnp.concatenate([jnp.full((1, lines), end, jnp.int32) for end in ends], axis=1)

        q = over_blocks(
            lambda n, ref: ref[c : c + step, 0:lines, :].reshape(part_count, DH), row_refs, 0
        )
        o_grad = over_blocks(
            lambda n, ref: ref[c : c + step, lines : 2 * lines, :].reshape(part_count, DH),
            row_refs,
            0,
        )
        dots = over_blocks(
            lambda n, ref: line_values(ref, sources, lines, PIECES), row_refs, 1
        )
        lse = over_blocks(
            lambda n, ref: lse_lines(lse_ref, n, scalars, c, part_count, held, lines), row_refs, 1
        )
        end = over_blocks(end_lines, row_refs, 1)
        dq_t = jnp.zeros((DH, count), jnp.float32)
        lanes = slice(c * lines * NEAR, c * lines * NEAR + count)
        for i, ref in enumerate(pair_refs):
            k, v = pair_keys(ref, tokens), pair_values(ref, tokens)
            scores = lax.dot_general(
                k, q, (((1,), (1,)), ((), ())), preferred_element_type=jnp.float32
            )
            starts = pair_starts(scalars, i, groups, heads, tokens)
            visible = jnp.concatenate([offset < end - start for start in starts], axis=0)
            prob = jnp.where(visible, jnp.exp(scores * SCALE - lse), 0.0)
            dprob = lax.dot_general(
                v, o_grad, (((1,), (1,)), ((), ())), preferred_element_type=jnp.float32
            )
            dscore = (prob * (dprob - dots)).astype(jnp.bfloat16)
            prob_ref[i, :, lanes] = prob.astype(jnp.bfloat16)
            dscore_ref[i, :, lanes] = dscore
            dq_t = dq_t + jnp.dot(k.T, dscore, preferred_element_type=jnp.float32)
        for n, ref in enumerate(dq_refs):
            dq = dq_t[:, n * part_count : (n + 1) * part_count]
            ref[:, c * lines : c * lines + part_count] = dq.astype(jnp.bfloat16)


def token_kernel(parts, rows, tokens, scalars, resp_len, *refs):
    row_refs, refs = refs[:NEAR], refs[NEAR:]
    (prob_ref, dscore_ref), lse_refs, refs = refs[:2], refs[2 : 2 + parts], refs[2 + parts :]
    dkv_keep_ref, dkv_send_ref, weight_ref, dk_acc, dv_acc = refs
    all_sources, lines = row_refs[0].shape[0], (row_refs[0].shape[1] - STAT_ROWS) // 2
    held = all_sources * lines // DH
    step = min(all_sources, STEP_LINES // lines)
    part_count = step * lines
    count = NEAR * part_count
    lane = lax.broadcasted_iota(jnp.int32, (1, 2 * lines), 1)
    for c in range(0, all_sources, step):
        sources = range(c, c + step)

        def live_lines(n, _):
            live = []
            for s in sources[::2]:
                device = (s + jnp.where(lane < lines, 0, 1)) * NEAR + (scalars[2] ^ n)
                row = (device * rows + (lane & (rows - 1))) & (RESP_LEN - 1)
                live.append((row < resp_len[response_of(s, rows)]).astype(jnp.int32))
            return jnp.concatenate(live, axis=1)

        part_lse = [
            over_blocks(
                lambda n, ref: lse_lines(lse_ref, n, scalars, c, part_count, held, lines),
                row_refs,
                1,
            )
            for lse_ref in lse_refs
        ]
        self_lse = over_blocks(lambda n, ref: line_values(ref, sources, lines, 0), row_refs, 1)
        peak = functools.reduce(jnp.maximum, part_lse, self_lse)
        total = sum(jnp.exp(x - peak) for x in part_lse) + jnp.exp(self_lse - peak)
        live = over_blocks(live_lines, row_refs, 1)
        lse = jnp.where(live > 0, peak + jnp.log(total), DEAD_LSE)
        weights = [jnp.exp(x - lse) for x in part_lse[:NEAR]]
        for n, weight in enumerate(weights):
            weight_ref[n : n + 1, c * lines : c * lines + part_count] = weight[:, :part_count]
        weight = jnp.broadcast_to(weights[0], (DH, count)).T

        def scaled(first):
            x = over_blocks(
                lambda n, ref: ref[c : c + step, first : first + lines, :].reshape(part_count, DH),
                row_refs,
                0,
            )
            return (x.astype(jnp.float32) * weight).astype(jnp.bfloat16)

        q, o_grad = scaled(0), scaled(lines)
        lanes = slice(c * lines * NEAR, c * lines * NEAR + count)
        for i in range(len(KEEP)):
            dk = jnp.dot(dscore_ref[i, :, lanes], q, preferred_element_type=jnp.float32) * SCALE
            dv = jnp.dot(prob_ref[i, :, lanes], o_grad, preferred_element_type=jnp.float32)
            if c > 0:
                dk = dk + dk_acc[i]
                dv = dv + dv_acc[i]
            if c + step < all_sources:
                dk_acc[i] = dk
                dv_acc[i] = dv
            else:
                for n, out in enumerate((dkv_keep_ref, dkv_send_ref)):
                    inner = slice(n * tokens, (n + 1) * tokens)
                    out[i, 0:tokens, :] = dk[inner].astype(jnp.bfloat16)
                    out[i, tokens : 2 * tokens, :] = dv[inner].astype(jnp.bfloat16)


def add_query_kernel(own_ref, came_ref, weight_ref, out_ref):
    sources, lines, _ = out_ref.shape
    total = own_ref[...].astype(jnp.float32) * weight_ref[0:1, :]
    total = total + came_ref[...].astype(jnp.float32) * weight_ref[1:2, :]
    out_ref[...] = (total * SCALE).T.astype(jnp.bfloat16).reshape(sources, lines, DH)


def tie_kernel(*refs):
    pass


def write_query_kernel(far, groups, dq_ref, out_ref):
    lines = dq_ref.shape[1]
    for g in range(groups):
        total = dq_ref[g].astype(jnp.float32)
        for f in range(1, far):
            total = total + dq_ref[f * groups + g].astype(jnp.float32)
        out_ref[g * lines : (g + 1) * lines, :] = total.astype(jnp.bfloat16)


def write_kv_kernel(groups, heads, scalars, *refs):
    pair_refs, (out_k_ref, out_v_ref, sems) = refs[: len(KEEP)], refs[len(KEEP) :]
    tokens = out_k_ref.shape[0]
    copies = []
    for i, ref in enumerate(pair_refs):
        for n, other in enumerate((0, FIRST)):
            columns = pl.ds(column_of(scalars[0] ^ KEEP[i] ^ other, groups, heads), DH)
            copies.append((ref.at[n, 0:tokens, :], out_k_ref.at[:, columns]))
            copies.append((ref.at[n, tokens : 2 * tokens, :], out_v_ref.at[:, columns]))
    copies = [pltpu.make_async_copy(s, t, sems.at[n]) for n, (s, t) in enumerate(copies)]
    for copy in copies:
        copy.start()
    for copy in copies:
        copy.wait()


def swap(x, axis, distance, size):
    return lax.ppermute(x, axis, [(i, i ^ distance) for i in range(size)])


def swap_pairs(keep, send):
    members = ("group", "head")
    came = swap(send, members, FIRST, KVH)
    pairs = [jnp.stack([keep[i], came[i]]) for i in range(len(KEEP))]
    return [swap(x, members, j, KVH) if j else x for x, j in zip(pairs, KEEP)]


def exchange_slabs(x):
    return lax.all_to_all(x, ("far", "group"), split_axis=0, concat_axis=0, tiled=True)


def shards(far, groups, heads, queries, grad_out, outputs, lse_self, keys, values, resp_len, prompt_end):
    rows = queries.shape[0]
    own_heads = queries.shape[1] // DH
    own_lines = rows * own_heads
    lines = own_lines // groups
    tokens = keys.shape[0]
    sources = far * groups
    parts = far * NEAR
    assert 2 * lines == DH and RESP_LEN % (256 // lines * NEAR * rows) == 0
    member = lax.axis_index("group") * heads + lax.axis_index("head")
    scalars = jnp.stack([member, lax.axis_index("far"), lax.axis_index("near")]).astype(jnp.int32)

    def as_lines(x):
        return x.reshape(rows, own_heads, DH).transpose(1, 0, 2).reshape(own_lines, DH)

    def in_hbm(x):
        return pltpu.with_memory_space_constraint(x, pltpu.HBM)

    half_shape = jax.ShapeDtypeStruct((len(KEEP), 2 * tokens, DH), jnp.bfloat16)
    slabs, kv_keep, kv_send = pl.pallas_call(
        functools.partial(pack_kernel, far, groups, heads),
        in_specs=[SMEM] + [HBM] * 6,
        out_specs=[VMEM] * 3,
        out_shape=[
            jax.ShapeDtypeStruct((sources, 2 * lines + STAT_ROWS, DH), jnp.bfloat16),
            half_shape,
            half_shape,
        ],
        scratch_shapes=[
            pltpu.VMEM((own_lines, DH), jnp.bfloat16),
            pltpu.VMEM(lse_self.shape, jnp.float32),
            pltpu.SemaphoreType.DMA((2 + 2 * sources + 4 * len(KEEP),)),
        ],
        compiler_params=PARAMS,
    )(
        scalars,
        in_hbm(as_lines(queries)),
        in_hbm(as_lines(grad_out)),
        in_hbm(as_lines(outputs)),
        in_hbm(lse_self),
        in_hbm(keys),
        in_hbm(values),
    )
    pairs = swap_pairs(kv_keep, kv_send)
    slabs = exchange_slabs(slabs)
    slabs = pl.pallas_call(
        tie_kernel,
        in_specs=[ANY] * (1 + len(KEEP)),
        out_specs=ANY,
        out_shape=jax.ShapeDtypeStruct(slabs.shape, slabs.dtype),
        input_output_aliases={0: 0},
        compiler_params=PARAMS,
    )(slabs, *pairs)
    blocks = [slabs, swap(slabs, "near", 1, NEAR)]

    lse = []
    for n, block in enumerate(blocks):
        lse = [
            pl.pallas_call(
                functools.partial(stat_kernel, n, groups, heads, rows, tokens),
                in_specs=[SMEM] * 2 + [VMEM] * (1 + len(KEEP) + n),
                out_shape=jax.ShapeDtypeStruct(((n + 1) * sources * lines // DH, DH), jnp.float32),
                compiler_params=PARAMS,
            )(scalars, prompt_end, block, *pairs, *lse)
        ]
    every_lse = lse + [swap(lse[0], ("far", "near"), d, parts) for d in range(1, parts)]

    score_shape = jax.ShapeDtypeStruct(
        (len(KEEP), 2 * tokens, NEAR * sources * lines), jnp.bfloat16
    )
    dq_shape = jax.ShapeDtypeStruct((DH, sources * lines), jnp.bfloat16)
    prob, dscore, dq_keep, dq_send = pl.pallas_call(
        functools.partial(part_kernel, groups, heads, rows, tokens),
        in_specs=[SMEM] * 2 + [VMEM] * (NEAR + len(KEEP) + 1),
        out_specs=[VMEM] * 4,
        out_shape=[score_shape] * 2 + [dq_shape] * NEAR,
        compiler_params=PARAMS,
    )(scalars, prompt_end, *blocks, *pairs, *lse)
    came = swap(dq_send, "near", 1, NEAR)
    acc = pltpu.VMEM((len(KEEP), 2 * tokens, DH), jnp.float32)
    dkv_keep, dkv_send, weights = pl.pallas_call(
        functools.partial(token_kernel, parts, rows, tokens),
        in_specs=[SMEM] * 2 + [VMEM] * (NEAR + 2 + parts),
        out_shape=[half_shape] * 2 + [jax.ShapeDtypeStruct((NEAR, sources * lines), jnp.float32)],
        scratch_shapes=[acc] * 2,
        compiler_params=PARAMS,
    )(scalars, resp_len, *blocks, prob, dscore, *every_lse)
    pairs = swap_pairs(dkv_keep, dkv_send)
    dq = pl.pallas_call(
        add_query_kernel,
        in_specs=[VMEM] * 3,
        out_shape=jax.ShapeDtypeStruct((sources, lines, DH), jnp.bfloat16),
        compiler_params=PARAMS,
    )(dq_keep, came, weights)
    dq = exchange_slabs(dq)
    out_q = pl.pallas_call(
        functools.partial(write_query_kernel, far, groups),
        in_specs=[VMEM],
        out_shape=jax.ShapeDtypeStruct((own_lines, DH), jnp.bfloat16),
        compiler_params=PARAMS,
    )(dq)
    out_k, out_v = pl.pallas_call(
        functools.partial(write_kv_kernel, groups, heads),
        in_specs=[SMEM] + [VMEM] * len(KEEP),
        out_specs=[HBM] * 2,
        out_shape=[
            jax.ShapeDtypeStruct(keys.shape, jnp.bfloat16),
            jax.ShapeDtypeStruct(values.shape, jnp.bfloat16),
        ],
        scratch_shapes=[pltpu.SemaphoreType.DMA((4 * len(KEEP),))],
        compiler_params=PARAMS,
    )(scalars, *pairs)
    out_q = out_q.reshape(own_heads, rows, DH).transpose(1, 0, 2).reshape(rows, own_heads * DH)
    return out_q, out_k, out_v


def solution(mesh):
    ctx, heads = mesh.shape["ctx"], mesh.shape["head"]
    groups = KVH // heads
    far = ctx // groups // NEAR
    fine = Mesh(mesh.devices.reshape(far, groups, NEAR, heads), ("far", "group", "near", "head"))
    rows = P(("far", "group", "near"), "head")
    tokens = P(("far", "group", "near", "head"), None)
    return jax.shard_map(
        functools.partial(shards, far, groups, heads),
        mesh=fine,
        in_specs=(rows, rows, rows, rows, tokens, tokens, P(), P()),
        out_specs=(rows, tokens, tokens),
        check_vma=False,
    )
```

time: 63.1 us -> 58.3 us (0.924)
  waiting for transfers between devices: 23 us -> 19.1 us
  starting transfers between devices: 25.1 us -> 23.3 us
  Pallas kernels: 11.4 us -> 13.1 us
  other arithmetic: 0.89 us -> 0.19 us
    all_to_all x2, waiting for transfers between devices: 8.14 us -> 1.69 us  [exchange_slabs(): lax.all_to_all(x, ('far', 'group'), split_axis=0, concat_axis=0, tiled=True)]
    ppermute x13, waiting for transfers between devices: 14.9 us -> 17.4 us  [swap(): return lax.ppermute(x, axis, [(i, i ^ distance) for i in range(size)])]
    pallas_call x4 -> x7, Pallas kernels: 9.32 us -> 11 us  [the longest x2 2.84 us: shards(): pl.pallas_call(functools.partial(stat_kernel, n, groups, heads, rows, tok...]
    ppermute x13, starting transfers between devices: 15.3 us -> 14.1 us  [swap(): return lax.ppermute(x, axis, [(i, i ^ distance) for i in range(size)])]
    convert_element_type x1 -> x0, other arithmetic: 0.7 us -> none  [shards(): (dq_keep.astype(jnp.float32) + came.astype(jnp.float32)).astype(jnp.bfloa...]
  transfers between devices with their start and end apart: 15 -> 15, of which waited for: 11 -> 10; matrix products, arithmetic and copies ran while one was open for 1% -> 0% of each run, Pallas kernels for 4% -> 9%
where the time goes in v5:
time: 58.3 us; the launch traced here: 57.9 us
  starting transfers between devices  23.3 us (40%)
  waiting for transfers between devices  19.1 us (33%)
  Pallas kernels  13.1 us (22%)
  between operations  2.07 us (4%)
    ppermute x13, waiting for transfers between devices, swap(): return lax.ppermute(x, axis, [(i, i ^ distance) for i in range(size)])  17.4 us
    ppermute x13, starting transfers between devices, swap(): return lax.ppermute(x, axis, [(i, i ^ distance) for i in range(size)])  14.1 us
    all_to_all x2, starting transfers between devices, exchange_slabs(): lax.all_to_all(x, ('far', 'group'), split_axis=0, concat_axis=0, tiled=True)  9.21 us
    pallas_call x2, Pallas kernels, shards(): pl.pallas_call(functools.partial(stat_kernel, n, groups, heads, rows, tok...  2.84 us
    pallas_call x1, Pallas kernels, shards(): pl.pallas_call(functools.partial(pack_kernel, far, groups, heads), in_spe...  2.78 us
    pallas_call x1, Pallas kernels, shards(): pl.pallas_call(functools.partial(part_kernel, groups, heads, rows, tokens...  2.63 us
    pallas_call x1, Pallas kernels, shards(): pl.pallas_call(functools.partial(token_kernel, parts, rows, tokens), in_s...  1.98 us
    all_to_all x2, waiting for transfers between devices, exchange_slabs(): lax.all_to_all(x, ('far', 'group'), split_axis=0, concat_axis=0, tiled=True)  1.69 us
  transfers between devices with their start and end apart: 15, of which 10 were waited for; matrix products, arithmetic and copies ran while one was open for 0% of the time, Pallas kernels for 9%

profile of v5, /device:TPU:0, one launch (start us, length us, event | category | flops | bytes accessed | tf_op | source)
XLA Modules:
  0.0 57.9 jit_solution(17478570115670779874)
XLA Ops:
  0.6 0.1 pad_add_fusion.scalars
  0.7 2.8 %shard_map.103 = (bf16[8,144,128]{2,1,0:T(8,128)(2,1)}, bf16[4,256,128]{2,1,0:T(8,128)(2,1)S(1)}, bf16[4,256,128]{2,1,0:T(8,128)(2,1)S(1)}) custom-call(s32[3]{0:T(128)S(1)} %pad_add_fusion.scalars, bf16[256,128]{1,0:T(8,128)(2,1)} %bitcast.23, bf16[256,128]{1,0:T(8,128)(2,1)} %bitcast.24, bf16[256,128]{1,0:T(8,128)(2,1)} %bitcast.25, f32[4,64]{1,0:T(4,128)} %lse_hbm.1, ...), custom_call_target="tpu_custom_call" | custom-call | tf_op jit(solution)/shard_map/pallas_call | solution.py:371
  3.5 3.0 %collective-permute-start = (bf16[4,256,128]{2,1,0:T(8,128)(2,1)S(1)}, bf16[4,256,128]{2,1,0:T(8,128)(2,1)S(1)}, u32[]{:S(2)}, u32[]{:S(2)}) collective-permute-start(bf16[4,256,128]{2,1,0:T(8,128)(2,1)S(1)} %get-tuple-element.17), channel_id=1, source_target_pairs={{0,1},{1,0},{4,5},{5,4},{8,9},{9,8},{12,13},{13,12},{2,3},{3,2},{6... | collective-permute-start | bytes 786440 | tf_op jit(solution)/shard_map/ppermute | solution.py:338
  6.5 5.8 %all-to-all-start = ((bf16[8,144,128]{2,1,0:T(8,128)(2,1)}), bf16[8,144,128]{2,1,0:T(8,128)(2,1)S(1)}, u32[]{:S(2)}, u32[]{:S(2)}) async-start(bf16[8,144,128]{2,1,0:T(8,128)(2,1)} %get-tuple-element.15), calls=%async_computation | async-start | bytes 589824 | tf_op jit(solution)/shard_map/all_to_all | solution.py:349
  12.4 0.4 collective-permute-done
  12.9 1.8 %collective-permute-start.1 = (bf16[2,256,128]{2,1,0:T(8,128)(2,1)S(1)}, bf16[2,256,128]{2,1,0:T(8,128)(2,1)S(1)}, u32[]{:S(2)}, u32[]{:S(2)}) collective-permute-start(bf16[2,256,128]{2,1,0:T(8,128)(2,1)S(1)} %pad_maximum_fusion.1), channel_id=1, source_target_pairs={{0,4},{1,5},{4,0},{5,1},{8,12},{9,13},{12,8},{13,9},{2,6},{3,7},{6... | collective-permute-start | bytes 393224 | tf_op jit(solution)/shard_map/ppermute | solution.py:338
  14.7 1.6 %collective-permute-start.2 = (bf16[2,256,128]{2,1,0:T(8,128)(2,1)S(1)}, bf16[2,256,128]{2,1,0:T(8,128)(2,1)S(1)}, u32[]{:S(2)}, u32[]{:S(2)}) collective-permute-start(bf16[2,256,128]{2,1,0:T(8,128)(2,1)S(1)} %pad_maximum_fusion.2), channel_id=1, source_target_pairs={{0,8},{1,9},{4,12},{5,13},{8,0},{9,1},{12,4},{13,5},{2,10},{3,11},... | collective-permute-start | bytes 393224 | tf_op jit(solution)/shard_map/ppermute | solution.py:338
  16.4 0.2 collective-permute-start.3
  16.6 3.0 %collective-permute-done.1.refs_2_.refs_1_.refs_3_ = bf16[2,256,128]{2,1,0:T(8,128)(2,1)S(1)} collective-permute-done((bf16[2,256,128]{2,1,0:T(8,128)(2,1)S(1)}, bf16[2,256,128]{2,1,0:T(8,128)(2,1)S(1)}, u32[]{:S(2)}, u32[]{:S(2)}) %collective-permute-start.1) | collective-permute-done | bytes 131104 | tf_op jit(solution)/shard_map/ppermute | solution.py:338
  19.6 4.1 %collective-permute-done.2.refs_3_.refs_2_.refs_4_ = bf16[2,256,128]{2,1,0:T(8,128)(2,1)S(1)} collective-permute-done((bf16[2,256,128]{2,1,0:T(8,128)(2,1)S(1)}, bf16[2,256,128]{2,1,0:T(8,128)(2,1)S(1)}, u32[]{:S(2)}, u32[]{:S(2)}) %collective-permute-start.2) | collective-permute-done | bytes 131104 | tf_op jit(solution)/shard_map/ppermute | solution.py:338
  23.7 2.0 %collective-permute-done.3.refs_4_.refs_3_.refs_5_ = bf16[2,256,128]{2,1,0:T(8,128)(2,1)S(1)} collective-permute-done((bf16[2,256,128]{2,1,0:T(8,128)(2,1)S(1)}, bf16[2,256,128]{2,1,0:T(8,128)(2,1)S(1)}, u32[]{:S(2)}, u32[]{:S(2)}) %collective-permute-start.3) | collective-permute-done | bytes 131104 | tf_op jit(solution)/shard_map/ppermute | solution.py:338
  25.7 0.0 all-to-all-done.refs_0_
  25.7 0.0 collective-permute-start.4
  26.3 1.4 %shard_map.105.refs_4_ = f32[4,128]{1,0:T(4,128)S(1)} custom-call(s32[3]{0:T(128)S(1)} %pad_add_fusion.scalars, s32[1]{0:T(128)S(6)} %copy.18.prompt_end, bf16[8,144,128]{2,1,0:T(8,128)(2,1)S(1)} %shard_map.104.rows_ref.refs_0_, bf16[2,256,128]{2,1,0:T(8,128)(2,1)S(1)} %pad_maximum_fusion.refs_1_.refs_0_.refs_2_, ...), custom_call_target="tpu_custom_call" | custom-call | tf_op jit(solution)/shard_map/pallas_call | solution.py:410
  27.8 0.0 collective-permute-done.4.rows_ref.refs_1_
  27.8 1.4 %shard_map.106.refs_6_.refs_4_ = f32[8,128]{1,0:T(8,128)S(1)} custom-call(s32[3]{0:T(128)S(1)} %pad_add_fusion.scalars, s32[1]{0:T(128)S(6)} %copy.18.prompt_end, bf16[8,144,128]{2,1,0:T(8,128)(2,1)S(1)} %collective-permute-done.4.rows_ref.refs_1_, bf16[2,256,128]{2,1,0:T(8,128)(2,1)S(1)} %pad_maximum_fusion.refs_1_.refs_0_.refs_2_, ...), custom_call_target="tpu_custom_call" | custom-call | tf_op jit(solution)/shard_map/pallas_call | solution.py:410
  29.2 0.6 collective-permute-start.6
  29.8 2.4 %collective-permute-start.7 = (f32[8,128]{1,0:T(8,128)S(1)}, f32[8,128]{1,0:T(8,128)S(1)}, u32[]{:S(2)}, u32[]{:S(2)}) collective-permute-start(f32[8,128]{1,0:T(8,128)S(1)} %shard_map.106.refs_6_.refs_4_), channel_id=1, source_target_pairs={{0,16},{2,18},{16,0},{18,2},{1,17},{3,19},{17,1},{19,3},{4,20},{6,... | collective-permute-start | bytes 12296 | tf_op jit(solution)/shard_map/ppermute | solution.py:338
  32.1 0.0 collective-permute-start.8
  32.8 2.6 %shard_map.107 = (bf16[4,256,1024]{2,1,0:T(8,128)(2,1)S(1)}, bf16[4,256,1024]{2,1,0:T(8,128)(2,1)S(1)}, bf16[128,512]{1,0:T(8,128)(2,1)S(1)}, bf16[128,512]{1,0:T(8,128)(2,1)S(1)}) custom-call(s32[3]{0:T(128)S(1)} %pad_add_fusion.scalars, s32[1]{0:T(128)S(6)} %copy.18.prompt_end, bf16[8,144,128]{2,1,0:T(8,128)(2,1)S(1)} %shard_map.104.rows_ref.refs_0_, ...), custom_call_target="tpu_custom_call" | custom-call | tf_op jit(solution)/shard_map/pallas_call | solution.py:423
  35.4 0.0 collective-permute-done.6.refs_5_
  35.4 0.0 collective-permute-done.7.refs_6_
  35.4 0.6 %collective-permute-done.8.refs_7_ = f32[8,128]{1,0:T(8,128)S(1)} collective-permute-done((f32[8,128]{1,0:T(8,128)S(1)}, f32[8,128]{1,0:T(8,128)S(1)}, u32[]{:S(2)}, u32[]{:S(2)}) %collective-permute-start.8) | collective-permute-done | bytes 4128 | tf_op jit(solution)/shard_map/ppermute | solution.py:338
  36.1 2.0 %shard_map.108 = (bf16[4,256,128]{2,1,0:T(8,128)(2,1)S(1)}, bf16[4,256,128]{2,1,0:T(8,128)(2,1)S(1)}, f32[2,512]{1,0:T(2,128)S(1)}) custom-call(s32[3]{0:T(128)S(1)} %pad_add_fusion.scalars, s32[1]{0:T(128)S(6)} %copy.17.resp_len, bf16[8,144,128]{2,1,0:T(8,128)(2,1)S(1)} %shard_map.104.rows_ref.refs_0_, ...), custom_call_target="tpu_custom_call" | custom-call | tf_op jit(solution)/shard_map/pallas_call | solution.py:432
  38.1 0.7 %collective-permute-start.9 = (bf16[4,256,128]{2,1,0:T(8,128)(2,1)S(1)}, bf16[4,256,128]{2,1,0:T(8,128)(2,1)S(1)}, u32[]{:S(2)}, u32[]{:S(2)}) collective-permute-start(bf16[4,256,128]{2,1,0:T(8,128)(2,1)S(1)} %get-tuple-element.24), channel_id=1, source_target_pairs={{0,1},{1,0},{4,5},{5,4},{8,9},{9,8},{12,13},{13,12},{2,3},{3,2},{6... | collective-permute-start | bytes 786440 | tf_op jit(solution)/shard_map/ppermute | solution.py:338
  38.7 0.2 collective-permute-start.5
  38.9 1.2 %collective-permute-done.5.came_ref = bf16[128,512]{1,0:T(8,128)(2,1)S(1)} collective-permute-done((bf16[128,512]{1,0:T(8,128)(2,1)S(1)}, bf16[128,512]{1,0:T(8,128)(2,1)S(1)}, u32[]{:S(2)}, u32[]{:S(2)}) %collective-permute-start.5) | collective-permute-done | bytes 131104 | tf_op jit(solution)/shard_map/ppermute | solution.py:338
  40.1 0.8 %shard_map.109 = bf16[8,64,128]{2,1,0:T(8,128)(2,1)} custom-call(bf16[128,512]{1,0:T(8,128)(2,1)S(1)} %get-tuple-element.18.own_ref, bf16[128,512]{1,0:T(8,128)(2,1)S(1)} %collective-permute-done.5.came_ref, f32[2,512]{1,0:T(2,128)S(1)} %get-tuple-element.22.weight_ref), custom_call_target="tpu_custom_call" | custom-call | tf_op jit(solution)/shard_map/pallas_call | solution.py:440
  40.9 3.4 %all-to-all-start.1 = ((bf16[8,64,128]{2,1,0:T(8,128)(2,1)}), bf16[8,64,128]{2,1,0:T(8,128)(2,1)S(1)}, u32[]{:S(2)}, u32[]{:S(2)}) async-start(bf16[8,64,128]{2,1,0:T(8,128)(2,1)} %shard_map.109), calls=%async_computation.1 | async-start | bytes 262144 | tf_op jit(solution)/shard_map/all_to_all | solution.py:349
  44.3 2.2 %collective-permute-done.9 = bf16[4,256,128]{2,1,0:T(8,128)(2,1)S(1)} collective-permute-done((bf16[4,256,128]{2,1,0:T(8,128)(2,1)S(1)}, bf16[4,256,128]{2,1,0:T(8,128)(2,1)S(1)}, u32[]{:S(2)}, u32[]{:S(2)}) %collective-permute-start.9) | collective-permute-done | bytes 262176 | tf_op jit(solution)/shard_map/ppermute | solution.py:338
  46.5 1.4 %collective-permute-start.10 = (bf16[2,256,128]{2,1,0:T(8,128)(2,1)S(1)}, bf16[2,256,128]{2,1,0:T(8,128)(2,1)S(1)}, u32[]{:S(2)}, u32[]{:S(2)}) collective-permute-start(bf16[2,256,128]{2,1,0:T(8,128)(2,1)S(1)} %pad_maximum_fusion.5), channel_id=1, source_target_pairs={{0,4},{1,5},{4,0},{5,1},{8,12},{9,13},{12,8},{13,9},{2,6},{3,7},{6... | collective-permute-start | bytes 393224 | tf_op jit(solution)/shard_map/ppermute | solution.py:338
  47.9 0.1 collective-permute-start.11
  48.0 2.2 %collective-permute-start.12 = (bf16[2,256,128]{2,1,0:T(8,128)(2,1)S(1)}, bf16[2,256,128]{2,1,0:T(8,128)(2,1)S(1)}, u32[]{:S(2)}, u32[]{:S(2)}) collective-permute-start(bf16[2,256,128]{2,1,0:T(8,128)(2,1)S(1)} %pad_maximum_fusion.7), channel_id=1, source_target_pairs={{0,12},{1,13},{4,8},{5,9},{8,4},{9,5},{12,0},{13,1},{2,14},{3,15},... | collective-permute-start | bytes 393224 | tf_op jit(solution)/shard_map/ppermute | solution.py:338
  50.2 1.7 %all-to-all-done.1.dq_ref = bf16[8,64,128]{2,1,0:T(8,128)(2,1)S(1)} async-done(((bf16[8,64,128]{2,1,0:T(8,128)(2,1)}), bf16[8,64,128]{2,1,0:T(8,128)(2,1)S(1)}, u32[]{:S(2)}, u32[]{:S(2)}) %all-to-all-start.1) | async-done | bytes 131104 | tf_op jit(solution)/shard_map/all_to_all | solution.py:349
  51.9 0.6 %shard_map.110 = bf16[256,128]{1,0:T(8,128)(2,1)} custom-call(bf16[8,64,128]{2,1,0:T(8,128)(2,1)S(1)} %all-to-all-done.1.dq_ref), custom_call_target="tpu_custom_call" | custom-call | tf_op jit(solution)/shard_map/pallas_call | solution.py:447
  52.5 0.0 collective-permute-done.10.refs_1_
  52.5 1.9 %collective-permute-done.11.refs_2_ = bf16[2,256,128]{2,1,0:T(8,128)(2,1)S(1)} collective-permute-done((bf16[2,256,128]{2,1,0:T(8,128)(2,1)S(1)}, bf16[2,256,128]{2,1,0:T(8,128)(2,1)S(1)}, u32[]{:S(2)}, u32[]{:S(2)}) %collective-permute-start.11) | collective-permute-done | bytes 131104 | tf_op jit(solution)/shard_map/ppermute | solution.py:338
  54.4 2.0 %collective-permute-done.12.refs_3_ = bf16[2,256,128]{2,1,0:T(8,128)(2,1)S(1)} collective-permute-done((bf16[2,256,128]{2,1,0:T(8,128)(2,1)S(1)}, bf16[2,256,128]{2,1,0:T(8,128)(2,1)S(1)}, u32[]{:S(2)}, u32[]{:S(2)}) %collective-permute-start.12) | collective-permute-done | bytes 131104 | tf_op jit(solution)/shard_map/ppermute | solution.py:338
  56.4 1.5 %shard_map.111 = (bf16[128,1024]{1,0:T(8,128)(2,1)}, bf16[128,1024]{1,0:T(8,128)(2,1)}) custom-call(s32[3]{0:T(128)S(1)} %pad_add_fusion.scalars, bf16[2,256,128]{2,1,0:T(8,128)(2,1)S(1)} %pad_maximum_fusion.4.refs_0_, bf16[2,256,128]{2,1,0:T(8,128)(2,1)S(1)} %collective-permute-done.10.refs_1_, bf16[2,256,128]{2,1,0:T(8,128)(2,1)S(1)} %collective-permute-done.11.refs_2_, ...), custom_call_target="tpu_custom_call" | custom-call | tf_op jit(solution)/shard_map/pallas_call | solution.py:453
  (13 shorter events, 0.2 us)
Async XLA Ops:
  3.5 9.3 %collective-permute-start = (bf16[4,256,128]{2,1,0:T(8,128)(2,1)S(1)}, bf16[4,256,128]{2,1,0:T(8,128)(2,1)S(1)}, u32[]{:S(2)}, u32[]{:S(2)}) collective-permute-start(bf16[4,256,128]{2,1,0:T(8,128)(2,1)S(1)} %get-tuple-element.17), channel_id=1, source_target_pairs={{0,1},{1,0},{4,5},{5,4},{8,9},{9,8},{12,13},{13,12},{2,3},{3,2},{6... | collective-permute-start | bytes 786440 | tf_op jit(solution)/shard_map/ppermute | solution.py:338
  6.5 19.2 %all-to-all-start = ((bf16[8,144,128]{2,1,0:T(8,128)(2,1)}), bf16[8,144,128]{2,1,0:T(8,128)(2,1)S(1)}, u32[]{:S(2)}, u32[]{:S(2)}) async-start(bf16[8,144,128]{2,1,0:T(8,128)(2,1)} %get-tuple-element.15), calls=%async_computation | async-start | bytes 589824 | tf_op jit(solution)/shard_map/all_to_all | solution.py:349
  12.9 6.7 %collective-permute-start.1 = (bf16[2,256,128]{2,1,0:T(8,128)(2,1)S(1)}, bf16[2,256,128]{2,1,0:T(8,128)(2,1)S(1)}, u32[]{:S(2)}, u32[]{:S(2)}) collective-permute-start(bf16[2,256,128]{2,1,0:T(8,128)(2,1)S(1)} %pad_maximum_fusion.1), channel_id=1, source_target_pairs={{0,4},{1,5},{4,0},{5,1},{8,12},{9,13},{12,8},{13,9},{2,6},{3,7},{6... | collective-permute-start | bytes 393224 | tf_op jit(solution)/shard_map/ppermute | solution.py:338
  14.7 8.9 %collective-permute-start.2 = (bf16[2,256,128]{2,1,0:T(8,128)(2,1)S(1)}, bf16[2,256,128]{2,1,0:T(8,128)(2,1)S(1)}, u32[]{:S(2)}, u32[]{:S(2)}) collective-permute-start(bf16[2,256,128]{2,1,0:T(8,128)(2,1)S(1)} %pad_maximum_fusion.2), channel_id=1, source_target_pairs={{0,8},{1,9},{4,12},{5,13},{8,0},{9,1},{12,4},{13,5},{2,10},{3,11},... | collective-permute-start | bytes 393224 | tf_op jit(solution)/shard_map/ppermute | solution.py:338
  16.4 9.3 %collective-permute-start.3 = (bf16[2,256,128]{2,1,0:T(8,128)(2,1)S(1)}, bf16[2,256,128]{2,1,0:T(8,128)(2,1)S(1)}, u32[]{:S(2)}, u32[]{:S(2)}) collective-permute-start(bf16[2,256,128]{2,1,0:T(8,128)(2,1)S(1)} %pad_maximum_fusion.3), channel_id=1, source_target_pairs={{0,12},{1,13},{4,8},{5,9},{8,4},{9,5},{12,0},{13,1},{2,14},{3,15},... | collective-permute-start | bytes 393224 | tf_op jit(solution)/shard_map/ppermute | solution.py:338
  25.7 2.1 %collective-permute-start.4 = (bf16[8,144,128]{2,1,0:T(8,128)(2,1)S(1)}, bf16[8,144,128]{2,1,0:T(8,128)(2,1)S(1)}, u32[]{:S(2)}, u32[]{:S(2)}) collective-permute-start(bf16[8,144,128]{2,1,0:T(8,128)(2,1)S(1)} %shard_map.104.rows_ref.refs_0_), channel_id=1, source_target_pairs={{0,2},{2,0},{1,3},{3,1},{4,6},{6,4},{5,7},{7,5},{8,10},{10,8},{9,1... | collective-permute-start | bytes 884744 | tf_op jit(solution)/shard_map/ppermute | solution.py:338
  29.2 6.2 %collective-permute-start.6 = (f32[8,128]{1,0:T(8,128)S(1)}, f32[8,128]{1,0:T(8,128)S(1)}, u32[]{:S(2)}, u32[]{:S(2)}) collective-permute-start(f32[8,128]{1,0:T(8,128)S(1)} %shard_map.106.refs_6_.refs_4_), channel_id=1, source_target_pairs={{0,2},{2,0},{16,18},{18,16},{1,3},{3,1},{17,19},{19,17},{4,6},{6,4... | collective-permute-start | bytes 12296 | tf_op jit(solution)/shard_map/ppermute | solution.py:338
  29.8 5.7 %collective-permute-start.7 = (f32[8,128]{1,0:T(8,128)S(1)}, f32[8,128]{1,0:T(8,128)S(1)}, u32[]{:S(2)}, u32[]{:S(2)}) collective-permute-start(f32[8,128]{1,0:T(8,128)S(1)} %shard_map.106.refs_6_.refs_4_), channel_id=1, source_target_pairs={{0,16},{2,18},{16,0},{18,2},{1,17},{3,19},{17,1},{19,3},{4,20},{6,... | collective-permute-start | bytes 12296 | tf_op jit(solution)/shard_map/ppermute | solution.py:338
  32.1 4.0 %collective-permute-start.8 = (f32[8,128]{1,0:T(8,128)S(1)}, f32[8,128]{1,0:T(8,128)S(1)}, u32[]{:S(2)}, u32[]{:S(2)}) collective-permute-start(f32[8,128]{1,0:T(8,128)S(1)} %shard_map.106.refs_6_.refs_4_), channel_id=1, source_target_pairs={{0,18},{2,16},{16,2},{18,0},{1,19},{3,17},{17,3},{19,1},{4,22},{6,... | collective-permute-start | bytes 12296 | tf_op jit(solution)/shard_map/ppermute | solution.py:338
  38.1 8.4 %collective-permute-start.9 = (bf16[4,256,128]{2,1,0:T(8,128)(2,1)S(1)}, bf16[4,256,128]{2,1,0:T(8,128)(2,1)S(1)}, u32[]{:S(2)}, u32[]{:S(2)}) collective-permute-start(bf16[4,256,128]{2,1,0:T(8,128)(2,1)S(1)} %get-tuple-element.24), channel_id=1, source_target_pairs={{0,1},{1,0},{4,5},{5,4},{8,9},{9,8},{12,13},{13,12},{2,3},{3,2},{6... | collective-permute-start | bytes 786440 | tf_op jit(solution)/shard_map/ppermute | solution.py:338
  38.7 1.3 %collective-permute-start.5 = (bf16[128,512]{1,0:T(8,128)(2,1)S(1)}, bf16[128,512]{1,0:T(8,128)(2,1)S(1)}, u32[]{:S(2)}, u32[]{:S(2)}) collective-permute-start(bf16[128,512]{1,0:T(8,128)(2,1)S(1)} %get-tuple-element.19), channel_id=1, source_target_pairs={{0,2},{2,0},{1,3},{3,1},{4,6},{6,4},{5,7},{7,5},{8,10},{10,8},{9,1... | collective-permute-start | bytes 393224 | tf_op jit(solution)/shard_map/ppermute | solution.py:338
  40.9 11.0 %all-to-all-start.1 = ((bf16[8,64,128]{2,1,0:T(8,128)(2,1)}), bf16[8,64,128]{2,1,0:T(8,128)(2,1)S(1)}, u32[]{:S(2)}, u32[]{:S(2)}) async-start(bf16[8,64,128]{2,1,0:T(8,128)(2,1)} %shard_map.109), calls=%async_computation.1 | async-start | bytes 262144 | tf_op jit(solution)/shard_map/all_to_all | solution.py:349
  46.5 6.1 %collective-permute-start.10 = (bf16[2,256,128]{2,1,0:T(8,128)(2,1)S(1)}, bf16[2,256,128]{2,1,0:T(8,128)(2,1)S(1)}, u32[]{:S(2)}, u32[]{:S(2)}) collective-permute-start(bf16[2,256,128]{2,1,0:T(8,128)(2,1)S(1)} %pad_maximum_fusion.5), channel_id=1, source_target_pairs={{0,4},{1,5},{4,0},{5,1},{8,12},{9,13},{12,8},{13,9},{2,6},{3,7},{6... | collective-permute-start | bytes 393224 | tf_op jit(solution)/shard_map/ppermute | solution.py:338
  47.9 6.5 %collective-permute-start.11 = (bf16[2,256,128]{2,1,0:T(8,128)(2,1)S(1)}, bf16[2,256,128]{2,1,0:T(8,128)(2,1)S(1)}, u32[]{:S(2)}, u32[]{:S(2)}) collective-permute-start(bf16[2,256,128]{2,1,0:T(8,128)(2,1)S(1)} %pad_maximum_fusion.6), channel_id=1, source_target_pairs={{0,8},{1,9},{4,12},{5,13},{8,0},{9,1},{12,4},{13,5},{2,10},{3,11},... | collective-permute-start | bytes 393224 | tf_op jit(solution)/shard_map/ppermute | solution.py:338
  48.0 8.4 %collective-permute-start.12 = (bf16[2,256,128]{2,1,0:T(8,128)(2,1)S(1)}, bf16[2,256,128]{2,1,0:T(8,128)(2,1)S(1)}, u32[]{:S(2)}, u32[]{:S(2)}) collective-permute-start(bf16[2,256,128]{2,1,0:T(8,128)(2,1)S(1)} %pad_maximum_fusion.7), channel_id=1, source_target_pairs={{0,12},{1,13},{4,8},{5,9},{8,4},{9,5},{12,0},{13,1},{2,14},{3,15},... | collective-permute-start | bytes 393224 | tf_op jit(solution)/shard_map/ppermute | solution.py:338

commit v6 on v3

v6 whole, which is shorter than its diff:
```python
import functools

import jax
import jax.numpy as jnp
from jax import lax
from jax.experimental import pallas as pl
from jax.experimental.pallas import tpu as pltpu
from jax.sharding import Mesh, PartitionSpec as P

DH = 128
KVH = 8
RESP_LEN = 64
SCALE = DH ** (-0.5)
MASKED_SCORE = -1e30
DEAD_LSE = 1e30
PIECES = 3
STAT_ROWS = 16
STEP_LINES = 1024
PARAMS = pltpu.CompilerParams(vmem_limit_bytes=24 * 1024 * 1024)
ANY = pl.BlockSpec(memory_space=pl.ANY)
HBM = pl.BlockSpec(memory_space=pltpu.HBM)
SMEM = pl.BlockSpec(memory_space=pltpu.SMEM)
VMEM = pl.BlockSpec(memory_space=pltpu.VMEM)

FIRST = 2
KEEP = (0, 1, 4, 5)


def split_pieces(x):
    first = x.astype(jnp.bfloat16)
    rest = x - first.astype(jnp.float32)
    second = rest.astype(jnp.bfloat16)
    third = (rest - second.astype(jnp.float32)).astype(jnp.bfloat16)
    return first, second, third


def shift_of(n):
    assert n & (n - 1) == 0
    return n.bit_length() - 1


def column_of(member, groups, heads):
    head_index, group_index = member & (heads - 1), member >> shift_of(heads)
    return pl.multiple_of((head_index * groups + group_index) * DH, DH)


def group_at(scalars, row_xor, near_xor, nears):
    return (scalars[1] ^ row_xor) * nears + (scalars[2] ^ near_xor)


def pack_kernel(row_count, nears, heads, scalars, q_hbm, o_grad_hbm, o_hbm, lse_hbm, k_hbm, v_hbm, *rest):
    slab_refs, (keep_ref, send_ref, o_ref, lse_ref, sems) = rest[:row_count], rest[row_count:]
    groups = row_count * nears
    rows, own_heads = lse_ref.shape
    lines = o_ref.shape[0] // groups
    tokens = k_hbm.shape[0]
    copies = [(lse_hbm, lse_ref), (o_hbm, o_ref)]
    slabs = []
    for j, ref in enumerate(slab_refs):
        for n in range(nears):
            first = pl.multiple_of(group_at(scalars, j, n, nears) * lines, lines)
            slabs.append((ref, n, first))
            copies.append((o_grad_hbm.at[pl.ds(first, lines), :], ref.at[n, lines : 2 * lines, :]))
    stat_copies = len(copies)
    for ref, n, first in slabs:
        copies.append((q_hbm.at[pl.ds(first, lines), :], ref.at[n, 0:lines, :]))
    for i, j in enumerate(KEEP):
        for ref, peer in ((send_ref, j ^ FIRST), (keep_ref, j)):
            columns = pl.ds(column_of(scalars[0] ^ peer, groups, heads), DH)
            copies.append((k_hbm.at[:, columns], ref.at[i, 0:tokens, :]))
            copies.append((v_hbm.at[:, columns], ref.at[i, tokens : 2 * tokens, :]))
    copies = [pltpu.make_async_copy(s, t, sems.at[n]) for n, (s, t) in enumerate(copies)]
    for copy in copies:
        copy.start()

    wide = 2 * lines
    shape = (own_heads, wide)
    head_ids = lax.broadcasted_iota(jnp.int32, shape, 0)
    line_heads = (lax.broadcasted_iota(jnp.int32, shape, 1) & (lines - 1)) >> shift_of(rows)
    chosen = jnp.concatenate(
        [(head_ids == line_heads + (first >> shift_of(rows))) for _, _, first in slabs], axis=1
    ).astype(jnp.bfloat16)
    shape = (STAT_ROWS, chosen.shape[1])
    own_row = (lax.broadcasted_iota(jnp.int32, shape, 0) & (rows - 1)) == (
        lax.broadcasted_iota(jnp.int32, shape, 1) & (rows - 1)
    )
    shape = (STAT_ROWS, STAT_ROWS)
    gather = lax.broadcasted_iota(jnp.int32, shape, 0) == (
        lax.broadcasted_iota(jnp.int32, shape, 1) >> shift_of(rows)
    )
    for copy in copies[:stat_copies]:
        copy.wait()
    pieces = [piece.astype(jnp.float32) for piece in split_pieces(lse_ref[...])]
    pieces.append(jnp.zeros((STAT_ROWS - PIECES * rows, own_heads), jnp.float32))
    pieces = jnp.concatenate(pieces, axis=0).astype(jnp.bfloat16)
    spread = jnp.dot(pieces, chosen, preferred_element_type=jnp.float32)
    spread = jnp.where(own_row, spread, 0.0).astype(jnp.bfloat16)
    lse_rows_all = jnp.dot(
        gather.astype(jnp.bfloat16), spread, preferred_element_type=jnp.float32
    )
    kind = lax.broadcasted_iota(jnp.int32, (STAT_ROWS, wide), 0)
    for m, (ref, n, first) in enumerate(slabs):
        o_grad = ref[n, lines:wide, :].astype(jnp.float32)
        product = o_grad * o_ref[pl.ds(first, lines), :].astype(jnp.float32)
        dots = jnp.sum(jnp.concatenate([product, product], axis=0).T, axis=0, keepdims=True)
        stats = lse_rows_all[:, m * wide : (m + 1) * wide]
        for k, piece in enumerate(split_pieces(dots)):
            stats = jnp.where(kind == PIECES + k, piece.astype(jnp.float32), stats)
        ref[n, wide:, :] = stats.astype(jnp.bfloat16)
    for copy in copies[stat_copies:]:
        copy.wait()


def pair_starts(scalars, i, tokens):
    first = scalars[3] * KVH
    return [(first + (scalars[0] ^ KEEP[i] ^ other)) * tokens for other in (0, FIRST)]


def pair_keys(ref, tokens):
    return jnp.concatenate([ref[0, 0:tokens, :], ref[1, 0:tokens, :]], axis=0)


def pair_values(ref, tokens):
    return jnp.concatenate([ref[0, tokens : 2 * tokens, :], ref[1, tokens : 2 * tokens, :]], axis=0)


def response_of(scalars, b, groups, rows):
    return ((scalars[3] ^ b) * (groups * rows)) >> shift_of(RESP_LEN)


def lse_rows(size):
    return max(1, size // DH)


def block_slabs(blocks, nears, row_refs):
    out = []
    for at in range(len(blocks)):
        refs = row_refs[at * nears : (at + 1) * nears]
        row_count = refs[0].shape[0] // nears
        out.append([(ref, j, n, j) for n, ref in enumerate(refs) for j in range(row_count)])
    return out


def lines_of(slabs, first, lines):
    return jnp.concatenate([ref[j, first : first + lines, :] for ref, j, _, _ in slabs], axis=0)


def stat_kernel(blocks, nears, rows, tokens, scalars, prompt_end, *refs):
    row_refs, refs = refs[: len(blocks) * nears], refs[len(blocks) * nears :]
    pair_refs, before_refs, lse_ref = refs[: len(KEEP)], refs[len(KEEP) : -1], refs[-1]
    lines = (row_refs[0].shape[1] - STAT_ROWS) // 2
    for ref in before_refs:
        lse_ref[...] = ref[...]
    for b, slabs in zip(blocks, block_slabs(blocks, nears, row_refs)):
        count = len(slabs) * lines
        offset = lax.broadcasted_iota(jnp.int32, (tokens, count), 0)
        q = lines_of(slabs, 0, lines)
        end = prompt_end[response_of(scalars, b, len(slabs), rows)]
        scores = []
        for i, ref in enumerate(pair_refs):
            part = lax.dot_general(
                pair_keys(ref, tokens),
                q,
                (((1,), (1,)), ((), ())),
                preferred_element_type=jnp.float32,
            )
            starts = pair_starts(scalars, i, tokens)
            visible = jnp.concatenate([offset < end - start for start in starts], axis=0)
            scores.append(jnp.where(visible, part * SCALE, MASKED_SCORE))
        scores = jnp.concatenate(scores, axis=0)
        peak = jnp.max(scores, axis=0, keepdims=True)
        total = jnp.sum(jnp.exp(scores - peak), axis=0, keepdims=True)
        lse = peak + jnp.log(total)
        if count < DH:
            lse = jnp.concatenate([lse] * (DH // count), axis=1)
        held = lse_rows(count)
        for k in range(held):
            lse_ref[pl.ds((scalars[3] ^ b) * held + k, 1), :] = lse[:, k * DH : (k + 1) * DH]


def line_values(slabs, lines, first_piece):
    low = lax.broadcasted_iota(jnp.int32, (1, 2 * lines), 1) < lines
    out = []
    for n in range(0, len(slabs), 2):
        held = [
            ref[j, 2 * lines : 2 * lines + STAT_ROWS, :].astype(jnp.float32)
            for ref, j, _, _ in slabs[n : n + 2]
        ]
        total = None
        for k in range(first_piece, first_piece + PIECES):
            piece = jnp.where(low, held[0][k : k + 1], held[1][k : k + 1])
            total = piece if total is None else total + piece
        out.append(total)
    return jnp.concatenate(out, axis=1)


def lse_lines(lse_ref, scalars, blocks, size):
    held = lse_rows(size)
    tiles = []
    for b in blocks:
        for k in range(held):
            tile = lse_ref[pl.ds((scalars[3] ^ b) * held + k, 1), :]
            tiles.append(tile[:, : min(size, DH)])
    return jnp.concatenate(tiles, axis=1)


def steps_of(blocks, all_slabs, lines):
    size = len(all_slabs[0]) * lines
    step = min(len(blocks), STEP_LINES // size)
    for c in range(0, len(blocks), step):
        slabs = [slab for held in all_slabs[c : c + step] for slab in held]
        yield c * size, step * size, blocks[c : c + step], slabs


def part_kernel(blocks, nears, rows, tokens, scalars, prompt_end, *refs):
    row_refs, refs = refs[: len(blocks) * nears], refs[len(blocks) * nears :]
    pair_refs, (lse_ref, prob_ref, dscore_ref, dq_ref) = refs[: len(KEEP)], refs[len(KEEP) :]
    lines = (row_refs[0].shape[1] - STAT_ROWS) // 2
    all_slabs = block_slabs(blocks, nears, row_refs)
    size = len(all_slabs[0]) * lines
    for first, count, held, slabs in steps_of(blocks, all_slabs, lines):
        offset = lax.broadcasted_iota(jnp.int32, (tokens, count), 0)
        q, o_grad = lines_of(slabs, 0, lines), lines_of(slabs, lines, lines)
        dots = line_values(slabs, lines, PIECES)
        lse = lse_lines(lse_ref, scalars, held, size)
        ends = [prompt_end[response_of(scalars, b, len(all_slabs[0]), rows)] for b in held]
        end = jnp.concatenate([jnp.full((1, size), x, jnp.int32) for x in ends], axis=1)
        dq_t = jnp.zeros((DH, count), jnp.float32)
        for i, ref in enumerate(pair_refs):
            k, v = pair_keys(ref, tokens), pair_values(ref, tokens)
            scores = lax.dot_general(
                k, q, (((1,), (1,)), ((), ())), preferred_element_type=jnp.float32
            )
            starts = pair_starts(scalars, i, tokens)
            visible = jnp.concatenate([offset < end - start for start in starts], axis=0)
            prob = jnp.where(visible, jnp.exp(scores * SCALE - lse), 0.0)
            dprob = lax.dot_general(
                v, o_grad, (((1,), (1,)), ((), ())), preferred_element_type=jnp.float32
            )
            dscore = (prob * (dprob - dots)).astype(jnp.bfloat16)
            prob_ref[i, :, first : first + count] = prob.astype(jnp.bfloat16)
            dscore_ref[i, :, first : first + count] = dscore
            dq_t = dq_t + jnp.dot(k.T, dscore, preferred_element_type=jnp.float32)
        dq_ref[:, first : first + count] = dq_t


def token_kernel(blocks, nears, rows, tokens, scalars, resp_len, *refs):
    row_refs, refs = refs[: len(blocks) * nears], refs[len(blocks) * nears :]
    (prob_ref, dscore_ref, dq_ref), refs = refs[:3], refs[3:]
    lse_refs, refs = refs[: len(blocks)], refs[len(blocks) :]
    dkv_refs, (*dq_refs, dk_acc, dv_acc) = refs[: len(KEEP)], refs[len(KEEP) :]
    lines = (row_refs[0].shape[1] - STAT_ROWS) // 2
    all_slabs = block_slabs(blocks, nears, row_refs)
    size = len(all_slabs[0]) * lines
    groups, row_count = len(all_slabs[0]), len(all_slabs[0]) // nears
    lane = lax.broadcasted_iota(jnp.int32, (1, 2 * lines), 1)
    for first, count, held, slabs in steps_of(blocks, all_slabs, lines):
        sources = [(b, slab) for b in held for slab in all_slabs[blocks.index(b)]]
        live = []
        for m in range(0, len(sources), 2):
            row, length = [], []
            for b, (_, _, n, j) in sources[m : m + 2]:
                device = (scalars[3] ^ b) * groups + group_at(scalars, j, n, nears)
                row.append(device * rows & (RESP_LEN - 1))
                length.append(resp_len[response_of(scalars, b, groups, rows)])
            row = jnp.where(lane < lines, row[0], row[1]) + (lane & (rows - 1))
            live.append((row < jnp.where(lane < lines, length[0], length[1])).astype(jnp.int32))
        live = jnp.concatenate(live, axis=1)
        part_lse = [lse_lines(ref, scalars, held, size) for ref in lse_refs]
        self_lse = line_values(slabs, lines, 0)
        peak = functools.reduce(jnp.maximum, part_lse, self_lse)
        total = sum(jnp.exp(x - peak) for x in part_lse) + jnp.exp(self_lse - peak)
        lse = jnp.where(live > 0, peak + jnp.log(total), DEAD_LSE)
        weight = jnp.exp(part_lse[0] - lse)
        weight_t = jnp.broadcast_to(weight, (DH, count)).T
        q, o_grad = (
            (lines_of(slabs, start, lines).astype(jnp.float32) * weight_t).astype(jnp.bfloat16)
            for start in (0, lines)
        )
        for i in range(len(KEEP)):
            dscore, prob = dscore_ref[i, :, first : first + count], prob_ref[i, :, first : first + count]
            dk = jnp.dot(dscore, q, preferred_element_type=jnp.float32) * SCALE
            dv = jnp.dot(prob, o_grad, preferred_element_type=jnp.float32)
            if first > 0:
                dk = dk + dk_acc[i]
                dv = dv + dv_acc[i]
            if first + count < len(blocks) * size:
                dk_acc[i] = dk
                dv_acc[i] = dv
            else:
                for n in range(2):
                    inner = slice(n * tokens, (n + 1) * tokens)
                    dkv_refs[i][n, 0:tokens, :] = dk[inner].astype(jnp.bfloat16)
                    dkv_refs[i][n, tokens : 2 * tokens, :] = dv[inner].astype(jnp.bfloat16)
        dq = (dq_ref[:, first : first + count] * (weight * SCALE)).T.astype(jnp.bfloat16)
        for m, (b, (_, _, n, j)) in enumerate(sources):
            dq_refs[n][blocks.index(b), j] = dq[m * lines : (m + 1) * lines]


def add_query_kernel(nears, *refs):
    own_refs, came_refs, out_refs = refs[:nears], refs[nears:-2], refs[-2:]
    row_count = own_refs[0].shape[0]
    for n in range(nears):
        for j in range(row_count):
            total = own_refs[n][j].astype(jnp.float32)
            for ref in came_refs:
                total = total + ref[n, j].astype(jnp.float32)
            out_refs[min(j, 1)][n] = total.astype(jnp.bfloat16)


def tie_kernel(*refs):
    pass


def write_query_kernel(nears, scalars, *refs):
    slab_refs, out_ref = refs[:-1], refs[-1]
    lines = slab_refs[0].shape[1]
    for j, ref in enumerate(slab_refs):
        for n in range(nears):
            first = pl.multiple_of(group_at(scalars, j, n, nears) * lines, lines)
            out_ref[pl.ds(first, lines), :] = ref[n]


def write_kv_kernel(groups, heads, scalars, *refs):
    pair_refs, (came_ref, out_k_ref, out_v_ref, sems) = refs[: len(KEEP)], refs[len(KEEP) :]
    tokens = out_k_ref.shape[0]
    copies = []
    for i, ref in enumerate(pair_refs):
        for source, other in ((ref.at[0], 0), (came_ref.at[i], FIRST)):
            columns = pl.ds(column_of(scalars[0] ^ KEEP[i] ^ other, groups, heads), DH)
            copies.append((source.at[0:tokens, :], out_k_ref.at[:, columns]))
            copies.append((source.at[tokens : 2 * tokens, :], out_v_ref.at[:, columns]))
    copies = [pltpu.make_async_copy(s, t, sems.at[n]) for n, (s, t) in enumerate(copies)]
    for copy in copies:
        copy.start()
    for copy in copies:
        copy.wait()


def swap(x, axis, distance, size):
    return lax.ppermute(x, axis, [(i, i ^ distance) for i in range(size)])


def swap_pairs(keep, send):
    members = ("row", "near", "head")
    came = swap(send, members, FIRST, KVH)
    pairs = [jnp.stack([keep[i], came[i]]) for i in range(len(KEEP))]
    return [swap(x, members, j, KVH) if j else x for x, j in zip(pairs, KEEP)]


def tie(x, others):
    return pl.pallas_call(
        tie_kernel,
        in_specs=[ANY] * (1 + len(others)),
        out_specs=ANY,
        out_shape=jax.ShapeDtypeStruct(x.shape, x.dtype),
        input_output_aliases={0: 0},
        compiler_params=PARAMS,
    )(x, *others)


def swap_back(pairs, others):
    members = ("row", "near", "head")
    pairs = [swap(x, members, j, KVH) if j else x for x, j in zip(pairs, KEEP)]
    return pairs, swap(tie(jnp.stack([x[1] for x in pairs]), others), members, FIRST, KVH)


def shards(parts, row_count, nears, heads, queries, grad_out, outputs, lse_self, keys, values, resp_len, prompt_end):
    rows = queries.shape[0]
    own_heads = queries.shape[1] // DH
    own_lines = rows * own_heads
    groups = row_count * nears
    lines = own_lines // groups
    tokens = keys.shape[0]
    assert 2 * lines == DH and RESP_LEN % (groups * rows) == 0 and row_count <= 2 and nears <= 2
    row, near = lax.axis_index("row"), lax.axis_index("near")
    member = (row * nears + near) * heads + lax.axis_index("head")
    scalars = jnp.stack([member, row, near, lax.axis_index("part")]).astype(jnp.int32)

    def as_lines(x):
        return x.reshape(rows, own_heads, DH).transpose(1, 0, 2).reshape(own_lines, DH)

    def in_hbm(x):
        return pltpu.with_memory_space_constraint(x, pltpu.HBM)

    half_shape = jax.ShapeDtypeStruct((len(KEEP), 2 * tokens, DH), jnp.bfloat16)
    slab_shape = jax.ShapeDtypeStruct((nears, 2 * lines + STAT_ROWS, DH), jnp.bfloat16)
    *slabs, kv_keep, kv_send = pl.pallas_call(
        functools.partial(pack_kernel, row_count, nears, heads),
        in_specs=[SMEM] + [HBM] * 6,
        out_specs=[VMEM] * (row_count + 2),
        out_shape=[slab_shape] * row_count + [half_shape] * 2,
        scratch_shapes=[
            pltpu.VMEM((own_lines, DH), jnp.bfloat16),
            pltpu.VMEM(lse_self.shape, jnp.float32),
            pltpu.SemaphoreType.DMA((2 + 2 * groups + 4 * len(KEEP),)),
        ],
        compiler_params=PARAMS,
    )(
        scalars,
        in_hbm(as_lines(queries)),
        in_hbm(as_lines(grad_out)),
        in_hbm(as_lines(outputs)),
        in_hbm(lse_self),
        in_hbm(keys),
        in_hbm(values),
    )
    slabs = [swap(x, "row", j, row_count) if j else x for j, x in enumerate(slabs)]
    own_block = jnp.stack([x[n] for n in range(nears) for x in slabs])
    pairs = swap_pairs(kv_keep, kv_send)
    far = [1 << n for n in reversed(range(shift_of(parts)))]
    order, came = [0], [own_block]
    for d in far:
        if d == 1:
            came = came[:1] + [tie(x, pairs[1:]) for x in came[1:]]
        came = came + [swap(x, "part", d, parts) for x in came]
        order = order + [b ^ d for b in order]
    blocks = order

    def row_refs_of(x):
        return [x, swap(x[row_count:], "near", 1, nears)] if nears > 1 else [x]

    def part_lse(held, refs, before):
        return pl.pallas_call(
            functools.partial(stat_kernel, held, nears, rows, tokens),
            in_specs=[SMEM] * 2 + [VMEM] * (len(refs) + len(KEEP) + len(before)),
            out_shape=jax.ShapeDtypeStruct((parts * lse_rows(groups * lines), DH), jnp.float32),
            compiler_params=PARAMS,
        )(scalars, prompt_end, *refs, *pairs, *before)

    row_refs = [ref for x in came[:-1] for ref in row_refs_of(x)]
    lse = [part_lse(blocks[:-1], row_refs, [])]
    last_refs = row_refs_of(tie(came[-1], lse))
    lse = [part_lse(blocks[-1:], last_refs, lse)]
    row_refs = row_refs + last_refs
    every_lse = lse + [swap(lse[0], "part", d, parts) for d in range(1, parts)]

    all_lines = parts * groups * lines
    score_shape = jax.ShapeDtypeStruct((len(KEEP), 2 * tokens, all_lines), jnp.bfloat16)
    prob, dscore, dq = pl.pallas_call(
        functools.partial(part_kernel, blocks, nears, rows, tokens),
        in_specs=[SMEM] * 2 + [VMEM] * (len(row_refs) + len(KEEP) + 1),
        out_specs=[VMEM] * 3,
        out_shape=[score_shape] * 2 + [jax.ShapeDtypeStruct((DH, all_lines), jnp.float32)],
        compiler_params=PARAMS,
    )(scalars, prompt_end, *row_refs, *pairs, *lse)
    dq_shape = jax.ShapeDtypeStruct((parts, row_count, lines, DH), jnp.bfloat16)
    acc = pltpu.VMEM((len(KEEP), 2 * tokens, DH), jnp.float32)
    pair_shape = jax.ShapeDtypeStruct((2, 2 * tokens, DH), jnp.bfloat16)
    outs = pl.pallas_call(
        functools.partial(token_kernel, blocks, nears, rows, tokens),
        in_specs=[SMEM] * 2 + [VMEM] * (len(row_refs) + 3 + parts),
        out_shape=[pair_shape] * len(KEEP) + [dq_shape] * nears,
        scratch_shapes=[acc] * 2,
        compiler_params=PARAMS,
    )(scalars, resp_len, *row_refs, prob, dscore, dq, *every_lse)
    dkv, dq = outs[: len(KEEP)], outs[len(KEEP) :]

    dq = [swap(x, "near", n, nears) if n else x for n, x in enumerate(dq)]
    came = [
        swap(jnp.stack([x[at] for x in dq]), "part", b, parts) for at, b in enumerate(blocks) if b
    ]
    sum_shape = jax.ShapeDtypeStruct((nears, lines, DH), jnp.bfloat16)
    own_sum, sent_sum = pl.pallas_call(
        functools.partial(add_query_kernel, nears),
        in_specs=[VMEM] * (nears + len(came)),
        out_shape=[sum_shape] * 2,
        compiler_params=PARAMS,
    )(*[x[0] for x in dq], *came)
    sums = [own_sum, swap(sent_sum, "row", 1, row_count)][:row_count]
    pairs, came = swap_back(dkv, came)
    out_q = pl.pallas_call(
        functools.partial(write_query_kernel, nears),
        in_specs=[SMEM] + [VMEM] * row_count,
        out_shape=jax.ShapeDtypeStruct((own_lines, DH), jnp.bfloat16),
        compiler_params=PARAMS,
    )(scalars, *sums)
    out_k, out_v = pl.pallas_call(
        functools.partial(write_kv_kernel, groups, heads),
        in_specs=[SMEM] + [VMEM] * (len(KEEP) + 1),
        out_specs=[HBM] * 2,
        out_shape=[
            jax.ShapeDtypeStruct(keys.shape, jnp.bfloat16),
            jax.ShapeDtypeStruct(values.shape, jnp.bfloat16),
        ],
        scratch_shapes=[pltpu.SemaphoreType.DMA((4 * len(KEEP),))],
        compiler_params=PARAMS,
    )(scalars, *pairs, came)
    out_q = out_q.reshape(own_heads, rows, DH).transpose(1, 0, 2).reshape(rows, own_heads * DH)
    return out_q, out_k, out_v


def solution(mesh):
    ctx, heads = mesh.shape["ctx"], mesh.shape["head"]
    groups = KVH // heads
    parts = ctx // groups
    nears = min(2, groups)
    row_count = groups // nears
    fine = Mesh(
        mesh.devices.reshape(parts, row_count, nears, heads), ("part", "row", "near", "head")
    )
    rows = P(("part", "row", "near"), "head")
    tokens = P(("part", "row", "near", "head"), None)
    return jax.shard_map(
        functools.partial(shards, parts, row_count, nears, heads),
        mesh=fine,
        in_specs=(rows, rows, rows, rows, tokens, tokens, P(), P()),
        out_specs=(rows, tokens, tokens),
        check_vma=False,
    )
```

time: 68.6 us -> 57.4 us (0.84)
  blocking collectives: 37.1 us -> 0 us
  starting transfers between devices: 13.3 us -> 26.8 us
  waiting for transfers between devices: 5.06 us -> 15.6 us
  Pallas kernels: 10.4 us -> 12.2 us
    all_to_all x2 -> x0, blocking collectives: 37.1 us -> none  [one_step(): lax.all_to_all(x, ('part', 'group'), split_axis=0, concat_axis=0, tiled=T...]
    ppermute x11 -> x24, starting transfers between devices: 13.3 us -> 26.8 us  [swap(): return lax.ppermute(x, axis, [(i, i ^ distance) for i in range(size)])]
    ppermute x11 -> x24, waiting for transfers between devices: 5.06 us -> 15.6 us  [swap(): return lax.ppermute(x, axis, [(i, i ^ distance) for i in range(size)])]
    pallas_call x5 -> x11, Pallas kernels: 10.4 us -> 12.2 us  [the longest x2 2.84 us: part_lse(): pl.pallas_call(functools.partial(stat_kernel, held, nears, rows, tokens),...]
  transfers between devices with their start and end apart: 11 -> 24, of which waited for: 4 -> 13; matrix products, arithmetic and copies ran while one was open for 0% -> 0% of each run, Pallas kernels for 2% -> 10%
where the time goes in v6:
time: 57.4 us; the launch traced here: 57.2 us
  starting transfers between devices  26.8 us (47%)
  waiting for transfers between devices  15.6 us (27%)
  Pallas kernels  12.2 us (21%)
  between operations  2.18 us (4%)
    ppermute x24, starting transfers between devices, swap(): return lax.ppermute(x, axis, [(i, i ^ distance) for i in range(size)])  26.8 us
    ppermute x24, waiting for transfers between devices, swap(): return lax.ppermute(x, axis, [(i, i ^ distance) for i in range(size)])  15.6 us
    pallas_call x2, Pallas kernels, part_lse(): pl.pallas_call(functools.partial(stat_kernel, held, nears, rows, tokens),...  2.84 us
    pallas_call x1, Pallas kernels, shards(): pl.pallas_call(functools.partial(part_kernel, blocks, nears, rows, tokens...  2.76 us
    pallas_call x1, Pallas kernels, shards(): pl.pallas_call(functools.partial(token_kernel, blocks, nears, rows, token...  2 us
    pallas_call x1, Pallas kernels, shards(): pl.pallas_call(functools.partial(pack_kernel, row_count, nears, heads), i...  1.91 us
    pallas_call x1, Pallas kernels, shards(): pl.pallas_call(functools.partial(write_kv_kernel, groups, heads), in_spec...  1.46 us
    pallas_call x1, Pallas kernels, shards(): pl.pallas_call(functools.partial(write_query_kernel, nears), in_specs=[SM...  1.18 us
  transfers between devices with their start and end apart: 24, of which 13 were waited for; matrix products, arithmetic and copies ran while one was open for 0% of the time, Pallas kernels for 10%

profile of v6, /device:TPU:0, one launch (start us, length us, event | category | flops | bytes accessed | tf_op | source)
XLA Modules:
  0.0 57.2 jit_solution(7512569283333609111)
XLA Ops:
  0.6 0.1 pad_add_fusion.scalars
  0.7 1.9 %shard_map.103 = (bf16[2,144,128]{2,1,0:T(8,128)(2,1)S(1)}, bf16[2,144,128]{2,1,0:T(8,128)(2,1)S(1)}, bf16[4,256,128]{2,1,0:T(8,128)(2,1)S(1)}, bf16[4,256,128]{2,1,0:T(8,128)(2,1)S(1)}) custom-call(s32[4]{0:T(128)S(1)} %pad_add_fusion.scalars, bf16[256,128]{1,0:T(8,128)(2,1)} %bitcast.28, bf16[256,128]{1,0:T(8,128)(2,1)} %bitcast.29, ...), custom_call_target="tpu_custom_call" | custom-call | tf_op jit(solution)/shard_map/pallas_call | solution.py:388
  2.6 3.0 %collective-permute-start = (bf16[2,144,128]{2,1,0:T(8,128)(2,1)S(1)}, bf16[2,144,128]{2,1,0:T(8,128)(2,1)S(1)}, u32[]{:S(2)}, u32[]{:S(2)}) collective-permute-start(bf16[2,144,128]{2,1,0:T(8,128)(2,1)S(1)} %get-tuple-element.21), channel_id=1, source_target_pairs={{0,4},{4,0},{1,5},{5,1},{2,6},{6,2},{3,7},{7,3},{8,12},{12,8},{9,1... | collective-permute-start | bytes 221192 | tf_op jit(solution)/shard_map/ppermute | solution.py:341
  5.7 0.0 collective-permute-start.3
  5.7 2.3 %collective-permute-done = bf16[2,144,128]{2,1,0:T(8,128)(2,1)S(1)} collective-permute-done((bf16[2,144,128]{2,1,0:T(8,128)(2,1)S(1)}, bf16[2,144,128]{2,1,0:T(8,128)(2,1)S(1)}, u32[]{:S(2)}, u32[]{:S(2)}) %collective-permute-start) | collective-permute-done | bytes 73760 | tf_op jit(solution)/shard_map/ppermute | solution.py:341
  8.0 3.2 %collective-permute-start.2 = (bf16[4,144,128]{2,1,0:T(8,128)(2,1)S(1)}, bf16[4,144,128]{2,1,0:T(8,128)(2,1)S(1)}, u32[]{:S(2)}, u32[]{:S(2)}) collective-permute-start(bf16[4,144,128]{2,1,0:T(8,128)(2,1)S(1)} %pad_maximum_fusion.1.refs_0_), channel_id=1, source_target_pairs={{0,16},{8,24},{16,0},{24,8},{1,17},{9,25},{17,1},{25,9},{2,18},{10... | collective-permute-start | bytes 442376 | tf_op jit(solution)/shard_map/ppermute | solution.py:341
  11.2 0.0 collective-permute-done.3
  11.2 1.6 %collective-permute-start.4 = (bf16[2,256,128]{2,1,0:T(8,128)(2,1)S(1)}, bf16[2,256,128]{2,1,0:T(8,128)(2,1)S(1)}, u32[]{:S(2)}, u32[]{:S(2)}) collective-permute-start(bf16[2,256,128]{2,1,0:T(8,128)(2,1)S(1)} %pad_maximum_fusion.2), channel_id=1, source_target_pairs={{0,1},{1,0},{2,3},{3,2},{4,5},{5,4},{6,7},{7,6},{8,9},{9,8},{10,11... | collective-permute-start | bytes 393224 | tf_op jit(solution)/shard_map/ppermute | solution.py:341
  12.8 1.6 %collective-permute-start.5 = (bf16[2,256,128]{2,1,0:T(8,128)(2,1)S(1)}, bf16[2,256,128]{2,1,0:T(8,128)(2,1)S(1)}, u32[]{:S(2)}, u32[]{:S(2)}) collective-permute-start(bf16[2,256,128]{2,1,0:T(8,128)(2,1)S(1)} %pad_maximum_fusion.3), channel_id=1, source_target_pairs={{0,4},{1,5},{2,6},{3,7},{4,0},{5,1},{6,2},{7,3},{8,12},{9,13},{10,... | collective-permute-start | bytes 393224 | tf_op jit(solution)/shard_map/ppermute | solution.py:341
  14.4 0.5 collective-permute-start.6
  15.0 1.6 %collective-permute-start.8 = (bf16[4,144,128]{2,1,0:T(8,128)(2,1)S(1)}, bf16[4,144,128]{2,1,0:T(8,128)(2,1)S(1)}, u32[]{:S(2)}, u32[]{:S(2)}) collective-permute-start(bf16[4,144,128]{2,1,0:T(8,128)(2,1)S(1)} %pad_maximum_fusion.1.refs_0_), channel_id=1, source_target_pairs={{0,8},{8,0},{16,24},{24,16},{1,9},{9,1},{17,25},{25,17},{2,10},{10... | collective-permute-start | bytes 442376 | tf_op jit(solution)/shard_map/ppermute | solution.py:341
  17.2 0.5 collective-permute-done.4.refs_1_.refs_7_.refs_3_.refs_9_
  17.7 1.3 %collective-permute-done.5.refs_2_.refs_8_.refs_4_.refs_10_ = bf16[2,256,128]{2,1,0:T(8,128)(2,1)S(1)} collective-permute-done((bf16[2,256,128]{2,1,0:T(8,128)(2,1)S(1)}, bf16[2,256,128]{2,1,0:T(8,128)(2,1)S(1)}, u32[]{:S(2)}, u32[]{:S(2)}) %collective-permute-start.5) | collective-permute-done | bytes 131104 | tf_op jit(solution)/shard_map/ppermute | solution.py:341
  18.9 1.4 %collective-permute-done.6.refs_3_.refs_9_.refs_5_.refs_11_ = bf16[2,256,128]{2,1,0:T(8,128)(2,1)S(1)} collective-permute-done((bf16[2,256,128]{2,1,0:T(8,128)(2,1)S(1)}, bf16[2,256,128]{2,1,0:T(8,128)(2,1)S(1)}, u32[]{:S(2)}, u32[]{:S(2)}) %collective-permute-start.6) | collective-permute-done | bytes 131104 | tf_op jit(solution)/shard_map/ppermute | solution.py:341
  20.3 1.6 %collective-permute-start.10 = (bf16[4,144,128]{2,1,0:T(8,128)(2,1)S(1)}, bf16[4,144,128]{2,1,0:T(8,128)(2,1)S(1)}, u32[]{:S(2)}, u32[]{:S(2)}) collective-permute-start(bf16[4,144,128]{2,1,0:T(8,128)(2,1)S(1)} %shard_map.104.refs_2_), channel_id=1, source_target_pairs={{0,8},{8,0},{16,24},{24,16},{1,9},{9,1},{17,25},{25,17},{2,10},{10... | collective-permute-start | bytes 442376 | tf_op jit(solution)/shard_map/ppermute | solution.py:341
  21.9 0.1 collective-permute-start.1
  22.0 0.0 collective-permute-done.8.refs_4_
  22.0 0.5 collective-permute-start.9
  22.6 0.1 collective-permute-start.7
  22.7 0.6 collective-permute-done.1.refs_1_
  23.3 0.2 collective-permute-done.9.refs_5_
  23.5 0.4 collective-permute-done.7.refs_3_
  23.9 1.8 %shard_map.105.refs_1_.refs_6_ = f32[8,128]{1,0:T(8,128)S(1)} custom-call(s32[4]{0:T(128)S(1)} %pad_add_fusion.scalars, s32[1]{0:T(128)S(6)} %copy.22.prompt_end, bf16[4,144,128]{2,1,0:T(8,128)(2,1)S(1)} %pad_maximum_fusion.1.refs_0_, bf16[2,144,128]{2,1,0:T(8,128)(2,1)S(1)} %collective-permute-done.1.refs_1_, bf16[4,144,128]{2,1,0:T(8,128)(2,1)S(1)} %shard_map.104.refs_2_, ...), custom_call_target="tpu_custom_call" | custom-call | tf_op jit(solution)/shard_map/pallas_call | solution.py:424
  25.7 0.2 collective-permute-start.11
  25.9 1.1 %collective-permute-done.11.refs_1_.refs_7_ = bf16[2,144,128]{2,1,0:T(8,128)(2,1)S(1)} collective-permute-done((bf16[2,144,128]{2,1,0:T(8,128)(2,1)S(1)}, bf16[2,144,128]{2,1,0:T(8,128)(2,1)S(1)}, u32[]{:S(2)}, u32[]{:S(2)}) %collective-permute-start.11) | collective-permute-done | bytes 73760 | tf_op jit(solution)/shard_map/ppermute | solution.py:341
  27.0 1.1 %shard_map.107.refs_12_.refs_11_ = f32[8,128]{1,0:T(8,128)S(1)} custom-call(s32[4]{0:T(128)S(1)} %pad_add_fusion.scalars, s32[1]{0:T(128)S(6)} %copy.22.prompt_end, bf16[4,144,128]{2,1,0:T(8,128)(2,1)S(1)} %shard_map.106.refs_0_.refs_6_, bf16[2,144,128]{2,1,0:T(8,128)(2,1)S(1)} %collective-permute-done.11.refs_1_.refs_7_, ...), custom_call_target="tpu_custom_call" | custom-call | tf_op jit(solution)/shard_map/pallas_call | solution.py:424
  28.1 1.2 %collective-permute-start.14 = (f32[8,128]{1,0:T(8,128)S(1)}, f32[8,128]{1,0:T(8,128)S(1)}, u32[]{:S(2)}, u32[]{:S(2)}) collective-permute-start(f32[8,128]{1,0:T(8,128)S(1)} %shard_map.107.refs_12_.refs_11_), channel_id=1, source_target_pairs={{0,24},{8,16},{16,8},{24,0},{1,25},{9,17},{17,9},{25,1},{2,26},{10... | collective-permute-start | bytes 12296 | tf_op jit(solution)/shard_map/ppermute | solution.py:341
  29.3 1.7 %collective-permute-start.13 = (f32[8,128]{1,0:T(8,128)S(1)}, f32[8,128]{1,0:T(8,128)S(1)}, u32[]{:S(2)}, u32[]{:S(2)}) collective-permute-start(f32[8,128]{1,0:T(8,128)S(1)} %shard_map.107.refs_12_.refs_11_), channel_id=1, source_target_pairs={{0,16},{8,24},{16,0},{24,8},{1,17},{9,25},{17,1},{25,9},{2,18},{10... | collective-permute-start | bytes 12296 | tf_op jit(solution)/shard_map/ppermute | solution.py:341
  31.0 1.5 %collective-permute-start.12 = (f32[8,128]{1,0:T(8,128)S(1)}, f32[8,128]{1,0:T(8,128)S(1)}, u32[]{:S(2)}, u32[]{:S(2)}) collective-permute-start(f32[8,128]{1,0:T(8,128)S(1)} %shard_map.107.refs_12_.refs_11_), channel_id=1, source_target_pairs={{0,8},{8,0},{16,24},{24,16},{1,9},{9,1},{17,25},{25,17},{2,10},{10... | collective-permute-start | bytes 12296 | tf_op jit(solution)/shard_map/ppermute | solution.py:341
  33.2 2.8 %shard_map.108 = (bf16[4,256,1024]{2,1,0:T(8,128)(2,1)S(1)}, bf16[4,256,1024]{2,1,0:T(8,128)(2,1)S(1)}, f32[128,1024]{1,0:T(8,128)S(1)}) custom-call(s32[4]{0:T(128)S(1)} %pad_add_fusion.scalars, s32[1]{0:T(128)S(6)} %copy.22.prompt_end, bf16[4,144,128]{2,1,0:T(8,128)(2,1)S(1)} %pad_maximum_fusion.1.refs_0_, ...), custom_call_target="tpu_custom_call" | custom-call | tf_op jit(solution)/shard_map/pallas_call | solution.py:440
  36.0 0.0 collective-permute-done.12.refs_12_
  36.0 2.0 %shard_map.109 = (bf16[2,256,128]{2,1,0:T(8,128)(2,1)S(1)}, bf16[2,256,128]{2,1,0:T(8,128)(2,1)S(1)}, bf16[2,256,128]{2,1,0:T(8,128)(2,1)S(1)}, bf16[2,256,128]{...) custom-call(s32[4]{0:T(128)S(1)} %pad_add_fusion.scalars, ...), custom_call_target="tpu_custom_call" | custom-call | tf_op jit(solution)/shard_map/pallas_call | solution.py:450
  38.0 0.1 collective-permute-start.15
  38.1 0.6 %collective-permute-start.20 = (bf16[2,256,128]{2,1,0:T(8,128)(2,1)S(1)}, bf16[2,256,128]{2,1,0:T(8,128)(2,1)S(1)}, u32[]{:S(2)}, u32[]{:S(2)}) collective-permute-start(bf16[2,256,128]{2,1,0:T(8,128)(2,1)S(1)} %get-tuple-element.32), channel_id=1, source_target_pairs={{0,1},{1,0},{2,3},{3,2},{4,5},{5,4},{6,7},{7,6},{8,9},{9,8},{10,11... | collective-permute-start | bytes 393224 | tf_op jit(solution)/shard_map/ppermute | solution.py:341
  38.7 1.7 %collective-permute-start.21 = (bf16[2,256,128]{2,1,0:T(8,128)(2,1)S(1)}, bf16[2,256,128]{2,1,0:T(8,128)(2,1)S(1)}, u32[]{:S(2)}, u32[]{:S(2)}) collective-permute-start(bf16[2,256,128]{2,1,0:T(8,128)(2,1)S(1)} %get-tuple-element.33), channel_id=1, source_target_pairs={{0,4},{1,5},{2,6},{3,7},{4,0},{5,1},{6,2},{7,3},{8,12},{9,13},{10,... | collective-permute-start | bytes 393224 | tf_op jit(solution)/shard_map/ppermute | solution.py:341
  40.3 1.3 %collective-permute-start.22 = (bf16[2,256,128]{2,1,0:T(8,128)(2,1)S(1)}, bf16[2,256,128]{2,1,0:T(8,128)(2,1)S(1)}, u32[]{:S(2)}, u32[]{:S(2)}) collective-permute-start(bf16[2,256,128]{2,1,0:T(8,128)(2,1)S(1)} %get-tuple-element.34), channel_id=1, source_target_pairs={{0,5},{1,4},{2,7},{3,6},{4,1},{5,0},{6,3},{7,2},{8,13},{9,12},{10,... | collective-permute-start | bytes 393224 | tf_op jit(solution)/shard_map/ppermute | solution.py:341
  41.7 0.1 collective-permute-start.16
  41.8 1.8 %collective-permute-start.17 = (bf16[2,2,64,128]{3,2,1,0:T(8,128)(2,1)S(1)}, bf16[2,2,64,128]{3,2,1,0:T(8,128)(2,1)S(1)}, u32[]{:S(2)}, u32[]{:S(2)}) collective-permute-start(bf16[2,2,64,128]{3,2,1,0:T(8,128)(2,1)S(1)} %pad_maximum_fusion.8), channel_id=1, source_target_pairs={{0,8},{8,0},{16,24},{24,16},{1,9},{9,1},{17,25},{25,17},{2,10},{10... | collective-permute-start | bytes 196616 | tf_op jit(solution)/shard_map/ppermute | solution.py:341
  43.6 0.9 %collective-permute-done.20.refs_1_ = bf16[2,256,128]{2,1,0:T(8,128)(2,1)S(1)} collective-permute-done((bf16[2,256,128]{2,1,0:T(8,128)(2,1)S(1)}, bf16[2,256,128]{2,1,0:T(8,128)(2,1)S(1)}, u32[]{:S(2)}, u32[]{:S(2)}) %collective-permute-start.20) | collective-permute-done | bytes 131104 | tf_op jit(solution)/shard_map/ppermute | solution.py:341
  44.4 1.9 %collective-permute-start.18 = (bf16[2,2,64,128]{3,2,1,0:T(8,128)(2,1)S(1)}, bf16[2,2,64,128]{3,2,1,0:T(8,128)(2,1)S(1)}, u32[]{:S(2)}, u32[]{:S(2)}) collective-permute-start(bf16[2,2,64,128]{3,2,1,0:T(8,128)(2,1)S(1)} %pad_maximum_fusion.9), channel_id=1, source_target_pairs={{0,24},{8,16},{16,8},{24,0},{1,25},{9,17},{17,9},{25,1},{2,26},{10... | collective-permute-start | bytes 196616 | tf_op jit(solution)/shard_map/ppermute | solution.py:341
  46.3 0.9 %collective-permute-done.22.refs_3_ = bf16[2,256,128]{2,1,0:T(8,128)(2,1)S(1)} collective-permute-done((bf16[2,256,128]{2,1,0:T(8,128)(2,1)S(1)}, bf16[2,256,128]{2,1,0:T(8,128)(2,1)S(1)}, u32[]{:S(2)}, u32[]{:S(2)}) %collective-permute-start.22) | collective-permute-done | bytes 131104 | tf_op jit(solution)/shard_map/ppermute | solution.py:341
  47.3 1.2 %collective-permute-done.16.refs_2_.refs_1_ = bf16[2,2,64,128]{3,2,1,0:T(8,128)(2,1)S(1)} collective-permute-done((bf16[2,2,64,128]{3,2,1,0:T(8,128)(2,1)S(1)}, bf16[2,2,64,128]{3,2,1,0:T(8,128)(2,1)S(1)}, u32[]{:S(2)}, u32[]{:S(2)}) %collective-permute-start.16) | collective-permute-done | bytes 65568 | tf_op jit(solution)/shard_map/ppermute | solution.py:341
  48.5 0.0 collective-permute-done.17.refs_3_.refs_2_
  48.5 2.0 %collective-permute-done.18.refs_4_.refs_3_ = bf16[2,2,64,128]{3,2,1,0:T(8,128)(2,1)S(1)} collective-permute-done((bf16[2,2,64,128]{3,2,1,0:T(8,128)(2,1)S(1)}, bf16[2,2,64,128]{3,2,1,0:T(8,128)(2,1)S(1)}, u32[]{:S(2)}, u32[]{:S(2)}) %collective-permute-start.18) | collective-permute-done | bytes 65568 | tf_op jit(solution)/shard_map/ppermute | solution.py:341
  50.5 1.1 %collective-permute-start.19 = (bf16[2,64,128]{2,1,0:T(8,128)(2,1)S(1)}, bf16[2,64,128]{2,1,0:T(8,128)(2,1)S(1)}, u32[]{:S(2)}, u32[]{:S(2)}) collective-permute-start(bf16[2,64,128]{2,1,0:T(8,128)(2,1)S(1)} %get-tuple-element.30), channel_id=1, source_target_pairs={{0,4},{4,0},{1,5},{5,1},{2,6},{6,2},{3,7},{7,3},{8,12},{12,8},{9,1... | collective-permute-start | bytes 98312 | tf_op jit(solution)/shard_map/ppermute | solution.py:341
  51.6 2.9 %collective-permute-done.19.refs_1_ = bf16[2,64,128]{2,1,0:T(8,128)(2,1)S(1)} collective-permute-done((bf16[2,64,128]{2,1,0:T(8,128)(2,1)S(1)}, bf16[2,64,128]{2,1,0:T(8,128)(2,1)S(1)}, u32[]{:S(2)}, u32[]{:S(2)}) %collective-permute-start.19) | collective-permute-done | bytes 32800 | tf_op jit(solution)/shard_map/ppermute | solution.py:341
  54.5 1.2 %shard_map.111 = bf16[256,128]{1,0:T(8,128)(2,1)} custom-call(s32[4]{0:T(128)S(1)} %pad_add_fusion.scalars, bf16[2,64,128]{2,1,0:T(8,128)(2,1)S(1)} %get-tuple-element.29.refs_0_, bf16[2,64,128]{2,1,0:T(8,128)(2,1)S(1)} %collective-permute-done.19.refs_1_), custom_call_target="tpu_custom_call" | custom-call | tf_op jit(solution)/shard_map/pallas_call | solution.py:472
  55.7 1.5 %shard_map.113 = (bf16[128,1024]{1,0:T(8,128)(2,1)}, bf16[128,1024]{1,0:T(8,128)(2,1)}) custom-call(s32[4]{0:T(128)S(1)} %pad_add_fusion.scalars, bf16[2,256,128]{2,1,0:T(8,128)(2,1)S(1)} %get-tuple-element.31.refs_0_, bf16[2,256,128]{2,1,0:T(8,128)(2,1)S(1)} %collective-permute-done.20.refs_1_, bf16[2,256,128]{2,1,0:T(8,128)(2,1)S(1)} %collective-permute-done.21.refs_2_, ...), custom_call_target="tpu_custom_call" | custom-call | tf_op jit(solution)/shard_map/pallas_call | solution.py:478
  (35 shorter events, 0.3 us)
Async XLA Ops:
  2.6 5.4 %collective-permute-start = (bf16[2,144,128]{2,1,0:T(8,128)(2,1)S(1)}, bf16[2,144,128]{2,1,0:T(8,128)(2,1)S(1)}, u32[]{:S(2)}, u32[]{:S(2)}) collective-permute-start(bf16[2,144,128]{2,1,0:T(8,128)(2,1)S(1)} %get-tuple-element.21), channel_id=1, source_target_pairs={{0,4},{4,0},{1,5},{5,1},{2,6},{6,2},{3,7},{7,3},{8,12},{12,8},{9,1... | collective-permute-start | bytes 221192 | tf_op jit(solution)/shard_map/ppermute | solution.py:341
  5.7 5.5 %collective-permute-start.3 = (bf16[4,256,128]{2,1,0:T(8,128)(2,1)S(1)}, bf16[4,256,128]{2,1,0:T(8,128)(2,1)S(1)}, u32[]{:S(2)}, u32[]{:S(2)}) collective-permute-start(bf16[4,256,128]{2,1,0:T(8,128)(2,1)S(1)} %get-tuple-element.23), channel_id=1, source_target_pairs={{0,2},{1,3},{2,0},{3,1},{4,6},{5,7},{6,4},{7,5},{8,10},{9,11},{10,... | collective-permute-start | bytes 786440 | tf_op jit(solution)/shard_map/ppermute | solution.py:341
  8.0 9.2 %collective-permute-start.2 = (bf16[4,144,128]{2,1,0:T(8,128)(2,1)S(1)}, bf16[4,144,128]{2,1,0:T(8,128)(2,1)S(1)}, u32[]{:S(2)}, u32[]{:S(2)}) collective-permute-start(bf16[4,144,128]{2,1,0:T(8,128)(2,1)S(1)} %pad_maximum_fusion.1.refs_0_), channel_id=1, source_target_pairs={{0,16},{8,24},{16,0},{24,8},{1,17},{9,25},{17,1},{25,9},{2,18},{10... | collective-permute-start | bytes 442376 | tf_op jit(solution)/shard_map/ppermute | solution.py:341
  11.2 6.4 %collective-permute-start.4 = (bf16[2,256,128]{2,1,0:T(8,128)(2,1)S(1)}, bf16[2,256,128]{2,1,0:T(8,128)(2,1)S(1)}, u32[]{:S(2)}, u32[]{:S(2)}) collective-permute-start(bf16[2,256,128]{2,1,0:T(8,128)(2,1)S(1)} %pad_maximum_fusion.2), channel_id=1, source_target_pairs={{0,1},{1,0},{2,3},{3,2},{4,5},{5,4},{6,7},{7,6},{8,9},{9,8},{10,11... | collective-permute-start | bytes 393224 | tf_op jit(solution)/shard_map/ppermute | solution.py:341
  12.8 6.1 %collective-permute-start.5 = (bf16[2,256,128]{2,1,0:T(8,128)(2,1)S(1)}, bf16[2,256,128]{2,1,0:T(8,128)(2,1)S(1)}, u32[]{:S(2)}, u32[]{:S(2)}) collective-permute-start(bf16[2,256,128]{2,1,0:T(8,128)(2,1)S(1)} %pad_maximum_fusion.3), channel_id=1, source_target_pairs={{0,4},{1,5},{2,6},{3,7},{4,0},{5,1},{6,2},{7,3},{8,12},{9,13},{10,... | collective-permute-start | bytes 393224 | tf_op jit(solution)/shard_map/ppermute | solution.py:341
  14.4 5.9 %collective-permute-start.6 = (bf16[2,256,128]{2,1,0:T(8,128)(2,1)S(1)}, bf16[2,256,128]{2,1,0:T(8,128)(2,1)S(1)}, u32[]{:S(2)}, u32[]{:S(2)}) collective-permute-start(bf16[2,256,128]{2,1,0:T(8,128)(2,1)S(1)} %pad_maximum_fusion.4), channel_id=1, source_target_pairs={{0,5},{1,4},{2,7},{3,6},{4,1},{5,0},{6,3},{7,2},{8,13},{9,12},{10,... | collective-permute-start | bytes 393224 | tf_op jit(solution)/shard_map/ppermute | solution.py:341
  15.0 7.1 %collective-permute-start.8 = (bf16[4,144,128]{2,1,0:T(8,128)(2,1)S(1)}, bf16[4,144,128]{2,1,0:T(8,128)(2,1)S(1)}, u32[]{:S(2)}, u32[]{:S(2)}) collective-permute-start(bf16[4,144,128]{2,1,0:T(8,128)(2,1)S(1)} %pad_maximum_fusion.1.refs_0_), channel_id=1, source_target_pairs={{0,8},{8,0},{16,24},{24,16},{1,9},{9,1},{17,25},{25,17},{2,10},{10... | collective-permute-start | bytes 442376 | tf_op jit(solution)/shard_map/ppermute | solution.py:341
  20.3 5.3 %collective-permute-start.10 = (bf16[4,144,128]{2,1,0:T(8,128)(2,1)S(1)}, bf16[4,144,128]{2,1,0:T(8,128)(2,1)S(1)}, u32[]{:S(2)}, u32[]{:S(2)}) collective-permute-start(bf16[4,144,128]{2,1,0:T(8,128)(2,1)S(1)} %shard_map.104.refs_2_), channel_id=1, source_target_pairs={{0,8},{8,0},{16,24},{24,16},{1,9},{9,1},{17,25},{25,17},{2,10},{10... | collective-permute-start | bytes 442376 | tf_op jit(solution)/shard_map/ppermute | solution.py:341
  21.9 1.3 %collective-permute-start.1 = (bf16[2,144,128]{2,1,0:T(8,128)(2,1)S(1)}, bf16[2,144,128]{2,1,0:T(8,128)(2,1)S(1)}, u32[]{:S(2)}, u32[]{:S(2)}) collective-permute-start(bf16[2,144,128]{2,1,0:T(8,128)(2,1)S(1)} %pad_maximum_fusion.6), channel_id=1, source_target_pairs={{0,2},{2,0},{1,3},{3,1},{4,6},{6,4},{5,7},{7,5},{8,10},{10,8},{9,1... | collective-permute-start | bytes 221192 | tf_op jit(solution)/shard_map/ppermute | solution.py:341
  22.0 1.5 %collective-permute-start.9 = (bf16[2,144,128]{2,1,0:T(8,128)(2,1)S(1)}, bf16[2,144,128]{2,1,0:T(8,128)(2,1)S(1)}, u32[]{:S(2)}, u32[]{:S(2)}) collective-permute-start(bf16[2,144,128]{2,1,0:T(8,128)(2,1)S(1)} %slice.116), channel_id=1, source_target_pairs={{0,2},{2,0},{1,3},{3,1},{4,6},{6,4},{5,7},{7,5},{8,10},{10,8},{9,1... | collective-permute-start | bytes 221192 | tf_op jit(solution)/shard_map/ppermute | solution.py:341
  22.6 1.3 %collective-permute-start.7 = (bf16[2,144,128]{2,1,0:T(8,128)(2,1)S(1)}, bf16[2,144,128]{2,1,0:T(8,128)(2,1)S(1)}, u32[]{:S(2)}, u32[]{:S(2)}) collective-permute-start(bf16[2,144,128]{2,1,0:T(8,128)(2,1)S(1)} %slice.115), channel_id=1, source_target_pairs={{0,2},{2,0},{1,3},{3,1},{4,6},{6,4},{5,7},{7,5},{8,10},{10,8},{9,1... | collective-permute-start | bytes 221192 | tf_op jit(solution)/shard_map/ppermute | solution.py:341
  25.7 1.3 %collective-permute-start.11 = (bf16[2,144,128]{2,1,0:T(8,128)(2,1)S(1)}, bf16[2,144,128]{2,1,0:T(8,128)(2,1)S(1)}, u32[]{:S(2)}, u32[]{:S(2)}) collective-permute-start(bf16[2,144,128]{2,1,0:T(8,128)(2,1)S(1)} %slice.118), channel_id=1, source_target_pairs={{0,2},{2,0},{1,3},{3,1},{4,6},{6,4},{5,7},{7,5},{8,10},{10,8},{9,1... | collective-permute-start | bytes 221192 | tf_op jit(solution)/shard_map/ppermute | solution.py:341
  28.1 7.9 %collective-permute-start.14 = (f32[8,128]{1,0:T(8,128)S(1)}, f32[8,128]{1,0:T(8,128)S(1)}, u32[]{:S(2)}, u32[]{:S(2)}) collective-permute-start(f32[8,128]{1,0:T(8,128)S(1)} %shard_map.107.refs_12_.refs_11_), channel_id=1, source_target_pairs={{0,24},{8,16},{16,8},{24,0},{1,25},{9,17},{17,9},{25,1},{2,26},{10... | collective-permute-start | bytes 12296 | tf_op jit(solution)/shard_map/ppermute | solution.py:341
  29.3 6.7 %collective-permute-start.13 = (f32[8,128]{1,0:T(8,128)S(1)}, f32[8,128]{1,0:T(8,128)S(1)}, u32[]{:S(2)}, u32[]{:S(2)}) collective-permute-start(f32[8,128]{1,0:T(8,128)S(1)} %shard_map.107.refs_12_.refs_11_), channel_id=1, source_target_pairs={{0,16},{8,24},{16,0},{24,8},{1,17},{9,25},{17,1},{25,9},{2,18},{10... | collective-permute-start | bytes 12296 | tf_op jit(solution)/shard_map/ppermute | solution.py:341
  31.0 5.0 %collective-permute-start.12 = (f32[8,128]{1,0:T(8,128)S(1)}, f32[8,128]{1,0:T(8,128)S(1)}, u32[]{:S(2)}, u32[]{:S(2)}) collective-permute-start(f32[8,128]{1,0:T(8,128)S(1)} %shard_map.107.refs_12_.refs_11_), channel_id=1, source_target_pairs={{0,8},{8,0},{16,24},{24,16},{1,9},{9,1},{17,25},{25,17},{2,10},{10... | collective-permute-start | bytes 12296 | tf_op jit(solution)/shard_map/ppermute | solution.py:341
  38.0 3.6 %collective-permute-start.15 = (bf16[4,2,64,128]{3,2,1,0:T(8,128)(2,1)S(1)}, bf16[4,2,64,128]{3,2,1,0:T(8,128)(2,1)S(1)}, u32[]{:S(2)}, u32[]{:S(2)}) collective-permute-start(bf16[4,2,64,128]{3,2,1,0:T(8,128)(2,1)S(1)} %get-tuple-element.28), channel_id=1, source_target_pairs={{0,2},{2,0},{1,3},{3,1},{4,6},{6,4},{5,7},{7,5},{8,10},{10,8},{9,1... | collective-permute-start | bytes 393224 | tf_op jit(solution)/shard_map/ppermute | solution.py:341
  38.1 6.4 %collective-permute-start.20 = (bf16[2,256,128]{2,1,0:T(8,128)(2,1)S(1)}, bf16[2,256,128]{2,1,0:T(8,128)(2,1)S(1)}, u32[]{:S(2)}, u32[]{:S(2)}) collective-permute-start(bf16[2,256,128]{2,1,0:T(8,128)(2,1)S(1)} %get-tuple-element.32), channel_id=1, source_target_pairs={{0,1},{1,0},{2,3},{3,2},{4,5},{5,4},{6,7},{7,6},{8,9},{9,8},{10,11... | collective-permute-start | bytes 393224 | tf_op jit(solution)/shard_map/ppermute | solution.py:341
  38.7 7.6 %collective-permute-start.21 = (bf16[2,256,128]{2,1,0:T(8,128)(2,1)S(1)}, bf16[2,256,128]{2,1,0:T(8,128)(2,1)S(1)}, u32[]{:S(2)}, u32[]{:S(2)}) collective-permute-start(bf16[2,256,128]{2,1,0:T(8,128)(2,1)S(1)} %get-tuple-element.33), channel_id=1, source_target_pairs={{0,4},{1,5},{2,6},{3,7},{4,0},{5,1},{6,2},{7,3},{8,12},{9,13},{10,... | collective-permute-start | bytes 393224 | tf_op jit(solution)/shard_map/ppermute | solution.py:341
  40.3 6.9 %collective-permute-start.22 = (bf16[2,256,128]{2,1,0:T(8,128)(2,1)S(1)}, bf16[2,256,128]{2,1,0:T(8,128)(2,1)S(1)}, u32[]{:S(2)}, u32[]{:S(2)}) collective-permute-start(bf16[2,256,128]{2,1,0:T(8,128)(2,1)S(1)} %get-tuple-element.34), channel_id=1, source_target_pairs={{0,5},{1,4},{2,7},{3,6},{4,1},{5,0},{6,3},{7,2},{8,13},{9,12},{10,... | collective-permute-start | bytes 393224 | tf_op jit(solution)/shard_map/ppermute | solution.py:341
  41.7 6.8 %collective-permute-start.16 = (bf16[2,2,64,128]{3,2,1,0:T(8,128)(2,1)S(1)}, bf16[2,2,64,128]{3,2,1,0:T(8,128)(2,1)S(1)}, u32[]{:S(2)}, u32[]{:S(2)}) collective-permute-start(bf16[2,2,64,128]{3,2,1,0:T(8,128)(2,1)S(1)} %pad_maximum_fusion.7), channel_id=1, source_target_pairs={{0,16},{8,24},{16,0},{24,8},{1,17},{9,25},{17,1},{25,9},{2,18},{10... | collective-permute-start | bytes 196616 | tf_op jit(solution)/shard_map/ppermute | solution.py:341
  41.8 6.8 %collective-permute-start.17 = (bf16[2,2,64,128]{3,2,1,0:T(8,128)(2,1)S(1)}, bf16[2,2,64,128]{3,2,1,0:T(8,128)(2,1)S(1)}, u32[]{:S(2)}, u32[]{:S(2)}) collective-permute-start(bf16[2,2,64,128]{3,2,1,0:T(8,128)(2,1)S(1)} %pad_maximum_fusion.8), channel_id=1, source_target_pairs={{0,8},{8,0},{16,24},{24,16},{1,9},{9,1},{17,25},{25,17},{2,10},{10... | collective-permute-start | bytes 196616 | tf_op jit(solution)/shard_map/ppermute | solution.py:341
  44.4 6.1 %collective-permute-start.18 = (bf16[2,2,64,128]{3,2,1,0:T(8,128)(2,1)S(1)}, bf16[2,2,64,128]{3,2,1,0:T(8,128)(2,1)S(1)}, u32[]{:S(2)}, u32[]{:S(2)}) collective-permute-start(bf16[2,2,64,128]{3,2,1,0:T(8,128)(2,1)S(1)} %pad_maximum_fusion.9), channel_id=1, source_target_pairs={{0,24},{8,16},{16,8},{24,0},{1,25},{9,17},{17,9},{25,1},{2,26},{10... | collective-permute-start | bytes 196616 | tf_op jit(solution)/shard_map/ppermute | solution.py:341
  50.5 5.2 %collective-permute-start.23 = (bf16[4,256,128]{2,1,0:T(8,128)(2,1)S(1)}, bf16[4,256,128]{2,1,0:T(8,128)(2,1)S(1)}, u32[]{:S(2)}, u32[]{:S(2)}) collective-permute-start(bf16[4,256,128]{2,1,0:T(8,128)(2,1)S(1)} %shard_map.112), channel_id=1, source_target_pairs={{0,2},{1,3},{2,0},{3,1},{4,6},{5,7},{6,4},{7,5},{8,10},{9,11},{10,... | collective-permute-start | bytes 786440 | tf_op jit(solution)/shard_map/ppermute | solution.py:341
  50.5 4.0 %collective-permute-start.19 = (bf16[2,64,128]{2,1,0:T(8,128)(2,1)S(1)}, bf16[2,64,128]{2,1,0:T(8,128)(2,1)S(1)}, u32[]{:S(2)}, u32[]{:S(2)}) collective-permute-start(bf16[2,64,128]{2,1,0:T(8,128)(2,1)S(1)} %get-tuple-element.30), channel_id=1, source_target_pairs={{0,4},{4,0},{1,5},{5,1},{2,6},{6,2},{3,7},{7,3},{8,12},{12,8},{9,1... | collective-permute-start | bytes 98312 | tf_op jit(solution)/shard_map/ppermute | solution.py:341

commit v7 on v6

--- a/solution.py
+++ b/solution.py
@@ -11,6 +11,7 @@
 KVH = 8
 RESP_LEN = 64
 SCALE = DH ** (-0.5)
+LOG2E = 1.4426950408889634
 MASKED_SCORE = -1e30
 DEAD_LSE = 1e30
 PIECES = 3
@@ -128,6 +129,27 @@
     return ((scalars[3] ^ b) * (groups * rows)) >> shift_of(RESP_LEN)
 
 
+def prompt_end_of(scalars, response):
+    return scalars[4 + response]
+
+
+def resp_len_of(scalars, response):
+    return scalars[4 + (scalars.shape[0] - 4) // 2 + response]
+
+
+def all_visible(scalars, tokens):
+    last = (scalars[3] + 1) * (KVH * tokens)
+    seen = prompt_end_of(scalars, 0) >= last
+    for response in range(1, (scalars.shape[0] - 4) // 2):
+        seen = jnp.logical_and(seen, prompt_end_of(scalars, response) >= last)
+    return seen
+
+
+def in_branches(condition, body):
+    pl.when(condition)(functools.partial(body, True))
+    pl.when(jnp.logical_not(condition))(functools.partial(body, False))
+
+
 def lse_rows(size):
     return max(1, size // DH)
 
@@ -145,37 +167,43 @@
     return jnp.concatenate([ref[j, first : first + lines, :] for ref, j, _, _ in slabs], axis=0)
 
 
-def stat_kernel(blocks, nears, rows, tokens, scalars, prompt_end, *refs):
+def stat_kernel(blocks, nears, rows, tokens, scalars, *refs):
     row_refs, refs = refs[: len(blocks) * nears], refs[len(blocks) * nears :]
     pair_refs, before_refs, lse_ref = refs[: len(KEEP)], refs[len(KEEP) : -1], refs[-1]
     lines = (row_refs[0].shape[1] - STAT_ROWS) // 2
     for ref in before_refs:
         lse_ref[...] = ref[...]
-    for b, slabs in zip(blocks, block_slabs(blocks, nears, row_refs)):
-        count = len(slabs) * lines
-        offset = lax.broadcasted_iota(jnp.int32, (tokens, count), 0)
-        q = lines_of(slabs, 0, lines)
-        end = prompt_end[response_of(scalars, b, len(slabs), rows)]
-        scores = []
-        for i, ref in enumerate(pair_refs):
-            part = lax.dot_general(
-                pair_keys(ref, tokens),
-                q,
-                (((1,), (1,)), ((), ())),
-                preferred_element_type=jnp.float32,
-            )
-            starts = pair_starts(scalars, i, tokens)
-            visible = jnp.concatenate([offset < end - start for start in starts], axis=0)
-            scores.append(jnp.where(visible, part * SCALE, MASKED_SCORE))
-        scores = jnp.concatenate(scores, axis=0)
-        peak = jnp.max(scores, axis=0, keepdims=True)
-        total = jnp.sum(jnp.exp(scores - peak), axis=0, keepdims=True)
-        lse = peak + jnp.log(total)
-        if count < DH:
-            lse = jnp.concatenate([lse] * (DH // count), axis=1)
-        held = lse_rows(count)
-        for k in range(held):
-            lse_ref[pl.ds((scalars[3] ^ b) * held + k, 1), :] = lse[:, k * DH : (k + 1) * DH]
+
+    def body(seen):
+        for b, slabs in zip(blocks, block_slabs(blocks, nears, row_refs)):
+            count = len(slabs) * lines
+            q = lines_of(slabs, 0, lines)
+            end = prompt_end_of(scalars, response_of(scalars, b, len(slabs), rows))
+            scores = []
+            for i, ref in enumerate(pair_refs):
+                part = lax.dot_general(
+                    pair_keys(ref, tokens),
+                    q,
+                    (((1,), (1,)), ((), ())),
+                    preferred_element_type=jnp.float32,
+                )
+                if not seen:
+                    offset = lax.broadcasted_iota(jnp.int32, (tokens, count), 0)
+                    starts = pair_starts(scalars, i, tokens)
+                    visible = jnp.concatenate([offset < end - x for x in starts], axis=0)
+                    part = jnp.where(visible, part, MASKED_SCORE)
+                scores.append(part)
+            scores = jnp.concatenate(scores, axis=0)
+            peak = jnp.max(scores, axis=0, keepdims=True)
+            total = jnp.sum(jnp.exp2((scores - peak) * (SCALE * LOG2E)), axis=0, keepdims=True)
+            lse = peak * SCALE + jnp.log(total)
+            if count < DH:
+                lse = jnp.concatenate([lse] * (DH // count), axis=1)
+            held = lse_rows(count)
+            for k in range(held):
+                lse_ref[pl.ds((scalars[3] ^ b) * held + k, 1), :] = lse[:, k * DH : (k + 1) * DH]
+
+    in_branches(all_visible(scalars, tokens), body)
 
 
 def line_values(slabs, lines, first_piece):
@@ -212,47 +240,54 @@
         yield c * size, step * size, blocks[c : c + step], slabs
 
 
-def part_kernel(blocks, nears, rows, tokens, scalars, prompt_end, *refs):
+def part_kernel(blocks, nears, rows, tokens, scalars, *refs):
     row_refs, refs = refs[: len(blocks) * nears], refs[len(blocks) * nears :]
     pair_refs, (lse_ref, prob_ref, dscore_ref, dq_ref) = refs[: len(KEEP)], refs[len(KEEP) :]
     lines = (row_refs[0].shape[1] - STAT_ROWS) // 2
     all_slabs = block_slabs(blocks, nears, row_refs)
     size = len(all_slabs[0]) * lines
-    for first, count, held, slabs in steps_of(blocks, all_slabs, lines):
-        offset = lax.broadcasted_iota(jnp.int32, (tokens, count), 0)
-        q, o_grad = lines_of(slabs, 0, lines), lines_of(slabs, lines, lines)
-        dots = line_values(slabs, lines, PIECES)
-        lse = lse_lines(lse_ref, scalars, held, size)
-        ends = [prompt_end[response_of(scalars, b, len(all_slabs[0]), rows)] for b in held]
-        end = jnp.concatenate([jnp.full((1, size), x, jnp.int32) for x in ends], axis=1)
-        dq_t = jnp.zeros((DH, count), jnp.float32)
-        for i, ref in enumerate(pair_refs):
-            k, v = pair_keys(ref, tokens), pair_values(ref, tokens)
-            scores = lax.dot_general(
-                k, q, (((1,), (1,)), ((), ())), preferred_element_type=jnp.float32
-            )
-            starts = pair_starts(scalars, i, tokens)
-            visible = jnp.concatenate([offset < end - start for start in starts], axis=0)
-            prob = jnp.where(visible, jnp.exp(scores * SCALE - lse), 0.0)
-            dprob = lax.dot_general(
-                v, o_grad, (((1,), (1,)), ((), ())), preferred_element_type=jnp.float32
-            )
-            dscore = (prob * (dprob - dots)).astype(jnp.bfloat16)
-            prob_ref[i, :, first : first + count] = prob.astype(jnp.bfloat16)
-            dscore_ref[i, :, first : first + count] = dscore
-            dq_t = dq_t + jnp.dot(k.T, dscore, preferred_element_type=jnp.float32)
-        dq_ref[:, first : first + count] = dq_t
-
-
-def token_kernel(blocks, nears, rows, tokens, scalars, resp_len, *refs):
+
+    def body(seen):
+        for first, count, held, slabs in steps_of(blocks, all_slabs, lines):
+            q, o_grad = lines_of(slabs, 0, lines), lines_of(slabs, lines, lines)
+            dots = line_values(slabs, lines, PIECES)
+            lse = lse_lines(lse_ref, scalars, held, size) * LOG2E
+            dq_t = jnp.zeros((DH, count), jnp.float32)
+            for i, ref in enumerate(pair_refs):
+                k, v = pair_keys(ref, tokens), pair_values(ref, tokens)
+                scores = lax.dot_general(
+                    k, q, (((1,), (1,)), ((), ())), preferred_element_type=jnp.float32
+                )
+                prob = jnp.exp2(scores * (SCALE * LOG2E) - lse)
+                if not seen:
+                    responses = [response_of(scalars, b, len(all_slabs[0]), rows) for b in held]
+                    end = jnp.concatenate(
+                        [jnp.full((1, size), prompt_end_of(scalars, r), jnp.int32) for r in responses],
+                        axis=1,
+                    )
+                    offset = lax.broadcasted_iota(jnp.int32, (tokens, count), 0)
+                    starts = pair_starts(scalars, i, tokens)
+                    visible = jnp.concatenate([offset < end - x for x in starts], axis=0)
+                    prob = jnp.where(visible, prob, 0.0)
+                dprob = lax.dot_general(
+                    v, o_grad, (((1,), (1,)), ((), ())), preferred_element_type=jnp.float32
+                )
+                dscore = (prob * (dprob - dots)).astype(jnp.bfloat16)
+                prob_ref[i, :, first : first + count] = prob.astype(jnp.bfloat16)
+                dscore_ref[i, :, first : first + count] = dscore
+                dq_t = dq_t + jnp.dot(k.T, dscore, preferred_element_type=jnp.float32)
+            dq_ref[:, first : first + count] = dq_t
+
+    in_branches(all_visible(scalars, tokens), body)
+
+
+def weight_kernel(blocks, nears, rows, scalars, *refs):
     row_refs, refs = refs[: len(blocks) * nears], refs[len(blocks) * nears :]
-    (prob_ref, dscore_ref, dq_ref), refs = refs[:3], refs[3:]
-    lse_refs, refs = refs[: len(blocks)], refs[len(blocks) :]
-    dkv_refs, (*dq_refs, dk_acc, dv_acc) = refs[: len(KEEP)], refs[len(KEEP) :]
+    lse_refs, (dq_ref, weight_ref, *dq_refs) = refs[: len(blocks)], refs[len(blocks) :]
     lines = (row_refs[0].shape[1] - STAT_ROWS) // 2
     all_slabs = block_slabs(blocks, nears, row_refs)
-    size = len(all_slabs[0]) * lines
-    groups, row_count = len(all_slabs[0]), len(all_slabs[0]) // nears
+    groups = len(all_slabs[0])
+    size = groups * lines
     lane = lax.broadcasted_iota(jnp.int32, (1, 2 * lines), 1)
     for first, count, held, slabs in steps_of(blocks, all_slabs, lines):
         sources = [(b, slab) for b in held for slab in all_slabs[blocks.index(b)]]
@@ -262,7 +297,7 @@
             for b, (_, _, n, j) in sources[m : m + 2]:
                 device = (scalars[3] ^ b) * groups + group_at(scalars, j, n, nears)
                 row.append(device * rows & (RESP_LEN - 1))
-                length.append(resp_len[response_of(scalars, b, groups, rows)])
+                length.append(resp_len_of(scalars, response_of(scalars, b, groups, rows)))
             row = jnp.where(lane < lines, row[0], row[1]) + (lane & (rows - 1))
             live.append((row < jnp.where(lane < lines, length[0], length[1])).astype(jnp.int32))
         live = jnp.concatenate(live, axis=1)
@@ -272,9 +307,24 @@
         total = sum(jnp.exp(x - peak) for x in part_lse) + jnp.exp(self_lse - peak)
         lse = jnp.where(live > 0, peak + jnp.log(total), DEAD_LSE)
         weight = jnp.exp(part_lse[0] - lse)
-        weight_t = jnp.broadcast_to(weight, (DH, count)).T
+        weight_ref[:, first : first + count] = weight
+        dq = (dq_ref[:, first : first + count] * (weight * SCALE)).T.astype(jnp.bfloat16)
+        for m, (b, (_, _, n, j)) in enumerate(sources):
+            source = (scalars[3] ^ b) * (groups // nears) + (scalars[1] ^ j)
+            dq_refs[n][source] = dq[m * lines : (m + 1) * lines]
+
+
+def token_kernel(blocks, nears, tokens, *refs):
+    row_refs, refs = refs[: len(blocks) * nears], refs[len(blocks) * nears :]
+    (prob_ref, dscore_ref, weight_ref), refs = refs[:3], refs[3:]
+    *dkv_refs, dk_acc, dv_acc = refs
+    lines = (row_refs[0].shape[1] - STAT_ROWS) // 2
+    all_slabs = block_slabs(blocks, nears, row_refs)
+    size = len(all_slabs[0]) * lines
+    for first, count, held, slabs in steps_of(blocks, all_slabs, lines):
+        weight = jnp.broadcast_to(weight_ref[:, first : first + count], (DH, count)).T
         q, o_grad = (
-            (lines_of(slabs, start, lines).astype(jnp.float32) * weight_t).astype(jnp.bfloat16)
+            (lines_of(slabs, start, lines).astype(jnp.float32) * weight).astype(jnp.bfloat16)
             for start in (0, lines)
         )
         for i in range(len(KEEP)):
@@ -288,51 +338,38 @@
                 dk_acc[i] = dk
                 dv_acc[i] = dv
             else:
-                for n in range(2):
+                for n, out in enumerate(dkv_refs):
                     inner = slice(n * tokens, (n + 1) * tokens)
-                    dkv_refs[i][n, 0:tokens, :] = dk[inner].astype(jnp.bfloat16)
-                    dkv_refs[i][n, tokens : 2 * tokens, :] = dv[inner].astype(jnp.bfloat16)
-        dq = (dq_ref[:, first : first + count] * (weight * SCALE)).T.astype(jnp.bfloat16)
-        for m, (b, (_, _, n, j)) in enumerate(sources):
-            dq_refs[n][blocks.index(b), j] = dq[m * lines : (m + 1) * lines]
-
-
-def add_query_kernel(nears, *refs):
-    own_refs, came_refs, out_refs = refs[:nears], refs[nears:-2], refs[-2:]
-    row_count = own_refs[0].shape[0]
-    for n in range(nears):
-        for j in range(row_count):
-            total = own_refs[n][j].astype(jnp.float32)
-            for ref in came_refs:
-                total = total + ref[n, j].astype(jnp.float32)
-            out_refs[min(j, 1)][n] = total.astype(jnp.bfloat16)
+                    out[i, 0:tokens, :] = dk[inner].astype(jnp.bfloat16)
+                    out[i, tokens : 2 * tokens, :] = dv[inner].astype(jnp.bfloat16)
 
 
 def tie_kernel(*refs):
     pass
 
 
-def write_query_kernel(nears, scalars, *refs):
-    slab_refs, out_ref = refs[:-1], refs[-1]
-    lines = slab_refs[0].shape[1]
-    for j, ref in enumerate(slab_refs):
-        for n in range(nears):
-            first = pl.multiple_of(group_at(scalars, j, n, nears) * lines, lines)
-            out_ref[pl.ds(first, lines), :] = ref[n]
-
-
-def write_kv_kernel(groups, heads, scalars, *refs):
-    pair_refs, (came_ref, out_k_ref, out_v_ref, sems) = refs[: len(KEEP)], refs[len(KEEP) :]
-    tokens = out_k_ref.shape[0]
+def write_kernel(row_count, nears, heads, scalars, *refs):
+    dq_ref, pair_refs, (out_q_ref, out_k_ref, out_v_ref, sum_ref, sems) = refs[0], refs[1:-5], refs[-5:]
+    groups, lines, tokens = row_count * nears, dq_ref.shape[2], out_k_ref.shape[0]
     copies = []
     for i, ref in enumerate(pair_refs):
-        for source, other in ((ref.at[0], 0), (came_ref.at[i], FIRST)):
+        for n, other in enumerate((0, FIRST)):
             columns = pl.ds(column_of(scalars[0] ^ KEEP[i] ^ other, groups, heads), DH)
-            copies.append((source.at[0:tokens, :], out_k_ref.at[:, columns]))
-            copies.append((source.at[tokens : 2 * tokens, :], out_v_ref.at[:, columns]))
+            copies.append((ref.at[n, 0:tokens, :], out_k_ref.at[:, columns]))
+            copies.append((ref.at[n, tokens : 2 * tokens, :], out_v_ref.at[:, columns]))
+    for row in range(row_count):
+        for n in range(nears):
+            first = pl.multiple_of((row * nears + (scalars[2] ^ n)) * lines, lines)
+            copies.append((sum_ref.at[row * nears + n], out_q_ref.at[pl.ds(first, lines), :]))
     copies = [pltpu.make_async_copy(s, t, sems.at[n]) for n, (s, t) in enumerate(copies)]
-    for copy in copies:
+    for copy in copies[:-groups]:
         copy.start()
+    for g in range(groups):
+        total = dq_ref[g // nears, g % nears].astype(jnp.float32)
+        for source in range(g // nears + row_count, dq_ref.shape[0], row_count):
+            total = total + dq_ref[source, g % nears].astype(jnp.float32)
+        sum_ref[g] = total.astype(jnp.bfloat16)
+        copies[g - groups].start()
     for copy in copies:
         copy.wait()
 
@@ -348,21 +385,15 @@
     return [swap(x, members, j, KVH) if j else x for x, j in zip(pairs, KEEP)]
 
 
-def tie(x, others):
+def tie(x, others, scalars):
     return pl.pallas_call(
         tie_kernel,
-        in_specs=[ANY] * (1 + len(others)),
+        in_specs=[SMEM] + [ANY] * (1 + len(others)),
         out_specs=ANY,
         out_shape=jax.ShapeDtypeStruct(x.shape, x.dtype),
-        input_output_aliases={0: 0},
+        input_output_aliases={1: 0},
         compiler_params=PARAMS,
-    )(x, *others)
-
-
-def swap_back(pairs, others):
-    members = ("row", "near", "head")
-    pairs = [swap(x, members, j, KVH) if j else x for x, j in zip(pairs, KEEP)]
-    return pairs, swap(tie(jnp.stack([x[1] for x in pairs]), others), members, FIRST, KVH)
+    )(scalars, x, *others)
 
 
 def shards(parts, row_count, nears, heads, queries, grad_out, outputs, lse_self, keys, values, resp_len, prompt_end):
@@ -375,7 +406,9 @@
     assert 2 * lines == DH and RESP_LEN % (groups * rows) == 0 and row_count <= 2 and nears <= 2
     row, near = lax.axis_index("row"), lax.axis_index("near")
     member = (row * nears + near) * heads + lax.axis_index("head")
-    scalars = jnp.stack([member, row, near, lax.axis_index("part")]).astype(jnp.int32)
+    place = jnp.stack([member, row, near, lax.axis_index("part")]).astype(jnp.int32)
+    scalars = jnp.concatenate([place, prompt_end, resp_len])
+    place, scalars = (pltpu.with_memory_space_constraint(x, pltpu.SMEM) for x in (place, scalars))
 
     def as_lines(x):
         return x.reshape(rows, own_heads, DH).transpose(1, 0, 2).reshape(own_lines, DH)
@@ -397,7 +430,7 @@
         ],
         compiler_params=PARAMS,
     )(
-        scalars,
+        place,
         in_hbm(as_lines(queries)),
         in_hbm(as_lines(grad_out)),
         in_hbm(as_lines(outputs)),
@@ -409,28 +442,29 @@
     own_block = jnp.stack([x[n] for n in range(nears) for x in slabs])
     pairs = swap_pairs(kv_keep, kv_send)
     far = [1 << n for n in reversed(range(shift_of(parts)))]
-    order, came = [0], [own_block]
+
+    def row_refs_of(x):
+        return [x, swap(x[row_count:], "near", 1, nears)] if nears > 1 else [x]
+
+    row_refs = row_refs_of(own_block)
+    blocks, came = [0], [own_block]
     for d in far:
         if d == 1:
-            came = came[:1] + [tie(x, pairs[1:]) for x in came[1:]]
+            came = came[:1] + [tie(x, pairs[1:], scalars) for x in came[1:]]
         came = came + [swap(x, "part", d, parts) for x in came]
-        order = order + [b ^ d for b in order]
-    blocks = order
-
-    def row_refs_of(x):
-        return [x, swap(x[row_count:], "near", 1, nears)] if nears > 1 else [x]
+        blocks = blocks + [b ^ d for b in blocks]
 
     def part_lse(held, refs, before):
         return pl.pallas_call(
             functools.partial(stat_kernel, held, nears, rows, tokens),
-            in_specs=[SMEM] * 2 + [VMEM] * (len(refs) + len(KEEP) + len(before)),
+            in_specs=[SMEM] + [VMEM] * (len(refs) + len(KEEP) + len(before)),
             out_shape=jax.ShapeDtypeStruct((parts * lse_rows(groups * lines), DH), jnp.float32),
             compiler_params=PARAMS,
-        )(scalars, prompt_end, *refs, *pairs, *before)
-
-    row_refs = [ref for x in came[:-1] for ref in row_refs_of(x)]
+        )(scalars, *refs, *pairs, *before)
+
+    row_refs = row_refs + [ref for x in came[1:-1] for ref in row_refs_of(x)]
     lse = [part_lse(blocks[:-1], row_refs, [])]
-    last_refs = row_refs_of(tie(came[-1], lse))
+    last_refs = row_refs_of(tie(came[-1], lse, scalars))
     lse = [part_lse(blocks[-1:], last_refs, lse)]
     row_refs = row_refs + last_refs
     every_lse = lse + [swap(lse[0], "part", d, parts) for d in range(1, parts)]
@@ -439,53 +473,46 @@
     score_shape = jax.ShapeDtypeStruct((len(KEEP), 2 * tokens, all_lines), jnp.bfloat16)
     prob, dscore, dq = pl.pallas_call(
         functools.partial(part_kernel, blocks, nears, rows, tokens),
-        in_specs=[SMEM] * 2 + [VMEM] * (len(row_refs) + len(KEEP) + 1),
+        in_specs=[SMEM] + [VMEM] * (len(row_refs) + len(KEEP) + 1),
         out_specs=[VMEM] * 3,
         out_shape=[score_shape] * 2 + [jax.ShapeDtypeStruct((DH, all_lines), jnp.float32)],
         compiler_params=PARAMS,
-    )(scalars, prompt_end, *row_refs, *pairs, *lse)
-    dq_shape = jax.ShapeDtypeStruct((parts, row_count, lines, DH), jnp.bfloat16)
+    )(scalars, *row_refs, *pairs, *lse)
+    dq_shape = jax.ShapeDtypeStruct((parts * row_count, lines, DH), jnp.bfloat16)
+    weight, *dq = pl.pallas_call(
+        functools.partial(weight_kernel, blocks, nears, rows),
+        in_specs=[SMEM] + [VMEM] * (len(row_refs) + parts + 1),
+        out_shape=[jax.ShapeDtypeStruct((1, all_lines), jnp.float32)] + [dq_shape] * nears,
+        compiler_params=PARAMS,
+    )(scalars, *row_refs, *every_lse, dq)
+    dq = [swap(x, "near", n, nears) if n else x for n, x in enumerate(dq)]
     acc = pltpu.VMEM((len(KEEP), 2 * tokens, DH), jnp.float32)
-    pair_shape = jax.ShapeDtypeStruct((2, 2 * tokens, DH), jnp.bfloat16)
-    outs = pl.pallas_call(
-        functools.partial(token_kernel, blocks, nears, rows, tokens),
-        in_specs=[SMEM] * 2 + [VMEM] * (len(row_refs) + 3 + parts),
-        out_shape=[pair_shape] * len(KEEP) + [dq_shape] * nears,
+    dkv_keep, dkv_send = pl.pallas_call(
+        functools.partial(token_kernel, blocks, nears, tokens),
+        in_specs=[VMEM] * (len(row_refs) + 3),
+        out_shape=[half_shape] * 2,
         scratch_shapes=[acc] * 2,
         compiler_params=PARAMS,
-    )(scalars, resp_len, *row_refs, prob, dscore, dq, *every_lse)
-    dkv, dq = outs[: len(KEEP)], outs[len(KEEP) :]
-
-    dq = [swap(x, "near", n, nears) if n else x for n, x in enumerate(dq)]
-    came = [
-        swap(jnp.stack([x[at] for x in dq]), "part", b, parts) for at, b in enumerate(blocks) if b
-    ]
-    sum_shape = jax.ShapeDtypeStruct((nears, lines, DH), jnp.bfloat16)
-    own_sum, sent_sum = pl.pallas_call(
-        functools.partial(add_query_kernel, nears),
-        in_specs=[VMEM] * (nears + len(came)),
-        out_shape=[sum_shape] * 2,
-        compiler_params=PARAMS,
-    )(*[x[0] for x in dq], *came)
-    sums = [own_sum, swap(sent_sum, "row", 1, row_count)][:row_count]
-    pairs, came = swap_back(dkv, came)
-    out_q = pl.pallas_call(
-        functools.partial(write_query_kernel, nears),
-        in_specs=[SMEM] + [VMEM] * row_count,
-        out_shape=jax.ShapeDtypeStruct((own_lines, DH), jnp.bfloat16),
-        compiler_params=PARAMS,
-    )(scalars, *sums)
-    out_k, out_v = pl.pallas_call(
-        functools.partial(write_kv_kernel, groups, heads),
-        in_specs=[SMEM] + [VMEM] * (len(KEEP) + 1),
-        out_specs=[HBM] * 2,
+    )(*row_refs, prob, dscore, weight)
+    dq = lax.all_to_all(
+        jnp.stack(dq, axis=1), ("part", "row"), split_axis=0, concat_axis=0, tiled=True
+    )
+    pairs = swap_pairs(dkv_keep, dkv_send)
+    out_q, out_k, out_v = pl.pallas_call(
+        functools.partial(write_kernel, row_count, nears, heads),
+        in_specs=[SMEM] + [VMEM] * (1 + len(KEEP)),
+        out_specs=[HBM] * 3,
         out_shape=[
+            jax.ShapeDtypeStruct((own_lines, DH), jnp.bfloat16),
             jax.ShapeDtypeStruct(keys.shape, jnp.bfloat16),
             jax.ShapeDtypeStruct(values.shape, jnp.bfloat16),
         ],
-        scratch_shapes=[pltpu.SemaphoreType.DMA((4 * len(KEEP),))],
+        scratch_shapes=[
+            pltpu.VMEM((groups, lines, DH), jnp.bfloat16),
+            pltpu.SemaphoreType.DMA((4 * len(KEEP) + groups,)),
+        ],
         compiler_params=PARAMS,
-    )(scalars, *pairs, came)
+    )(scalars, dq, *pairs)
     out_q = out_q.reshape(own_heads, rows, DH).transpose(1, 0, 2).reshape(rows, own_heads * DH)
     return out_q, out_k, out_v
 

time: 57.4 us -> 58.7 us (1.023)
  waiting for transfers between devices: 15.6 us -> 16.5 us
  other arithmetic: 0.23 us -> 0.95 us
    all_to_all x0 -> x1, starting transfers between devices: none -> 4.19 us  [shards(): lax.all_to_all(jnp.stack(dq, axis=1), ('part', 'row'), split_axis=0, conc...]
    ppermute x24 -> x20, starting transfers between devices: 26.8 us -> 22.7 us  [swap(): return lax.ppermute(x, axis, [(i, i ^ distance) for i in range(size)])]
    ppermute x24 -> x20, waiting for transfers between devices: 15.6 us -> 16.5 us  [swap(): return lax.ppermute(x, axis, [(i, i ^ distance) for i in range(size)])]
    another operation x4 -> x1, other arithmetic: 0.06 us -> 0.73 us  [shards(): jnp.stack(dq, axis=1)]
    pallas_call x7 -> x5, Pallas kernels: 4.68 us -> 4.71 us  [the longest x1 1.52 us: shards(): pl.pallas_call(functools.partial(write_kernel, row_count, nears, heads),...]
  transfers between devices with their start and end apart: 24 -> 21, of which waited for: 13 -> 12; matrix products, arithmetic and copies ran while one was open for 0% -> 2% of each run, Pallas kernels for 10% -> 8%
where the time goes in v7:
time: 58.7 us; the launch traced here: 58.4 us
  starting transfers between devices  26.9 us (46%)
  waiting for transfers between devices  16.5 us (28%)
  Pallas kernels  11.7 us (20%)
  between operations  2.13 us (4%)
  other arithmetic  0.95 us (2%)
    ppermute x20, starting transfers between devices, swap(): return lax.ppermute(x, axis, [(i, i ^ distance) for i in range(size)])  22.7 us
    ppermute x20, waiting for transfers between devices, swap(): return lax.ppermute(x, axis, [(i, i ^ distance) for i in range(size)])  16.5 us
    all_to_all x1, starting transfers between devices, shards(): lax.all_to_all(jnp.stack(dq, axis=1), ('part', 'row'), split_axis=0, conc...  4.19 us
    pallas_call x2, Pallas kernels, part_lse(): pl.pallas_call(functools.partial(stat_kernel, held, nears, rows, tokens),...  2.62 us
    pallas_call x1, Pallas kernels, shards(): pl.pallas_call(functools.partial(part_kernel, blocks, nears, rows, tokens...  2.45 us
    pallas_call x1, Pallas kernels, shards(): pl.pallas_call(functools.partial(pack_kernel, row_count, nears, heads), i...  1.91 us
    pallas_call x1, Pallas kernels, shards(): pl.pallas_call(functools.partial(write_kernel, row_count, nears, heads),...  1.52 us
    pallas_call x1, Pallas kernels, shards(): pl.pallas_call(functools.partial(token_kernel, blocks, nears, tokens), in...  1.38 us
  transfers between devices with their start and end apart: 21, of which 12 were waited for; matrix products, arithmetic and copies ran while one was open for 2% of the time, Pallas kernels for 8%

profile of v7, /device:TPU:0, one launch (start us, length us, event | category | flops | bytes accessed | tf_op | source)
XLA Modules:
  0.0 58.4 jit_solution(1342975949651673991)
XLA Ops:
  0.6 0.1 pad_add_fusion.scalars
  0.7 1.9 %shard_map.103 = (bf16[2,144,128]{2,1,0:T(8,128)(2,1)S(1)}, bf16[2,144,128]{2,1,0:T(8,128)(2,1)S(1)}, bf16[4,256,128]{2,1,0:T(8,128)(2,1)S(1)}, bf16[4,256,128]{2,1,0:T(8,128)(2,1)S(1)}) custom-call(s32[4]{0:T(128)S(1)} %pad_add_fusion.scalars, bf16[256,128]{1,0:T(8,128)(2,1)} %bitcast.28, bf16[256,128]{1,0:T(8,128)(2,1)} %bitcast.29, ...), custom_call_target="tpu_custom_call" | custom-call | tf_op jit(solution)/shard_map/pallas_call | solution.py:421
  2.6 3.0 %collective-permute-start = (bf16[2,144,128]{2,1,0:T(8,128)(2,1)S(1)}, bf16[2,144,128]{2,1,0:T(8,128)(2,1)S(1)}, u32[]{:S(2)}, u32[]{:S(2)}) collective-permute-start(bf16[2,144,128]{2,1,0:T(8,128)(2,1)S(1)} %get-tuple-element.19), channel_id=1, source_target_pairs={{0,4},{4,0},{1,5},{5,1},{2,6},{6,2},{3,7},{7,3},{8,12},{12,8},{9,1... | collective-permute-start | bytes 221192 | tf_op jit(solution)/shard_map/ppermute | solution.py:378
  5.7 2.3 %collective-permute-done = bf16[2,144,128]{2,1,0:T(8,128)(2,1)S(1)} collective-permute-done((bf16[2,144,128]{2,1,0:T(8,128)(2,1)S(1)}, bf16[2,144,128]{2,1,0:T(8,128)(2,1)S(1)}, u32[]{:S(2)}, u32[]{:S(2)}) %collective-permute-start) | collective-permute-done | bytes 73760 | tf_op jit(solution)/shard_map/ppermute | solution.py:378
  8.0 3.2 %collective-permute-start.2 = (bf16[4,144,128]{2,1,0:T(8,128)(2,1)S(1)}, bf16[4,144,128]{2,1,0:T(8,128)(2,1)S(1)}, u32[]{:S(2)}, u32[]{:S(2)}) collective-permute-start(bf16[4,144,128]{2,1,0:T(8,128)(2,1)S(1)} %pad_maximum_fusion.1.refs_0_), channel_id=1, source_target_pairs={{0,16},{8,24},{16,0},{24,8},{1,17},{9,25},{17,1},{25,9},{2,18},{10... | collective-permute-start | bytes 442376 | tf_op jit(solution)/shard_map/ppermute | solution.py:378
  11.2 1.6 %collective-permute-start.4 = (bf16[2,256,128]{2,1,0:T(8,128)(2,1)S(1)}, bf16[2,256,128]{2,1,0:T(8,128)(2,1)S(1)}, u32[]{:S(2)}, u32[]{:S(2)}) collective-permute-start(bf16[2,256,128]{2,1,0:T(8,128)(2,1)S(1)} %pad_maximum_fusion.2), channel_id=1, source_target_pairs={{0,1},{1,0},{2,3},{3,2},{4,5},{5,4},{6,7},{7,6},{8,9},{9,8},{10,11... | collective-permute-start | bytes 393224 | tf_op jit(solution)/shard_map/ppermute | solution.py:378
  12.8 1.6 %collective-permute-start.5 = (bf16[2,256,128]{2,1,0:T(8,128)(2,1)S(1)}, bf16[2,256,128]{2,1,0:T(8,128)(2,1)S(1)}, u32[]{:S(2)}, u32[]{:S(2)}) collective-permute-start(bf16[2,256,128]{2,1,0:T(8,128)(2,1)S(1)} %pad_maximum_fusion.3), channel_id=1, source_target_pairs={{0,4},{1,5},{2,6},{3,7},{4,0},{5,1},{6,2},{7,3},{8,12},{9,13},{10,... | collective-permute-start | bytes 393224 | tf_op jit(solution)/shard_map/ppermute | solution.py:378
  14.4 0.5 collective-permute-start.6
  15.0 1.6 %collective-permute-start.8 = (bf16[4,144,128]{2,1,0:T(8,128)(2,1)S(1)}, bf16[4,144,128]{2,1,0:T(8,128)(2,1)S(1)}, u32[]{:S(2)}, u32[]{:S(2)}) collective-permute-start(bf16[4,144,128]{2,1,0:T(8,128)(2,1)S(1)} %pad_maximum_fusion.1.refs_0_), channel_id=1, source_target_pairs={{0,8},{8,0},{16,24},{24,16},{1,9},{9,1},{17,25},{25,17},{2,10},{10... | collective-permute-start | bytes 442376 | tf_op jit(solution)/shard_map/ppermute | solution.py:378
  17.8 0.1 concatenate.5.refs_0_.scalars
  17.9 0.0 collective-permute-done.2.refs_1_
  17.9 0.0 collective-permute-done.4.refs_2_.refs_7_.refs_3_.refs_9_
  17.9 1.0 %collective-permute-done.5.refs_3_.refs_8_.refs_4_.refs_10_ = bf16[2,256,128]{2,1,0:T(8,128)(2,1)S(1)} collective-permute-done((bf16[2,256,128]{2,1,0:T(8,128)(2,1)S(1)}, bf16[2,256,128]{2,1,0:T(8,128)(2,1)S(1)}, u32[]{:S(2)}, u32[]{:S(2)}) %collective-permute-start.5) | collective-permute-done | bytes 131104 | tf_op jit(solution)/shard_map/ppermute | solution.py:378
  18.9 1.4 %collective-permute-done.6.refs_4_.refs_9_.refs_5_.refs_11_ = bf16[2,256,128]{2,1,0:T(8,128)(2,1)S(1)} collective-permute-done((bf16[2,256,128]{2,1,0:T(8,128)(2,1)S(1)}, bf16[2,256,128]{2,1,0:T(8,128)(2,1)S(1)}, u32[]{:S(2)}, u32[]{:S(2)}) %collective-permute-start.6) | collective-permute-done | bytes 131104 | tf_op jit(solution)/shard_map/ppermute | solution.py:378
  20.4 0.5 shard_map.104.refs_2_
  20.9 1.6 %collective-permute-start.10 = (bf16[4,144,128]{2,1,0:T(8,128)(2,1)S(1)}, bf16[4,144,128]{2,1,0:T(8,128)(2,1)S(1)}, u32[]{:S(2)}, u32[]{:S(2)}) collective-permute-start(bf16[4,144,128]{2,1,0:T(8,128)(2,1)S(1)} %shard_map.104.refs_2_), channel_id=1, source_target_pairs={{0,8},{8,0},{16,24},{24,16},{1,9},{9,1},{17,25},{25,17},{2,10},{10... | collective-permute-start | bytes 442376 | tf_op jit(solution)/shard_map/ppermute | solution.py:378
  22.6 0.1 collective-permute-start.1
  22.6 0.0 collective-permute-done.8.refs_4_
  22.7 0.5 collective-permute-start.9
  23.2 0.1 collective-permute-start.7
  23.3 0.6 collective-permute-done.1.refs_1_
  23.9 0.2 collective-permute-done.9.refs_5_
  24.1 0.4 collective-permute-done.7.refs_3_
  24.5 1.5 %shard_map.105.refs_2_.refs_6_ = f32[8,128]{1,0:T(8,128)S(1)} custom-call(s32[6]{0:T(128)S(1)} %concatenate.5.refs_0_.scalars, bf16[4,144,128]{2,1,0:T(8,128)(2,1)S(1)} %pad_maximum_fusion.1.refs_0_, bf16[2,144,128]{2,1,0:T(8,128)(2,1)S(1)} %collective-permute-done.1.refs_1_, bf16[4,144,128]{2,1,0:T(8,128)(2,1)S(1)} %shard_map.104.refs_2_, ...), custom_call_target="tpu_custom_call" | custom-call | tf_op jit(solution)/shard_map/pallas_call | solution.py:458
  26.0 0.1 collective-permute-done.10.refs_1_
  26.1 0.5 shard_map.106.refs_0_.refs_6_
  26.7 0.2 collective-permute-start.11
  26.8 1.2 %collective-permute-done.11.refs_1_.refs_7_ = bf16[2,144,128]{2,1,0:T(8,128)(2,1)S(1)} collective-permute-done((bf16[2,144,128]{2,1,0:T(8,128)(2,1)S(1)}, bf16[2,144,128]{2,1,0:T(8,128)(2,1)S(1)}, u32[]{:S(2)}, u32[]{:S(2)}) %collective-permute-start.11) | collective-permute-done | bytes 73760 | tf_op jit(solution)/shard_map/ppermute | solution.py:378
  28.0 1.1 %shard_map.107.refs_12_.refs_8_ = f32[8,128]{1,0:T(8,128)S(1)} custom-call(s32[6]{0:T(128)S(1)} %concatenate.5.refs_0_.scalars, bf16[4,144,128]{2,1,0:T(8,128)(2,1)S(1)} %shard_map.106.refs_0_.refs_6_, bf16[2,144,128]{2,1,0:T(8,128)(2,1)S(1)} %collective-permute-done.11.refs_1_.refs_7_, bf16[2,256,128]{2,1,0:T(8,128)(2,1)S(1)} %pad_maximum_fusion.5.refs_6_.refs_2_.refs_8_, ...), custom_call_target="tpu_custom_call" | custom-call | tf_op jit(solution)/shard_map/pallas_call | solution.py:458
  29.1 1.6 %collective-permute-start.12 = (f32[8,128]{1,0:T(8,128)S(1)}, f32[8,128]{1,0:T(8,128)S(1)}, u32[]{:S(2)}, u32[]{:S(2)}) collective-permute-start(f32[8,128]{1,0:T(8,128)S(1)} %shard_map.107.refs_12_.refs_8_), channel_id=1, source_target_pairs={{0,8},{8,0},{16,24},{24,16},{1,9},{9,1},{17,25},{25,17},{2,10},{10... | collective-permute-start | bytes 12296 | tf_op jit(solution)/shard_map/ppermute | solution.py:378
  30.7 0.3 collective-permute-start.13
  31.1 2.5 %collective-permute-start.14 = (f32[8,128]{1,0:T(8,128)S(1)}, f32[8,128]{1,0:T(8,128)S(1)}, u32[]{:S(2)}, u32[]{:S(2)}) collective-permute-start(f32[8,128]{1,0:T(8,128)S(1)} %shard_map.107.refs_12_.refs_8_), channel_id=1, source_target_pairs={{0,24},{8,16},{16,8},{24,0},{1,25},{9,17},{17,9},{25,1},{2,26},{10... | collective-permute-start | bytes 12296 | tf_op jit(solution)/shard_map/ppermute | solution.py:378
  33.5 2.5 %shard_map.108 = (bf16[4,256,1024]{2,1,0:T(8,128)(2,1)S(1)}, bf16[4,256,1024]{2,1,0:T(8,128)(2,1)S(1)}, f32[128,1024]{1,0:T(8,128)S(1)}) custom-call(s32[6]{0:T(128)S(1)} %concatenate.5.refs_0_.scalars, bf16[4,144,128]{2,1,0:T(8,128)(2,1)S(1)} %pad_maximum_fusion.1.refs_0_, bf16[2,144,128]{2,1,0:T(8,128)(2,1)S(1)} %collective-permute-done.1.refs_1_, ...), custom_call_target="tpu_custom_call" | custom-call | tf_op jit(solution)/shard_map/pallas_call | solution.py:474
  36.0 0.0 collective-permute-done.12.refs_9_
  36.0 0.4 collective-permute-done.14.refs_11_
  36.5 0.7 %shard_map.109 = (f32[1,1024]{1,0:T(1,128)S(1)}, bf16[8,64,128]{2,1,0:T(8,128)(2,1)S(1)}, bf16[8,64,128]{2,1,0:T(8,128)(2,1)S(1)}) custom-call(s32[6]{0:T(128)S(1)} %concatenate.5.refs_0_.scalars, bf16[4,144,128]{2,1,0:T(8,128)(2,1)S(1)} %pad_maximum_fusion.1.refs_0_, bf16[2,144,128]{2,1,0:T(8,128)(2,1)S(1)} %collective-permute-done.1.refs_1_, ...), custom_call_target="tpu_custom_call" | custom-call | tf_op jit(solution)/shard_map/pallas_call | solution.py:482
  37.2 1.4 %shard_map.110 = (bf16[4,256,128]{2,1,0:T(8,128)(2,1)S(1)}, bf16[4,256,128]{2,1,0:T(8,128)(2,1)S(1)}) custom-call(bf16[4,144,128]{2,1,0:T(8,128)(2,1)S(1)} %pad_maximum_fusion.1.refs_0_, bf16[2,144,128]{2,1,0:T(8,128)(2,1)S(1)} %collective-permute-done.1.refs_1_, bf16[4,144,128]{2,1,0:T(8,128)(2,1)S(1)} %shard_map.104.refs_2_, ...), custom_call_target="tpu_custom_call" | custom-call | tf_op jit(solution)/shard_map/pallas_call | solution.py:490
  38.6 0.1 collective-permute-start.16
  38.7 0.5 collective-permute-start.15
  39.2 1.2 %collective-permute-done.15 = bf16[8,64,128]{2,1,0:T(8,128)(2,1)S(1)} collective-permute-done((bf16[8,64,128]{2,1,0:T(8,128)(2,1)S(1)}, bf16[8,64,128]{2,1,0:T(8,128)(2,1)S(1)}, u32[]{:S(2)}, u32[]{:S(2)}) %collective-permute-start.15) | collective-permute-done | bytes 131104 | tf_op jit(solution)/shard_map/ppermute | solution.py:378
  40.4 0.7 %pad_maximum_fusion = bf16[8,2,64,128]{3,2,1,0:T(8,128)(2,1)} fusion(bf16[8,1,64,128]{3,2,1,0:T(8,128)(2,1)S(1)} %bitcast.27, bf16[8,1,64,128]{3,2,1,0:T(8,128)(2,1)S(1)} %bitcast.26), kind=kLoop, calls=%fused_computation | loop fusion | flops 131072 | bytes 524288 | tf_op jit(solution)/shard_map/stack | solution.py:498
  41.1 4.2 %all-to-all-start = ((bf16[8,2,64,128]{3,2,1,0:T(8,128)(2,1)}), bf16[8,2,64,128]{3,2,1,0:T(8,128)(2,1)S(1)}, u32[]{:S(2)}, u32[]{:S(2)}) async-start(bf16[8,2,64,128]{3,2,1,0:T(8,128)(2,1)} %pad_maximum_fusion), calls=%async_computation | async-start | bytes 524288 | tf_op jit(solution)/shard_map/all_to_all | solution.py:497
  45.3 1.6 %collective-permute-start.19 = (bf16[2,256,128]{2,1,0:T(8,128)(2,1)S(1)}, bf16[2,256,128]{2,1,0:T(8,128)(2,1)S(1)}, u32[]{:S(2)}, u32[]{:S(2)}) collective-permute-start(bf16[2,256,128]{2,1,0:T(8,128)(2,1)S(1)} %pad_maximum_fusion.9), channel_id=1, source_target_pairs={{0,5},{1,4},{2,7},{3,6},{4,1},{5,0},{6,3},{7,2},{8,13},{9,12},{10,... | collective-permute-start | bytes 393224 | tf_op jit(solution)/shard_map/ppermute | solution.py:378
  47.0 0.5 collective-permute-start.18
  47.5 1.5 %collective-permute-start.17 = (bf16[2,256,128]{2,1,0:T(8,128)(2,1)S(1)}, bf16[2,256,128]{2,1,0:T(8,128)(2,1)S(1)}, u32[]{:S(2)}, u32[]{:S(2)}) collective-permute-start(bf16[2,256,128]{2,1,0:T(8,128)(2,1)S(1)} %pad_maximum_fusion.7), channel_id=1, source_target_pairs={{0,1},{1,0},{2,3},{3,2},{4,5},{5,4},{6,7},{7,6},{8,9},{9,8},{10,11... | collective-permute-start | bytes 393224 | tf_op jit(solution)/shard_map/ppermute | solution.py:378
  49.1 4.3 %collective-permute-done.19.refs_4_ = bf16[2,256,128]{2,1,0:T(8,128)(2,1)S(1)} collective-permute-done((bf16[2,256,128]{2,1,0:T(8,128)(2,1)S(1)}, bf16[2,256,128]{2,1,0:T(8,128)(2,1)S(1)}, u32[]{:S(2)}, u32[]{:S(2)}) %collective-permute-start.19) | collective-permute-done | bytes 131104 | tf_op jit(solution)/shard_map/ppermute | solution.py:378
  53.4 3.4 %collective-permute-done.18.refs_3_ = bf16[2,256,128]{2,1,0:T(8,128)(2,1)S(1)} collective-permute-done((bf16[2,256,128]{2,1,0:T(8,128)(2,1)S(1)}, bf16[2,256,128]{2,1,0:T(8,128)(2,1)S(1)}, u32[]{:S(2)}, u32[]{:S(2)}) %collective-permute-start.18) | collective-permute-done | bytes 131104 | tf_op jit(solution)/shard_map/ppermute | solution.py:378
  56.8 1.5 %shard_map.111 = (bf16[256,128]{1,0:T(8,128)(2,1)}, bf16[128,1024]{1,0:T(8,128)(2,1)}, bf16[128,1024]{1,0:T(8,128)(2,1)}) custom-call(s32[6]{0:T(128)S(1)} %concatenate.5.refs_0_.scalars, bf16[8,2,64,128]{3,2,1,0:T(8,128)(2,1)S(1)} %all-to-all-done.refs_0_, bf16[2,256,128]{2,1,0:T(8,128)(2,1)S(1)} %pad_maximum_fusion.6.refs_1_, ...), custom_call_target="tpu_custom_call" | custom-call | tf_op jit(solution)/shard_map/pallas_call | solution.py:501
  (25 shorter events, 0.3 us)
Async XLA Ops:
  2.6 5.4 %collective-permute-start = (bf16[2,144,128]{2,1,0:T(8,128)(2,1)S(1)}, bf16[2,144,128]{2,1,0:T(8,128)(2,1)S(1)}, u32[]{:S(2)}, u32[]{:S(2)}) collective-permute-start(bf16[2,144,128]{2,1,0:T(8,128)(2,1)S(1)} %get-tuple-element.19), channel_id=1, source_target_pairs={{0,4},{4,0},{1,5},{5,1},{2,6},{6,2},{3,7},{7,3},{8,12},{12,8},{9,1... | collective-permute-start | bytes 221192 | tf_op jit(solution)/shard_map/ppermute | solution.py:378
  5.7 5.5 %collective-permute-start.3 = (bf16[4,256,128]{2,1,0:T(8,128)(2,1)S(1)}, bf16[4,256,128]{2,1,0:T(8,128)(2,1)S(1)}, u32[]{:S(2)}, u32[]{:S(2)}) collective-permute-start(bf16[4,256,128]{2,1,0:T(8,128)(2,1)S(1)} %get-tuple-element.21), channel_id=1, source_target_pairs={{0,2},{1,3},{2,0},{3,1},{4,6},{5,7},{6,4},{7,5},{8,10},{9,11},{10,... | collective-permute-start | bytes 786440 | tf_op jit(solution)/shard_map/ppermute | solution.py:378
  8.0 9.9 %collective-permute-start.2 = (bf16[4,144,128]{2,1,0:T(8,128)(2,1)S(1)}, bf16[4,144,128]{2,1,0:T(8,128)(2,1)S(1)}, u32[]{:S(2)}, u32[]{:S(2)}) collective-permute-start(bf16[4,144,128]{2,1,0:T(8,128)(2,1)S(1)} %pad_maximum_fusion.1.refs_0_), channel_id=1, source_target_pairs={{0,16},{8,24},{16,0},{24,8},{1,17},{9,25},{17,1},{25,9},{2,18},{10... | collective-permute-start | bytes 442376 | tf_op jit(solution)/shard_map/ppermute | solution.py:378
  11.2 6.7 %collective-permute-start.4 = (bf16[2,256,128]{2,1,0:T(8,128)(2,1)S(1)}, bf16[2,256,128]{2,1,0:T(8,128)(2,1)S(1)}, u32[]{:S(2)}, u32[]{:S(2)}) collective-permute-start(bf16[2,256,128]{2,1,0:T(8,128)(2,1)S(1)} %pad_maximum_fusion.2), channel_id=1, source_target_pairs={{0,1},{1,0},{2,3},{3,2},{4,5},{5,4},{6,7},{7,6},{8,9},{9,8},{10,11... | collective-permute-start | bytes 393224 | tf_op jit(solution)/shard_map/ppermute | solution.py:378
  12.8 6.1 %collective-permute-start.5 = (bf16[2,256,128]{2,1,0:T(8,128)(2,1)S(1)}, bf16[2,256,128]{2,1,0:T(8,128)(2,1)S(1)}, u32[]{:S(2)}, u32[]{:S(2)}) collective-permute-start(bf16[2,256,128]{2,1,0:T(8,128)(2,1)S(1)} %pad_maximum_fusion.3), channel_id=1, source_target_pairs={{0,4},{1,5},{2,6},{3,7},{4,0},{5,1},{6,2},{7,3},{8,12},{9,13},{10,... | collective-permute-start | bytes 393224 | tf_op jit(solution)/shard_map/ppermute | solution.py:378
  14.4 5.9 %collective-permute-start.6 = (bf16[2,256,128]{2,1,0:T(8,128)(2,1)S(1)}, bf16[2,256,128]{2,1,0:T(8,128)(2,1)S(1)}, u32[]{:S(2)}, u32[]{:S(2)}) collective-permute-start(bf16[2,256,128]{2,1,0:T(8,128)(2,1)S(1)} %pad_maximum_fusion.4), channel_id=1, source_target_pairs={{0,5},{1,4},{2,7},{3,6},{4,1},{5,0},{6,3},{7,2},{8,13},{9,12},{10,... | collective-permute-start | bytes 393224 | tf_op jit(solution)/shard_map/ppermute | solution.py:378
  15.0 7.7 %collective-permute-start.8 = (bf16[4,144,128]{2,1,0:T(8,128)(2,1)S(1)}, bf16[4,144,128]{2,1,0:T(8,128)(2,1)S(1)}, u32[]{:S(2)}, u32[]{:S(2)}) collective-permute-start(bf16[4,144,128]{2,1,0:T(8,128)(2,1)S(1)} %pad_maximum_fusion.1.refs_0_), channel_id=1, source_target_pairs={{0,8},{8,0},{16,24},{24,16},{1,9},{9,1},{17,25},{25,17},{2,10},{10... | collective-permute-start | bytes 442376 | tf_op jit(solution)/shard_map/ppermute | solution.py:378
  20.9 5.2 %collective-permute-start.10 = (bf16[4,144,128]{2,1,0:T(8,128)(2,1)S(1)}, bf16[4,144,128]{2,1,0:T(8,128)(2,1)S(1)}, u32[]{:S(2)}, u32[]{:S(2)}) collective-permute-start(bf16[4,144,128]{2,1,0:T(8,128)(2,1)S(1)} %shard_map.104.refs_2_), channel_id=1, source_target_pairs={{0,8},{8,0},{16,24},{24,16},{1,9},{9,1},{17,25},{25,17},{2,10},{10... | collective-permute-start | bytes 442376 | tf_op jit(solution)/shard_map/ppermute | solution.py:378
  22.6 1.3 %collective-permute-start.1 = (bf16[2,144,128]{2,1,0:T(8,128)(2,1)S(1)}, bf16[2,144,128]{2,1,0:T(8,128)(2,1)S(1)}, u32[]{:S(2)}, u32[]{:S(2)}) collective-permute-start(bf16[2,144,128]{2,1,0:T(8,128)(2,1)S(1)} %pad_maximum_fusion.10), channel_id=1, source_target_pairs={{0,2},{2,0},{1,3},{3,1},{4,6},{6,4},{5,7},{7,5},{8,10},{10,8},{9,1... | collective-permute-start | bytes 221192 | tf_op jit(solution)/shard_map/ppermute | solution.py:378
  22.7 1.5 %collective-permute-start.9 = (bf16[2,144,128]{2,1,0:T(8,128)(2,1)S(1)}, bf16[2,144,128]{2,1,0:T(8,128)(2,1)S(1)}, u32[]{:S(2)}, u32[]{:S(2)}) collective-permute-start(bf16[2,144,128]{2,1,0:T(8,128)(2,1)S(1)} %slice.100), channel_id=1, source_target_pairs={{0,2},{2,0},{1,3},{3,1},{4,6},{6,4},{5,7},{7,5},{8,10},{10,8},{9,1... | collective-permute-start | bytes 221192 | tf_op jit(solution)/shard_map/ppermute | solution.py:378
  23.2 1.3 %collective-permute-start.7 = (bf16[2,144,128]{2,1,0:T(8,128)(2,1)S(1)}, bf16[2,144,128]{2,1,0:T(8,128)(2,1)S(1)}, u32[]{:S(2)}, u32[]{:S(2)}) collective-permute-start(bf16[2,144,128]{2,1,0:T(8,128)(2,1)S(1)} %slice.99), channel_id=1, source_target_pairs={{0,2},{2,0},{1,3},{3,1},{4,6},{6,4},{5,7},{7,5},{8,10},{10,8},{9,1... | collective-permute-start | bytes 221192 | tf_op jit(solution)/shard_map/ppermute | solution.py:378
  26.7 1.3 %collective-permute-start.11 = (bf16[2,144,128]{2,1,0:T(8,128)(2,1)S(1)}, bf16[2,144,128]{2,1,0:T(8,128)(2,1)S(1)}, u32[]{:S(2)}, u32[]{:S(2)}) collective-permute-start(bf16[2,144,128]{2,1,0:T(8,128)(2,1)S(1)} %slice.102), channel_id=1, source_target_pairs={{0,2},{2,0},{1,3},{3,1},{4,6},{6,4},{5,7},{7,5},{8,10},{10,8},{9,1... | collective-permute-start | bytes 221192 | tf_op jit(solution)/shard_map/ppermute | solution.py:378
  29.1 6.9 %collective-permute-start.12 = (f32[8,128]{1,0:T(8,128)S(1)}, f32[8,128]{1,0:T(8,128)S(1)}, u32[]{:S(2)}, u32[]{:S(2)}) collective-permute-start(f32[8,128]{1,0:T(8,128)S(1)} %shard_map.107.refs_12_.refs_8_), channel_id=1, source_target_pairs={{0,8},{8,0},{16,24},{24,16},{1,9},{9,1},{17,25},{25,17},{2,10},{10... | collective-permute-start | bytes 12296 | tf_op jit(solution)/shard_map/ppermute | solution.py:378
  30.7 5.3 %collective-permute-start.13 = (f32[8,128]{1,0:T(8,128)S(1)}, f32[8,128]{1,0:T(8,128)S(1)}, u32[]{:S(2)}, u32[]{:S(2)}) collective-permute-start(f32[8,128]{1,0:T(8,128)S(1)} %shard_map.107.refs_12_.refs_8_), channel_id=1, source_target_pairs={{0,16},{8,24},{16,0},{24,8},{1,17},{9,25},{17,1},{25,9},{2,18},{10... | collective-permute-start | bytes 12296 | tf_op jit(solution)/shard_map/ppermute | solution.py:378
  31.1 5.4 %collective-permute-start.14 = (f32[8,128]{1,0:T(8,128)S(1)}, f32[8,128]{1,0:T(8,128)S(1)}, u32[]{:S(2)}, u32[]{:S(2)}) collective-permute-start(f32[8,128]{1,0:T(8,128)S(1)} %shard_map.107.refs_12_.refs_8_), channel_id=1, source_target_pairs={{0,24},{8,16},{16,8},{24,0},{1,25},{9,17},{17,9},{25,1},{2,26},{10... | collective-permute-start | bytes 12296 | tf_op jit(solution)/shard_map/ppermute | solution.py:378
  38.6 6.7 %collective-permute-start.16 = (bf16[4,256,128]{2,1,0:T(8,128)(2,1)S(1)}, bf16[4,256,128]{2,1,0:T(8,128)(2,1)S(1)}, u32[]{:S(2)}, u32[]{:S(2)}) collective-permute-start(bf16[4,256,128]{2,1,0:T(8,128)(2,1)S(1)} %get-tuple-element.29), channel_id=1, source_target_pairs={{0,2},{1,3},{2,0},{3,1},{4,6},{5,7},{6,4},{7,5},{8,10},{9,11},{10,... | collective-permute-start | bytes 786440 | tf_op jit(solution)/shard_map/ppermute | solution.py:378
  38.7 1.7 %collective-permute-start.15 = (bf16[8,64,128]{2,1,0:T(8,128)(2,1)S(1)}, bf16[8,64,128]{2,1,0:T(8,128)(2,1)S(1)}, u32[]{:S(2)}, u32[]{:S(2)}) collective-permute-start(bf16[8,64,128]{2,1,0:T(8,128)(2,1)S(1)} %get-tuple-element.24), channel_id=1, source_target_pairs={{0,2},{2,0},{1,3},{3,1},{4,6},{6,4},{5,7},{7,5},{8,10},{10,8},{9,1... | collective-permute-start | bytes 393224 | tf_op jit(solution)/shard_map/ppermute | solution.py:378
  41.1 15.7 %all-to-all-start = ((bf16[8,2,64,128]{3,2,1,0:T(8,128)(2,1)}), bf16[8,2,64,128]{3,2,1,0:T(8,128)(2,1)S(1)}, u32[]{:S(2)}, u32[]{:S(2)}) async-start(bf16[8,2,64,128]{3,2,1,0:T(8,128)(2,1)} %pad_maximum_fusion), calls=%async_computation | async-start | bytes 524288 | tf_op jit(solution)/shard_map/all_to_all | solution.py:497
  45.3 8.1 %collective-permute-start.19 = (bf16[2,256,128]{2,1,0:T(8,128)(2,1)S(1)}, bf16[2,256,128]{2,1,0:T(8,128)(2,1)S(1)}, u32[]{:S(2)}, u32[]{:S(2)}) collective-permute-start(bf16[2,256,128]{2,1,0:T(8,128)(2,1)S(1)} %pad_maximum_fusion.9), channel_id=1, source_target_pairs={{0,5},{1,4},{2,7},{3,6},{4,1},{5,0},{6,3},{7,2},{8,13},{9,12},{10,... | collective-permute-start | bytes 393224 | tf_op jit(solution)/shard_map/ppermute | solution.py:378
  47.0 9.8 %collective-permute-start.18 = (bf16[2,256,128]{2,1,0:T(8,128)(2,1)S(1)}, bf16[2,256,128]{2,1,0:T(8,128)(2,1)S(1)}, u32[]{:S(2)}, u32[]{:S(2)}) collective-permute-start(bf16[2,256,128]{2,1,0:T(8,128)(2,1)S(1)} %pad_maximum_fusion.8), channel_id=1, source_target_pairs={{0,4},{1,5},{2,6},{3,7},{4,0},{5,1},{6,2},{7,3},{8,12},{9,13},{10,... | collective-permute-start | bytes 393224 | tf_op jit(solution)/shard_map/ppermute | solution.py:378
  47.5 9.3 %collective-permute-start.17 = (bf16[2,256,128]{2,1,0:T(8,128)(2,1)S(1)}, bf16[2,256,128]{2,1,0:T(8,128)(2,1)S(1)}, u32[]{:S(2)}, u32[]{:S(2)}) collective-permute-start(bf16[2,256,128]{2,1,0:T(8,128)(2,1)S(1)} %pad_maximum_fusion.7), channel_id=1, source_target_pairs={{0,1},{1,0},{2,3},{3,2},{4,5},{5,4},{6,7},{7,6},{8,9},{9,8},{10,11... | collective-permute-start | bytes 393224 | tf_op jit(solution)/shard_map/ppermute | solution.py:378

commit v8 on v7

v8 whole, which is shorter than its diff:
```python
import functools

import jax
import jax.numpy as jnp
from jax import lax
from jax.experimental import pallas as pl
from jax.experimental.pallas import tpu as pltpu
from jax.sharding import Mesh, PartitionSpec as P

DH = 128
KVH = 8
RESP_LEN = 64
SCALE = DH ** (-0.5)
LOG2E = 1.4426950408889634
MASKED_SCORE = -1e30
DEAD_LSE = 1e30
PIECES = 3
STAT_ROWS = 16
STEP_LINES = 1024
PARAMS = pltpu.CompilerParams(vmem_limit_bytes=24 * 1024 * 1024)
ANY = pl.BlockSpec(memory_space=pl.ANY)
HBM = pl.BlockSpec(memory_space=pltpu.HBM)
VMEM = pl.BlockSpec(memory_space=pltpu.VMEM)

FIRST = 2
KEEP = (0, 1, 4, 5)


def split_pieces(x):
    first = x.astype(jnp.bfloat16)
    rest = x - first.astype(jnp.float32)
    second = rest.astype(jnp.bfloat16)
    third = (rest - second.astype(jnp.float32)).astype(jnp.bfloat16)
    return first, second, third


def shift_of(n):
    assert n & (n - 1) == 0
    return n.bit_length() - 1


def column_of(member, groups, heads):
    head_index, group_index = member & (heads - 1), member >> shift_of(heads)
    return pl.multiple_of((head_index * groups + group_index) * DH, DH)


def place(nears, heads):
    row, near = lax.axis_index("row"), lax.axis_index("near")
    member = (row * nears + near) * heads + lax.axis_index("head")
    return member, row, near, lax.axis_index("part")


def group_at(at, row_xor, near_xor, nears):
    return (at[1] ^ row_xor) * nears + (at[2] ^ near_xor)


def pack_kernel(row_count, nears, heads, q_hbm, o_grad_hbm, o_hbm, lse_hbm, k_hbm, v_hbm, *rest):
    slab_refs, (keep_ref, send_ref, o_ref, lse_ref, sems) = rest[:row_count], rest[row_count:]
    at = place(nears, heads)
    groups = row_count * nears
    rows, own_heads = lse_ref.shape
    lines = o_ref.shape[0] // groups
    tokens = k_hbm.shape[0]
    copies = [(lse_hbm, lse_ref), (o_hbm, o_ref)]
    slabs = []
    for j, ref in enumerate(slab_refs):
        for n in range(nears):
            first = pl.multiple_of(group_at(at, j, n, nears) * lines, lines)
            slabs.append((ref, n, first))
            copies.append((o_grad_hbm.at[pl.ds(first, lines), :], ref.at[n, lines : 2 * lines, :]))
    stat_copies = len(copies)
    for ref, n, first in slabs:
        copies.append((q_hbm.at[pl.ds(first, lines), :], ref.at[n, 0:lines, :]))
    for i, j in enumerate(KEEP):
        for ref, peer in ((send_ref, j ^ FIRST), (keep_ref, j)):
            columns = pl.ds(column_of(at[0] ^ peer, groups, heads), DH)
            copies.append((k_hbm.at[:, columns], ref.at[i, 0:tokens, :]))
            copies.append((v_hbm.at[:, columns], ref.at[i, tokens : 2 * tokens, :]))
    copies = [pltpu.make_async_copy(s, t, sems.at[n]) for n, (s, t) in enumerate(copies)]
    for copy in copies:
        copy.start()

    wide = 2 * lines
    shape = (own_heads, wide)
    head_ids = lax.broadcasted_iota(jnp.int32, shape, 0)
    line_heads = (lax.broadcasted_iota(jnp.int32, shape, 1) & (lines - 1)) >> shift_of(rows)
    chosen = jnp.concatenate(
        [(head_ids == line_heads + (first >> shift_of(rows))) for _, _, first in slabs], axis=1
    ).astype(jnp.bfloat16)
    shape = (STAT_ROWS, chosen.shape[1])
    own_row = (lax.broadcasted_iota(jnp.int32, shape, 0) & (rows - 1)) == (
        lax.broadcasted_iota(jnp.int32, shape, 1) & (rows - 1)
    )
    shape = (STAT_ROWS, STAT_ROWS)
    gather = lax.broadcasted_iota(jnp.int32, shape, 0) == (
        lax.broadcasted_iota(jnp.int32, shape, 1) >> shift_of(rows)
    )
    for copy in copies[:stat_copies]:
        copy.wait()
    pieces = [piece.astype(jnp.float32) for piece in split_pieces(lse_ref[...])]
    pieces.append(jnp.zeros((STAT_ROWS - PIECES * rows, own_heads), jnp.float32))
    pieces = jnp.concatenate(pieces, axis=0).astype(jnp.bfloat16)
    spread = jnp.dot(pieces, chosen, preferred_element_type=jnp.float32)
    spread = jnp.where(own_row, spread, 0.0).astype(jnp.bfloat16)
    lse_rows_all = jnp.dot(
        gather.astype(jnp.bfloat16), spread, preferred_element_type=jnp.float32
    )
    kind = lax.broadcasted_iota(jnp.int32, (STAT_ROWS, wide), 0)
    for m, (ref, n, first) in enumerate(slabs):
        o_grad = ref[n, lines:wide, :].astype(jnp.float32)
        product = o_grad * o_ref[pl.ds(first, lines), :].astype(jnp.float32)
        dots = jnp.sum(jnp.concatenate([product, product], axis=0).T, axis=0, keepdims=True)
        stats = lse_rows_all[:, m * wide : (m + 1) * wide]
        for k, piece in enumerate(split_pieces(dots)):
            stats = jnp.where(kind == PIECES + k, piece.astype(jnp.float32), stats)
        ref[n, wide:, :] = stats.astype(jnp.bfloat16)
    for copy in copies[stat_copies:]:
        copy.wait()


def pair_starts(at, i, tokens):
    first = at[3] * KVH
    return [(first + (at[0] ^ KEEP[i] ^ other)) * tokens for other in (0, FIRST)]


def pair_keys(ref, tokens):
    return jnp.concatenate([ref[0, 0:tokens, :], ref[1, 0:tokens, :]], axis=0)


def pair_values(ref, tokens):
    return jnp.concatenate([ref[0, tokens : 2 * tokens, :], ref[1, tokens : 2 * tokens, :]], axis=0)


def all_visible(at, ends, tokens):
    last = (at[3] + 1) * (KVH * tokens)
    return jnp.min(ends.astype(jnp.float32)) >= last.astype(jnp.float32)


def hide(values, ends, at, i, tokens, hidden):
    offset = lax.broadcasted_iota(jnp.int32, (tokens, values.shape[1]), 0)
    starts = pair_starts(at, i, tokens)
    visible = jnp.concatenate([offset < ends - start for start in starts], axis=0)
    return jnp.where(visible, values, hidden)


def in_branches(condition, body):
    pl.when(condition)(functools.partial(body, True))
    pl.when(jnp.logical_not(condition))(functools.partial(body, False))


def lse_rows(size):
    return max(1, size // DH)


def block_slabs(blocks, nears, row_refs):
    out = []
    for at in range(len(blocks)):
        refs = row_refs[at * nears : (at + 1) * nears]
        row_count = refs[0].shape[0] // nears
        out.append([(ref, j, n, j) for n, ref in enumerate(refs) for j in range(row_count)])
    return out


def lines_of(slabs, first, lines):
    return jnp.concatenate([ref[j, first : first + lines, :] for ref, j, _, _ in slabs], axis=0)


def stat_kernel(blocks, first, nears, heads, tokens, ends_ref, *refs):
    at = place(nears, heads)
    row_refs, refs = refs[: len(blocks) * nears], refs[len(blocks) * nears :]
    pair_refs, before_refs, lse_ref = refs[: len(KEEP)], refs[len(KEEP) : -1], refs[-1]
    lines = (row_refs[0].shape[1] - STAT_ROWS) // 2
    for ref in before_refs:
        lse_ref[...] = ref[...]

    def body(seen):
        for m, (b, slabs) in enumerate(zip(blocks, block_slabs(blocks, nears, row_refs))):
            count = len(slabs) * lines
            q = lines_of(slabs, 0, lines)
            ends = ends_ref[:, first + m * count : first + (m + 1) * count]
            scores = []
            for i, ref in enumerate(pair_refs):
                part = lax.dot_general(
                    pair_keys(ref, tokens),
                    q,
                    (((1,), (1,)), ((), ())),
                    preferred_element_type=jnp.float32,
                )
                scores.append(part if seen else hide(part, ends, at, i, tokens, MASKED_SCORE))
            scores = jnp.concatenate(scores, axis=0)
            peak = jnp.max(scores, axis=0, keepdims=True)
            total = jnp.sum(jnp.exp2((scores - peak) * (SCALE * LOG2E)), axis=0, keepdims=True)
            lse = peak * SCALE + jnp.log(total)
            if count < DH:
                lse = jnp.concatenate([lse] * (DH // count), axis=1)
            held = lse_rows(count)
            for k in range(held):
                lse_ref[pl.ds((at[3] ^ b) * held + k, 1), :] = lse[:, k * DH : (k + 1) * DH]

    in_branches(all_visible(at, ends_ref[...], tokens), body)


def line_values(slabs, lines, first_piece):
    low = lax.broadcasted_iota(jnp.int32, (1, 2 * lines), 1) < lines
    out = []
    for n in range(0, len(slabs), 2):
        held = [
            ref[j, 2 * lines : 2 * lines + STAT_ROWS, :].astype(jnp.float32)
            for ref, j, _, _ in slabs[n : n + 2]
        ]
        total = None
        for k in range(first_piece, first_piece + PIECES):
            piece = jnp.where(low, held[0][k : k + 1], held[1][k : k + 1])
            total = piece if total is None else total + piece
        out.append(total)
    return jnp.concatenate(out, axis=1)


def lse_lines(lse_ref, at, blocks, size):
    held = lse_rows(size)
    tiles = []
    for b in blocks:
        for k in range(held):
            tile = lse_ref[pl.ds((at[3] ^ b) * held + k, 1), :]
            tiles.append(tile[:, : min(size, DH)])
    return jnp.concatenate(tiles, axis=1)


def steps_of(blocks, all_slabs, lines):
    size = len(all_slabs[0]) * lines
    step = min(len(blocks), STEP_LINES // size)
    for c in range(0, len(blocks), step):
        slabs = [slab for held in all_slabs[c : c + step] for slab in held]
        yield c * size, step * size, blocks[c : c + step], slabs


def part_kernel(blocks, nears, heads, tokens, ends_ref, *refs):
    at = place(nears, heads)
    row_refs, refs = refs[: len(blocks) * nears], refs[len(blocks) * nears :]
    pair_refs, (lse_ref, prob_ref, dscore_ref, dq_ref) = refs[: len(KEEP)], refs[len(KEEP) :]
    lines = (row_refs[0].shape[1] - STAT_ROWS) // 2
    all_slabs = block_slabs(blocks, nears, row_refs)
    size = len(all_slabs[0]) * lines

    def body(seen):
        for first, count, held, slabs in steps_of(blocks, all_slabs, lines):
            q, o_grad = lines_of(slabs, 0, lines), lines_of(slabs, lines, lines)
            dots = line_values(slabs, lines, PIECES)
            lse = lse_lines(lse_ref, at, held, size) * LOG2E
            lanes = slice(first, first + count)
            dq_t = jnp.zeros((DH, count), jnp.float32)
            for i, ref in enumerate(pair_refs):
                k, v = pair_keys(ref, tokens), pair_values(ref, tokens)
                scores = lax.dot_general(
                    k, q, (((1,), (1,)), ((), ())), preferred_element_type=jnp.float32
                )
                prob = jnp.exp2(scores * (SCALE * LOG2E) - lse)
                if not seen:
                    prob = hide(prob, ends_ref[:, lanes], at, i, tokens, 0.0)
                dprob = lax.dot_general(
                    v, o_grad, (((1,), (1,)), ((), ())), preferred_element_type=jnp.float32
                )
                dscore = (prob * (dprob - dots)).astype(jnp.bfloat16)
                prob_ref[i, :, lanes] = prob.astype(jnp.bfloat16)
                dscore_ref[i, :, lanes] = dscore
                dq_t = dq_t + jnp.dot(k.T, dscore, preferred_element_type=jnp.float32)
            dq_ref[:, lanes] = dq_t

    in_branches(all_visible(at, ends_ref[...], tokens), body)


def weight_kernel(blocks, nears, heads, live_ref, *refs):
    at = place(nears, heads)
    row_refs, refs = refs[: len(blocks) * nears], refs[len(blocks) * nears :]
    lse_refs, (dq_ref, weight_ref, *dq_refs) = refs[: len(blocks)], refs[len(blocks) :]
    lines = (row_refs[0].shape[1] - STAT_ROWS) // 2
    all_slabs = block_slabs(blocks, nears, row_refs)
    size = len(all_slabs[0]) * lines
    for first, count, held, slabs in steps_of(blocks, all_slabs, lines):
        lanes = slice(first, first + count)
        part_lse = [lse_lines(ref, at, held, size) for ref in lse_refs]
        self_lse = line_values(slabs, lines, 0)
        peak = functools.reduce(jnp.maximum, part_lse, self_lse)
        total = sum(jnp.exp(x - peak) for x in part_lse) + jnp.exp(self_lse - peak)
        lse = jnp.where(live_ref[:, lanes] > 0, peak + jnp.log(total), DEAD_LSE)
        weight = jnp.exp(part_lse[0] - lse)
        weight_ref[:, lanes] = weight
        dq = (dq_ref[:, lanes] * (weight * SCALE)).T.astype(jnp.bfloat16)
        sources = [(b, slab) for b in held for slab in all_slabs[blocks.index(b)]]
        for m, (b, (_, _, n, j)) in enumerate(sources):
            dq_refs[n][blocks.index(b), j] = dq[m * lines : (m + 1) * lines]


def token_kernel(blocks, nears, tokens, *refs):
    row_refs, refs = refs[: len(blocks) * nears], refs[len(blocks) * nears :]
    (prob_ref, dscore_ref, weight_ref), refs = refs[:3], refs[3:]
    dkv_refs, (dk_acc, dv_acc) = refs[: len(KEEP)], refs[len(KEEP) :]
    lines = (row_refs[0].shape[1] - STAT_ROWS) // 2
    all_slabs = block_slabs(blocks, nears, row_refs)
    size = len(all_slabs[0]) * lines
    for first, count, held, slabs in steps_of(blocks, all_slabs, lines):
        weight = jnp.broadcast_to(weight_ref[:, first : first + count], (DH, count)).T
        q, o_grad = (
            (lines_of(slabs, start, lines).astype(jnp.float32) * weight).astype(jnp.bfloat16)
            for start in (0, lines)
        )
        for i in range(len(KEEP)):
            dscore, prob = dscore_ref[i, :, first : first + count], prob_ref[i, :, first : first + count]
            dk = jnp.dot(dscore, q, preferred_element_type=jnp.float32) * SCALE
            dv = jnp.dot(prob, o_grad, preferred_element_type=jnp.float32)
            if first > 0:
                dk = dk + dk_acc[i]
                dv = dv + dv_acc[i]
            if first + count < len(blocks) * size:
                dk_acc[i] = dk
                dv_acc[i] = dv
            else:
                for n in range(2):
                    inner = slice(n * tokens, (n + 1) * tokens)
                    dkv_refs[i][n, 0:tokens, :] = dk[inner].astype(jnp.bfloat16)
                    dkv_refs[i][n, tokens : 2 * tokens, :] = dv[inner].astype(jnp.bfloat16)


def add_query_kernel(nears, *refs):
    own_refs, came_refs, out_refs = refs[:nears], refs[nears:-2], refs[-2:]
    for n in range(nears):
        for j in range(own_refs[0].shape[1]):
            total = own_refs[n][0, j].astype(jnp.float32)
            for ref in came_refs:
                total = total + ref[n, j].astype(jnp.float32)
            out_refs[min(j, 1)][n] = total.astype(jnp.bfloat16)


def tie_kernel(*refs):
    pass


def write_kernel(nears, heads, *refs):
    at = place(nears, heads)
    slab_refs, refs = refs[: -len(KEEP) - 5], refs[-len(KEEP) - 5 :]
    pair_refs, (came_ref, out_q_ref, out_k_ref, out_v_ref, sems) = refs[: len(KEEP)], refs[len(KEEP) :]
    groups, lines, tokens = len(slab_refs) * nears, slab_refs[0].shape[1], out_k_ref.shape[0]
    copies = []
    for i, ref in enumerate(pair_refs):
        for source, other in ((ref.at[0], 0), (came_ref.at[i], FIRST)):
            columns = pl.ds(column_of(at[0] ^ KEEP[i] ^ other, groups, heads), DH)
            copies.append((source.at[0:tokens, :], out_k_ref.at[:, columns]))
            copies.append((source.at[tokens : 2 * tokens, :], out_v_ref.at[:, columns]))
    for j, ref in enumerate(slab_refs):
        for n in range(nears):
            first = pl.multiple_of(group_at(at, j, n, nears) * lines, lines)
            copies.append((ref.at[n], out_q_ref.at[pl.ds(first, lines), :]))
    copies = [pltpu.make_async_copy(s, t, sems.at[n]) for n, (s, t) in enumerate(copies)]
    for copy in copies:
        copy.start()
    for copy in copies:
        copy.wait()


def swap(x, axis, distance, size):
    return lax.ppermute(x, axis, [(i, i ^ distance) for i in range(size)])


def swap_pairs(keep, send):
    members = ("row", "near", "head")
    came = swap(send, members, FIRST, KVH)
    pairs = [jnp.stack([keep[i], came[i]]) for i in range(len(KEEP))]
    return [swap(x, members, j, KVH) if j else x for x, j in zip(pairs, KEEP)]


def tie(x, others):
    return pl.pallas_call(
        tie_kernel,
        in_specs=[ANY] * (1 + len(others)),
        out_specs=ANY,
        out_shape=jax.ShapeDtypeStruct(x.shape, x.dtype),
        input_output_aliases={0: 0},
        compiler_params=PARAMS,
    )(x, *others)


def swap_back(pairs, after):
    members = ("row", "near", "head")
    pairs = [pairs[0]] + [
        tie(swap(x, members, j, KVH), after) for x, j in zip(pairs[1:], KEEP[1:])
    ]
    return [*pairs, swap(jnp.stack([x[1] for x in pairs]), members, FIRST, KVH)]


def line_limits(parts, row_count, nears, rows, lines, resp_len, prompt_end):
    line = lax.broadcasted_iota(jnp.int32, (1, parts * nears * row_count * lines), 1)
    slab = line >> shift_of(lines)
    row_xor = slab & (row_count - 1)
    near_xor = (slab >> shift_of(row_count)) & (nears - 1)
    place_of_block = slab >> shift_of(row_count * nears)
    block, bits = jnp.zeros_like(line), shift_of(parts)
    for k in range(bits):
        block = block | (((place_of_block >> k) & 1) << (bits - 1 - k))
    device = (lax.axis_index("part") ^ block) * row_count + (lax.axis_index("row") ^ row_xor)
    device = device * nears + (lax.axis_index("near") ^ near_xor)
    row = device * rows + (line & (rows - 1))
    ends, lengths = jnp.zeros_like(row), jnp.zeros_like(row)
    for r in range(resp_len.shape[0]):
        own = row >> shift_of(RESP_LEN) == r
        ends, lengths = jnp.where(own, prompt_end[r], ends), jnp.where(own, resp_len[r], lengths)
    return ends, ((row & (RESP_LEN - 1)) < lengths).astype(jnp.int32)


def shards(parts, row_count, nears, heads, queries, grad_out, outputs, lse_self, keys, values, resp_len, prompt_end):
    rows = queries.shape[0]
    own_heads = queries.shape[1] // DH
    own_lines = rows * own_heads
    groups = row_count * nears
    lines = own_lines // groups
    tokens = keys.shape[0]
    assert 2 * lines == DH and RESP_LEN % (groups * rows) == 0 and row_count <= 2 and nears <= 2

    def as_lines(x):
        return x.reshape(rows, own_heads, DH).transpose(1, 0, 2).reshape(own_lines, DH)

    def in_hbm(x):
        return pltpu.with_memory_space_constraint(x, pltpu.HBM)

    half_shape = jax.ShapeDtypeStruct((len(KEEP), 2 * tokens, DH), jnp.bfloat16)
    slab_shape = jax.ShapeDtypeStruct((nears, 2 * lines + STAT_ROWS, DH), jnp.bfloat16)
    *slabs, kv_keep, kv_send = pl.pallas_call(
        functools.partial(pack_kernel, row_count, nears, heads),
        in_specs=[HBM] * 6,
        out_specs=[VMEM] * (row_count + 2),
        out_shape=[slab_shape] * row_count + [half_shape] * 2,
        scratch_shapes=[
            pltpu.VMEM((own_lines, DH), jnp.bfloat16),
            pltpu.VMEM(lse_self.shape, jnp.float32),
            pltpu.SemaphoreType.DMA((2 + 2 * groups + 4 * len(KEEP),)),
        ],
        compiler_params=PARAMS,
    )(
        in_hbm(as_lines(queries)),
        in_hbm(as_lines(grad_out)),
        in_hbm(as_lines(outputs)),
        in_hbm(lse_self),
        in_hbm(keys),
        in_hbm(values),
    )
    slabs = [swap(x, "row", j, row_count) if j else x for j, x in enumerate(slabs)]
    own_block = jnp.stack([x[n] for n in range(nears) for x in slabs])
    pairs = swap_pairs(kv_keep, kv_send)
    far = [1 << n for n in reversed(range(shift_of(parts)))]

    def row_refs_of(x):
        return [x, swap(x[row_count:], "near", 1, nears)] if nears > 1 else [x]

    blocks, came = [0], [own_block]
    row_refs = row_refs_of(tie(own_block, pairs[1:2]))
    for d in far:
        if d == 1:
            came = came[:1] + [tie(x, pairs[1:] + row_refs[1:]) for x in came[1:]]
        came = came + [swap(x, "part", d, parts) for x in came]
        blocks = blocks + [b ^ d for b in blocks]
    ends, live = line_limits(parts, row_count, nears, rows, lines, resp_len, prompt_end)

    def part_lse(held, first, refs, before):
        return pl.pallas_call(
            functools.partial(stat_kernel, held, first, nears, heads, tokens),
            in_specs=[VMEM] * (1 + len(refs) + len(KEEP) + len(before)),
            out_shape=jax.ShapeDtypeStruct((parts * lse_rows(groups * lines), DH), jnp.float32),
            compiler_params=PARAMS,
        )(ends, *refs, *pairs, *before)

    row_refs = row_refs + [ref for x in came[1:-1] for ref in row_refs_of(x)]
    lse = [part_lse(blocks[:-1], 0, row_refs, [])]
    last_refs = row_refs_of(tie(came[-1], lse))
    lse = [part_lse(blocks[-1:], (parts - 1) * groups * lines, last_refs, lse)]
    row_refs = row_refs + last_refs
    every_lse = lse + [swap(lse[0], "part", d, parts) for d in range(1, parts)]

    all_lines = parts * groups * lines
    score_shape = jax.ShapeDtypeStruct((len(KEEP), 2 * tokens, all_lines), jnp.bfloat16)
    prob, dscore, dq = pl.pallas_call(
        functools.partial(part_kernel, blocks, nears, heads, tokens),
        in_specs=[VMEM] * (1 + len(row_refs) + len(KEEP) + 1),
        out_specs=[VMEM] * 3,
        out_shape=[score_shape] * 2 + [jax.ShapeDtypeStruct((DH, all_lines), jnp.float32)],
        compiler_params=PARAMS,
    )(ends, *row_refs, *pairs, *lse)
    dq_shape = jax.ShapeDtypeStruct((parts, row_count, lines, DH), jnp.bfloat16)
    weight, *dq = pl.pallas_call(
        functools.partial(weight_kernel, blocks, nears, heads),
        in_specs=[VMEM] * (1 + len(row_refs) + parts + 1),
        out_shape=[jax.ShapeDtypeStruct((1, all_lines), jnp.float32)] + [dq_shape] * nears,
        compiler_params=PARAMS,
    )(live, *row_refs, *every_lse, dq)
    dq = [swap(x, "near", n, nears) if n else x for n, x in enumerate(dq)]
    acc = pltpu.VMEM((len(KEEP), 2 * tokens, DH), jnp.float32)
    dkv = pl.pallas_call(
        functools.partial(token_kernel, blocks, nears, tokens),
        in_specs=[VMEM] * (len(row_refs) + 3),
        out_shape=[jax.ShapeDtypeStruct((2, 2 * tokens, DH), jnp.bfloat16)] * len(KEEP),
        scratch_shapes=[acc] * 2,
        compiler_params=PARAMS,
    )(*row_refs, prob, dscore, weight)
    from_parts = [
        swap(jnp.stack([x[at] for x in dq]), "part", b, parts) for at, b in enumerate(blocks) if b
    ]
    sum_shape = jax.ShapeDtypeStruct((nears, lines, DH), jnp.bfloat16)
    sums = pl.pallas_call(
        functools.partial(add_query_kernel, nears),
        in_specs=[VMEM] * (nears + len(from_parts)),
        out_shape=[sum_shape] * 2,
        compiler_params=PARAMS,
    )(*dq, *from_parts)
    pairs = swap_back(dkv, sums[:1])
    sums = [swap(x, "row", j, row_count) if j else x for j, x in enumerate(sums[:row_count])]
    out_q, out_k, out_v = pl.pallas_call(
        functools.partial(write_kernel, nears, heads),
        in_specs=[VMEM] * (row_count + len(pairs)),
        out_specs=[HBM] * 3,
        out_shape=[
            jax.ShapeDtypeStruct((own_lines, DH), jnp.bfloat16),
            jax.ShapeDtypeStruct(keys.shape, jnp.bfloat16),
            jax.ShapeDtypeStruct(values.shape, jnp.bfloat16),
        ],
        scratch_shapes=[pltpu.SemaphoreType.DMA((4 * len(KEEP) + groups,))],
        compiler_params=PARAMS,
    )(*sums, *pairs)
    out_q = out_q.reshape(own_heads, rows, DH).transpose(1, 0, 2).reshape(rows, own_heads * DH)
    return out_q, out_k, out_v


def solution(mesh):
    ctx, heads = mesh.shape["ctx"], mesh.shape["head"]
    groups = KVH // heads
    parts = ctx // groups
    nears = min(2, groups)
    row_count = groups // nears
    fine = Mesh(
        mesh.devices.reshape(parts, row_count, nears, heads), ("part", "row", "near", "head")
    )
    rows = P(("part", "row", "near"), "head")
    tokens = P(("part", "row", "near", "head"), None)
    return jax.shard_map(
        functools.partial(shards, parts, row_count, nears, heads),
        mesh=fine,
        in_specs=(rows, rows, rows, rows, tokens, tokens, P(), P()),
        out_specs=(rows, tokens, tokens),
        check_vma=False,
    )
```

time: 58.7 us -> 58.5 us (level)
  waiting for transfers between devices: 16.5 us -> 23.8 us
  Pallas kernels: 11.7 us -> 7.79 us
  starting transfers between devices: 26.9 us -> 24.2 us
  other arithmetic: 0.95 us -> 0.22 us
    ppermute x20 -> x24, waiting for transfers between devices: 16.5 us -> 23.8 us  [swap(): return lax.ppermute(x, axis, [(i, i ^ distance) for i in range(size)])]
    all_to_all x1 -> x0, starting transfers between devices: 4.19 us -> none  [shards(): lax.all_to_all(jnp.stack(dq, axis=1), ('part', 'row'), split_axis=0, conc...]
    pallas_call x7 -> x12, Pallas kernels: 8.4 us -> 5.03 us  [the longest x1 2.03 us: shards(): pl.pallas_call(functools.partial(part_kernel, blocks, nears, heads, token...]
    ppermute x20 -> x24, starting transfers between devices: 22.7 us -> 24.2 us  [swap(): return lax.ppermute(x, axis, [(i, i ^ distance) for i in range(size)])]
    another operation x2 -> x4, other arithmetic: 0.81 us -> 0.06 us  [the longest x1 0.04 us: swap_back(): return [*pairs, swap(jnp.stack([x[1] for x in pairs]), members, FIRST, KVH)]]
  transfers between devices with their start and end apart: 21 -> 24, of which waited for: 12 -> 15; matrix products, arithmetic and copies ran while one was open for 2% -> 0% of each run, Pallas kernels for 8% -> 5%
where the time goes in v8:
time: 58.5 us; the launch traced here: 58.3 us
  starting transfers between devices  24.2 us (41%)
  waiting for transfers between devices  23.8 us (41%)
  Pallas kernels  7.79 us (13%)
  between operations  2.21 us (4%)
    ppermute x24, starting transfers between devices, swap(): return lax.ppermute(x, axis, [(i, i ^ distance) for i in range(size)])  24.2 us
    ppermute x24, waiting for transfers between devices, swap(): return lax.ppermute(x, axis, [(i, i ^ distance) for i in range(size)])  23.8 us
    pallas_call x1, Pallas kernels, shards(): pl.pallas_call(functools.partial(part_kernel, blocks, nears, heads, token...  2.03 us
    pallas_call x2, Pallas kernels, part_lse(): pl.pallas_call(functools.partial(stat_kernel, held, first, nears, heads,...  1.77 us
    pallas_call x1, Pallas kernels, shards(): pl.pallas_call(functools.partial(token_kernel, blocks, nears, tokens), in...  1.39 us
    pallas_call x1, Pallas kernels, shards(): pl.pallas_call(functools.partial(pack_kernel, row_count, nears, heads), i...  1.37 us
  transfers between devices with their start and end apart: 24, of which 15 were waited for; matrix products, arithmetic and copies ran while one was open for 0% of the time, Pallas kernels for 5%

profile of v8, /device:TPU:0, one launch (start us, length us, event | category | flops | bytes accessed | tf_op | source)
XLA Modules:
  0.0 58.3 jit_solution(7232798285718554753)
XLA Ops:
  0.6 1.4 %shard_map.103 = (bf16[2,144,128]{2,1,0:T(8,128)(2,1)S(1)}, bf16[2,144,128]{2,1,0:T(8,128)(2,1)S(1)}, bf16[4,256,128]{2,1,0:T(8,128)(2,1)S(1)}, bf16[4,256,128]{2,1,0:T(8,128)(2,1)S(1)}) custom-call(bf16[256,128]{1,0:T(8,128)(2,1)} %bitcast.24, bf16[256,128]{1,0:T(8,128)(2,1)} %bitcast.25, bf16[256,128]{1,0:T(8,128)(2,1)} %bitcast.26, f32[4,64]{1,0:T(4,128)} %lse_hbm.1, ...), custom_call_target="tpu_custom_call" | custom-call | tf_op jit(solution)/shard_map/pallas_call | solution.py:426
  2.0 3.0 %collective-permute-start = (bf16[2,144,128]{2,1,0:T(8,128)(2,1)S(1)}, bf16[2,144,128]{2,1,0:T(8,128)(2,1)S(1)}, u32[]{:S(2)}, u32[]{:S(2)}) collective-permute-start(bf16[2,144,128]{2,1,0:T(8,128)(2,1)S(1)} %get-tuple-element.23), channel_id=1, source_target_pairs={{0,4},{4,0},{1,5},{5,1},{2,6},{6,2},{3,7},{7,3},{8,12},{12,8},{9,1... | collective-permute-start | bytes 221192 | tf_op jit(solution)/shard_map/ppermute | solution.py:361
  5.0 0.0 collective-permute-start.1
  5.1 2.3 %collective-permute-done = bf16[2,144,128]{2,1,0:T(8,128)(2,1)S(1)} collective-permute-done((bf16[2,144,128]{2,1,0:T(8,128)(2,1)S(1)}, bf16[2,144,128]{2,1,0:T(8,128)(2,1)S(1)}, u32[]{:S(2)}, u32[]{:S(2)}) %collective-permute-start) | collective-permute-done | bytes 73760 | tf_op jit(solution)/shard_map/ppermute | solution.py:361
  7.4 2.1 %collective-permute-start.8 = (bf16[4,144,128]{2,1,0:T(8,128)(2,1)S(1)}, bf16[4,144,128]{2,1,0:T(8,128)(2,1)S(1)}, u32[]{:S(2)}, u32[]{:S(2)}) collective-permute-start(bf16[4,144,128]{2,1,0:T(8,128)(2,1)S(1)} %pad_maximum_fusion.1.refs_0_), channel_id=1, source_target_pairs={{0,8},{8,0},{16,24},{24,16},{1,9},{9,1},{17,25},{25,17},{2,10},{10... | collective-permute-start | bytes 442376 | tf_op jit(solution)/shard_map/ppermute | solution.py:361
  9.6 2.6 %collective-permute-start.4 = (bf16[4,144,128]{2,1,0:T(8,128)(2,1)S(1)}, bf16[4,144,128]{2,1,0:T(8,128)(2,1)S(1)}, u32[]{:S(2)}, u32[]{:S(2)}) collective-permute-start(bf16[4,144,128]{2,1,0:T(8,128)(2,1)S(1)} %pad_maximum_fusion.1.refs_0_), channel_id=1, source_target_pairs={{0,16},{8,24},{16,0},{24,8},{1,17},{9,25},{17,1},{25,9},{2,18},{10... | collective-permute-start | bytes 442376 | tf_op jit(solution)/shard_map/ppermute | solution.py:361
  12.1 0.0 collective-permute-done.1
  12.2 1.6 %collective-permute-start.2 = (bf16[2,256,128]{2,1,0:T(8,128)(2,1)S(1)}, bf16[2,256,128]{2,1,0:T(8,128)(2,1)S(1)}, u32[]{:S(2)}, u32[]{:S(2)}) collective-permute-start(bf16[2,256,128]{2,1,0:T(8,128)(2,1)S(1)} %pad_maximum_fusion.2), channel_id=1, source_target_pairs={{0,1},{1,0},{2,3},{3,2},{4,5},{5,4},{6,7},{7,6},{8,9},{9,8},{10,11... | collective-permute-start | bytes 393224 | tf_op jit(solution)/shard_map/ppermute | solution.py:361
  13.8 1.6 %collective-permute-start.5 = (bf16[2,256,128]{2,1,0:T(8,128)(2,1)S(1)}, bf16[2,256,128]{2,1,0:T(8,128)(2,1)S(1)}, u32[]{:S(2)}, u32[]{:S(2)}) collective-permute-start(bf16[2,256,128]{2,1,0:T(8,128)(2,1)S(1)} %pad_maximum_fusion.3), channel_id=1, source_target_pairs={{0,4},{1,5},{2,6},{3,7},{4,0},{5,1},{6,2},{7,3},{8,12},{9,13},{10,... | collective-permute-start | bytes 393224 | tf_op jit(solution)/shard_map/ppermute | solution.py:361
  15.4 0.5 collective-permute-start.6
  15.9 1.9 %collective-permute-done.4.refs_0_ = bf16[4,144,128]{2,1,0:T(8,128)(2,1)S(1)} collective-permute-done((bf16[4,144,128]{2,1,0:T(8,128)(2,1)S(1)}, bf16[4,144,128]{2,1,0:T(8,128)(2,1)S(1)}, u32[]{:S(2)}, u32[]{:S(2)}) %collective-permute-start.4) | collective-permute-done | bytes 147488 | tf_op jit(solution)/shard_map/ppermute | solution.py:361
  17.8 0.5 collective-permute-done.2.refs_1_.refs_7_.refs_3_.refs_9_
  18.4 0.1 collective-permute-start.3
  19.1 0.5 collective-permute-done.5.refs_2_.refs_8_.refs_4_.refs_10_
  19.6 1.7 %collective-permute-done.6.refs_3_.refs_9_.refs_5_.refs_11_ = bf16[2,256,128]{2,1,0:T(8,128)(2,1)S(1)} collective-permute-done((bf16[2,256,128]{2,1,0:T(8,128)(2,1)S(1)}, bf16[2,256,128]{2,1,0:T(8,128)(2,1)S(1)}, u32[]{:S(2)}, u32[]{:S(2)}) %collective-permute-start.6) | collective-permute-done | bytes 131104 | tf_op jit(solution)/shard_map/ppermute | solution.py:361
  21.3 0.0 collective-permute-done.3.refs_4_.refs_1_
  21.3 0.5 collective-permute-start.10
  21.8 0.1 collective-permute-start.9
  21.9 0.5 collective-permute-start.7
  22.4 0.7 %collective-permute-done.9.refs_5_ = bf16[2,144,128]{2,1,0:T(8,128)(2,1)S(1)} collective-permute-done((bf16[2,144,128]{2,1,0:T(8,128)(2,1)S(1)}, bf16[2,144,128]{2,1,0:T(8,128)(2,1)S(1)}, u32[]{:S(2)}, u32[]{:S(2)}) %collective-permute-start.9) | collective-permute-done | bytes 73760 | tf_op jit(solution)/shard_map/ppermute | solution.py:361
  23.1 0.2 collective-permute-done.7.refs_3_
  23.3 1.1 %shard_map.106.refs_1_.refs_6_ = f32[8,128]{1,0:T(8,128)S(1)} custom-call(s32[1,1024]{1,0:T(1,128)S(1)} %compare_select_fusion.ends_ref, bf16[4,144,128]{2,1,0:T(8,128)(2,1)S(1)} %shard_map.104.refs_0_, bf16[2,144,128]{2,1,0:T(8,128)(2,1)S(1)} %collective-permute-done.3.refs_4_.refs_1_, bf16[4,144,128]{2,1,0:T(8,128)(2,1)S(1)} %shard_map.105.refs_2_, ...), custom_call_target="tpu_custom_call" | custom-call | tf_op jit(solution)/shard_map/pallas_call | solution.py:463
  24.4 2.0 %collective-permute-done.10.refs_0_ = bf16[4,144,128]{2,1,0:T(8,128)(2,1)S(1)} collective-permute-done((bf16[4,144,128]{2,1,0:T(8,128)(2,1)S(1)}, bf16[4,144,128]{2,1,0:T(8,128)(2,1)S(1)}, u32[]{:S(2)}, u32[]{:S(2)}) %collective-permute-start.10) | collective-permute-done | bytes 147488 | tf_op jit(solution)/shard_map/ppermute | solution.py:361
  26.5 0.1 collective-permute-start.11
  27.2 0.6 %collective-permute-done.11.refs_1_.refs_7_ = bf16[2,144,128]{2,1,0:T(8,128)(2,1)S(1)} collective-permute-done((bf16[2,144,128]{2,1,0:T(8,128)(2,1)S(1)}, bf16[2,144,128]{2,1,0:T(8,128)(2,1)S(1)}, u32[]{:S(2)}, u32[]{:S(2)}) %collective-permute-start.11) | collective-permute-done | bytes 73760 | tf_op jit(solution)/shard_map/ppermute | solution.py:361
  27.8 0.6 %shard_map.108.refs_12_.refs_8_ = f32[8,128]{1,0:T(8,128)S(1)} custom-call(s32[1,1024]{1,0:T(1,128)S(1)} %compare_select_fusion.ends_ref, bf16[4,144,128]{2,1,0:T(8,128)(2,1)S(1)} %shard_map.107.refs_0_.refs_6_, bf16[2,144,128]{2,1,0:T(8,128)(2,1)S(1)} %collective-permute-done.11.refs_1_.refs_7_, ...), custom_call_target="tpu_custom_call" | custom-call | tf_op jit(solution)/shard_map/pallas_call | solution.py:463
  28.4 0.5 collective-permute-start.12
  28.9 1.4 %collective-permute-start.13 = (f32[8,128]{1,0:T(8,128)S(1)}, f32[8,128]{1,0:T(8,128)S(1)}, u32[]{:S(2)}, u32[]{:S(2)}) collective-permute-start(f32[8,128]{1,0:T(8,128)S(1)} %shard_map.108.refs_12_.refs_8_), channel_id=1, source_target_pairs={{0,16},{8,24},{16,0},{24,8},{1,17},{9,25},{17,1},{25,9},{2,18},{10... | collective-permute-start | bytes 12296 | tf_op jit(solution)/shard_map/ppermute | solution.py:361
  30.3 2.6 %collective-permute-start.14 = (f32[8,128]{1,0:T(8,128)S(1)}, f32[8,128]{1,0:T(8,128)S(1)}, u32[]{:S(2)}, u32[]{:S(2)}) collective-permute-start(f32[8,128]{1,0:T(8,128)S(1)} %shard_map.108.refs_12_.refs_8_), channel_id=1, source_target_pairs={{0,24},{8,16},{16,8},{24,0},{1,25},{9,17},{17,9},{25,1},{2,26},{10... | collective-permute-start | bytes 12296 | tf_op jit(solution)/shard_map/ppermute | solution.py:361
  32.9 2.0 %shard_map.109 = (bf16[4,256,1024]{2,1,0:T(8,128)(2,1)S(1)}, bf16[4,256,1024]{2,1,0:T(8,128)(2,1)S(1)}, f32[128,1024]{1,0:T(8,128)S(1)}) custom-call(s32[1,1024]{1,0:T(1,128)S(1)} %compare_select_fusion.ends_ref, bf16[4,144,128]{2,1,0:T(8,128)(2,1)S(1)} %shard_map.104.refs_0_, bf16[2,144,128]{2,1,0:T(8,128)(2,1)S(1)} %collective-permute-done.3.refs_4_.refs_1_, ...), custom_call_target="tpu_custom_call" | custom-call | tf_op jit(solution)/shard_map/pallas_call | solution.py:479
  35.0 0.0 collective-permute-done.13.refs_10_
  35.0 0.7 %collective-permute-done.14.refs_11_ = f32[8,128]{1,0:T(8,128)S(1)} collective-permute-done((f32[8,128]{1,0:T(8,128)S(1)}, f32[8,128]{1,0:T(8,128)S(1)}, u32[]{:S(2)}, u32[]{:S(2)}) %collective-permute-start.14) | collective-permute-done | bytes 4128 | tf_op jit(solution)/shard_map/ppermute | solution.py:361
  35.7 0.2 shard_map.110
  35.9 1.4 %shard_map.112 = (bf16[2,256,128]{2,1,0:T(8,128)(2,1)S(1)}, bf16[2,256,128]{2,1,0:T(8,128)(2,1)S(1)}, bf16[2,256,128]{2,1,0:T(8,128)(2,1)S(1)}, bf16[2,256,128]{2,1,0:T(8,128)(2,1)S(1)}) custom-call(bf16[4,144,128]{2,1,0:T(8,128)(2,1)S(1)} %shard_map.104.refs_0_, bf16[2,144,128]{2,1,0:T(8,128)(2,1)S(1)} %collective-permute-done.3.refs_4_.refs_1_, ...), custom_call_target="tpu_custom_call" | custom-call | tf_op jit(solution)/shard_map/pallas_call | solution.py:495
  37.3 2.5 %collective-permute-start.22 = (bf16[2,256,128]{2,1,0:T(8,128)(2,1)S(1)}, bf16[2,256,128]{2,1,0:T(8,128)(2,1)S(1)}, u32[]{:S(2)}, u32[]{:S(2)}) collective-permute-start(bf16[2,256,128]{2,1,0:T(8,128)(2,1)S(1)} %get-tuple-element.37), channel_id=1, source_target_pairs={{0,5},{1,4},{2,7},{3,6},{4,1},{5,0},{6,3},{7,2},{8,13},{9,12},{10,... | collective-permute-start | bytes 393224 | tf_op jit(solution)/shard_map/ppermute | solution.py:361
  39.8 0.0 collective-permute-start.15
  39.8 0.5 collective-permute-start.21
  40.4 0.5 collective-permute-start.20
  40.9 0.3 collective-permute-done.15.refs_1_
  41.2 2.3 %collective-permute-start.18 = (bf16[2,2,64,128]{3,2,1,0:T(8,128)(2,1)S(1)}, bf16[2,2,64,128]{3,2,1,0:T(8,128)(2,1)S(1)}, u32[]{:S(2)}, u32[]{:S(2)}) collective-permute-start(bf16[2,2,64,128]{3,2,1,0:T(8,128)(2,1)S(1)} %pad_maximum_fusion.8), channel_id=1, source_target_pairs={{0,24},{8,16},{16,8},{24,0},{1,25},{9,17},{17,9},{25,1},{2,26},{10... | collective-permute-start | bytes 196616 | tf_op jit(solution)/shard_map/ppermute | solution.py:361
  43.6 0.1 collective-permute-start.17
  43.7 4.3 %collective-permute-done.18.refs_4_ = bf16[2,2,64,128]{3,2,1,0:T(8,128)(2,1)S(1)} collective-permute-done((bf16[2,2,64,128]{3,2,1,0:T(8,128)(2,1)S(1)}, bf16[2,2,64,128]{3,2,1,0:T(8,128)(2,1)S(1)}, u32[]{:S(2)}, u32[]{:S(2)}) %collective-permute-start.18) | collective-permute-done | bytes 65568 | tf_op jit(solution)/shard_map/ppermute | solution.py:361
  47.9 0.7 %collective-permute-done.17.refs_3_ = bf16[2,2,64,128]{3,2,1,0:T(8,128)(2,1)S(1)} collective-permute-done((bf16[2,2,64,128]{3,2,1,0:T(8,128)(2,1)S(1)}, bf16[2,2,64,128]{3,2,1,0:T(8,128)(2,1)S(1)}, u32[]{:S(2)}, u32[]{:S(2)}) %collective-permute-start.17) | collective-permute-done | bytes 65568 | tf_op jit(solution)/shard_map/ppermute | solution.py:361
  48.6 4.5 %collective-permute-done.16.refs_2_ = bf16[2,2,64,128]{3,2,1,0:T(8,128)(2,1)S(1)} collective-permute-done((bf16[2,2,64,128]{3,2,1,0:T(8,128)(2,1)S(1)}, bf16[2,2,64,128]{3,2,1,0:T(8,128)(2,1)S(1)}, u32[]{:S(2)}, u32[]{:S(2)}) %collective-permute-start.16) | collective-permute-done | bytes 65568 | tf_op jit(solution)/shard_map/ppermute | solution.py:361
  53.3 0.1 collective-permute-start.23
  53.4 1.1 %collective-permute-start.19 = (bf16[2,64,128]{2,1,0:T(8,128)(2,1)S(1)}, bf16[2,64,128]{2,1,0:T(8,128)(2,1)S(1)}, u32[]{:S(2)}, u32[]{:S(2)}) collective-permute-start(bf16[2,64,128]{2,1,0:T(8,128)(2,1)S(1)} %get-tuple-element.30), channel_id=1, source_target_pairs={{0,4},{4,0},{1,5},{5,1},{2,6},{6,2},{3,7},{7,3},{8,12},{12,8},{9,1... | collective-permute-start | bytes 98312 | tf_op jit(solution)/shard_map/ppermute | solution.py:361
  54.5 2.8 %collective-permute-done.19.refs_1_ = bf16[2,64,128]{2,1,0:T(8,128)(2,1)S(1)} collective-permute-done((bf16[2,64,128]{2,1,0:T(8,128)(2,1)S(1)}, bf16[2,64,128]{2,1,0:T(8,128)(2,1)S(1)}, u32[]{:S(2)}, u32[]{:S(2)}) %collective-permute-start.19) | collective-permute-done | bytes 32800 | tf_op jit(solution)/shard_map/ppermute | solution.py:361
  57.3 1.0 %shard_map.116 = (bf16[256,128]{1,0:T(8,128)(2,1)}, bf16[128,1024]{1,0:T(8,128)(2,1)}, bf16[128,1024]{1,0:T(8,128)(2,1)}) custom-call(bf16[2,64,128]{2,1,0:T(8,128)(2,1)S(1)} %get-tuple-element.29.refs_1_.refs_0_, bf16[2,64,128]{2,1,0:T(8,128)(2,1)S(1)} %collective-permute-done.19.refs_1_, bf16[2,256,128]{2,1,0:T(8,128)(2,1)S(1)} %get-tuple-element.34.refs_2_, ...), custom_call_target="tpu_custom_call" | custom-call | tf_op jit(solution)/shard_map/pallas_call | solution.py:514
  (39 shorter events, 0.4 us)
Async XLA Ops:
  2.0 5.4 %collective-permute-start = (bf16[2,144,128]{2,1,0:T(8,128)(2,1)S(1)}, bf16[2,144,128]{2,1,0:T(8,128)(2,1)S(1)}, u32[]{:S(2)}, u32[]{:S(2)}) collective-permute-start(bf16[2,144,128]{2,1,0:T(8,128)(2,1)S(1)} %get-tuple-element.23), channel_id=1, source_target_pairs={{0,4},{4,0},{1,5},{5,1},{2,6},{6,2},{3,7},{7,3},{8,12},{12,8},{9,1... | collective-permute-start | bytes 221192 | tf_op jit(solution)/shard_map/ppermute | solution.py:361
  5.0 7.1 %collective-permute-start.1 = (bf16[4,256,128]{2,1,0:T(8,128)(2,1)S(1)}, bf16[4,256,128]{2,1,0:T(8,128)(2,1)S(1)}, u32[]{:S(2)}, u32[]{:S(2)}) collective-permute-start(bf16[4,256,128]{2,1,0:T(8,128)(2,1)S(1)} %get-tuple-element.25), channel_id=1, source_target_pairs={{0,2},{1,3},{2,0},{3,1},{4,6},{5,7},{6,4},{7,5},{8,10},{9,11},{10,... | collective-permute-start | bytes 786440 | tf_op jit(solution)/shard_map/ppermute | solution.py:361
  7.4 8.5 %collective-permute-start.8 = (bf16[4,144,128]{2,1,0:T(8,128)(2,1)S(1)}, bf16[4,144,128]{2,1,0:T(8,128)(2,1)S(1)}, u32[]{:S(2)}, u32[]{:S(2)}) collective-permute-start(bf16[4,144,128]{2,1,0:T(8,128)(2,1)S(1)} %pad_maximum_fusion.1.refs_0_), channel_id=1, source_target_pairs={{0,8},{8,0},{16,24},{24,16},{1,9},{9,1},{17,25},{25,17},{2,10},{10... | collective-permute-start | bytes 442376 | tf_op jit(solution)/shard_map/ppermute | solution.py:361
  9.6 8.3 %collective-permute-start.4 = (bf16[4,144,128]{2,1,0:T(8,128)(2,1)S(1)}, bf16[4,144,128]{2,1,0:T(8,128)(2,1)S(1)}, u32[]{:S(2)}, u32[]{:S(2)}) collective-permute-start(bf16[4,144,128]{2,1,0:T(8,128)(2,1)S(1)} %pad_maximum_fusion.1.refs_0_), channel_id=1, source_target_pairs={{0,16},{8,24},{16,0},{24,8},{1,17},{9,25},{17,1},{25,9},{2,18},{10... | collective-permute-start | bytes 442376 | tf_op jit(solution)/shard_map/ppermute | solution.py:361
  12.2 6.2 %collective-permute-start.2 = (bf16[2,256,128]{2,1,0:T(8,128)(2,1)S(1)}, bf16[2,256,128]{2,1,0:T(8,128)(2,1)S(1)}, u32[]{:S(2)}, u32[]{:S(2)}) collective-permute-start(bf16[2,256,128]{2,1,0:T(8,128)(2,1)S(1)} %pad_maximum_fusion.2), channel_id=1, source_target_pairs={{0,1},{1,0},{2,3},{3,2},{4,5},{5,4},{6,7},{7,6},{8,9},{9,8},{10,11... | collective-permute-start | bytes 393224 | tf_op jit(solution)/shard_map/ppermute | solution.py:361
  13.8 5.8 %collective-permute-start.5 = (bf16[2,256,128]{2,1,0:T(8,128)(2,1)S(1)}, bf16[2,256,128]{2,1,0:T(8,128)(2,1)S(1)}, u32[]{:S(2)}, u32[]{:S(2)}) collective-permute-start(bf16[2,256,128]{2,1,0:T(8,128)(2,1)S(1)} %pad_maximum_fusion.3), channel_id=1, source_target_pairs={{0,4},{1,5},{2,6},{3,7},{4,0},{5,1},{6,2},{7,3},{8,12},{9,13},{10,... | collective-permute-start | bytes 393224 | tf_op jit(solution)/shard_map/ppermute | solution.py:361
  15.4 5.9 %collective-permute-start.6 = (bf16[2,256,128]{2,1,0:T(8,128)(2,1)S(1)}, bf16[2,256,128]{2,1,0:T(8,128)(2,1)S(1)}, u32[]{:S(2)}, u32[]{:S(2)}) collective-permute-start(bf16[2,256,128]{2,1,0:T(8,128)(2,1)S(1)} %pad_maximum_fusion.4), channel_id=1, source_target_pairs={{0,5},{1,4},{2,7},{3,6},{4,1},{5,0},{6,3},{7,2},{8,13},{9,12},{10,... | collective-permute-start | bytes 393224 | tf_op jit(solution)/shard_map/ppermute | solution.py:361
  18.4 3.0 %collective-permute-start.3 = (bf16[2,144,128]{2,1,0:T(8,128)(2,1)S(1)}, bf16[2,144,128]{2,1,0:T(8,128)(2,1)S(1)}, u32[]{:S(2)}, u32[]{:S(2)}) collective-permute-start(bf16[2,144,128]{2,1,0:T(8,128)(2,1)S(1)} %slice.107), channel_id=1, source_target_pairs={{0,2},{2,0},{1,3},{3,1},{4,6},{6,4},{5,7},{7,5},{8,10},{10,8},{9,1... | collective-permute-start | bytes 221192 | tf_op jit(solution)/shard_map/ppermute | solution.py:361
  21.3 5.1 %collective-permute-start.10 = (bf16[4,144,128]{2,1,0:T(8,128)(2,1)S(1)}, bf16[4,144,128]{2,1,0:T(8,128)(2,1)S(1)}, u32[]{:S(2)}, u32[]{:S(2)}) collective-permute-start(bf16[4,144,128]{2,1,0:T(8,128)(2,1)S(1)} %shard_map.105.refs_2_), channel_id=1, source_target_pairs={{0,8},{8,0},{16,24},{24,16},{1,9},{9,1},{17,25},{25,17},{2,10},{10... | collective-permute-start | bytes 442376 | tf_op jit(solution)/shard_map/ppermute | solution.py:361
  21.8 1.3 %collective-permute-start.9 = (bf16[2,144,128]{2,1,0:T(8,128)(2,1)S(1)}, bf16[2,144,128]{2,1,0:T(8,128)(2,1)S(1)}, u32[]{:S(2)}, u32[]{:S(2)}) collective-permute-start(bf16[2,144,128]{2,1,0:T(8,128)(2,1)S(1)} %slice.111), channel_id=1, source_target_pairs={{0,2},{2,0},{1,3},{3,1},{4,6},{6,4},{5,7},{7,5},{8,10},{10,8},{9,1... | collective-permute-start | bytes 221192 | tf_op jit(solution)/shard_map/ppermute | solution.py:361
  21.9 1.4 %collective-permute-start.7 = (bf16[2,144,128]{2,1,0:T(8,128)(2,1)S(1)}, bf16[2,144,128]{2,1,0:T(8,128)(2,1)S(1)}, u32[]{:S(2)}, u32[]{:S(2)}) collective-permute-start(bf16[2,144,128]{2,1,0:T(8,128)(2,1)S(1)} %slice.110), channel_id=1, source_target_pairs={{0,2},{2,0},{1,3},{3,1},{4,6},{6,4},{5,7},{7,5},{8,10},{10,8},{9,1... | collective-permute-start | bytes 221192 | tf_op jit(solution)/shard_map/ppermute | solution.py:361
  26.5 1.3 %collective-permute-start.11 = (bf16[2,144,128]{2,1,0:T(8,128)(2,1)S(1)}, bf16[2,144,128]{2,1,0:T(8,128)(2,1)S(1)}, u32[]{:S(2)}, u32[]{:S(2)}) collective-permute-start(bf16[2,144,128]{2,1,0:T(8,128)(2,1)S(1)} %slice.113), channel_id=1, source_target_pairs={{0,2},{2,0},{1,3},{3,1},{4,6},{6,4},{5,7},{7,5},{8,10},{10,8},{9,1... | collective-permute-start | bytes 221192 | tf_op jit(solution)/shard_map/ppermute | solution.py:361
  28.4 6.5 %collective-permute-start.12 = (f32[8,128]{1,0:T(8,128)S(1)}, f32[8,128]{1,0:T(8,128)S(1)}, u32[]{:S(2)}, u32[]{:S(2)}) collective-permute-start(f32[8,128]{1,0:T(8,128)S(1)} %shard_map.108.refs_12_.refs_8_), channel_id=1, source_target_pairs={{0,8},{8,0},{16,24},{24,16},{1,9},{9,1},{17,25},{25,17},{2,10},{10... | collective-permute-start | bytes 12296 | tf_op jit(solution)/shard_map/ppermute | solution.py:361
  28.9 6.0 %collective-permute-start.13 = (f32[8,128]{1,0:T(8,128)S(1)}, f32[8,128]{1,0:T(8,128)S(1)}, u32[]{:S(2)}, u32[]{:S(2)}) collective-permute-start(f32[8,128]{1,0:T(8,128)S(1)} %shard_map.108.refs_12_.refs_8_), channel_id=1, source_target_pairs={{0,16},{8,24},{16,0},{24,8},{1,17},{9,25},{17,1},{25,9},{2,18},{10... | collective-permute-start | bytes 12296 | tf_op jit(solution)/shard_map/ppermute | solution.py:361
  30.3 5.4 %collective-permute-start.14 = (f32[8,128]{1,0:T(8,128)S(1)}, f32[8,128]{1,0:T(8,128)S(1)}, u32[]{:S(2)}, u32[]{:S(2)}) collective-permute-start(f32[8,128]{1,0:T(8,128)S(1)} %shard_map.108.refs_12_.refs_8_), channel_id=1, source_target_pairs={{0,24},{8,16},{16,8},{24,0},{1,25},{9,17},{17,9},{25,1},{2,26},{10... | collective-permute-start | bytes 12296 | tf_op jit(solution)/shard_map/ppermute | solution.py:361
  37.3 15.8 %collective-permute-start.22 = (bf16[2,256,128]{2,1,0:T(8,128)(2,1)S(1)}, bf16[2,256,128]{2,1,0:T(8,128)(2,1)S(1)}, u32[]{:S(2)}, u32[]{:S(2)}) collective-permute-start(bf16[2,256,128]{2,1,0:T(8,128)(2,1)S(1)} %get-tuple-element.37), channel_id=1, source_target_pairs={{0,5},{1,4},{2,7},{3,6},{4,1},{5,0},{6,3},{7,2},{8,13},{9,12},{10,... | collective-permute-start | bytes 393224 | tf_op jit(solution)/shard_map/ppermute | solution.py:361
  39.8 1.3 %collective-permute-start.15 = (bf16[4,2,64,128]{3,2,1,0:T(8,128)(2,1)S(1)}, bf16[4,2,64,128]{3,2,1,0:T(8,128)(2,1)S(1)}, u32[]{:S(2)}, u32[]{:S(2)}) collective-permute-start(bf16[4,2,64,128]{3,2,1,0:T(8,128)(2,1)S(1)} %get-tuple-element.28), channel_id=1, source_target_pairs={{0,2},{2,0},{1,3},{3,1},{4,6},{6,4},{5,7},{7,5},{8,10},{10,8},{9,1... | collective-permute-start | bytes 393224 | tf_op jit(solution)/shard_map/ppermute | solution.py:361
  39.8 13.3 %collective-permute-start.21 = (bf16[2,256,128]{2,1,0:T(8,128)(2,1)S(1)}, bf16[2,256,128]{2,1,0:T(8,128)(2,1)S(1)}, u32[]{:S(2)}, u32[]{:S(2)}) collective-permute-start(bf16[2,256,128]{2,1,0:T(8,128)(2,1)S(1)} %get-tuple-element.36), channel_id=1, source_target_pairs={{0,4},{1,5},{2,6},{3,7},{4,0},{5,1},{6,2},{7,3},{8,12},{9,13},{10,... | collective-permute-start | bytes 393224 | tf_op jit(solution)/shard_map/ppermute | solution.py:361
  40.4 12.9 %collective-permute-start.20 = (bf16[2,256,128]{2,1,0:T(8,128)(2,1)S(1)}, bf16[2,256,128]{2,1,0:T(8,128)(2,1)S(1)}, u32[]{:S(2)}, u32[]{:S(2)}) collective-permute-start(bf16[2,256,128]{2,1,0:T(8,128)(2,1)S(1)} %get-tuple-element.35), channel_id=1, source_target_pairs={{0,1},{1,0},{2,3},{3,2},{4,5},{5,4},{6,7},{7,6},{8,9},{9,8},{10,11... | collective-permute-start | bytes 393224 | tf_op jit(solution)/shard_map/ppermute | solution.py:361
  41.2 6.7 %collective-permute-start.18 = (bf16[2,2,64,128]{3,2,1,0:T(8,128)(2,1)S(1)}, bf16[2,2,64,128]{3,2,1,0:T(8,128)(2,1)S(1)}, u32[]{:S(2)}, u32[]{:S(2)}) collective-permute-start(bf16[2,2,64,128]{3,2,1,0:T(8,128)(2,1)S(1)} %pad_maximum_fusion.8), channel_id=1, source_target_pairs={{0,24},{8,16},{16,8},{24,0},{1,25},{9,17},{17,9},{25,1},{2,26},{10... | collective-permute-start | bytes 196616 | tf_op jit(solution)/shard_map/ppermute | solution.py:361
  43.6 5.1 %collective-permute-start.17 = (bf16[2,2,64,128]{3,2,1,0:T(8,128)(2,1)S(1)}, bf16[2,2,64,128]{3,2,1,0:T(8,128)(2,1)S(1)}, u32[]{:S(2)}, u32[]{:S(2)}) collective-permute-start(bf16[2,2,64,128]{3,2,1,0:T(8,128)(2,1)S(1)} %pad_maximum_fusion.7), channel_id=1, source_target_pairs={{0,8},{8,0},{16,24},{24,16},{1,9},{9,1},{17,25},{25,17},{2,10},{10... | collective-permute-start | bytes 196616 | tf_op jit(solution)/shard_map/ppermute | solution.py:361
  47.9 5.2 %collective-permute-start.16 = (bf16[2,2,64,128]{3,2,1,0:T(8,128)(2,1)S(1)}, bf16[2,2,64,128]{3,2,1,0:T(8,128)(2,1)S(1)}, u32[]{:S(2)}, u32[]{:S(2)}) collective-permute-start(bf16[2,2,64,128]{3,2,1,0:T(8,128)(2,1)S(1)} %pad_maximum_fusion.6), channel_id=1, source_target_pairs={{0,16},{8,24},{16,0},{24,8},{1,17},{9,25},{17,1},{25,9},{2,18},{10... | collective-permute-start | bytes 196616 | tf_op jit(solution)/shard_map/ppermute | solution.py:361
  53.3 4.1 %collective-permute-start.23 = (bf16[4,256,128]{2,1,0:T(8,128)(2,1)S(1)}, bf16[4,256,128]{2,1,0:T(8,128)(2,1)S(1)}, u32[]{:S(2)}, u32[]{:S(2)}) collective-permute-start(bf16[4,256,128]{2,1,0:T(8,128)(2,1)S(1)} %pad_maximum_fusion), channel_id=1, source_target_pairs={{0,2},{1,3},{2,0},{3,1},{4,6},{5,7},{6,4},{7,5},{8,10},{9,11},{10,... | collective-permute-start | bytes 786440 | tf_op jit(solution)/shard_map/ppermute | solution.py:361
  53.4 4.0 %collective-permute-start.19 = (bf16[2,64,128]{2,1,0:T(8,128)(2,1)S(1)}, bf16[2,64,128]{2,1,0:T(8,128)(2,1)S(1)}, u32[]{:S(2)}, u32[]{:S(2)}) collective-permute-start(bf16[2,64,128]{2,1,0:T(8,128)(2,1)S(1)} %get-tuple-element.30), channel_id=1, source_target_pairs={{0,4},{4,0},{1,5},{5,1},{2,6},{6,2},{3,7},{7,3},{8,12},{12,8},{9,1... | collective-permute-start | bytes 98312 | tf_op jit(solution)/shard_map/ppermute | solution.py:361

commit v9 on v8

--- a/solution.py
+++ b/solution.py
@@ -269,10 +269,12 @@
     in_branches(all_visible(at, ends_ref[...], tokens), body)
 
 
-def weight_kernel(blocks, nears, heads, live_ref, *refs):
+def token_kernel(blocks, nears, heads, tokens, live_ref, *refs):
     at = place(nears, heads)
     row_refs, refs = refs[: len(blocks) * nears], refs[len(blocks) * nears :]
-    lse_refs, (dq_ref, weight_ref, *dq_refs) = refs[: len(blocks)], refs[len(blocks) :]
+    (prob_ref, dscore_ref, dq_ref), refs = refs[:3], refs[3:]
+    lse_refs, refs = refs[: len(blocks)], refs[len(blocks) :]
+    dkv_refs, (*dq_refs, dk_acc, dv_acc) = refs[: len(KEEP)], refs[len(KEEP) :]
     lines = (row_refs[0].shape[1] - STAT_ROWS) // 2
     all_slabs = block_slabs(blocks, nears, row_refs)
     size = len(all_slabs[0]) * lines
@@ -284,30 +286,18 @@
         total = sum(jnp.exp(x - peak) for x in part_lse) + jnp.exp(self_lse - peak)
         lse = jnp.where(live_ref[:, lanes] > 0, peak + jnp.log(total), DEAD_LSE)
         weight = jnp.exp(part_lse[0] - lse)
-        weight_ref[:, lanes] = weight
         dq = (dq_ref[:, lanes] * (weight * SCALE)).T.astype(jnp.bfloat16)
         sources = [(b, slab) for b in held for slab in all_slabs[blocks.index(b)]]
         for m, (b, (_, _, n, j)) in enumerate(sources):
             dq_refs[n][blocks.index(b), j] = dq[m * lines : (m + 1) * lines]
-
-
-def token_kernel(blocks, nears, tokens, *refs):
-    row_refs, refs = refs[: len(blocks) * nears], refs[len(blocks) * nears :]
-    (prob_ref, dscore_ref, weight_ref), refs = refs[:3], refs[3:]
-    dkv_refs, (dk_acc, dv_acc) = refs[: len(KEEP)], refs[len(KEEP) :]
-    lines = (row_refs[0].shape[1] - STAT_ROWS) // 2
-    all_slabs = block_slabs(blocks, nears, row_refs)
-    size = len(all_slabs[0]) * lines
-    for first, count, held, slabs in steps_of(blocks, all_slabs, lines):
-        weight = jnp.broadcast_to(weight_ref[:, first : first + count], (DH, count)).T
+        weight_t = jnp.broadcast_to(weight, (DH, count)).T
         q, o_grad = (
-            (lines_of(slabs, start, lines).astype(jnp.float32) * weight).astype(jnp.bfloat16)
+            (lines_of(slabs, start, lines).astype(jnp.float32) * weight_t).astype(jnp.bfloat16)
             for start in (0, lines)
         )
         for i in range(len(KEEP)):
-            dscore, prob = dscore_ref[i, :, first : first + count], prob_ref[i, :, first : first + count]
-            dk = jnp.dot(dscore, q, preferred_element_type=jnp.float32) * SCALE
-            dv = jnp.dot(prob, o_grad, preferred_element_type=jnp.float32)
+            dk = jnp.dot(dscore_ref[i, :, lanes], q, preferred_element_type=jnp.float32) * SCALE
+            dv = jnp.dot(prob_ref[i, :, lanes], o_grad, preferred_element_type=jnp.float32)
             if first > 0:
                 dk = dk + dk_acc[i]
                 dv = dv + dv_acc[i]
@@ -381,10 +371,9 @@
 
 def swap_back(pairs, after):
     members = ("row", "near", "head")
-    pairs = [pairs[0]] + [
-        tie(swap(x, members, j, KVH), after) for x, j in zip(pairs[1:], KEEP[1:])
-    ]
-    return [*pairs, swap(jnp.stack([x[1] for x in pairs]), members, FIRST, KVH)]
+    pairs = [swap(x, members, j, KVH) if j else x for x, j in zip(pairs, KEEP)]
+    beyond = tie(jnp.stack([x[1] for x in pairs]), after)
+    return [*pairs, swap(beyond, members, FIRST, KVH)]
 
 
 def line_limits(parts, row_count, nears, rows, lines, resp_len, prompt_end):
@@ -451,10 +440,10 @@
         return [x, swap(x[row_count:], "near", 1, nears)] if nears > 1 else [x]
 
     blocks, came = [0], [own_block]
-    row_refs = row_refs_of(tie(own_block, pairs[1:2]))
+    row_refs = row_refs_of(own_block)
     for d in far:
         if d == 1:
-            came = came[:1] + [tie(x, pairs[1:] + row_refs[1:]) for x in came[1:]]
+            came = came[:1] + [tie(x, pairs[1:]) for x in came[1:]]
         came = came + [swap(x, "part", d, parts) for x in came]
         blocks = blocks + [b ^ d for b in blocks]
     ends, live = line_limits(parts, row_count, nears, rows, lines, resp_len, prompt_end)
@@ -484,21 +473,17 @@
         compiler_params=PARAMS,
     )(ends, *row_refs, *pairs, *lse)
     dq_shape = jax.ShapeDtypeStruct((parts, row_count, lines, DH), jnp.bfloat16)
-    weight, *dq = pl.pallas_call(
-        functools.partial(weight_kernel, blocks, nears, heads),
-        in_specs=[VMEM] * (1 + len(row_refs) + parts + 1),
-        out_shape=[jax.ShapeDtypeStruct((1, all_lines), jnp.float32)] + [dq_shape] * nears,
-        compiler_params=PARAMS,
-    )(live, *row_refs, *every_lse, dq)
-    dq = [swap(x, "near", n, nears) if n else x for n, x in enumerate(dq)]
     acc = pltpu.VMEM((len(KEEP), 2 * tokens, DH), jnp.float32)
-    dkv = pl.pallas_call(
-        functools.partial(token_kernel, blocks, nears, tokens),
-        in_specs=[VMEM] * (len(row_refs) + 3),
-        out_shape=[jax.ShapeDtypeStruct((2, 2 * tokens, DH), jnp.bfloat16)] * len(KEEP),
+    outs = pl.pallas_call(
+        functools.partial(token_kernel, blocks, nears, heads, tokens),
+        in_specs=[VMEM] * (1 + len(row_refs) + 3 + parts),
+        out_shape=[jax.ShapeDtypeStruct((2, 2 * tokens, DH), jnp.bfloat16)] * len(KEEP)
+        + [dq_shape] * nears,
         scratch_shapes=[acc] * 2,
         compiler_params=PARAMS,
-    )(*row_refs, prob, dscore, weight)
+    )(live, *row_refs, prob, dscore, dq, *every_lse)
+    dkv, dq = outs[: len(KEEP)], outs[len(KEEP) :]
+    dq = [swap(x, "near", n, nears) if n else x for n, x in enumerate(dq)]
     from_parts = [
         swap(jnp.stack([x[at] for x in dq]), "part", b, parts) for at, b in enumerate(blocks) if b
     ]
@@ -509,7 +494,7 @@
         out_shape=[sum_shape] * 2,
         compiler_params=PARAMS,
     )(*dq, *from_parts)
-    pairs = swap_back(dkv, sums[:1])
+    pairs = swap_back(dkv, from_parts)
     sums = [swap(x, "row", j, row_count) if j else x for j, x in enumerate(sums[:row_count])]
     out_q, out_k, out_v = pl.pallas_call(
         functools.partial(write_kernel, nears, heads),

time: 58.5 us -> 52.8 us (0.903)
  waiting for transfers between devices: 23.8 us -> 15.2 us
  starting transfers between devices: 24.2 us -> 27.2 us
    ppermute x24, waiting for transfers between devices: 23.8 us -> 15.2 us  [swap(): return lax.ppermute(x, axis, [(i, i ^ distance) for i in range(size)])]
    ppermute x24, starting transfers between devices: 24.2 us -> 27.2 us  [swap(): return lax.ppermute(x, axis, [(i, i ^ distance) for i in range(size)])]
    pallas_call x2 -> x1, Pallas kernels: 1.59 us -> 1.48 us  [shards(): pl.pallas_call(functools.partial(token_kernel, blocks, nears, heads, toke...]
  transfers between devices with their start and end apart: 24 -> 24, of which waited for: 15 -> 15; matrix products, arithmetic and copies ran while one was open for 0% -> 1% of each run, Pallas kernels for 5% -> 6%
where the time goes in v9:
time: 52.8 us; the launch traced here: 52.6 us
  starting transfers between devices  27.2 us (52%)
  waiting for transfers between devices  15.2 us (29%)
  Pallas kernels  7.67 us (15%)
  between operations  2.15 us (4%)
    ppermute x24, starting transfers between devices, swap(): return lax.ppermute(x, axis, [(i, i ^ distance) for i in range(size)])  27.2 us
    ppermute x24, waiting for transfers between devices, swap(): return lax.ppermute(x, axis, [(i, i ^ distance) for i in range(size)])  15.2 us
    pallas_call x1, Pallas kernels, shards(): pl.pallas_call(functools.partial(part_kernel, blocks, nears, heads, token...  2.04 us
    pallas_call x2, Pallas kernels, part_lse(): pl.pallas_call(functools.partial(stat_kernel, held, first, nears, heads,...  1.76 us
    pallas_call x1, Pallas kernels, shards(): pl.pallas_call(functools.partial(token_kernel, blocks, nears, heads, toke...  1.48 us
    pallas_call x1, Pallas kernels, shards(): pl.pallas_call(functools.partial(pack_kernel, row_count, nears, heads), i...  1.37 us
  transfers between devices with their start and end apart: 24, of which 15 were waited for; matrix products, arithmetic and copies ran while one was open for 1% of the time, Pallas kernels for 6%

profile of v9, /device:TPU:0, one launch (start us, length us, event | category | flops | bytes accessed | tf_op | source)
XLA Modules:
  0.0 52.6 jit_solution(2935480842954728911)
XLA Ops:
  0.6 1.4 %shard_map.103 = (bf16[2,144,128]{2,1,0:T(8,128)(2,1)S(1)}, bf16[2,144,128]{2,1,0:T(8,128)(2,1)S(1)}, bf16[4,256,128]{2,1,0:T(8,128)(2,1)S(1)}, bf16[4,256,128]{2,1,0:T(8,128)(2,1)S(1)}) custom-call(bf16[256,128]{1,0:T(8,128)(2,1)} %bitcast.24, bf16[256,128]{1,0:T(8,128)(2,1)} %bitcast.25, bf16[256,128]{1,0:T(8,128)(2,1)} %bitcast.26, f32[4,64]{1,0:T(4,128)} %lse_hbm.1, ...), custom_call_target="tpu_custom_call" | custom-call | tf_op jit(solution)/shard_map/pallas_call | solution.py:415
  2.0 3.0 %collective-permute-start = (bf16[2,144,128]{2,1,0:T(8,128)(2,1)S(1)}, bf16[2,144,128]{2,1,0:T(8,128)(2,1)S(1)}, u32[]{:S(2)}, u32[]{:S(2)}) collective-permute-start(bf16[2,144,128]{2,1,0:T(8,128)(2,1)S(1)} %get-tuple-element.22), channel_id=1, source_target_pairs={{0,4},{4,0},{1,5},{5,1},{2,6},{6,2},{3,7},{7,3},{8,12},{12,8},{9,1... | collective-permute-start | bytes 221192 | tf_op jit(solution)/shard_map/ppermute | solution.py:351
  5.0 0.0 collective-permute-start.3
  5.1 2.3 %collective-permute-done = bf16[2,144,128]{2,1,0:T(8,128)(2,1)S(1)} collective-permute-done((bf16[2,144,128]{2,1,0:T(8,128)(2,1)S(1)}, bf16[2,144,128]{2,1,0:T(8,128)(2,1)S(1)}, u32[]{:S(2)}, u32[]{:S(2)}) %collective-permute-start) | collective-permute-done | bytes 73760 | tf_op jit(solution)/shard_map/ppermute | solution.py:351
  7.4 3.2 %collective-permute-start.2 = (bf16[4,144,128]{2,1,0:T(8,128)(2,1)S(1)}, bf16[4,144,128]{2,1,0:T(8,128)(2,1)S(1)}, u32[]{:S(2)}, u32[]{:S(2)}) collective-permute-start(bf16[4,144,128]{2,1,0:T(8,128)(2,1)S(1)} %pad_maximum_fusion.1.refs_0_), channel_id=1, source_target_pairs={{0,16},{8,24},{16,0},{24,8},{1,17},{9,25},{17,1},{25,9},{2,18},{10... | collective-permute-start | bytes 442376 | tf_op jit(solution)/shard_map/ppermute | solution.py:351
  10.6 1.6 %collective-permute-start.4 = (bf16[2,256,128]{2,1,0:T(8,128)(2,1)S(1)}, bf16[2,256,128]{2,1,0:T(8,128)(2,1)S(1)}, u32[]{:S(2)}, u32[]{:S(2)}) collective-permute-start(bf16[2,256,128]{2,1,0:T(8,128)(2,1)S(1)} %pad_maximum_fusion.2), channel_id=1, source_target_pairs={{0,1},{1,0},{2,3},{3,2},{4,5},{5,4},{6,7},{7,6},{8,9},{9,8},{10,11... | collective-permute-start | bytes 393224 | tf_op jit(solution)/shard_map/ppermute | solution.py:351
  12.2 1.6 %collective-permute-start.5 = (bf16[2,256,128]{2,1,0:T(8,128)(2,1)S(1)}, bf16[2,256,128]{2,1,0:T(8,128)(2,1)S(1)}, u32[]{:S(2)}, u32[]{:S(2)}) collective-permute-start(bf16[2,256,128]{2,1,0:T(8,128)(2,1)S(1)} %pad_maximum_fusion.3), channel_id=1, source_target_pairs={{0,4},{1,5},{2,6},{3,7},{4,0},{5,1},{6,2},{7,3},{8,12},{9,13},{10,... | collective-permute-start | bytes 393224 | tf_op jit(solution)/shard_map/ppermute | solution.py:351
  13.8 0.5 %collective-permute-start.6 = (bf16[2,256,128]{2,1,0:T(8,128)(2,1)S(1)}, bf16[2,256,128]{2,1,0:T(8,128)(2,1)S(1)}, u32[]{:S(2)}, u32[]{:S(2)}) collective-permute-start(bf16[2,256,128]{2,1,0:T(8,128)(2,1)S(1)} %pad_maximum_fusion.4), channel_id=1, source_target_pairs={{0,5},{1,4},{2,7},{3,6},{4,1},{5,0},{6,3},{7,2},{8,13},{9,12},{10,... | collective-permute-start | bytes 393224 | tf_op jit(solution)/shard_map/ppermute | solution.py:351
  15.0 1.6 %collective-permute-start.8 = (bf16[4,144,128]{2,1,0:T(8,128)(2,1)S(1)}, bf16[4,144,128]{2,1,0:T(8,128)(2,1)S(1)}, u32[]{:S(2)}, u32[]{:S(2)}) collective-permute-start(bf16[4,144,128]{2,1,0:T(8,128)(2,1)S(1)} %pad_maximum_fusion.1.refs_0_), channel_id=1, source_target_pairs={{0,8},{8,0},{16,24},{24,16},{1,9},{9,1},{17,25},{25,17},{2,10},{10... | collective-permute-start | bytes 442376 | tf_op jit(solution)/shard_map/ppermute | solution.py:351
  16.7 0.0 collective-permute-done.2.refs_0_
  16.7 0.4 collective-permute-done.4.refs_1_.refs_7_.refs_3_.refs_9_
  17.0 1.3 %collective-permute-done.5.refs_2_.refs_8_.refs_4_.refs_10_ = bf16[2,256,128]{2,1,0:T(8,128)(2,1)S(1)} collective-permute-done((bf16[2,256,128]{2,1,0:T(8,128)(2,1)S(1)}, bf16[2,256,128]{2,1,0:T(8,128)(2,1)S(1)}, u32[]{:S(2)}, u32[]{:S(2)}) %collective-permute-start.5) | collective-permute-done | bytes 131104 | tf_op jit(solution)/shard_map/ppermute | solution.py:351
  18.3 1.4 %collective-permute-done.6.refs_3_.refs_9_.refs_5_.refs_11_ = bf16[2,256,128]{2,1,0:T(8,128)(2,1)S(1)} collective-permute-done((bf16[2,256,128]{2,1,0:T(8,128)(2,1)S(1)}, bf16[2,256,128]{2,1,0:T(8,128)(2,1)S(1)}, u32[]{:S(2)}, u32[]{:S(2)}) %collective-permute-start.6) | collective-permute-done | bytes 131104 | tf_op jit(solution)/shard_map/ppermute | solution.py:351
  19.7 1.6 %collective-permute-start.10 = (bf16[4,144,128]{2,1,0:T(8,128)(2,1)S(1)}, bf16[4,144,128]{2,1,0:T(8,128)(2,1)S(1)}, u32[]{:S(2)}, u32[]{:S(2)}) collective-permute-start(bf16[4,144,128]{2,1,0:T(8,128)(2,1)S(1)} %shard_map.104.refs_2_), channel_id=1, source_target_pairs={{0,8},{8,0},{16,24},{24,16},{1,9},{9,1},{17,25},{25,17},{2,10},{10... | collective-permute-start | bytes 442376 | tf_op jit(solution)/shard_map/ppermute | solution.py:351
  21.3 0.1 collective-permute-start.1
  21.4 0.5 %collective-permute-start.9 = (bf16[2,144,128]{2,1,0:T(8,128)(2,1)S(1)}, bf16[2,144,128]{2,1,0:T(8,128)(2,1)S(1)}, u32[]{:S(2)}, u32[]{:S(2)}) collective-permute-start(bf16[2,144,128]{2,1,0:T(8,128)(2,1)S(1)} %slice.108), channel_id=1, source_target_pairs={{0,2},{2,0},{1,3},{3,1},{4,6},{6,4},{5,7},{7,5},{8,10},{10,8},{9,1... | collective-permute-start | bytes 221192 | tf_op jit(solution)/shard_map/ppermute | solution.py:351
  22.0 0.1 collective-permute-start.7
  22.1 0.6 %collective-permute-done.1.refs_1_ = bf16[2,144,128]{2,1,0:T(8,128)(2,1)S(1)} collective-permute-done((bf16[2,144,128]{2,1,0:T(8,128)(2,1)S(1)}, bf16[2,144,128]{2,1,0:T(8,128)(2,1)S(1)}, u32[]{:S(2)}, u32[]{:S(2)}) %collective-permute-start.1) | collective-permute-done | bytes 73760 | tf_op jit(solution)/shard_map/ppermute | solution.py:351
  22.6 0.2 collective-permute-done.9.refs_5_
  22.9 0.4 collective-permute-done.7.refs_3_
  23.2 1.1 %shard_map.105.refs_1_.refs_6_ = f32[8,128]{1,0:T(8,128)S(1)} custom-call(s32[1,1024]{1,0:T(1,128)S(1)} %compare_select_fusion.ends_ref, bf16[4,144,128]{2,1,0:T(8,128)(2,1)S(1)} %pad_maximum_fusion.1.refs_0_, bf16[2,144,128]{2,1,0:T(8,128)(2,1)S(1)} %collective-permute-done.1.refs_1_, bf16[4,144,128]{2,1,0:T(8,128)(2,1)S(1)} %shard_map.104.refs_2_, ...), custom_call_target="tpu_custom_call" | custom-call | tf_op jit(solution)/shard_map/pallas_call | solution.py:452
  24.4 0.5 collective-permute-done.10.refs_0_
  24.9 0.1 collective-permute-start.11
  25.6 0.6 %collective-permute-done.11.refs_1_.refs_7_ = bf16[2,144,128]{2,1,0:T(8,128)(2,1)S(1)} collective-permute-done((bf16[2,144,128]{2,1,0:T(8,128)(2,1)S(1)}, bf16[2,144,128]{2,1,0:T(8,128)(2,1)S(1)}, u32[]{:S(2)}, u32[]{:S(2)}) %collective-permute-start.11) | collective-permute-done | bytes 73760 | tf_op jit(solution)/shard_map/ppermute | solution.py:351
  26.2 0.6 %shard_map.107.refs_12_.refs_11_ = f32[8,128]{1,0:T(8,128)S(1)} custom-call(s32[1,1024]{1,0:T(1,128)S(1)} %compare_select_fusion.ends_ref, bf16[4,144,128]{2,1,0:T(8,128)(2,1)S(1)} %shard_map.106.refs_0_.refs_6_, bf16[2,144,128]{2,1,0:T(8,128)(2,1)S(1)} %collective-permute-done.11.refs_1_.refs_7_, ...), custom_call_target="tpu_custom_call" | custom-call | tf_op jit(solution)/shard_map/pallas_call | solution.py:452
  26.8 1.4 %collective-permute-start.14 = (f32[8,128]{1,0:T(8,128)S(1)}, f32[8,128]{1,0:T(8,128)S(1)}, u32[]{:S(2)}, u32[]{:S(2)}) collective-permute-start(f32[8,128]{1,0:T(8,128)S(1)} %shard_map.107.refs_12_.refs_11_), channel_id=1, source_target_pairs={{0,24},{8,16},{16,8},{24,0},{1,25},{9,17},{17,9},{25,1},{2,26},{10... | collective-permute-start | bytes 12296 | tf_op jit(solution)/shard_map/ppermute | solution.py:351
  28.3 1.7 %collective-permute-start.13 = (f32[8,128]{1,0:T(8,128)S(1)}, f32[8,128]{1,0:T(8,128)S(1)}, u32[]{:S(2)}, u32[]{:S(2)}) collective-permute-start(f32[8,128]{1,0:T(8,128)S(1)} %shard_map.107.refs_12_.refs_11_), channel_id=1, source_target_pairs={{0,16},{8,24},{16,0},{24,8},{1,17},{9,25},{17,1},{25,9},{2,18},{10... | collective-permute-start | bytes 12296 | tf_op jit(solution)/shard_map/ppermute | solution.py:351
  30.0 1.3 %collective-permute-start.12 = (f32[8,128]{1,0:T(8,128)S(1)}, f32[8,128]{1,0:T(8,128)S(1)}, u32[]{:S(2)}, u32[]{:S(2)}) collective-permute-start(f32[8,128]{1,0:T(8,128)S(1)} %shard_map.107.refs_12_.refs_11_), channel_id=1, source_target_pairs={{0,8},{8,0},{16,24},{24,16},{1,9},{9,1},{17,25},{25,17},{2,10},{10... | collective-permute-start | bytes 12296 | tf_op jit(solution)/shard_map/ppermute | solution.py:351
  31.3 2.0 %shard_map.108 = (bf16[4,256,1024]{2,1,0:T(8,128)(2,1)S(1)}, bf16[4,256,1024]{2,1,0:T(8,128)(2,1)S(1)}, f32[128,1024]{1,0:T(8,128)S(1)}) custom-call(s32[1,1024]{1,0:T(1,128)S(1)} %compare_select_fusion.ends_ref, bf16[4,144,128]{2,1,0:T(8,128)(2,1)S(1)} %pad_maximum_fusion.1.refs_0_, bf16[2,144,128]{2,1,0:T(8,128)(2,1)S(1)} %collective-permute-done.1.refs_1_, ...), custom_call_target="tpu_custom_call" | custom-call | tf_op jit(solution)/shard_map/pallas_call | solution.py:468
  33.4 0.0 collective-permute-done.13.refs_13_
  33.4 0.2 collective-permute-done.12.refs_12_
  33.6 1.5 %shard_map.109 = (bf16[2,256,128]{2,1,0:T(8,128)(2,1)S(1)}, bf16[2,256,128]{2,1,0:T(8,128)(2,1)S(1)}, bf16[2,256,128]{2,1,0:T(8,128)(2,1)S(1)}, bf16[2,256,128]{...) custom-call(s32[1,1024]{1,0:T(1,128)S(1)} %compare_convert_fusion.live_ref, ...), custom_call_target="tpu_custom_call" | custom-call | tf_op jit(solution)/shard_map/pallas_call | solution.py:477
  35.1 0.1 collective-permute-start.15
  35.1 1.0 %collective-permute-start.20 = (bf16[2,256,128]{2,1,0:T(8,128)(2,1)S(1)}, bf16[2,256,128]{2,1,0:T(8,128)(2,1)S(1)}, u32[]{:S(2)}, u32[]{:S(2)}) collective-permute-start(bf16[2,256,128]{2,1,0:T(8,128)(2,1)S(1)} %get-tuple-element.33), channel_id=1, source_target_pairs={{0,1},{1,0},{2,3},{3,2},{4,5},{5,4},{6,7},{7,6},{8,9},{9,8},{10,11... | collective-permute-start | bytes 393224 | tf_op jit(solution)/shard_map/ppermute | solution.py:351
  36.1 0.9 %collective-permute-start.21 = (bf16[2,256,128]{2,1,0:T(8,128)(2,1)S(1)}, bf16[2,256,128]{2,1,0:T(8,128)(2,1)S(1)}, u32[]{:S(2)}, u32[]{:S(2)}) collective-permute-start(bf16[2,256,128]{2,1,0:T(8,128)(2,1)S(1)} %get-tuple-element.34), channel_id=1, source_target_pairs={{0,4},{1,5},{2,6},{3,7},{4,0},{5,1},{6,2},{7,3},{8,12},{9,13},{10,... | collective-permute-start | bytes 393224 | tf_op jit(solution)/shard_map/ppermute | solution.py:351
  37.1 1.6 %collective-permute-start.22 = (bf16[2,256,128]{2,1,0:T(8,128)(2,1)S(1)}, bf16[2,256,128]{2,1,0:T(8,128)(2,1)S(1)}, u32[]{:S(2)}, u32[]{:S(2)}) collective-permute-start(bf16[2,256,128]{2,1,0:T(8,128)(2,1)S(1)} %get-tuple-element.35), channel_id=1, source_target_pairs={{0,5},{1,4},{2,7},{3,6},{4,1},{5,0},{6,3},{7,2},{8,13},{9,12},{10,... | collective-permute-start | bytes 393224 | tf_op jit(solution)/shard_map/ppermute | solution.py:351
  38.7 1.3 %collective-permute-start.16 = (bf16[2,2,64,128]{3,2,1,0:T(8,128)(2,1)S(1)}, bf16[2,2,64,128]{3,2,1,0:T(8,128)(2,1)S(1)}, u32[]{:S(2)}, u32[]{:S(2)}) collective-permute-start(bf16[2,2,64,128]{3,2,1,0:T(8,128)(2,1)S(1)} %pad_maximum_fusion.7), channel_id=1, source_target_pairs={{0,16},{8,24},{16,0},{24,8},{1,17},{9,25},{17,1},{25,9},{2,18},{10... | collective-permute-start | bytes 196616 | tf_op jit(solution)/shard_map/ppermute | solution.py:351
  40.1 1.1 %collective-permute-start.17 = (bf16[2,2,64,128]{3,2,1,0:T(8,128)(2,1)S(1)}, bf16[2,2,64,128]{3,2,1,0:T(8,128)(2,1)S(1)}, u32[]{:S(2)}, u32[]{:S(2)}) collective-permute-start(bf16[2,2,64,128]{3,2,1,0:T(8,128)(2,1)S(1)} %pad_maximum_fusion.8), channel_id=1, source_target_pairs={{0,8},{8,0},{16,24},{24,16},{1,9},{9,1},{17,25},{25,17},{2,10},{10... | collective-permute-start | bytes 196616 | tf_op jit(solution)/shard_map/ppermute | solution.py:351
  41.2 0.4 collective-permute-done.20.refs_3_
  41.5 1.8 %collective-permute-start.18 = (bf16[2,2,64,128]{3,2,1,0:T(8,128)(2,1)S(1)}, bf16[2,2,64,128]{3,2,1,0:T(8,128)(2,1)S(1)}, u32[]{:S(2)}, u32[]{:S(2)}) collective-permute-start(bf16[2,2,64,128]{3,2,1,0:T(8,128)(2,1)S(1)} %pad_maximum_fusion.9), channel_id=1, source_target_pairs={{0,24},{8,16},{16,8},{24,0},{1,25},{9,17},{17,9},{25,1},{2,26},{10... | collective-permute-start | bytes 196616 | tf_op jit(solution)/shard_map/ppermute | solution.py:351
  43.4 1.1 %collective-permute-done.21.refs_4_ = bf16[2,256,128]{2,1,0:T(8,128)(2,1)S(1)} collective-permute-done((bf16[2,256,128]{2,1,0:T(8,128)(2,1)S(1)}, bf16[2,256,128]{2,1,0:T(8,128)(2,1)S(1)}, u32[]{:S(2)}, u32[]{:S(2)}) %collective-permute-start.21) | collective-permute-done | bytes 131104 | tf_op jit(solution)/shard_map/ppermute | solution.py:351
  44.6 0.0 collective-permute-done.16.refs_2_.refs_1_
  44.6 0.2 collective-permute-done.17.refs_3_.refs_2_
  44.8 2.8 %collective-permute-done.18.refs_4_.refs_3_ = bf16[2,2,64,128]{3,2,1,0:T(8,128)(2,1)S(1)} collective-permute-done((bf16[2,2,64,128]{3,2,1,0:T(8,128)(2,1)S(1)}, bf16[2,2,64,128]{3,2,1,0:T(8,128)(2,1)S(1)}, u32[]{:S(2)}, u32[]{:S(2)}) %collective-permute-start.18) | collective-permute-done | bytes 65568 | tf_op jit(solution)/shard_map/ppermute | solution.py:351
  47.6 0.0 collective-permute-start.23
  47.7 1.1 %collective-permute-start.19 = (bf16[2,64,128]{2,1,0:T(8,128)(2,1)S(1)}, bf16[2,64,128]{2,1,0:T(8,128)(2,1)S(1)}, u32[]{:S(2)}, u32[]{:S(2)}) collective-permute-start(bf16[2,64,128]{2,1,0:T(8,128)(2,1)S(1)} %get-tuple-element.31), channel_id=1, source_target_pairs={{0,4},{4,0},{1,5},{5,1},{2,6},{6,2},{3,7},{7,3},{8,12},{12,8},{9,1... | collective-permute-start | bytes 98312 | tf_op jit(solution)/shard_map/ppermute | solution.py:351
  48.7 2.9 %collective-permute-done.19.refs_1_ = bf16[2,64,128]{2,1,0:T(8,128)(2,1)S(1)} collective-permute-done((bf16[2,64,128]{2,1,0:T(8,128)(2,1)S(1)}, bf16[2,64,128]{2,1,0:T(8,128)(2,1)S(1)}, u32[]{:S(2)}, u32[]{:S(2)}) %collective-permute-start.19) | collective-permute-done | bytes 32800 | tf_op jit(solution)/shard_map/ppermute | solution.py:351
  51.6 1.0 %shard_map.112 = (bf16[256,128]{1,0:T(8,128)(2,1)}, bf16[128,1024]{1,0:T(8,128)(2,1)}, bf16[128,1024]{1,0:T(8,128)(2,1)}) custom-call(bf16[2,64,128]{2,1,0:T(8,128)(2,1)S(1)} %get-tuple-element.30.refs_0_, bf16[2,64,128]{2,1,0:T(8,128)(2,1)S(1)} %collective-permute-done.19.refs_1_, bf16[2,256,128]{2,1,0:T(8,128)(2,1)S(1)} %get-tuple-element.32.refs_2_, ...), custom_call_target="tpu_custom_call" | custom-call | tf_op jit(solution)/shard_map/pallas_call | solution.py:499
  (35 shorter events, 0.4 us)
Async XLA Ops:
  2.0 5.4 %collective-permute-start = (bf16[2,144,128]{2,1,0:T(8,128)(2,1)S(1)}, bf16[2,144,128]{2,1,0:T(8,128)(2,1)S(1)}, u32[]{:S(2)}, u32[]{:S(2)}) collective-permute-start(bf16[2,144,128]{2,1,0:T(8,128)(2,1)S(1)} %get-tuple-element.22), channel_id=1, source_target_pairs={{0,4},{4,0},{1,5},{5,1},{2,6},{6,2},{3,7},{7,3},{8,12},{12,8},{9,1... | collective-permute-start | bytes 221192 | tf_op jit(solution)/shard_map/ppermute | solution.py:351
  5.0 5.5 %collective-permute-start.3 = (bf16[4,256,128]{2,1,0:T(8,128)(2,1)S(1)}, bf16[4,256,128]{2,1,0:T(8,128)(2,1)S(1)}, u32[]{:S(2)}, u32[]{:S(2)}) collective-permute-start(bf16[4,256,128]{2,1,0:T(8,128)(2,1)S(1)} %get-tuple-element.24), channel_id=1, source_target_pairs={{0,2},{1,3},{2,0},{3,1},{4,6},{5,7},{6,4},{7,5},{8,10},{9,11},{10,... | collective-permute-start | bytes 786440 | tf_op jit(solution)/shard_map/ppermute | solution.py:351
  7.4 9.3 %collective-permute-start.2 = (bf16[4,144,128]{2,1,0:T(8,128)(2,1)S(1)}, bf16[4,144,128]{2,1,0:T(8,128)(2,1)S(1)}, u32[]{:S(2)}, u32[]{:S(2)}) collective-permute-start(bf16[4,144,128]{2,1,0:T(8,128)(2,1)S(1)} %pad_maximum_fusion.1.refs_0_), channel_id=1, source_target_pairs={{0,16},{8,24},{16,0},{24,8},{1,17},{9,25},{17,1},{25,9},{2,18},{10... | collective-permute-start | bytes 442376 | tf_op jit(solution)/shard_map/ppermute | solution.py:351
  10.6 6.4 %collective-permute-start.4 = (bf16[2,256,128]{2,1,0:T(8,128)(2,1)S(1)}, bf16[2,256,128]{2,1,0:T(8,128)(2,1)S(1)}, u32[]{:S(2)}, u32[]{:S(2)}) collective-permute-start(bf16[2,256,128]{2,1,0:T(8,128)(2,1)S(1)} %pad_maximum_fusion.2), channel_id=1, source_target_pairs={{0,1},{1,0},{2,3},{3,2},{4,5},{5,4},{6,7},{7,6},{8,9},{9,8},{10,11... | collective-permute-start | bytes 393224 | tf_op jit(solution)/shard_map/ppermute | solution.py:351
  12.2 6.1 %collective-permute-start.5 = (bf16[2,256,128]{2,1,0:T(8,128)(2,1)S(1)}, bf16[2,256,128]{2,1,0:T(8,128)(2,1)S(1)}, u32[]{:S(2)}, u32[]{:S(2)}) collective-permute-start(bf16[2,256,128]{2,1,0:T(8,128)(2,1)S(1)} %pad_maximum_fusion.3), channel_id=1, source_target_pairs={{0,4},{1,5},{2,6},{3,7},{4,0},{5,1},{6,2},{7,3},{8,12},{9,13},{10,... | collective-permute-start | bytes 393224 | tf_op jit(solution)/shard_map/ppermute | solution.py:351
  13.8 5.9 %collective-permute-start.6 = (bf16[2,256,128]{2,1,0:T(8,128)(2,1)S(1)}, bf16[2,256,128]{2,1,0:T(8,128)(2,1)S(1)}, u32[]{:S(2)}, u32[]{:S(2)}) collective-permute-start(bf16[2,256,128]{2,1,0:T(8,128)(2,1)S(1)} %pad_maximum_fusion.4), channel_id=1, source_target_pairs={{0,5},{1,4},{2,7},{3,6},{4,1},{5,0},{6,3},{7,2},{8,13},{9,12},{10,... | collective-permute-start | bytes 393224 | tf_op jit(solution)/shard_map/ppermute | solution.py:351
  15.0 6.4 %collective-permute-start.8 = (bf16[4,144,128]{2,1,0:T(8,128)(2,1)S(1)}, bf16[4,144,128]{2,1,0:T(8,128)(2,1)S(1)}, u32[]{:S(2)}, u32[]{:S(2)}) collective-permute-start(bf16[4,144,128]{2,1,0:T(8,128)(2,1)S(1)} %pad_maximum_fusion.1.refs_0_), channel_id=1, source_target_pairs={{0,8},{8,0},{16,24},{24,16},{1,9},{9,1},{17,25},{25,17},{2,10},{10... | collective-permute-start | bytes 442376 | tf_op jit(solution)/shard_map/ppermute | solution.py:351
  19.7 5.1 %collective-permute-start.10 = (bf16[4,144,128]{2,1,0:T(8,128)(2,1)S(1)}, bf16[4,144,128]{2,1,0:T(8,128)(2,1)S(1)}, u32[]{:S(2)}, u32[]{:S(2)}) collective-permute-start(bf16[4,144,128]{2,1,0:T(8,128)(2,1)S(1)} %shard_map.104.refs_2_), channel_id=1, source_target_pairs={{0,8},{8,0},{16,24},{24,16},{1,9},{9,1},{17,25},{25,17},{2,10},{10... | collective-permute-start | bytes 442376 | tf_op jit(solution)/shard_map/ppermute | solution.py:351
  21.3 1.3 %collective-permute-start.1 = (bf16[2,144,128]{2,1,0:T(8,128)(2,1)S(1)}, bf16[2,144,128]{2,1,0:T(8,128)(2,1)S(1)}, u32[]{:S(2)}, u32[]{:S(2)}) collective-permute-start(bf16[2,144,128]{2,1,0:T(8,128)(2,1)S(1)} %pad_maximum_fusion.6), channel_id=1, source_target_pairs={{0,2},{2,0},{1,3},{3,1},{4,6},{6,4},{5,7},{7,5},{8,10},{10,8},{9,1... | collective-permute-start | bytes 221192 | tf_op jit(solution)/shard_map/ppermute | solution.py:351
  21.4 1.5 %collective-permute-start.9 = (bf16[2,144,128]{2,1,0:T(8,128)(2,1)S(1)}, bf16[2,144,128]{2,1,0:T(8,128)(2,1)S(1)}, u32[]{:S(2)}, u32[]{:S(2)}) collective-permute-start(bf16[2,144,128]{2,1,0:T(8,128)(2,1)S(1)} %slice.108), channel_id=1, source_target_pairs={{0,2},{2,0},{1,3},{3,1},{4,6},{6,4},{5,7},{7,5},{8,10},{10,8},{9,1... | collective-permute-start | bytes 221192 | tf_op jit(solution)/shard_map/ppermute | solution.py:351
  22.0 1.3 %collective-permute-start.7 = (bf16[2,144,128]{2,1,0:T(8,128)(2,1)S(1)}, bf16[2,144,128]{2,1,0:T(8,128)(2,1)S(1)}, u32[]{:S(2)}, u32[]{:S(2)}) collective-permute-start(bf16[2,144,128]{2,1,0:T(8,128)(2,1)S(1)} %slice.107), channel_id=1, source_target_pairs={{0,2},{2,0},{1,3},{3,1},{4,6},{6,4},{5,7},{7,5},{8,10},{10,8},{9,1... | collective-permute-start | bytes 221192 | tf_op jit(solution)/shard_map/ppermute | solution.py:351
  24.9 1.3 %collective-permute-start.11 = (bf16[2,144,128]{2,1,0:T(8,128)(2,1)S(1)}, bf16[2,144,128]{2,1,0:T(8,128)(2,1)S(1)}, u32[]{:S(2)}, u32[]{:S(2)}) collective-permute-start(bf16[2,144,128]{2,1,0:T(8,128)(2,1)S(1)} %slice.110), channel_id=1, source_target_pairs={{0,2},{2,0},{1,3},{3,1},{4,6},{6,4},{5,7},{7,5},{8,10},{10,8},{9,1... | collective-permute-start | bytes 221192 | tf_op jit(solution)/shard_map/ppermute | solution.py:351
  26.8 6.5 %collective-permute-start.14 = (f32[8,128]{1,0:T(8,128)S(1)}, f32[8,128]{1,0:T(8,128)S(1)}, u32[]{:S(2)}, u32[]{:S(2)}) collective-permute-start(f32[8,128]{1,0:T(8,128)S(1)} %shard_map.107.refs_12_.refs_11_), channel_id=1, source_target_pairs={{0,24},{8,16},{16,8},{24,0},{1,25},{9,17},{17,9},{25,1},{2,26},{10... | collective-permute-start | bytes 12296 | tf_op jit(solution)/shard_map/ppermute | solution.py:351
  28.3 5.1 %collective-permute-start.13 = (f32[8,128]{1,0:T(8,128)S(1)}, f32[8,128]{1,0:T(8,128)S(1)}, u32[]{:S(2)}, u32[]{:S(2)}) collective-permute-start(f32[8,128]{1,0:T(8,128)S(1)} %shard_map.107.refs_12_.refs_11_), channel_id=1, source_target_pairs={{0,16},{8,24},{16,0},{24,8},{1,17},{9,25},{17,1},{25,9},{2,18},{10... | collective-permute-start | bytes 12296 | tf_op jit(solution)/shard_map/ppermute | solution.py:351
  30.0 3.6 %collective-permute-start.12 = (f32[8,128]{1,0:T(8,128)S(1)}, f32[8,128]{1,0:T(8,128)S(1)}, u32[]{:S(2)}, u32[]{:S(2)}) collective-permute-start(f32[8,128]{1,0:T(8,128)S(1)} %shard_map.107.refs_12_.refs_11_), channel_id=1, source_target_pairs={{0,8},{8,0},{16,24},{24,16},{1,9},{9,1},{17,25},{25,17},{2,10},{10... | collective-permute-start | bytes 12296 | tf_op jit(solution)/shard_map/ppermute | solution.py:351
  35.1 3.6 %collective-permute-start.15 = (bf16[4,2,64,128]{3,2,1,0:T(8,128)(2,1)S(1)}, bf16[4,2,64,128]{3,2,1,0:T(8,128)(2,1)S(1)}, u32[]{:S(2)}, u32[]{:S(2)}) collective-permute-start(bf16[4,2,64,128]{3,2,1,0:T(8,128)(2,1)S(1)} %get-tuple-element.29), channel_id=1, source_target_pairs={{0,2},{2,0},{1,3},{3,1},{4,6},{6,4},{5,7},{7,5},{8,10},{10,8},{9,1... | collective-permute-start | bytes 393224 | tf_op jit(solution)/shard_map/ppermute | solution.py:351
  35.1 6.4 %collective-permute-start.20 = (bf16[2,256,128]{2,1,0:T(8,128)(2,1)S(1)}, bf16[2,256,128]{2,1,0:T(8,128)(2,1)S(1)}, u32[]{:S(2)}, u32[]{:S(2)}) collective-permute-start(bf16[2,256,128]{2,1,0:T(8,128)(2,1)S(1)} %get-tuple-element.33), channel_id=1, source_target_pairs={{0,1},{1,0},{2,3},{3,2},{4,5},{5,4},{6,7},{7,6},{8,9},{9,8},{10,11... | collective-permute-start | bytes 393224 | tf_op jit(solution)/shard_map/ppermute | solution.py:351
  36.1 8.4 %collective-permute-start.21 = (bf16[2,256,128]{2,1,0:T(8,128)(2,1)S(1)}, bf16[2,256,128]{2,1,0:T(8,128)(2,1)S(1)}, u32[]{:S(2)}, u32[]{:S(2)}) collective-permute-start(bf16[2,256,128]{2,1,0:T(8,128)(2,1)S(1)} %get-tuple-element.34), channel_id=1, source_target_pairs={{0,4},{1,5},{2,6},{3,7},{4,0},{5,1},{6,2},{7,3},{8,12},{9,13},{10,... | collective-permute-start | bytes 393224 | tf_op jit(solution)/shard_map/ppermute | solution.py:351
  37.1 7.4 %collective-permute-start.22 = (bf16[2,256,128]{2,1,0:T(8,128)(2,1)S(1)}, bf16[2,256,128]{2,1,0:T(8,128)(2,1)S(1)}, u32[]{:S(2)}, u32[]{:S(2)}) collective-permute-start(bf16[2,256,128]{2,1,0:T(8,128)(2,1)S(1)} %get-tuple-element.35), channel_id=1, source_target_pairs={{0,5},{1,4},{2,7},{3,6},{4,1},{5,0},{6,3},{7,2},{8,13},{9,12},{10,... | collective-permute-start | bytes 393224 | tf_op jit(solution)/shard_map/ppermute | solution.py:351
  38.7 5.8 %collective-permute-start.16 = (bf16[2,2,64,128]{3,2,1,0:T(8,128)(2,1)S(1)}, bf16[2,2,64,128]{3,2,1,0:T(8,128)(2,1)S(1)}, u32[]{:S(2)}, u32[]{:S(2)}) collective-permute-start(bf16[2,2,64,128]{3,2,1,0:T(8,128)(2,1)S(1)} %pad_maximum_fusion.7), channel_id=1, source_target_pairs={{0,16},{8,24},{16,0},{24,8},{1,17},{9,25},{17,1},{25,9},{2,18},{10... | collective-permute-start | bytes 196616 | tf_op jit(solution)/shard_map/ppermute | solution.py:351
  40.1 4.7 %collective-permute-start.17 = (bf16[2,2,64,128]{3,2,1,0:T(8,128)(2,1)S(1)}, bf16[2,2,64,128]{3,2,1,0:T(8,128)(2,1)S(1)}, u32[]{:S(2)}, u32[]{:S(2)}) collective-permute-start(bf16[2,2,64,128]{3,2,1,0:T(8,128)(2,1)S(1)} %pad_maximum_fusion.8), channel_id=1, source_target_pairs={{0,8},{8,0},{16,24},{24,16},{1,9},{9,1},{17,25},{25,17},{2,10},{10... | collective-permute-start | bytes 196616 | tf_op jit(solution)/shard_map/ppermute | solution.py:351
  41.5 6.1 %collective-permute-start.18 = (bf16[2,2,64,128]{3,2,1,0:T(8,128)(2,1)S(1)}, bf16[2,2,64,128]{3,2,1,0:T(8,128)(2,1)S(1)}, u32[]{:S(2)}, u32[]{:S(2)}) collective-permute-start(bf16[2,2,64,128]{3,2,1,0:T(8,128)(2,1)S(1)} %pad_maximum_fusion.9), channel_id=1, source_target_pairs={{0,24},{8,16},{16,8},{24,0},{1,25},{9,17},{17,9},{25,1},{2,26},{10... | collective-permute-start | bytes 196616 | tf_op jit(solution)/shard_map/ppermute | solution.py:351
  47.6 4.0 %collective-permute-start.23 = (bf16[4,256,128]{2,1,0:T(8,128)(2,1)S(1)}, bf16[4,256,128]{2,1,0:T(8,128)(2,1)S(1)}, u32[]{:S(2)}, u32[]{:S(2)}) collective-permute-start(bf16[4,256,128]{2,1,0:T(8,128)(2,1)S(1)} %shard_map.111), channel_id=1, source_target_pairs={{0,2},{1,3},{2,0},{3,1},{4,6},{5,7},{6,4},{7,5},{8,10},{9,11},{10,... | collective-permute-start | bytes 786440 | tf_op jit(solution)/shard_map/ppermute | solution.py:351
  47.7 4.0 %collective-permute-start.19 = (bf16[2,64,128]{2,1,0:T(8,128)(2,1)S(1)}, bf16[2,64,128]{2,1,0:T(8,128)(2,1)S(1)}, u32[]{:S(2)}, u32[]{:S(2)}) collective-permute-start(bf16[2,64,128]{2,1,0:T(8,128)(2,1)S(1)} %get-tuple-element.31), channel_id=1, source_target_pairs={{0,4},{4,0},{1,5},{5,1},{2,6},{6,2},{3,7},{7,3},{8,12},{12,8},{9,1... | collective-permute-start | bytes 98312 | tf_op jit(solution)/shard_map/ppermute | solution.py:351

commit v10 on v9

--- a/solution.py
+++ b/solution.py
@@ -277,7 +277,8 @@
     dkv_refs, (*dq_refs, dk_acc, dv_acc) = refs[: len(KEEP)], refs[len(KEEP) :]
     lines = (row_refs[0].shape[1] - STAT_ROWS) // 2
     all_slabs = block_slabs(blocks, nears, row_refs)
-    size = len(all_slabs[0]) * lines
+    groups = len(all_slabs[0])
+    size = groups * lines
     for first, count, held, slabs in steps_of(blocks, all_slabs, lines):
         lanes = slice(first, first + count)
         part_lse = [lse_lines(ref, at, held, size) for ref in lse_refs]
@@ -289,7 +290,8 @@
         dq = (dq_ref[:, lanes] * (weight * SCALE)).T.astype(jnp.bfloat16)
         sources = [(b, slab) for b in held for slab in all_slabs[blocks.index(b)]]
         for m, (b, (_, _, n, j)) in enumerate(sources):
-            dq_refs[n][blocks.index(b), j] = dq[m * lines : (m + 1) * lines]
+            source = (at[3] ^ b) * (groups // nears) + (at[1] ^ j)
+            dq_refs[n][source] = dq[m * lines : (m + 1) * lines]
         weight_t = jnp.broadcast_to(weight, (DH, count)).T
         q, o_grad = (
             (lines_of(slabs, start, lines).astype(jnp.float32) * weight_t).astype(jnp.bfloat16)
@@ -311,38 +313,39 @@
                     dkv_refs[i][n, tokens : 2 * tokens, :] = dv[inner].astype(jnp.bfloat16)
 
 
-def add_query_kernel(nears, *refs):
-    own_refs, came_refs, out_refs = refs[:nears], refs[nears:-2], refs[-2:]
-    for n in range(nears):
-        for j in range(own_refs[0].shape[1]):
-            total = own_refs[n][0, j].astype(jnp.float32)
-            for ref in came_refs:
-                total = total + ref[n, j].astype(jnp.float32)
-            out_refs[min(j, 1)][n] = total.astype(jnp.bfloat16)
+def join_kernel(*refs):
+    for n, ref in enumerate(refs[:-1]):
+        refs[-1][:, n] = ref[...]
 
 
 def tie_kernel(*refs):
     pass
 
 
-def write_kernel(nears, heads, *refs):
+def write_kernel(row_count, nears, heads, *refs):
     at = place(nears, heads)
-    slab_refs, refs = refs[: -len(KEEP) - 5], refs[-len(KEEP) - 5 :]
-    pair_refs, (came_ref, out_q_ref, out_k_ref, out_v_ref, sems) = refs[: len(KEEP)], refs[len(KEEP) :]
-    groups, lines, tokens = len(slab_refs) * nears, slab_refs[0].shape[1], out_k_ref.shape[0]
+    dq_ref, pair_refs, refs = refs[0], refs[1 : 1 + len(KEEP)], refs[1 + len(KEEP) :]
+    came_ref, out_q_ref, out_k_ref, out_v_ref, sum_ref, sems = refs
+    groups, lines, tokens = row_count * nears, dq_ref.shape[2], out_k_ref.shape[0]
     copies = []
     for i, ref in enumerate(pair_refs):
         for source, other in ((ref.at[0], 0), (came_ref.at[i], FIRST)):
             columns = pl.ds(column_of(at[0] ^ KEEP[i] ^ other, groups, heads), DH)
             copies.append((source.at[0:tokens, :], out_k_ref.at[:, columns]))
             copies.append((source.at[tokens : 2 * tokens, :], out_v_ref.at[:, columns]))
-    for j, ref in enumerate(slab_refs):
+    for row in range(row_count):
         for n in range(nears):
-            first = pl.multiple_of(group_at(at, j, n, nears) * lines, lines)
-            copies.append((ref.at[n], out_q_ref.at[pl.ds(first, lines), :]))
+            first = pl.multiple_of((row * nears + (at[2] ^ n)) * lines, lines)
+            copies.append((sum_ref.at[row * nears + n], out_q_ref.at[pl.ds(first, lines), :]))
     copies = [pltpu.make_async_copy(s, t, sems.at[n]) for n, (s, t) in enumerate(copies)]
-    for copy in copies:
+    for copy in copies[:-groups]:
         copy.start()
+    for g in range(groups):
+        total = dq_ref[g // nears, g % nears].astype(jnp.float32)
+        for source in range(g // nears + row_count, dq_ref.shape[0], row_count):
+            total = total + dq_ref[source, g % nears].astype(jnp.float32)
+        sum_ref[g] = total.astype(jnp.bfloat16)
+        copies[g - groups].start()
     for copy in copies:
         copy.wait()
 
@@ -371,9 +374,8 @@
 
 def swap_back(pairs, after):
     members = ("row", "near", "head")
-    pairs = [swap(x, members, j, KVH) if j else x for x, j in zip(pairs, KEEP)]
-    beyond = tie(jnp.stack([x[1] for x in pairs]), after)
-    return [*pairs, swap(beyond, members, FIRST, KVH)]
+    pairs = [tie(swap(x, members, j, KVH), after) if j else x for x, j in zip(pairs, KEEP)]
+    return [*pairs, swap(jnp.stack([x[1] for x in pairs]), members, FIRST, KVH)]
 
 
 def line_limits(parts, row_count, nears, rows, lines, resp_len, prompt_end):
@@ -472,7 +474,7 @@
         out_shape=[score_shape] * 2 + [jax.ShapeDtypeStruct((DH, all_lines), jnp.float32)],
         compiler_params=PARAMS,
     )(ends, *row_refs, *pairs, *lse)
-    dq_shape = jax.ShapeDtypeStruct((parts, row_count, lines, DH), jnp.bfloat16)
+    dq_shape = jax.ShapeDtypeStruct((parts * row_count, lines, DH), jnp.bfloat16)
     acc = pltpu.VMEM((len(KEEP), 2 * tokens, DH), jnp.float32)
     outs = pl.pallas_call(
         functools.partial(token_kernel, blocks, nears, heads, tokens),
@@ -484,30 +486,29 @@
     )(live, *row_refs, prob, dscore, dq, *every_lse)
     dkv, dq = outs[: len(KEEP)], outs[len(KEEP) :]
     dq = [swap(x, "near", n, nears) if n else x for n, x in enumerate(dq)]
-    from_parts = [
-        swap(jnp.stack([x[at] for x in dq]), "part", b, parts) for at, b in enumerate(blocks) if b
-    ]
-    sum_shape = jax.ShapeDtypeStruct((nears, lines, DH), jnp.bfloat16)
-    sums = pl.pallas_call(
-        functools.partial(add_query_kernel, nears),
-        in_specs=[VMEM] * (nears + len(from_parts)),
-        out_shape=[sum_shape] * 2,
+    dq = pl.pallas_call(
+        join_kernel,
+        in_specs=[VMEM] * nears,
+        out_shape=jax.ShapeDtypeStruct((parts * row_count, nears, lines, DH), jnp.bfloat16),
         compiler_params=PARAMS,
-    )(*dq, *from_parts)
-    pairs = swap_back(dkv, from_parts)
-    sums = [swap(x, "row", j, row_count) if j else x for j, x in enumerate(sums[:row_count])]
+    )(*dq)
+    pairs = swap_back(dkv, [dq])
+    dq = lax.all_to_all(dq, ("part", "row"), split_axis=0, concat_axis=0, tiled=True)
     out_q, out_k, out_v = pl.pallas_call(
-        functools.partial(write_kernel, nears, heads),
-        in_specs=[VMEM] * (row_count + len(pairs)),
+        functools.partial(write_kernel, row_count, nears, heads),
+        in_specs=[VMEM] * (1 + len(pairs)),
         out_specs=[HBM] * 3,
         out_shape=[
             jax.ShapeDtypeStruct((own_lines, DH), jnp.bfloat16),
             jax.ShapeDtypeStruct(keys.shape, jnp.bfloat16),
             jax.ShapeDtypeStruct(values.shape, jnp.bfloat16),
         ],
-        scratch_shapes=[pltpu.SemaphoreType.DMA((4 * len(KEEP) + groups,))],
+        scratch_shapes=[
+            pltpu.VMEM((groups, lines, DH), jnp.bfloat16),
+            pltpu.SemaphoreType.DMA((4 * len(KEEP) + groups,)),
+        ],
         compiler_params=PARAMS,
-    )(*sums, *pairs)
+    )(dq, *pairs)
     out_q = out_q.reshape(own_heads, rows, DH).transpose(1, 0, 2).reshape(rows, own_heads * DH)
     return out_q, out_k, out_v
 

time: 52.8 us -> 53 us (level)
  starting transfers between devices: 27.2 us -> 25.4 us
  waiting for transfers between devices: 15.2 us -> 16.5 us
  Pallas kernels: 7.67 us -> 8.37 us
    all_to_all x0 -> x1, waiting for transfers between devices: none -> 5.57 us  [shards(): lax.all_to_all(dq, ('part', 'row'), split_axis=0, concat_axis=0, tiled=True)]
    ppermute x24 -> x20, starting transfers between devices: 27.2 us -> 22 us  [swap(): return lax.ppermute(x, axis, [(i, i ^ distance) for i in range(size)])]
    ppermute x24 -> x20, waiting for transfers between devices: 15.2 us -> 10.9 us  [swap(): return lax.ppermute(x, axis, [(i, i ^ distance) for i in range(size)])]
    all_to_all x0 -> x1, starting transfers between devices: none -> 3.42 us  [shards(): lax.all_to_all(dq, ('part', 'row'), split_axis=0, concat_axis=0, tiled=True)]
    pallas_call x2, Pallas kernels: 1 us -> 1.7 us  [the longest x1 0.98 us: shards(): pl.pallas_call(functools.partial(write_kernel, row_count, nears, heads),...]
  transfers between devices with their start and end apart: 24 -> 21, of which waited for: 15 -> 13; matrix products, arithmetic and copies ran while one was open for 1% -> 1% of each run, Pallas kernels for 6% -> 7%
where the time goes in v10:
time: 53 us; the launch traced here: 52.7 us
  starting transfers between devices  25.4 us (48%)
  waiting for transfers between devices  16.5 us (31%)
  Pallas kernels  8.37 us (16%)
  between operations  2.15 us (4%)
    ppermute x20, starting transfers between devices, swap(): return lax.ppermute(x, axis, [(i, i ^ distance) for i in range(size)])  22 us
    ppermute x20, waiting for transfers between devices, swap(): return lax.ppermute(x, axis, [(i, i ^ distance) for i in range(size)])  10.9 us
    all_to_all x1, waiting for transfers between devices, shards(): lax.all_to_all(dq, ('part', 'row'), split_axis=0, concat_axis=0, tiled=True)  5.57 us
    all_to_all x1, starting transfers between devices, shards(): lax.all_to_all(dq, ('part', 'row'), split_axis=0, concat_axis=0, tiled=True)  3.42 us
    pallas_call x1, Pallas kernels, shards(): pl.pallas_call(functools.partial(part_kernel, blocks, nears, heads, token...  2.04 us
    pallas_call x2, Pallas kernels, part_lse(): pl.pallas_call(functools.partial(stat_kernel, held, first, nears, heads,...  1.76 us
    pallas_call x1, Pallas kernels, shards(): pl.pallas_call(functools.partial(token_kernel, blocks, nears, heads, toke...  1.48 us
    pallas_call x1, Pallas kernels, shards(): pl.pallas_call(functools.partial(pack_kernel, row_count, nears, heads), i...  1.37 us
  transfers between devices with their start and end apart: 21, of which 13 were waited for; matrix products, arithmetic and copies ran while one was open for 1% of the time, Pallas kernels for 7%

profile of v10, /device:TPU:0, one launch (start us, length us, event | category | flops | bytes accessed | tf_op | source)
XLA Modules:
  0.0 52.7 jit_solution(11286683895554048832)
XLA Ops:
  0.6 1.4 %shard_map.103 = (bf16[2,144,128]{2,1,0:T(8,128)(2,1)S(1)}, bf16[2,144,128]{2,1,0:T(8,128)(2,1)S(1)}, bf16[4,256,128]{2,1,0:T(8,128)(2,1)S(1)}, bf16[4,256,128]{2,1,0:T(8,128)(2,1)S(1)}) custom-call(bf16[256,128]{1,0:T(8,128)(2,1)} %bitcast.24, bf16[256,128]{1,0:T(8,128)(2,1)} %bitcast.25, bf16[256,128]{1,0:T(8,128)(2,1)} %bitcast.26, f32[4,64]{1,0:T(4,128)} %lse_hbm.1, ...), custom_call_target="tpu_custom_call" | custom-call | tf_op jit(solution)/shard_map/pallas_call | solution.py:417
  2.0 3.0 %collective-permute-start = (bf16[2,144,128]{2,1,0:T(8,128)(2,1)S(1)}, bf16[2,144,128]{2,1,0:T(8,128)(2,1)S(1)}, u32[]{:S(2)}, u32[]{:S(2)}) collective-permute-start(bf16[2,144,128]{2,1,0:T(8,128)(2,1)S(1)} %get-tuple-element.20), channel_id=1, source_target_pairs={{0,4},{4,0},{1,5},{5,1},{2,6},{6,2},{3,7},{7,3},{8,12},{12,8},{9,1... | collective-permute-start | bytes 221192 | tf_op jit(solution)/shard_map/ppermute | solution.py:354
  5.0 0.0 collective-permute-start.3
  5.1 2.3 %collective-permute-done = bf16[2,144,128]{2,1,0:T(8,128)(2,1)S(1)} collective-permute-done((bf16[2,144,128]{2,1,0:T(8,128)(2,1)S(1)}, bf16[2,144,128]{2,1,0:T(8,128)(2,1)S(1)}, u32[]{:S(2)}, u32[]{:S(2)}) %collective-permute-start) | collective-permute-done | bytes 73760 | tf_op jit(solution)/shard_map/ppermute | solution.py:354
  7.4 3.2 %collective-permute-start.2 = (bf16[4,144,128]{2,1,0:T(8,128)(2,1)S(1)}, bf16[4,144,128]{2,1,0:T(8,128)(2,1)S(1)}, u32[]{:S(2)}, u32[]{:S(2)}) collective-permute-start(bf16[4,144,128]{2,1,0:T(8,128)(2,1)S(1)} %pad_maximum_fusion.1.refs_0_), channel_id=1, source_target_pairs={{0,16},{8,24},{16,0},{24,8},{1,17},{9,25},{17,1},{25,9},{2,18},{10... | collective-permute-start | bytes 442376 | tf_op jit(solution)/shard_map/ppermute | solution.py:354
  10.6 0.0 collective-permute-done.3
  10.6 1.6 %collective-permute-start.4 = (bf16[2,256,128]{2,1,0:T(8,128)(2,1)S(1)}, bf16[2,256,128]{2,1,0:T(8,128)(2,1)S(1)}, u32[]{:S(2)}, u32[]{:S(2)}) collective-permute-start(bf16[2,256,128]{2,1,0:T(8,128)(2,1)S(1)} %pad_maximum_fusion.2), channel_id=1, source_target_pairs={{0,1},{1,0},{2,3},{3,2},{4,5},{5,4},{6,7},{7,6},{8,9},{9,8},{10,11... | collective-permute-start | bytes 393224 | tf_op jit(solution)/shard_map/ppermute | solution.py:354
  12.2 1.6 %collective-permute-start.5 = (bf16[2,256,128]{2,1,0:T(8,128)(2,1)S(1)}, bf16[2,256,128]{2,1,0:T(8,128)(2,1)S(1)}, u32[]{:S(2)}, u32[]{:S(2)}) collective-permute-start(bf16[2,256,128]{2,1,0:T(8,128)(2,1)S(1)} %pad_maximum_fusion.3), channel_id=1, source_target_pairs={{0,4},{1,5},{2,6},{3,7},{4,0},{5,1},{6,2},{7,3},{8,12},{9,13},{10,... | collective-permute-start | bytes 393224 | tf_op jit(solution)/shard_map/ppermute | solution.py:354
  13.8 0.5 %collective-permute-start.6 = (bf16[2,256,128]{2,1,0:T(8,128)(2,1)S(1)}, bf16[2,256,128]{2,1,0:T(8,128)(2,1)S(1)}, u32[]{:S(2)}, u32[]{:S(2)}) collective-permute-start(bf16[2,256,128]{2,1,0:T(8,128)(2,1)S(1)} %pad_maximum_fusion.4), channel_id=1, source_target_pairs={{0,5},{1,4},{2,7},{3,6},{4,1},{5,0},{6,3},{7,2},{8,13},{9,12},{10,... | collective-permute-start | bytes 393224 | tf_op jit(solution)/shard_map/ppermute | solution.py:354
  15.0 1.6 %collective-permute-start.8 = (bf16[4,144,128]{2,1,0:T(8,128)(2,1)S(1)}, bf16[4,144,128]{2,1,0:T(8,128)(2,1)S(1)}, u32[]{:S(2)}, u32[]{:S(2)}) collective-permute-start(bf16[4,144,128]{2,1,0:T(8,128)(2,1)S(1)} %pad_maximum_fusion.1.refs_0_), channel_id=1, source_target_pairs={{0,8},{8,0},{16,24},{24,16},{1,9},{9,1},{17,25},{25,17},{2,10},{10... | collective-permute-start | bytes 442376 | tf_op jit(solution)/shard_map/ppermute | solution.py:354
  16.7 0.0 collective-permute-done.2.refs_0_
  16.7 0.4 collective-permute-done.4.refs_1_.refs_7_.refs_3_.refs_9_
  17.0 1.3 %collective-permute-done.5.refs_2_.refs_8_.refs_4_.refs_10_ = bf16[2,256,128]{2,1,0:T(8,128)(2,1)S(1)} collective-permute-done((bf16[2,256,128]{2,1,0:T(8,128)(2,1)S(1)}, bf16[2,256,128]{2,1,0:T(8,128)(2,1)S(1)}, u32[]{:S(2)}, u32[]{:S(2)}) %collective-permute-start.5) | collective-permute-done | bytes 131104 | tf_op jit(solution)/shard_map/ppermute | solution.py:354
  18.3 1.4 %collective-permute-done.6.refs_3_.refs_9_.refs_5_.refs_11_ = bf16[2,256,128]{2,1,0:T(8,128)(2,1)S(1)} collective-permute-done((bf16[2,256,128]{2,1,0:T(8,128)(2,1)S(1)}, bf16[2,256,128]{2,1,0:T(8,128)(2,1)S(1)}, u32[]{:S(2)}, u32[]{:S(2)}) %collective-permute-start.6) | collective-permute-done | bytes 131104 | tf_op jit(solution)/shard_map/ppermute | solution.py:354
  19.7 1.6 %collective-permute-start.10 = (bf16[4,144,128]{2,1,0:T(8,128)(2,1)S(1)}, bf16[4,144,128]{2,1,0:T(8,128)(2,1)S(1)}, u32[]{:S(2)}, u32[]{:S(2)}) collective-permute-start(bf16[4,144,128]{2,1,0:T(8,128)(2,1)S(1)} %shard_map.104.refs_2_), channel_id=1, source_target_pairs={{0,8},{8,0},{16,24},{24,16},{1,9},{9,1},{17,25},{25,17},{2,10},{10... | collective-permute-start | bytes 442376 | tf_op jit(solution)/shard_map/ppermute | solution.py:354
  21.3 0.1 collective-permute-start.1
  21.4 0.0 collective-permute-done.8.refs_4_
  21.4 0.5 %collective-permute-start.9 = (bf16[2,144,128]{2,1,0:T(8,128)(2,1)S(1)}, bf16[2,144,128]{2,1,0:T(8,128)(2,1)S(1)}, u32[]{:S(2)}, u32[]{:S(2)}) collective-permute-start(bf16[2,144,128]{2,1,0:T(8,128)(2,1)S(1)} %slice.84), channel_id=1, source_target_pairs={{0,2},{2,0},{1,3},{3,1},{4,6},{6,4},{5,7},{7,5},{8,10},{10,8},{9,1... | collective-permute-start | bytes 221192 | tf_op jit(solution)/shard_map/ppermute | solution.py:354
  22.0 0.1 collective-permute-start.7
  22.1 0.6 %collective-permute-done.1.refs_1_ = bf16[2,144,128]{2,1,0:T(8,128)(2,1)S(1)} collective-permute-done((bf16[2,144,128]{2,1,0:T(8,128)(2,1)S(1)}, bf16[2,144,128]{2,1,0:T(8,128)(2,1)S(1)}, u32[]{:S(2)}, u32[]{:S(2)}) %collective-permute-start.1) | collective-permute-done | bytes 73760 | tf_op jit(solution)/shard_map/ppermute | solution.py:354
  22.6 0.2 collective-permute-done.9.refs_5_
  22.9 0.4 collective-permute-done.7.refs_3_
  23.2 1.1 %shard_map.105.refs_1_.refs_6_ = f32[8,128]{1,0:T(8,128)S(1)} custom-call(s32[1,1024]{1,0:T(1,128)S(1)} %compare_select_fusion.ends_ref, bf16[4,144,128]{2,1,0:T(8,128)(2,1)S(1)} %pad_maximum_fusion.1.refs_0_, bf16[2,144,128]{2,1,0:T(8,128)(2,1)S(1)} %collective-permute-done.1.refs_1_, bf16[4,144,128]{2,1,0:T(8,128)(2,1)S(1)} %shard_map.104.refs_2_, ...), custom_call_target="tpu_custom_call" | custom-call | tf_op jit(solution)/shard_map/pallas_call | solution.py:454
  24.4 0.5 collective-permute-done.10.refs_0_
  24.9 0.1 collective-permute-start.11
  25.6 0.6 %collective-permute-done.11.refs_1_.refs_7_ = bf16[2,144,128]{2,1,0:T(8,128)(2,1)S(1)} collective-permute-done((bf16[2,144,128]{2,1,0:T(8,128)(2,1)S(1)}, bf16[2,144,128]{2,1,0:T(8,128)(2,1)S(1)}, u32[]{:S(2)}, u32[]{:S(2)}) %collective-permute-start.11) | collective-permute-done | bytes 73760 | tf_op jit(solution)/shard_map/ppermute | solution.py:354
  26.2 0.6 %shard_map.107.refs_12_.refs_11_ = f32[8,128]{1,0:T(8,128)S(1)} custom-call(s32[1,1024]{1,0:T(1,128)S(1)} %compare_select_fusion.ends_ref, bf16[4,144,128]{2,1,0:T(8,128)(2,1)S(1)} %shard_map.106.refs_0_.refs_6_, bf16[2,144,128]{2,1,0:T(8,128)(2,1)S(1)} %collective-permute-done.11.refs_1_.refs_7_, ...), custom_call_target="tpu_custom_call" | custom-call | tf_op jit(solution)/shard_map/pallas_call | solution.py:454
  26.8 1.4 %collective-permute-start.14 = (f32[8,128]{1,0:T(8,128)S(1)}, f32[8,128]{1,0:T(8,128)S(1)}, u32[]{:S(2)}, u32[]{:S(2)}) collective-permute-start(f32[8,128]{1,0:T(8,128)S(1)} %shard_map.107.refs_12_.refs_11_), channel_id=1, source_target_pairs={{0,24},{8,16},{16,8},{24,0},{1,25},{9,17},{17,9},{25,1},{2,26},{10... | collective-permute-start | bytes 12296 | tf_op jit(solution)/shard_map/ppermute | solution.py:354
  28.3 1.7 %collective-permute-start.13 = (f32[8,128]{1,0:T(8,128)S(1)}, f32[8,128]{1,0:T(8,128)S(1)}, u32[]{:S(2)}, u32[]{:S(2)}) collective-permute-start(f32[8,128]{1,0:T(8,128)S(1)} %shard_map.107.refs_12_.refs_11_), channel_id=1, source_target_pairs={{0,16},{8,24},{16,0},{24,8},{1,17},{9,25},{17,1},{25,9},{2,18},{10... | collective-permute-start | bytes 12296 | tf_op jit(solution)/shard_map/ppermute | solution.py:354
  30.0 1.3 %collective-permute-start.12 = (f32[8,128]{1,0:T(8,128)S(1)}, f32[8,128]{1,0:T(8,128)S(1)}, u32[]{:S(2)}, u32[]{:S(2)}) collective-permute-start(f32[8,128]{1,0:T(8,128)S(1)} %shard_map.107.refs_12_.refs_11_), channel_id=1, source_target_pairs={{0,8},{8,0},{16,24},{24,16},{1,9},{9,1},{17,25},{25,17},{2,10},{10... | collective-permute-start | bytes 12296 | tf_op jit(solution)/shard_map/ppermute | solution.py:354
  31.3 2.0 %shard_map.108 = (bf16[4,256,1024]{2,1,0:T(8,128)(2,1)S(1)}, bf16[4,256,1024]{2,1,0:T(8,128)(2,1)S(1)}, f32[128,1024]{1,0:T(8,128)S(1)}) custom-call(s32[1,1024]{1,0:T(1,128)S(1)} %compare_select_fusion.ends_ref, bf16[4,144,128]{2,1,0:T(8,128)(2,1)S(1)} %pad_maximum_fusion.1.refs_0_, bf16[2,144,128]{2,1,0:T(8,128)(2,1)S(1)} %collective-permute-done.1.refs_1_, ...), custom_call_target="tpu_custom_call" | custom-call | tf_op jit(solution)/shard_map/pallas_call | solution.py:470
  33.4 0.0 collective-permute-done.13.refs_13_
  33.4 0.2 collective-permute-done.12.refs_12_
  33.6 1.5 %shard_map.109 = (bf16[2,256,128]{2,1,0:T(8,128)(2,1)S(1)}, bf16[2,256,128]{2,1,0:T(8,128)(2,1)S(1)}, bf16[2,256,128]{2,1,0:T(8,128)(2,1)S(1)}, bf16[2,256,128]{...) custom-call(s32[1,1024]{1,0:T(1,128)S(1)} %compare_convert_fusion.live_ref, ...), custom_call_target="tpu_custom_call" | custom-call | tf_op jit(solution)/shard_map/pallas_call | solution.py:479
  35.1 0.1 collective-permute-start.15
  35.1 1.0 %collective-permute-start.16 = (bf16[2,256,128]{2,1,0:T(8,128)(2,1)S(1)}, bf16[2,256,128]{2,1,0:T(8,128)(2,1)S(1)}, u32[]{:S(2)}, u32[]{:S(2)}) collective-permute-start(bf16[2,256,128]{2,1,0:T(8,128)(2,1)S(1)} %get-tuple-element.29), channel_id=1, source_target_pairs={{0,1},{1,0},{2,3},{3,2},{4,5},{5,4},{6,7},{7,6},{8,9},{9,8},{10,11... | collective-permute-start | bytes 393224 | tf_op jit(solution)/shard_map/ppermute | solution.py:354
  36.1 0.9 %collective-permute-start.17 = (bf16[2,256,128]{2,1,0:T(8,128)(2,1)S(1)}, bf16[2,256,128]{2,1,0:T(8,128)(2,1)S(1)}, u32[]{:S(2)}, u32[]{:S(2)}) collective-permute-start(bf16[2,256,128]{2,1,0:T(8,128)(2,1)S(1)} %get-tuple-element.30), channel_id=1, source_target_pairs={{0,4},{1,5},{2,6},{3,7},{4,0},{5,1},{6,2},{7,3},{8,12},{9,13},{10,... | collective-permute-start | bytes 393224 | tf_op jit(solution)/shard_map/ppermute | solution.py:354
  37.0 1.6 %collective-permute-start.18 = (bf16[2,256,128]{2,1,0:T(8,128)(2,1)S(1)}, bf16[2,256,128]{2,1,0:T(8,128)(2,1)S(1)}, u32[]{:S(2)}, u32[]{:S(2)}) collective-permute-start(bf16[2,256,128]{2,1,0:T(8,128)(2,1)S(1)} %get-tuple-element.31), channel_id=1, source_target_pairs={{0,5},{1,4},{2,7},{3,6},{4,1},{5,0},{6,3},{7,2},{8,13},{9,12},{10,... | collective-permute-start | bytes 393224 | tf_op jit(solution)/shard_map/ppermute | solution.py:354
  38.7 0.0 collective-permute-done.15.refs_1_
  38.7 0.7 %shard_map.110.refs_1_ = bf16[8,2,64,128]{3,2,1,0:T(8,128)(2,1)} custom-call(bf16[8,64,128]{2,1,0:T(8,128)(2,1)S(1)} %get-tuple-element.26.refs_0_, bf16[8,64,128]{2,1,0:T(8,128)(2,1)S(1)} %collective-permute-done.15.refs_1_), custom_call_target="tpu_custom_call" | custom-call | tf_op jit(solution)/shard_map/pallas_call | solution.py:489
  39.4 3.4 %all-to-all-start = ((bf16[8,2,64,128]{3,2,1,0:T(8,128)(2,1)}), bf16[8,2,64,128]{3,2,1,0:T(8,128)(2,1)S(1)}, u32[]{:S(2)}, u32[]{:S(2)}) async-start(bf16[8,2,64,128]{3,2,1,0:T(8,128)(2,1)} %shard_map.110.refs_1_), calls=%async_computation | async-start | bytes 524288 | tf_op jit(solution)/shard_map/all_to_all | solution.py:496
  42.8 0.0 collective-permute-done.16.refs_0_
  42.9 1.6 %collective-permute-done.17.refs_0_ = bf16[2,256,128]{2,1,0:T(8,128)(2,1)S(1)} collective-permute-done((bf16[2,256,128]{2,1,0:T(8,128)(2,1)S(1)}, bf16[2,256,128]{2,1,0:T(8,128)(2,1)S(1)}, u32[]{:S(2)}, u32[]{:S(2)}) %collective-permute-start.17) | collective-permute-done | bytes 131104 | tf_op jit(solution)/shard_map/ppermute | solution.py:354
  44.5 0.0 collective-permute-done.18.refs_0_
  44.6 0.1 collective-permute-start.19
  44.6 1.5 %collective-permute-done.19.refs_5_ = bf16[4,256,128]{2,1,0:T(8,128)(2,1)S(1)} collective-permute-done((bf16[4,256,128]{2,1,0:T(8,128)(2,1)S(1)}, bf16[4,256,128]{2,1,0:T(8,128)(2,1)S(1)}, u32[]{:S(2)}, u32[]{:S(2)}) %collective-permute-start.19) | collective-permute-done | bytes 262176 | tf_op jit(solution)/shard_map/ppermute | solution.py:354
  46.2 5.6 %all-to-all-done.refs_0_ = bf16[8,2,64,128]{3,2,1,0:T(8,128)(2,1)S(1)} async-done(((bf16[8,2,64,128]{3,2,1,0:T(8,128)(2,1)}), bf16[8,2,64,128]{3,2,1,0:T(8,128)(2,1)S(1)}, u32[]{:S(2)}, u32[]{:S(2)}) %all-to-all-start) | async-done | bytes 262176 | tf_op jit(solution)/shard_map/all_to_all | solution.py:496
  51.7 1.0 %shard_map.114 = (bf16[256,128]{1,0:T(8,128)(2,1)}, bf16[128,1024]{1,0:T(8,128)(2,1)}, bf16[128,1024]{1,0:T(8,128)(2,1)}) custom-call(bf16[8,2,64,128]{3,2,1,0:T(8,128)(2,1)S(1)} %all-to-all-done.refs_0_, bf16[2,256,128]{2,1,0:T(8,128)(2,1)S(1)} %get-tuple-element.28.refs_1_, bf16[2,256,128]{2,1,0:T(8,128)(2,1)S(1)} %shard_map.111.refs_2_, ...), custom_call_target="tpu_custom_call" | custom-call | tf_op jit(solution)/shard_map/pallas_call | solution.py:497
  (26 shorter events, 0.3 us)
Async XLA Ops:
  2.0 5.4 %collective-permute-start = (bf16[2,144,128]{2,1,0:T(8,128)(2,1)S(1)}, bf16[2,144,128]{2,1,0:T(8,128)(2,1)S(1)}, u32[]{:S(2)}, u32[]{:S(2)}) collective-permute-start(bf16[2,144,128]{2,1,0:T(8,128)(2,1)S(1)} %get-tuple-element.20), channel_id=1, source_target_pairs={{0,4},{4,0},{1,5},{5,1},{2,6},{6,2},{3,7},{7,3},{8,12},{12,8},{9,1... | collective-permute-start | bytes 221192 | tf_op jit(solution)/shard_map/ppermute | solution.py:354
  5.0 5.5 %collective-permute-start.3 = (bf16[4,256,128]{2,1,0:T(8,128)(2,1)S(1)}, bf16[4,256,128]{2,1,0:T(8,128)(2,1)S(1)}, u32[]{:S(2)}, u32[]{:S(2)}) collective-permute-start(bf16[4,256,128]{2,1,0:T(8,128)(2,1)S(1)} %get-tuple-element.22), channel_id=1, source_target_pairs={{0,2},{1,3},{2,0},{3,1},{4,6},{5,7},{6,4},{7,5},{8,10},{9,11},{10,... | collective-permute-start | bytes 786440 | tf_op jit(solution)/shard_map/ppermute | solution.py:354
  7.4 9.3 %collective-permute-start.2 = (bf16[4,144,128]{2,1,0:T(8,128)(2,1)S(1)}, bf16[4,144,128]{2,1,0:T(8,128)(2,1)S(1)}, u32[]{:S(2)}, u32[]{:S(2)}) collective-permute-start(bf16[4,144,128]{2,1,0:T(8,128)(2,1)S(1)} %pad_maximum_fusion.1.refs_0_), channel_id=1, source_target_pairs={{0,16},{8,24},{16,0},{24,8},{1,17},{9,25},{17,1},{25,9},{2,18},{10... | collective-permute-start | bytes 442376 | tf_op jit(solution)/shard_map/ppermute | solution.py:354
  10.6 6.4 %collective-permute-start.4 = (bf16[2,256,128]{2,1,0:T(8,128)(2,1)S(1)}, bf16[2,256,128]{2,1,0:T(8,128)(2,1)S(1)}, u32[]{:S(2)}, u32[]{:S(2)}) collective-permute-start(bf16[2,256,128]{2,1,0:T(8,128)(2,1)S(1)} %pad_maximum_fusion.2), channel_id=1, source_target_pairs={{0,1},{1,0},{2,3},{3,2},{4,5},{5,4},{6,7},{7,6},{8,9},{9,8},{10,11... | collective-permute-start | bytes 393224 | tf_op jit(solution)/shard_map/ppermute | solution.py:354
  12.2 6.1 %collective-permute-start.5 = (bf16[2,256,128]{2,1,0:T(8,128)(2,1)S(1)}, bf16[2,256,128]{2,1,0:T(8,128)(2,1)S(1)}, u32[]{:S(2)}, u32[]{:S(2)}) collective-permute-start(bf16[2,256,128]{2,1,0:T(8,128)(2,1)S(1)} %pad_maximum_fusion.3), channel_id=1, source_target_pairs={{0,4},{1,5},{2,6},{3,7},{4,0},{5,1},{6,2},{7,3},{8,12},{9,13},{10,... | collective-permute-start | bytes 393224 | tf_op jit(solution)/shard_map/ppermute | solution.py:354
  13.8 5.9 %collective-permute-start.6 = (bf16[2,256,128]{2,1,0:T(8,128)(2,1)S(1)}, bf16[2,256,128]{2,1,0:T(8,128)(2,1)S(1)}, u32[]{:S(2)}, u32[]{:S(2)}) collective-permute-start(bf16[2,256,128]{2,1,0:T(8,128)(2,1)S(1)} %pad_maximum_fusion.4), channel_id=1, source_target_pairs={{0,5},{1,4},{2,7},{3,6},{4,1},{5,0},{6,3},{7,2},{8,13},{9,12},{10,... | collective-permute-start | bytes 393224 | tf_op jit(solution)/shard_map/ppermute | solution.py:354
  15.0 6.4 %collective-permute-start.8 = (bf16[4,144,128]{2,1,0:T(8,128)(2,1)S(1)}, bf16[4,144,128]{2,1,0:T(8,128)(2,1)S(1)}, u32[]{:S(2)}, u32[]{:S(2)}) collective-permute-start(bf16[4,144,128]{2,1,0:T(8,128)(2,1)S(1)} %pad_maximum_fusion.1.refs_0_), channel_id=1, source_target_pairs={{0,8},{8,0},{16,24},{24,16},{1,9},{9,1},{17,25},{25,17},{2,10},{10... | collective-permute-start | bytes 442376 | tf_op jit(solution)/shard_map/ppermute | solution.py:354
  19.7 5.1 %collective-permute-start.10 = (bf16[4,144,128]{2,1,0:T(8,128)(2,1)S(1)}, bf16[4,144,128]{2,1,0:T(8,128)(2,1)S(1)}, u32[]{:S(2)}, u32[]{:S(2)}) collective-permute-start(bf16[4,144,128]{2,1,0:T(8,128)(2,1)S(1)} %shard_map.104.refs_2_), channel_id=1, source_target_pairs={{0,8},{8,0},{16,24},{24,16},{1,9},{9,1},{17,25},{25,17},{2,10},{10... | collective-permute-start | bytes 442376 | tf_op jit(solution)/shard_map/ppermute | solution.py:354
  21.3 1.3 %collective-permute-start.1 = (bf16[2,144,128]{2,1,0:T(8,128)(2,1)S(1)}, bf16[2,144,128]{2,1,0:T(8,128)(2,1)S(1)}, u32[]{:S(2)}, u32[]{:S(2)}) collective-permute-start(bf16[2,144,128]{2,1,0:T(8,128)(2,1)S(1)} %pad_maximum_fusion.6), channel_id=1, source_target_pairs={{0,2},{2,0},{1,3},{3,1},{4,6},{6,4},{5,7},{7,5},{8,10},{10,8},{9,1... | collective-permute-start | bytes 221192 | tf_op jit(solution)/shard_map/ppermute | solution.py:354
  21.4 1.5 %collective-permute-start.9 = (bf16[2,144,128]{2,1,0:T(8,128)(2,1)S(1)}, bf16[2,144,128]{2,1,0:T(8,128)(2,1)S(1)}, u32[]{:S(2)}, u32[]{:S(2)}) collective-permute-start(bf16[2,144,128]{2,1,0:T(8,128)(2,1)S(1)} %slice.84), channel_id=1, source_target_pairs={{0,2},{2,0},{1,3},{3,1},{4,6},{6,4},{5,7},{7,5},{8,10},{10,8},{9,1... | collective-permute-start | bytes 221192 | tf_op jit(solution)/shard_map/ppermute | solution.py:354
  22.0 1.3 %collective-permute-start.7 = (bf16[2,144,128]{2,1,0:T(8,128)(2,1)S(1)}, bf16[2,144,128]{2,1,0:T(8,128)(2,1)S(1)}, u32[]{:S(2)}, u32[]{:S(2)}) collective-permute-start(bf16[2,144,128]{2,1,0:T(8,128)(2,1)S(1)} %slice.83), channel_id=1, source_target_pairs={{0,2},{2,0},{1,3},{3,1},{4,6},{6,4},{5,7},{7,5},{8,10},{10,8},{9,1... | collective-permute-start | bytes 221192 | tf_op jit(solution)/shard_map/ppermute | solution.py:354
  24.9 1.3 %collective-permute-start.11 = (bf16[2,144,128]{2,1,0:T(8,128)(2,1)S(1)}, bf16[2,144,128]{2,1,0:T(8,128)(2,1)S(1)}, u32[]{:S(2)}, u32[]{:S(2)}) collective-permute-start(bf16[2,144,128]{2,1,0:T(8,128)(2,1)S(1)} %slice.86), channel_id=1, source_target_pairs={{0,2},{2,0},{1,3},{3,1},{4,6},{6,4},{5,7},{7,5},{8,10},{10,8},{9,1... | collective-permute-start | bytes 221192 | tf_op jit(solution)/shard_map/ppermute | solution.py:354
  26.8 6.5 %collective-permute-start.14 = (f32[8,128]{1,0:T(8,128)S(1)}, f32[8,128]{1,0:T(8,128)S(1)}, u32[]{:S(2)}, u32[]{:S(2)}) collective-permute-start(f32[8,128]{1,0:T(8,128)S(1)} %shard_map.107.refs_12_.refs_11_), channel_id=1, source_target_pairs={{0,24},{8,16},{16,8},{24,0},{1,25},{9,17},{17,9},{25,1},{2,26},{10... | collective-permute-start | bytes 12296 | tf_op jit(solution)/shard_map/ppermute | solution.py:354
  28.3 5.1 %collective-permute-start.13 = (f32[8,128]{1,0:T(8,128)S(1)}, f32[8,128]{1,0:T(8,128)S(1)}, u32[]{:S(2)}, u32[]{:S(2)}) collective-permute-start(f32[8,128]{1,0:T(8,128)S(1)} %shard_map.107.refs_12_.refs_11_), channel_id=1, source_target_pairs={{0,16},{8,24},{16,0},{24,8},{1,17},{9,25},{17,1},{25,9},{2,18},{10... | collective-permute-start | bytes 12296 | tf_op jit(solution)/shard_map/ppermute | solution.py:354
  30.0 3.6 %collective-permute-start.12 = (f32[8,128]{1,0:T(8,128)S(1)}, f32[8,128]{1,0:T(8,128)S(1)}, u32[]{:S(2)}, u32[]{:S(2)}) collective-permute-start(f32[8,128]{1,0:T(8,128)S(1)} %shard_map.107.refs_12_.refs_11_), channel_id=1, source_target_pairs={{0,8},{8,0},{16,24},{24,16},{1,9},{9,1},{17,25},{25,17},{2,10},{10... | collective-permute-start | bytes 12296 | tf_op jit(solution)/shard_map/ppermute | solution.py:354
  35.1 3.6 %collective-permute-start.15 = (bf16[8,64,128]{2,1,0:T(8,128)(2,1)S(1)}, bf16[8,64,128]{2,1,0:T(8,128)(2,1)S(1)}, u32[]{:S(2)}, u32[]{:S(2)}) collective-permute-start(bf16[8,64,128]{2,1,0:T(8,128)(2,1)S(1)} %get-tuple-element.27), channel_id=1, source_target_pairs={{0,2},{2,0},{1,3},{3,1},{4,6},{6,4},{5,7},{7,5},{8,10},{10,8},{9,1... | collective-permute-start | bytes 393224 | tf_op jit(solution)/shard_map/ppermute | solution.py:354
  35.1 7.7 %collective-permute-start.16 = (bf16[2,256,128]{2,1,0:T(8,128)(2,1)S(1)}, bf16[2,256,128]{2,1,0:T(8,128)(2,1)S(1)}, u32[]{:S(2)}, u32[]{:S(2)}) collective-permute-start(bf16[2,256,128]{2,1,0:T(8,128)(2,1)S(1)} %get-tuple-element.29), channel_id=1, source_target_pairs={{0,1},{1,0},{2,3},{3,2},{4,5},{5,4},{6,7},{7,6},{8,9},{9,8},{10,11... | collective-permute-start | bytes 393224 | tf_op jit(solution)/shard_map/ppermute | solution.py:354
  36.1 8.4 %collective-permute-start.17 = (bf16[2,256,128]{2,1,0:T(8,128)(2,1)S(1)}, bf16[2,256,128]{2,1,0:T(8,128)(2,1)S(1)}, u32[]{:S(2)}, u32[]{:S(2)}) collective-permute-start(bf16[2,256,128]{2,1,0:T(8,128)(2,1)S(1)} %get-tuple-element.30), channel_id=1, source_target_pairs={{0,4},{1,5},{2,6},{3,7},{4,0},{5,1},{6,2},{7,3},{8,12},{9,13},{10,... | collective-permute-start | bytes 393224 | tf_op jit(solution)/shard_map/ppermute | solution.py:354
  37.0 7.4 %collective-permute-start.18 = (bf16[2,256,128]{2,1,0:T(8,128)(2,1)S(1)}, bf16[2,256,128]{2,1,0:T(8,128)(2,1)S(1)}, u32[]{:S(2)}, u32[]{:S(2)}) collective-permute-start(bf16[2,256,128]{2,1,0:T(8,128)(2,1)S(1)} %get-tuple-element.31), channel_id=1, source_target_pairs={{0,5},{1,4},{2,7},{3,6},{4,1},{5,0},{6,3},{7,2},{8,13},{9,12},{10,... | collective-permute-start | bytes 393224 | tf_op jit(solution)/shard_map/ppermute | solution.py:354
  39.4 12.3 %all-to-all-start = ((bf16[8,2,64,128]{3,2,1,0:T(8,128)(2,1)}), bf16[8,2,64,128]{3,2,1,0:T(8,128)(2,1)S(1)}, u32[]{:S(2)}, u32[]{:S(2)}) async-start(bf16[8,2,64,128]{3,2,1,0:T(8,128)(2,1)} %shard_map.110.refs_1_), calls=%async_computation | async-start | bytes 524288 | tf_op jit(solution)/shard_map/all_to_all | solution.py:496
  44.6 1.6 %collective-permute-start.19 = (bf16[4,256,128]{2,1,0:T(8,128)(2,1)S(1)}, bf16[4,256,128]{2,1,0:T(8,128)(2,1)S(1)}, u32[]{:S(2)}, u32[]{:S(2)}) collective-permute-start(bf16[4,256,128]{2,1,0:T(8,128)(2,1)S(1)} %pad_maximum_fusion), channel_id=1, source_target_pairs={{0,2},{1,3},{2,0},{3,1},{4,6},{5,7},{6,4},{7,5},{8,10},{9,11},{10,... | collective-permute-start | bytes 786440 | tf_op jit(solution)/shard_map/ppermute | solution.py:354

commit v11 on v9

--- a/solution.py
+++ b/solution.py
@@ -55,22 +55,21 @@
 
 
 def pack_kernel(row_count, nears, heads, q_hbm, o_grad_hbm, o_hbm, lse_hbm, k_hbm, v_hbm, *rest):
-    slab_refs, (keep_ref, send_ref, o_ref, lse_ref, sems) = rest[:row_count], rest[row_count:]
+    groups = row_count * nears
+    slab_refs, (keep_ref, send_ref, o_ref, lse_ref, sems) = rest[:groups], rest[groups:]
     at = place(nears, heads)
-    groups = row_count * nears
     rows, own_heads = lse_ref.shape
     lines = o_ref.shape[0] // groups
     tokens = k_hbm.shape[0]
     copies = [(lse_hbm, lse_ref), (o_hbm, o_ref)]
     slabs = []
-    for j, ref in enumerate(slab_refs):
-        for n in range(nears):
-            first = pl.multiple_of(group_at(at, j, n, nears) * lines, lines)
-            slabs.append((ref, n, first))
-            copies.append((o_grad_hbm.at[pl.ds(first, lines), :], ref.at[n, lines : 2 * lines, :]))
+    for m, ref in enumerate(slab_refs):
+        first = pl.multiple_of(group_at(at, m // nears, m % nears, nears) * lines, lines)
+        slabs.append((ref, first))
+        copies.append((o_grad_hbm.at[pl.ds(first, lines), :], ref.at[lines : 2 * lines, :]))
     stat_copies = len(copies)
-    for ref, n, first in slabs:
-        copies.append((q_hbm.at[pl.ds(first, lines), :], ref.at[n, 0:lines, :]))
+    for ref, first in slabs:
+        copies.append((q_hbm.at[pl.ds(first, lines), :], ref.at[0:lines, :]))
     for i, j in enumerate(KEEP):
         for ref, peer in ((send_ref, j ^ FIRST), (keep_ref, j)):
             columns = pl.ds(column_of(at[0] ^ peer, groups, heads), DH)
@@ -85,7 +84,7 @@
     head_ids = lax.broadcasted_iota(jnp.int32, shape, 0)
     line_heads = (lax.broadcasted_iota(jnp.int32, shape, 1) & (lines - 1)) >> shift_of(rows)
     chosen = jnp.concatenate(
-        [(head_ids == line_heads + (first >> shift_of(rows))) for _, _, first in slabs], axis=1
+        [(head_ids == line_heads + (first >> shift_of(rows))) for _, first in slabs], axis=1
     ).astype(jnp.bfloat16)
     shape = (STAT_ROWS, chosen.shape[1])
     own_row = (lax.broadcasted_iota(jnp.int32, shape, 0) & (rows - 1)) == (
@@ -106,14 +105,14 @@
         gather.astype(jnp.bfloat16), spread, preferred_element_type=jnp.float32
     )
     kind = lax.broadcasted_iota(jnp.int32, (STAT_ROWS, wide), 0)
-    for m, (ref, n, first) in enumerate(slabs):
-        o_grad = ref[n, lines:wide, :].astype(jnp.float32)
+    for m, (ref, first) in enumerate(slabs):
+        o_grad = ref[lines:wide, :].astype(jnp.float32)
         product = o_grad * o_ref[pl.ds(first, lines), :].astype(jnp.float32)
         dots = jnp.sum(jnp.concatenate([product, product], axis=0).T, axis=0, keepdims=True)
         stats = lse_rows_all[:, m * wide : (m + 1) * wide]
         for k, piece in enumerate(split_pieces(dots)):
             stats = jnp.where(kind == PIECES + k, piece.astype(jnp.float32), stats)
-        ref[n, wide:, :] = stats.astype(jnp.bfloat16)
+        ref[wide:, :] = stats.astype(jnp.bfloat16)
     for copy in copies[stat_copies:]:
         copy.wait()
 
@@ -152,29 +151,24 @@
     return max(1, size // DH)
 
 
-def block_slabs(blocks, nears, row_refs):
-    out = []
-    for at in range(len(blocks)):
-        refs = row_refs[at * nears : (at + 1) * nears]
-        row_count = refs[0].shape[0] // nears
-        out.append([(ref, j, n, j) for n, ref in enumerate(refs) for j in range(row_count)])
-    return out
+def slabs_of(row_refs):
+    return [[(ref, m) for m in range(ref.shape[0])] for ref in row_refs]
 
 
 def lines_of(slabs, first, lines):
-    return jnp.concatenate([ref[j, first : first + lines, :] for ref, j, _, _ in slabs], axis=0)
+    return jnp.concatenate([ref[j, first : first + lines, :] for ref, j in slabs], axis=0)
 
 
 def stat_kernel(blocks, first, nears, heads, tokens, ends_ref, *refs):
     at = place(nears, heads)
-    row_refs, refs = refs[: len(blocks) * nears], refs[len(blocks) * nears :]
+    row_refs, refs = refs[: len(blocks)], refs[len(blocks) :]
     pair_refs, before_refs, lse_ref = refs[: len(KEEP)], refs[len(KEEP) : -1], refs[-1]
     lines = (row_refs[0].shape[1] - STAT_ROWS) // 2
     for ref in before_refs:
         lse_ref[...] = ref[...]
 
     def body(seen):
-        for m, (b, slabs) in enumerate(zip(blocks, block_slabs(blocks, nears, row_refs))):
+        for m, (b, slabs) in enumerate(zip(blocks, slabs_of(row_refs))):
             count = len(slabs) * lines
             q = lines_of(slabs, 0, lines)
             ends = ends_ref[:, first + m * count : first + (m + 1) * count]
@@ -206,7 +200,7 @@
     for n in range(0, len(slabs), 2):
         held = [
             ref[j, 2 * lines : 2 * lines + STAT_ROWS, :].astype(jnp.float32)
-            for ref, j, _, _ in slabs[n : n + 2]
+            for ref, j in slabs[n : n + 2]
         ]
         total = None
         for k in range(first_piece, first_piece + PIECES):
@@ -236,10 +230,10 @@
 
 def part_kernel(blocks, nears, heads, tokens, ends_ref, *refs):
     at = place(nears, heads)
-    row_refs, refs = refs[: len(blocks) * nears], refs[len(blocks) * nears :]
+    row_refs, refs = refs[: len(blocks)], refs[len(blocks) :]
     pair_refs, (lse_ref, prob_ref, dscore_ref, dq_ref) = refs[: len(KEEP)], refs[len(KEEP) :]
     lines = (row_refs[0].shape[1] - STAT_ROWS) // 2
-    all_slabs = block_slabs(blocks, nears, row_refs)
+    all_slabs = slabs_of(row_refs)
     size = len(all_slabs[0]) * lines
 
     def body(seen):
@@ -271,12 +265,12 @@
 
 def token_kernel(blocks, nears, heads, tokens, live_ref, *refs):
     at = place(nears, heads)
-    row_refs, refs = refs[: len(blocks) * nears], refs[len(blocks) * nears :]
+    row_refs, refs = refs[: len(blocks)], refs[len(blocks) :]
     (prob_ref, dscore_ref, dq_ref), refs = refs[:3], refs[3:]
     lse_refs, refs = refs[: len(blocks)], refs[len(blocks) :]
     dkv_refs, (*dq_refs, dk_acc, dv_acc) = refs[: len(KEEP)], refs[len(KEEP) :]
     lines = (row_refs[0].shape[1] - STAT_ROWS) // 2
-    all_slabs = block_slabs(blocks, nears, row_refs)
+    all_slabs = slabs_of(row_refs)
     size = len(all_slabs[0]) * lines
     for first, count, held, slabs in steps_of(blocks, all_slabs, lines):
         lanes = slice(first, first + count)
@@ -287,9 +281,10 @@
         lse = jnp.where(live_ref[:, lanes] > 0, peak + jnp.log(total), DEAD_LSE)
         weight = jnp.exp(part_lse[0] - lse)
         dq = (dq_ref[:, lanes] * (weight * SCALE)).T.astype(jnp.bfloat16)
-        sources = [(b, slab) for b in held for slab in all_slabs[blocks.index(b)]]
-        for m, (b, (_, _, n, j)) in enumerate(sources):
-            dq_refs[n][blocks.index(b), j] = dq[m * lines : (m + 1) * lines]
+        groups = len(dq_refs)
+        for m in range(len(slabs)):
+            block = first // size + m // groups
+            dq_refs[m % groups][block] = dq[m * lines : (m + 1) * lines]
         weight_t = jnp.broadcast_to(weight, (DH, count)).T
         q, o_grad = (
             (lines_of(slabs, start, lines).astype(jnp.float32) * weight_t).astype(jnp.bfloat16)
@@ -311,38 +306,35 @@
                     dkv_refs[i][n, tokens : 2 * tokens, :] = dv[inner].astype(jnp.bfloat16)
 
 
-def add_query_kernel(nears, *refs):
-    own_refs, came_refs, out_refs = refs[:nears], refs[nears:-2], refs[-2:]
-    for n in range(nears):
-        for j in range(own_refs[0].shape[1]):
-            total = own_refs[n][0, j].astype(jnp.float32)
-            for ref in came_refs:
-                total = total + ref[n, j].astype(jnp.float32)
-            out_refs[min(j, 1)][n] = total.astype(jnp.bfloat16)
-
-
 def tie_kernel(*refs):
     pass
 
 
 def write_kernel(nears, heads, *refs):
     at = place(nears, heads)
-    slab_refs, refs = refs[: -len(KEEP) - 5], refs[-len(KEEP) - 5 :]
-    pair_refs, (came_ref, out_q_ref, out_k_ref, out_v_ref, sems) = refs[: len(KEEP)], refs[len(KEEP) :]
-    groups, lines, tokens = len(slab_refs) * nears, slab_refs[0].shape[1], out_k_ref.shape[0]
+    out_q_ref, out_k_ref, out_v_ref, sum_ref, sems = refs[-5:]
+    pair_refs, came_ref, refs = refs[: len(KEEP)], refs[len(KEEP)], refs[len(KEEP) + 1 : -5]
+    groups, lines, _ = sum_ref.shape
+    own_refs, part_refs = refs[:groups], refs[groups:]
+    tokens = out_k_ref.shape[0]
     copies = []
     for i, ref in enumerate(pair_refs):
         for source, other in ((ref.at[0], 0), (came_ref.at[i], FIRST)):
             columns = pl.ds(column_of(at[0] ^ KEEP[i] ^ other, groups, heads), DH)
             copies.append((source.at[0:tokens, :], out_k_ref.at[:, columns]))
             copies.append((source.at[tokens : 2 * tokens, :], out_v_ref.at[:, columns]))
-    for j, ref in enumerate(slab_refs):
-        for n in range(nears):
-            first = pl.multiple_of(group_at(at, j, n, nears) * lines, lines)
-            copies.append((ref.at[n], out_q_ref.at[pl.ds(first, lines), :]))
+    for m in range(groups):
+        first = pl.multiple_of(group_at(at, m // nears, m % nears, nears) * lines, lines)
+        copies.append((sum_ref.at[m], out_q_ref.at[pl.ds(first, lines), :]))
     copies = [pltpu.make_async_copy(s, t, sems.at[n]) for n, (s, t) in enumerate(copies)]
-    for copy in copies:
+    for copy in copies[:-groups]:
         copy.start()
+    for m in range(groups):
+        total = own_refs[m][0].astype(jnp.float32)
+        for ref in part_refs:
+            total = total + ref[m].astype(jnp.float32)
+        sum_ref[m] = total.astype(jnp.bfloat16)
+        copies[m - groups].start()
     for copy in copies:
         copy.wait()
 
@@ -376,11 +368,15 @@
     return [*pairs, swap(beyond, members, FIRST, KVH)]
 
 
+def swap_slabs(slabs, groups):
+    return [swap(x, ("row", "near"), m, groups) if m else x for m, x in enumerate(slabs)]
+
+
 def line_limits(parts, row_count, nears, rows, lines, resp_len, prompt_end):
     line = lax.broadcasted_iota(jnp.int32, (1, parts * nears * row_count * lines), 1)
     slab = line >> shift_of(lines)
-    row_xor = slab & (row_count - 1)
-    near_xor = (slab >> shift_of(row_count)) & (nears - 1)
+    near_xor = slab & (nears - 1)
+    row_xor = (slab >> shift_of(nears)) & (row_count - 1)
     place_of_block = slab >> shift_of(row_count * nears)
     block, bits = jnp.zeros_like(line), shift_of(parts)
     for k in range(bits):
@@ -411,12 +407,12 @@
         return pltpu.with_memory_space_constraint(x, pltpu.HBM)
 
     half_shape = jax.ShapeDtypeStruct((len(KEEP), 2 * tokens, DH), jnp.bfloat16)
-    slab_shape = jax.ShapeDtypeStruct((nears, 2 * lines + STAT_ROWS, DH), jnp.bfloat16)
+    slab_shape = jax.ShapeDtypeStruct((2 * lines + STAT_ROWS, DH), jnp.bfloat16)
     *slabs, kv_keep, kv_send = pl.pallas_call(
         functools.partial(pack_kernel, row_count, nears, heads),
         in_specs=[HBM] * 6,
-        out_specs=[VMEM] * (row_count + 2),
-        out_shape=[slab_shape] * row_count + [half_shape] * 2,
+        out_specs=[VMEM] * (groups + 2),
+        out_shape=[slab_shape] * groups + [half_shape] * 2,
         scratch_shapes=[
             pltpu.VMEM((own_lines, DH), jnp.bfloat16),
             pltpu.VMEM(lse_self.shape, jnp.float32),
@@ -431,16 +427,11 @@
         in_hbm(keys),
         in_hbm(values),
     )
-    slabs = [swap(x, "row", j, row_count) if j else x for j, x in enumerate(slabs)]
-    own_block = jnp.stack([x[n] for n in range(nears) for x in slabs])
+    own_block = jnp.stack(swap_slabs(slabs, groups))
     pairs = swap_pairs(kv_keep, kv_send)
     far = [1 << n for n in reversed(range(shift_of(parts)))]
 
-    def row_refs_of(x):
-        return [x, swap(x[row_count:], "near", 1, nears)] if nears > 1 else [x]
-
     blocks, came = [0], [own_block]
-    row_refs = row_refs_of(own_block)
     for d in far:
         if d == 1:
             came = came[:1] + [tie(x, pairs[1:]) for x in came[1:]]
@@ -456,11 +447,9 @@
             compiler_params=PARAMS,
         )(ends, *refs, *pairs, *before)
 
-    row_refs = row_refs + [ref for x in came[1:-1] for ref in row_refs_of(x)]
-    lse = [part_lse(blocks[:-1], 0, row_refs, [])]
-    last_refs = row_refs_of(tie(came[-1], lse))
-    lse = [part_lse(blocks[-1:], (parts - 1) * groups * lines, last_refs, lse)]
-    row_refs = row_refs + last_refs
+    lse = [part_lse(blocks[:-1], 0, came[:-1], [])]
+    row_refs = [*came[:-1], tie(came[-1], lse)]
+    lse = [part_lse(blocks[-1:], (parts - 1) * groups * lines, row_refs[-1:], lse)]
     every_lse = lse + [swap(lse[0], "part", d, parts) for d in range(1, parts)]
 
     all_lines = parts * groups * lines
@@ -472,42 +461,37 @@
         out_shape=[score_shape] * 2 + [jax.ShapeDtypeStruct((DH, all_lines), jnp.float32)],
         compiler_params=PARAMS,
     )(ends, *row_refs, *pairs, *lse)
-    dq_shape = jax.ShapeDtypeStruct((parts, row_count, lines, DH), jnp.bfloat16)
+    dq_shape = jax.ShapeDtypeStruct((parts, lines, DH), jnp.bfloat16)
     acc = pltpu.VMEM((len(KEEP), 2 * tokens, DH), jnp.float32)
     outs = pl.pallas_call(
         functools.partial(token_kernel, blocks, nears, heads, tokens),
         in_specs=[VMEM] * (1 + len(row_refs) + 3 + parts),
         out_shape=[jax.ShapeDtypeStruct((2, 2 * tokens, DH), jnp.bfloat16)] * len(KEEP)
-        + [dq_shape] * nears,
+        + [dq_shape] * groups,
         scratch_shapes=[acc] * 2,
         compiler_params=PARAMS,
     )(live, *row_refs, prob, dscore, dq, *every_lse)
     dkv, dq = outs[: len(KEEP)], outs[len(KEEP) :]
-    dq = [swap(x, "near", n, nears) if n else x for n, x in enumerate(dq)]
+    dq = swap_slabs(dq, groups)
     from_parts = [
         swap(jnp.stack([x[at] for x in dq]), "part", b, parts) for at, b in enumerate(blocks) if b
     ]
-    sum_shape = jax.ShapeDtypeStruct((nears, lines, DH), jnp.bfloat16)
-    sums = pl.pallas_call(
-        functools.partial(add_query_kernel, nears),
-        in_specs=[VMEM] * (nears + len(from_parts)),
-        out_shape=[sum_shape] * 2,
-        compiler_params=PARAMS,
-    )(*dq, *from_parts)
     pairs = swap_back(dkv, from_parts)
-    sums = [swap(x, "row", j, row_count) if j else x for j, x in enumerate(sums[:row_count])]
     out_q, out_k, out_v = pl.pallas_call(
         functools.partial(write_kernel, nears, heads),
-        in_specs=[VMEM] * (row_count + len(pairs)),
+        in_specs=[VMEM] * (len(pairs) + groups + parts - 1),
         out_specs=[HBM] * 3,
         out_shape=[
             jax.ShapeDtypeStruct((own_lines, DH), jnp.bfloat16),
             jax.ShapeDtypeStruct(keys.shape, jnp.bfloat16),
             jax.ShapeDtypeStruct(values.shape, jnp.bfloat16),
         ],
-        scratch_shapes=[pltpu.SemaphoreType.DMA((4 * len(KEEP) + groups,))],
+        scratch_shapes=[
+            pltpu.VMEM((groups, lines, DH), jnp.bfloat16),
+            pltpu.SemaphoreType.DMA((4 * len(KEEP) + groups,)),
+        ],
         compiler_params=PARAMS,
-    )(*sums, *pairs)
+    )(*pairs, *dq, *from_parts)
     out_q = out_q.reshape(own_heads, rows, DH).transpose(1, 0, 2).reshape(rows, own_heads * DH)
     return out_q, out_k, out_v
 

time: 52.8 us -> 52.8 us (level)
    ppermute x24 -> x23, starting transfers between devices: 27.2 us -> 27.4 us  [swap(): return lax.ppermute(x, axis, [(i, i ^ distance) for i in range(size)])]
    ppermute x24 -> x23, waiting for transfers between devices: 15.2 us -> 15.1 us  [swap(): return lax.ppermute(x, axis, [(i, i ^ distance) for i in range(size)])]
  transfers between devices with their start and end apart: 24 -> 23, of which waited for: 15 -> 11; matrix products, arithmetic and copies ran while one was open for 1% -> 1% of each run, Pallas kernels for 6% -> 6%
where the time goes in v11:
time: 52.8 us; the launch traced here: 52.6 us
  starting transfers between devices  27.4 us (52%)
  waiting for transfers between devices  15.1 us (29%)
  Pallas kernels  7.65 us (14%)
  between operations  2.11 us (4%)
    ppermute x23, starting transfers between devices, swap(): return lax.ppermute(x, axis, [(i, i ^ distance) for i in range(size)])  27.4 us
    ppermute x23, waiting for transfers between devices, swap(): return lax.ppermute(x, axis, [(i, i ^ distance) for i in range(size)])  15.1 us
    pallas_call x1, Pallas kernels, shards(): pl.pallas_call(functools.partial(part_kernel, blocks, nears, heads, token...  2.04 us
    pallas_call x2, Pallas kernels, part_lse(): pl.pallas_call(functools.partial(stat_kernel, held, first, nears, heads,...  1.77 us
    pallas_call x1, Pallas kernels, shards(): pl.pallas_call(functools.partial(token_kernel, blocks, nears, heads, toke...  1.48 us
    pallas_call x1, Pallas kernels, shards(): pl.pallas_call(functools.partial(pack_kernel, row_count, nears, heads), i...  1.37 us
  transfers between devices with their start and end apart: 23, of which 11 were waited for; matrix products, arithmetic and copies ran while one was open for 1% of the time, Pallas kernels for 6%

profile of v11, /device:TPU:0, one launch (start us, length us, event | category | flops | bytes accessed | tf_op | source)
XLA Modules:
  0.0 52.6 jit_solution(1939848000575591811)
XLA Ops:
  0.6 1.4 %shard_map.103 = (bf16[144,128]{1,0:T(8,128)(2,1)S(1)}, bf16[144,128]{1,0:T(8,128)(2,1)S(1)}, bf16[144,128]{1,0:T(8,128)(2,1)S(1)}, bf16[144,128]{1,0:T(8,128)(2...) custom-call(bf16[256,128]{1,0:T(8,128)(2,1)} %bitcast.29, bf16[256,128]{1,0:T(8,128)(2,1)} %bitcast.30, ...), custom_call_target="tpu_custom_call" | custom-call | tf_op jit(solution)/shard_map/pallas_call | solution.py:411
  2.0 0.5 collective-permute-start
  2.5 2.6 %collective-permute-start.1 = (bf16[144,128]{1,0:T(8,128)(2,1)S(1)}, bf16[144,128]{1,0:T(8,128)(2,1)S(1)}, u32[]{:S(2)}, u32[]{:S(2)}) collective-permute-start(bf16[144,128]{1,0:T(8,128)(2,1)S(1)} %get-tuple-element.25), channel_id=1, source_target_pairs={{0,4},{2,6},{4,0},{6,2},{1,5},{3,7},{5,1},{7,3},{8,12},{10,14},{12... | collective-permute-start | bytes 110600 | tf_op jit(solution)/shard_map/ppermute | solution.py:343
  5.1 0.1 collective-permute-start.2
  5.2 0.1 collective-permute-start.4
  5.4 1.8 %collective-permute-done.1 = bf16[144,128]{1,0:T(8,128)(2,1)S(1)} collective-permute-done((bf16[144,128]{1,0:T(8,128)(2,1)S(1)}, bf16[144,128]{1,0:T(8,128)(2,1)S(1)}, u32[]{:S(2)}, u32[]{:S(2)}) %collective-permute-start.1) | collective-permute-done | bytes 36896 | tf_op jit(solution)/shard_map/ppermute | solution.py:343
  7.2 1.4 %collective-permute-done.2 = bf16[144,128]{1,0:T(8,128)(2,1)S(1)} collective-permute-done((bf16[144,128]{1,0:T(8,128)(2,1)S(1)}, bf16[144,128]{1,0:T(8,128)(2,1)S(1)}, u32[]{:S(2)}, u32[]{:S(2)}) %collective-permute-start.2) | collective-permute-done | bytes 36896 | tf_op jit(solution)/shard_map/ppermute | solution.py:343
  8.6 2.7 %collective-permute-start.3 = (bf16[4,144,128]{2,1,0:T(8,128)(2,1)S(1)}, bf16[4,144,128]{2,1,0:T(8,128)(2,1)S(1)}, u32[]{:S(2)}, u32[]{:S(2)}) collective-permute-start(bf16[4,144,128]{2,1,0:T(8,128)(2,1)S(1)} %pad_maximum_fusion.1.refs_0_), channel_id=1, source_target_pairs={{0,16},{8,24},{16,0},{24,8},{1,17},{9,25},{17,1},{25,9},{2,18},{10... | collective-permute-start | bytes 442376 | tf_op jit(solution)/shard_map/ppermute | solution.py:343
  11.2 0.0 collective-permute-done.4
  11.3 1.6 %collective-permute-start.5 = (bf16[2,256,128]{2,1,0:T(8,128)(2,1)S(1)}, bf16[2,256,128]{2,1,0:T(8,128)(2,1)S(1)}, u32[]{:S(2)}, u32[]{:S(2)}) collective-permute-start(bf16[2,256,128]{2,1,0:T(8,128)(2,1)S(1)} %pad_maximum_fusion.2), channel_id=1, source_target_pairs={{0,1},{1,0},{2,3},{3,2},{4,5},{5,4},{6,7},{7,6},{8,9},{9,8},{10,11... | collective-permute-start | bytes 393224 | tf_op jit(solution)/shard_map/ppermute | solution.py:343
  12.9 0.9 %collective-permute-start.6 = (bf16[2,256,128]{2,1,0:T(8,128)(2,1)S(1)}, bf16[2,256,128]{2,1,0:T(8,128)(2,1)S(1)}, u32[]{:S(2)}, u32[]{:S(2)}) collective-permute-start(bf16[2,256,128]{2,1,0:T(8,128)(2,1)S(1)} %pad_maximum_fusion.3), channel_id=1, source_target_pairs={{0,4},{1,5},{2,6},{3,7},{4,0},{5,1},{6,2},{7,3},{8,12},{9,13},{10,... | collective-permute-start | bytes 393224 | tf_op jit(solution)/shard_map/ppermute | solution.py:343
  13.8 1.2 %collective-permute-start.7 = (bf16[2,256,128]{2,1,0:T(8,128)(2,1)S(1)}, bf16[2,256,128]{2,1,0:T(8,128)(2,1)S(1)}, u32[]{:S(2)}, u32[]{:S(2)}) collective-permute-start(bf16[2,256,128]{2,1,0:T(8,128)(2,1)S(1)} %pad_maximum_fusion.4), channel_id=1, source_target_pairs={{0,5},{1,4},{2,7},{3,6},{4,1},{5,0},{6,3},{7,2},{8,13},{9,12},{10,... | collective-permute-start | bytes 393224 | tf_op jit(solution)/shard_map/ppermute | solution.py:343
  15.7 1.6 %collective-permute-start.8 = (bf16[4,144,128]{2,1,0:T(8,128)(2,1)S(1)}, bf16[4,144,128]{2,1,0:T(8,128)(2,1)S(1)}, u32[]{:S(2)}, u32[]{:S(2)}) collective-permute-start(bf16[4,144,128]{2,1,0:T(8,128)(2,1)S(1)} %pad_maximum_fusion.1.refs_0_), channel_id=1, source_target_pairs={{0,8},{8,0},{16,24},{24,16},{1,9},{9,1},{17,25},{25,17},{2,10},{10... | collective-permute-start | bytes 442376 | tf_op jit(solution)/shard_map/ppermute | solution.py:343
  17.3 1.4 %collective-permute-done.3.refs_0_ = bf16[4,144,128]{2,1,0:T(8,128)(2,1)S(1)} collective-permute-done((bf16[4,144,128]{2,1,0:T(8,128)(2,1)S(1)}, bf16[4,144,128]{2,1,0:T(8,128)(2,1)S(1)}, u32[]{:S(2)}, u32[]{:S(2)}) %collective-permute-start.3) | collective-permute-done | bytes 147488 | tf_op jit(solution)/shard_map/ppermute | solution.py:343
  18.7 0.0 collective-permute-done.5.refs_1_.refs_4_.refs_2_.refs_5_
  18.7 2.0 %collective-permute-done.6.refs_2_.refs_5_.refs_3_.refs_6_ = bf16[2,256,128]{2,1,0:T(8,128)(2,1)S(1)} collective-permute-done((bf16[2,256,128]{2,1,0:T(8,128)(2,1)S(1)}, bf16[2,256,128]{2,1,0:T(8,128)(2,1)S(1)}, u32[]{:S(2)}, u32[]{:S(2)}) %collective-permute-start.6) | collective-permute-done | bytes 131104 | tf_op jit(solution)/shard_map/ppermute | solution.py:343
  20.7 0.0 collective-permute-done.7.refs_3_.refs_6_.refs_4_.refs_7_
  20.7 1.6 %collective-permute-start.9 = (bf16[4,144,128]{2,1,0:T(8,128)(2,1)S(1)}, bf16[4,144,128]{2,1,0:T(8,128)(2,1)S(1)}, u32[]{:S(2)}, u32[]{:S(2)}) collective-permute-start(bf16[4,144,128]{2,1,0:T(8,128)(2,1)S(1)} %shard_map.104.refs_1_), channel_id=1, source_target_pairs={{0,8},{8,0},{16,24},{24,16},{1,9},{9,1},{17,25},{25,17},{2,10},{10... | collective-permute-start | bytes 442376 | tf_op jit(solution)/shard_map/ppermute | solution.py:343
  23.0 0.0 collective-permute-done.8.refs_2_
  23.0 1.1 %shard_map.105.refs_1_.refs_5_ = f32[8,128]{1,0:T(8,128)S(1)} custom-call(s32[1,1024]{1,0:T(1,128)S(1)} %compare_select_fusion.ends_ref, bf16[4,144,128]{2,1,0:T(8,128)(2,1)S(1)} %pad_maximum_fusion.1.refs_0_, bf16[4,144,128]{2,1,0:T(8,128)(2,1)S(1)} %shard_map.104.refs_1_, bf16[4,144,128]{2,1,0:T(8,128)(2,1)S(1)} %collective-permute-done.8.refs_2_, ...), custom_call_target="tpu_custom_call" | custom-call | tf_op jit(solution)/shard_map/pallas_call | solution.py:443
  24.2 1.7 %collective-permute-done.9.refs_0_ = bf16[4,144,128]{2,1,0:T(8,128)(2,1)S(1)} collective-permute-done((bf16[4,144,128]{2,1,0:T(8,128)(2,1)S(1)}, bf16[4,144,128]{2,1,0:T(8,128)(2,1)S(1)}, u32[]{:S(2)}, u32[]{:S(2)}) %collective-permute-start.9) | collective-permute-done | bytes 147488 | tf_op jit(solution)/shard_map/ppermute | solution.py:343
  25.9 0.6 %shard_map.107.refs_8_.refs_7_ = f32[8,128]{1,0:T(8,128)S(1)} custom-call(s32[1,1024]{1,0:T(1,128)S(1)} %compare_select_fusion.ends_ref, bf16[4,144,128]{2,1,0:T(8,128)(2,1)S(1)} %shard_map.106.refs_0_.refs_3_, bf16[2,256,128]{2,1,0:T(8,128)(2,1)S(1)} %pad_maximum_fusion.5.refs_3_.refs_1_.refs_4_, ...), custom_call_target="tpu_custom_call" | custom-call | tf_op jit(solution)/shard_map/pallas_call | solution.py:443
  26.5 2.3 %collective-permute-start.12 = (f32[8,128]{1,0:T(8,128)S(1)}, f32[8,128]{1,0:T(8,128)S(1)}, u32[]{:S(2)}, u32[]{:S(2)}) collective-permute-start(f32[8,128]{1,0:T(8,128)S(1)} %shard_map.107.refs_8_.refs_7_), channel_id=1, source_target_pairs={{0,24},{8,16},{16,8},{24,0},{1,25},{9,17},{17,9},{25,1},{2,26},{10... | collective-permute-start | bytes 12296 | tf_op jit(solution)/shard_map/ppermute | solution.py:343
  28.8 0.8 %collective-permute-start.11 = (f32[8,128]{1,0:T(8,128)S(1)}, f32[8,128]{1,0:T(8,128)S(1)}, u32[]{:S(2)}, u32[]{:S(2)}) collective-permute-start(f32[8,128]{1,0:T(8,128)S(1)} %shard_map.107.refs_8_.refs_7_), channel_id=1, source_target_pairs={{0,16},{8,24},{16,0},{24,8},{1,17},{9,25},{17,1},{25,9},{2,18},{10... | collective-permute-start | bytes 12296 | tf_op jit(solution)/shard_map/ppermute | solution.py:343
  29.6 1.3 %collective-permute-start.10 = (f32[8,128]{1,0:T(8,128)S(1)}, f32[8,128]{1,0:T(8,128)S(1)}, u32[]{:S(2)}, u32[]{:S(2)}) collective-permute-start(f32[8,128]{1,0:T(8,128)S(1)} %shard_map.107.refs_8_.refs_7_), channel_id=1, source_target_pairs={{0,8},{8,0},{16,24},{24,16},{1,9},{9,1},{17,25},{25,17},{2,10},{10... | collective-permute-start | bytes 12296 | tf_op jit(solution)/shard_map/ppermute | solution.py:343
  31.0 2.0 %shard_map.108 = (bf16[4,256,1024]{2,1,0:T(8,128)(2,1)S(1)}, bf16[4,256,1024]{2,1,0:T(8,128)(2,1)S(1)}, f32[128,1024]{1,0:T(8,128)S(1)}) custom-call(s32[1,1024]{1,0:T(1,128)S(1)} %compare_select_fusion.ends_ref, bf16[4,144,128]{2,1,0:T(8,128)(2,1)S(1)} %pad_maximum_fusion.1.refs_0_, bf16[4,144,128]{2,1,0:T(8,128)(2,1)S(1)} %shard_map.104.refs_1_, ...), custom_call_target="tpu_custom_call" | custom-call | tf_op jit(solution)/shard_map/pallas_call | solution.py:457
  33.1 0.0 collective-permute-done.12.refs_10_
  33.1 0.2 collective-permute-done.11.refs_9_
  33.3 0.0 collective-permute-done.10.refs_8_
  33.3 1.5 %shard_map.109 = (bf16[2,256,128]{2,1,0:T(8,128)(2,1)S(1)}, bf16[2,256,128]{2,1,0:T(8,128)(2,1)S(1)}, bf16[2,256,128]{2,1,0:T(8,128)(2,1)S(1)}, bf16[2,256,128]{...) custom-call(s32[1,1024]{1,0:T(1,128)S(1)} %compare_convert_fusion.li, ...), custom_call_target="tpu_custom_call" | custom-call | tf_op jit(solution)/shard_map/pallas_call | solution.py:466
  34.8 0.1 collective-permute-start.16
  34.9 1.0 %collective-permute-start.17 = (bf16[4,64,128]{2,1,0:T(8,128)(2,1)S(1)}, bf16[4,64,128]{2,1,0:T(8,128)(2,1)S(1)}, u32[]{:S(2)}, u32[]{:S(2)}) collective-permute-start(bf16[4,64,128]{2,1,0:T(8,128)(2,1)S(1)} %get-tuple-element.38), channel_id=1, source_target_pairs={{0,4},{2,6},{4,0},{6,2},{1,5},{3,7},{5,1},{7,3},{8,12},{10,14},{12... | collective-permute-start | bytes 196616 | tf_op jit(solution)/shard_map/ppermute | solution.py:343
  35.9 0.9 %collective-permute-start.18 = (bf16[4,64,128]{2,1,0:T(8,128)(2,1)S(1)}, bf16[4,64,128]{2,1,0:T(8,128)(2,1)S(1)}, u32[]{:S(2)}, u32[]{:S(2)}) collective-permute-start(bf16[4,64,128]{2,1,0:T(8,128)(2,1)S(1)} %get-tuple-element.39), channel_id=1, source_target_pairs={{0,6},{2,4},{4,2},{6,0},{1,7},{3,5},{5,3},{7,1},{8,14},{10,12},{12... | collective-permute-start | bytes 196616 | tf_op jit(solution)/shard_map/ppermute | solution.py:343
  36.8 1.5 %collective-permute-start.13 = (bf16[2,256,128]{2,1,0:T(8,128)(2,1)S(1)}, bf16[2,256,128]{2,1,0:T(8,128)(2,1)S(1)}, u32[]{:S(2)}, u32[]{:S(2)}) collective-permute-start(bf16[2,256,128]{2,1,0:T(8,128)(2,1)S(1)} %get-tuple-element.33), channel_id=1, source_target_pairs={{0,1},{1,0},{2,3},{3,2},{4,5},{5,4},{6,7},{7,6},{8,9},{9,8},{10,11... | collective-permute-start | bytes 393224 | tf_op jit(solution)/shard_map/ppermute | solution.py:343
  38.3 0.9 %collective-permute-start.14 = (bf16[2,256,128]{2,1,0:T(8,128)(2,1)S(1)}, bf16[2,256,128]{2,1,0:T(8,128)(2,1)S(1)}, u32[]{:S(2)}, u32[]{:S(2)}) collective-permute-start(bf16[2,256,128]{2,1,0:T(8,128)(2,1)S(1)} %get-tuple-element.34), channel_id=1, source_target_pairs={{0,4},{1,5},{2,6},{3,7},{4,0},{5,1},{6,2},{7,3},{8,12},{9,13},{10,... | collective-permute-start | bytes 393224 | tf_op jit(solution)/shard_map/ppermute | solution.py:343
  39.2 0.0 collective-permute-done.16.refs_6_
  39.2 1.1 %collective-permute-start.15 = (bf16[2,256,128]{2,1,0:T(8,128)(2,1)S(1)}, bf16[2,256,128]{2,1,0:T(8,128)(2,1)S(1)}, u32[]{:S(2)}, u32[]{:S(2)}) collective-permute-start(bf16[2,256,128]{2,1,0:T(8,128)(2,1)S(1)} %get-tuple-element.35), channel_id=1, source_target_pairs={{0,5},{1,4},{2,7},{3,6},{4,1},{5,0},{6,3},{7,2},{8,13},{9,12},{10,... | collective-permute-start | bytes 393224 | tf_op jit(solution)/shard_map/ppermute | solution.py:343
  40.3 0.0 collective-permute-done.17.refs_7_
  40.3 0.1 collective-permute-done.18.refs_8_
  40.5 2.1 %collective-permute-start.19 = (bf16[4,64,128]{2,1,0:T(8,128)(2,1)S(1)}, bf16[4,64,128]{2,1,0:T(8,128)(2,1)S(1)}, u32[]{:S(2)}, u32[]{:S(2)}) collective-permute-start(bf16[4,64,128]{2,1,0:T(8,128)(2,1)S(1)} %pad_maximum_fusion.6), channel_id=1, source_target_pairs={{0,16},{8,24},{16,0},{24,8},{1,17},{9,25},{17,1},{25,9},{2,18},{10... | collective-permute-start | bytes 196616 | tf_op jit(solution)/shard_map/ppermute | solution.py:343
  42.6 0.6 %collective-permute-start.20 = (bf16[4,64,128]{2,1,0:T(8,128)(2,1)S(1)}, bf16[4,64,128]{2,1,0:T(8,128)(2,1)S(1)}, u32[]{:S(2)}, u32[]{:S(2)}) collective-permute-start(bf16[4,64,128]{2,1,0:T(8,128)(2,1)S(1)} %pad_maximum_fusion.7), channel_id=1, source_target_pairs={{0,8},{8,0},{16,24},{24,16},{1,9},{9,1},{17,25},{25,17},{2,10},{10... | collective-permute-start | bytes 196616 | tf_op jit(solution)/shard_map/ppermute | solution.py:343
  43.2 0.0 collective-permute-done.13.refs_1_
  43.2 1.9 %collective-permute-start.21 = (bf16[4,64,128]{2,1,0:T(8,128)(2,1)S(1)}, bf16[4,64,128]{2,1,0:T(8,128)(2,1)S(1)}, u32[]{:S(2)}, u32[]{:S(2)}) collective-permute-start(bf16[4,64,128]{2,1,0:T(8,128)(2,1)S(1)} %pad_maximum_fusion.8), channel_id=1, source_target_pairs={{0,24},{8,16},{16,8},{24,0},{1,25},{9,17},{17,9},{25,1},{2,26},{10... | collective-permute-start | bytes 196616 | tf_op jit(solution)/shard_map/ppermute | solution.py:343
  45.1 1.5 %collective-permute-done.14.refs_2_ = bf16[2,256,128]{2,1,0:T(8,128)(2,1)S(1)} collective-permute-done((bf16[2,256,128]{2,1,0:T(8,128)(2,1)S(1)}, bf16[2,256,128]{2,1,0:T(8,128)(2,1)S(1)}, u32[]{:S(2)}, u32[]{:S(2)}) %collective-permute-start.14) | collective-permute-done | bytes 131104 | tf_op jit(solution)/shard_map/ppermute | solution.py:343
  46.6 0.8 %collective-permute-done.19.refs_1_.refs_9_ = bf16[4,64,128]{2,1,0:T(8,128)(2,1)S(1)} collective-permute-done((bf16[4,64,128]{2,1,0:T(8,128)(2,1)S(1)}, bf16[4,64,128]{2,1,0:T(8,128)(2,1)S(1)}, u32[]{:S(2)}, u32[]{:S(2)}) %collective-permute-start.19) | collective-permute-done | bytes 65568 | tf_op jit(solution)/shard_map/ppermute | solution.py:343
  47.5 2.6 %collective-permute-done.21.refs_3_.refs_11_ = bf16[4,64,128]{2,1,0:T(8,128)(2,1)S(1)} collective-permute-done((bf16[4,64,128]{2,1,0:T(8,128)(2,1)S(1)}, bf16[4,64,128]{2,1,0:T(8,128)(2,1)S(1)}, u32[]{:S(2)}, u32[]{:S(2)}) %collective-permute-start.21) | collective-permute-done | bytes 65568 | tf_op jit(solution)/shard_map/ppermute | solution.py:343
  50.0 1.5 %collective-permute-done.22.refs_4_ = bf16[4,256,128]{2,1,0:T(8,128)(2,1)S(1)} collective-permute-done((bf16[4,256,128]{2,1,0:T(8,128)(2,1)S(1)}, bf16[4,256,128]{2,1,0:T(8,128)(2,1)S(1)}, u32[]{:S(2)}, u32[]{:S(2)}) %collective-permute-start.22) | collective-permute-done | bytes 262176 | tf_op jit(solution)/shard_map/ppermute | solution.py:343
  51.6 1.0 %shard_map.111 = (bf16[256,128]{1,0:T(8,128)(2,1)}, bf16[128,1024]{1,0:T(8,128)(2,1)}, bf16[128,1024]{1,0:T(8,128)(2,1)}) custom-call(bf16[2,256,128]{2,1,0:T(8,128)(2,1)S(1)} %get-tuple-element.32.refs_0_, bf16[2,256,128]{2,1,0:T(8,128)(2,1)S(1)} %collective-permute-done.13.refs_1_, bf16[2,256,128]{2,1,0:T(8,128)(2,1)S(1)} %collective-permute-done.14.refs_2_, ...), custom_call_target="tpu_custom_call" | custom-call | tf_op jit(solution)/shard_map/pallas_call | solution.py:480
  (28 shorter events, 0.3 us)
Async XLA Ops:
  2.0 3.3 %collective-permute-start = (bf16[144,128]{1,0:T(8,128)(2,1)S(1)}, bf16[144,128]{1,0:T(8,128)(2,1)S(1)}, u32[]{:S(2)}, u32[]{:S(2)}) collective-permute-start(bf16[144,128]{1,0:T(8,128)(2,1)S(1)} %get-tuple-element.24), channel_id=1, source_target_pairs={{0,2},{2,0},{4,6},{6,4},{1,3},{3,1},{5,7},{7,5},{8,10},{10,8},{12,... | collective-permute-start | bytes 110600 | tf_op jit(solution)/shard_map/ppermute | solution.py:343
  2.5 4.7 %collective-permute-start.1 = (bf16[144,128]{1,0:T(8,128)(2,1)S(1)}, bf16[144,128]{1,0:T(8,128)(2,1)S(1)}, u32[]{:S(2)}, u32[]{:S(2)}) collective-permute-start(bf16[144,128]{1,0:T(8,128)(2,1)S(1)} %get-tuple-element.25), channel_id=1, source_target_pairs={{0,4},{2,6},{4,0},{6,2},{1,5},{3,7},{5,1},{7,3},{8,12},{10,14},{12... | collective-permute-start | bytes 110600 | tf_op jit(solution)/shard_map/ppermute | solution.py:343
  5.1 3.4 %collective-permute-start.2 = (bf16[144,128]{1,0:T(8,128)(2,1)S(1)}, bf16[144,128]{1,0:T(8,128)(2,1)S(1)}, u32[]{:S(2)}, u32[]{:S(2)}) collective-permute-start(bf16[144,128]{1,0:T(8,128)(2,1)S(1)} %get-tuple-element.26), channel_id=1, source_target_pairs={{0,6},{2,4},{4,2},{6,0},{1,7},{3,5},{5,3},{7,1},{8,14},{10,12},{12... | collective-permute-start | bytes 110600 | tf_op jit(solution)/shard_map/ppermute | solution.py:343
  5.2 6.0 %collective-permute-start.4 = (bf16[4,256,128]{2,1,0:T(8,128)(2,1)S(1)}, bf16[4,256,128]{2,1,0:T(8,128)(2,1)S(1)}, u32[]{:S(2)}, u32[]{:S(2)}) collective-permute-start(bf16[4,256,128]{2,1,0:T(8,128)(2,1)S(1)} %get-tuple-element.28), channel_id=1, source_target_pairs={{0,2},{1,3},{2,0},{3,1},{4,6},{5,7},{6,4},{7,5},{8,10},{9,11},{10,... | collective-permute-start | bytes 786440 | tf_op jit(solution)/shard_map/ppermute | solution.py:343
  8.6 10.1 %collective-permute-start.3 = (bf16[4,144,128]{2,1,0:T(8,128)(2,1)S(1)}, bf16[4,144,128]{2,1,0:T(8,128)(2,1)S(1)}, u32[]{:S(2)}, u32[]{:S(2)}) collective-permute-start(bf16[4,144,128]{2,1,0:T(8,128)(2,1)S(1)} %pad_maximum_fusion.1.refs_0_), channel_id=1, source_target_pairs={{0,16},{8,24},{16,0},{24,8},{1,17},{9,25},{17,1},{25,9},{2,18},{10... | collective-permute-start | bytes 442376 | tf_op jit(solution)/shard_map/ppermute | solution.py:343
  11.3 7.4 %collective-permute-start.5 = (bf16[2,256,128]{2,1,0:T(8,128)(2,1)S(1)}, bf16[2,256,128]{2,1,0:T(8,128)(2,1)S(1)}, u32[]{:S(2)}, u32[]{:S(2)}) collective-permute-start(bf16[2,256,128]{2,1,0:T(8,128)(2,1)S(1)} %pad_maximum_fusion.2), channel_id=1, source_target_pairs={{0,1},{1,0},{2,3},{3,2},{4,5},{5,4},{6,7},{7,6},{8,9},{9,8},{10,11... | collective-permute-start | bytes 393224 | tf_op jit(solution)/shard_map/ppermute | solution.py:343
  12.9 7.9 %collective-permute-start.6 = (bf16[2,256,128]{2,1,0:T(8,128)(2,1)S(1)}, bf16[2,256,128]{2,1,0:T(8,128)(2,1)S(1)}, u32[]{:S(2)}, u32[]{:S(2)}) collective-permute-start(bf16[2,256,128]{2,1,0:T(8,128)(2,1)S(1)} %pad_maximum_fusion.3), channel_id=1, source_target_pairs={{0,4},{1,5},{2,6},{3,7},{4,0},{5,1},{6,2},{7,3},{8,12},{9,13},{10,... | collective-permute-start | bytes 393224 | tf_op jit(solution)/shard_map/ppermute | solution.py:343
  13.8 6.9 %collective-permute-start.7 = (bf16[2,256,128]{2,1,0:T(8,128)(2,1)S(1)}, bf16[2,256,128]{2,1,0:T(8,128)(2,1)S(1)}, u32[]{:S(2)}, u32[]{:S(2)}) collective-permute-start(bf16[2,256,128]{2,1,0:T(8,128)(2,1)S(1)} %pad_maximum_fusion.4), channel_id=1, source_target_pairs={{0,5},{1,4},{2,7},{3,6},{4,1},{5,0},{6,3},{7,2},{8,13},{9,12},{10,... | collective-permute-start | bytes 393224 | tf_op jit(solution)/shard_map/ppermute | solution.py:343
  15.7 7.4 %collective-permute-start.8 = (bf16[4,144,128]{2,1,0:T(8,128)(2,1)S(1)}, bf16[4,144,128]{2,1,0:T(8,128)(2,1)S(1)}, u32[]{:S(2)}, u32[]{:S(2)}) collective-permute-start(bf16[4,144,128]{2,1,0:T(8,128)(2,1)S(1)} %pad_maximum_fusion.1.refs_0_), channel_id=1, source_target_pairs={{0,8},{8,0},{16,24},{24,16},{1,9},{9,1},{17,25},{25,17},{2,10},{10... | collective-permute-start | bytes 442376 | tf_op jit(solution)/shard_map/ppermute | solution.py:343
  20.7 5.1 %collective-permute-start.9 = (bf16[4,144,128]{2,1,0:T(8,128)(2,1)S(1)}, bf16[4,144,128]{2,1,0:T(8,128)(2,1)S(1)}, u32[]{:S(2)}, u32[]{:S(2)}) collective-permute-start(bf16[4,144,128]{2,1,0:T(8,128)(2,1)S(1)} %shard_map.104.refs_1_), channel_id=1, source_target_pairs={{0,8},{8,0},{16,24},{24,16},{1,9},{9,1},{17,25},{25,17},{2,10},{10... | collective-permute-start | bytes 442376 | tf_op jit(solution)/shard_map/ppermute | solution.py:343
  26.5 6.5 %collective-permute-start.12 = (f32[8,128]{1,0:T(8,128)S(1)}, f32[8,128]{1,0:T(8,128)S(1)}, u32[]{:S(2)}, u32[]{:S(2)}) collective-permute-start(f32[8,128]{1,0:T(8,128)S(1)} %shard_map.107.refs_8_.refs_7_), channel_id=1, source_target_pairs={{0,24},{8,16},{16,8},{24,0},{1,25},{9,17},{17,9},{25,1},{2,26},{10... | collective-permute-start | bytes 12296 | tf_op jit(solution)/shard_map/ppermute | solution.py:343
  28.8 4.5 %collective-permute-start.11 = (f32[8,128]{1,0:T(8,128)S(1)}, f32[8,128]{1,0:T(8,128)S(1)}, u32[]{:S(2)}, u32[]{:S(2)}) collective-permute-start(f32[8,128]{1,0:T(8,128)S(1)} %shard_map.107.refs_8_.refs_7_), channel_id=1, source_target_pairs={{0,16},{8,24},{16,0},{24,8},{1,17},{9,25},{17,1},{25,9},{2,18},{10... | collective-permute-start | bytes 12296 | tf_op jit(solution)/shard_map/ppermute | solution.py:343
  29.6 3.7 %collective-permute-start.10 = (f32[8,128]{1,0:T(8,128)S(1)}, f32[8,128]{1,0:T(8,128)S(1)}, u32[]{:S(2)}, u32[]{:S(2)}) collective-permute-start(f32[8,128]{1,0:T(8,128)S(1)} %shard_map.107.refs_8_.refs_7_), channel_id=1, source_target_pairs={{0,8},{8,0},{16,24},{24,16},{1,9},{9,1},{17,25},{25,17},{2,10},{10... | collective-permute-start | bytes 12296 | tf_op jit(solution)/shard_map/ppermute | solution.py:343
  34.8 4.4 %collective-permute-start.16 = (bf16[4,64,128]{2,1,0:T(8,128)(2,1)S(1)}, bf16[4,64,128]{2,1,0:T(8,128)(2,1)S(1)}, u32[]{:S(2)}, u32[]{:S(2)}) collective-permute-start(bf16[4,64,128]{2,1,0:T(8,128)(2,1)S(1)} %get-tuple-element.37), channel_id=1, source_target_pairs={{0,2},{2,0},{4,6},{6,4},{1,3},{3,1},{5,7},{7,5},{8,10},{10,8},{12,... | collective-permute-start | bytes 196616 | tf_op jit(solution)/shard_map/ppermute | solution.py:343
  34.9 5.4 %collective-permute-start.17 = (bf16[4,64,128]{2,1,0:T(8,128)(2,1)S(1)}, bf16[4,64,128]{2,1,0:T(8,128)(2,1)S(1)}, u32[]{:S(2)}, u32[]{:S(2)}) collective-permute-start(bf16[4,64,128]{2,1,0:T(8,128)(2,1)S(1)} %get-tuple-element.38), channel_id=1, source_target_pairs={{0,4},{2,6},{4,0},{6,2},{1,5},{3,7},{5,1},{7,3},{8,12},{10,14},{12... | collective-permute-start | bytes 196616 | tf_op jit(solution)/shard_map/ppermute | solution.py:343
  35.9 4.6 %collective-permute-start.18 = (bf16[4,64,128]{2,1,0:T(8,128)(2,1)S(1)}, bf16[4,64,128]{2,1,0:T(8,128)(2,1)S(1)}, u32[]{:S(2)}, u32[]{:S(2)}) collective-permute-start(bf16[4,64,128]{2,1,0:T(8,128)(2,1)S(1)} %get-tuple-element.39), channel_id=1, source_target_pairs={{0,6},{2,4},{4,2},{6,0},{1,7},{3,5},{5,3},{7,1},{8,14},{10,12},{12... | collective-permute-start | bytes 196616 | tf_op jit(solution)/shard_map/ppermute | solution.py:343
  36.8 6.4 %collective-permute-start.13 = (bf16[2,256,128]{2,1,0:T(8,128)(2,1)S(1)}, bf16[2,256,128]{2,1,0:T(8,128)(2,1)S(1)}, u32[]{:S(2)}, u32[]{:S(2)}) collective-permute-start(bf16[2,256,128]{2,1,0:T(8,128)(2,1)S(1)} %get-tuple-element.33), channel_id=1, source_target_pairs={{0,1},{1,0},{2,3},{3,2},{4,5},{5,4},{6,7},{7,6},{8,9},{9,8},{10,11... | collective-permute-start | bytes 393224 | tf_op jit(solution)/shard_map/ppermute | solution.py:343
  38.3 8.2 %collective-permute-start.14 = (bf16[2,256,128]{2,1,0:T(8,128)(2,1)S(1)}, bf16[2,256,128]{2,1,0:T(8,128)(2,1)S(1)}, u32[]{:S(2)}, u32[]{:S(2)}) collective-permute-start(bf16[2,256,128]{2,1,0:T(8,128)(2,1)S(1)} %get-tuple-element.34), channel_id=1, source_target_pairs={{0,4},{1,5},{2,6},{3,7},{4,0},{5,1},{6,2},{7,3},{8,12},{9,13},{10,... | collective-permute-start | bytes 393224 | tf_op jit(solution)/shard_map/ppermute | solution.py:343
  39.2 7.4 %collective-permute-start.15 = (bf16[2,256,128]{2,1,0:T(8,128)(2,1)S(1)}, bf16[2,256,128]{2,1,0:T(8,128)(2,1)S(1)}, u32[]{:S(2)}, u32[]{:S(2)}) collective-permute-start(bf16[2,256,128]{2,1,0:T(8,128)(2,1)S(1)} %get-tuple-element.35), channel_id=1, source_target_pairs={{0,5},{1,4},{2,7},{3,6},{4,1},{5,0},{6,3},{7,2},{8,13},{9,12},{10,... | collective-permute-start | bytes 393224 | tf_op jit(solution)/shard_map/ppermute | solution.py:343
  40.5 7.0 %collective-permute-start.19 = (bf16[4,64,128]{2,1,0:T(8,128)(2,1)S(1)}, bf16[4,64,128]{2,1,0:T(8,128)(2,1)S(1)}, u32[]{:S(2)}, u32[]{:S(2)}) collective-permute-start(bf16[4,64,128]{2,1,0:T(8,128)(2,1)S(1)} %pad_maximum_fusion.6), channel_id=1, source_target_pairs={{0,16},{8,24},{16,0},{24,8},{1,17},{9,25},{17,1},{25,9},{2,18},{10... | collective-permute-start | bytes 196616 | tf_op jit(solution)/shard_map/ppermute | solution.py:343
  42.6 4.9 %collective-permute-start.20 = (bf16[4,64,128]{2,1,0:T(8,128)(2,1)S(1)}, bf16[4,64,128]{2,1,0:T(8,128)(2,1)S(1)}, u32[]{:S(2)}, u32[]{:S(2)}) collective-permute-start(bf16[4,64,128]{2,1,0:T(8,128)(2,1)S(1)} %pad_maximum_fusion.7), channel_id=1, source_target_pairs={{0,8},{8,0},{16,24},{24,16},{1,9},{9,1},{17,25},{25,17},{2,10},{10... | collective-permute-start | bytes 196616 | tf_op jit(solution)/shard_map/ppermute | solution.py:343
  43.2 6.9 %collective-permute-start.21 = (bf16[4,64,128]{2,1,0:T(8,128)(2,1)S(1)}, bf16[4,64,128]{2,1,0:T(8,128)(2,1)S(1)}, u32[]{:S(2)}, u32[]{:S(2)}) collective-permute-start(bf16[4,64,128]{2,1,0:T(8,128)(2,1)S(1)} %pad_maximum_fusion.8), channel_id=1, source_target_pairs={{0,24},{8,16},{16,8},{24,0},{1,25},{9,17},{17,9},{25,1},{2,26},{10... | collective-permute-start | bytes 196616 | tf_op jit(solution)/shard_map/ppermute | solution.py:343
  50.0 1.5 %collective-permute-start.22 = (bf16[4,256,128]{2,1,0:T(8,128)(2,1)S(1)}, bf16[4,256,128]{2,1,0:T(8,128)(2,1)S(1)}, u32[]{:S(2)}, u32[]{:S(2)}) collective-permute-start(bf16[4,256,128]{2,1,0:T(8,128)(2,1)S(1)} %shard_map.110), channel_id=1, source_target_pairs={{0,2},{1,3},{2,0},{3,1},{4,6},{5,7},{6,4},{7,5},{8,10},{9,11},{10,... | collective-permute-start | bytes 786440 | tf_op jit(solution)/shard_map/ppermute | solution.py:343

commit v12 on v11

--- a/solution.py
+++ b/solution.py
@@ -281,10 +281,10 @@
         lse = jnp.where(live_ref[:, lanes] > 0, peak + jnp.log(total), DEAD_LSE)
         weight = jnp.exp(part_lse[0] - lse)
         dq = (dq_ref[:, lanes] * (weight * SCALE)).T.astype(jnp.bfloat16)
-        groups = len(dq_refs)
+        groups = len(all_slabs[0])
         for m in range(len(slabs)):
-            block = first // size + m // groups
-            dq_refs[m % groups][block] = dq[m * lines : (m + 1) * lines]
+            block, j, n = first // size + m // groups, m % groups // nears, m % nears
+            dq_refs[n][block, j] = dq[m * lines : (m + 1) * lines]
         weight_t = jnp.broadcast_to(weight, (DH, count)).T
         q, o_grad = (
             (lines_of(slabs, start, lines).astype(jnp.float32) * weight_t).astype(jnp.bfloat16)
@@ -306,35 +306,38 @@
                     dkv_refs[i][n, tokens : 2 * tokens, :] = dv[inner].astype(jnp.bfloat16)
 
 
+def add_query_kernel(nears, *refs):
+    own_refs, came_refs, out_refs = refs[:nears], refs[nears:-2], refs[-2:]
+    for n in range(nears):
+        for j in range(own_refs[0].shape[1]):
+            total = own_refs[n][0, j].astype(jnp.float32)
+            for ref in came_refs:
+                total = total + ref[n, j].astype(jnp.float32)
+            out_refs[min(j, 1)][n] = total.astype(jnp.bfloat16)
+
+
 def tie_kernel(*refs):
     pass
 
 
 def write_kernel(nears, heads, *refs):
     at = place(nears, heads)
-    out_q_ref, out_k_ref, out_v_ref, sum_ref, sems = refs[-5:]
-    pair_refs, came_ref, refs = refs[: len(KEEP)], refs[len(KEEP)], refs[len(KEEP) + 1 : -5]
-    groups, lines, _ = sum_ref.shape
-    own_refs, part_refs = refs[:groups], refs[groups:]
-    tokens = out_k_ref.shape[0]
+    pair_refs, came_ref, refs = refs[: len(KEEP)], refs[len(KEEP)], refs[len(KEEP) + 1 :]
+    slab_refs, (out_q_ref, out_k_ref, out_v_ref, sems) = refs[:-4], refs[-4:]
+    groups, lines, tokens = len(slab_refs) * nears, slab_refs[0].shape[1], out_k_ref.shape[0]
     copies = []
     for i, ref in enumerate(pair_refs):
         for source, other in ((ref.at[0], 0), (came_ref.at[i], FIRST)):
             columns = pl.ds(column_of(at[0] ^ KEEP[i] ^ other, groups, heads), DH)
             copies.append((source.at[0:tokens, :], out_k_ref.at[:, columns]))
             copies.append((source.at[tokens : 2 * tokens, :], out_v_ref.at[:, columns]))
-    for m in range(groups):
-        first = pl.multiple_of(group_at(at, m // nears, m % nears, nears) * lines, lines)
-        copies.append((sum_ref.at[m], out_q_ref.at[pl.ds(first, lines), :]))
+    for j, ref in enumerate(slab_refs):
+        for n in range(nears):
+            first = pl.multiple_of(group_at(at, j, n, nears) * lines, lines)
+            copies.append((ref.at[n], out_q_ref.at[pl.ds(first, lines), :]))
     copies = [pltpu.make_async_copy(s, t, sems.at[n]) for n, (s, t) in enumerate(copies)]
-    for copy in copies[:-groups]:
+    for copy in copies:
         copy.start()
-    for m in range(groups):
-        total = own_refs[m][0].astype(jnp.float32)
-        for ref in part_refs:
-            total = total + ref[m].astype(jnp.float32)
-        sum_ref[m] = total.astype(jnp.bfloat16)
-        copies[m - groups].start()
     for copy in copies:
         copy.wait()
 
@@ -461,37 +464,42 @@
         out_shape=[score_shape] * 2 + [jax.ShapeDtypeStruct((DH, all_lines), jnp.float32)],
         compiler_params=PARAMS,
     )(ends, *row_refs, *pairs, *lse)
-    dq_shape = jax.ShapeDtypeStruct((parts, lines, DH), jnp.bfloat16)
+    dq_shape = jax.ShapeDtypeStruct((parts, row_count, lines, DH), jnp.bfloat16)
     acc = pltpu.VMEM((len(KEEP), 2 * tokens, DH), jnp.float32)
     outs = pl.pallas_call(
         functools.partial(token_kernel, blocks, nears, heads, tokens),
         in_specs=[VMEM] * (1 + len(row_refs) + 3 + parts),
         out_shape=[jax.ShapeDtypeStruct((2, 2 * tokens, DH), jnp.bfloat16)] * len(KEEP)
-        + [dq_shape] * groups,
+        + [dq_shape] * nears,
         scratch_shapes=[acc] * 2,
         compiler_params=PARAMS,
     )(live, *row_refs, prob, dscore, dq, *every_lse)
     dkv, dq = outs[: len(KEEP)], outs[len(KEEP) :]
-    dq = swap_slabs(dq, groups)
+    dq = [swap(x, "near", n, nears) if n else x for n, x in enumerate(dq)]
     from_parts = [
         swap(jnp.stack([x[at] for x in dq]), "part", b, parts) for at, b in enumerate(blocks) if b
     ]
-    pairs = swap_back(dkv, from_parts)
+    sum_shape = jax.ShapeDtypeStruct((nears, lines, DH), jnp.bfloat16)
+    sums = pl.pallas_call(
+        functools.partial(add_query_kernel, nears),
+        in_specs=[VMEM] * (nears + len(from_parts)),
+        out_shape=[sum_shape] * 2,
+        compiler_params=PARAMS,
+    )(*dq, *from_parts)
+    sums = [swap(x, "row", j, row_count) if j else x for j, x in enumerate(sums[:row_count])]
+    pairs = swap_back(dkv, sums[:1])
     out_q, out_k, out_v = pl.pallas_call(
         functools.partial(write_kernel, nears, heads),
-        in_specs=[VMEM] * (len(pairs) + groups + parts - 1),
+        in_specs=[VMEM] * (row_count + len(pairs)),
         out_specs=[HBM] * 3,
         out_shape=[
             jax.ShapeDtypeStruct((own_lines, DH), jnp.bfloat16),
             jax.ShapeDtypeStruct(keys.shape, jnp.bfloat16),
             jax.ShapeDtypeStruct(values.shape, jnp.bfloat16),
         ],
-        scratch_shapes=[
-            pltpu.VMEM((groups, lines, DH), jnp.bfloat16),
-            pltpu.SemaphoreType.DMA((4 * len(KEEP) + groups,)),
-        ],
+        scratch_shapes=[pltpu.SemaphoreType.DMA((4 * len(KEEP) + groups,))],
         compiler_params=PARAMS,
-    )(*pairs, *dq, *from_parts)
+    )(*pairs, *sums)
     out_q = out_q.reshape(own_heads, rows, DH).transpose(1, 0, 2).reshape(rows, own_heads * DH)
     return out_q, out_k, out_v
 

time: 52.8 us -> 53.9 us (1.021)
  waiting for transfers between devices: 15.1 us -> 17.1 us
  starting transfers between devices: 27.4 us -> 26.5 us
    ppermute x23 -> x22, waiting for transfers between devices: 15.1 us -> 17.1 us  [swap(): return lax.ppermute(x, axis, [(i, i ^ distance) for i in range(size)])]
    ppermute x23 -> x22, starting transfers between devices: 27.4 us -> 26.5 us  [swap(): return lax.ppermute(x, axis, [(i, i ^ distance) for i in range(size)])]
  transfers between devices with their start and end apart: 23 -> 22, of which waited for: 11 -> 10; matrix products, arithmetic and copies ran while one was open for 1% -> 1% of each run, Pallas kernels for 6% -> 6%
where the time goes in v12:
time: 53.9 us; the launch traced here: 53.7 us
  starting transfers between devices  26.5 us (49%)
  waiting for transfers between devices  17.1 us (32%)
  Pallas kernels  7.67 us (14%)
  between operations  2.12 us (4%)
    ppermute x22, starting transfers between devices, swap(): return lax.ppermute(x, axis, [(i, i ^ distance) for i in range(size)])  26.5 us
    ppermute x22, waiting for transfers between devices, swap(): return lax.ppermute(x, axis, [(i, i ^ distance) for i in range(size)])  17.1 us
    pallas_call x1, Pallas kernels, shards(): pl.pallas_call(functools.partial(part_kernel, blocks, nears, heads, token...  2.04 us
    pallas_call x2, Pallas kernels, part_lse(): pl.pallas_call(functools.partial(stat_kernel, held, first, nears, heads,...  1.77 us
    pallas_call x1, Pallas kernels, shards(): pl.pallas_call(functools.partial(token_kernel, blocks, nears, heads, toke...  1.48 us
    pallas_call x1, Pallas kernels, shards(): pl.pallas_call(functools.partial(pack_kernel, row_count, nears, heads), i...  1.37 us
  transfers between devices with their start and end apart: 22, of which 10 were waited for; matrix products, arithmetic and copies ran while one was open for 1% of the time, Pallas kernels for 6%

profile of v12, /device:TPU:0, one launch (start us, length us, event | category | flops | bytes accessed | tf_op | source)
XLA Modules:
  0.0 53.7 jit_solution(11657489592091505270)
XLA Ops:
  0.6 1.4 %shard_map.103 = (bf16[144,128]{1,0:T(8,128)(2,1)S(1)}, bf16[144,128]{1,0:T(8,128)(2,1)S(1)}, bf16[144,128]{1,0:T(8,128)(2,1)S(1)}, bf16[144,128]{1,0:T(8,128)(2...) custom-call(bf16[256,128]{1,0:T(8,128)(2,1)} %bitcast.29, bf16[256,128]{1,0:T(8,128)(2,1)} %bitcast.30, ...), custom_call_target="tpu_custom_call" | custom-call | tf_op jit(solution)/shard_map/pallas_call | solution.py:414
  2.0 0.5 collective-permute-start
  2.5 2.6 %collective-permute-start.1 = (bf16[144,128]{1,0:T(8,128)(2,1)S(1)}, bf16[144,128]{1,0:T(8,128)(2,1)S(1)}, u32[]{:S(2)}, u32[]{:S(2)}) collective-permute-start(bf16[144,128]{1,0:T(8,128)(2,1)S(1)} %get-tuple-element.25), channel_id=1, source_target_pairs={{0,4},{2,6},{4,0},{6,2},{1,5},{3,7},{5,1},{7,3},{8,12},{10,14},{12... | collective-permute-start | bytes 110600 | tf_op jit(solution)/shard_map/ppermute | solution.py:346
  5.1 0.1 collective-permute-start.2
  5.2 0.1 collective-permute-start.4
  5.4 0.0 collective-permute-done
  5.4 1.8 %collective-permute-done.1 = bf16[144,128]{1,0:T(8,128)(2,1)S(1)} collective-permute-done((bf16[144,128]{1,0:T(8,128)(2,1)S(1)}, bf16[144,128]{1,0:T(8,128)(2,1)S(1)}, u32[]{:S(2)}, u32[]{:S(2)}) %collective-permute-start.1) | collective-permute-done | bytes 36896 | tf_op jit(solution)/shard_map/ppermute | solution.py:346
  7.2 1.4 %collective-permute-done.2 = bf16[144,128]{1,0:T(8,128)(2,1)S(1)} collective-permute-done((bf16[144,128]{1,0:T(8,128)(2,1)S(1)}, bf16[144,128]{1,0:T(8,128)(2,1)S(1)}, u32[]{:S(2)}, u32[]{:S(2)}) %collective-permute-start.2) | collective-permute-done | bytes 36896 | tf_op jit(solution)/shard_map/ppermute | solution.py:346
  8.6 2.7 %collective-permute-start.3 = (bf16[4,144,128]{2,1,0:T(8,128)(2,1)S(1)}, bf16[4,144,128]{2,1,0:T(8,128)(2,1)S(1)}, u32[]{:S(2)}, u32[]{:S(2)}) collective-permute-start(bf16[4,144,128]{2,1,0:T(8,128)(2,1)S(1)} %pad_maximum_fusion.1.refs_0_), channel_id=1, source_target_pairs={{0,16},{8,24},{16,0},{24,8},{1,17},{9,25},{17,1},{25,9},{2,18},{10... | collective-permute-start | bytes 442376 | tf_op jit(solution)/shard_map/ppermute | solution.py:346
  11.2 0.0 collective-permute-done.4
  11.3 1.6 %collective-permute-start.5 = (bf16[2,256,128]{2,1,0:T(8,128)(2,1)S(1)}, bf16[2,256,128]{2,1,0:T(8,128)(2,1)S(1)}, u32[]{:S(2)}, u32[]{:S(2)}) collective-permute-start(bf16[2,256,128]{2,1,0:T(8,128)(2,1)S(1)} %pad_maximum_fusion.2), channel_id=1, source_target_pairs={{0,1},{1,0},{2,3},{3,2},{4,5},{5,4},{6,7},{7,6},{8,9},{9,8},{10,11... | collective-permute-start | bytes 393224 | tf_op jit(solution)/shard_map/ppermute | solution.py:346
  12.9 0.9 %collective-permute-start.6 = (bf16[2,256,128]{2,1,0:T(8,128)(2,1)S(1)}, bf16[2,256,128]{2,1,0:T(8,128)(2,1)S(1)}, u32[]{:S(2)}, u32[]{:S(2)}) collective-permute-start(bf16[2,256,128]{2,1,0:T(8,128)(2,1)S(1)} %pad_maximum_fusion.3), channel_id=1, source_target_pairs={{0,4},{1,5},{2,6},{3,7},{4,0},{5,1},{6,2},{7,3},{8,12},{9,13},{10,... | collective-permute-start | bytes 393224 | tf_op jit(solution)/shard_map/ppermute | solution.py:346
  13.8 1.2 %collective-permute-start.7 = (bf16[2,256,128]{2,1,0:T(8,128)(2,1)S(1)}, bf16[2,256,128]{2,1,0:T(8,128)(2,1)S(1)}, u32[]{:S(2)}, u32[]{:S(2)}) collective-permute-start(bf16[2,256,128]{2,1,0:T(8,128)(2,1)S(1)} %pad_maximum_fusion.4), channel_id=1, source_target_pairs={{0,5},{1,4},{2,7},{3,6},{4,1},{5,0},{6,3},{7,2},{8,13},{9,12},{10,... | collective-permute-start | bytes 393224 | tf_op jit(solution)/shard_map/ppermute | solution.py:346
  15.7 1.6 %collective-permute-start.8 = (bf16[4,144,128]{2,1,0:T(8,128)(2,1)S(1)}, bf16[4,144,128]{2,1,0:T(8,128)(2,1)S(1)}, u32[]{:S(2)}, u32[]{:S(2)}) collective-permute-start(bf16[4,144,128]{2,1,0:T(8,128)(2,1)S(1)} %pad_maximum_fusion.1.refs_0_), channel_id=1, source_target_pairs={{0,8},{8,0},{16,24},{24,16},{1,9},{9,1},{17,25},{25,17},{2,10},{10... | collective-permute-start | bytes 442376 | tf_op jit(solution)/shard_map/ppermute | solution.py:346
  17.3 1.4 %collective-permute-done.3.refs_0_ = bf16[4,144,128]{2,1,0:T(8,128)(2,1)S(1)} collective-permute-done((bf16[4,144,128]{2,1,0:T(8,128)(2,1)S(1)}, bf16[4,144,128]{2,1,0:T(8,128)(2,1)S(1)}, u32[]{:S(2)}, u32[]{:S(2)}) %collective-permute-start.3) | collective-permute-done | bytes 147488 | tf_op jit(solution)/shard_map/ppermute | solution.py:346
  18.7 0.0 collective-permute-done.5.refs_1_.refs_4_.refs_2_.refs_5_
  18.7 2.0 %collective-permute-done.6.refs_2_.refs_5_.refs_3_.refs_6_ = bf16[2,256,128]{2,1,0:T(8,128)(2,1)S(1)} collective-permute-done((bf16[2,256,128]{2,1,0:T(8,128)(2,1)S(1)}, bf16[2,256,128]{2,1,0:T(8,128)(2,1)S(1)}, u32[]{:S(2)}, u32[]{:S(2)}) %collective-permute-start.6) | collective-permute-done | bytes 131104 | tf_op jit(solution)/shard_map/ppermute | solution.py:346
  20.7 0.0 collective-permute-done.7.refs_3_.refs_6_.refs_4_.refs_7_
  20.7 1.6 %collective-permute-start.9 = (bf16[4,144,128]{2,1,0:T(8,128)(2,1)S(1)}, bf16[4,144,128]{2,1,0:T(8,128)(2,1)S(1)}, u32[]{:S(2)}, u32[]{:S(2)}) collective-permute-start(bf16[4,144,128]{2,1,0:T(8,128)(2,1)S(1)} %shard_map.104.refs_1_), channel_id=1, source_target_pairs={{0,8},{8,0},{16,24},{24,16},{1,9},{9,1},{17,25},{25,17},{2,10},{10... | collective-permute-start | bytes 442376 | tf_op jit(solution)/shard_map/ppermute | solution.py:346
  23.0 0.0 collective-permute-done.8.refs_2_
  23.0 1.1 %shard_map.105.refs_1_.refs_5_ = f32[8,128]{1,0:T(8,128)S(1)} custom-call(s32[1,1024]{1,0:T(1,128)S(1)} %compare_select_fusion.ends_ref, bf16[4,144,128]{2,1,0:T(8,128)(2,1)S(1)} %pad_maximum_fusion.1.refs_0_, bf16[4,144,128]{2,1,0:T(8,128)(2,1)S(1)} %shard_map.104.refs_1_, bf16[4,144,128]{2,1,0:T(8,128)(2,1)S(1)} %collective-permute-done.8.refs_2_, ...), custom_call_target="tpu_custom_call" | custom-call | tf_op jit(solution)/shard_map/pallas_call | solution.py:446
  24.2 1.7 %collective-permute-done.9.refs_0_ = bf16[4,144,128]{2,1,0:T(8,128)(2,1)S(1)} collective-permute-done((bf16[4,144,128]{2,1,0:T(8,128)(2,1)S(1)}, bf16[4,144,128]{2,1,0:T(8,128)(2,1)S(1)}, u32[]{:S(2)}, u32[]{:S(2)}) %collective-permute-start.9) | collective-permute-done | bytes 147488 | tf_op jit(solution)/shard_map/ppermute | solution.py:346
  25.9 0.6 %shard_map.107.refs_8_.refs_7_ = f32[8,128]{1,0:T(8,128)S(1)} custom-call(s32[1,1024]{1,0:T(1,128)S(1)} %compare_select_fusion.ends_ref, bf16[4,144,128]{2,1,0:T(8,128)(2,1)S(1)} %shard_map.106.refs_0_.refs_3_, bf16[2,256,128]{2,1,0:T(8,128)(2,1)S(1)} %pad_maximum_fusion.5.refs_3_.refs_1_.refs_4_, ...), custom_call_target="tpu_custom_call" | custom-call | tf_op jit(solution)/shard_map/pallas_call | solution.py:446
  26.5 2.3 %collective-permute-start.12 = (f32[8,128]{1,0:T(8,128)S(1)}, f32[8,128]{1,0:T(8,128)S(1)}, u32[]{:S(2)}, u32[]{:S(2)}) collective-permute-start(f32[8,128]{1,0:T(8,128)S(1)} %shard_map.107.refs_8_.refs_7_), channel_id=1, source_target_pairs={{0,24},{8,16},{16,8},{24,0},{1,25},{9,17},{17,9},{25,1},{2,26},{10... | collective-permute-start | bytes 12296 | tf_op jit(solution)/shard_map/ppermute | solution.py:346
  28.8 0.8 %collective-permute-start.11 = (f32[8,128]{1,0:T(8,128)S(1)}, f32[8,128]{1,0:T(8,128)S(1)}, u32[]{:S(2)}, u32[]{:S(2)}) collective-permute-start(f32[8,128]{1,0:T(8,128)S(1)} %shard_map.107.refs_8_.refs_7_), channel_id=1, source_target_pairs={{0,16},{8,24},{16,0},{24,8},{1,17},{9,25},{17,1},{25,9},{2,18},{10... | collective-permute-start | bytes 12296 | tf_op jit(solution)/shard_map/ppermute | solution.py:346
  29.6 1.3 %collective-permute-start.10 = (f32[8,128]{1,0:T(8,128)S(1)}, f32[8,128]{1,0:T(8,128)S(1)}, u32[]{:S(2)}, u32[]{:S(2)}) collective-permute-start(f32[8,128]{1,0:T(8,128)S(1)} %shard_map.107.refs_8_.refs_7_), channel_id=1, source_target_pairs={{0,8},{8,0},{16,24},{24,16},{1,9},{9,1},{17,25},{25,17},{2,10},{10... | collective-permute-start | bytes 12296 | tf_op jit(solution)/shard_map/ppermute | solution.py:346
  31.0 2.0 %shard_map.108 = (bf16[4,256,1024]{2,1,0:T(8,128)(2,1)S(1)}, bf16[4,256,1024]{2,1,0:T(8,128)(2,1)S(1)}, f32[128,1024]{1,0:T(8,128)S(1)}) custom-call(s32[1,1024]{1,0:T(1,128)S(1)} %compare_select_fusion.ends_ref, bf16[4,144,128]{2,1,0:T(8,128)(2,1)S(1)} %pad_maximum_fusion.1.refs_0_, bf16[4,144,128]{2,1,0:T(8,128)(2,1)S(1)} %shard_map.104.refs_1_, ...), custom_call_target="tpu_custom_call" | custom-call | tf_op jit(solution)/shard_map/pallas_call | solution.py:460
  33.1 0.0 collective-permute-done.12.refs_10_
  33.1 0.2 collective-permute-done.11.refs_9_
  33.3 0.0 collective-permute-done.10.refs_8_
  33.3 1.5 %shard_map.109 = (bf16[2,256,128]{2,1,0:T(8,128)(2,1)S(1)}, bf16[2,256,128]{2,1,0:T(8,128)(2,1)S(1)}, bf16[2,256,128]{2,1,0:T(8,128)(2,1)S(1)}, bf16[2,256,128]{...) custom-call(s32[1,1024]{1,0:T(1,128)S(1)} %compare_convert_fusion.live_ref, ...), custom_call_target="tpu_custom_call" | custom-call | tf_op jit(solution)/shard_map/pallas_call | solution.py:469
  34.8 1.6 %collective-permute-start.13 = (bf16[2,256,128]{2,1,0:T(8,128)(2,1)S(1)}, bf16[2,256,128]{2,1,0:T(8,128)(2,1)S(1)}, u32[]{:S(2)}, u32[]{:S(2)}) collective-permute-start(bf16[2,256,128]{2,1,0:T(8,128)(2,1)S(1)} %get-tuple-element.33), channel_id=1, source_target_pairs={{0,1},{1,0},{2,3},{3,2},{4,5},{5,4},{6,7},{7,6},{8,9},{9,8},{10,11... | collective-permute-start | bytes 393224 | tf_op jit(solution)/shard_map/ppermute | solution.py:346
  36.4 0.9 %collective-permute-start.14 = (bf16[2,256,128]{2,1,0:T(8,128)(2,1)S(1)}, bf16[2,256,128]{2,1,0:T(8,128)(2,1)S(1)}, u32[]{:S(2)}, u32[]{:S(2)}) collective-permute-start(bf16[2,256,128]{2,1,0:T(8,128)(2,1)S(1)} %get-tuple-element.34), channel_id=1, source_target_pairs={{0,4},{1,5},{2,6},{3,7},{4,0},{5,1},{6,2},{7,3},{8,12},{9,13},{10,... | collective-permute-start | bytes 393224 | tf_op jit(solution)/shard_map/ppermute | solution.py:346
  37.3 1.1 %collective-permute-start.15 = (bf16[2,256,128]{2,1,0:T(8,128)(2,1)S(1)}, bf16[2,256,128]{2,1,0:T(8,128)(2,1)S(1)}, u32[]{:S(2)}, u32[]{:S(2)}) collective-permute-start(bf16[2,256,128]{2,1,0:T(8,128)(2,1)S(1)} %get-tuple-element.35), channel_id=1, source_target_pairs={{0,5},{1,4},{2,7},{3,6},{4,1},{5,0},{6,3},{7,2},{8,13},{9,12},{10,... | collective-permute-start | bytes 393224 | tf_op jit(solution)/shard_map/ppermute | solution.py:346
  38.4 0.0 collective-permute-start.16
  38.4 1.3 %collective-permute-done.16.refs_1_ = bf16[4,2,64,128]{3,2,1,0:T(8,128)(2,1)S(1)} collective-permute-done((bf16[4,2,64,128]{3,2,1,0:T(8,128)(2,1)S(1)}, bf16[4,2,64,128]{3,2,1,0:T(8,128)(2,1)S(1)}, u32[]{:S(2)}, u32[]{:S(2)}) %collective-permute-start.16) | collective-permute-done | bytes 131104 | tf_op jit(solution)/shard_map/ppermute | solution.py:346
  39.7 2.1 %collective-permute-start.17 = (bf16[2,2,64,128]{3,2,1,0:T(8,128)(2,1)S(1)}, bf16[2,2,64,128]{3,2,1,0:T(8,128)(2,1)S(1)}, u32[]{:S(2)}, u32[]{:S(2)}) collective-permute-start(bf16[2,2,64,128]{3,2,1,0:T(8,128)(2,1)S(1)} %pad_maximum_fusion.6), channel_id=1, source_target_pairs={{0,16},{8,24},{16,0},{24,8},{1,17},{9,25},{17,1},{25,9},{2,18},{10... | collective-permute-start | bytes 196616 | tf_op jit(solution)/shard_map/ppermute | solution.py:346
  41.8 0.6 %collective-permute-start.18 = (bf16[2,2,64,128]{3,2,1,0:T(8,128)(2,1)S(1)}, bf16[2,2,64,128]{3,2,1,0:T(8,128)(2,1)S(1)}, u32[]{:S(2)}, u32[]{:S(2)}) collective-permute-start(bf16[2,2,64,128]{3,2,1,0:T(8,128)(2,1)S(1)} %pad_maximum_fusion.7), channel_id=1, source_target_pairs={{0,8},{8,0},{16,24},{24,16},{1,9},{9,1},{17,25},{25,17},{2,10},{10... | collective-permute-start | bytes 196616 | tf_op jit(solution)/shard_map/ppermute | solution.py:346
  42.4 0.0 collective-permute-done.13.refs_1_
  42.5 1.9 %collective-permute-start.19 = (bf16[2,2,64,128]{3,2,1,0:T(8,128)(2,1)S(1)}, bf16[2,2,64,128]{3,2,1,0:T(8,128)(2,1)S(1)}, u32[]{:S(2)}, u32[]{:S(2)}) collective-permute-start(bf16[2,2,64,128]{3,2,1,0:T(8,128)(2,1)S(1)} %pad_maximum_fusion.8), channel_id=1, source_target_pairs={{0,24},{8,16},{16,8},{24,0},{1,25},{9,17},{17,9},{25,1},{2,26},{10... | collective-permute-start | bytes 196616 | tf_op jit(solution)/shard_map/ppermute | solution.py:346
  44.4 2.1 %collective-permute-done.17.refs_2_ = bf16[2,2,64,128]{3,2,1,0:T(8,128)(2,1)S(1)} collective-permute-done((bf16[2,2,64,128]{3,2,1,0:T(8,128)(2,1)S(1)}, bf16[2,2,64,128]{3,2,1,0:T(8,128)(2,1)S(1)}, u32[]{:S(2)}, u32[]{:S(2)}) %collective-permute-start.17) | collective-permute-done | bytes 65568 | tf_op jit(solution)/shard_map/ppermute | solution.py:346
  46.5 0.0 collective-permute-done.18.refs_3_
  46.5 2.1 %collective-permute-done.19.refs_4_ = bf16[2,2,64,128]{3,2,1,0:T(8,128)(2,1)S(1)} collective-permute-done((bf16[2,2,64,128]{3,2,1,0:T(8,128)(2,1)S(1)}, bf16[2,2,64,128]{3,2,1,0:T(8,128)(2,1)S(1)}, u32[]{:S(2)}, u32[]{:S(2)}) %collective-permute-start.19) | collective-permute-done | bytes 65568 | tf_op jit(solution)/shard_map/ppermute | solution.py:346
  48.7 0.1 collective-permute-start.20
  48.8 1.0 %collective-permute-start.21 = (bf16[2,64,128]{2,1,0:T(8,128)(2,1)S(1)}, bf16[2,64,128]{2,1,0:T(8,128)(2,1)S(1)}, u32[]{:S(2)}, u32[]{:S(2)}) collective-permute-start(bf16[2,64,128]{2,1,0:T(8,128)(2,1)S(1)} %get-tuple-element.39), channel_id=1, source_target_pairs={{0,4},{4,0},{1,5},{5,1},{2,6},{6,2},{3,7},{7,3},{8,12},{12,8},{9,1... | collective-permute-start | bytes 98312 | tf_op jit(solution)/shard_map/ppermute | solution.py:346
  49.7 3.0 %collective-permute-done.21.refs_6_ = bf16[2,64,128]{2,1,0:T(8,128)(2,1)S(1)} collective-permute-done((bf16[2,64,128]{2,1,0:T(8,128)(2,1)S(1)}, bf16[2,64,128]{2,1,0:T(8,128)(2,1)S(1)}, u32[]{:S(2)}, u32[]{:S(2)}) %collective-permute-start.21) | collective-permute-done | bytes 32800 | tf_op jit(solution)/shard_map/ppermute | solution.py:346
  52.7 0.0 collective-permute-done.20.refs_4_
  52.8 1.0 %shard_map.112 = (bf16[256,128]{1,0:T(8,128)(2,1)}, bf16[128,1024]{1,0:T(8,128)(2,1)}, bf16[128,1024]{1,0:T(8,128)(2,1)}) custom-call(bf16[2,256,128]{2,1,0:T(8,128)(2,1)S(1)} %get-tuple-element.32.refs_0_, bf16[2,256,128]{2,1,0:T(8,128)(2,1)S(1)} %collective-permute-done.13.refs_1_, bf16[2,256,128]{2,1,0:T(8,128)(2,1)S(1)} %collective-permute-done.14.refs_2_, ...), custom_call_target="tpu_custom_call" | custom-call | tf_op jit(solution)/shard_map/pallas_call | solution.py:491
  (25 shorter events, 0.3 us)
Async XLA Ops:
  2.0 3.3 %collective-permute-start = (bf16[144,128]{1,0:T(8,128)(2,1)S(1)}, bf16[144,128]{1,0:T(8,128)(2,1)S(1)}, u32[]{:S(2)}, u32[]{:S(2)}) collective-permute-start(bf16[144,128]{1,0:T(8,128)(2,1)S(1)} %get-tuple-element.24), channel_id=1, source_target_pairs={{0,2},{2,0},{4,6},{6,4},{1,3},{3,1},{5,7},{7,5},{8,10},{10,8},{12,... | collective-permute-start | bytes 110600 | tf_op jit(solution)/shard_map/ppermute | solution.py:346
  2.5 4.7 %collective-permute-start.1 = (bf16[144,128]{1,0:T(8,128)(2,1)S(1)}, bf16[144,128]{1,0:T(8,128)(2,1)S(1)}, u32[]{:S(2)}, u32[]{:S(2)}) collective-permute-start(bf16[144,128]{1,0:T(8,128)(2,1)S(1)} %get-tuple-element.25), channel_id=1, source_target_pairs={{0,4},{2,6},{4,0},{6,2},{1,5},{3,7},{5,1},{7,3},{8,12},{10,14},{12... | collective-permute-start | bytes 110600 | tf_op jit(solution)/shard_map/ppermute | solution.py:346
  5.1 3.4 %collective-permute-start.2 = (bf16[144,128]{1,0:T(8,128)(2,1)S(1)}, bf16[144,128]{1,0:T(8,128)(2,1)S(1)}, u32[]{:S(2)}, u32[]{:S(2)}) collective-permute-start(bf16[144,128]{1,0:T(8,128)(2,1)S(1)} %get-tuple-element.26), channel_id=1, source_target_pairs={{0,6},{2,4},{4,2},{6,0},{1,7},{3,5},{5,3},{7,1},{8,14},{10,12},{12... | collective-permute-start | bytes 110600 | tf_op jit(solution)/shard_map/ppermute | solution.py:346
  5.2 6.0 %collective-permute-start.4 = (bf16[4,256,128]{2,1,0:T(8,128)(2,1)S(1)}, bf16[4,256,128]{2,1,0:T(8,128)(2,1)S(1)}, u32[]{:S(2)}, u32[]{:S(2)}) collective-permute-start(bf16[4,256,128]{2,1,0:T(8,128)(2,1)S(1)} %get-tuple-element.28), channel_id=1, source_target_pairs={{0,2},{1,3},{2,0},{3,1},{4,6},{5,7},{6,4},{7,5},{8,10},{9,11},{10,... | collective-permute-start | bytes 786440 | tf_op jit(solution)/shard_map/ppermute | solution.py:346
  8.6 10.1 %collective-permute-start.3 = (bf16[4,144,128]{2,1,0:T(8,128)(2,1)S(1)}, bf16[4,144,128]{2,1,0:T(8,128)(2,1)S(1)}, u32[]{:S(2)}, u32[]{:S(2)}) collective-permute-start(bf16[4,144,128]{2,1,0:T(8,128)(2,1)S(1)} %pad_maximum_fusion.1.refs_0_), channel_id=1, source_target_pairs={{0,16},{8,24},{16,0},{24,8},{1,17},{9,25},{17,1},{25,9},{2,18},{10... | collective-permute-start | bytes 442376 | tf_op jit(solution)/shard_map/ppermute | solution.py:346
  11.3 7.4 %collective-permute-start.5 = (bf16[2,256,128]{2,1,0:T(8,128)(2,1)S(1)}, bf16[2,256,128]{2,1,0:T(8,128)(2,1)S(1)}, u32[]{:S(2)}, u32[]{:S(2)}) collective-permute-start(bf16[2,256,128]{2,1,0:T(8,128)(2,1)S(1)} %pad_maximum_fusion.2), channel_id=1, source_target_pairs={{0,1},{1,0},{2,3},{3,2},{4,5},{5,4},{6,7},{7,6},{8,9},{9,8},{10,11... | collective-permute-start | bytes 393224 | tf_op jit(solution)/shard_map/ppermute | solution.py:346
  12.9 7.9 %collective-permute-start.6 = (bf16[2,256,128]{2,1,0:T(8,128)(2,1)S(1)}, bf16[2,256,128]{2,1,0:T(8,128)(2,1)S(1)}, u32[]{:S(2)}, u32[]{:S(2)}) collective-permute-start(bf16[2,256,128]{2,1,0:T(8,128)(2,1)S(1)} %pad_maximum_fusion.3), channel_id=1, source_target_pairs={{0,4},{1,5},{2,6},{3,7},{4,0},{5,1},{6,2},{7,3},{8,12},{9,13},{10,... | collective-permute-start | bytes 393224 | tf_op jit(solution)/shard_map/ppermute | solution.py:346
  13.8 6.9 %collective-permute-start.7 = (bf16[2,256,128]{2,1,0:T(8,128)(2,1)S(1)}, bf16[2,256,128]{2,1,0:T(8,128)(2,1)S(1)}, u32[]{:S(2)}, u32[]{:S(2)}) collective-permute-start(bf16[2,256,128]{2,1,0:T(8,128)(2,1)S(1)} %pad_maximum_fusion.4), channel_id=1, source_target_pairs={{0,5},{1,4},{2,7},{3,6},{4,1},{5,0},{6,3},{7,2},{8,13},{9,12},{10,... | collective-permute-start | bytes 393224 | tf_op jit(solution)/shard_map/ppermute | solution.py:346
  15.7 7.4 %collective-permute-start.8 = (bf16[4,144,128]{2,1,0:T(8,128)(2,1)S(1)}, bf16[4,144,128]{2,1,0:T(8,128)(2,1)S(1)}, u32[]{:S(2)}, u32[]{:S(2)}) collective-permute-start(bf16[4,144,128]{2,1,0:T(8,128)(2,1)S(1)} %pad_maximum_fusion.1.refs_0_), channel_id=1, source_target_pairs={{0,8},{8,0},{16,24},{24,16},{1,9},{9,1},{17,25},{25,17},{2,10},{10... | collective-permute-start | bytes 442376 | tf_op jit(solution)/shard_map/ppermute | solution.py:346
  20.7 5.1 %collective-permute-start.9 = (bf16[4,144,128]{2,1,0:T(8,128)(2,1)S(1)}, bf16[4,144,128]{2,1,0:T(8,128)(2,1)S(1)}, u32[]{:S(2)}, u32[]{:S(2)}) collective-permute-start(bf16[4,144,128]{2,1,0:T(8,128)(2,1)S(1)} %shard_map.104.refs_1_), channel_id=1, source_target_pairs={{0,8},{8,0},{16,24},{24,16},{1,9},{9,1},{17,25},{25,17},{2,10},{10... | collective-permute-start | bytes 442376 | tf_op jit(solution)/shard_map/ppermute | solution.py:346
  26.5 6.5 %collective-permute-start.12 = (f32[8,128]{1,0:T(8,128)S(1)}, f32[8,128]{1,0:T(8,128)S(1)}, u32[]{:S(2)}, u32[]{:S(2)}) collective-permute-start(f32[8,128]{1,0:T(8,128)S(1)} %shard_map.107.refs_8_.refs_7_), channel_id=1, source_target_pairs={{0,24},{8,16},{16,8},{24,0},{1,25},{9,17},{17,9},{25,1},{2,26},{10... | collective-permute-start | bytes 12296 | tf_op jit(solution)/shard_map/ppermute | solution.py:346
  28.8 4.5 %collective-permute-start.11 = (f32[8,128]{1,0:T(8,128)S(1)}, f32[8,128]{1,0:T(8,128)S(1)}, u32[]{:S(2)}, u32[]{:S(2)}) collective-permute-start(f32[8,128]{1,0:T(8,128)S(1)} %shard_map.107.refs_8_.refs_7_), channel_id=1, source_target_pairs={{0,16},{8,24},{16,0},{24,8},{1,17},{9,25},{17,1},{25,9},{2,18},{10... | collective-permute-start | bytes 12296 | tf_op jit(solution)/shard_map/ppermute | solution.py:346
  29.6 3.7 %collective-permute-start.10 = (f32[8,128]{1,0:T(8,128)S(1)}, f32[8,128]{1,0:T(8,128)S(1)}, u32[]{:S(2)}, u32[]{:S(2)}) collective-permute-start(f32[8,128]{1,0:T(8,128)S(1)} %shard_map.107.refs_8_.refs_7_), channel_id=1, source_target_pairs={{0,8},{8,0},{16,24},{24,16},{1,9},{9,1},{17,25},{25,17},{2,10},{10... | collective-permute-start | bytes 12296 | tf_op jit(solution)/shard_map/ppermute | solution.py:346
  34.8 7.6 %collective-permute-start.13 = (bf16[2,256,128]{2,1,0:T(8,128)(2,1)S(1)}, bf16[2,256,128]{2,1,0:T(8,128)(2,1)S(1)}, u32[]{:S(2)}, u32[]{:S(2)}) collective-permute-start(bf16[2,256,128]{2,1,0:T(8,128)(2,1)S(1)} %get-tuple-element.33), channel_id=1, source_target_pairs={{0,1},{1,0},{2,3},{3,2},{4,5},{5,4},{6,7},{7,6},{8,9},{9,8},{10,11... | collective-permute-start | bytes 393224 | tf_op jit(solution)/shard_map/ppermute | solution.py:346
  36.4 8.0 %collective-permute-start.14 = (bf16[2,256,128]{2,1,0:T(8,128)(2,1)S(1)}, bf16[2,256,128]{2,1,0:T(8,128)(2,1)S(1)}, u32[]{:S(2)}, u32[]{:S(2)}) collective-permute-start(bf16[2,256,128]{2,1,0:T(8,128)(2,1)S(1)} %get-tuple-element.34), channel_id=1, source_target_pairs={{0,4},{1,5},{2,6},{3,7},{4,0},{5,1},{6,2},{7,3},{8,12},{9,13},{10,... | collective-permute-start | bytes 393224 | tf_op jit(solution)/shard_map/ppermute | solution.py:346
  37.3 7.1 %collective-permute-start.15 = (bf16[2,256,128]{2,1,0:T(8,128)(2,1)S(1)}, bf16[2,256,128]{2,1,0:T(8,128)(2,1)S(1)}, u32[]{:S(2)}, u32[]{:S(2)}) collective-permute-start(bf16[2,256,128]{2,1,0:T(8,128)(2,1)S(1)} %get-tuple-element.35), channel_id=1, source_target_pairs={{0,5},{1,4},{2,7},{3,6},{4,1},{5,0},{6,3},{7,2},{8,13},{9,12},{10,... | collective-permute-start | bytes 393224 | tf_op jit(solution)/shard_map/ppermute | solution.py:346
  38.4 1.3 %collective-permute-start.16 = (bf16[4,2,64,128]{3,2,1,0:T(8,128)(2,1)S(1)}, bf16[4,2,64,128]{3,2,1,0:T(8,128)(2,1)S(1)}, u32[]{:S(2)}, u32[]{:S(2)}) collective-permute-start(bf16[4,2,64,128]{3,2,1,0:T(8,128)(2,1)S(1)} %get-tuple-element.37), channel_id=1, source_target_pairs={{0,2},{2,0},{1,3},{3,1},{4,6},{6,4},{5,7},{7,5},{8,10},{10,8},{9,1... | collective-permute-start | bytes 393224 | tf_op jit(solution)/shard_map/ppermute | solution.py:346
  39.7 6.8 %collective-permute-start.17 = (bf16[2,2,64,128]{3,2,1,0:T(8,128)(2,1)S(1)}, bf16[2,2,64,128]{3,2,1,0:T(8,128)(2,1)S(1)}, u32[]{:S(2)}, u32[]{:S(2)}) collective-permute-start(bf16[2,2,64,128]{3,2,1,0:T(8,128)(2,1)S(1)} %pad_maximum_fusion.6), channel_id=1, source_target_pairs={{0,16},{8,24},{16,0},{24,8},{1,17},{9,25},{17,1},{25,9},{2,18},{10... | collective-permute-start | bytes 196616 | tf_op jit(solution)/shard_map/ppermute | solution.py:346
  41.8 4.7 %collective-permute-start.18 = (bf16[2,2,64,128]{3,2,1,0:T(8,128)(2,1)S(1)}, bf16[2,2,64,128]{3,2,1,0:T(8,128)(2,1)S(1)}, u32[]{:S(2)}, u32[]{:S(2)}) collective-permute-start(bf16[2,2,64,128]{3,2,1,0:T(8,128)(2,1)S(1)} %pad_maximum_fusion.7), channel_id=1, source_target_pairs={{0,8},{8,0},{16,24},{24,16},{1,9},{9,1},{17,25},{25,17},{2,10},{10... | collective-permute-start | bytes 196616 | tf_op jit(solution)/shard_map/ppermute | solution.py:346
  42.5 6.2 %collective-permute-start.19 = (bf16[2,2,64,128]{3,2,1,0:T(8,128)(2,1)S(1)}, bf16[2,2,64,128]{3,2,1,0:T(8,128)(2,1)S(1)}, u32[]{:S(2)}, u32[]{:S(2)}) collective-permute-start(bf16[2,2,64,128]{3,2,1,0:T(8,128)(2,1)S(1)} %pad_maximum_fusion.8), channel_id=1, source_target_pairs={{0,24},{8,16},{16,8},{24,0},{1,25},{9,17},{17,9},{25,1},{2,26},{10... | collective-permute-start | bytes 196616 | tf_op jit(solution)/shard_map/ppermute | solution.py:346
  48.7 4.1 %collective-permute-start.20 = (bf16[4,256,128]{2,1,0:T(8,128)(2,1)S(1)}, bf16[4,256,128]{2,1,0:T(8,128)(2,1)S(1)}, u32[]{:S(2)}, u32[]{:S(2)}) collective-permute-start(bf16[4,256,128]{2,1,0:T(8,128)(2,1)S(1)} %shard_map.111), channel_id=1, source_target_pairs={{0,2},{1,3},{2,0},{3,1},{4,6},{5,7},{6,4},{7,5},{8,10},{9,11},{10,... | collective-permute-start | bytes 786440 | tf_op jit(solution)/shard_map/ppermute | solution.py:346
  48.8 4.0 %collective-permute-start.21 = (bf16[2,64,128]{2,1,0:T(8,128)(2,1)S(1)}, bf16[2,64,128]{2,1,0:T(8,128)(2,1)S(1)}, u32[]{:S(2)}, u32[]{:S(2)}) collective-permute-start(bf16[2,64,128]{2,1,0:T(8,128)(2,1)S(1)} %get-tuple-element.39), channel_id=1, source_target_pairs={{0,4},{4,0},{1,5},{5,1},{2,6},{6,2},{3,7},{7,3},{8,12},{12,8},{9,1... | collective-permute-start | bytes 98312 | tf_op jit(solution)/shard_map/ppermute | solution.py:346

commit v13 on v12

--- a/solution.py
+++ b/solution.py
@@ -151,19 +151,37 @@
     return max(1, size // DH)
 
 
+def block_kernel(*refs):
+    slab_refs, out_ref = refs[:-1], refs[-1]
+    low = lax.broadcasted_iota(jnp.int32, (STAT_ROWS, DH), 1) < DH // 2
+    stats = []
+    for m, ref in enumerate(slab_refs):
+        out_ref[m * DH : (m + 1) * DH, :] = ref[0:DH, :]
+        stats.append(ref[DH : DH + STAT_ROWS, :].astype(jnp.float32))
+    if len(stats) > 1:
+        pairs = [
+            jnp.where(low, stats[m], stats[m + 1])[: 2 * PIECES] for m in range(0, len(stats), 2)
+        ]
+        rest = STAT_ROWS - len(pairs) * 2 * PIECES
+        stats = [jnp.concatenate([*pairs, jnp.zeros((rest, DH), jnp.float32)], axis=0)]
+    out_ref[len(slab_refs) * DH :, :] = stats[0].astype(jnp.bfloat16)
+
+
 def slabs_of(row_refs):
-    return [[(ref, m) for m in range(ref.shape[0])] for ref in row_refs]
+    return [[(ref, m) for m in range(ref.shape[0] // DH)] for ref in row_refs]
 
 
 def lines_of(slabs, first, lines):
-    return jnp.concatenate([ref[j, first : first + lines, :] for ref, j in slabs], axis=0)
+    return jnp.concatenate(
+        [ref[m * DH + first : m * DH + first + lines, :] for ref, m in slabs], axis=0
+    )
 
 
 def stat_kernel(blocks, first, nears, heads, tokens, ends_ref, *refs):
     at = place(nears, heads)
     row_refs, refs = refs[: len(blocks)], refs[len(blocks) :]
     pair_refs, before_refs, lse_ref = refs[: len(KEEP)], refs[len(KEEP) : -1], refs[-1]
-    lines = (row_refs[0].shape[1] - STAT_ROWS) // 2
+    lines = DH // 2
     for ref in before_refs:
         lse_ref[...] = ref[...]
 
@@ -196,15 +214,21 @@
 
 def line_values(slabs, lines, first_piece):
     low = lax.broadcasted_iota(jnp.int32, (1, 2 * lines), 1) < lines
+
+    def stats_of(ref):
+        first = ref.shape[0] - STAT_ROWS
+        return ref[first : first + STAT_ROWS, :].astype(jnp.float32)
+
     out = []
     for n in range(0, len(slabs), 2):
-        held = [
-            ref[j, 2 * lines : 2 * lines + STAT_ROWS, :].astype(jnp.float32)
-            for ref, j in slabs[n : n + 2]
-        ]
+        ref, m = slabs[n]
         total = None
         for k in range(first_piece, first_piece + PIECES):
-            piece = jnp.where(low, held[0][k : k + 1], held[1][k : k + 1])
+            if ref.shape[0] > DH + STAT_ROWS:
+                k = m // 2 * (2 * PIECES) + k
+                piece = stats_of(ref)[k : k + 1]
+            else:
+                piece = jnp.where(low, stats_of(ref)[k : k + 1], stats_of(slabs[n + 1][0])[k : k + 1])
             total = piece if total is None else total + piece
         out.append(total)
     return jnp.concatenate(out, axis=1)
@@ -232,7 +256,7 @@
     at = place(nears, heads)
     row_refs, refs = refs[: len(blocks)], refs[len(blocks) :]
     pair_refs, (lse_ref, prob_ref, dscore_ref, dq_ref) = refs[: len(KEEP)], refs[len(KEEP) :]
-    lines = (row_refs[0].shape[1] - STAT_ROWS) // 2
+    lines = DH // 2
     all_slabs = slabs_of(row_refs)
     size = len(all_slabs[0]) * lines
 
@@ -269,7 +293,7 @@
     (prob_ref, dscore_ref, dq_ref), refs = refs[:3], refs[3:]
     lse_refs, refs = refs[: len(blocks)], refs[len(blocks) :]
     dkv_refs, (*dq_refs, dk_acc, dv_acc) = refs[: len(KEEP)], refs[len(KEEP) :]
-    lines = (row_refs[0].shape[1] - STAT_ROWS) // 2
+    lines = DH // 2
     all_slabs = slabs_of(row_refs)
     size = len(all_slabs[0]) * lines
     for first, count, held, slabs in steps_of(blocks, all_slabs, lines):
@@ -322,8 +346,8 @@
 
 def write_kernel(nears, heads, *refs):
     at = place(nears, heads)
-    pair_refs, came_ref, refs = refs[: len(KEEP)], refs[len(KEEP)], refs[len(KEEP) + 1 :]
-    slab_refs, (out_q_ref, out_k_ref, out_v_ref, sems) = refs[:-4], refs[-4:]
+    slab_refs, refs = refs[: -len(KEEP) - 5], refs[-len(KEEP) - 5 :]
+    pair_refs, (came_ref, out_q_ref, out_k_ref, out_v_ref, sems) = refs[: len(KEEP)], refs[len(KEEP) :]
     groups, lines, tokens = len(slab_refs) * nears, slab_refs[0].shape[1], out_k_ref.shape[0]
     copies = []
     for i, ref in enumerate(pair_refs):
@@ -430,7 +454,13 @@
         in_hbm(keys),
         in_hbm(values),
     )
-    own_block = jnp.stack(swap_slabs(slabs, groups))
+    own_block = pl.pallas_call(
+        block_kernel,
+        in_specs=[VMEM] * groups,
+        out_specs=VMEM,
+        out_shape=jax.ShapeDtypeStruct((groups * DH + STAT_ROWS, DH), jnp.bfloat16),
+        compiler_params=PARAMS,
+    )(*swap_slabs(slabs, groups))
     pairs = swap_pairs(kv_keep, kv_send)
     far = [1 << n for n in reversed(range(shift_of(parts)))]
 
@@ -486,8 +516,8 @@
         out_shape=[sum_shape] * 2,
         compiler_params=PARAMS,
     )(*dq, *from_parts)
+    pairs = swap_back(dkv, from_parts)
     sums = [swap(x, "row", j, row_count) if j else x for j, x in enumerate(sums[:row_count])]
-    pairs = swap_back(dkv, sums[:1])
     out_q, out_k, out_v = pl.pallas_call(
         functools.partial(write_kernel, nears, heads),
         in_specs=[VMEM] * (row_count + len(pairs)),
@@ -499,7 +529,7 @@
         ],
         scratch_shapes=[pltpu.SemaphoreType.DMA((4 * len(KEEP) + groups,))],
         compiler_params=PARAMS,
-    )(*pairs, *sums)
+    )(*sums, *pairs)
     out_q = out_q.reshape(own_heads, rows, DH).transpose(1, 0, 2).reshape(rows, own_heads * DH)
     return out_q, out_k, out_v
 

time: 53.9 us -> 53.1 us (0.985)
  transfers between devices with their start and end apart: 22 -> 22, of which waited for: 10 -> 11; matrix products, arithmetic and copies ran while one was open for 1% -> 1% of each run, Pallas kernels for 6% -> 6%
where the time goes in v13:
time: 53.1 us; the launch traced here: 52.8 us
  starting transfers between devices  26.1 us (49%)
  waiting for transfers between devices  16.6 us (31%)
  Pallas kernels  7.71 us (15%)
  between operations  2.12 us (4%)
    ppermute x22, starting transfers between devices, swap(): return lax.ppermute(x, axis, [(i, i ^ distance) for i in range(size)])  26.1 us
    ppermute x22, waiting for transfers between devices, swap(): return lax.ppermute(x, axis, [(i, i ^ distance) for i in range(size)])  16.6 us
    pallas_call x1, Pallas kernels, shards(): pl.pallas_call(functools.partial(part_kernel, blocks, nears, heads, token...  2.06 us
    pallas_call x2, Pallas kernels, part_lse(): pl.pallas_call(functools.partial(stat_kernel, held, first, nears, heads,...  1.8 us
    pallas_call x1, Pallas kernels, shards(): pl.pallas_call(functools.partial(token_kernel, blocks, nears, heads, toke...  1.46 us
    pallas_call x1, Pallas kernels, shards(): pl.pallas_call(functools.partial(pack_kernel, row_count, nears, heads), i...  1.37 us
  transfers between devices with their start and end apart: 22, of which 11 were waited for; matrix products, arithmetic and copies ran while one was open for 1% of the time, Pallas kernels for 6%

profile of v13, /device:TPU:0, one launch (start us, length us, event | category | flops | bytes accessed | tf_op | source)
XLA Modules:
  0.0 52.8 jit_solution(2649488999354995708)
XLA Ops:
  0.6 1.4 %shard_map.103 = (bf16[144,128]{1,0:T(8,128)(2,1)S(1)}, bf16[144,128]{1,0:T(8,128)(2,1)S(1)}, bf16[144,128]{1,0:T(8,128)(2,1)S(1)}, bf16[144,128]{1,0:T(8,128)(2...) custom-call(bf16[256,128]{1,0:T(8,128)(2,1)} %bitcast.24, bf16[256,128]{1,0:T(8,128)(2,1)} %bitcast.25, ...), custom_call_target="tpu_custom_call" | custom-call | tf_op jit(solution)/shard_map/pallas_call | solution.py:438
  2.0 0.5 collective-permute-start.4
  2.5 0.1 collective-permute-start
  2.6 2.9 %collective-permute-start.1 = (bf16[144,128]{1,0:T(8,128)(2,1)S(1)}, bf16[144,128]{1,0:T(8,128)(2,1)S(1)}, u32[]{:S(2)}, u32[]{:S(2)}) collective-permute-start(bf16[144,128]{1,0:T(8,128)(2,1)S(1)} %get-tuple-element.25), channel_id=1, source_target_pairs={{0,4},{2,6},{4,0},{6,2},{1,5},{3,7},{5,1},{7,3},{8,12},{10,14},{12... | collective-permute-start | bytes 110600 | tf_op jit(solution)/shard_map/ppermute | solution.py:370
  5.6 0.0 collective-permute-start.2
  5.6 0.0 collective-permute-done.refs_1_
  5.6 1.9 %collective-permute-done.1.refs_2_ = bf16[144,128]{1,0:T(8,128)(2,1)S(1)} collective-permute-done((bf16[144,128]{1,0:T(8,128)(2,1)S(1)}, bf16[144,128]{1,0:T(8,128)(2,1)S(1)}, u32[]{:S(2)}, u32[]{:S(2)}) %collective-permute-start.1) | collective-permute-done | bytes 36896 | tf_op jit(solution)/shard_map/ppermute | solution.py:370
  7.5 1.8 %collective-permute-done.2.refs_3_ = bf16[144,128]{1,0:T(8,128)(2,1)S(1)} collective-permute-done((bf16[144,128]{1,0:T(8,128)(2,1)S(1)}, bf16[144,128]{1,0:T(8,128)(2,1)S(1)}, u32[]{:S(2)}, u32[]{:S(2)}) %collective-permute-start.2) | collective-permute-done | bytes 36896 | tf_op jit(solution)/shard_map/ppermute | solution.py:370
  9.3 2.7 %collective-permute-start.3 = (bf16[528,128]{1,0:T(8,128)(2,1)S(1)}, bf16[528,128]{1,0:T(8,128)(2,1)S(1)}, u32[]{:S(2)}, u32[]{:S(2)}) collective-permute-start(bf16[528,128]{1,0:T(8,128)(2,1)S(1)} %shard_map.104.refs_0_), channel_id=1, source_target_pairs={{0,16},{8,24},{16,0},{24,8},{1,17},{9,25},{17,1},{25,9},{2,18},{10... | collective-permute-start | bytes 405512 | tf_op jit(solution)/shard_map/ppermute | solution.py:370
  12.0 0.0 collective-permute-done.4
  12.0 1.6 %collective-permute-start.5 = (bf16[2,256,128]{2,1,0:T(8,128)(2,1)S(1)}, bf16[2,256,128]{2,1,0:T(8,128)(2,1)S(1)}, u32[]{:S(2)}, u32[]{:S(2)}) collective-permute-start(bf16[2,256,128]{2,1,0:T(8,128)(2,1)S(1)} %pad_maximum_fusion.1), channel_id=1, source_target_pairs={{0,1},{1,0},{2,3},{3,2},{4,5},{5,4},{6,7},{7,6},{8,9},{9,8},{10,11... | collective-permute-start | bytes 393224 | tf_op jit(solution)/shard_map/ppermute | solution.py:370
  13.6 0.6 %collective-permute-start.6 = (bf16[2,256,128]{2,1,0:T(8,128)(2,1)S(1)}, bf16[2,256,128]{2,1,0:T(8,128)(2,1)S(1)}, u32[]{:S(2)}, u32[]{:S(2)}) collective-permute-start(bf16[2,256,128]{2,1,0:T(8,128)(2,1)S(1)} %pad_maximum_fusion.2), channel_id=1, source_target_pairs={{0,4},{1,5},{2,6},{3,7},{4,0},{5,1},{6,2},{7,3},{8,12},{9,13},{10,... | collective-permute-start | bytes 393224 | tf_op jit(solution)/shard_map/ppermute | solution.py:370
  14.2 1.5 %collective-permute-start.7 = (bf16[2,256,128]{2,1,0:T(8,128)(2,1)S(1)}, bf16[2,256,128]{2,1,0:T(8,128)(2,1)S(1)}, u32[]{:S(2)}, u32[]{:S(2)}) collective-permute-start(bf16[2,256,128]{2,1,0:T(8,128)(2,1)S(1)} %pad_maximum_fusion.3), channel_id=1, source_target_pairs={{0,5},{1,4},{2,7},{3,6},{4,1},{5,0},{6,3},{7,2},{8,13},{9,12},{10,... | collective-permute-start | bytes 393224 | tf_op jit(solution)/shard_map/ppermute | solution.py:370
  16.4 1.6 %collective-permute-start.8 = (bf16[528,128]{1,0:T(8,128)(2,1)S(1)}, bf16[528,128]{1,0:T(8,128)(2,1)S(1)}, u32[]{:S(2)}, u32[]{:S(2)}) collective-permute-start(bf16[528,128]{1,0:T(8,128)(2,1)S(1)} %shard_map.104.refs_0_), channel_id=1, source_target_pairs={{0,8},{8,0},{16,24},{24,16},{1,9},{9,1},{17,25},{25,17},{2,10},{10... | collective-permute-start | bytes 405512 | tf_op jit(solution)/shard_map/ppermute | solution.py:370
  18.0 0.8 %collective-permute-done.3.refs_0_ = bf16[528,128]{1,0:T(8,128)(2,1)S(1)} collective-permute-done((bf16[528,128]{1,0:T(8,128)(2,1)S(1)}, bf16[528,128]{1,0:T(8,128)(2,1)S(1)}, u32[]{:S(2)}, u32[]{:S(2)}) %collective-permute-start.3) | collective-permute-done | bytes 135200 | tf_op jit(solution)/shard_map/ppermute | solution.py:370
  18.8 0.0 collective-permute-done.5.refs_1_.refs_4_.refs_2_.refs_5_
  18.9 2.6 %collective-permute-done.6.refs_2_.refs_5_.refs_3_.refs_6_ = bf16[2,256,128]{2,1,0:T(8,128)(2,1)S(1)} collective-permute-done((bf16[2,256,128]{2,1,0:T(8,128)(2,1)S(1)}, bf16[2,256,128]{2,1,0:T(8,128)(2,1)S(1)}, u32[]{:S(2)}, u32[]{:S(2)}) %collective-permute-start.6) | collective-permute-done | bytes 131104 | tf_op jit(solution)/shard_map/ppermute | solution.py:370
  21.4 0.0 collective-permute-done.7.refs_3_.refs_6_.refs_4_.refs_7_
  21.4 1.6 %collective-permute-start.9 = (bf16[528,128]{1,0:T(8,128)(2,1)S(1)}, bf16[528,128]{1,0:T(8,128)(2,1)S(1)}, u32[]{:S(2)}, u32[]{:S(2)}) collective-permute-start(bf16[528,128]{1,0:T(8,128)(2,1)S(1)} %shard_map.105.refs_1_), channel_id=1, source_target_pairs={{0,8},{8,0},{16,24},{24,16},{1,9},{9,1},{17,25},{25,17},{2,10},{10... | collective-permute-start | bytes 405512 | tf_op jit(solution)/shard_map/ppermute | solution.py:370
  23.7 0.0 collective-permute-done.8.refs_2_
  23.7 1.1 %shard_map.106.refs_1_.refs_5_ = f32[8,128]{1,0:T(8,128)S(1)} custom-call(s32[1,1024]{1,0:T(1,128)S(1)} %compare_select_fusion.ends_ref, bf16[528,128]{1,0:T(8,128)(2,1)S(1)} %shard_map.104.refs_0_, bf16[528,128]{1,0:T(8,128)(2,1)S(1)} %shard_map.105.refs_1_, bf16[528,128]{1,0:T(8,128)(2,1)S(1)} %collective-permute-done.8.refs_2_, ...), custom_call_target="tpu_custom_call" | custom-call | tf_op jit(solution)/shard_map/pallas_call | solution.py:476
  24.9 1.6 %collective-permute-done.9.refs_0_ = bf16[528,128]{1,0:T(8,128)(2,1)S(1)} collective-permute-done((bf16[528,128]{1,0:T(8,128)(2,1)S(1)}, bf16[528,128]{1,0:T(8,128)(2,1)S(1)}, u32[]{:S(2)}, u32[]{:S(2)}) %collective-permute-start.9) | collective-permute-done | bytes 135200 | tf_op jit(solution)/shard_map/ppermute | solution.py:370
  26.5 0.6 %shard_map.108.refs_8_.refs_7_ = f32[8,128]{1,0:T(8,128)S(1)} custom-call(s32[1,1024]{1,0:T(1,128)S(1)} %compare_select_fusion.ends_ref, bf16[528,128]{1,0:T(8,128)(2,1)S(1)} %shard_map.107.refs_0_.refs_3_, bf16[2,256,128]{2,1,0:T(8,128)(2,1)S(1)} %pad_maximum_fusion.4.refs_3_.refs_1_.refs_4_, ...), custom_call_target="tpu_custom_call" | custom-call | tf_op jit(solution)/shard_map/pallas_call | solution.py:476
  27.1 1.6 %collective-permute-start.12 = (f32[8,128]{1,0:T(8,128)S(1)}, f32[8,128]{1,0:T(8,128)S(1)}, u32[]{:S(2)}, u32[]{:S(2)}) collective-permute-start(f32[8,128]{1,0:T(8,128)S(1)} %shard_map.108.refs_8_.refs_7_), channel_id=1, source_target_pairs={{0,24},{8,16},{16,8},{24,0},{1,25},{9,17},{17,9},{25,1},{2,26},{10... | collective-permute-start | bytes 12296 | tf_op jit(solution)/shard_map/ppermute | solution.py:370
  28.7 1.5 %collective-permute-start.11 = (f32[8,128]{1,0:T(8,128)S(1)}, f32[8,128]{1,0:T(8,128)S(1)}, u32[]{:S(2)}, u32[]{:S(2)}) collective-permute-start(f32[8,128]{1,0:T(8,128)S(1)} %shard_map.108.refs_8_.refs_7_), channel_id=1, source_target_pairs={{0,16},{8,24},{16,0},{24,8},{1,17},{9,25},{17,1},{25,9},{2,18},{10... | collective-permute-start | bytes 12296 | tf_op jit(solution)/shard_map/ppermute | solution.py:370
  30.2 1.4 %collective-permute-start.10 = (f32[8,128]{1,0:T(8,128)S(1)}, f32[8,128]{1,0:T(8,128)S(1)}, u32[]{:S(2)}, u32[]{:S(2)}) collective-permute-start(f32[8,128]{1,0:T(8,128)S(1)} %shard_map.108.refs_8_.refs_7_), channel_id=1, source_target_pairs={{0,8},{8,0},{16,24},{24,16},{1,9},{9,1},{17,25},{25,17},{2,10},{10... | collective-permute-start | bytes 12296 | tf_op jit(solution)/shard_map/ppermute | solution.py:370
  31.6 2.1 %shard_map.109 = (bf16[4,256,1024]{2,1,0:T(8,128)(2,1)S(1)}, bf16[4,256,1024]{2,1,0:T(8,128)(2,1)S(1)}, f32[128,1024]{1,0:T(8,128)S(1)}) custom-call(s32[1,1024]{1,0:T(1,128)S(1)} %compare_select_fusion.ends_ref, bf16[528,128]{1,0:T(8,128)(2,1)S(1)} %shard_map.104.refs_0_, bf16[528,128]{1,0:T(8,128)(2,1)S(1)} %shard_map.105.refs_1_, ...), custom_call_target="tpu_custom_call" | custom-call | tf_op jit(solution)/shard_map/pallas_call | solution.py:490
  33.7 0.0 collective-permute-done.11.refs_9_
  33.7 0.1 collective-permute-done.10.refs_8_
  33.8 1.5 %shard_map.110 = (bf16[2,256,128]{2,1,0:T(8,128)(2,1)S(1)}, bf16[2,256,128]{2,1,0:T(8,128)(2,1)S(1)}, bf16[2,256,128]{2,1,0:T(8,128)(2,1)S(1)}, bf16[2,256,128]{...) custom-call(s32[1,1024]{1,0:T(1,128)S(1)} %compare_convert_fusion.live_ref, ...), custom_call_target="tpu_custom_call" | custom-call | tf_op jit(solution)/shard_map/pallas_call | solution.py:499
  35.3 0.1 collective-permute-start.13
  35.4 0.9 %collective-permute-start.18 = (bf16[2,256,128]{2,1,0:T(8,128)(2,1)S(1)}, bf16[2,256,128]{2,1,0:T(8,128)(2,1)S(1)}, u32[]{:S(2)}, u32[]{:S(2)}) collective-permute-start(bf16[2,256,128]{2,1,0:T(8,128)(2,1)S(1)} %get-tuple-element.37), channel_id=1, source_target_pairs={{0,1},{1,0},{2,3},{3,2},{4,5},{5,4},{6,7},{7,6},{8,9},{9,8},{10,11... | collective-permute-start | bytes 393224 | tf_op jit(solution)/shard_map/ppermute | solution.py:370
  36.3 0.8 %collective-permute-start.19 = (bf16[2,256,128]{2,1,0:T(8,128)(2,1)S(1)}, bf16[2,256,128]{2,1,0:T(8,128)(2,1)S(1)}, u32[]{:S(2)}, u32[]{:S(2)}) collective-permute-start(bf16[2,256,128]{2,1,0:T(8,128)(2,1)S(1)} %get-tuple-element.38), channel_id=1, source_target_pairs={{0,4},{1,5},{2,6},{3,7},{4,0},{5,1},{6,2},{7,3},{8,12},{9,13},{10,... | collective-permute-start | bytes 393224 | tf_op jit(solution)/shard_map/ppermute | solution.py:370
  37.1 1.9 %collective-permute-start.20 = (bf16[2,256,128]{2,1,0:T(8,128)(2,1)S(1)}, bf16[2,256,128]{2,1,0:T(8,128)(2,1)S(1)}, u32[]{:S(2)}, u32[]{:S(2)}) collective-permute-start(bf16[2,256,128]{2,1,0:T(8,128)(2,1)S(1)} %get-tuple-element.39), channel_id=1, source_target_pairs={{0,5},{1,4},{2,7},{3,6},{4,1},{5,0},{6,3},{7,2},{8,13},{9,12},{10,... | collective-permute-start | bytes 393224 | tf_op jit(solution)/shard_map/ppermute | solution.py:370
  39.0 1.5 %collective-permute-start.14 = (bf16[2,2,64,128]{3,2,1,0:T(8,128)(2,1)S(1)}, bf16[2,2,64,128]{3,2,1,0:T(8,128)(2,1)S(1)}, u32[]{:S(2)}, u32[]{:S(2)}) collective-permute-start(bf16[2,2,64,128]{3,2,1,0:T(8,128)(2,1)S(1)} %pad_maximum_fusion.5), channel_id=1, source_target_pairs={{0,16},{8,24},{16,0},{24,8},{1,17},{9,25},{17,1},{25,9},{2,18},{10... | collective-permute-start | bytes 196616 | tf_op jit(solution)/shard_map/ppermute | solution.py:370
  40.4 0.9 %collective-permute-start.15 = (bf16[2,2,64,128]{3,2,1,0:T(8,128)(2,1)S(1)}, bf16[2,2,64,128]{3,2,1,0:T(8,128)(2,1)S(1)}, u32[]{:S(2)}, u32[]{:S(2)}) collective-permute-start(bf16[2,2,64,128]{3,2,1,0:T(8,128)(2,1)S(1)} %pad_maximum_fusion.6), channel_id=1, source_target_pairs={{0,8},{8,0},{16,24},{24,16},{1,9},{9,1},{17,25},{25,17},{2,10},{10... | collective-permute-start | bytes 196616 | tf_op jit(solution)/shard_map/ppermute | solution.py:370
  41.4 0.3 collective-permute-done.18.refs_3_
  41.7 1.8 %collective-permute-start.16 = (bf16[2,2,64,128]{3,2,1,0:T(8,128)(2,1)S(1)}, bf16[2,2,64,128]{3,2,1,0:T(8,128)(2,1)S(1)}, u32[]{:S(2)}, u32[]{:S(2)}) collective-permute-start(bf16[2,2,64,128]{3,2,1,0:T(8,128)(2,1)S(1)} %pad_maximum_fusion.7), channel_id=1, source_target_pairs={{0,24},{8,16},{16,8},{24,0},{1,25},{9,17},{17,9},{25,1},{2,26},{10... | collective-permute-start | bytes 196616 | tf_op jit(solution)/shard_map/ppermute | solution.py:370
  43.6 1.1 %collective-permute-done.19.refs_4_ = bf16[2,256,128]{2,1,0:T(8,128)(2,1)S(1)} collective-permute-done((bf16[2,256,128]{2,1,0:T(8,128)(2,1)S(1)}, bf16[2,256,128]{2,1,0:T(8,128)(2,1)S(1)}, u32[]{:S(2)}, u32[]{:S(2)}) %collective-permute-start.19) | collective-permute-done | bytes 131104 | tf_op jit(solution)/shard_map/ppermute | solution.py:370
  44.7 0.0 collective-permute-done.20.refs_5_
  44.8 0.0 collective-permute-done.14.refs_2_.refs_1_
  44.8 0.3 collective-permute-done.15.refs_3_.refs_2_
  45.0 2.8 %collective-permute-done.16.refs_4_.refs_3_ = bf16[2,2,64,128]{3,2,1,0:T(8,128)(2,1)S(1)} collective-permute-done((bf16[2,2,64,128]{3,2,1,0:T(8,128)(2,1)S(1)}, bf16[2,2,64,128]{3,2,1,0:T(8,128)(2,1)S(1)}, u32[]{:S(2)}, u32[]{:S(2)}) %collective-permute-start.16) | collective-permute-done | bytes 65568 | tf_op jit(solution)/shard_map/ppermute | solution.py:370
  47.8 0.0 collective-permute-start.21
  47.9 0.7 %collective-permute-start.17 = (bf16[2,64,128]{2,1,0:T(8,128)(2,1)S(1)}, bf16[2,64,128]{2,1,0:T(8,128)(2,1)S(1)}, u32[]{:S(2)}, u32[]{:S(2)}) collective-permute-start(bf16[2,64,128]{2,1,0:T(8,128)(2,1)S(1)} %get-tuple-element.35), channel_id=1, source_target_pairs={{0,4},{4,0},{1,5},{5,1},{2,6},{6,2},{3,7},{7,3},{8,12},{12,8},{9,1... | collective-permute-start | bytes 98312 | tf_op jit(solution)/shard_map/ppermute | solution.py:370
  48.6 3.3 %collective-permute-done.17.refs_1_ = bf16[2,64,128]{2,1,0:T(8,128)(2,1)S(1)} collective-permute-done((bf16[2,64,128]{2,1,0:T(8,128)(2,1)S(1)}, bf16[2,64,128]{2,1,0:T(8,128)(2,1)S(1)}, u32[]{:S(2)}, u32[]{:S(2)}) %collective-permute-start.17) | collective-permute-done | bytes 32800 | tf_op jit(solution)/shard_map/ppermute | solution.py:370
  51.9 0.0 collective-permute-done.21.refs_6_
  51.9 1.0 %shard_map.113 = (bf16[256,128]{1,0:T(8,128)(2,1)}, bf16[128,1024]{1,0:T(8,128)(2,1)}, bf16[128,1024]{1,0:T(8,128)(2,1)}) custom-call(bf16[2,64,128]{2,1,0:T(8,128)(2,1)S(1)} %get-tuple-element.34.refs_0_, bf16[2,64,128]{2,1,0:T(8,128)(2,1)S(1)} %collective-permute-done.17.refs_1_, bf16[2,256,128]{2,1,0:T(8,128)(2,1)S(1)} %get-tuple-element.36.refs_2_, ...), custom_call_target="tpu_custom_call" | custom-call | tf_op jit(solution)/shard_map/pallas_call | solution.py:521
  (25 shorter events, 0.3 us)
Async XLA Ops:
  2.0 10.0 %collective-permute-start.4 = (bf16[4,256,128]{2,1,0:T(8,128)(2,1)S(1)}, bf16[4,256,128]{2,1,0:T(8,128)(2,1)S(1)}, u32[]{:S(2)}, u32[]{:S(2)}) collective-permute-start(bf16[4,256,128]{2,1,0:T(8,128)(2,1)S(1)} %get-tuple-element.28), channel_id=1, source_target_pairs={{0,2},{1,3},{2,0},{3,1},{4,6},{5,7},{6,4},{7,5},{8,10},{9,11},{10,... | collective-permute-start | bytes 786440 | tf_op jit(solution)/shard_map/ppermute | solution.py:370
  2.5 3.1 %collective-permute-start = (bf16[144,128]{1,0:T(8,128)(2,1)S(1)}, bf16[144,128]{1,0:T(8,128)(2,1)S(1)}, u32[]{:S(2)}, u32[]{:S(2)}) collective-permute-start(bf16[144,128]{1,0:T(8,128)(2,1)S(1)} %get-tuple-element.24), channel_id=1, source_target_pairs={{0,2},{2,0},{4,6},{6,4},{1,3},{3,1},{5,7},{7,5},{8,10},{10,8},{12,... | collective-permute-start | bytes 110600 | tf_op jit(solution)/shard_map/ppermute | solution.py:370
  2.6 4.9 %collective-permute-start.1 = (bf16[144,128]{1,0:T(8,128)(2,1)S(1)}, bf16[144,128]{1,0:T(8,128)(2,1)S(1)}, u32[]{:S(2)}, u32[]{:S(2)}) collective-permute-start(bf16[144,128]{1,0:T(8,128)(2,1)S(1)} %get-tuple-element.25), channel_id=1, source_target_pairs={{0,4},{2,6},{4,0},{6,2},{1,5},{3,7},{5,1},{7,3},{8,12},{10,14},{12... | collective-permute-start | bytes 110600 | tf_op jit(solution)/shard_map/ppermute | solution.py:370
  5.6 3.8 %collective-permute-start.2 = (bf16[144,128]{1,0:T(8,128)(2,1)S(1)}, bf16[144,128]{1,0:T(8,128)(2,1)S(1)}, u32[]{:S(2)}, u32[]{:S(2)}) collective-permute-start(bf16[144,128]{1,0:T(8,128)(2,1)S(1)} %get-tuple-element.26), channel_id=1, source_target_pairs={{0,6},{2,4},{4,2},{6,0},{1,7},{3,5},{5,3},{7,1},{8,14},{10,12},{12... | collective-permute-start | bytes 110600 | tf_op jit(solution)/shard_map/ppermute | solution.py:370
  9.3 9.5 %collective-permute-start.3 = (bf16[528,128]{1,0:T(8,128)(2,1)S(1)}, bf16[528,128]{1,0:T(8,128)(2,1)S(1)}, u32[]{:S(2)}, u32[]{:S(2)}) collective-permute-start(bf16[528,128]{1,0:T(8,128)(2,1)S(1)} %shard_map.104.refs_0_), channel_id=1, source_target_pairs={{0,16},{8,24},{16,0},{24,8},{1,17},{9,25},{17,1},{25,9},{2,18},{10... | collective-permute-start | bytes 405512 | tf_op jit(solution)/shard_map/ppermute | solution.py:370
  12.0 6.8 %collective-permute-start.5 = (bf16[2,256,128]{2,1,0:T(8,128)(2,1)S(1)}, bf16[2,256,128]{2,1,0:T(8,128)(2,1)S(1)}, u32[]{:S(2)}, u32[]{:S(2)}) collective-permute-start(bf16[2,256,128]{2,1,0:T(8,128)(2,1)S(1)} %pad_maximum_fusion.1), channel_id=1, source_target_pairs={{0,1},{1,0},{2,3},{3,2},{4,5},{5,4},{6,7},{7,6},{8,9},{9,8},{10,11... | collective-permute-start | bytes 393224 | tf_op jit(solution)/shard_map/ppermute | solution.py:370
  13.6 7.8 %collective-permute-start.6 = (bf16[2,256,128]{2,1,0:T(8,128)(2,1)S(1)}, bf16[2,256,128]{2,1,0:T(8,128)(2,1)S(1)}, u32[]{:S(2)}, u32[]{:S(2)}) collective-permute-start(bf16[2,256,128]{2,1,0:T(8,128)(2,1)S(1)} %pad_maximum_fusion.2), channel_id=1, source_target_pairs={{0,4},{1,5},{2,6},{3,7},{4,0},{5,1},{6,2},{7,3},{8,12},{9,13},{10,... | collective-permute-start | bytes 393224 | tf_op jit(solution)/shard_map/ppermute | solution.py:370
  14.2 7.2 %collective-permute-start.7 = (bf16[2,256,128]{2,1,0:T(8,128)(2,1)S(1)}, bf16[2,256,128]{2,1,0:T(8,128)(2,1)S(1)}, u32[]{:S(2)}, u32[]{:S(2)}) collective-permute-start(bf16[2,256,128]{2,1,0:T(8,128)(2,1)S(1)} %pad_maximum_fusion.3), channel_id=1, source_target_pairs={{0,5},{1,4},{2,7},{3,6},{4,1},{5,0},{6,3},{7,2},{8,13},{9,12},{10,... | collective-permute-start | bytes 393224 | tf_op jit(solution)/shard_map/ppermute | solution.py:370
  16.4 7.3 %collective-permute-start.8 = (bf16[528,128]{1,0:T(8,128)(2,1)S(1)}, bf16[528,128]{1,0:T(8,128)(2,1)S(1)}, u32[]{:S(2)}, u32[]{:S(2)}) collective-permute-start(bf16[528,128]{1,0:T(8,128)(2,1)S(1)} %shard_map.104.refs_0_), channel_id=1, source_target_pairs={{0,8},{8,0},{16,24},{24,16},{1,9},{9,1},{17,25},{25,17},{2,10},{10... | collective-permute-start | bytes 405512 | tf_op jit(solution)/shard_map/ppermute | solution.py:370
  21.4 5.0 %collective-permute-start.9 = (bf16[528,128]{1,0:T(8,128)(2,1)S(1)}, bf16[528,128]{1,0:T(8,128)(2,1)S(1)}, u32[]{:S(2)}, u32[]{:S(2)}) collective-permute-start(bf16[528,128]{1,0:T(8,128)(2,1)S(1)} %shard_map.105.refs_1_), channel_id=1, source_target_pairs={{0,8},{8,0},{16,24},{24,16},{1,9},{9,1},{17,25},{25,17},{2,10},{10... | collective-permute-start | bytes 405512 | tf_op jit(solution)/shard_map/ppermute | solution.py:370
  27.1 6.6 %collective-permute-start.12 = (f32[8,128]{1,0:T(8,128)S(1)}, f32[8,128]{1,0:T(8,128)S(1)}, u32[]{:S(2)}, u32[]{:S(2)}) collective-permute-start(f32[8,128]{1,0:T(8,128)S(1)} %shard_map.108.refs_8_.refs_7_), channel_id=1, source_target_pairs={{0,24},{8,16},{16,8},{24,0},{1,25},{9,17},{17,9},{25,1},{2,26},{10... | collective-permute-start | bytes 12296 | tf_op jit(solution)/shard_map/ppermute | solution.py:370
  28.7 5.0 %collective-permute-start.11 = (f32[8,128]{1,0:T(8,128)S(1)}, f32[8,128]{1,0:T(8,128)S(1)}, u32[]{:S(2)}, u32[]{:S(2)}) collective-permute-start(f32[8,128]{1,0:T(8,128)S(1)} %shard_map.108.refs_8_.refs_7_), channel_id=1, source_target_pairs={{0,16},{8,24},{16,0},{24,8},{1,17},{9,25},{17,1},{25,9},{2,18},{10... | collective-permute-start | bytes 12296 | tf_op jit(solution)/shard_map/ppermute | solution.py:370
  30.2 3.6 %collective-permute-start.10 = (f32[8,128]{1,0:T(8,128)S(1)}, f32[8,128]{1,0:T(8,128)S(1)}, u32[]{:S(2)}, u32[]{:S(2)}) collective-permute-start(f32[8,128]{1,0:T(8,128)S(1)} %shard_map.108.refs_8_.refs_7_), channel_id=1, source_target_pairs={{0,8},{8,0},{16,24},{24,16},{1,9},{9,1},{17,25},{25,17},{2,10},{10... | collective-permute-start | bytes 12296 | tf_op jit(solution)/shard_map/ppermute | solution.py:370
  35.3 3.6 %collective-permute-start.13 = (bf16[4,2,64,128]{3,2,1,0:T(8,128)(2,1)S(1)}, bf16[4,2,64,128]{3,2,1,0:T(8,128)(2,1)S(1)}, u32[]{:S(2)}, u32[]{:S(2)}) collective-permute-start(bf16[4,2,64,128]{3,2,1,0:T(8,128)(2,1)S(1)} %get-tuple-element.33), channel_id=1, source_target_pairs={{0,2},{2,0},{1,3},{3,1},{4,6},{6,4},{5,7},{7,5},{8,10},{10,8},{9,1... | collective-permute-start | bytes 393224 | tf_op jit(solution)/shard_map/ppermute | solution.py:370
  35.4 6.4 %collective-permute-start.18 = (bf16[2,256,128]{2,1,0:T(8,128)(2,1)S(1)}, bf16[2,256,128]{2,1,0:T(8,128)(2,1)S(1)}, u32[]{:S(2)}, u32[]{:S(2)}) collective-permute-start(bf16[2,256,128]{2,1,0:T(8,128)(2,1)S(1)} %get-tuple-element.37), channel_id=1, source_target_pairs={{0,1},{1,0},{2,3},{3,2},{4,5},{5,4},{6,7},{7,6},{8,9},{9,8},{10,11... | collective-permute-start | bytes 393224 | tf_op jit(solution)/shard_map/ppermute | solution.py:370
  36.3 8.4 %collective-permute-start.19 = (bf16[2,256,128]{2,1,0:T(8,128)(2,1)S(1)}, bf16[2,256,128]{2,1,0:T(8,128)(2,1)S(1)}, u32[]{:S(2)}, u32[]{:S(2)}) collective-permute-start(bf16[2,256,128]{2,1,0:T(8,128)(2,1)S(1)} %get-tuple-element.38), channel_id=1, source_target_pairs={{0,4},{1,5},{2,6},{3,7},{4,0},{5,1},{6,2},{7,3},{8,12},{9,13},{10,... | collective-permute-start | bytes 393224 | tf_op jit(solution)/shard_map/ppermute | solution.py:370
  37.1 7.6 %collective-permute-start.20 = (bf16[2,256,128]{2,1,0:T(8,128)(2,1)S(1)}, bf16[2,256,128]{2,1,0:T(8,128)(2,1)S(1)}, u32[]{:S(2)}, u32[]{:S(2)}) collective-permute-start(bf16[2,256,128]{2,1,0:T(8,128)(2,1)S(1)} %get-tuple-element.39), channel_id=1, source_target_pairs={{0,5},{1,4},{2,7},{3,6},{4,1},{5,0},{6,3},{7,2},{8,13},{9,12},{10,... | collective-permute-start | bytes 393224 | tf_op jit(solution)/shard_map/ppermute | solution.py:370
  39.0 5.8 %collective-permute-start.14 = (bf16[2,2,64,128]{3,2,1,0:T(8,128)(2,1)S(1)}, bf16[2,2,64,128]{3,2,1,0:T(8,128)(2,1)S(1)}, u32[]{:S(2)}, u32[]{:S(2)}) collective-permute-start(bf16[2,2,64,128]{3,2,1,0:T(8,128)(2,1)S(1)} %pad_maximum_fusion.5), channel_id=1, source_target_pairs={{0,16},{8,24},{16,0},{24,8},{1,17},{9,25},{17,1},{25,9},{2,18},{10... | collective-permute-start | bytes 196616 | tf_op jit(solution)/shard_map/ppermute | solution.py:370
  40.4 4.6 %collective-permute-start.15 = (bf16[2,2,64,128]{3,2,1,0:T(8,128)(2,1)S(1)}, bf16[2,2,64,128]{3,2,1,0:T(8,128)(2,1)S(1)}, u32[]{:S(2)}, u32[]{:S(2)}) collective-permute-start(bf16[2,2,64,128]{3,2,1,0:T(8,128)(2,1)S(1)} %pad_maximum_fusion.6), channel_id=1, source_target_pairs={{0,8},{8,0},{16,24},{24,16},{1,9},{9,1},{17,25},{25,17},{2,10},{10... | collective-permute-start | bytes 196616 | tf_op jit(solution)/shard_map/ppermute | solution.py:370
  41.7 6.1 %collective-permute-start.16 = (bf16[2,2,64,128]{3,2,1,0:T(8,128)(2,1)S(1)}, bf16[2,2,64,128]{3,2,1,0:T(8,128)(2,1)S(1)}, u32[]{:S(2)}, u32[]{:S(2)}) collective-permute-start(bf16[2,2,64,128]{3,2,1,0:T(8,128)(2,1)S(1)} %pad_maximum_fusion.7), channel_id=1, source_target_pairs={{0,24},{8,16},{16,8},{24,0},{1,25},{9,17},{17,9},{25,1},{2,26},{10... | collective-permute-start | bytes 196616 | tf_op jit(solution)/shard_map/ppermute | solution.py:370
  47.8 4.0 %collective-permute-start.21 = (bf16[4,256,128]{2,1,0:T(8,128)(2,1)S(1)}, bf16[4,256,128]{2,1,0:T(8,128)(2,1)S(1)}, u32[]{:S(2)}, u32[]{:S(2)}) collective-permute-start(bf16[4,256,128]{2,1,0:T(8,128)(2,1)S(1)} %shard_map.112), channel_id=1, source_target_pairs={{0,2},{1,3},{2,0},{3,1},{4,6},{5,7},{6,4},{7,5},{8,10},{9,11},{10,... | collective-permute-start | bytes 786440 | tf_op jit(solution)/shard_map/ppermute | solution.py:370
  47.9 4.0 %collective-permute-start.17 = (bf16[2,64,128]{2,1,0:T(8,128)(2,1)S(1)}, bf16[2,64,128]{2,1,0:T(8,128)(2,1)S(1)}, u32[]{:S(2)}, u32[]{:S(2)}) collective-permute-start(bf16[2,64,128]{2,1,0:T(8,128)(2,1)S(1)} %get-tuple-element.35), channel_id=1, source_target_pairs={{0,4},{4,0},{1,5},{5,1},{2,6},{6,2},{3,7},{7,3},{8,12},{12,8},{9,1... | collective-permute-start | bytes 98312 | tf_op jit(solution)/shard_map/ppermute | solution.py:370

commit v14 on v13

--- a/solution.py
+++ b/solution.py
@@ -91,9 +91,8 @@
         lax.broadcasted_iota(jnp.int32, shape, 1) & (rows - 1)
     )
     shape = (STAT_ROWS, STAT_ROWS)
-    gather = lax.broadcasted_iota(jnp.int32, shape, 0) == (
-        lax.broadcasted_iota(jnp.int32, shape, 1) >> shift_of(rows)
-    )
+    piece_of = lax.broadcasted_iota(jnp.int32, shape, 1) >> shift_of(rows)
+    stat_row = lax.broadcasted_iota(jnp.int32, shape, 0)
     for copy in copies[:stat_copies]:
         copy.wait()
     pieces = [piece.astype(jnp.float32) for piece in split_pieces(lse_ref[...])]
@@ -101,17 +100,20 @@
     pieces = jnp.concatenate(pieces, axis=0).astype(jnp.bfloat16)
     spread = jnp.dot(pieces, chosen, preferred_element_type=jnp.float32)
     spread = jnp.where(own_row, spread, 0.0).astype(jnp.bfloat16)
-    lse_rows_all = jnp.dot(
-        gather.astype(jnp.bfloat16), spread, preferred_element_type=jnp.float32
-    )
     kind = lax.broadcasted_iota(jnp.int32, (STAT_ROWS, wide), 0)
+    half = lax.broadcasted_iota(jnp.int32, (STAT_ROWS, wide), 1) >> shift_of(lines)
     for m, (ref, first) in enumerate(slabs):
+        top = m // 2 * (2 * PIECES)
+        gather = (stat_row - top == piece_of).astype(jnp.bfloat16)
+        own = spread[:, m * wide : (m + 1) * wide]
+        stats = jnp.dot(gather, own, preferred_element_type=jnp.float32)
         o_grad = ref[lines:wide, :].astype(jnp.float32)
         product = o_grad * o_ref[pl.ds(first, lines), :].astype(jnp.float32)
         dots = jnp.sum(jnp.concatenate([product, product], axis=0).T, axis=0, keepdims=True)
-        stats = lse_rows_all[:, m * wide : (m + 1) * wide]
         for k, piece in enumerate(split_pieces(dots)):
-            stats = jnp.where(kind == PIECES + k, piece.astype(jnp.float32), stats)
+            stats = jnp.where(kind == top + PIECES + k, piece.astype(jnp.float32), stats)
+        if len(slabs) > 1:
+            stats = jnp.where(half == m % 2, stats, 0.0)
         ref[wide:, :] = stats.astype(jnp.bfloat16)
     for copy in copies[stat_copies:]:
         copy.wait()
@@ -149,22 +151,6 @@
 
 def lse_rows(size):
     return max(1, size // DH)
-
-
-def block_kernel(*refs):
-    slab_refs, out_ref = refs[:-1], refs[-1]
-    low = lax.broadcasted_iota(jnp.int32, (STAT_ROWS, DH), 1) < DH // 2
-    stats = []
-    for m, ref in enumerate(slab_refs):
-        out_ref[m * DH : (m + 1) * DH, :] = ref[0:DH, :]
-        stats.append(ref[DH : DH + STAT_ROWS, :].astype(jnp.float32))
-    if len(stats) > 1:
-        pairs = [
-            jnp.where(low, stats[m], stats[m + 1])[: 2 * PIECES] for m in range(0, len(stats), 2)
-        ]
-        rest = STAT_ROWS - len(pairs) * 2 * PIECES
-        stats = [jnp.concatenate([*pairs, jnp.zeros((rest, DH), jnp.float32)], axis=0)]
-    out_ref[len(slab_refs) * DH :, :] = stats[0].astype(jnp.bfloat16)
 
 
 def slabs_of(row_refs):
@@ -454,20 +440,15 @@
         in_hbm(keys),
         in_hbm(values),
     )
-    own_block = pl.pallas_call(
-        block_kernel,
-        in_specs=[VMEM] * groups,
-        out_specs=VMEM,
-        out_shape=jax.ShapeDtypeStruct((groups * DH + STAT_ROWS, DH), jnp.bfloat16),
-        compiler_params=PARAMS,
-    )(*swap_slabs(slabs, groups))
+    slabs = swap_slabs(slabs, groups)
+    own_block = jnp.concatenate([x[:DH] for x in slabs] + [sum(x[DH:] for x in slabs)], axis=0)
     pairs = swap_pairs(kv_keep, kv_send)
     far = [1 << n for n in reversed(range(shift_of(parts)))]
 
     blocks, came = [0], [own_block]
     for d in far:
         if d == 1:
-            came = came[:1] + [tie(x, pairs[1:]) for x in came[1:]]
+            came = came[:1] + [tie(x, pairs[1:3]) for x in came[1:]]
         came = came + [swap(x, "part", d, parts) for x in came]
         blocks = blocks + [b ^ d for b in blocks]
     ends, live = line_limits(parts, row_count, nears, rows, lines, resp_len, prompt_end)

time: 53.1 us -> 51.7 us (0.974)
  waiting for transfers between devices: 16.6 us -> 13.7 us
  starting transfers between devices: 26.1 us -> 27.7 us
    ppermute x22, waiting for transfers between devices: 16.6 us -> 13.7 us  [swap(): return lax.ppermute(x, axis, [(i, i ^ distance) for i in range(size)])]
    ppermute x22, starting transfers between devices: 26.1 us -> 27.7 us  [swap(): return lax.ppermute(x, axis, [(i, i ^ distance) for i in range(size)])]
  transfers between devices with their start and end apart: 22 -> 22, of which waited for: 11 -> 10; matrix products, arithmetic and copies ran while one was open for 1% -> 1% of each run, Pallas kernels for 6% -> 6%
where the time goes in v14:
time: 51.7 us; the launch traced here: 51.5 us
  starting transfers between devices  27.7 us (54%)
  waiting for transfers between devices  13.7 us (26%)
  Pallas kernels  7.66 us (15%)
  between operations  2.12 us (4%)
    ppermute x22, starting transfers between devices, swap(): return lax.ppermute(x, axis, [(i, i ^ distance) for i in range(size)])  27.7 us
    ppermute x22, waiting for transfers between devices, swap(): return lax.ppermute(x, axis, [(i, i ^ distance) for i in range(size)])  13.7 us
    pallas_call x1, Pallas kernels, shards(): pl.pallas_call(functools.partial(part_kernel, blocks, nears, heads, token...  2.05 us
    pallas_call x2, Pallas kernels, part_lse(): pl.pallas_call(functools.partial(stat_kernel, held, first, nears, heads,...  1.76 us
    pallas_call x1, Pallas kernels, shards(): pl.pallas_call(functools.partial(token_kernel, blocks, nears, heads, toke...  1.46 us
    pallas_call x1, Pallas kernels, shards(): pl.pallas_call(functools.partial(pack_kernel, row_count, nears, heads), i...  1.38 us
  transfers between devices with their start and end apart: 22, of which 10 were waited for; matrix products, arithmetic and copies ran while one was open for 1% of the time, Pallas kernels for 6%

profile of v14, /device:TPU:0, one launch (start us, length us, event | category | flops | bytes accessed | tf_op | source)
XLA Modules:
  0.0 51.5 jit_solution(9459093959536576976)
XLA Ops:
  0.6 1.4 %shard_map.103 = (bf16[144,128]{1,0:T(8,128)(2,1)S(1)}, bf16[144,128]{1,0:T(8,128)(2,1)S(1)}, bf16[144,128]{1,0:T(8,128)(2,1)S(1)}, bf16[144,128]{1,0:T(8,128)(2...) custom-call(bf16[256,128]{1,0:T(8,128)(2,1)} %bitcast.24, bf16[256,128]{1,0:T(8,128)(2,1)} %bitcast.25, ...), custom_call_target="tpu_custom_call" | custom-call | tf_op jit(solution)/shard_map/pallas_call | solution.py:424
  2.0 0.5 %collective-permute-start = (bf16[144,128]{1,0:T(8,128)(2,1)S(1)}, bf16[144,128]{1,0:T(8,128)(2,1)S(1)}, u32[]{:S(2)}, u32[]{:S(2)}) collective-permute-start(bf16[144,128]{1,0:T(8,128)(2,1)S(1)} %get-tuple-element.24), channel_id=1, source_target_pairs={{0,2},{2,0},{4,6},{6,4},{1,3},{3,1},{5,7},{7,5},{8,10},{10,8},{12,... | collective-permute-start | bytes 110600 | tf_op jit(solution)/shard_map/ppermute | solution.py:356
  2.5 2.6 %collective-permute-start.1 = (bf16[144,128]{1,0:T(8,128)(2,1)S(1)}, bf16[144,128]{1,0:T(8,128)(2,1)S(1)}, u32[]{:S(2)}, u32[]{:S(2)}) collective-permute-start(bf16[144,128]{1,0:T(8,128)(2,1)S(1)} %get-tuple-element.25), channel_id=1, source_target_pairs={{0,4},{2,6},{4,0},{6,2},{1,5},{3,7},{5,1},{7,3},{8,12},{10,14},{12... | collective-permute-start | bytes 110600 | tf_op jit(solution)/shard_map/ppermute | solution.py:356
  5.1 0.1 collective-permute-start.2
  5.2 0.1 collective-permute-start.4
  5.4 0.0 collective-permute-done
  5.4 1.8 %collective-permute-done.1 = bf16[144,128]{1,0:T(8,128)(2,1)S(1)} collective-permute-done((bf16[144,128]{1,0:T(8,128)(2,1)S(1)}, bf16[144,128]{1,0:T(8,128)(2,1)S(1)}, u32[]{:S(2)}, u32[]{:S(2)}) %collective-permute-start.1) | collective-permute-done | bytes 36896 | tf_op jit(solution)/shard_map/ppermute | solution.py:356
  7.2 1.4 %collective-permute-done.2 = bf16[144,128]{1,0:T(8,128)(2,1)S(1)} collective-permute-done((bf16[144,128]{1,0:T(8,128)(2,1)S(1)}, bf16[144,128]{1,0:T(8,128)(2,1)S(1)}, u32[]{:S(2)}, u32[]{:S(2)}) %collective-permute-start.2) | collective-permute-done | bytes 36896 | tf_op jit(solution)/shard_map/ppermute | solution.py:356
  8.6 2.7 %collective-permute-start.3 = (bf16[528,128]{1,0:T(8,128)(2,1)S(1)}, bf16[528,128]{1,0:T(8,128)(2,1)S(1)}, u32[]{:S(2)}, u32[]{:S(2)}) collective-permute-start(bf16[528,128]{1,0:T(8,128)(2,1)S(1)} %constant_dynamic-update-slice_fusion.refs_0_), channel_id=1, source_target_pairs={{0,16},{8,24},{16,0},{24,8},{1,17},{9,25},{17,1},{25,9},{2,18},{10... | collective-permute-start | bytes 405512 | tf_op jit(solution)/shard_map/ppermute | solution.py:356
  11.2 0.0 collective-permute-done.4
  11.3 1.6 %collective-permute-start.5 = (bf16[2,256,128]{2,1,0:T(8,128)(2,1)S(1)}, bf16[2,256,128]{2,1,0:T(8,128)(2,1)S(1)}, u32[]{:S(2)}, u32[]{:S(2)}) collective-permute-start(bf16[2,256,128]{2,1,0:T(8,128)(2,1)S(1)} %pad_maximum_fusion.1), channel_id=1, source_target_pairs={{0,1},{1,0},{2,3},{3,2},{4,5},{5,4},{6,7},{7,6},{8,9},{9,8},{10,11... | collective-permute-start | bytes 393224 | tf_op jit(solution)/shard_map/ppermute | solution.py:356
  12.9 0.9 %collective-permute-start.6 = (bf16[2,256,128]{2,1,0:T(8,128)(2,1)S(1)}, bf16[2,256,128]{2,1,0:T(8,128)(2,1)S(1)}, u32[]{:S(2)}, u32[]{:S(2)}) collective-permute-start(bf16[2,256,128]{2,1,0:T(8,128)(2,1)S(1)} %pad_maximum_fusion.2), channel_id=1, source_target_pairs={{0,4},{1,5},{2,6},{3,7},{4,0},{5,1},{6,2},{7,3},{8,12},{9,13},{10,... | collective-permute-start | bytes 393224 | tf_op jit(solution)/shard_map/ppermute | solution.py:356
  14.5 1.6 %collective-permute-start.7 = (bf16[528,128]{1,0:T(8,128)(2,1)S(1)}, bf16[528,128]{1,0:T(8,128)(2,1)S(1)}, u32[]{:S(2)}, u32[]{:S(2)}) collective-permute-start(bf16[528,128]{1,0:T(8,128)(2,1)S(1)} %constant_dynamic-update-slice_fusion.refs_0_), channel_id=1, source_target_pairs={{0,8},{8,0},{16,24},{24,16},{1,9},{9,1},{17,25},{25,17},{2,10},{10... | collective-permute-start | bytes 405512 | tf_op jit(solution)/shard_map/ppermute | solution.py:356
  16.1 1.2 %collective-permute-start.9 = (bf16[2,256,128]{2,1,0:T(8,128)(2,1)S(1)}, bf16[2,256,128]{2,1,0:T(8,128)(2,1)S(1)}, u32[]{:S(2)}, u32[]{:S(2)}) collective-permute-start(bf16[2,256,128]{2,1,0:T(8,128)(2,1)S(1)} %pad_maximum_fusion.4), channel_id=1, source_target_pairs={{0,5},{1,4},{2,7},{3,6},{4,1},{5,0},{6,3},{7,2},{8,13},{9,12},{10,... | collective-permute-start | bytes 393224 | tf_op jit(solution)/shard_map/ppermute | solution.py:356
  17.3 0.9 %collective-permute-done.3.refs_0_ = bf16[528,128]{1,0:T(8,128)(2,1)S(1)} collective-permute-done((bf16[528,128]{1,0:T(8,128)(2,1)S(1)}, bf16[528,128]{1,0:T(8,128)(2,1)S(1)}, u32[]{:S(2)}, u32[]{:S(2)}) %collective-permute-start.3) | collective-permute-done | bytes 135200 | tf_op jit(solution)/shard_map/ppermute | solution.py:356
  18.2 0.0 collective-permute-done.5.refs_1_.refs_4_.refs_2_.refs_5_
  18.2 0.0 collective-permute-done.6.refs_2_.refs_5_.refs_3_.refs_6_
  18.2 2.7 %collective-permute-start.8 = (bf16[528,128]{1,0:T(8,128)(2,1)S(1)}, bf16[528,128]{1,0:T(8,128)(2,1)S(1)}, u32[]{:S(2)}, u32[]{:S(2)}) collective-permute-start(bf16[528,128]{1,0:T(8,128)(2,1)S(1)} %shard_map.104.refs_1_), channel_id=1, source_target_pairs={{0,8},{8,0},{16,24},{24,16},{1,9},{9,1},{17,25},{25,17},{2,10},{10... | collective-permute-start | bytes 405512 | tf_op jit(solution)/shard_map/ppermute | solution.py:356
  21.6 0.0 collective-permute-done.7.refs_2_
  21.6 0.4 collective-permute-done.9.refs_6_.refs_4_.refs_7_
  22.0 1.1 %shard_map.105.refs_1_.refs_5_ = f32[8,128]{1,0:T(8,128)S(1)} custom-call(s32[1,1024]{1,0:T(1,128)S(1)} %compare_select_fusion.ends_ref, bf16[528,128]{1,0:T(8,128)(2,1)S(1)} %constant_dynamic-update-slice_fusion.refs_0_, bf16[528,128]{1,0:T(8,128)(2,1)S(1)} %shard_map.104.refs_1_, bf16[528,128]{1,0:T(8,128)(2,1)S(1)} %collective-permute-done.7.refs_2_, ...), custom_call_target="tpu_custom_call" | custom-call | tf_op jit(solution)/shard_map/pallas_call | solution.py:457
  23.2 0.7 %collective-permute-done.8.refs_0_ = bf16[528,128]{1,0:T(8,128)(2,1)S(1)} collective-permute-done((bf16[528,128]{1,0:T(8,128)(2,1)S(1)}, bf16[528,128]{1,0:T(8,128)(2,1)S(1)}, u32[]{:S(2)}, u32[]{:S(2)}) %collective-permute-start.8) | collective-permute-done | bytes 135200 | tf_op jit(solution)/shard_map/ppermute | solution.py:356
  23.9 0.6 %shard_map.107.refs_8_.refs_7_ = f32[8,128]{1,0:T(8,128)S(1)} custom-call(s32[1,1024]{1,0:T(1,128)S(1)} %compare_select_fusion.ends_ref, bf16[528,128]{1,0:T(8,128)(2,1)S(1)} %shard_map.106.refs_0_.refs_3_, bf16[2,256,128]{2,1,0:T(8,128)(2,1)S(1)} %pad_maximum_fusion.3.refs_3_.refs_1_.refs_4_, ...), custom_call_target="tpu_custom_call" | custom-call | tf_op jit(solution)/shard_map/pallas_call | solution.py:457
  24.6 3.4 %collective-permute-start.12 = (f32[8,128]{1,0:T(8,128)S(1)}, f32[8,128]{1,0:T(8,128)S(1)}, u32[]{:S(2)}, u32[]{:S(2)}) collective-permute-start(f32[8,128]{1,0:T(8,128)S(1)} %shard_map.107.refs_8_.refs_7_), channel_id=1, source_target_pairs={{0,24},{8,16},{16,8},{24,0},{1,25},{9,17},{17,9},{25,1},{2,26},{10... | collective-permute-start | bytes 12296 | tf_op jit(solution)/shard_map/ppermute | solution.py:356
  27.9 0.2 collective-permute-start.11
  28.1 0.9 %collective-permute-start.10 = (f32[8,128]{1,0:T(8,128)S(1)}, f32[8,128]{1,0:T(8,128)S(1)}, u32[]{:S(2)}, u32[]{:S(2)}) collective-permute-start(f32[8,128]{1,0:T(8,128)S(1)} %shard_map.107.refs_8_.refs_7_), channel_id=1, source_target_pairs={{0,8},{8,0},{16,24},{24,16},{1,9},{9,1},{17,25},{25,17},{2,10},{10... | collective-permute-start | bytes 12296 | tf_op jit(solution)/shard_map/ppermute | solution.py:356
  29.0 2.1 %shard_map.108 = (bf16[4,256,1024]{2,1,0:T(8,128)(2,1)S(1)}, bf16[4,256,1024]{2,1,0:T(8,128)(2,1)S(1)}, f32[128,1024]{1,0:T(8,128)S(1)}) custom-call(s32[1,1024]{1,0:T(1,128)S(1)} %compare_select_fusion.ends_ref, bf16[528,128]{1,0:T(8,128)(2,1)S(1)} %constant_dynamic-update-slice_fusion.refs_0_, bf16[528,128]{1,0:T(8,128)(2,1)S(1)} %shard_map.104.refs_1_, ...), custom_call_target="tpu_custom_call" | custom-call | tf_op jit(solution)/shard_map/pallas_call | solution.py:471
  31.1 0.0 collective-permute-done.12.refs_10_
  31.1 1.3 %collective-permute-done.11.refs_9_ = f32[8,128]{1,0:T(8,128)S(1)} collective-permute-done((f32[8,128]{1,0:T(8,128)S(1)}, f32[8,128]{1,0:T(8,128)S(1)}, u32[]{:S(2)}, u32[]{:S(2)}) %collective-permute-start.11) | collective-permute-done | bytes 4128 | tf_op jit(solution)/shard_map/ppermute | solution.py:356
  32.5 0.0 collective-permute-done.10.refs_8_
  32.5 1.5 %shard_map.109 = (bf16[2,256,128]{2,1,0:T(8,128)(2,1)S(1)}, bf16[2,256,128]{2,1,0:T(8,128)(2,1)S(1)}, bf16[2,256,128]{2,1,0:T(8,128)(2,1)S(1)}, bf16[2,256,128]{...) custom-call(s32[1,1024]{1,0:T(1,128)S(1)} %compare_convert_fusion.live_ref, ...), custom_call_target="tpu_custom_call" | custom-call | tf_op jit(solution)/shard_map/pallas_call | solution.py:480
  33.9 0.1 collective-permute-start.13
  34.0 1.6 %collective-permute-start.18 = (bf16[2,256,128]{2,1,0:T(8,128)(2,1)S(1)}, bf16[2,256,128]{2,1,0:T(8,128)(2,1)S(1)}, u32[]{:S(2)}, u32[]{:S(2)}) collective-permute-start(bf16[2,256,128]{2,1,0:T(8,128)(2,1)S(1)} %get-tuple-element.37), channel_id=1, source_target_pairs={{0,1},{1,0},{2,3},{3,2},{4,5},{5,4},{6,7},{7,6},{8,9},{9,8},{10,11... | collective-permute-start | bytes 393224 | tf_op jit(solution)/shard_map/ppermute | solution.py:356
  35.6 0.9 %collective-permute-start.19 = (bf16[2,256,128]{2,1,0:T(8,128)(2,1)S(1)}, bf16[2,256,128]{2,1,0:T(8,128)(2,1)S(1)}, u32[]{:S(2)}, u32[]{:S(2)}) collective-permute-start(bf16[2,256,128]{2,1,0:T(8,128)(2,1)S(1)} %get-tuple-element.38), channel_id=1, source_target_pairs={{0,4},{1,5},{2,6},{3,7},{4,0},{5,1},{6,2},{7,3},{8,12},{9,13},{10,... | collective-permute-start | bytes 393224 | tf_op jit(solution)/shard_map/ppermute | solution.py:356
  36.5 1.1 %collective-permute-start.20 = (bf16[2,256,128]{2,1,0:T(8,128)(2,1)S(1)}, bf16[2,256,128]{2,1,0:T(8,128)(2,1)S(1)}, u32[]{:S(2)}, u32[]{:S(2)}) collective-permute-start(bf16[2,256,128]{2,1,0:T(8,128)(2,1)S(1)} %get-tuple-element.39), channel_id=1, source_target_pairs={{0,5},{1,4},{2,7},{3,6},{4,1},{5,0},{6,3},{7,2},{8,13},{9,12},{10,... | collective-permute-start | bytes 393224 | tf_op jit(solution)/shard_map/ppermute | solution.py:356
  37.6 0.0 collective-permute-done.13.refs_1_
  37.6 2.1 %collective-permute-start.14 = (bf16[2,2,64,128]{3,2,1,0:T(8,128)(2,1)S(1)}, bf16[2,2,64,128]{3,2,1,0:T(8,128)(2,1)S(1)}, u32[]{:S(2)}, u32[]{:S(2)}) collective-permute-start(bf16[2,2,64,128]{3,2,1,0:T(8,128)(2,1)S(1)} %pad_maximum_fusion.5), channel_id=1, source_target_pairs={{0,16},{8,24},{16,0},{24,8},{1,17},{9,25},{17,1},{25,9},{2,18},{10... | collective-permute-start | bytes 196616 | tf_op jit(solution)/shard_map/ppermute | solution.py:356
  39.7 0.6 %collective-permute-start.15 = (bf16[2,2,64,128]{3,2,1,0:T(8,128)(2,1)S(1)}, bf16[2,2,64,128]{3,2,1,0:T(8,128)(2,1)S(1)}, u32[]{:S(2)}, u32[]{:S(2)}) collective-permute-start(bf16[2,2,64,128]{3,2,1,0:T(8,128)(2,1)S(1)} %pad_maximum_fusion.6), channel_id=1, source_target_pairs={{0,8},{8,0},{16,24},{24,16},{1,9},{9,1},{17,25},{25,17},{2,10},{10... | collective-permute-start | bytes 196616 | tf_op jit(solution)/shard_map/ppermute | solution.py:356
  40.4 1.9 %collective-permute-start.16 = (bf16[2,2,64,128]{3,2,1,0:T(8,128)(2,1)S(1)}, bf16[2,2,64,128]{3,2,1,0:T(8,128)(2,1)S(1)}, u32[]{:S(2)}, u32[]{:S(2)}) collective-permute-start(bf16[2,2,64,128]{3,2,1,0:T(8,128)(2,1)S(1)} %pad_maximum_fusion.7), channel_id=1, source_target_pairs={{0,24},{8,16},{16,8},{24,0},{1,25},{9,17},{17,9},{25,1},{2,26},{10... | collective-permute-start | bytes 196616 | tf_op jit(solution)/shard_map/ppermute | solution.py:356
  42.3 1.6 %collective-permute-done.19.refs_4_ = bf16[2,256,128]{2,1,0:T(8,128)(2,1)S(1)} collective-permute-done((bf16[2,256,128]{2,1,0:T(8,128)(2,1)S(1)}, bf16[2,256,128]{2,1,0:T(8,128)(2,1)S(1)}, u32[]{:S(2)}, u32[]{:S(2)}) %collective-permute-start.19) | collective-permute-done | bytes 131104 | tf_op jit(solution)/shard_map/ppermute | solution.py:356
  43.9 0.0 collective-permute-done.20.refs_5_
  44.0 0.0 collective-permute-done.14.refs_2_.refs_1_
  44.0 0.2 collective-permute-done.15.refs_3_.refs_2_
  44.2 2.2 %collective-permute-done.16.refs_4_.refs_3_ = bf16[2,2,64,128]{3,2,1,0:T(8,128)(2,1)S(1)} collective-permute-done((bf16[2,2,64,128]{3,2,1,0:T(8,128)(2,1)S(1)}, bf16[2,2,64,128]{3,2,1,0:T(8,128)(2,1)S(1)}, u32[]{:S(2)}, u32[]{:S(2)}) %collective-permute-start.16) | collective-permute-done | bytes 65568 | tf_op jit(solution)/shard_map/ppermute | solution.py:356
  46.5 1.0 %collective-permute-start.17 = (bf16[2,64,128]{2,1,0:T(8,128)(2,1)S(1)}, bf16[2,64,128]{2,1,0:T(8,128)(2,1)S(1)}, u32[]{:S(2)}, u32[]{:S(2)}) collective-permute-start(bf16[2,64,128]{2,1,0:T(8,128)(2,1)S(1)} %get-tuple-element.35), channel_id=1, source_target_pairs={{0,4},{4,0},{1,5},{5,1},{2,6},{6,2},{3,7},{7,3},{8,12},{12,8},{9,1... | collective-permute-start | bytes 98312 | tf_op jit(solution)/shard_map/ppermute | solution.py:356
  47.5 3.0 %collective-permute-done.17.refs_1_ = bf16[2,64,128]{2,1,0:T(8,128)(2,1)S(1)} collective-permute-done((bf16[2,64,128]{2,1,0:T(8,128)(2,1)S(1)}, bf16[2,64,128]{2,1,0:T(8,128)(2,1)S(1)}, u32[]{:S(2)}, u32[]{:S(2)}) %collective-permute-start.17) | collective-permute-done | bytes 32800 | tf_op jit(solution)/shard_map/ppermute | solution.py:356
  50.5 0.0 collective-permute-done.21.refs_6_
  50.5 1.0 %shard_map.112 = (bf16[256,128]{1,0:T(8,128)(2,1)}, bf16[128,1024]{1,0:T(8,128)(2,1)}, bf16[128,1024]{1,0:T(8,128)(2,1)}) custom-call(bf16[2,64,128]{2,1,0:T(8,128)(2,1)S(1)} %get-tuple-element.34.refs_0_, bf16[2,64,128]{2,1,0:T(8,128)(2,1)S(1)} %collective-permute-done.17.refs_1_, bf16[2,256,128]{2,1,0:T(8,128)(2,1)S(1)} %get-tuple-element.36.refs_2_, ...), custom_call_target="tpu_custom_call" | custom-call | tf_op jit(solution)/shard_map/pallas_call | solution.py:502
  (29 shorter events, 0.4 us)
Async XLA Ops:
  2.0 3.4 %collective-permute-start = (bf16[144,128]{1,0:T(8,128)(2,1)S(1)}, bf16[144,128]{1,0:T(8,128)(2,1)S(1)}, u32[]{:S(2)}, u32[]{:S(2)}) collective-permute-start(bf16[144,128]{1,0:T(8,128)(2,1)S(1)} %get-tuple-element.24), channel_id=1, source_target_pairs={{0,2},{2,0},{4,6},{6,4},{1,3},{3,1},{5,7},{7,5},{8,10},{10,8},{12,... | collective-permute-start | bytes 110600 | tf_op jit(solution)/shard_map/ppermute | solution.py:356
  2.5 4.7 %collective-permute-start.1 = (bf16[144,128]{1,0:T(8,128)(2,1)S(1)}, bf16[144,128]{1,0:T(8,128)(2,1)S(1)}, u32[]{:S(2)}, u32[]{:S(2)}) collective-permute-start(bf16[144,128]{1,0:T(8,128)(2,1)S(1)} %get-tuple-element.25), channel_id=1, source_target_pairs={{0,4},{2,6},{4,0},{6,2},{1,5},{3,7},{5,1},{7,3},{8,12},{10,14},{12... | collective-permute-start | bytes 110600 | tf_op jit(solution)/shard_map/ppermute | solution.py:356
  5.1 3.4 %collective-permute-start.2 = (bf16[144,128]{1,0:T(8,128)(2,1)S(1)}, bf16[144,128]{1,0:T(8,128)(2,1)S(1)}, u32[]{:S(2)}, u32[]{:S(2)}) collective-permute-start(bf16[144,128]{1,0:T(8,128)(2,1)S(1)} %get-tuple-element.26), channel_id=1, source_target_pairs={{0,6},{2,4},{4,2},{6,0},{1,7},{3,5},{5,3},{7,1},{8,14},{10,12},{12... | collective-permute-start | bytes 110600 | tf_op jit(solution)/shard_map/ppermute | solution.py:356
  5.2 6.0 %collective-permute-start.4 = (bf16[4,256,128]{2,1,0:T(8,128)(2,1)S(1)}, bf16[4,256,128]{2,1,0:T(8,128)(2,1)S(1)}, u32[]{:S(2)}, u32[]{:S(2)}) collective-permute-start(bf16[4,256,128]{2,1,0:T(8,128)(2,1)S(1)} %get-tuple-element.28), channel_id=1, source_target_pairs={{0,2},{1,3},{2,0},{3,1},{4,6},{5,7},{6,4},{7,5},{8,10},{9,11},{10,... | collective-permute-start | bytes 786440 | tf_op jit(solution)/shard_map/ppermute | solution.py:356
  8.6 9.6 %collective-permute-start.3 = (bf16[528,128]{1,0:T(8,128)(2,1)S(1)}, bf16[528,128]{1,0:T(8,128)(2,1)S(1)}, u32[]{:S(2)}, u32[]{:S(2)}) collective-permute-start(bf16[528,128]{1,0:T(8,128)(2,1)S(1)} %constant_dynamic-update-slice_fusion.refs_0_), channel_id=1, source_target_pairs={{0,16},{8,24},{16,0},{24,8},{1,17},{9,25},{17,1},{25,9},{2,18},{10... | collective-permute-start | bytes 405512 | tf_op jit(solution)/shard_map/ppermute | solution.py:356
  11.3 6.9 %collective-permute-start.5 = (bf16[2,256,128]{2,1,0:T(8,128)(2,1)S(1)}, bf16[2,256,128]{2,1,0:T(8,128)(2,1)S(1)}, u32[]{:S(2)}, u32[]{:S(2)}) collective-permute-start(bf16[2,256,128]{2,1,0:T(8,128)(2,1)S(1)} %pad_maximum_fusion.1), channel_id=1, source_target_pairs={{0,1},{1,0},{2,3},{3,2},{4,5},{5,4},{6,7},{7,6},{8,9},{9,8},{10,11... | collective-permute-start | bytes 393224 | tf_op jit(solution)/shard_map/ppermute | solution.py:356
  12.9 5.4 %collective-permute-start.6 = (bf16[2,256,128]{2,1,0:T(8,128)(2,1)S(1)}, bf16[2,256,128]{2,1,0:T(8,128)(2,1)S(1)}, u32[]{:S(2)}, u32[]{:S(2)}) collective-permute-start(bf16[2,256,128]{2,1,0:T(8,128)(2,1)S(1)} %pad_maximum_fusion.2), channel_id=1, source_target_pairs={{0,4},{1,5},{2,6},{3,7},{4,0},{5,1},{6,2},{7,3},{8,12},{9,13},{10,... | collective-permute-start | bytes 393224 | tf_op jit(solution)/shard_map/ppermute | solution.py:356
  14.5 7.2 %collective-permute-start.7 = (bf16[528,128]{1,0:T(8,128)(2,1)S(1)}, bf16[528,128]{1,0:T(8,128)(2,1)S(1)}, u32[]{:S(2)}, u32[]{:S(2)}) collective-permute-start(bf16[528,128]{1,0:T(8,128)(2,1)S(1)} %constant_dynamic-update-slice_fusion.refs_0_), channel_id=1, source_target_pairs={{0,8},{8,0},{16,24},{24,16},{1,9},{9,1},{17,25},{25,17},{2,10},{10... | collective-permute-start | bytes 405512 | tf_op jit(solution)/shard_map/ppermute | solution.py:356
  16.1 5.9 %collective-permute-start.9 = (bf16[2,256,128]{2,1,0:T(8,128)(2,1)S(1)}, bf16[2,256,128]{2,1,0:T(8,128)(2,1)S(1)}, u32[]{:S(2)}, u32[]{:S(2)}) collective-permute-start(bf16[2,256,128]{2,1,0:T(8,128)(2,1)S(1)} %pad_maximum_fusion.4), channel_id=1, source_target_pairs={{0,5},{1,4},{2,7},{3,6},{4,1},{5,0},{6,3},{7,2},{8,13},{9,12},{10,... | collective-permute-start | bytes 393224 | tf_op jit(solution)/shard_map/ppermute | solution.py:356
  18.2 5.7 %collective-permute-start.8 = (bf16[528,128]{1,0:T(8,128)(2,1)S(1)}, bf16[528,128]{1,0:T(8,128)(2,1)S(1)}, u32[]{:S(2)}, u32[]{:S(2)}) collective-permute-start(bf16[528,128]{1,0:T(8,128)(2,1)S(1)} %shard_map.104.refs_1_), channel_id=1, source_target_pairs={{0,8},{8,0},{16,24},{24,16},{1,9},{9,1},{17,25},{25,17},{2,10},{10... | collective-permute-start | bytes 405512 | tf_op jit(solution)/shard_map/ppermute | solution.py:356
  24.6 6.6 %collective-permute-start.12 = (f32[8,128]{1,0:T(8,128)S(1)}, f32[8,128]{1,0:T(8,128)S(1)}, u32[]{:S(2)}, u32[]{:S(2)}) collective-permute-start(f32[8,128]{1,0:T(8,128)S(1)} %shard_map.107.refs_8_.refs_7_), channel_id=1, source_target_pairs={{0,24},{8,16},{16,8},{24,0},{1,25},{9,17},{17,9},{25,1},{2,26},{10... | collective-permute-start | bytes 12296 | tf_op jit(solution)/shard_map/ppermute | solution.py:356
  27.9 4.5 %collective-permute-start.11 = (f32[8,128]{1,0:T(8,128)S(1)}, f32[8,128]{1,0:T(8,128)S(1)}, u32[]{:S(2)}, u32[]{:S(2)}) collective-permute-start(f32[8,128]{1,0:T(8,128)S(1)} %shard_map.107.refs_8_.refs_7_), channel_id=1, source_target_pairs={{0,16},{8,24},{16,0},{24,8},{1,17},{9,25},{17,1},{25,9},{2,18},{10... | collective-permute-start | bytes 12296 | tf_op jit(solution)/shard_map/ppermute | solution.py:356
  28.1 4.3 %collective-permute-start.10 = (f32[8,128]{1,0:T(8,128)S(1)}, f32[8,128]{1,0:T(8,128)S(1)}, u32[]{:S(2)}, u32[]{:S(2)}) collective-permute-start(f32[8,128]{1,0:T(8,128)S(1)} %shard_map.107.refs_8_.refs_7_), channel_id=1, source_target_pairs={{0,8},{8,0},{16,24},{24,16},{1,9},{9,1},{17,25},{25,17},{2,10},{10... | collective-permute-start | bytes 12296 | tf_op jit(solution)/shard_map/ppermute | solution.py:356
  33.9 3.6 %collective-permute-start.13 = (bf16[4,2,64,128]{3,2,1,0:T(8,128)(2,1)S(1)}, bf16[4,2,64,128]{3,2,1,0:T(8,128)(2,1)S(1)}, u32[]{:S(2)}, u32[]{:S(2)}) collective-permute-start(bf16[4,2,64,128]{3,2,1,0:T(8,128)(2,1)S(1)} %get-tuple-element.33), channel_id=1, source_target_pairs={{0,2},{2,0},{1,3},{3,1},{4,6},{6,4},{5,7},{7,5},{8,10},{10,8},{9,1... | collective-permute-start | bytes 393224 | tf_op jit(solution)/shard_map/ppermute | solution.py:356
  34.0 6.3 %collective-permute-start.18 = (bf16[2,256,128]{2,1,0:T(8,128)(2,1)S(1)}, bf16[2,256,128]{2,1,0:T(8,128)(2,1)S(1)}, u32[]{:S(2)}, u32[]{:S(2)}) collective-permute-start(bf16[2,256,128]{2,1,0:T(8,128)(2,1)S(1)} %get-tuple-element.37), channel_id=1, source_target_pairs={{0,1},{1,0},{2,3},{3,2},{4,5},{5,4},{6,7},{7,6},{8,9},{9,8},{10,11... | collective-permute-start | bytes 393224 | tf_op jit(solution)/shard_map/ppermute | solution.py:356
  35.6 8.4 %collective-permute-start.19 = (bf16[2,256,128]{2,1,0:T(8,128)(2,1)S(1)}, bf16[2,256,128]{2,1,0:T(8,128)(2,1)S(1)}, u32[]{:S(2)}, u32[]{:S(2)}) collective-permute-start(bf16[2,256,128]{2,1,0:T(8,128)(2,1)S(1)} %get-tuple-element.38), channel_id=1, source_target_pairs={{0,4},{1,5},{2,6},{3,7},{4,0},{5,1},{6,2},{7,3},{8,12},{9,13},{10,... | collective-permute-start | bytes 393224 | tf_op jit(solution)/shard_map/ppermute | solution.py:356
  36.5 7.5 %collective-permute-start.20 = (bf16[2,256,128]{2,1,0:T(8,128)(2,1)S(1)}, bf16[2,256,128]{2,1,0:T(8,128)(2,1)S(1)}, u32[]{:S(2)}, u32[]{:S(2)}) collective-permute-start(bf16[2,256,128]{2,1,0:T(8,128)(2,1)S(1)} %get-tuple-element.39), channel_id=1, source_target_pairs={{0,5},{1,4},{2,7},{3,6},{4,1},{5,0},{6,3},{7,2},{8,13},{9,12},{10,... | collective-permute-start | bytes 393224 | tf_op jit(solution)/shard_map/ppermute | solution.py:356
  37.6 6.4 %collective-permute-start.14 = (bf16[2,2,64,128]{3,2,1,0:T(8,128)(2,1)S(1)}, bf16[2,2,64,128]{3,2,1,0:T(8,128)(2,1)S(1)}, u32[]{:S(2)}, u32[]{:S(2)}) collective-permute-start(bf16[2,2,64,128]{3,2,1,0:T(8,128)(2,1)S(1)} %pad_maximum_fusion.5), channel_id=1, source_target_pairs={{0,16},{8,24},{16,0},{24,8},{1,17},{9,25},{17,1},{25,9},{2,18},{10... | collective-permute-start | bytes 196616 | tf_op jit(solution)/shard_map/ppermute | solution.py:356
  39.7 4.5 %collective-permute-start.15 = (bf16[2,2,64,128]{3,2,1,0:T(8,128)(2,1)S(1)}, bf16[2,2,64,128]{3,2,1,0:T(8,128)(2,1)S(1)}, u32[]{:S(2)}, u32[]{:S(2)}) collective-permute-start(bf16[2,2,64,128]{3,2,1,0:T(8,128)(2,1)S(1)} %pad_maximum_fusion.6), channel_id=1, source_target_pairs={{0,8},{8,0},{16,24},{24,16},{1,9},{9,1},{17,25},{25,17},{2,10},{10... | collective-permute-start | bytes 196616 | tf_op jit(solution)/shard_map/ppermute | solution.py:356
  40.4 6.1 %collective-permute-start.16 = (bf16[2,2,64,128]{3,2,1,0:T(8,128)(2,1)S(1)}, bf16[2,2,64,128]{3,2,1,0:T(8,128)(2,1)S(1)}, u32[]{:S(2)}, u32[]{:S(2)}) collective-permute-start(bf16[2,2,64,128]{3,2,1,0:T(8,128)(2,1)S(1)} %pad_maximum_fusion.7), channel_id=1, source_target_pairs={{0,24},{8,16},{16,8},{24,0},{1,25},{9,17},{17,9},{25,1},{2,26},{10... | collective-permute-start | bytes 196616 | tf_op jit(solution)/shard_map/ppermute | solution.py:356
  46.5 4.0 %collective-permute-start.21 = (bf16[4,256,128]{2,1,0:T(8,128)(2,1)S(1)}, bf16[4,256,128]{2,1,0:T(8,128)(2,1)S(1)}, u32[]{:S(2)}, u32[]{:S(2)}) collective-permute-start(bf16[4,256,128]{2,1,0:T(8,128)(2,1)S(1)} %shard_map.111), channel_id=1, source_target_pairs={{0,2},{1,3},{2,0},{3,1},{4,6},{5,7},{6,4},{7,5},{8,10},{9,11},{10,... | collective-permute-start | bytes 786440 | tf_op jit(solution)/shard_map/ppermute | solution.py:356
  46.5 4.0 %collective-permute-start.17 = (bf16[2,64,128]{2,1,0:T(8,128)(2,1)S(1)}, bf16[2,64,128]{2,1,0:T(8,128)(2,1)S(1)}, u32[]{:S(2)}, u32[]{:S(2)}) collective-permute-start(bf16[2,64,128]{2,1,0:T(8,128)(2,1)S(1)} %get-tuple-element.35), channel_id=1, source_target_pairs={{0,4},{4,0},{1,5},{5,1},{2,6},{6,2},{3,7},{7,3},{8,12},{12,8},{9,1... | collective-permute-start | bytes 98312 | tf_op jit(solution)/shard_map/ppermute | solution.py:356

commit v15 on v14

--- a/solution.py
+++ b/solution.py
@@ -443,14 +443,10 @@
     slabs = swap_slabs(slabs, groups)
     own_block = jnp.concatenate([x[:DH] for x in slabs] + [sum(x[DH:] for x in slabs)], axis=0)
     pairs = swap_pairs(kv_keep, kv_send)
-    far = [1 << n for n in reversed(range(shift_of(parts)))]
-
-    blocks, came = [0], [own_block]
-    for d in far:
-        if d == 1:
-            came = came[:1] + [tie(x, pairs[1:3]) for x in came[1:]]
-        came = came + [swap(x, "part", d, parts) for x in came]
+    blocks = [0]
+    for d in [1 << n for n in reversed(range(shift_of(parts)))]:
         blocks = blocks + [b ^ d for b in blocks]
+    came = [swap(own_block, "part", b, parts) if b else own_block for b in blocks]
     ends, live = line_limits(parts, row_count, nears, rows, lines, resp_len, prompt_end)
 
     def part_lse(held, first, refs, before):

time: 51.7 us -> 54 us (1.044)
  waiting for transfers between devices: 13.7 us -> 18.1 us
  starting transfers between devices: 27.7 us -> 25.6 us
    ppermute x22, waiting for transfers between devices: 13.7 us -> 18.1 us  [swap(): return lax.ppermute(x, axis, [(i, i ^ distance) for i in range(size)])]
    ppermute x22, starting transfers between devices: 27.7 us -> 25.6 us  [swap(): return lax.ppermute(x, axis, [(i, i ^ distance) for i in range(size)])]
  transfers between devices with their start and end apart: 22 -> 22, of which waited for: 10 -> 9; matrix products, arithmetic and copies ran while one was open for 1% -> 1% of each run, Pallas kernels for 6% -> 6%
where the time goes in v15:
time: 54 us; the launch traced here: 53.8 us
  starting transfers between devices  25.6 us (47%)
  waiting for transfers between devices  18.1 us (34%)
  Pallas kernels  7.71 us (14%)
  between operations  2.15 us (4%)
    ppermute x22, starting transfers between devices, swap(): return lax.ppermute(x, axis, [(i, i ^ distance) for i in range(size)])  25.6 us
    ppermute x22, waiting for transfers between devices, swap(): return lax.ppermute(x, axis, [(i, i ^ distance) for i in range(size)])  18.1 us
    pallas_call x1, Pallas kernels, shards(): pl.pallas_call(functools.partial(part_kernel, blocks, nears, heads, token...  2.06 us
    pallas_call x2, Pallas kernels, part_lse(): pl.pallas_call(functools.partial(stat_kernel, held, first, nears, heads,...  1.78 us
    pallas_call x1, Pallas kernels, shards(): pl.pallas_call(functools.partial(token_kernel, blocks, nears, heads, toke...  1.49 us
    pallas_call x1, Pallas kernels, shards(): pl.pallas_call(functools.partial(pack_kernel, row_count, nears, heads), i...  1.38 us
  transfers between devices with their start and end apart: 22, of which 9 were waited for; matrix products, arithmetic and copies ran while one was open for 1% of the time, Pallas kernels for 6%

profile of v15, /device:TPU:0, one launch (start us, length us, event | category | flops | bytes accessed | tf_op | source)
XLA Modules:
  0.0 53.8 jit_solution(4587784572016121978)
XLA Ops:
  0.6 1.4 %shard_map.103 = (bf16[144,128]{1,0:T(8,128)(2,1)S(1)}, bf16[144,128]{1,0:T(8,128)(2,1)S(1)}, bf16[144,128]{1,0:T(8,128)(2,1)S(1)}, bf16[144,128]{1,0:T(8,128)(2...) custom-call(bf16[256,128]{1,0:T(8,128)(2,1)} %bitcast.24, bf16[256,128]{1,0:T(8,128)(2,1)} %bitcast.25, ...), custom_call_target="tpu_custom_call" | custom-call | tf_op jit(solution)/shard_map/pallas_call | solution.py:424
  2.0 0.5 collective-permute-start
  2.5 2.6 %collective-permute-start.1 = (bf16[144,128]{1,0:T(8,128)(2,1)S(1)}, bf16[144,128]{1,0:T(8,128)(2,1)S(1)}, u32[]{:S(2)}, u32[]{:S(2)}) collective-permute-start(bf16[144,128]{1,0:T(8,128)(2,1)S(1)} %get-tuple-element.25), channel_id=1, source_target_pairs={{0,4},{2,6},{4,0},{6,2},{1,5},{3,7},{5,1},{7,3},{8,12},{10,14},{12... | collective-permute-start | bytes 110600 | tf_op jit(solution)/shard_map/ppermute | solution.py:356
  5.1 0.1 collective-permute-start.2
  5.2 0.1 collective-permute-start.6
  6.0 0.0 collective-permute-done
  6.0 1.1 %collective-permute-done.1 = bf16[144,128]{1,0:T(8,128)(2,1)S(1)} collective-permute-done((bf16[144,128]{1,0:T(8,128)(2,1)S(1)}, bf16[144,128]{1,0:T(8,128)(2,1)S(1)}, u32[]{:S(2)}, u32[]{:S(2)}) %collective-permute-start.1) | collective-permute-done | bytes 36896 | tf_op jit(solution)/shard_map/ppermute | solution.py:356
  7.2 1.4 %collective-permute-done.2 = bf16[144,128]{1,0:T(8,128)(2,1)S(1)} collective-permute-done((bf16[144,128]{1,0:T(8,128)(2,1)S(1)}, bf16[144,128]{1,0:T(8,128)(2,1)S(1)}, u32[]{:S(2)}, u32[]{:S(2)}) %collective-permute-start.2) | collective-permute-done | bytes 36896 | tf_op jit(solution)/shard_map/ppermute | solution.py:356
  8.6 3.7 %collective-permute-start.5 = (bf16[528,128]{1,0:T(8,128)(2,1)S(1)}, bf16[528,128]{1,0:T(8,128)(2,1)S(1)}, u32[]{:S(2)}, u32[]{:S(2)}) collective-permute-start(bf16[528,128]{1,0:T(8,128)(2,1)S(1)} %constant_dynamic-update-slice_fusion.refs_0_), channel_id=1, source_target_pairs={{0,24},{8,16},{16,8},{24,0},{1,25},{9,17},{17,9},{25,1},{2,26},{10... | collective-permute-start | bytes 405512 | tf_op jit(solution)/shard_map/ppermute | solution.py:356
  12.2 0.0 collective-permute-start.4
  12.3 0.8 %collective-permute-start.3 = (bf16[528,128]{1,0:T(8,128)(2,1)S(1)}, bf16[528,128]{1,0:T(8,128)(2,1)S(1)}, u32[]{:S(2)}, u32[]{:S(2)}) collective-permute-start(bf16[528,128]{1,0:T(8,128)(2,1)S(1)} %constant_dynamic-update-slice_fusion.refs_0_), channel_id=1, source_target_pairs={{0,16},{8,24},{16,0},{24,8},{1,17},{9,25},{17,1},{25,9},{2,18},{10... | collective-permute-start | bytes 405512 | tf_op jit(solution)/shard_map/ppermute | solution.py:356
  13.0 0.0 collective-permute-done.6
  13.1 1.6 %collective-permute-start.7 = (bf16[2,256,128]{2,1,0:T(8,128)(2,1)S(1)}, bf16[2,256,128]{2,1,0:T(8,128)(2,1)S(1)}, u32[]{:S(2)}, u32[]{:S(2)}) collective-permute-start(bf16[2,256,128]{2,1,0:T(8,128)(2,1)S(1)} %pad_maximum_fusion.2), channel_id=1, source_target_pairs={{0,1},{1,0},{2,3},{3,2},{4,5},{5,4},{6,7},{7,6},{8,9},{9,8},{10,11... | collective-permute-start | bytes 393224 | tf_op jit(solution)/shard_map/ppermute | solution.py:356
  14.7 0.9 %collective-permute-start.8 = (bf16[2,256,128]{2,1,0:T(8,128)(2,1)S(1)}, bf16[2,256,128]{2,1,0:T(8,128)(2,1)S(1)}, u32[]{:S(2)}, u32[]{:S(2)}) collective-permute-start(bf16[2,256,128]{2,1,0:T(8,128)(2,1)S(1)} %pad_maximum_fusion.3), channel_id=1, source_target_pairs={{0,4},{1,5},{2,6},{3,7},{4,0},{5,1},{6,2},{7,3},{8,12},{9,13},{10,... | collective-permute-start | bytes 393224 | tf_op jit(solution)/shard_map/ppermute | solution.py:356
  15.6 4.5 %collective-permute-done.4.refs_2_ = bf16[528,128]{1,0:T(8,128)(2,1)S(1)} collective-permute-done((bf16[528,128]{1,0:T(8,128)(2,1)S(1)}, bf16[528,128]{1,0:T(8,128)(2,1)S(1)}, u32[]{:S(2)}, u32[]{:S(2)}) %collective-permute-start.4) | collective-permute-done | bytes 135200 | tf_op jit(solution)/shard_map/ppermute | solution.py:356
  20.2 1.8 %collective-permute-start.9 = (bf16[2,256,128]{2,1,0:T(8,128)(2,1)S(1)}, bf16[2,256,128]{2,1,0:T(8,128)(2,1)S(1)}, u32[]{:S(2)}, u32[]{:S(2)}) collective-permute-start(bf16[2,256,128]{2,1,0:T(8,128)(2,1)S(1)} %pad_maximum_fusion.4), channel_id=1, source_target_pairs={{0,5},{1,4},{2,7},{3,6},{4,1},{5,0},{6,3},{7,2},{8,13},{9,12},{10,... | collective-permute-start | bytes 393224 | tf_op jit(solution)/shard_map/ppermute | solution.py:356
  22.7 1.3 %collective-permute-done.3.refs_1_ = bf16[528,128]{1,0:T(8,128)(2,1)S(1)} collective-permute-done((bf16[528,128]{1,0:T(8,128)(2,1)S(1)}, bf16[528,128]{1,0:T(8,128)(2,1)S(1)}, u32[]{:S(2)}, u32[]{:S(2)}) %collective-permute-start.3) | collective-permute-done | bytes 135200 | tf_op jit(solution)/shard_map/ppermute | solution.py:356
  24.0 0.0 collective-permute-done.7.refs_4_.refs_2_.refs_5_
  24.0 0.0 collective-permute-done.8.refs_5_.refs_3_.refs_6_
  24.0 2.5 %collective-permute-done.9.refs_6_.refs_4_.refs_7_ = bf16[2,256,128]{2,1,0:T(8,128)(2,1)S(1)} collective-permute-done((bf16[2,256,128]{2,1,0:T(8,128)(2,1)S(1)}, bf16[2,256,128]{2,1,0:T(8,128)(2,1)S(1)}, u32[]{:S(2)}, u32[]{:S(2)}) %collective-permute-start.9) | collective-permute-done | bytes 131104 | tf_op jit(solution)/shard_map/ppermute | solution.py:356
  26.5 1.1 %shard_map.104.refs_1_.refs_5_ = f32[8,128]{1,0:T(8,128)S(1)} custom-call(s32[1,1024]{1,0:T(1,128)S(1)} %compare_select_fusion.ends_ref, bf16[528,128]{1,0:T(8,128)(2,1)S(1)} %constant_dynamic-update-slice_fusion.refs_0_, bf16[528,128]{1,0:T(8,128)(2,1)S(1)} %collective-permute-done.3.refs_1_, bf16[528,128]{1,0:T(8,128)(2,1)S(1)} %collective-permute-done.4.refs_2_, ...), custom_call_target="tpu_custom_call" | custom-call | tf_op jit(solution)/shard_map/pallas_call | solution.py:453
  27.6 0.0 collective-permute-done.5.refs_0_
  27.6 0.6 %shard_map.106.refs_8_.refs_7_ = f32[8,128]{1,0:T(8,128)S(1)} custom-call(s32[1,1024]{1,0:T(1,128)S(1)} %compare_select_fusion.ends_ref, bf16[528,128]{1,0:T(8,128)(2,1)S(1)} %shard_map.105.refs_0_.refs_3_, bf16[2,256,128]{2,1,0:T(8,128)(2,1)S(1)} %pad_maximum_fusion.1.refs_3_.refs_1_.refs_4_, ...), custom_call_target="tpu_custom_call" | custom-call | tf_op jit(solution)/shard_map/pallas_call | solution.py:453
  28.3 1.7 %collective-permute-start.12 = (f32[8,128]{1,0:T(8,128)S(1)}, f32[8,128]{1,0:T(8,128)S(1)}, u32[]{:S(2)}, u32[]{:S(2)}) collective-permute-start(f32[8,128]{1,0:T(8,128)S(1)} %shard_map.106.refs_8_.refs_7_), channel_id=1, source_target_pairs={{0,24},{8,16},{16,8},{24,0},{1,25},{9,17},{17,9},{25,1},{2,26},{10... | collective-permute-start | bytes 12296 | tf_op jit(solution)/shard_map/ppermute | solution.py:356
  30.0 0.8 %collective-permute-start.11 = (f32[8,128]{1,0:T(8,128)S(1)}, f32[8,128]{1,0:T(8,128)S(1)}, u32[]{:S(2)}, u32[]{:S(2)}) collective-permute-start(f32[8,128]{1,0:T(8,128)S(1)} %shard_map.106.refs_8_.refs_7_), channel_id=1, source_target_pairs={{0,16},{8,24},{16,0},{24,8},{1,17},{9,25},{17,1},{25,9},{2,18},{10... | collective-permute-start | bytes 12296 | tf_op jit(solution)/shard_map/ppermute | solution.py:356
  30.8 1.9 %collective-permute-start.10 = (f32[8,128]{1,0:T(8,128)S(1)}, f32[8,128]{1,0:T(8,128)S(1)}, u32[]{:S(2)}, u32[]{:S(2)}) collective-permute-start(f32[8,128]{1,0:T(8,128)S(1)} %shard_map.106.refs_8_.refs_7_), channel_id=1, source_target_pairs={{0,8},{8,0},{16,24},{24,16},{1,9},{9,1},{17,25},{25,17},{2,10},{10... | collective-permute-start | bytes 12296 | tf_op jit(solution)/shard_map/ppermute | solution.py:356
  32.8 2.1 %shard_map.107 = (bf16[4,256,1024]{2,1,0:T(8,128)(2,1)S(1)}, bf16[4,256,1024]{2,1,0:T(8,128)(2,1)S(1)}, f32[128,1024]{1,0:T(8,128)S(1)}) custom-call(s32[1,1024]{1,0:T(1,128)S(1)} %compare_select_fusion.ends_ref, bf16[528,128]{1,0:T(8,128)(2,1)S(1)} %constant_dynamic-update-slice_fusion.refs_0_, bf16[528,128]{1,0:T(8,128)(2,1)S(1)} %collective-permute-done.3.refs_1_, ...), custom_call_target="tpu_custom_call" | custom-call | tf_op jit(solution)/shard_map/pallas_call | solution.py:467
  34.8 0.0 collective-permute-done.12.refs_10_
  34.9 0.0 collective-permute-done.11.refs_9_
  34.9 0.0 collective-permute-done.10.refs_8_
  34.9 1.5 %shard_map.108 = (bf16[2,256,128]{2,1,0:T(8,128)(2,1)S(1)}, bf16[2,256,128]{2,1,0:T(8,128)(2,1)S(1)}, bf16[2,256,128]{2,1,0:T(8,128)(2,1)S(1)}, bf16[2,256,128]{...) custom-call(s32[1,1024]{1,0:T(1,128)S(1)} %compare_convert_fusion.live_ref, ...), custom_call_target="tpu_custom_call" | custom-call | tf_op jit(solution)/shard_map/pallas_call | solution.py:476
  36.4 0.1 collective-permute-start.13
  36.5 1.6 %collective-permute-start.18 = (bf16[2,256,128]{2,1,0:T(8,128)(2,1)S(1)}, bf16[2,256,128]{2,1,0:T(8,128)(2,1)S(1)}, u32[]{:S(2)}, u32[]{:S(2)}) collective-permute-start(bf16[2,256,128]{2,1,0:T(8,128)(2,1)S(1)} %get-tuple-element.37), channel_id=1, source_target_pairs={{0,1},{1,0},{2,3},{3,2},{4,5},{5,4},{6,7},{7,6},{8,9},{9,8},{10,11... | collective-permute-start | bytes 393224 | tf_op jit(solution)/shard_map/ppermute | solution.py:356
  38.0 0.9 %collective-permute-start.19 = (bf16[2,256,128]{2,1,0:T(8,128)(2,1)S(1)}, bf16[2,256,128]{2,1,0:T(8,128)(2,1)S(1)}, u32[]{:S(2)}, u32[]{:S(2)}) collective-permute-start(bf16[2,256,128]{2,1,0:T(8,128)(2,1)S(1)} %get-tuple-element.38), channel_id=1, source_target_pairs={{0,4},{1,5},{2,6},{3,7},{4,0},{5,1},{6,2},{7,3},{8,12},{9,13},{10,... | collective-permute-start | bytes 393224 | tf_op jit(solution)/shard_map/ppermute | solution.py:356
  38.9 1.1 %collective-permute-start.20 = (bf16[2,256,128]{2,1,0:T(8,128)(2,1)S(1)}, bf16[2,256,128]{2,1,0:T(8,128)(2,1)S(1)}, u32[]{:S(2)}, u32[]{:S(2)}) collective-permute-start(bf16[2,256,128]{2,1,0:T(8,128)(2,1)S(1)} %get-tuple-element.39), channel_id=1, source_target_pairs={{0,5},{1,4},{2,7},{3,6},{4,1},{5,0},{6,3},{7,2},{8,13},{9,12},{10,... | collective-permute-start | bytes 393224 | tf_op jit(solution)/shard_map/ppermute | solution.py:356
  40.0 0.0 collective-permute-done.13.refs_1_
  40.1 1.7 %collective-permute-start.14 = (bf16[2,2,64,128]{3,2,1,0:T(8,128)(2,1)S(1)}, bf16[2,2,64,128]{3,2,1,0:T(8,128)(2,1)S(1)}, u32[]{:S(2)}, u32[]{:S(2)}) collective-permute-start(bf16[2,2,64,128]{3,2,1,0:T(8,128)(2,1)S(1)} %pad_maximum_fusion.5), channel_id=1, source_target_pairs={{0,16},{8,24},{16,0},{24,8},{1,17},{9,25},{17,1},{25,9},{2,18},{10... | collective-permute-start | bytes 196616 | tf_op jit(solution)/shard_map/ppermute | solution.py:356
  41.8 0.8 %collective-permute-start.15 = (bf16[2,2,64,128]{3,2,1,0:T(8,128)(2,1)S(1)}, bf16[2,2,64,128]{3,2,1,0:T(8,128)(2,1)S(1)}, u32[]{:S(2)}, u32[]{:S(2)}) collective-permute-start(bf16[2,2,64,128]{3,2,1,0:T(8,128)(2,1)S(1)} %pad_maximum_fusion.6), channel_id=1, source_target_pairs={{0,8},{8,0},{16,24},{24,16},{1,9},{9,1},{17,25},{25,17},{2,10},{10... | collective-permute-start | bytes 196616 | tf_op jit(solution)/shard_map/ppermute | solution.py:356
  42.6 0.2 collective-permute-done.18.refs_3_
  42.7 1.9 %collective-permute-start.16 = (bf16[2,2,64,128]{3,2,1,0:T(8,128)(2,1)S(1)}, bf16[2,2,64,128]{3,2,1,0:T(8,128)(2,1)S(1)}, u32[]{:S(2)}, u32[]{:S(2)}) collective-permute-start(bf16[2,2,64,128]{3,2,1,0:T(8,128)(2,1)S(1)} %pad_maximum_fusion.7), channel_id=1, source_target_pairs={{0,24},{8,16},{16,8},{24,0},{1,25},{9,17},{17,9},{25,1},{2,26},{10... | collective-permute-start | bytes 196616 | tf_op jit(solution)/shard_map/ppermute | solution.py:356
  44.7 1.7 %collective-permute-done.19.refs_4_ = bf16[2,256,128]{2,1,0:T(8,128)(2,1)S(1)} collective-permute-done((bf16[2,256,128]{2,1,0:T(8,128)(2,1)S(1)}, bf16[2,256,128]{2,1,0:T(8,128)(2,1)S(1)}, u32[]{:S(2)}, u32[]{:S(2)}) %collective-permute-start.19) | collective-permute-done | bytes 131104 | tf_op jit(solution)/shard_map/ppermute | solution.py:356
  46.4 0.0 collective-permute-done.20.refs_5_
  46.5 0.0 collective-permute-done.14.refs_2_.refs_1_
  46.5 2.3 %collective-permute-done.16.refs_4_.refs_3_ = bf16[2,2,64,128]{3,2,1,0:T(8,128)(2,1)S(1)} collective-permute-done((bf16[2,2,64,128]{3,2,1,0:T(8,128)(2,1)S(1)}, bf16[2,2,64,128]{3,2,1,0:T(8,128)(2,1)S(1)}, u32[]{:S(2)}, u32[]{:S(2)}) %collective-permute-start.16) | collective-permute-done | bytes 65568 | tf_op jit(solution)/shard_map/ppermute | solution.py:356
  48.8 0.0 collective-permute-start.21
  48.9 1.0 %collective-permute-start.17 = (bf16[2,64,128]{2,1,0:T(8,128)(2,1)S(1)}, bf16[2,64,128]{2,1,0:T(8,128)(2,1)S(1)}, u32[]{:S(2)}, u32[]{:S(2)}) collective-permute-start(bf16[2,64,128]{2,1,0:T(8,128)(2,1)S(1)} %get-tuple-element.35), channel_id=1, source_target_pairs={{0,4},{4,0},{1,5},{5,1},{2,6},{6,2},{3,7},{7,3},{8,12},{12,8},{9,1... | collective-permute-start | bytes 98312 | tf_op jit(solution)/shard_map/ppermute | solution.py:356
  49.9 3.0 %collective-permute-done.17.refs_1_ = bf16[2,64,128]{2,1,0:T(8,128)(2,1)S(1)} collective-permute-done((bf16[2,64,128]{2,1,0:T(8,128)(2,1)S(1)}, bf16[2,64,128]{2,1,0:T(8,128)(2,1)S(1)}, u32[]{:S(2)}, u32[]{:S(2)}) %collective-permute-start.17) | collective-permute-done | bytes 32800 | tf_op jit(solution)/shard_map/ppermute | solution.py:356
  52.9 1.0 %shard_map.111 = (bf16[256,128]{1,0:T(8,128)(2,1)}, bf16[128,1024]{1,0:T(8,128)(2,1)}, bf16[128,1024]{1,0:T(8,128)(2,1)}) custom-call(bf16[2,64,128]{2,1,0:T(8,128)(2,1)S(1)} %get-tuple-element.34.refs_0_, bf16[2,64,128]{2,1,0:T(8,128)(2,1)S(1)} %collective-permute-done.17.refs_1_, bf16[2,256,128]{2,1,0:T(8,128)(2,1)S(1)} %get-tuple-element.36.refs_2_, ...), custom_call_target="tpu_custom_call" | custom-call | tf_op jit(solution)/shard_map/pallas_call | solution.py:498
  (28 shorter events, 0.4 us)
Async XLA Ops:
  2.0 4.0 %collective-permute-start = (bf16[144,128]{1,0:T(8,128)(2,1)S(1)}, bf16[144,128]{1,0:T(8,128)(2,1)S(1)}, u32[]{:S(2)}, u32[]{:S(2)}) collective-permute-start(bf16[144,128]{1,0:T(8,128)(2,1)S(1)} %get-tuple-element.24), channel_id=1, source_target_pairs={{0,2},{2,0},{4,6},{6,4},{1,3},{3,1},{5,7},{7,5},{8,10},{10,8},{12,... | collective-permute-start | bytes 110600 | tf_op jit(solution)/shard_map/ppermute | solution.py:356
  2.5 4.7 %collective-permute-start.1 = (bf16[144,128]{1,0:T(8,128)(2,1)S(1)}, bf16[144,128]{1,0:T(8,128)(2,1)S(1)}, u32[]{:S(2)}, u32[]{:S(2)}) collective-permute-start(bf16[144,128]{1,0:T(8,128)(2,1)S(1)} %get-tuple-element.25), channel_id=1, source_target_pairs={{0,4},{2,6},{4,0},{6,2},{1,5},{3,7},{5,1},{7,3},{8,12},{10,14},{12... | collective-permute-start | bytes 110600 | tf_op jit(solution)/shard_map/ppermute | solution.py:356
  5.1 3.4 %collective-permute-start.2 = (bf16[144,128]{1,0:T(8,128)(2,1)S(1)}, bf16[144,128]{1,0:T(8,128)(2,1)S(1)}, u32[]{:S(2)}, u32[]{:S(2)}) collective-permute-start(bf16[144,128]{1,0:T(8,128)(2,1)S(1)} %get-tuple-element.26), channel_id=1, source_target_pairs={{0,6},{2,4},{4,2},{6,0},{1,7},{3,5},{5,3},{7,1},{8,14},{10,12},{12... | collective-permute-start | bytes 110600 | tf_op jit(solution)/shard_map/ppermute | solution.py:356
  5.2 7.8 %collective-permute-start.6 = (bf16[4,256,128]{2,1,0:T(8,128)(2,1)S(1)}, bf16[4,256,128]{2,1,0:T(8,128)(2,1)S(1)}, u32[]{:S(2)}, u32[]{:S(2)}) collective-permute-start(bf16[4,256,128]{2,1,0:T(8,128)(2,1)S(1)} %get-tuple-element.28), channel_id=1, source_target_pairs={{0,2},{1,3},{2,0},{3,1},{4,6},{5,7},{6,4},{7,5},{8,10},{9,11},{10,... | collective-permute-start | bytes 786440 | tf_op jit(solution)/shard_map/ppermute | solution.py:356
  8.6 19.0 %collective-permute-start.5 = (bf16[528,128]{1,0:T(8,128)(2,1)S(1)}, bf16[528,128]{1,0:T(8,128)(2,1)S(1)}, u32[]{:S(2)}, u32[]{:S(2)}) collective-permute-start(bf16[528,128]{1,0:T(8,128)(2,1)S(1)} %constant_dynamic-update-slice_fusion.refs_0_), channel_id=1, source_target_pairs={{0,24},{8,16},{16,8},{24,0},{1,25},{9,17},{17,9},{25,1},{2,26},{10... | collective-permute-start | bytes 405512 | tf_op jit(solution)/shard_map/ppermute | solution.py:356
  12.2 7.9 %collective-permute-start.4 = (bf16[528,128]{1,0:T(8,128)(2,1)S(1)}, bf16[528,128]{1,0:T(8,128)(2,1)S(1)}, u32[]{:S(2)}, u32[]{:S(2)}) collective-permute-start(bf16[528,128]{1,0:T(8,128)(2,1)S(1)} %constant_dynamic-update-slice_fusion.refs_0_), channel_id=1, source_target_pairs={{0,8},{8,0},{16,24},{24,16},{1,9},{9,1},{17,25},{25,17},{2,10},{10... | collective-permute-start | bytes 405512 | tf_op jit(solution)/shard_map/ppermute | solution.py:356
  12.3 11.8 %collective-permute-start.3 = (bf16[528,128]{1,0:T(8,128)(2,1)S(1)}, bf16[528,128]{1,0:T(8,128)(2,1)S(1)}, u32[]{:S(2)}, u32[]{:S(2)}) collective-permute-start(bf16[528,128]{1,0:T(8,128)(2,1)S(1)} %constant_dynamic-update-slice_fusion.refs_0_), channel_id=1, source_target_pairs={{0,16},{8,24},{16,0},{24,8},{1,17},{9,25},{17,1},{25,9},{2,18},{10... | collective-permute-start | bytes 405512 | tf_op jit(solution)/shard_map/ppermute | solution.py:356
  13.1 10.9 %collective-permute-start.7 = (bf16[2,256,128]{2,1,0:T(8,128)(2,1)S(1)}, bf16[2,256,128]{2,1,0:T(8,128)(2,1)S(1)}, u32[]{:S(2)}, u32[]{:S(2)}) collective-permute-start(bf16[2,256,128]{2,1,0:T(8,128)(2,1)S(1)} %pad_maximum_fusion.2), channel_id=1, source_target_pairs={{0,1},{1,0},{2,3},{3,2},{4,5},{5,4},{6,7},{7,6},{8,9},{9,8},{10,11... | collective-permute-start | bytes 393224 | tf_op jit(solution)/shard_map/ppermute | solution.py:356
  14.7 9.4 %collective-permute-start.8 = (bf16[2,256,128]{2,1,0:T(8,128)(2,1)S(1)}, bf16[2,256,128]{2,1,0:T(8,128)(2,1)S(1)}, u32[]{:S(2)}, u32[]{:S(2)}) collective-permute-start(bf16[2,256,128]{2,1,0:T(8,128)(2,1)S(1)} %pad_maximum_fusion.3), channel_id=1, source_target_pairs={{0,4},{1,5},{2,6},{3,7},{4,0},{5,1},{6,2},{7,3},{8,12},{9,13},{10,... | collective-permute-start | bytes 393224 | tf_op jit(solution)/shard_map/ppermute | solution.py:356
  20.2 6.3 %collective-permute-start.9 = (bf16[2,256,128]{2,1,0:T(8,128)(2,1)S(1)}, bf16[2,256,128]{2,1,0:T(8,128)(2,1)S(1)}, u32[]{:S(2)}, u32[]{:S(2)}) collective-permute-start(bf16[2,256,128]{2,1,0:T(8,128)(2,1)S(1)} %pad_maximum_fusion.4), channel_id=1, source_target_pairs={{0,5},{1,4},{2,7},{3,6},{4,1},{5,0},{6,3},{7,2},{8,13},{9,12},{10,... | collective-permute-start | bytes 393224 | tf_op jit(solution)/shard_map/ppermute | solution.py:356
  28.3 6.6 %collective-permute-start.12 = (f32[8,128]{1,0:T(8,128)S(1)}, f32[8,128]{1,0:T(8,128)S(1)}, u32[]{:S(2)}, u32[]{:S(2)}) collective-permute-start(f32[8,128]{1,0:T(8,128)S(1)} %shard_map.106.refs_8_.refs_7_), channel_id=1, source_target_pairs={{0,24},{8,16},{16,8},{24,0},{1,25},{9,17},{17,9},{25,1},{2,26},{10... | collective-permute-start | bytes 12296 | tf_op jit(solution)/shard_map/ppermute | solution.py:356
  30.0 4.9 %collective-permute-start.11 = (f32[8,128]{1,0:T(8,128)S(1)}, f32[8,128]{1,0:T(8,128)S(1)}, u32[]{:S(2)}, u32[]{:S(2)}) collective-permute-start(f32[8,128]{1,0:T(8,128)S(1)} %shard_map.106.refs_8_.refs_7_), channel_id=1, source_target_pairs={{0,16},{8,24},{16,0},{24,8},{1,17},{9,25},{17,1},{25,9},{2,18},{10... | collective-permute-start | bytes 12296 | tf_op jit(solution)/shard_map/ppermute | solution.py:356
  30.8 4.0 %collective-permute-start.10 = (f32[8,128]{1,0:T(8,128)S(1)}, f32[8,128]{1,0:T(8,128)S(1)}, u32[]{:S(2)}, u32[]{:S(2)}) collective-permute-start(f32[8,128]{1,0:T(8,128)S(1)} %shard_map.106.refs_8_.refs_7_), channel_id=1, source_target_pairs={{0,8},{8,0},{16,24},{24,16},{1,9},{9,1},{17,25},{25,17},{2,10},{10... | collective-permute-start | bytes 12296 | tf_op jit(solution)/shard_map/ppermute | solution.py:356
  36.4 3.6 %collective-permute-start.13 = (bf16[4,2,64,128]{3,2,1,0:T(8,128)(2,1)S(1)}, bf16[4,2,64,128]{3,2,1,0:T(8,128)(2,1)S(1)}, u32[]{:S(2)}, u32[]{:S(2)}) collective-permute-start(bf16[4,2,64,128]{3,2,1,0:T(8,128)(2,1)S(1)} %get-tuple-element.33), channel_id=1, source_target_pairs={{0,2},{2,0},{1,3},{3,1},{4,6},{6,4},{5,7},{7,5},{8,10},{10,8},{9,1... | collective-permute-start | bytes 393224 | tf_op jit(solution)/shard_map/ppermute | solution.py:356
  36.5 6.3 %collective-permute-start.18 = (bf16[2,256,128]{2,1,0:T(8,128)(2,1)S(1)}, bf16[2,256,128]{2,1,0:T(8,128)(2,1)S(1)}, u32[]{:S(2)}, u32[]{:S(2)}) collective-permute-start(bf16[2,256,128]{2,1,0:T(8,128)(2,1)S(1)} %get-tuple-element.37), channel_id=1, source_target_pairs={{0,1},{1,0},{2,3},{3,2},{4,5},{5,4},{6,7},{7,6},{8,9},{9,8},{10,11... | collective-permute-start | bytes 393224 | tf_op jit(solution)/shard_map/ppermute | solution.py:356
  38.0 8.4 %collective-permute-start.19 = (bf16[2,256,128]{2,1,0:T(8,128)(2,1)S(1)}, bf16[2,256,128]{2,1,0:T(8,128)(2,1)S(1)}, u32[]{:S(2)}, u32[]{:S(2)}) collective-permute-start(bf16[2,256,128]{2,1,0:T(8,128)(2,1)S(1)} %get-tuple-element.38), channel_id=1, source_target_pairs={{0,4},{1,5},{2,6},{3,7},{4,0},{5,1},{6,2},{7,3},{8,12},{9,13},{10,... | collective-permute-start | bytes 393224 | tf_op jit(solution)/shard_map/ppermute | solution.py:356
  38.9 7.5 %collective-permute-start.20 = (bf16[2,256,128]{2,1,0:T(8,128)(2,1)S(1)}, bf16[2,256,128]{2,1,0:T(8,128)(2,1)S(1)}, u32[]{:S(2)}, u32[]{:S(2)}) collective-permute-start(bf16[2,256,128]{2,1,0:T(8,128)(2,1)S(1)} %get-tuple-element.39), channel_id=1, source_target_pairs={{0,5},{1,4},{2,7},{3,6},{4,1},{5,0},{6,3},{7,2},{8,13},{9,12},{10,... | collective-permute-start | bytes 393224 | tf_op jit(solution)/shard_map/ppermute | solution.py:356
  40.1 6.4 %collective-permute-start.14 = (bf16[2,2,64,128]{3,2,1,0:T(8,128)(2,1)S(1)}, bf16[2,2,64,128]{3,2,1,0:T(8,128)(2,1)S(1)}, u32[]{:S(2)}, u32[]{:S(2)}) collective-permute-start(bf16[2,2,64,128]{3,2,1,0:T(8,128)(2,1)S(1)} %pad_maximum_fusion.5), channel_id=1, source_target_pairs={{0,16},{8,24},{16,0},{24,8},{1,17},{9,25},{17,1},{25,9},{2,18},{10... | collective-permute-start | bytes 196616 | tf_op jit(solution)/shard_map/ppermute | solution.py:356
  41.8 4.7 %collective-permute-start.15 = (bf16[2,2,64,128]{3,2,1,0:T(8,128)(2,1)S(1)}, bf16[2,2,64,128]{3,2,1,0:T(8,128)(2,1)S(1)}, u32[]{:S(2)}, u32[]{:S(2)}) collective-permute-start(bf16[2,2,64,128]{3,2,1,0:T(8,128)(2,1)S(1)} %pad_maximum_fusion.6), channel_id=1, source_target_pairs={{0,8},{8,0},{16,24},{24,16},{1,9},{9,1},{17,25},{25,17},{2,10},{10... | collective-permute-start | bytes 196616 | tf_op jit(solution)/shard_map/ppermute | solution.py:356
  42.7 6.1 %collective-permute-start.16 = (bf16[2,2,64,128]{3,2,1,0:T(8,128)(2,1)S(1)}, bf16[2,2,64,128]{3,2,1,0:T(8,128)(2,1)S(1)}, u32[]{:S(2)}, u32[]{:S(2)}) collective-permute-start(bf16[2,2,64,128]{3,2,1,0:T(8,128)(2,1)S(1)} %pad_maximum_fusion.7), channel_id=1, source_target_pairs={{0,24},{8,16},{16,8},{24,0},{1,25},{9,17},{17,9},{25,1},{2,26},{10... | collective-permute-start | bytes 196616 | tf_op jit(solution)/shard_map/ppermute | solution.py:356
  48.8 4.0 %collective-permute-start.21 = (bf16[4,256,128]{2,1,0:T(8,128)(2,1)S(1)}, bf16[4,256,128]{2,1,0:T(8,128)(2,1)S(1)}, u32[]{:S(2)}, u32[]{:S(2)}) collective-permute-start(bf16[4,256,128]{2,1,0:T(8,128)(2,1)S(1)} %shard_map.110), channel_id=1, source_target_pairs={{0,2},{1,3},{2,0},{3,1},{4,6},{5,7},{6,4},{7,5},{8,10},{9,11},{10,... | collective-permute-start | bytes 786440 | tf_op jit(solution)/shard_map/ppermute | solution.py:356
  48.9 4.0 %collective-permute-start.17 = (bf16[2,64,128]{2,1,0:T(8,128)(2,1)S(1)}, bf16[2,64,128]{2,1,0:T(8,128)(2,1)S(1)}, u32[]{:S(2)}, u32[]{:S(2)}) collective-permute-start(bf16[2,64,128]{2,1,0:T(8,128)(2,1)S(1)} %get-tuple-element.35), channel_id=1, source_target_pairs={{0,4},{4,0},{1,5},{5,1},{2,6},{6,2},{3,7},{7,3},{8,12},{12,8},{9,1... | collective-permute-start | bytes 98312 | tf_op jit(solution)/shard_map/ppermute | solution.py:356

commit v16 on v14

--- a/solution.py
+++ b/solution.py
@@ -488,7 +488,8 @@
     dkv, dq = outs[: len(KEEP)], outs[len(KEEP) :]
     dq = [swap(x, "near", n, nears) if n else x for n, x in enumerate(dq)]
     from_parts = [
-        swap(jnp.stack([x[at] for x in dq]), "part", b, parts) for at, b in enumerate(blocks) if b
+        swap(jnp.stack([x[blocks.index(b)] for x in dq]), "part", b, parts)
+        for b in range(parts - 1, 0, -1)
     ]
     sum_shape = jax.ShapeDtypeStruct((nears, lines, DH), jnp.bfloat16)
     sums = pl.pallas_call(

time: 51.7 us -> 51.4 us (level)
    ppermute x22, starting transfers between devices: 27.7 us -> 27.2 us  [swap(): return lax.ppermute(x, axis, [(i, i ^ distance) for i in range(size)])]
  transfers between devices with their start and end apart: 22 -> 22, of which waited for: 10 -> 11; matrix products, arithmetic and copies ran while one was open for 1% -> 1% of each run, Pallas kernels for 6% -> 6%
where the time goes in v16:
time: 51.4 us; the launch traced here: 51.2 us
  starting transfers between devices  27.2 us (53%)
  waiting for transfers between devices  13.9 us (27%)
  Pallas kernels  7.66 us (15%)
  between operations  2.12 us (4%)
    ppermute x22, starting transfers between devices, swap(): return lax.ppermute(x, axis, [(i, i ^ distance) for i in range(size)])  27.2 us
    ppermute x22, waiting for transfers between devices, swap(): return lax.ppermute(x, axis, [(i, i ^ distance) for i in range(size)])  13.9 us
    pallas_call x1, Pallas kernels, shards(): pl.pallas_call(functools.partial(part_kernel, blocks, nears, heads, token...  2.05 us
    pallas_call x2, Pallas kernels, part_lse(): pl.pallas_call(functools.partial(stat_kernel, held, first, nears, heads,...  1.76 us
    pallas_call x1, Pallas kernels, shards(): pl.pallas_call(functools.partial(token_kernel, blocks, nears, heads, toke...  1.46 us
    pallas_call x1, Pallas kernels, shards(): pl.pallas_call(functools.partial(pack_kernel, row_count, nears, heads), i...  1.38 us
  transfers between devices with their start and end apart: 22, of which 11 were waited for; matrix products, arithmetic and copies ran while one was open for 1% of the time, Pallas kernels for 6%

profile of v16, /device:TPU:0, one launch (start us, length us, event | category | flops | bytes accessed | tf_op | source)
XLA Modules:
  0.0 51.2 jit_solution(12321510531994165008)
XLA Ops:
  0.6 1.4 %shard_map.103 = (bf16[144,128]{1,0:T(8,128)(2,1)S(1)}, bf16[144,128]{1,0:T(8,128)(2,1)S(1)}, bf16[144,128]{1,0:T(8,128)(2,1)S(1)}, bf16[144,128]{1,0:T(8,128)(2...) custom-call(bf16[256,128]{1,0:T(8,128)(2,1)} %bitcast.24, bf16[256,128]{1,0:T(8,128)(2,1)} %bitcast.25, ...), custom_call_target="tpu_custom_call" | custom-call | tf_op jit(solution)/shard_map/pallas_call | solution.py:424
  2.0 0.5 %collective-permute-start = (bf16[144,128]{1,0:T(8,128)(2,1)S(1)}, bf16[144,128]{1,0:T(8,128)(2,1)S(1)}, u32[]{:S(2)}, u32[]{:S(2)}) collective-permute-start(bf16[144,128]{1,0:T(8,128)(2,1)S(1)} %get-tuple-element.24), channel_id=1, source_target_pairs={{0,2},{2,0},{4,6},{6,4},{1,3},{3,1},{5,7},{7,5},{8,10},{10,8},{12,... | collective-permute-start | bytes 110600 | tf_op jit(solution)/shard_map/ppermute | solution.py:356
  2.5 2.6 %collective-permute-start.1 = (bf16[144,128]{1,0:T(8,128)(2,1)S(1)}, bf16[144,128]{1,0:T(8,128)(2,1)S(1)}, u32[]{:S(2)}, u32[]{:S(2)}) collective-permute-start(bf16[144,128]{1,0:T(8,128)(2,1)S(1)} %get-tuple-element.25), channel_id=1, source_target_pairs={{0,4},{2,6},{4,0},{6,2},{1,5},{3,7},{5,1},{7,3},{8,12},{10,14},{12... | collective-permute-start | bytes 110600 | tf_op jit(solution)/shard_map/ppermute | solution.py:356
  5.1 0.1 collective-permute-start.2
  5.2 0.1 collective-permute-start.4
  5.4 0.0 collective-permute-done
  5.4 1.8 %collective-permute-done.1 = bf16[144,128]{1,0:T(8,128)(2,1)S(1)} collective-permute-done((bf16[144,128]{1,0:T(8,128)(2,1)S(1)}, bf16[144,128]{1,0:T(8,128)(2,1)S(1)}, u32[]{:S(2)}, u32[]{:S(2)}) %collective-permute-start.1) | collective-permute-done | bytes 36896 | tf_op jit(solution)/shard_map/ppermute | solution.py:356
  7.2 1.4 %collective-permute-done.2 = bf16[144,128]{1,0:T(8,128)(2,1)S(1)} collective-permute-done((bf16[144,128]{1,0:T(8,128)(2,1)S(1)}, bf16[144,128]{1,0:T(8,128)(2,1)S(1)}, u32[]{:S(2)}, u32[]{:S(2)}) %collective-permute-start.2) | collective-permute-done | bytes 36896 | tf_op jit(solution)/shard_map/ppermute | solution.py:356
  8.6 2.7 %collective-permute-start.3 = (bf16[528,128]{1,0:T(8,128)(2,1)S(1)}, bf16[528,128]{1,0:T(8,128)(2,1)S(1)}, u32[]{:S(2)}, u32[]{:S(2)}) collective-permute-start(bf16[528,128]{1,0:T(8,128)(2,1)S(1)} %constant_dynamic-update-slice_fusion.refs_0_), channel_id=1, source_target_pairs={{0,16},{8,24},{16,0},{24,8},{1,17},{9,25},{17,1},{25,9},{2,18},{10... | collective-permute-start | bytes 405512 | tf_op jit(solution)/shard_map/ppermute | solution.py:356
  11.2 0.0 collective-permute-done.4
  11.3 1.6 %collective-permute-start.5 = (bf16[2,256,128]{2,1,0:T(8,128)(2,1)S(1)}, bf16[2,256,128]{2,1,0:T(8,128)(2,1)S(1)}, u32[]{:S(2)}, u32[]{:S(2)}) collective-permute-start(bf16[2,256,128]{2,1,0:T(8,128)(2,1)S(1)} %pad_maximum_fusion.1), channel_id=1, source_target_pairs={{0,1},{1,0},{2,3},{3,2},{4,5},{5,4},{6,7},{7,6},{8,9},{9,8},{10,11... | collective-permute-start | bytes 393224 | tf_op jit(solution)/shard_map/ppermute | solution.py:356
  12.9 0.9 %collective-permute-start.6 = (bf16[2,256,128]{2,1,0:T(8,128)(2,1)S(1)}, bf16[2,256,128]{2,1,0:T(8,128)(2,1)S(1)}, u32[]{:S(2)}, u32[]{:S(2)}) collective-permute-start(bf16[2,256,128]{2,1,0:T(8,128)(2,1)S(1)} %pad_maximum_fusion.2), channel_id=1, source_target_pairs={{0,4},{1,5},{2,6},{3,7},{4,0},{5,1},{6,2},{7,3},{8,12},{9,13},{10,... | collective-permute-start | bytes 393224 | tf_op jit(solution)/shard_map/ppermute | solution.py:356
  14.5 1.6 %collective-permute-start.7 = (bf16[528,128]{1,0:T(8,128)(2,1)S(1)}, bf16[528,128]{1,0:T(8,128)(2,1)S(1)}, u32[]{:S(2)}, u32[]{:S(2)}) collective-permute-start(bf16[528,128]{1,0:T(8,128)(2,1)S(1)} %constant_dynamic-update-slice_fusion.refs_0_), channel_id=1, source_target_pairs={{0,8},{8,0},{16,24},{24,16},{1,9},{9,1},{17,25},{25,17},{2,10},{10... | collective-permute-start | bytes 405512 | tf_op jit(solution)/shard_map/ppermute | solution.py:356
  16.1 1.2 %collective-permute-start.9 = (bf16[2,256,128]{2,1,0:T(8,128)(2,1)S(1)}, bf16[2,256,128]{2,1,0:T(8,128)(2,1)S(1)}, u32[]{:S(2)}, u32[]{:S(2)}) collective-permute-start(bf16[2,256,128]{2,1,0:T(8,128)(2,1)S(1)} %pad_maximum_fusion.4), channel_id=1, source_target_pairs={{0,5},{1,4},{2,7},{3,6},{4,1},{5,0},{6,3},{7,2},{8,13},{9,12},{10,... | collective-permute-start | bytes 393224 | tf_op jit(solution)/shard_map/ppermute | solution.py:356
  17.3 0.9 %collective-permute-done.3.refs_0_ = bf16[528,128]{1,0:T(8,128)(2,1)S(1)} collective-permute-done((bf16[528,128]{1,0:T(8,128)(2,1)S(1)}, bf16[528,128]{1,0:T(8,128)(2,1)S(1)}, u32[]{:S(2)}, u32[]{:S(2)}) %collective-permute-start.3) | collective-permute-done | bytes 135200 | tf_op jit(solution)/shard_map/ppermute | solution.py:356
  18.2 0.0 collective-permute-done.5.refs_1_.refs_4_.refs_2_.refs_5_
  18.2 0.0 collective-permute-done.6.refs_2_.refs_5_.refs_3_.refs_6_
  18.2 2.7 %collective-permute-start.8 = (bf16[528,128]{1,0:T(8,128)(2,1)S(1)}, bf16[528,128]{1,0:T(8,128)(2,1)S(1)}, u32[]{:S(2)}, u32[]{:S(2)}) collective-permute-start(bf16[528,128]{1,0:T(8,128)(2,1)S(1)} %shard_map.104.refs_1_), channel_id=1, source_target_pairs={{0,8},{8,0},{16,24},{24,16},{1,9},{9,1},{17,25},{25,17},{2,10},{10... | collective-permute-start | bytes 405512 | tf_op jit(solution)/shard_map/ppermute | solution.py:356
  21.6 0.0 collective-permute-done.7.refs_2_
  21.6 0.4 collective-permute-done.9.refs_6_.refs_4_.refs_7_
  22.0 1.1 %shard_map.105.refs_1_.refs_5_ = f32[8,128]{1,0:T(8,128)S(1)} custom-call(s32[1,1024]{1,0:T(1,128)S(1)} %compare_select_fusion.ends_ref, bf16[528,128]{1,0:T(8,128)(2,1)S(1)} %constant_dynamic-update-slice_fusion.refs_0_, bf16[528,128]{1,0:T(8,128)(2,1)S(1)} %shard_map.104.refs_1_, bf16[528,128]{1,0:T(8,128)(2,1)S(1)} %collective-permute-done.7.refs_2_, ...), custom_call_target="tpu_custom_call" | custom-call | tf_op jit(solution)/shard_map/pallas_call | solution.py:457
  23.2 0.7 %collective-permute-done.8.refs_0_ = bf16[528,128]{1,0:T(8,128)(2,1)S(1)} collective-permute-done((bf16[528,128]{1,0:T(8,128)(2,1)S(1)}, bf16[528,128]{1,0:T(8,128)(2,1)S(1)}, u32[]{:S(2)}, u32[]{:S(2)}) %collective-permute-start.8) | collective-permute-done | bytes 135200 | tf_op jit(solution)/shard_map/ppermute | solution.py:356
  23.9 0.6 %shard_map.107.refs_8_.refs_7_ = f32[8,128]{1,0:T(8,128)S(1)} custom-call(s32[1,1024]{1,0:T(1,128)S(1)} %compare_select_fusion.ends_ref, bf16[528,128]{1,0:T(8,128)(2,1)S(1)} %shard_map.106.refs_0_.refs_3_, bf16[2,256,128]{2,1,0:T(8,128)(2,1)S(1)} %pad_maximum_fusion.3.refs_3_.refs_1_.refs_4_, ...), custom_call_target="tpu_custom_call" | custom-call | tf_op jit(solution)/shard_map/pallas_call | solution.py:457
  24.6 3.4 %collective-permute-start.12 = (f32[8,128]{1,0:T(8,128)S(1)}, f32[8,128]{1,0:T(8,128)S(1)}, u32[]{:S(2)}, u32[]{:S(2)}) collective-permute-start(f32[8,128]{1,0:T(8,128)S(1)} %shard_map.107.refs_8_.refs_7_), channel_id=1, source_target_pairs={{0,24},{8,16},{16,8},{24,0},{1,25},{9,17},{17,9},{25,1},{2,26},{10... | collective-permute-start | bytes 12296 | tf_op jit(solution)/shard_map/ppermute | solution.py:356
  27.9 0.2 collective-permute-start.11
  28.1 0.9 %collective-permute-start.10 = (f32[8,128]{1,0:T(8,128)S(1)}, f32[8,128]{1,0:T(8,128)S(1)}, u32[]{:S(2)}, u32[]{:S(2)}) collective-permute-start(f32[8,128]{1,0:T(8,128)S(1)} %shard_map.107.refs_8_.refs_7_), channel_id=1, source_target_pairs={{0,8},{8,0},{16,24},{24,16},{1,9},{9,1},{17,25},{25,17},{2,10},{10... | collective-permute-start | bytes 12296 | tf_op jit(solution)/shard_map/ppermute | solution.py:356
  29.0 2.1 %shard_map.108 = (bf16[4,256,1024]{2,1,0:T(8,128)(2,1)S(1)}, bf16[4,256,1024]{2,1,0:T(8,128)(2,1)S(1)}, f32[128,1024]{1,0:T(8,128)S(1)}) custom-call(s32[1,1024]{1,0:T(1,128)S(1)} %compare_select_fusion.ends_ref, bf16[528,128]{1,0:T(8,128)(2,1)S(1)} %constant_dynamic-update-slice_fusion.refs_0_, bf16[528,128]{1,0:T(8,128)(2,1)S(1)} %shard_map.104.refs_1_, ...), custom_call_target="tpu_custom_call" | custom-call | tf_op jit(solution)/shard_map/pallas_call | solution.py:471
  31.1 0.0 collective-permute-done.12.refs_10_
  31.1 1.3 %collective-permute-done.11.refs_9_ = f32[8,128]{1,0:T(8,128)S(1)} collective-permute-done((f32[8,128]{1,0:T(8,128)S(1)}, f32[8,128]{1,0:T(8,128)S(1)}, u32[]{:S(2)}, u32[]{:S(2)}) %collective-permute-start.11) | collective-permute-done | bytes 4128 | tf_op jit(solution)/shard_map/ppermute | solution.py:356
  32.5 0.0 collective-permute-done.10.refs_8_
  32.5 1.5 %shard_map.109 = (bf16[2,256,128]{2,1,0:T(8,128)(2,1)S(1)}, bf16[2,256,128]{2,1,0:T(8,128)(2,1)S(1)}, bf16[2,256,128]{2,1,0:T(8,128)(2,1)S(1)}, bf16[2,256,128]{...) custom-call(s32[1,1024]{1,0:T(1,128)S(1)} %compare_convert_fusion.live_ref, ...), custom_call_target="tpu_custom_call" | custom-call | tf_op jit(solution)/shard_map/pallas_call | solution.py:480
  33.9 0.1 collective-permute-start.13
  34.0 1.6 %collective-permute-start.18 = (bf16[2,256,128]{2,1,0:T(8,128)(2,1)S(1)}, bf16[2,256,128]{2,1,0:T(8,128)(2,1)S(1)}, u32[]{:S(2)}, u32[]{:S(2)}) collective-permute-start(bf16[2,256,128]{2,1,0:T(8,128)(2,1)S(1)} %get-tuple-element.37), channel_id=1, source_target_pairs={{0,1},{1,0},{2,3},{3,2},{4,5},{5,4},{6,7},{7,6},{8,9},{9,8},{10,11... | collective-permute-start | bytes 393224 | tf_op jit(solution)/shard_map/ppermute | solution.py:356
  35.6 0.9 %collective-permute-start.19 = (bf16[2,256,128]{2,1,0:T(8,128)(2,1)S(1)}, bf16[2,256,128]{2,1,0:T(8,128)(2,1)S(1)}, u32[]{:S(2)}, u32[]{:S(2)}) collective-permute-start(bf16[2,256,128]{2,1,0:T(8,128)(2,1)S(1)} %get-tuple-element.38), channel_id=1, source_target_pairs={{0,4},{1,5},{2,6},{3,7},{4,0},{5,1},{6,2},{7,3},{8,12},{9,13},{10,... | collective-permute-start | bytes 393224 | tf_op jit(solution)/shard_map/ppermute | solution.py:356
  36.5 1.1 %collective-permute-start.20 = (bf16[2,256,128]{2,1,0:T(8,128)(2,1)S(1)}, bf16[2,256,128]{2,1,0:T(8,128)(2,1)S(1)}, u32[]{:S(2)}, u32[]{:S(2)}) collective-permute-start(bf16[2,256,128]{2,1,0:T(8,128)(2,1)S(1)} %get-tuple-element.39), channel_id=1, source_target_pairs={{0,5},{1,4},{2,7},{3,6},{4,1},{5,0},{6,3},{7,2},{8,13},{9,12},{10,... | collective-permute-start | bytes 393224 | tf_op jit(solution)/shard_map/ppermute | solution.py:356
  37.6 2.1 %collective-permute-start.14 = (bf16[2,2,64,128]{3,2,1,0:T(8,128)(2,1)S(1)}, bf16[2,2,64,128]{3,2,1,0:T(8,128)(2,1)S(1)}, u32[]{:S(2)}, u32[]{:S(2)}) collective-permute-start(bf16[2,2,64,128]{3,2,1,0:T(8,128)(2,1)S(1)} %pad_maximum_fusion.5), channel_id=1, source_target_pairs={{0,24},{8,16},{16,8},{24,0},{1,25},{9,17},{17,9},{25,1},{2,26},{10... | collective-permute-start | bytes 196616 | tf_op jit(solution)/shard_map/ppermute | solution.py:356
  39.7 0.1 collective-permute-start.15
  39.8 0.5 collective-permute-done.18.refs_3_
  40.3 1.9 %collective-permute-start.16 = (bf16[2,2,64,128]{3,2,1,0:T(8,128)(2,1)S(1)}, bf16[2,2,64,128]{3,2,1,0:T(8,128)(2,1)S(1)}, u32[]{:S(2)}, u32[]{:S(2)}) collective-permute-start(bf16[2,2,64,128]{3,2,1,0:T(8,128)(2,1)S(1)} %pad_maximum_fusion.7), channel_id=1, source_target_pairs={{0,8},{8,0},{16,24},{24,16},{1,9},{9,1},{17,25},{25,17},{2,10},{10... | collective-permute-start | bytes 196616 | tf_op jit(solution)/shard_map/ppermute | solution.py:356
  42.2 1.7 %collective-permute-done.19.refs_4_ = bf16[2,256,128]{2,1,0:T(8,128)(2,1)S(1)} collective-permute-done((bf16[2,256,128]{2,1,0:T(8,128)(2,1)S(1)}, bf16[2,256,128]{2,1,0:T(8,128)(2,1)S(1)}, u32[]{:S(2)}, u32[]{:S(2)}) %collective-permute-start.19) | collective-permute-done | bytes 131104 | tf_op jit(solution)/shard_map/ppermute | solution.py:356
  43.9 0.0 collective-permute-done.20.refs_5_
  44.0 0.2 collective-permute-done.14.refs_2_.refs_1_
  44.2 2.0 %collective-permute-done.15.refs_3_.refs_2_ = bf16[2,2,64,128]{3,2,1,0:T(8,128)(2,1)S(1)} collective-permute-done((bf16[2,2,64,128]{3,2,1,0:T(8,128)(2,1)S(1)}, bf16[2,2,64,128]{3,2,1,0:T(8,128)(2,1)S(1)}, u32[]{:S(2)}, u32[]{:S(2)}) %collective-permute-start.15) | collective-permute-done | bytes 65568 | tf_op jit(solution)/shard_map/ppermute | solution.py:356
  46.2 0.0 collective-permute-done.16.refs_4_.refs_3_
  46.2 1.0 %collective-permute-start.17 = (bf16[2,64,128]{2,1,0:T(8,128)(2,1)S(1)}, bf16[2,64,128]{2,1,0:T(8,128)(2,1)S(1)}, u32[]{:S(2)}, u32[]{:S(2)}) collective-permute-start(bf16[2,64,128]{2,1,0:T(8,128)(2,1)S(1)} %get-tuple-element.35), channel_id=1, source_target_pairs={{0,4},{4,0},{1,5},{5,1},{2,6},{6,2},{3,7},{7,3},{8,12},{12,8},{9,1... | collective-permute-start | bytes 98312 | tf_op jit(solution)/shard_map/ppermute | solution.py:356
  47.2 3.0 %collective-permute-done.17.refs_1_ = bf16[2,64,128]{2,1,0:T(8,128)(2,1)S(1)} collective-permute-done((bf16[2,64,128]{2,1,0:T(8,128)(2,1)S(1)}, bf16[2,64,128]{2,1,0:T(8,128)(2,1)S(1)}, u32[]{:S(2)}, u32[]{:S(2)}) %collective-permute-start.17) | collective-permute-done | bytes 32800 | tf_op jit(solution)/shard_map/ppermute | solution.py:356
  50.2 0.0 collective-permute-done.21.refs_6_
  50.2 1.0 %shard_map.112 = (bf16[256,128]{1,0:T(8,128)(2,1)}, bf16[128,1024]{1,0:T(8,128)(2,1)}, bf16[128,1024]{1,0:T(8,128)(2,1)}) custom-call(bf16[2,64,128]{2,1,0:T(8,128)(2,1)S(1)} %get-tuple-element.34.refs_0_, bf16[2,64,128]{2,1,0:T(8,128)(2,1)S(1)} %collective-permute-done.17.refs_1_, bf16[2,256,128]{2,1,0:T(8,128)(2,1)S(1)} %get-tuple-element.36.refs_2_, ...), custom_call_target="tpu_custom_call" | custom-call | tf_op jit(solution)/shard_map/pallas_call | solution.py:503
  (29 shorter events, 0.4 us)
Async XLA Ops:
  2.0 3.4 %collective-permute-start = (bf16[144,128]{1,0:T(8,128)(2,1)S(1)}, bf16[144,128]{1,0:T(8,128)(2,1)S(1)}, u32[]{:S(2)}, u32[]{:S(2)}) collective-permute-start(bf16[144,128]{1,0:T(8,128)(2,1)S(1)} %get-tuple-element.24), channel_id=1, source_target_pairs={{0,2},{2,0},{4,6},{6,4},{1,3},{3,1},{5,7},{7,5},{8,10},{10,8},{12,... | collective-permute-start | bytes 110600 | tf_op jit(solution)/shard_map/ppermute | solution.py:356
  2.5 4.7 %collective-permute-start.1 = (bf16[144,128]{1,0:T(8,128)(2,1)S(1)}, bf16[144,128]{1,0:T(8,128)(2,1)S(1)}, u32[]{:S(2)}, u32[]{:S(2)}) collective-permute-start(bf16[144,128]{1,0:T(8,128)(2,1)S(1)} %get-tuple-element.25), channel_id=1, source_target_pairs={{0,4},{2,6},{4,0},{6,2},{1,5},{3,7},{5,1},{7,3},{8,12},{10,14},{12... | collective-permute-start | bytes 110600 | tf_op jit(solution)/shard_map/ppermute | solution.py:356
  5.1 3.4 %collective-permute-start.2 = (bf16[144,128]{1,0:T(8,128)(2,1)S(1)}, bf16[144,128]{1,0:T(8,128)(2,1)S(1)}, u32[]{:S(2)}, u32[]{:S(2)}) collective-permute-start(bf16[144,128]{1,0:T(8,128)(2,1)S(1)} %get-tuple-element.26), channel_id=1, source_target_pairs={{0,6},{2,4},{4,2},{6,0},{1,7},{3,5},{5,3},{7,1},{8,14},{10,12},{12... | collective-permute-start | bytes 110600 | tf_op jit(solution)/shard_map/ppermute | solution.py:356
  5.2 6.0 %collective-permute-start.4 = (bf16[4,256,128]{2,1,0:T(8,128)(2,1)S(1)}, bf16[4,256,128]{2,1,0:T(8,128)(2,1)S(1)}, u32[]{:S(2)}, u32[]{:S(2)}) collective-permute-start(bf16[4,256,128]{2,1,0:T(8,128)(2,1)S(1)} %get-tuple-element.28), channel_id=1, source_target_pairs={{0,2},{1,3},{2,0},{3,1},{4,6},{5,7},{6,4},{7,5},{8,10},{9,11},{10,... | collective-permute-start | bytes 786440 | tf_op jit(solution)/shard_map/ppermute | solution.py:356
  8.6 9.6 %collective-permute-start.3 = (bf16[528,128]{1,0:T(8,128)(2,1)S(1)}, bf16[528,128]{1,0:T(8,128)(2,1)S(1)}, u32[]{:S(2)}, u32[]{:S(2)}) collective-permute-start(bf16[528,128]{1,0:T(8,128)(2,1)S(1)} %constant_dynamic-update-slice_fusion.refs_0_), channel_id=1, source_target_pairs={{0,16},{8,24},{16,0},{24,8},{1,17},{9,25},{17,1},{25,9},{2,18},{10... | collective-permute-start | bytes 405512 | tf_op jit(solution)/shard_map/ppermute | solution.py:356
  11.3 6.9 %collective-permute-start.5 = (bf16[2,256,128]{2,1,0:T(8,128)(2,1)S(1)}, bf16[2,256,128]{2,1,0:T(8,128)(2,1)S(1)}, u32[]{:S(2)}, u32[]{:S(2)}) collective-permute-start(bf16[2,256,128]{2,1,0:T(8,128)(2,1)S(1)} %pad_maximum_fusion.1), channel_id=1, source_target_pairs={{0,1},{1,0},{2,3},{3,2},{4,5},{5,4},{6,7},{7,6},{8,9},{9,8},{10,11... | collective-permute-start | bytes 393224 | tf_op jit(solution)/shard_map/ppermute | solution.py:356
  12.9 5.4 %collective-permute-start.6 = (bf16[2,256,128]{2,1,0:T(8,128)(2,1)S(1)}, bf16[2,256,128]{2,1,0:T(8,128)(2,1)S(1)}, u32[]{:S(2)}, u32[]{:S(2)}) collective-permute-start(bf16[2,256,128]{2,1,0:T(8,128)(2,1)S(1)} %pad_maximum_fusion.2), channel_id=1, source_target_pairs={{0,4},{1,5},{2,6},{3,7},{4,0},{5,1},{6,2},{7,3},{8,12},{9,13},{10,... | collective-permute-start | bytes 393224 | tf_op jit(solution)/shard_map/ppermute | solution.py:356
  14.5 7.2 %collective-permute-start.7 = (bf16[528,128]{1,0:T(8,128)(2,1)S(1)}, bf16[528,128]{1,0:T(8,128)(2,1)S(1)}, u32[]{:S(2)}, u32[]{:S(2)}) collective-permute-start(bf16[528,128]{1,0:T(8,128)(2,1)S(1)} %constant_dynamic-update-slice_fusion.refs_0_), channel_id=1, source_target_pairs={{0,8},{8,0},{16,24},{24,16},{1,9},{9,1},{17,25},{25,17},{2,10},{10... | collective-permute-start | bytes 405512 | tf_op jit(solution)/shard_map/ppermute | solution.py:356
  16.1 5.9 %collective-permute-start.9 = (bf16[2,256,128]{2,1,0:T(8,128)(2,1)S(1)}, bf16[2,256,128]{2,1,0:T(8,128)(2,1)S(1)}, u32[]{:S(2)}, u32[]{:S(2)}) collective-permute-start(bf16[2,256,128]{2,1,0:T(8,128)(2,1)S(1)} %pad_maximum_fusion.4), channel_id=1, source_target_pairs={{0,5},{1,4},{2,7},{3,6},{4,1},{5,0},{6,3},{7,2},{8,13},{9,12},{10,... | collective-permute-start | bytes 393224 | tf_op jit(solution)/shard_map/ppermute | solution.py:356
  18.2 5.7 %collective-permute-start.8 = (bf16[528,128]{1,0:T(8,128)(2,1)S(1)}, bf16[528,128]{1,0:T(8,128)(2,1)S(1)}, u32[]{:S(2)}, u32[]{:S(2)}) collective-permute-start(bf16[528,128]{1,0:T(8,128)(2,1)S(1)} %shard_map.104.refs_1_), channel_id=1, source_target_pairs={{0,8},{8,0},{16,24},{24,16},{1,9},{9,1},{17,25},{25,17},{2,10},{10... | collective-permute-start | bytes 405512 | tf_op jit(solution)/shard_map/ppermute | solution.py:356
  24.6 6.6 %collective-permute-start.12 = (f32[8,128]{1,0:T(8,128)S(1)}, f32[8,128]{1,0:T(8,128)S(1)}, u32[]{:S(2)}, u32[]{:S(2)}) collective-permute-start(f32[8,128]{1,0:T(8,128)S(1)} %shard_map.107.refs_8_.refs_7_), channel_id=1, source_target_pairs={{0,24},{8,16},{16,8},{24,0},{1,25},{9,17},{17,9},{25,1},{2,26},{10... | collective-permute-start | bytes 12296 | tf_op jit(solution)/shard_map/ppermute | solution.py:356
  27.9 4.5 %collective-permute-start.11 = (f32[8,128]{1,0:T(8,128)S(1)}, f32[8,128]{1,0:T(8,128)S(1)}, u32[]{:S(2)}, u32[]{:S(2)}) collective-permute-start(f32[8,128]{1,0:T(8,128)S(1)} %shard_map.107.refs_8_.refs_7_), channel_id=1, source_target_pairs={{0,16},{8,24},{16,0},{24,8},{1,17},{9,25},{17,1},{25,9},{2,18},{10... | collective-permute-start | bytes 12296 | tf_op jit(solution)/shard_map/ppermute | solution.py:356
  28.1 4.3 %collective-permute-start.10 = (f32[8,128]{1,0:T(8,128)S(1)}, f32[8,128]{1,0:T(8,128)S(1)}, u32[]{:S(2)}, u32[]{:S(2)}) collective-permute-start(f32[8,128]{1,0:T(8,128)S(1)} %shard_map.107.refs_8_.refs_7_), channel_id=1, source_target_pairs={{0,8},{8,0},{16,24},{24,16},{1,9},{9,1},{17,25},{25,17},{2,10},{10... | collective-permute-start | bytes 12296 | tf_op jit(solution)/shard_map/ppermute | solution.py:356
  33.9 3.6 %collective-permute-start.13 = (bf16[4,2,64,128]{3,2,1,0:T(8,128)(2,1)S(1)}, bf16[4,2,64,128]{3,2,1,0:T(8,128)(2,1)S(1)}, u32[]{:S(2)}, u32[]{:S(2)}) collective-permute-start(bf16[4,2,64,128]{3,2,1,0:T(8,128)(2,1)S(1)} %get-tuple-element.33), channel_id=1, source_target_pairs={{0,2},{2,0},{1,3},{3,1},{4,6},{6,4},{5,7},{7,5},{8,10},{10,8},{9,1... | collective-permute-start | bytes 393224 | tf_op jit(solution)/shard_map/ppermute | solution.py:356
  34.0 6.3 %collective-permute-start.18 = (bf16[2,256,128]{2,1,0:T(8,128)(2,1)S(1)}, bf16[2,256,128]{2,1,0:T(8,128)(2,1)S(1)}, u32[]{:S(2)}, u32[]{:S(2)}) collective-permute-start(bf16[2,256,128]{2,1,0:T(8,128)(2,1)S(1)} %get-tuple-element.37), channel_id=1, source_target_pairs={{0,1},{1,0},{2,3},{3,2},{4,5},{5,4},{6,7},{7,6},{8,9},{9,8},{10,11... | collective-permute-start | bytes 393224 | tf_op jit(solution)/shard_map/ppermute | solution.py:356
  35.6 8.4 %collective-permute-start.19 = (bf16[2,256,128]{2,1,0:T(8,128)(2,1)S(1)}, bf16[2,256,128]{2,1,0:T(8,128)(2,1)S(1)}, u32[]{:S(2)}, u32[]{:S(2)}) collective-permute-start(bf16[2,256,128]{2,1,0:T(8,128)(2,1)S(1)} %get-tuple-element.38), channel_id=1, source_target_pairs={{0,4},{1,5},{2,6},{3,7},{4,0},{5,1},{6,2},{7,3},{8,12},{9,13},{10,... | collective-permute-start | bytes 393224 | tf_op jit(solution)/shard_map/ppermute | solution.py:356
  36.5 7.5 %collective-permute-start.20 = (bf16[2,256,128]{2,1,0:T(8,128)(2,1)S(1)}, bf16[2,256,128]{2,1,0:T(8,128)(2,1)S(1)}, u32[]{:S(2)}, u32[]{:S(2)}) collective-permute-start(bf16[2,256,128]{2,1,0:T(8,128)(2,1)S(1)} %get-tuple-element.39), channel_id=1, source_target_pairs={{0,5},{1,4},{2,7},{3,6},{4,1},{5,0},{6,3},{7,2},{8,13},{9,12},{10,... | collective-permute-start | bytes 393224 | tf_op jit(solution)/shard_map/ppermute | solution.py:356
  37.6 6.6 %collective-permute-start.14 = (bf16[2,2,64,128]{3,2,1,0:T(8,128)(2,1)S(1)}, bf16[2,2,64,128]{3,2,1,0:T(8,128)(2,1)S(1)}, u32[]{:S(2)}, u32[]{:S(2)}) collective-permute-start(bf16[2,2,64,128]{3,2,1,0:T(8,128)(2,1)S(1)} %pad_maximum_fusion.5), channel_id=1, source_target_pairs={{0,24},{8,16},{16,8},{24,0},{1,25},{9,17},{17,9},{25,1},{2,26},{10... | collective-permute-start | bytes 196616 | tf_op jit(solution)/shard_map/ppermute | solution.py:356
  39.7 6.4 %collective-permute-start.15 = (bf16[2,2,64,128]{3,2,1,0:T(8,128)(2,1)S(1)}, bf16[2,2,64,128]{3,2,1,0:T(8,128)(2,1)S(1)}, u32[]{:S(2)}, u32[]{:S(2)}) collective-permute-start(bf16[2,2,64,128]{3,2,1,0:T(8,128)(2,1)S(1)} %pad_maximum_fusion.6), channel_id=1, source_target_pairs={{0,16},{8,24},{16,0},{24,8},{1,17},{9,25},{17,1},{25,9},{2,18},{10... | collective-permute-start | bytes 196616 | tf_op jit(solution)/shard_map/ppermute | solution.py:356
  40.3 5.9 %collective-permute-start.16 = (bf16[2,2,64,128]{3,2,1,0:T(8,128)(2,1)S(1)}, bf16[2,2,64,128]{3,2,1,0:T(8,128)(2,1)S(1)}, u32[]{:S(2)}, u32[]{:S(2)}) collective-permute-start(bf16[2,2,64,128]{3,2,1,0:T(8,128)(2,1)S(1)} %pad_maximum_fusion.7), channel_id=1, source_target_pairs={{0,8},{8,0},{16,24},{24,16},{1,9},{9,1},{17,25},{25,17},{2,10},{10... | collective-permute-start | bytes 196616 | tf_op jit(solution)/shard_map/ppermute | solution.py:356
  46.2 4.0 %collective-permute-start.21 = (bf16[4,256,128]{2,1,0:T(8,128)(2,1)S(1)}, bf16[4,256,128]{2,1,0:T(8,128)(2,1)S(1)}, u32[]{:S(2)}, u32[]{:S(2)}) collective-permute-start(bf16[4,256,128]{2,1,0:T(8,128)(2,1)S(1)} %shard_map.111), channel_id=1, source_target_pairs={{0,2},{1,3},{2,0},{3,1},{4,6},{5,7},{6,4},{7,5},{8,10},{9,11},{10,... | collective-permute-start | bytes 786440 | tf_op jit(solution)/shard_map/ppermute | solution.py:356
  46.2 4.0 %collective-permute-start.17 = (bf16[2,64,128]{2,1,0:T(8,128)(2,1)S(1)}, bf16[2,64,128]{2,1,0:T(8,128)(2,1)S(1)}, u32[]{:S(2)}, u32[]{:S(2)}) collective-permute-start(bf16[2,64,128]{2,1,0:T(8,128)(2,1)S(1)} %get-tuple-element.35), channel_id=1, source_target_pairs={{0,4},{4,0},{1,5},{5,1},{2,6},{6,2},{3,7},{7,3},{8,12},{12,8},{9,1... | collective-permute-start | bytes 98312 | tf_op jit(solution)/shard_map/ppermute | solution.py:356

commit v17 on v16

--- a/solution.py
+++ b/solution.py
@@ -382,7 +382,8 @@
 
 
 def swap_slabs(slabs, groups):
-    return [swap(x, ("row", "near"), m, groups) if m else x for m, x in enumerate(slabs)]
+    came = [swap(slabs[m], ("row", "near"), m, groups) for m in range(groups - 1, 0, -1)]
+    return [slabs[0], *came[::-1]]
 
 
 def line_limits(parts, row_count, nears, rows, lines, resp_len, prompt_end):

time: 51.4 us -> 51.4 us (level)
  no operation moved by 1% of the time
where the time goes in v17:
time: 51.4 us; the launch traced here: 51.2 us
  starting transfers between devices  27.2 us (53%)
  waiting for transfers between devices  13.9 us (27%)
  Pallas kernels  7.66 us (15%)
  between operations  2.12 us (4%)
    ppermute x22, starting transfers between devices, swap(): return lax.ppermute(x, axis, [(i, i ^ distance) for i in range(size)])  27.2 us
    ppermute x22, waiting for transfers between devices, swap(): return lax.ppermute(x, axis, [(i, i ^ distance) for i in range(size)])  13.9 us
    pallas_call x1, Pallas kernels, shards(): pl.pallas_call(functools.partial(part_kernel, blocks, nears, heads, token...  2.05 us
    pallas_call x2, Pallas kernels, part_lse(): pl.pallas_call(functools.partial(stat_kernel, held, first, nears, heads,...  1.76 us
    pallas_call x1, Pallas kernels, shards(): pl.pallas_call(functools.partial(token_kernel, blocks, nears, heads, toke...  1.46 us
    pallas_call x1, Pallas kernels, shards(): pl.pallas_call(functools.partial(pack_kernel, row_count, nears, heads), i...  1.38 us
  transfers between devices with their start and end apart: 22, of which 11 were waited for; matrix products, arithmetic and copies ran while one was open for 1% of the time, Pallas kernels for 6%

profile of v17, /device:TPU:0, one launch (start us, length us, event | category | flops | bytes accessed | tf_op | source)
XLA Modules:
  0.0 51.2 jit_solution(12321510531994165008)
XLA Ops:
  0.6 1.4 %shard_map.103 = (bf16[144,128]{1,0:T(8,128)(2,1)S(1)}, bf16[144,128]{1,0:T(8,128)(2,1)S(1)}, bf16[144,128]{1,0:T(8,128)(2,1)S(1)}, bf16[144,128]{1,0:T(8,128)(2...) custom-call(bf16[256,128]{1,0:T(8,128)(2,1)} %bitcast.24, bf16[256,128]{1,0:T(8,128)(2,1)} %bitcast.25, ...), custom_call_target="tpu_custom_call" | custom-call | tf_op jit(solution)/shard_map/pallas_call | solution.py:425
  2.0 0.5 %collective-permute-start = (bf16[144,128]{1,0:T(8,128)(2,1)S(1)}, bf16[144,128]{1,0:T(8,128)(2,1)S(1)}, u32[]{:S(2)}, u32[]{:S(2)}) collective-permute-start(bf16[144,128]{1,0:T(8,128)(2,1)S(1)} %get-tuple-element.24), channel_id=1, source_target_pairs={{0,2},{2,0},{4,6},{6,4},{1,3},{3,1},{5,7},{7,5},{8,10},{10,8},{12,... | collective-permute-start | bytes 110600 | tf_op jit(solution)/shard_map/ppermute | solution.py:356
  2.5 2.6 %collective-permute-start.1 = (bf16[144,128]{1,0:T(8,128)(2,1)S(1)}, bf16[144,128]{1,0:T(8,128)(2,1)S(1)}, u32[]{:S(2)}, u32[]{:S(2)}) collective-permute-start(bf16[144,128]{1,0:T(8,128)(2,1)S(1)} %get-tuple-element.25), channel_id=1, source_target_pairs={{0,4},{2,6},{4,0},{6,2},{1,5},{3,7},{5,1},{7,3},{8,12},{10,14},{12... | collective-permute-start | bytes 110600 | tf_op jit(solution)/shard_map/ppermute | solution.py:356
  5.1 0.1 collective-permute-start.2
  5.2 0.1 collective-permute-start.4
  5.4 0.0 collective-permute-done
  5.4 1.8 %collective-permute-done.1 = bf16[144,128]{1,0:T(8,128)(2,1)S(1)} collective-permute-done((bf16[144,128]{1,0:T(8,128)(2,1)S(1)}, bf16[144,128]{1,0:T(8,128)(2,1)S(1)}, u32[]{:S(2)}, u32[]{:S(2)}) %collective-permute-start.1) | collective-permute-done | bytes 36896 | tf_op jit(solution)/shard_map/ppermute | solution.py:356
  7.2 1.4 %collective-permute-done.2 = bf16[144,128]{1,0:T(8,128)(2,1)S(1)} collective-permute-done((bf16[144,128]{1,0:T(8,128)(2,1)S(1)}, bf16[144,128]{1,0:T(8,128)(2,1)S(1)}, u32[]{:S(2)}, u32[]{:S(2)}) %collective-permute-start.2) | collective-permute-done | bytes 36896 | tf_op jit(solution)/shard_map/ppermute | solution.py:356
  8.6 2.7 %collective-permute-start.3 = (bf16[528,128]{1,0:T(8,128)(2,1)S(1)}, bf16[528,128]{1,0:T(8,128)(2,1)S(1)}, u32[]{:S(2)}, u32[]{:S(2)}) collective-permute-start(bf16[528,128]{1,0:T(8,128)(2,1)S(1)} %constant_dynamic-update-slice_fusion.refs_0_), channel_id=1, source_target_pairs={{0,16},{8,24},{16,0},{24,8},{1,17},{9,25},{17,1},{25,9},{2,18},{10... | collective-permute-start | bytes 405512 | tf_op jit(solution)/shard_map/ppermute | solution.py:356
  11.2 0.0 collective-permute-done.4
  11.3 1.6 %collective-permute-start.5 = (bf16[2,256,128]{2,1,0:T(8,128)(2,1)S(1)}, bf16[2,256,128]{2,1,0:T(8,128)(2,1)S(1)}, u32[]{:S(2)}, u32[]{:S(2)}) collective-permute-start(bf16[2,256,128]{2,1,0:T(8,128)(2,1)S(1)} %pad_maximum_fusion.1), channel_id=1, source_target_pairs={{0,1},{1,0},{2,3},{3,2},{4,5},{5,4},{6,7},{7,6},{8,9},{9,8},{10,11... | collective-permute-start | bytes 393224 | tf_op jit(solution)/shard_map/ppermute | solution.py:356
  12.9 0.9 %collective-permute-start.6 = (bf16[2,256,128]{2,1,0:T(8,128)(2,1)S(1)}, bf16[2,256,128]{2,1,0:T(8,128)(2,1)S(1)}, u32[]{:S(2)}, u32[]{:S(2)}) collective-permute-start(bf16[2,256,128]{2,1,0:T(8,128)(2,1)S(1)} %pad_maximum_fusion.2), channel_id=1, source_target_pairs={{0,4},{1,5},{2,6},{3,7},{4,0},{5,1},{6,2},{7,3},{8,12},{9,13},{10,... | collective-permute-start | bytes 393224 | tf_op jit(solution)/shard_map/ppermute | solution.py:356
  14.5 1.6 %collective-permute-start.7 = (bf16[528,128]{1,0:T(8,128)(2,1)S(1)}, bf16[528,128]{1,0:T(8,128)(2,1)S(1)}, u32[]{:S(2)}, u32[]{:S(2)}) collective-permute-start(bf16[528,128]{1,0:T(8,128)(2,1)S(1)} %constant_dynamic-update-slice_fusion.refs_0_), channel_id=1, source_target_pairs={{0,8},{8,0},{16,24},{24,16},{1,9},{9,1},{17,25},{25,17},{2,10},{10... | collective-permute-start | bytes 405512 | tf_op jit(solution)/shard_map/ppermute | solution.py:356
  16.1 1.2 %collective-permute-start.9 = (bf16[2,256,128]{2,1,0:T(8,128)(2,1)S(1)}, bf16[2,256,128]{2,1,0:T(8,128)(2,1)S(1)}, u32[]{:S(2)}, u32[]{:S(2)}) collective-permute-start(bf16[2,256,128]{2,1,0:T(8,128)(2,1)S(1)} %pad_maximum_fusion.4), channel_id=1, source_target_pairs={{0,5},{1,4},{2,7},{3,6},{4,1},{5,0},{6,3},{7,2},{8,13},{9,12},{10,... | collective-permute-start | bytes 393224 | tf_op jit(solution)/shard_map/ppermute | solution.py:356
  17.3 0.9 %collective-permute-done.3.refs_0_ = bf16[528,128]{1,0:T(8,128)(2,1)S(1)} collective-permute-done((bf16[528,128]{1,0:T(8,128)(2,1)S(1)}, bf16[528,128]{1,0:T(8,128)(2,1)S(1)}, u32[]{:S(2)}, u32[]{:S(2)}) %collective-permute-start.3) | collective-permute-done | bytes 135200 | tf_op jit(solution)/shard_map/ppermute | solution.py:356
  18.2 0.0 collective-permute-done.5.refs_1_.refs_4_.refs_2_.refs_5_
  18.2 0.0 collective-permute-done.6.refs_2_.refs_5_.refs_3_.refs_6_
  18.2 2.7 %collective-permute-start.8 = (bf16[528,128]{1,0:T(8,128)(2,1)S(1)}, bf16[528,128]{1,0:T(8,128)(2,1)S(1)}, u32[]{:S(2)}, u32[]{:S(2)}) collective-permute-start(bf16[528,128]{1,0:T(8,128)(2,1)S(1)} %shard_map.104.refs_1_), channel_id=1, source_target_pairs={{0,8},{8,0},{16,24},{24,16},{1,9},{9,1},{17,25},{25,17},{2,10},{10... | collective-permute-start | bytes 405512 | tf_op jit(solution)/shard_map/ppermute | solution.py:356
  21.6 0.0 collective-permute-done.7.refs_2_
  21.6 0.4 collective-permute-done.9.refs_6_.refs_4_.refs_7_
  22.0 1.1 %shard_map.105.refs_1_.refs_5_ = f32[8,128]{1,0:T(8,128)S(1)} custom-call(s32[1,1024]{1,0:T(1,128)S(1)} %compare_select_fusion.ends_ref, bf16[528,128]{1,0:T(8,128)(2,1)S(1)} %constant_dynamic-update-slice_fusion.refs_0_, bf16[528,128]{1,0:T(8,128)(2,1)S(1)} %shard_map.104.refs_1_, bf16[528,128]{1,0:T(8,128)(2,1)S(1)} %collective-permute-done.7.refs_2_, ...), custom_call_target="tpu_custom_call" | custom-call | tf_op jit(solution)/shard_map/pallas_call | solution.py:458
  23.2 0.7 %collective-permute-done.8.refs_0_ = bf16[528,128]{1,0:T(8,128)(2,1)S(1)} collective-permute-done((bf16[528,128]{1,0:T(8,128)(2,1)S(1)}, bf16[528,128]{1,0:T(8,128)(2,1)S(1)}, u32[]{:S(2)}, u32[]{:S(2)}) %collective-permute-start.8) | collective-permute-done | bytes 135200 | tf_op jit(solution)/shard_map/ppermute | solution.py:356
  23.9 0.6 %shard_map.107.refs_8_.refs_7_ = f32[8,128]{1,0:T(8,128)S(1)} custom-call(s32[1,1024]{1,0:T(1,128)S(1)} %compare_select_fusion.ends_ref, bf16[528,128]{1,0:T(8,128)(2,1)S(1)} %shard_map.106.refs_0_.refs_3_, bf16[2,256,128]{2,1,0:T(8,128)(2,1)S(1)} %pad_maximum_fusion.3.refs_3_.refs_1_.refs_4_, ...), custom_call_target="tpu_custom_call" | custom-call | tf_op jit(solution)/shard_map/pallas_call | solution.py:458
  24.6 3.4 %collective-permute-start.12 = (f32[8,128]{1,0:T(8,128)S(1)}, f32[8,128]{1,0:T(8,128)S(1)}, u32[]{:S(2)}, u32[]{:S(2)}) collective-permute-start(f32[8,128]{1,0:T(8,128)S(1)} %shard_map.107.refs_8_.refs_7_), channel_id=1, source_target_pairs={{0,24},{8,16},{16,8},{24,0},{1,25},{9,17},{17,9},{25,1},{2,26},{10... | collective-permute-start | bytes 12296 | tf_op jit(solution)/shard_map/ppermute | solution.py:356
  27.9 0.2 collective-permute-start.11
  28.1 0.9 %collective-permute-start.10 = (f32[8,128]{1,0:T(8,128)S(1)}, f32[8,128]{1,0:T(8,128)S(1)}, u32[]{:S(2)}, u32[]{:S(2)}) collective-permute-start(f32[8,128]{1,0:T(8,128)S(1)} %shard_map.107.refs_8_.refs_7_), channel_id=1, source_target_pairs={{0,8},{8,0},{16,24},{24,16},{1,9},{9,1},{17,25},{25,17},{2,10},{10... | collective-permute-start | bytes 12296 | tf_op jit(solution)/shard_map/ppermute | solution.py:356
  29.0 2.1 %shard_map.108 = (bf16[4,256,1024]{2,1,0:T(8,128)(2,1)S(1)}, bf16[4,256,1024]{2,1,0:T(8,128)(2,1)S(1)}, f32[128,1024]{1,0:T(8,128)S(1)}) custom-call(s32[1,1024]{1,0:T(1,128)S(1)} %compare_select_fusion.ends_ref, bf16[528,128]{1,0:T(8,128)(2,1)S(1)} %constant_dynamic-update-slice_fusion.refs_0_, bf16[528,128]{1,0:T(8,128)(2,1)S(1)} %shard_map.104.refs_1_, ...), custom_call_target="tpu_custom_call" | custom-call | tf_op jit(solution)/shard_map/pallas_call | solution.py:472
  31.1 0.0 collective-permute-done.12.refs_10_
  31.1 1.3 %collective-permute-done.11.refs_9_ = f32[8,128]{1,0:T(8,128)S(1)} collective-permute-done((f32[8,128]{1,0:T(8,128)S(1)}, f32[8,128]{1,0:T(8,128)S(1)}, u32[]{:S(2)}, u32[]{:S(2)}) %collective-permute-start.11) | collective-permute-done | bytes 4128 | tf_op jit(solution)/shard_map/ppermute | solution.py:356
  32.5 0.0 collective-permute-done.10.refs_8_
  32.5 1.5 %shard_map.109 = (bf16[2,256,128]{2,1,0:T(8,128)(2,1)S(1)}, bf16[2,256,128]{2,1,0:T(8,128)(2,1)S(1)}, bf16[2,256,128]{2,1,0:T(8,128)(2,1)S(1)}, bf16[2,256,128]{...) custom-call(s32[1,1024]{1,0:T(1,128)S(1)} %compare_convert_fusion.live_ref, ...), custom_call_target="tpu_custom_call" | custom-call | tf_op jit(solution)/shard_map/pallas_call | solution.py:481
  33.9 0.1 collective-permute-start.13
  34.0 1.6 %collective-permute-start.18 = (bf16[2,256,128]{2,1,0:T(8,128)(2,1)S(1)}, bf16[2,256,128]{2,1,0:T(8,128)(2,1)S(1)}, u32[]{:S(2)}, u32[]{:S(2)}) collective-permute-start(bf16[2,256,128]{2,1,0:T(8,128)(2,1)S(1)} %get-tuple-element.37), channel_id=1, source_target_pairs={{0,1},{1,0},{2,3},{3,2},{4,5},{5,4},{6,7},{7,6},{8,9},{9,8},{10,11... | collective-permute-start | bytes 393224 | tf_op jit(solution)/shard_map/ppermute | solution.py:356
  35.6 0.9 %collective-permute-start.19 = (bf16[2,256,128]{2,1,0:T(8,128)(2,1)S(1)}, bf16[2,256,128]{2,1,0:T(8,128)(2,1)S(1)}, u32[]{:S(2)}, u32[]{:S(2)}) collective-permute-start(bf16[2,256,128]{2,1,0:T(8,128)(2,1)S(1)} %get-tuple-element.38), channel_id=1, source_target_pairs={{0,4},{1,5},{2,6},{3,7},{4,0},{5,1},{6,2},{7,3},{8,12},{9,13},{10,... | collective-permute-start | bytes 393224 | tf_op jit(solution)/shard_map/ppermute | solution.py:356
  36.5 1.1 %collective-permute-start.20 = (bf16[2,256,128]{2,1,0:T(8,128)(2,1)S(1)}, bf16[2,256,128]{2,1,0:T(8,128)(2,1)S(1)}, u32[]{:S(2)}, u32[]{:S(2)}) collective-permute-start(bf16[2,256,128]{2,1,0:T(8,128)(2,1)S(1)} %get-tuple-element.39), channel_id=1, source_target_pairs={{0,5},{1,4},{2,7},{3,6},{4,1},{5,0},{6,3},{7,2},{8,13},{9,12},{10,... | collective-permute-start | bytes 393224 | tf_op jit(solution)/shard_map/ppermute | solution.py:356
  37.6 2.1 %collective-permute-start.14 = (bf16[2,2,64,128]{3,2,1,0:T(8,128)(2,1)S(1)}, bf16[2,2,64,128]{3,2,1,0:T(8,128)(2,1)S(1)}, u32[]{:S(2)}, u32[]{:S(2)}) collective-permute-start(bf16[2,2,64,128]{3,2,1,0:T(8,128)(2,1)S(1)} %pad_maximum_fusion.5), channel_id=1, source_target_pairs={{0,24},{8,16},{16,8},{24,0},{1,25},{9,17},{17,9},{25,1},{2,26},{10... | collective-permute-start | bytes 196616 | tf_op jit(solution)/shard_map/ppermute | solution.py:356
  39.7 0.1 collective-permute-start.15
  39.8 0.5 collective-permute-done.18.refs_3_
  40.3 1.9 %collective-permute-start.16 = (bf16[2,2,64,128]{3,2,1,0:T(8,128)(2,1)S(1)}, bf16[2,2,64,128]{3,2,1,0:T(8,128)(2,1)S(1)}, u32[]{:S(2)}, u32[]{:S(2)}) collective-permute-start(bf16[2,2,64,128]{3,2,1,0:T(8,128)(2,1)S(1)} %pad_maximum_fusion.7), channel_id=1, source_target_pairs={{0,8},{8,0},{16,24},{24,16},{1,9},{9,1},{17,25},{25,17},{2,10},{10... | collective-permute-start | bytes 196616 | tf_op jit(solution)/shard_map/ppermute | solution.py:356
  42.2 1.7 %collective-permute-done.19.refs_4_ = bf16[2,256,128]{2,1,0:T(8,128)(2,1)S(1)} collective-permute-done((bf16[2,256,128]{2,1,0:T(8,128)(2,1)S(1)}, bf16[2,256,128]{2,1,0:T(8,128)(2,1)S(1)}, u32[]{:S(2)}, u32[]{:S(2)}) %collective-permute-start.19) | collective-permute-done | bytes 131104 | tf_op jit(solution)/shard_map/ppermute | solution.py:356
  43.9 0.0 collective-permute-done.20.refs_5_
  44.0 0.2 collective-permute-done.14.refs_2_.refs_1_
  44.2 2.0 %collective-permute-done.15.refs_3_.refs_2_ = bf16[2,2,64,128]{3,2,1,0:T(8,128)(2,1)S(1)} collective-permute-done((bf16[2,2,64,128]{3,2,1,0:T(8,128)(2,1)S(1)}, bf16[2,2,64,128]{3,2,1,0:T(8,128)(2,1)S(1)}, u32[]{:S(2)}, u32[]{:S(2)}) %collective-permute-start.15) | collective-permute-done | bytes 65568 | tf_op jit(solution)/shard_map/ppermute | solution.py:356
  46.2 0.0 collective-permute-done.16.refs_4_.refs_3_
  46.2 1.0 %collective-permute-start.17 = (bf16[2,64,128]{2,1,0:T(8,128)(2,1)S(1)}, bf16[2,64,128]{2,1,0:T(8,128)(2,1)S(1)}, u32[]{:S(2)}, u32[]{:S(2)}) collective-permute-start(bf16[2,64,128]{2,1,0:T(8,128)(2,1)S(1)} %get-tuple-element.35), channel_id=1, source_target_pairs={{0,4},{4,0},{1,5},{5,1},{2,6},{6,2},{3,7},{7,3},{8,12},{12,8},{9,1... | collective-permute-start | bytes 98312 | tf_op jit(solution)/shard_map/ppermute | solution.py:356
  47.2 3.0 %collective-permute-done.17.refs_1_ = bf16[2,64,128]{2,1,0:T(8,128)(2,1)S(1)} collective-permute-done((bf16[2,64,128]{2,1,0:T(8,128)(2,1)S(1)}, bf16[2,64,128]{2,1,0:T(8,128)(2,1)S(1)}, u32[]{:S(2)}, u32[]{:S(2)}) %collective-permute-start.17) | collective-permute-done | bytes 32800 | tf_op jit(solution)/shard_map/ppermute | solution.py:356
  50.2 0.0 collective-permute-done.21.refs_6_
  50.2 1.0 %shard_map.112 = (bf16[256,128]{1,0:T(8,128)(2,1)}, bf16[128,1024]{1,0:T(8,128)(2,1)}, bf16[128,1024]{1,0:T(8,128)(2,1)}) custom-call(bf16[2,64,128]{2,1,0:T(8,128)(2,1)S(1)} %get-tuple-element.34.refs_0_, bf16[2,64,128]{2,1,0:T(8,128)(2,1)S(1)} %collective-permute-done.17.refs_1_, bf16[2,256,128]{2,1,0:T(8,128)(2,1)S(1)} %get-tuple-element.36.refs_2_, ...), custom_call_target="tpu_custom_call" | custom-call | tf_op jit(solution)/shard_map/pallas_call | solution.py:504
  (29 shorter events, 0.4 us)
Async XLA Ops:
  2.0 3.4 %collective-permute-start = (bf16[144,128]{1,0:T(8,128)(2,1)S(1)}, bf16[144,128]{1,0:T(8,128)(2,1)S(1)}, u32[]{:S(2)}, u32[]{:S(2)}) collective-permute-start(bf16[144,128]{1,0:T(8,128)(2,1)S(1)} %get-tuple-element.24), channel_id=1, source_target_pairs={{0,2},{2,0},{4,6},{6,4},{1,3},{3,1},{5,7},{7,5},{8,10},{10,8},{12,... | collective-permute-start | bytes 110600 | tf_op jit(solution)/shard_map/ppermute | solution.py:356
  2.5 4.7 %collective-permute-start.1 = (bf16[144,128]{1,0:T(8,128)(2,1)S(1)}, bf16[144,128]{1,0:T(8,128)(2,1)S(1)}, u32[]{:S(2)}, u32[]{:S(2)}) collective-permute-start(bf16[144,128]{1,0:T(8,128)(2,1)S(1)} %get-tuple-element.25), channel_id=1, source_target_pairs={{0,4},{2,6},{4,0},{6,2},{1,5},{3,7},{5,1},{7,3},{8,12},{10,14},{12... | collective-permute-start | bytes 110600 | tf_op jit(solution)/shard_map/ppermute | solution.py:356
  5.1 3.4 %collective-permute-start.2 = (bf16[144,128]{1,0:T(8,128)(2,1)S(1)}, bf16[144,128]{1,0:T(8,128)(2,1)S(1)}, u32[]{:S(2)}, u32[]{:S(2)}) collective-permute-start(bf16[144,128]{1,0:T(8,128)(2,1)S(1)} %get-tuple-element.26), channel_id=1, source_target_pairs={{0,6},{2,4},{4,2},{6,0},{1,7},{3,5},{5,3},{7,1},{8,14},{10,12},{12... | collective-permute-start | bytes 110600 | tf_op jit(solution)/shard_map/ppermute | solution.py:356
  5.2 6.0 %collective-permute-start.4 = (bf16[4,256,128]{2,1,0:T(8,128)(2,1)S(1)}, bf16[4,256,128]{2,1,0:T(8,128)(2,1)S(1)}, u32[]{:S(2)}, u32[]{:S(2)}) collective-permute-start(bf16[4,256,128]{2,1,0:T(8,128)(2,1)S(1)} %get-tuple-element.28), channel_id=1, source_target_pairs={{0,2},{1,3},{2,0},{3,1},{4,6},{5,7},{6,4},{7,5},{8,10},{9,11},{10,... | collective-permute-start | bytes 786440 | tf_op jit(solution)/shard_map/ppermute | solution.py:356
  8.6 9.6 %collective-permute-start.3 = (bf16[528,128]{1,0:T(8,128)(2,1)S(1)}, bf16[528,128]{1,0:T(8,128)(2,1)S(1)}, u32[]{:S(2)}, u32[]{:S(2)}) collective-permute-start(bf16[528,128]{1,0:T(8,128)(2,1)S(1)} %constant_dynamic-update-slice_fusion.refs_0_), channel_id=1, source_target_pairs={{0,16},{8,24},{16,0},{24,8},{1,17},{9,25},{17,1},{25,9},{2,18},{10... | collective-permute-start | bytes 405512 | tf_op jit(solution)/shard_map/ppermute | solution.py:356
  11.3 6.9 %collective-permute-start.5 = (bf16[2,256,128]{2,1,0:T(8,128)(2,1)S(1)}, bf16[2,256,128]{2,1,0:T(8,128)(2,1)S(1)}, u32[]{:S(2)}, u32[]{:S(2)}) collective-permute-start(bf16[2,256,128]{2,1,0:T(8,128)(2,1)S(1)} %pad_maximum_fusion.1), channel_id=1, source_target_pairs={{0,1},{1,0},{2,3},{3,2},{4,5},{5,4},{6,7},{7,6},{8,9},{9,8},{10,11... | collective-permute-start | bytes 393224 | tf_op jit(solution)/shard_map/ppermute | solution.py:356
  12.9 5.4 %collective-permute-start.6 = (bf16[2,256,128]{2,1,0:T(8,128)(2,1)S(1)}, bf16[2,256,128]{2,1,0:T(8,128)(2,1)S(1)}, u32[]{:S(2)}, u32[]{:S(2)}) collective-permute-start(bf16[2,256,128]{2,1,0:T(8,128)(2,1)S(1)} %pad_maximum_fusion.2), channel_id=1, source_target_pairs={{0,4},{1,5},{2,6},{3,7},{4,0},{5,1},{6,2},{7,3},{8,12},{9,13},{10,... | collective-permute-start | bytes 393224 | tf_op jit(solution)/shard_map/ppermute | solution.py:356
  14.5 7.2 %collective-permute-start.7 = (bf16[528,128]{1,0:T(8,128)(2,1)S(1)}, bf16[528,128]{1,0:T(8,128)(2,1)S(1)}, u32[]{:S(2)}, u32[]{:S(2)}) collective-permute-start(bf16[528,128]{1,0:T(8,128)(2,1)S(1)} %constant_dynamic-update-slice_fusion.refs_0_), channel_id=1, source_target_pairs={{0,8},{8,0},{16,24},{24,16},{1,9},{9,1},{17,25},{25,17},{2,10},{10... | collective-permute-start | bytes 405512 | tf_op jit(solution)/shard_map/ppermute | solution.py:356
  16.1 5.9 %collective-permute-start.9 = (bf16[2,256,128]{2,1,0:T(8,128)(2,1)S(1)}, bf16[2,256,128]{2,1,0:T(8,128)(2,1)S(1)}, u32[]{:S(2)}, u32[]{:S(2)}) collective-permute-start(bf16[2,256,128]{2,1,0:T(8,128)(2,1)S(1)} %pad_maximum_fusion.4), channel_id=1, source_target_pairs={{0,5},{1,4},{2,7},{3,6},{4,1},{5,0},{6,3},{7,2},{8,13},{9,12},{10,... | collective-permute-start | bytes 393224 | tf_op jit(solution)/shard_map/ppermute | solution.py:356
  18.2 5.7 %collective-permute-start.8 = (bf16[528,128]{1,0:T(8,128)(2,1)S(1)}, bf16[528,128]{1,0:T(8,128)(2,1)S(1)}, u32[]{:S(2)}, u32[]{:S(2)}) collective-permute-start(bf16[528,128]{1,0:T(8,128)(2,1)S(1)} %shard_map.104.refs_1_), channel_id=1, source_target_pairs={{0,8},{8,0},{16,24},{24,16},{1,9},{9,1},{17,25},{25,17},{2,10},{10... | collective-permute-start | bytes 405512 | tf_op jit(solution)/shard_map/ppermute | solution.py:356
  24.6 6.6 %collective-permute-start.12 = (f32[8,128]{1,0:T(8,128)S(1)}, f32[8,128]{1,0:T(8,128)S(1)}, u32[]{:S(2)}, u32[]{:S(2)}) collective-permute-start(f32[8,128]{1,0:T(8,128)S(1)} %shard_map.107.refs_8_.refs_7_), channel_id=1, source_target_pairs={{0,24},{8,16},{16,8},{24,0},{1,25},{9,17},{17,9},{25,1},{2,26},{10... | collective-permute-start | bytes 12296 | tf_op jit(solution)/shard_map/ppermute | solution.py:356
  27.9 4.5 %collective-permute-start.11 = (f32[8,128]{1,0:T(8,128)S(1)}, f32[8,128]{1,0:T(8,128)S(1)}, u32[]{:S(2)}, u32[]{:S(2)}) collective-permute-start(f32[8,128]{1,0:T(8,128)S(1)} %shard_map.107.refs_8_.refs_7_), channel_id=1, source_target_pairs={{0,16},{8,24},{16,0},{24,8},{1,17},{9,25},{17,1},{25,9},{2,18},{10... | collective-permute-start | bytes 12296 | tf_op jit(solution)/shard_map/ppermute | solution.py:356
  28.1 4.3 %collective-permute-start.10 = (f32[8,128]{1,0:T(8,128)S(1)}, f32[8,128]{1,0:T(8,128)S(1)}, u32[]{:S(2)}, u32[]{:S(2)}) collective-permute-start(f32[8,128]{1,0:T(8,128)S(1)} %shard_map.107.refs_8_.refs_7_), channel_id=1, source_target_pairs={{0,8},{8,0},{16,24},{24,16},{1,9},{9,1},{17,25},{25,17},{2,10},{10... | collective-permute-start | bytes 12296 | tf_op jit(solution)/shard_map/ppermute | solution.py:356
  33.9 3.6 %collective-permute-start.13 = (bf16[4,2,64,128]{3,2,1,0:T(8,128)(2,1)S(1)}, bf16[4,2,64,128]{3,2,1,0:T(8,128)(2,1)S(1)}, u32[]{:S(2)}, u32[]{:S(2)}) collective-permute-start(bf16[4,2,64,128]{3,2,1,0:T(8,128)(2,1)S(1)} %get-tuple-element.33), channel_id=1, source_target_pairs={{0,2},{2,0},{1,3},{3,1},{4,6},{6,4},{5,7},{7,5},{8,10},{10,8},{9,1... | collective-permute-start | bytes 393224 | tf_op jit(solution)/shard_map/ppermute | solution.py:356
  34.0 6.3 %collective-permute-start.18 = (bf16[2,256,128]{2,1,0:T(8,128)(2,1)S(1)}, bf16[2,256,128]{2,1,0:T(8,128)(2,1)S(1)}, u32[]{:S(2)}, u32[]{:S(2)}) collective-permute-start(bf16[2,256,128]{2,1,0:T(8,128)(2,1)S(1)} %get-tuple-element.37), channel_id=1, source_target_pairs={{0,1},{1,0},{2,3},{3,2},{4,5},{5,4},{6,7},{7,6},{8,9},{9,8},{10,11... | collective-permute-start | bytes 393224 | tf_op jit(solution)/shard_map/ppermute | solution.py:356
  35.6 8.4 %collective-permute-start.19 = (bf16[2,256,128]{2,1,0:T(8,128)(2,1)S(1)}, bf16[2,256,128]{2,1,0:T(8,128)(2,1)S(1)}, u32[]{:S(2)}, u32[]{:S(2)}) collective-permute-start(bf16[2,256,128]{2,1,0:T(8,128)(2,1)S(1)} %get-tuple-element.38), channel_id=1, source_target_pairs={{0,4},{1,5},{2,6},{3,7},{4,0},{5,1},{6,2},{7,3},{8,12},{9,13},{10,... | collective-permute-start | bytes 393224 | tf_op jit(solution)/shard_map/ppermute | solution.py:356
  36.5 7.5 %collective-permute-start.20 = (bf16[2,256,128]{2,1,0:T(8,128)(2,1)S(1)}, bf16[2,256,128]{2,1,0:T(8,128)(2,1)S(1)}, u32[]{:S(2)}, u32[]{:S(2)}) collective-permute-start(bf16[2,256,128]{2,1,0:T(8,128)(2,1)S(1)} %get-tuple-element.39), channel_id=1, source_target_pairs={{0,5},{1,4},{2,7},{3,6},{4,1},{5,0},{6,3},{7,2},{8,13},{9,12},{10,... | collective-permute-start | bytes 393224 | tf_op jit(solution)/shard_map/ppermute | solution.py:356
  37.6 6.6 %collective-permute-start.14 = (bf16[2,2,64,128]{3,2,1,0:T(8,128)(2,1)S(1)}, bf16[2,2,64,128]{3,2,1,0:T(8,128)(2,1)S(1)}, u32[]{:S(2)}, u32[]{:S(2)}) collective-permute-start(bf16[2,2,64,128]{3,2,1,0:T(8,128)(2,1)S(1)} %pad_maximum_fusion.5), channel_id=1, source_target_pairs={{0,24},{8,16},{16,8},{24,0},{1,25},{9,17},{17,9},{25,1},{2,26},{10... | collective-permute-start | bytes 196616 | tf_op jit(solution)/shard_map/ppermute | solution.py:356
  39.7 6.4 %collective-permute-start.15 = (bf16[2,2,64,128]{3,2,1,0:T(8,128)(2,1)S(1)}, bf16[2,2,64,128]{3,2,1,0:T(8,128)(2,1)S(1)}, u32[]{:S(2)}, u32[]{:S(2)}) collective-permute-start(bf16[2,2,64,128]{3,2,1,0:T(8,128)(2,1)S(1)} %pad_maximum_fusion.6), channel_id=1, source_target_pairs={{0,16},{8,24},{16,0},{24,8},{1,17},{9,25},{17,1},{25,9},{2,18},{10... | collective-permute-start | bytes 196616 | tf_op jit(solution)/shard_map/ppermute | solution.py:356
  40.3 5.9 %collective-permute-start.16 = (bf16[2,2,64,128]{3,2,1,0:T(8,128)(2,1)S(1)}, bf16[2,2,64,128]{3,2,1,0:T(8,128)(2,1)S(1)}, u32[]{:S(2)}, u32[]{:S(2)}) collective-permute-start(bf16[2,2,64,128]{3,2,1,0:T(8,128)(2,1)S(1)} %pad_maximum_fusion.7), channel_id=1, source_target_pairs={{0,8},{8,0},{16,24},{24,16},{1,9},{9,1},{17,25},{25,17},{2,10},{10... | collective-permute-start | bytes 196616 | tf_op jit(solution)/shard_map/ppermute | solution.py:356
  46.2 4.0 %collective-permute-start.21 = (bf16[4,256,128]{2,1,0:T(8,128)(2,1)S(1)}, bf16[4,256,128]{2,1,0:T(8,128)(2,1)S(1)}, u32[]{:S(2)}, u32[]{:S(2)}) collective-permute-start(bf16[4,256,128]{2,1,0:T(8,128)(2,1)S(1)} %shard_map.111), channel_id=1, source_target_pairs={{0,2},{1,3},{2,0},{3,1},{4,6},{5,7},{6,4},{7,5},{8,10},{9,11},{10,... | collective-permute-start | bytes 786440 | tf_op jit(solution)/shard_map/ppermute | solution.py:356
  46.2 4.0 %collective-permute-start.17 = (bf16[2,64,128]{2,1,0:T(8,128)(2,1)S(1)}, bf16[2,64,128]{2,1,0:T(8,128)(2,1)S(1)}, u32[]{:S(2)}, u32[]{:S(2)}) collective-permute-start(bf16[2,64,128]{2,1,0:T(8,128)(2,1)S(1)} %get-tuple-element.35), channel_id=1, source_target_pairs={{0,4},{4,0},{1,5},{5,1},{2,6},{6,2},{3,7},{7,3},{8,12},{12,8},{9,1... | collective-permute-start | bytes 98312 | tf_op jit(solution)/shard_map/ppermute | solution.py:356

commit v18 on v16

--- a/solution.py
+++ b/solution.py
@@ -23,7 +23,7 @@
 VMEM = pl.BlockSpec(memory_space=pltpu.VMEM)
 
 FIRST = 2
-KEEP = (0, 1, 4, 5)
+KEEP = (0, 5, 1, 4)
 
 
 def split_pieces(x):

time: 51.4 us -> 52 us (1.012)
  waiting for transfers between devices: 13.9 us -> 16 us
  starting transfers between devices: 27.2 us -> 25.6 us
    ppermute x22, waiting for transfers between devices: 13.9 us -> 16 us  [swap(): return lax.ppermute(x, axis, [(i, i ^ distance) for i in range(size)])]
    ppermute x22, starting transfers between devices: 27.2 us -> 25.6 us  [swap(): return lax.ppermute(x, axis, [(i, i ^ distance) for i in range(size)])]
  transfers between devices with their start and end apart: 22 -> 22, of which waited for: 11 -> 14; matrix products, arithmetic and copies ran while one was open for 1% -> 1% of each run, Pallas kernels for 6% -> 6%
where the time goes in v18:
time: 52 us; the launch traced here: 51.7 us
  starting transfers between devices  25.6 us (49%)
  waiting for transfers between devices  16 us (31%)
  Pallas kernels  7.66 us (15%)
  between operations  2.11 us (4%)
    ppermute x22, starting transfers between devices, swap(): return lax.ppermute(x, axis, [(i, i ^ distance) for i in range(size)])  25.6 us
    ppermute x22, waiting for transfers between devices, swap(): return lax.ppermute(x, axis, [(i, i ^ distance) for i in range(size)])  16 us
    pallas_call x1, Pallas kernels, shards(): pl.pallas_call(functools.partial(part_kernel, blocks, nears, heads, token...  2.05 us
    pallas_call x2, Pallas kernels, part_lse(): pl.pallas_call(functools.partial(stat_kernel, held, first, nears, heads,...  1.77 us
    pallas_call x1, Pallas kernels, shards(): pl.pallas_call(functools.partial(token_kernel, blocks, nears, heads, toke...  1.46 us
    pallas_call x1, Pallas kernels, shards(): pl.pallas_call(functools.partial(pack_kernel, row_count, nears, heads), i...  1.38 us
  transfers between devices with their start and end apart: 22, of which 14 were waited for; matrix products, arithmetic and copies ran while one was open for 1% of the time, Pallas kernels for 6%

profile of v18, /device:TPU:0, one launch (start us, length us, event | category | flops | bytes accessed | tf_op | source)
XLA Modules:
  0.0 51.7 jit_solution(985317233723539551)
XLA Ops:
  0.6 1.4 %shard_map.103 = (bf16[144,128]{1,0:T(8,128)(2,1)S(1)}, bf16[144,128]{1,0:T(8,128)(2,1)S(1)}, bf16[144,128]{1,0:T(8,128)(2,1)S(1)}, bf16[144,128]{1,0:T(8,128)(2...) custom-call(bf16[256,128]{1,0:T(8,128)(2,1)} %bitcast.24, bf16[256,128]{1,0:T(8,128)(2,1)} %bitcast.25, ...), custom_call_target="tpu_custom_call" | custom-call | tf_op jit(solution)/shard_map/pallas_call | solution.py:424
  2.0 0.5 %collective-permute-start = (bf16[144,128]{1,0:T(8,128)(2,1)S(1)}, bf16[144,128]{1,0:T(8,128)(2,1)S(1)}, u32[]{:S(2)}, u32[]{:S(2)}) collective-permute-start(bf16[144,128]{1,0:T(8,128)(2,1)S(1)} %get-tuple-element.24), channel_id=1, source_target_pairs={{0,2},{2,0},{4,6},{6,4},{1,3},{3,1},{5,7},{7,5},{8,10},{10,8},{12,... | collective-permute-start | bytes 110600 | tf_op jit(solution)/shard_map/ppermute | solution.py:356
  2.5 2.6 %collective-permute-start.1 = (bf16[144,128]{1,0:T(8,128)(2,1)S(1)}, bf16[144,128]{1,0:T(8,128)(2,1)S(1)}, u32[]{:S(2)}, u32[]{:S(2)}) collective-permute-start(bf16[144,128]{1,0:T(8,128)(2,1)S(1)} %get-tuple-element.25), channel_id=1, source_target_pairs={{0,4},{2,6},{4,0},{6,2},{1,5},{3,7},{5,1},{7,3},{8,12},{10,14},{12... | collective-permute-start | bytes 110600 | tf_op jit(solution)/shard_map/ppermute | solution.py:356
  5.1 0.1 collective-permute-start.2
  5.2 0.1 collective-permute-start.4
  5.4 0.0 collective-permute-done
  5.4 1.8 %collective-permute-done.1 = bf16[144,128]{1,0:T(8,128)(2,1)S(1)} collective-permute-done((bf16[144,128]{1,0:T(8,128)(2,1)S(1)}, bf16[144,128]{1,0:T(8,128)(2,1)S(1)}, u32[]{:S(2)}, u32[]{:S(2)}) %collective-permute-start.1) | collective-permute-done | bytes 36896 | tf_op jit(solution)/shard_map/ppermute | solution.py:356
  7.2 1.4 %collective-permute-done.2 = bf16[144,128]{1,0:T(8,128)(2,1)S(1)} collective-permute-done((bf16[144,128]{1,0:T(8,128)(2,1)S(1)}, bf16[144,128]{1,0:T(8,128)(2,1)S(1)}, u32[]{:S(2)}, u32[]{:S(2)}) %collective-permute-start.2) | collective-permute-done | bytes 36896 | tf_op jit(solution)/shard_map/ppermute | solution.py:356
  8.6 2.7 %collective-permute-start.3 = (bf16[528,128]{1,0:T(8,128)(2,1)S(1)}, bf16[528,128]{1,0:T(8,128)(2,1)S(1)}, u32[]{:S(2)}, u32[]{:S(2)}) collective-permute-start(bf16[528,128]{1,0:T(8,128)(2,1)S(1)} %constant_dynamic-update-slice_fusion.refs_0_), channel_id=1, source_target_pairs={{0,16},{8,24},{16,0},{24,8},{1,17},{9,25},{17,1},{25,9},{2,18},{10... | collective-permute-start | bytes 405512 | tf_op jit(solution)/shard_map/ppermute | solution.py:356
  11.2 0.0 collective-permute-done.4
  11.3 1.9 %collective-permute-start.5 = (bf16[2,256,128]{2,1,0:T(8,128)(2,1)S(1)}, bf16[2,256,128]{2,1,0:T(8,128)(2,1)S(1)}, u32[]{:S(2)}, u32[]{:S(2)}) collective-permute-start(bf16[2,256,128]{2,1,0:T(8,128)(2,1)S(1)} %pad_maximum_fusion.1), channel_id=1, source_target_pairs={{0,5},{1,4},{2,7},{3,6},{4,1},{5,0},{6,3},{7,2},{8,13},{9,12},{10,... | collective-permute-start | bytes 393224 | tf_op jit(solution)/shard_map/ppermute | solution.py:356
  13.2 0.6 %collective-permute-start.6 = (bf16[2,256,128]{2,1,0:T(8,128)(2,1)S(1)}, bf16[2,256,128]{2,1,0:T(8,128)(2,1)S(1)}, u32[]{:S(2)}, u32[]{:S(2)}) collective-permute-start(bf16[2,256,128]{2,1,0:T(8,128)(2,1)S(1)} %pad_maximum_fusion.2), channel_id=1, source_target_pairs={{0,1},{1,0},{2,3},{3,2},{4,5},{5,4},{6,7},{7,6},{8,9},{9,8},{10,11... | collective-permute-start | bytes 393224 | tf_op jit(solution)/shard_map/ppermute | solution.py:356
  14.4 1.6 %collective-permute-start.7 = (bf16[528,128]{1,0:T(8,128)(2,1)S(1)}, bf16[528,128]{1,0:T(8,128)(2,1)S(1)}, u32[]{:S(2)}, u32[]{:S(2)}) collective-permute-start(bf16[528,128]{1,0:T(8,128)(2,1)S(1)} %constant_dynamic-update-slice_fusion.refs_0_), channel_id=1, source_target_pairs={{0,8},{8,0},{16,24},{24,16},{1,9},{9,1},{17,25},{25,17},{2,10},{10... | collective-permute-start | bytes 405512 | tf_op jit(solution)/shard_map/ppermute | solution.py:356
  16.1 1.2 %collective-permute-start.9 = (bf16[2,256,128]{2,1,0:T(8,128)(2,1)S(1)}, bf16[2,256,128]{2,1,0:T(8,128)(2,1)S(1)}, u32[]{:S(2)}, u32[]{:S(2)}) collective-permute-start(bf16[2,256,128]{2,1,0:T(8,128)(2,1)S(1)} %pad_maximum_fusion.4), channel_id=1, source_target_pairs={{0,4},{1,5},{2,6},{3,7},{4,0},{5,1},{6,2},{7,3},{8,12},{9,13},{10,... | collective-permute-start | bytes 393224 | tf_op jit(solution)/shard_map/ppermute | solution.py:356
  17.3 0.9 %collective-permute-done.3.refs_0_ = bf16[528,128]{1,0:T(8,128)(2,1)S(1)} collective-permute-done((bf16[528,128]{1,0:T(8,128)(2,1)S(1)}, bf16[528,128]{1,0:T(8,128)(2,1)S(1)}, u32[]{:S(2)}, u32[]{:S(2)}) %collective-permute-start.3) | collective-permute-done | bytes 135200 | tf_op jit(solution)/shard_map/ppermute | solution.py:356
  18.2 0.4 collective-permute-done.5.refs_1_.refs_4_.refs_2_.refs_5_
  18.6 1.2 %collective-permute-done.6.refs_2_.refs_5_.refs_3_.refs_6_ = bf16[2,256,128]{2,1,0:T(8,128)(2,1)S(1)} collective-permute-done((bf16[2,256,128]{2,1,0:T(8,128)(2,1)S(1)}, bf16[2,256,128]{2,1,0:T(8,128)(2,1)S(1)}, u32[]{:S(2)}, u32[]{:S(2)}) %collective-permute-start.6) | collective-permute-done | bytes 131104 | tf_op jit(solution)/shard_map/ppermute | solution.py:356
  19.8 1.6 %collective-permute-start.8 = (bf16[528,128]{1,0:T(8,128)(2,1)S(1)}, bf16[528,128]{1,0:T(8,128)(2,1)S(1)}, u32[]{:S(2)}, u32[]{:S(2)}) collective-permute-start(bf16[528,128]{1,0:T(8,128)(2,1)S(1)} %shard_map.104.refs_1_), channel_id=1, source_target_pairs={{0,8},{8,0},{16,24},{24,16},{1,9},{9,1},{17,25},{25,17},{2,10},{10... | collective-permute-start | bytes 405512 | tf_op jit(solution)/shard_map/ppermute | solution.py:356
  22.1 1.1 %shard_map.105.refs_1_.refs_5_ = f32[8,128]{1,0:T(8,128)S(1)} custom-call(s32[1,1024]{1,0:T(1,128)S(1)} %compare_select_fusion.ends_ref, bf16[528,128]{1,0:T(8,128)(2,1)S(1)} %constant_dynamic-update-slice_fusion.refs_0_, bf16[528,128]{1,0:T(8,128)(2,1)S(1)} %shard_map.104.refs_1_, bf16[528,128]{1,0:T(8,128)(2,1)S(1)} %collective-permute-done.7.refs_2_, ...), custom_call_target="tpu_custom_call" | custom-call | tf_op jit(solution)/shard_map/pallas_call | solution.py:457
  23.2 1.6 %collective-permute-done.8.refs_0_ = bf16[528,128]{1,0:T(8,128)(2,1)S(1)} collective-permute-done((bf16[528,128]{1,0:T(8,128)(2,1)S(1)}, bf16[528,128]{1,0:T(8,128)(2,1)S(1)}, u32[]{:S(2)}, u32[]{:S(2)}) %collective-permute-start.8) | collective-permute-done | bytes 135200 | tf_op jit(solution)/shard_map/ppermute | solution.py:356
  24.8 0.6 %shard_map.107.refs_8_.refs_7_ = f32[8,128]{1,0:T(8,128)S(1)} custom-call(s32[1,1024]{1,0:T(1,128)S(1)} %compare_select_fusion.ends_ref, bf16[528,128]{1,0:T(8,128)(2,1)S(1)} %shard_map.106.refs_0_.refs_3_, bf16[2,256,128]{2,1,0:T(8,128)(2,1)S(1)} %pad_maximum_fusion.3.refs_3_.refs_1_.refs_4_, ...), custom_call_target="tpu_custom_call" | custom-call | tf_op jit(solution)/shard_map/pallas_call | solution.py:457
  25.4 2.5 %collective-permute-start.12 = (f32[8,128]{1,0:T(8,128)S(1)}, f32[8,128]{1,0:T(8,128)S(1)}, u32[]{:S(2)}, u32[]{:S(2)}) collective-permute-start(f32[8,128]{1,0:T(8,128)S(1)} %shard_map.107.refs_8_.refs_7_), channel_id=1, source_target_pairs={{0,24},{8,16},{16,8},{24,0},{1,25},{9,17},{17,9},{25,1},{2,26},{10... | collective-permute-start | bytes 12296 | tf_op jit(solution)/shard_map/ppermute | solution.py:356
  27.9 0.6 %collective-permute-start.11 = (f32[8,128]{1,0:T(8,128)S(1)}, f32[8,128]{1,0:T(8,128)S(1)}, u32[]{:S(2)}, u32[]{:S(2)}) collective-permute-start(f32[8,128]{1,0:T(8,128)S(1)} %shard_map.107.refs_8_.refs_7_), channel_id=1, source_target_pairs={{0,16},{8,24},{16,0},{24,8},{1,17},{9,25},{17,1},{25,9},{2,18},{10... | collective-permute-start | bytes 12296 | tf_op jit(solution)/shard_map/ppermute | solution.py:356
  28.5 1.4 %collective-permute-start.10 = (f32[8,128]{1,0:T(8,128)S(1)}, f32[8,128]{1,0:T(8,128)S(1)}, u32[]{:S(2)}, u32[]{:S(2)}) collective-permute-start(f32[8,128]{1,0:T(8,128)S(1)} %shard_map.107.refs_8_.refs_7_), channel_id=1, source_target_pairs={{0,8},{8,0},{16,24},{24,16},{1,9},{9,1},{17,25},{25,17},{2,10},{10... | collective-permute-start | bytes 12296 | tf_op jit(solution)/shard_map/ppermute | solution.py:356
  29.9 2.1 %shard_map.108 = (bf16[4,256,1024]{2,1,0:T(8,128)(2,1)S(1)}, bf16[4,256,1024]{2,1,0:T(8,128)(2,1)S(1)}, f32[128,1024]{1,0:T(8,128)S(1)}) custom-call(s32[1,1024]{1,0:T(1,128)S(1)} %compare_select_fusion.ends_ref, bf16[528,128]{1,0:T(8,128)(2,1)S(1)} %constant_dynamic-update-slice_fusion.refs_0_, bf16[528,128]{1,0:T(8,128)(2,1)S(1)} %shard_map.104.refs_1_, ...), custom_call_target="tpu_custom_call" | custom-call | tf_op jit(solution)/shard_map/pallas_call | solution.py:471
  32.0 0.0 collective-permute-done.12.refs_10_
  32.0 0.4 collective-permute-done.11.refs_9_
  32.5 0.0 collective-permute-done.10.refs_8_
  32.5 1.5 %shard_map.109 = (bf16[2,256,128]{2,1,0:T(8,128)(2,1)S(1)}, bf16[2,256,128]{2,1,0:T(8,128)(2,1)S(1)}, bf16[2,256,128]{2,1,0:T(8,128)(2,1)S(1)}, bf16[2,256,128]{...) custom-call(s32[1,1024]{1,0:T(1,128)S(1)} %compare_convert_fusion.live_ref, ...), custom_call_target="tpu_custom_call" | custom-call | tf_op jit(solution)/shard_map/pallas_call | solution.py:480
  33.9 0.1 collective-permute-start.13
  34.0 1.9 %collective-permute-start.18 = (bf16[2,256,128]{2,1,0:T(8,128)(2,1)S(1)}, bf16[2,256,128]{2,1,0:T(8,128)(2,1)S(1)}, u32[]{:S(2)}, u32[]{:S(2)}) collective-permute-start(bf16[2,256,128]{2,1,0:T(8,128)(2,1)S(1)} %get-tuple-element.37), channel_id=1, source_target_pairs={{0,5},{1,4},{2,7},{3,6},{4,1},{5,0},{6,3},{7,2},{8,13},{9,12},{10,... | collective-permute-start | bytes 393224 | tf_op jit(solution)/shard_map/ppermute | solution.py:356
  35.9 0.5 collective-permute-start.19
  36.4 1.1 %collective-permute-start.20 = (bf16[2,256,128]{2,1,0:T(8,128)(2,1)S(1)}, bf16[2,256,128]{2,1,0:T(8,128)(2,1)S(1)}, u32[]{:S(2)}, u32[]{:S(2)}) collective-permute-start(bf16[2,256,128]{2,1,0:T(8,128)(2,1)S(1)} %get-tuple-element.39), channel_id=1, source_target_pairs={{0,4},{1,5},{2,6},{3,7},{4,0},{5,1},{6,2},{7,3},{8,12},{9,13},{10,... | collective-permute-start | bytes 393224 | tf_op jit(solution)/shard_map/ppermute | solution.py:356
  37.6 0.0 collective-permute-done.13.refs_1_
  37.6 2.1 %collective-permute-start.14 = (bf16[2,2,64,128]{3,2,1,0:T(8,128)(2,1)S(1)}, bf16[2,2,64,128]{3,2,1,0:T(8,128)(2,1)S(1)}, u32[]{:S(2)}, u32[]{:S(2)}) collective-permute-start(bf16[2,2,64,128]{3,2,1,0:T(8,128)(2,1)S(1)} %pad_maximum_fusion.5), channel_id=1, source_target_pairs={{0,24},{8,16},{16,8},{24,0},{1,25},{9,17},{17,9},{25,1},{2,26},{10... | collective-permute-start | bytes 196616 | tf_op jit(solution)/shard_map/ppermute | solution.py:356
  39.7 0.5 %collective-permute-start.15 = (bf16[2,2,64,128]{3,2,1,0:T(8,128)(2,1)S(1)}, bf16[2,2,64,128]{3,2,1,0:T(8,128)(2,1)S(1)}, u32[]{:S(2)}, u32[]{:S(2)}) collective-permute-start(bf16[2,2,64,128]{3,2,1,0:T(8,128)(2,1)S(1)} %pad_maximum_fusion.6), channel_id=1, source_target_pairs={{0,16},{8,24},{16,0},{24,8},{1,17},{9,25},{17,1},{25,9},{2,18},{10... | collective-permute-start | bytes 196616 | tf_op jit(solution)/shard_map/ppermute | solution.py:356
  40.3 1.0 %collective-permute-done.18.refs_3_ = bf16[2,256,128]{2,1,0:T(8,128)(2,1)S(1)} collective-permute-done((bf16[2,256,128]{2,1,0:T(8,128)(2,1)S(1)}, bf16[2,256,128]{2,1,0:T(8,128)(2,1)S(1)}, u32[]{:S(2)}, u32[]{:S(2)}) %collective-permute-start.18) | collective-permute-done | bytes 131104 | tf_op jit(solution)/shard_map/ppermute | solution.py:356
  41.3 1.1 %collective-permute-start.16 = (bf16[2,2,64,128]{3,2,1,0:T(8,128)(2,1)S(1)}, bf16[2,2,64,128]{3,2,1,0:T(8,128)(2,1)S(1)}, u32[]{:S(2)}, u32[]{:S(2)}) collective-permute-start(bf16[2,2,64,128]{3,2,1,0:T(8,128)(2,1)S(1)} %pad_maximum_fusion.7), channel_id=1, source_target_pairs={{0,8},{8,0},{16,24},{24,16},{1,9},{9,1},{17,25},{25,17},{2,10},{10... | collective-permute-start | bytes 196616 | tf_op jit(solution)/shard_map/ppermute | solution.py:356
  42.3 0.7 %collective-permute-done.19.refs_4_ = bf16[2,256,128]{2,1,0:T(8,128)(2,1)S(1)} collective-permute-done((bf16[2,256,128]{2,1,0:T(8,128)(2,1)S(1)}, bf16[2,256,128]{2,1,0:T(8,128)(2,1)S(1)}, u32[]{:S(2)}, u32[]{:S(2)}) %collective-permute-start.19) | collective-permute-done | bytes 131104 | tf_op jit(solution)/shard_map/ppermute | solution.py:356
  43.1 0.6 %collective-permute-done.20.refs_5_ = bf16[2,256,128]{2,1,0:T(8,128)(2,1)S(1)} collective-permute-done((bf16[2,256,128]{2,1,0:T(8,128)(2,1)S(1)}, bf16[2,256,128]{2,1,0:T(8,128)(2,1)S(1)}, u32[]{:S(2)}, u32[]{:S(2)}) %collective-permute-start.20) | collective-permute-done | bytes 131104 | tf_op jit(solution)/shard_map/ppermute | solution.py:356
  43.7 0.4 collective-permute-done.14.refs_2_.refs_1_
  44.0 2.6 %collective-permute-done.15.refs_3_.refs_2_ = bf16[2,2,64,128]{3,2,1,0:T(8,128)(2,1)S(1)} collective-permute-done((bf16[2,2,64,128]{3,2,1,0:T(8,128)(2,1)S(1)}, bf16[2,2,64,128]{3,2,1,0:T(8,128)(2,1)S(1)}, u32[]{:S(2)}, u32[]{:S(2)}) %collective-permute-start.15) | collective-permute-done | bytes 65568 | tf_op jit(solution)/shard_map/ppermute | solution.py:356
  46.6 0.1 collective-permute-done.16.refs_4_.refs_3_
  46.7 0.0 collective-permute-start.21
  46.8 1.0 %collective-permute-start.17 = (bf16[2,64,128]{2,1,0:T(8,128)(2,1)S(1)}, bf16[2,64,128]{2,1,0:T(8,128)(2,1)S(1)}, u32[]{:S(2)}, u32[]{:S(2)}) collective-permute-start(bf16[2,64,128]{2,1,0:T(8,128)(2,1)S(1)} %get-tuple-element.35), channel_id=1, source_target_pairs={{0,4},{4,0},{1,5},{5,1},{2,6},{6,2},{3,7},{7,3},{8,12},{12,8},{9,1... | collective-permute-start | bytes 98312 | tf_op jit(solution)/shard_map/ppermute | solution.py:356
  47.8 3.0 %collective-permute-done.17.refs_1_ = bf16[2,64,128]{2,1,0:T(8,128)(2,1)S(1)} collective-permute-done((bf16[2,64,128]{2,1,0:T(8,128)(2,1)S(1)}, bf16[2,64,128]{2,1,0:T(8,128)(2,1)S(1)}, u32[]{:S(2)}, u32[]{:S(2)}) %collective-permute-start.17) | collective-permute-done | bytes 32800 | tf_op jit(solution)/shard_map/ppermute | solution.py:356
  50.8 0.0 collective-permute-done.21.refs_6_
  50.8 1.0 %shard_map.112 = (bf16[256,128]{1,0:T(8,128)(2,1)}, bf16[128,1024]{1,0:T(8,128)(2,1)}, bf16[128,1024]{1,0:T(8,128)(2,1)}) custom-call(bf16[2,64,128]{2,1,0:T(8,128)(2,1)S(1)} %get-tuple-element.34.refs_0_, bf16[2,64,128]{2,1,0:T(8,128)(2,1)S(1)} %collective-permute-done.17.refs_1_, bf16[2,256,128]{2,1,0:T(8,128)(2,1)S(1)} %get-tuple-element.36.refs_2_, ...), custom_call_target="tpu_custom_call" | custom-call | tf_op jit(solution)/shard_map/pallas_call | solution.py:503
  (29 shorter events, 0.4 us)
Async XLA Ops:
  2.0 3.4 %collective-permute-start = (bf16[144,128]{1,0:T(8,128)(2,1)S(1)}, bf16[144,128]{1,0:T(8,128)(2,1)S(1)}, u32[]{:S(2)}, u32[]{:S(2)}) collective-permute-start(bf16[144,128]{1,0:T(8,128)(2,1)S(1)} %get-tuple-element.24), channel_id=1, source_target_pairs={{0,2},{2,0},{4,6},{6,4},{1,3},{3,1},{5,7},{7,5},{8,10},{10,8},{12,... | collective-permute-start | bytes 110600 | tf_op jit(solution)/shard_map/ppermute | solution.py:356
  2.5 4.7 %collective-permute-start.1 = (bf16[144,128]{1,0:T(8,128)(2,1)S(1)}, bf16[144,128]{1,0:T(8,128)(2,1)S(1)}, u32[]{:S(2)}, u32[]{:S(2)}) collective-permute-start(bf16[144,128]{1,0:T(8,128)(2,1)S(1)} %get-tuple-element.25), channel_id=1, source_target_pairs={{0,4},{2,6},{4,0},{6,2},{1,5},{3,7},{5,1},{7,3},{8,12},{10,14},{12... | collective-permute-start | bytes 110600 | tf_op jit(solution)/shard_map/ppermute | solution.py:356
  5.1 3.4 %collective-permute-start.2 = (bf16[144,128]{1,0:T(8,128)(2,1)S(1)}, bf16[144,128]{1,0:T(8,128)(2,1)S(1)}, u32[]{:S(2)}, u32[]{:S(2)}) collective-permute-start(bf16[144,128]{1,0:T(8,128)(2,1)S(1)} %get-tuple-element.26), channel_id=1, source_target_pairs={{0,6},{2,4},{4,2},{6,0},{1,7},{3,5},{5,3},{7,1},{8,14},{10,12},{12... | collective-permute-start | bytes 110600 | tf_op jit(solution)/shard_map/ppermute | solution.py:356
  5.2 6.0 %collective-permute-start.4 = (bf16[4,256,128]{2,1,0:T(8,128)(2,1)S(1)}, bf16[4,256,128]{2,1,0:T(8,128)(2,1)S(1)}, u32[]{:S(2)}, u32[]{:S(2)}) collective-permute-start(bf16[4,256,128]{2,1,0:T(8,128)(2,1)S(1)} %get-tuple-element.28), channel_id=1, source_target_pairs={{0,2},{1,3},{2,0},{3,1},{4,6},{5,7},{6,4},{7,5},{8,10},{9,11},{10,... | collective-permute-start | bytes 786440 | tf_op jit(solution)/shard_map/ppermute | solution.py:356
  8.6 9.6 %collective-permute-start.3 = (bf16[528,128]{1,0:T(8,128)(2,1)S(1)}, bf16[528,128]{1,0:T(8,128)(2,1)S(1)}, u32[]{:S(2)}, u32[]{:S(2)}) collective-permute-start(bf16[528,128]{1,0:T(8,128)(2,1)S(1)} %constant_dynamic-update-slice_fusion.refs_0_), channel_id=1, source_target_pairs={{0,16},{8,24},{16,0},{24,8},{1,17},{9,25},{17,1},{25,9},{2,18},{10... | collective-permute-start | bytes 405512 | tf_op jit(solution)/shard_map/ppermute | solution.py:356
  11.3 7.3 %collective-permute-start.5 = (bf16[2,256,128]{2,1,0:T(8,128)(2,1)S(1)}, bf16[2,256,128]{2,1,0:T(8,128)(2,1)S(1)}, u32[]{:S(2)}, u32[]{:S(2)}) collective-permute-start(bf16[2,256,128]{2,1,0:T(8,128)(2,1)S(1)} %pad_maximum_fusion.1), channel_id=1, source_target_pairs={{0,5},{1,4},{2,7},{3,6},{4,1},{5,0},{6,3},{7,2},{8,13},{9,12},{10,... | collective-permute-start | bytes 393224 | tf_op jit(solution)/shard_map/ppermute | solution.py:356
  13.2 6.6 %collective-permute-start.6 = (bf16[2,256,128]{2,1,0:T(8,128)(2,1)S(1)}, bf16[2,256,128]{2,1,0:T(8,128)(2,1)S(1)}, u32[]{:S(2)}, u32[]{:S(2)}) collective-permute-start(bf16[2,256,128]{2,1,0:T(8,128)(2,1)S(1)} %pad_maximum_fusion.2), channel_id=1, source_target_pairs={{0,1},{1,0},{2,3},{3,2},{4,5},{5,4},{6,7},{7,6},{8,9},{9,8},{10,11... | collective-permute-start | bytes 393224 | tf_op jit(solution)/shard_map/ppermute | solution.py:356
  14.4 7.7 %collective-permute-start.7 = (bf16[528,128]{1,0:T(8,128)(2,1)S(1)}, bf16[528,128]{1,0:T(8,128)(2,1)S(1)}, u32[]{:S(2)}, u32[]{:S(2)}) collective-permute-start(bf16[528,128]{1,0:T(8,128)(2,1)S(1)} %constant_dynamic-update-slice_fusion.refs_0_), channel_id=1, source_target_pairs={{0,8},{8,0},{16,24},{24,16},{1,9},{9,1},{17,25},{25,17},{2,10},{10... | collective-permute-start | bytes 405512 | tf_op jit(solution)/shard_map/ppermute | solution.py:356
  16.1 6.0 %collective-permute-start.9 = (bf16[2,256,128]{2,1,0:T(8,128)(2,1)S(1)}, bf16[2,256,128]{2,1,0:T(8,128)(2,1)S(1)}, u32[]{:S(2)}, u32[]{:S(2)}) collective-permute-start(bf16[2,256,128]{2,1,0:T(8,128)(2,1)S(1)} %pad_maximum_fusion.4), channel_id=1, source_target_pairs={{0,4},{1,5},{2,6},{3,7},{4,0},{5,1},{6,2},{7,3},{8,12},{9,13},{10,... | collective-permute-start | bytes 393224 | tf_op jit(solution)/shard_map/ppermute | solution.py:356
  19.8 5.0 %collective-permute-start.8 = (bf16[528,128]{1,0:T(8,128)(2,1)S(1)}, bf16[528,128]{1,0:T(8,128)(2,1)S(1)}, u32[]{:S(2)}, u32[]{:S(2)}) collective-permute-start(bf16[528,128]{1,0:T(8,128)(2,1)S(1)} %shard_map.104.refs_1_), channel_id=1, source_target_pairs={{0,8},{8,0},{16,24},{24,16},{1,9},{9,1},{17,25},{25,17},{2,10},{10... | collective-permute-start | bytes 405512 | tf_op jit(solution)/shard_map/ppermute | solution.py:356
  25.4 6.6 %collective-permute-start.12 = (f32[8,128]{1,0:T(8,128)S(1)}, f32[8,128]{1,0:T(8,128)S(1)}, u32[]{:S(2)}, u32[]{:S(2)}) collective-permute-start(f32[8,128]{1,0:T(8,128)S(1)} %shard_map.107.refs_8_.refs_7_), channel_id=1, source_target_pairs={{0,24},{8,16},{16,8},{24,0},{1,25},{9,17},{17,9},{25,1},{2,26},{10... | collective-permute-start | bytes 12296 | tf_op jit(solution)/shard_map/ppermute | solution.py:356
  27.9 4.5 %collective-permute-start.11 = (f32[8,128]{1,0:T(8,128)S(1)}, f32[8,128]{1,0:T(8,128)S(1)}, u32[]{:S(2)}, u32[]{:S(2)}) collective-permute-start(f32[8,128]{1,0:T(8,128)S(1)} %shard_map.107.refs_8_.refs_7_), channel_id=1, source_target_pairs={{0,16},{8,24},{16,0},{24,8},{1,17},{9,25},{17,1},{25,9},{2,18},{10... | collective-permute-start | bytes 12296 | tf_op jit(solution)/shard_map/ppermute | solution.py:356
  28.5 3.9 %collective-permute-start.10 = (f32[8,128]{1,0:T(8,128)S(1)}, f32[8,128]{1,0:T(8,128)S(1)}, u32[]{:S(2)}, u32[]{:S(2)}) collective-permute-start(f32[8,128]{1,0:T(8,128)S(1)} %shard_map.107.refs_8_.refs_7_), channel_id=1, source_target_pairs={{0,8},{8,0},{16,24},{24,16},{1,9},{9,1},{17,25},{25,17},{2,10},{10... | collective-permute-start | bytes 12296 | tf_op jit(solution)/shard_map/ppermute | solution.py:356
  33.9 3.6 %collective-permute-start.13 = (bf16[4,2,64,128]{3,2,1,0:T(8,128)(2,1)S(1)}, bf16[4,2,64,128]{3,2,1,0:T(8,128)(2,1)S(1)}, u32[]{:S(2)}, u32[]{:S(2)}) collective-permute-start(bf16[4,2,64,128]{3,2,1,0:T(8,128)(2,1)S(1)} %get-tuple-element.33), channel_id=1, source_target_pairs={{0,2},{2,0},{1,3},{3,1},{4,6},{6,4},{5,7},{7,5},{8,10},{10,8},{9,1... | collective-permute-start | bytes 393224 | tf_op jit(solution)/shard_map/ppermute | solution.py:356
  34.0 7.3 %collective-permute-start.18 = (bf16[2,256,128]{2,1,0:T(8,128)(2,1)S(1)}, bf16[2,256,128]{2,1,0:T(8,128)(2,1)S(1)}, u32[]{:S(2)}, u32[]{:S(2)}) collective-permute-start(bf16[2,256,128]{2,1,0:T(8,128)(2,1)S(1)} %get-tuple-element.37), channel_id=1, source_target_pairs={{0,5},{1,4},{2,7},{3,6},{4,1},{5,0},{6,3},{7,2},{8,13},{9,12},{10,... | collective-permute-start | bytes 393224 | tf_op jit(solution)/shard_map/ppermute | solution.py:356
  35.9 7.1 %collective-permute-start.19 = (bf16[2,256,128]{2,1,0:T(8,128)(2,1)S(1)}, bf16[2,256,128]{2,1,0:T(8,128)(2,1)S(1)}, u32[]{:S(2)}, u32[]{:S(2)}) collective-permute-start(bf16[2,256,128]{2,1,0:T(8,128)(2,1)S(1)} %get-tuple-element.38), channel_id=1, source_target_pairs={{0,1},{1,0},{2,3},{3,2},{4,5},{5,4},{6,7},{7,6},{8,9},{9,8},{10,11... | collective-permute-start | bytes 393224 | tf_op jit(solution)/shard_map/ppermute | solution.py:356
  36.4 7.2 %collective-permute-start.20 = (bf16[2,256,128]{2,1,0:T(8,128)(2,1)S(1)}, bf16[2,256,128]{2,1,0:T(8,128)(2,1)S(1)}, u32[]{:S(2)}, u32[]{:S(2)}) collective-permute-start(bf16[2,256,128]{2,1,0:T(8,128)(2,1)S(1)} %get-tuple-element.39), channel_id=1, source_target_pairs={{0,4},{1,5},{2,6},{3,7},{4,0},{5,1},{6,2},{7,3},{8,12},{9,13},{10,... | collective-permute-start | bytes 393224 | tf_op jit(solution)/shard_map/ppermute | solution.py:356
  37.6 6.4 %collective-permute-start.14 = (bf16[2,2,64,128]{3,2,1,0:T(8,128)(2,1)S(1)}, bf16[2,2,64,128]{3,2,1,0:T(8,128)(2,1)S(1)}, u32[]{:S(2)}, u32[]{:S(2)}) collective-permute-start(bf16[2,2,64,128]{3,2,1,0:T(8,128)(2,1)S(1)} %pad_maximum_fusion.5), channel_id=1, source_target_pairs={{0,24},{8,16},{16,8},{24,0},{1,25},{9,17},{17,9},{25,1},{2,26},{10... | collective-permute-start | bytes 196616 | tf_op jit(solution)/shard_map/ppermute | solution.py:356
  39.7 6.9 %collective-permute-start.15 = (bf16[2,2,64,128]{3,2,1,0:T(8,128)(2,1)S(1)}, bf16[2,2,64,128]{3,2,1,0:T(8,128)(2,1)S(1)}, u32[]{:S(2)}, u32[]{:S(2)}) collective-permute-start(bf16[2,2,64,128]{3,2,1,0:T(8,128)(2,1)S(1)} %pad_maximum_fusion.6), channel_id=1, source_target_pairs={{0,16},{8,24},{16,0},{24,8},{1,17},{9,25},{17,1},{25,9},{2,18},{10... | collective-permute-start | bytes 196616 | tf_op jit(solution)/shard_map/ppermute | solution.py:356
  41.3 5.5 %collective-permute-start.16 = (bf16[2,2,64,128]{3,2,1,0:T(8,128)(2,1)S(1)}, bf16[2,2,64,128]{3,2,1,0:T(8,128)(2,1)S(1)}, u32[]{:S(2)}, u32[]{:S(2)}) collective-permute-start(bf16[2,2,64,128]{3,2,1,0:T(8,128)(2,1)S(1)} %pad_maximum_fusion.7), channel_id=1, source_target_pairs={{0,8},{8,0},{16,24},{24,16},{1,9},{9,1},{17,25},{25,17},{2,10},{10... | collective-permute-start | bytes 196616 | tf_op jit(solution)/shard_map/ppermute | solution.py:356
  46.7 4.0 %collective-permute-start.21 = (bf16[4,256,128]{2,1,0:T(8,128)(2,1)S(1)}, bf16[4,256,128]{2,1,0:T(8,128)(2,1)S(1)}, u32[]{:S(2)}, u32[]{:S(2)}) collective-permute-start(bf16[4,256,128]{2,1,0:T(8,128)(2,1)S(1)} %shard_map.111), channel_id=1, source_target_pairs={{0,2},{1,3},{2,0},{3,1},{4,6},{5,7},{6,4},{7,5},{8,10},{9,11},{10,... | collective-permute-start | bytes 786440 | tf_op jit(solution)/shard_map/ppermute | solution.py:356
  46.8 4.0 %collective-permute-start.17 = (bf16[2,64,128]{2,1,0:T(8,128)(2,1)S(1)}, bf16[2,64,128]{2,1,0:T(8,128)(2,1)S(1)}, u32[]{:S(2)}, u32[]{:S(2)}) collective-permute-start(bf16[2,64,128]{2,1,0:T(8,128)(2,1)S(1)} %get-tuple-element.35), channel_id=1, source_target_pairs={{0,4},{4,0},{1,5},{5,1},{2,6},{6,2},{3,7},{7,3},{8,12},{12,8},{9,1... | collective-permute-start | bytes 98312 | tf_op jit(solution)/shard_map/ppermute | solution.py:356
